TPU v7x, 32 devices: a whole 2x2x4 slice. The times are simulated.
32 devices in a mesh: dp: 16 (over z, x, core), mp: 2 (over y).
Axes of the slice: x: 2, y: 2, z: 4, core: 2. Of those that a mesh axis runs over, the one named last changes fastest.
Arguments:
- gradients: bfloat16 [16, 34816, 128], P('dp', 'mp'), may hold values from -8 to 8
- weights: float32 [34816, 128], P('mp'), may hold values from -40 to 40
- first_moment: float32 [2, 17408, 128], P('mp', 'dp'), may hold values from -240 to 240
- second_moment: float32 [2, 17408, 128], P('mp', 'dp'), may hold values from 0.3 to 3
- owner_list: int32 [2, 17408], P('mp'), may hold values from 0 to 15, as said below
- norm_grads: bfloat16 [16, 2, 1024], P('dp'), may hold values from -6 to 6
- norm_state: float32 [3, 2, 1024], replicated, may hold values from -1.6 to 3, as said below
Outputs:
- new_weights: float32 [34816, 128], P('mp')
- new_first: float32 [2, 17408, 128], P('mp', 'dp')
- new_second: float32 [2, 17408, 128], P('mp', 'dp')
- new_norm_state: float32 [3, 2, 1024], replicated
- trust_ratios: float32 [7], replicated
Inputs may be any that keep to these rules, and one draw needn't show every extreme that they name: `owner_list`: in every mp shard each dp index owns exactly 1088 of the 17408 blocks. `norm_state`: gains near 1, second moments positive.
All inputs are finite; a program needn't handle non-finite values.
Results may differ from a plain program's by a relative error of at most 0.0003.
Values sent between devices are 32-bit elements; how exact they have to be, the bound alone decides.
No kernel may reach another device: no remote copies, remote signals or barrier semaphores. Data moves between devices by JAX's collectives and lax.ppermute only.
A program may use at most 64 MiB of HBM per device.

v0:
```python
import jax
import jax.numpy as jnp
from jax import lax
from jax.sharding import PartitionSpec as P

D = 1024
NTAB = 8
NKEYS = 256
KDIM = 128
LANE = 128
VROW_DEV = 512


beta_one = 0.9
beta_two = 0.99
bias_one = 1.0 - 0.9**4
bias_two = 1.0 - 0.99**4
epsilon = 1e-06
learning = 0.02
decay_rate = 0.01
matrices = 5


def block_matrix(block_count, narrow):
    query_blocks = D * D // (LANE * narrow)
    key_blocks = NTAB * NKEYS * KDIM // (LANE * narrow)
    value_blocks = VROW_DEV * D // LANE
    position = jnp.arange(block_count, dtype=jnp.int32)
    bounds = (
        query_blocks,
        query_blocks + key_blocks,
        query_blocks + key_blocks + value_blocks,
        2 * query_blocks + key_blocks + value_blocks,
    )
    result = jnp.zeros((block_count,), jnp.int32)
    for boundary in bounds:
        result = result + (position >= boundary).astype(jnp.int32)
    return result


def adam_step(gradient, moment_one, moment_two, weight):
    moment_one = beta_one * moment_one + (1.0 - beta_one) * gradient
    moment_two = beta_two * moment_two + (1.0 - beta_two) * gradient * gradient
    update = (
        moment_one / bias_one / (jnp.sqrt(moment_two / bias_two) + epsilon) + decay_rate * weight
    )
    return (moment_one, moment_two, update)


def member_table(matrix_of):
    return (matrix_of[:, None] == jnp.arange(matrices, dtype=jnp.int32)[None, :]).astype(
        jnp.float32
    )


def local(gradients, weights, first_moment, second_moment, owner_list, norm_grads, norm_state):
    narrow = lax.axis_size("mp")
    replicas = lax.axis_size("dp")
    block_count = weights.shape[0]
    per_owner = block_count // replicas
    matrix_of = block_matrix(block_count, narrow)
    owner_order = jnp.argsort(owner_list[0], stable=True)
    local_grads = gradients[0]
    gradient = lax.psum_scatter(
        local_grads[owner_order].astype(jnp.float32), "dp", scatter_dimension=0, tiled=True
    )
    norm_sum = lax.psum(norm_grads[0].astype(jnp.float32), "dp")
    owned_rows = lax.dynamic_slice_in_dim(owner_order, lax.axis_index("dp") * per_owner, per_owner)
    weight_own = weights[owned_rows]
    member = member_table(matrix_of[owned_rows])
    moment_one, moment_two, update = adam_step(
        gradient, first_moment[0], second_moment[0], weight_own
    )
    position_of = jnp.argsort(owner_order)
    squares = jnp.stack(
        [jnp.sum(weight_own * weight_own, axis=1), jnp.sum(update * update, axis=1)]
    )
    totals = lax.psum(jnp.dot(squares, member, precision=lax.Precision.HIGHEST), ("dp", "mp"))
    weight_sq = totals[0]
    update_sq = totals[1]
    ratios = jnp.sqrt(weight_sq) / (jnp.sqrt(update_sq) + epsilon)
    row_rates = jnp.dot(member, ratios, precision=lax.Precision.HIGHEST)
    fresh_rows = weight_own - learning * row_rates[:, None] * update
    new_weights = lax.all_gather(fresh_rows, "dp", axis=0, tiled=True)[position_of]
    gain_rows = norm_state[0]
    norm_one, norm_two, norm_update = adam_step(norm_sum, norm_state[1], norm_state[2], gain_rows)
    norm_ratio = jnp.sqrt(jnp.sum(gain_rows * gain_rows, axis=1)) / (
        jnp.sqrt(jnp.sum(norm_update * norm_update, axis=1)) + epsilon
    )
    new_gains = gain_rows - learning * norm_ratio[:, None] * norm_update
    new_state = jnp.stack([new_gains, norm_one, norm_two])
    trust_ratios = jnp.concatenate([ratios, norm_ratio])
    return (new_weights, moment_one[None], moment_two[None], new_state, trust_ratios)


def solution(mesh):
    in_specs = (
        P("dp", "mp", None),
        P("mp", None),
        P("mp", "dp", None),
        P("mp", "dp", None),
        P("mp", None),
        P("dp", None, None),
        P(),
    )
    out_specs = (P("mp", None), P("mp", "dp", None), P("mp", "dp", None), P(), P())
    return jax.shard_map(local, mesh=mesh, in_specs=in_specs, out_specs=out_specs, check_vma=False)
```

profile of v0, /device:TPU:0, one launch (start us, length us, event | category | flops | bytes accessed | tf_op | source)
XLA Modules:
  0.0 389.2 jit_solution(3976146532717158012)
XLA Ops:
  7.2 0.0 reduce-scatter.2.cloned.1.call-start
  7.2 12.0 %sort.34 = (s32[17408]{0:T(1024)}, s32[17408]{0:T(1024)S(1)}) sort(s32[17408]{0:T(1024)} %bitcast.60, s32[17408]{0:T(1024)S(1)} %iota.15), dimensions={0}, to_apply=%region_0.0 | sort | flops 261120 | bytes 278528 | tf_op jit(solution)/shard_map/jit(argsort)/sort | solution.py:62
  19.3 61.4 %gather_fusion.2 = bf16[17408,128]{1,0:T(8,128)(2,1)} fusion(bf16[17408,128]{1,0:T(8,128)(2,1)} %bitcast.59, s32[17408]{0:T(1024)S(1)} %fusion.6), kind=kCustom, calls=%fused_computation.2 | custom fusion | bytes 8982528 | tf_op jit(solution)/shard_map/gather | solution.py:65
  80.7 5.9 %convert_element_type.26 = f32[17408,128]{1,0:T(8,128)} convert(bf16[17408,128]{1,0:T(8,128)(2,1)} %gather_fusion.2) | non-fusion elementwise | flops 2228224 | bytes 13369344 | tf_op jit(solution)/shard_map/convert_element_type | solution.py:65
  86.6 0.0 reduce-scatter.2.cloned.1.call-update
  86.6 0.0 copy-start
  86.6 0.0 copy-start.1
  86.7 0.0 all-gather.2.cloned.1.call-start
  86.7 0.1 compare_select_fusion.2
  86.8 0.0 copy-start.3
  86.8 0.0 copy-start.2
  86.8 6.0 %gather_fusion = f32[1088,128]{1,0:T(8,128)S(1)} fusion(f32[17408,128]{1,0:T(8,128)} %param.8, s32[2048]{0:T(1024)S(1)} %pad_clamp_fusion), kind=kCustom, calls=%fused_computation | custom fusion | bytes 1118464 | tf_op jit(solution)/shard_map/gather | solution.py:69
  92.9 6.2 %gather_fusion.1 = s32[1088]{0:T(1024)S(1)} fusion(s32[17408]{0:T(1024)S(1)} %convert_add_fusion, s32[2048]{0:T(1024)S(1)} %pad_clamp_fusion), kind=kCustom, calls=%fused_computation.1 | custom fusion | bytes 13056 | tf_op jit(solution)/shard_map/gather | solution.py:70
  99.1 98.2 %reduce-scatter.2.cloned.1.call-done = f32[1088,128]{1,0:T(8,128)} async-done(((f32[17408,128]{1,0:T(8,128)}), f32[1088,128]{1,0:T(8,128)}) %reduce-scatter.2.cloned.1.call-update) | async-done | bytes 557072 | tf_op jit(solution)/shard_map/reduce_scatter | solution.py:64
  197.3 0.0 copy-done
  197.3 0.0 copy-done.1
  197.3 2.4 multiply_reduce_fusion
  199.7 0.4 fusion.1
  200.1 40.5 %psum.14 = f32[2,5]{1,0:T(2,128)S(1)} all-reduce(f32[2,5]{1,0:T(2,128)S(1)} %fusion.1), channel_id=1, replica_groups=mesh['dp'=16,'mp'=2] {'dp','mp'}, use_global_device_ids=true, to_apply=%region_4.5 | all-reduce | flops 10 | bytes 80 | tf_op jit(solution)/shard_map/psum | solution.py:78
  240.6 0.5 convolution_reduce_fusion
  241.1 1.0 multiply_subtract_fusion
  242.1 0.0 all-gather.2.cloned.1.call-update
  242.1 11.3 %sort.35 = (s32[17408]{0:T(1024)}, s32[17408]{0:T(1024)S(1)}) sort(s32[17408]{0:T(1024)S(1)} %get-tuple-element.7, s32[17408]{0:T(1024)S(1)} %iota.17), dimensions={0}, to_apply=%region_5.6 | sort | flops 261120 | bytes 278528 | tf_op jit(solution)/shard_map/jit(argsort)/sort | solution.py:74
  253.4 0.0 copy-done.3
  253.5 32.8 %psum.15 = f32[2,1024]{1,0:T(2,128)S(1)} all-reduce(f32[2,1024]{1,0:T(2,128)S(1)} %bitcast_convert_fusion), channel_id=1, replica_groups=mesh['dp'=16,'mp'=2] {'dp'}, use_global_device_ids=true, to_apply=%region_7.8 | all-reduce | flops 2048 | bytes 16384 | tf_op jit(solution)/shard_map/psum | solution.py:67
  286.3 0.0 copy-done.2
  286.3 0.2 multiply_reduce_fusion.2
  286.5 0.1 fusion.14
  286.5 0.6 pad_maximum_fusion
  287.2 0.6 pad_maximum_fusion.1
  287.8 32.6 %all-gather.2.cloned.1.call-done = f32[17408,128]{1,0:T(8,128)} async-done(((f32[1088,128]{1,0:T(8,128)}), f32[17408,128]{1,0:T(8,128)}) %all-gather.2.cloned.1.call-update) | async-done | bytes 8912912 | tf_op jit(solution)/shard_map/all_gather | solution.py:84
  320.4 62.0 %gather_fusion.3 = f32[17408,128]{1,0:T(8,128)} fusion(f32[17408,128]{1,0:T(8,128)} %all-gather.2.cloned.1.call-done, s32[17408]{0:T(1024)S(1)} %fusion.7), kind=kCustom, calls=%fused_computation.3 | custom fusion | bytes 17895424 | tf_op jit(solution)/shard_map/gather | solution.py:84
  (12 shorter events, 0.1 us)
Async XLA Ops:
  7.2 190.1 %reduce-scatter.2.cloned.1.call-start = ((), (), s32[]{:S(2)}) async-start(), calls=%async_computation.1 | async-start | bytes 9469952 | tf_op jit(solution)/shard_map/reduce_scatter | solution.py:64
  86.6 110.6 %copy-start = (f32[1,1088,128]{2,1,0:T(8,128)S(1)}, f32[1,1088,128]{2,1,0:T(8,128)}, u32[]{:S(2)}) copy-start(f32[1,1088,128]{2,1,0:T(8,128)} %param.10) | copy-start | bytes 1671172
  86.6 110.6 %copy-start.1 = (f32[1,1088,128]{2,1,0:T(8,128)S(1)}, f32[1,1088,128]{2,1,0:T(8,128)}, u32[]{:S(2)}) copy-start(f32[1,1088,128]{2,1,0:T(8,128)} %param.9) | copy-start | bytes 1671172
  86.7 233.7 %all-gather.2.cloned.1.call-start = ((), (), s32[]{:S(2)}) async-start(), calls=%async_computation.2 | async-start | bytes 9469952 | tf_op jit(solution)/shard_map/all_gather | solution.py:84
  86.8 166.6 %copy-start.3 = (bf16[1,2,1024]{2,1,0:T(2,128)(2,1)S(1)}, bf16[1,2,1024]{2,1,0:T(2,128)(2,1)}, u32[]{:S(2)}) copy-start(bf16[1,2,1024]{2,1,0:T(2,128)(2,1)} %param.12) | copy-start | bytes 12292
  86.8 199.4 %copy-start.2 = (f32[3,2,1024]{2,1,0:T(2,128)S(1)}, f32[3,2,1024]{2,1,0:T(2,128)}, u32[]{:S(2)}) copy-start(f32[3,2,1024]{2,1,0:T(2,128)} %param.13) | copy-start | bytes 73732
Sparse Core Ops, SparseCore 0:
  86.8 110.4 reduce-scatter.1
  242.3 78.1 all-gather.1
where the time goes:
time: 390 us; the launch traced here: 389 us
  local copies, waits for them, and re-layouts  136 us (35%)
  waiting for transfers between devices  131 us (34%)
  blocking collectives  73.3 us (19%)
  other arithmetic  34.4 us (9%)
  between operations  14.2 us (4%)
    reduce_scatter x1, waiting for transfers between devices, local(): lax.psum_scatter(local_grads[owner_order].astype(jnp.float32), 'dp', scat...  98.2 us
    gather x1, local copies, waits for them, and re-layouts, local(): lax.all_gather(fresh_rows, 'dp', axis=0, tiled=True)[position_of]  62 us
    gather x1, local copies, waits for them, and re-layouts, local(): local_grads[owner_order].astype(jnp.float32)  61.4 us
    psum x1, blocking collectives, local(): lax.psum(jnp.dot(squares, member, precision=lax.Precision.HIGHEST), ('dp'...  40.5 us
    psum x1, blocking collectives, local(): norm_sum = lax.psum(norm_grads[0].astype(jnp.float32), 'dp')  32.8 us
    all_gather x1, waiting for transfers between devices, local(): lax.all_gather(fresh_rows, 'dp', axis=0, tiled=True)[position_of]  32.6 us
    sort x1, other arithmetic, local(): owner_order = jnp.argsort(owner_list[0], stable=True)  12 us
    sort x1, other arithmetic, local(): position_of = jnp.argsort(owner_order)  11.3 us
  transfers between devices with their start and end apart: 2, of which 2 were waited for; matrix products, arithmetic and copies ran while one was open for 6% of the time, Pallas kernels for 0%

commit v1 on v0

v1 whole, which is shorter than its diff:
```python
import functools

import jax
import jax.numpy as jnp
from jax import lax
from jax.experimental import pallas as pl
from jax.experimental.pallas import tpu as pltpu
from jax.sharding import PartitionSpec as P

D = 1024
NTAB = 8
NKEYS = 256
KDIM = 128
LANE = 128
VROW_DEV = 512

beta_one = 0.9
beta_two = 0.99
bias_one = 1.0 - 0.9**4
bias_two = 1.0 - 0.99**4
epsilon = 1e-06
learning = 0.02
decay_rate = 0.01
matrices = 5
MIB = 1 << 20


def matrix_bounds(narrow):
    query_blocks = D * D // (LANE * narrow)
    key_blocks = NTAB * NKEYS * KDIM // (LANE * narrow)
    value_blocks = VROW_DEV * D // LANE
    return (
        query_blocks,
        query_blocks + key_blocks,
        query_blocks + key_blocks + value_blocks,
        2 * query_blocks + key_blocks + value_blocks,
    )


class Plan:
    def __init__(self, replicas, narrow, blocks):
        self.replicas, self.narrow, self.blocks = replicas, narrow, blocks
        chips = replicas // 2
        self.nz = 4 if chips % 4 == 0 else chips
        self.nx = chips // self.nz
        self.slots = chips
        self.own = blocks // replicas
        self.rows_a = int(self.own * 0.6 / 8 + 0.5) * 8
        self.rows_b = self.own - self.rows_a
        self.half = self.slots * self.own
        self.lists = -(-blocks // (8 * LANE)) * 8
        self.bounds = matrix_bounds(narrow)
        self.size_b = self.nx * self.rows_b
        self.size_a = self.nz * self.rows_a

    def index(self, z, x, c):
        return (z * self.nx + x) * 2 + c

    def send(self, value, axis, pairs):
        every = []
        for z in range(self.nz):
            for x in range(self.nx):
                for c in range(2):
                    here = {"z": z, "x": x, "c": c}
                    for source, target in pairs:
                        if here[axis] == source:
                            there = dict(here)
                            there[axis] = target
                            every.append((self.index(z, x, c), self.index(**there)))
        return lax.ppermute(value, "dp", every)

    def swap(self, value):
        return self.send(value, "c", [(0, 1), (1, 0)])


def line_reduce(plan, axis, count, blocks):
    if count == 1:
        return [blocks[0]]
    if count == 2:
        return [blocks[0], plan.send(blocks[1], axis, [(0, 1), (1, 0)])]
    up, down = blocks[count - 1], blocks[1]
    for step in range(1, count):
        from_low = plan.send(up, axis, [(i, i + 1) for i in range(count - 1) if i <= step - 1])
        from_high = plan.send(down, axis, [(i, i - 1) for i in range(1, count) if i >= count - step])
        if step < count - 1:
            up = blocks[count - 1 - step] + from_low
            down = blocks[step + 1] + from_high
    return [blocks[0], from_low, from_high]


def line_gather(plan, axis, count, value):
    if count == 1:
        return [value]
    if count == 2:
        return [value, plan.send(value, axis, [(0, 1), (1, 0)])]
    low, high = [value], [value]
    for step in range(1, count):
        low.append(plan.send(low[-1], axis, [(i, i + 1) for i in range(count - 1) if i >= step - 1]))
        high.append(plan.send(high[-1], axis, [(i, i - 1) for i in range(1, count) if i <= count - step]))
    return [value] + [high[r] + low[count - r] for r in range(1, count)]


def place_kernel(plan, place_ref, owner_ref, grads_ref, *refs):
    count_b, count_a = plan.nz, plan.nx
    out_refs, refs = refs[: 1 + count_b + count_a], refs[1 + count_b + count_a :]
    position_ref, raw, moved, position, sem_in, sem_position, sem_out = refs
    fetch = pltpu.make_async_copy(grads_ref, raw, sem_in)
    fetch.start()
    lists = plan.lists
    owners = owner_ref[...]
    my_z, my_x, my_c = place_ref[0], place_ref[1], place_ref[2]
    lane_in = lax.broadcasted_iota(jnp.int32, (LANE, LANE), 0)
    lane_out = lax.broadcasted_iota(jnp.int32, (LANE, LANE), 1)
    before = (lane_in < lane_out).astype(jnp.bfloat16)
    every = jnp.ones((LANE, LANE), jnp.bfloat16)
    row_out = lax.broadcasted_iota(jnp.int32, (lists, lists), 0)
    row_in = lax.broadcasted_iota(jnp.int32, (lists, lists), 1)
    above = (row_in < row_out).astype(jnp.bfloat16)
    result = jnp.zeros((lists, LANE), jnp.int32)
    for z in range(plan.nz):
        for x in range(plan.nx):
            for c in range(2):
                mine = owners == plan.index(z, x, c)
                flags = mine.astype(jnp.float32).astype(jnp.bfloat16)
                inner = jnp.dot(flags, before, preferred_element_type=jnp.float32)
                totals = jnp.dot(flags, every, preferred_element_type=jnp.float32)
                outer = jnp.dot(above, totals.astype(jnp.bfloat16), preferred_element_type=jnp.float32)
                rank = (inner + outer).astype(jnp.int32)
                far_z = lax.rem(z - my_z + plan.nz, plan.nz)
                far_x = lax.rem(x - my_x + plan.nx, plan.nx)
                start = jnp.where(my_c == c, plan.half, 0)
                start_b = start + (far_z * plan.nx + far_x) * plan.rows_b - plan.rows_a
                start_a = start + plan.slots * plan.rows_b + (far_x * plan.nz + far_z) * plan.rows_a
                spot = rank + jnp.where(rank < plan.rows_a, start_a, start_b)
                result = jnp.where(mine, spot, result)
    position_ref[...] = result
    to_scalar = pltpu.make_async_copy(position_ref, position, sem_position)
    to_scalar.start()
    to_scalar.wait()
    fetch.wait()

    @pl.loop(0, plan.blocks // 64)
    def _(step):
        base = step * 64
        line = step // 2
        column = (step % 2) * 64
        for part in range(4):
            rows = raw[pl.ds(pl.multiple_of(base + part * 16, 16), 16), :].astype(jnp.float32)
            for u in range(16):
                moved[pl.ds(position[line, column + part * 16 + u], 1), :] = rows[u : u + 1, :]

    copies = []
    starts = [0] + [plan.half + i * plan.size_b for i in range(count_b)]
    starts += [plan.half + plan.slots * plan.rows_b + i * plan.size_a for i in range(count_a)]
    for i, (start, out) in enumerate(zip(starts, out_refs)):
        copies.append(pltpu.make_async_copy(moved.at[pl.ds(start, out.shape[0])], out, sem_out.at[i]))
    for copy in copies:
        copy.start()
    for copy in copies:
        copy.wait()


def place(plan, my_place, owners, grads):
    shapes = [(plan.half, LANE)] + [(plan.size_b, LANE)] * plan.nz + [(plan.size_a, LANE)] * plan.nx
    outs = pl.pallas_call(
        functools.partial(place_kernel, plan),
        out_shape=[jax.ShapeDtypeStruct(s, jnp.float32) for s in shapes]
        + [jax.ShapeDtypeStruct((plan.lists, LANE), jnp.int32)],
        in_specs=[
            pl.BlockSpec(memory_space=pltpu.SMEM),
            pl.BlockSpec(memory_space=pltpu.VMEM),
            pl.BlockSpec(memory_space=pl.ANY),
        ],
        out_specs=[pl.BlockSpec(memory_space=pl.ANY)] * len(shapes) + [pl.BlockSpec(memory_space=pltpu.VMEM)],
        scratch_shapes=[
            pltpu.VMEM((plan.blocks, LANE), jnp.bfloat16),
            pltpu.VMEM((plan.blocks, LANE), jnp.float32),
            pltpu.SMEM((plan.lists, LANE), jnp.int32),
            pltpu.SemaphoreType.DMA,
            pltpu.SemaphoreType.DMA,
            pltpu.SemaphoreType.DMA((len(shapes),)),
        ],
        compiler_params=pltpu.CompilerParams(vmem_limit_bytes=40 * MIB),
        name="place_gradients",
    )(my_place, owners, grads)
    sibling, blocks, position = outs[0], outs[1:-1], outs[-1]
    return sibling, blocks[: plan.nz], blocks[plan.nz :], position


def owned_kernel(plan, position_ref, weights_ref, owned_ref, natural_ref, held, listed, order, sem_in, sem_order):
    fetch = pltpu.make_async_copy(weights_ref, held, sem_in)
    fetch.start()
    high_rows = listed.shape[0]
    start_b = plan.half
    start_a = plan.half + plan.slots * plan.rows_b
    sub_high = lax.broadcasted_iota(jnp.int32, (high_rows, LANE), 0)
    lanes = lax.broadcasted_iota(jnp.int32, (high_rows, LANE), 1).astype(jnp.float32)
    sub_low = lax.broadcasted_iota(jnp.int32, (LANE, LANE), 0)
    zero = jnp.zeros((high_rows, LANE), jnp.float32)

    def add(line, sums):
        spot = position_ref[pl.ds(line, 1), :]
        valid = line * LANE + lax.broadcasted_iota(jnp.int32, (1, LANE), 1) < plan.blocks
        in_a = (spot >= start_a) & (spot < start_a + plan.rows_a) & valid
        in_b = (spot >= start_b) & (spot < start_b + plan.rows_b) & valid
        rank = jnp.where(in_a, spot - start_a, jnp.where(in_b, spot - start_b + plan.rows_a, -1))
        high = rank >> 7
        low = rank & 127
        at_high = (sub_high == high).astype(jnp.float32)
        at_low = (sub_low == low).astype(jnp.float32).astype(jnp.bfloat16)
        left = jnp.concatenate([at_high, at_high * lanes], 0).astype(jnp.bfloat16)
        hits = lax.dot_general(left, at_low, (((1,), (1,)), ((), ())), preferred_element_type=jnp.float32)
        return (
            sums[0] + hits[:high_rows] * (line * LANE).astype(jnp.float32),
            sums[1] + hits[high_rows:],
        )

    sums = lax.fori_loop(0, plan.lists, add, (zero, zero), unroll=2)
    listed[...] = (sums[0] + sums[1]).astype(jnp.int32)
    to_scalar = pltpu.make_async_copy(listed, order, sem_order)
    to_scalar.start()
    to_scalar.wait()
    fetch.wait()

    @pl.loop(0, plan.own // 8)
    def _(step):
        base = pl.multiple_of(step * 8, 8)
        line = base // LANE
        column = base % LANE
        for u in range(8):
            block = order[line, column + u]
            owned_ref[pl.ds(base + u, 1), :] = held[pl.ds(block, 1), :]
            natural_ref[pl.ds(base + u, 1), :] = jnp.full((1, LANE), block, jnp.int32)


def owned(plan, position, weights):
    high_rows = -(-plan.own // (8 * LANE)) * 8
    return pl.pallas_call(
        functools.partial(owned_kernel, plan),
        out_shape=[
            jax.ShapeDtypeStruct((plan.own, LANE), jnp.float32),
            jax.ShapeDtypeStruct((plan.own, LANE), jnp.int32),
        ],
        in_specs=[pl.BlockSpec(memory_space=pltpu.VMEM), pl.BlockSpec(memory_space=pl.ANY)],
        out_specs=[pl.BlockSpec(memory_space=pltpu.VMEM)] * 2,
        scratch_shapes=[
            pltpu.VMEM((plan.blocks, LANE), jnp.float32),
            pltpu.VMEM((high_rows, LANE), jnp.int32),
            pltpu.SMEM((high_rows, LANE), jnp.int32),
            pltpu.SemaphoreType.DMA,
            pltpu.SemaphoreType.DMA,
        ],
        compiler_params=pltpu.CompilerParams(vmem_limit_bytes=24 * MIB),
        name="owned_weights",
    )(position, weights)


def update_kernel(plan, terms_a, terms_b, *refs):
    parts_a, parts_b, refs = refs[:terms_a], refs[terms_a : terms_a + terms_b], refs[terms_a + terms_b :]
    first_ref, second_ref, weight_ref, natural_ref = refs[:4]
    new_first_ref, new_second_ref, step_a_ref, step_b_ref, stats_ref = refs[4:]
    weight_sums = [jnp.zeros((8, LANE), jnp.float32)] * matrices
    step_sums = [jnp.zeros((8, LANE), jnp.float32)] * matrices
    for parts, start, rows, step_ref in (
        (parts_a, 0, plan.rows_a, step_a_ref),
        (parts_b, plan.rows_a, plan.rows_b, step_b_ref),
    ):
        gradient = parts[0][:rows, :]
        for part in parts[1:]:
            gradient = gradient + part[:rows, :]
        here = pl.ds(start, rows)
        moment_one = beta_one * first_ref[here, :] + (1.0 - beta_one) * gradient
        moment_two = beta_two * second_ref[here, :] + (1.0 - beta_two) * gradient * gradient
        new_first_ref[here, :] = moment_one
        new_second_ref[here, :] = moment_two
        step = moment_one / bias_one / (jnp.sqrt(moment_two / bias_two) + epsilon)
        step_ref[...] = step
        weight = weight_ref[here, :]
        direction = step + decay_rate * weight
        natural = natural_ref[here, :]
        limits = (0,) + plan.bounds + (plan.blocks,)
        weight_square = weight * weight
        direction_square = direction * direction
        for k in range(matrices):
            inside = (natural >= limits[k]) & (natural < limits[k + 1])
            for sums, squares in ((weight_sums, weight_square), (step_sums, direction_square)):
                kept = jnp.where(inside, squares, 0.0).reshape(rows // 8, 8, LANE)
                sums[k] = sums[k] + jnp.sum(kept, axis=0)
    for k in range(8):
        for base, sums in ((0, weight_sums), (8, step_sums)):
            row = jnp.sum(sums[k], axis=0, keepdims=True) if k < matrices else jnp.zeros((1, LANE), jnp.float32)
            stats_ref[base + k : base + k + 1, :] = row


def update(plan, parts_a, parts_b, first, second, weight, natural):
    vmem = pl.BlockSpec(memory_space=pltpu.VMEM)
    shapes = [(plan.own, LANE), (plan.own, LANE), (plan.rows_a, LANE), (plan.rows_b, LANE), (16, LANE)]
    return pl.pallas_call(
        functools.partial(update_kernel, plan, len(parts_a), len(parts_b)),
        out_shape=[jax.ShapeDtypeStruct(s, jnp.float32) for s in shapes],
        in_specs=[vmem] * (len(parts_a) + len(parts_b) + 4),
        out_specs=[vmem] * len(shapes),
        compiler_params=pltpu.CompilerParams(vmem_limit_bytes=32 * MIB),
        name="moments",
    )(*parts_a, *parts_b, first, second, weight, natural)


def finish_kernel(plan, tile, starts, position_ref, rates_ref, weights_ref, *refs):
    pieces, refs = refs[: len(starts)], refs[len(starts) :]
    out_ref, held, sems = refs
    now = pl.program_id(0)

    @pl.when(now == 0)
    def _():
        copies = [
            pltpu.make_async_copy(piece, held.at[pl.ds(start, piece.shape[0])], sems.at[i])
            for i, (piece, start) in enumerate(zip(pieces, starts))
        ]
        for copy in copies:
            copy.start()
        for copy in copies:
            copy.wait()

    matrix = jnp.int32(0)
    for bound in plan.bounds:
        matrix = matrix + (now * tile >= bound).astype(jnp.int32)
    rate = rates_ref[matrix]
    lines = tile // LANE

    @pl.loop(0, tile // 64)
    def _(step):
        line = now * lines + step // 2
        column = (step % 2) * 64
        for group in range(8):
            rows = [held[pl.ds(position_ref[line, column + group * 8 + u], 1), :] for u in range(8)]
            here = pl.ds(pl.multiple_of(step * 64 + group * 8, 8), 8)
            weight = weights_ref[here, :]
            direction = jnp.concatenate(rows, 0) + decay_rate * weight
            out_ref[here, :] = weight - rate * direction


def finish(plan, position, rates, weights, pieces, starts):
    tile = LANE
    while tile < 1024 and all(b % (2 * tile) == 0 for b in plan.bounds + (plan.blocks,)):
        tile *= 2
    smem = pl.BlockSpec(memory_space=pltpu.SMEM)
    return pl.pallas_call(
        functools.partial(finish_kernel, plan, tile, starts),
        grid=(plan.blocks // tile,),
        out_shape=jax.ShapeDtypeStruct((plan.blocks, LANE), jnp.float32),
        in_specs=[smem, smem, pl.BlockSpec((tile, LANE), lambda i: (i, 0))]
        + [pl.BlockSpec(memory_space=pl.ANY)] * len(pieces),
        out_specs=pl.BlockSpec((tile, LANE), lambda i: (i, 0)),
        scratch_shapes=[
            pltpu.VMEM((plan.blocks, LANE), jnp.float32),
            pltpu.SemaphoreType.DMA((len(pieces),)),
        ],
        compiler_params=pltpu.CompilerParams(vmem_limit_bytes=24 * MIB),
        name="new_weights",
    )(position, rates, weights, *pieces)


def adam_step(gradient, moment_one, moment_two, weight):
    moment_one = beta_one * moment_one + (1.0 - beta_one) * gradient
    moment_two = beta_two * moment_two + (1.0 - beta_two) * gradient * gradient
    step = moment_one / bias_one / (jnp.sqrt(moment_two / bias_two) + epsilon) + decay_rate * weight
    return (moment_one, moment_two, step)


def local(gradients, weights, first_moment, second_moment, owner_list, norm_grads, norm_state):
    plan = Plan(lax.axis_size("dp"), lax.axis_size("mp"), weights.shape[0])
    me = lax.axis_index("dp").astype(jnp.int32)
    my_place = jnp.stack([me // (2 * plan.nx), (me // 2) % plan.nx, me % 2]).astype(jnp.int32)
    owners = jnp.pad(owner_list[0], (0, plan.lists * LANE - plan.blocks), constant_values=-1)
    owners = owners.reshape(plan.lists, LANE)
    sibling, blocks_b, blocks_a, position = place(plan, my_place, owners, gradients[0])

    other = plan.swap(sibling)
    size_b, size_a = plan.size_b, plan.size_a
    after_b = plan.slots * plan.rows_b
    blocks_b = [b + other[i * size_b : (i + 1) * size_b] for i, b in enumerate(blocks_b)]
    blocks_a = [b + other[after_b + i * size_a : after_b + (i + 1) * size_a] for i, b in enumerate(blocks_a)]
    terms = line_reduce(plan, "x", plan.nx, blocks_a)
    summed_a = sum(terms[1:], terms[0])
    rows_a, rows_b = plan.rows_a, plan.rows_b
    parts_a = line_reduce(plan, "z", plan.nz, [summed_a[i * rows_a : (i + 1) * rows_a] for i in range(plan.nz)])
    terms = line_reduce(plan, "z", plan.nz, blocks_b)
    summed_b = sum(terms[1:], terms[0])
    parts_b = line_reduce(plan, "x", plan.nx, [summed_b[i * rows_b : (i + 1) * rows_b] for i in range(plan.nx)])

    weight_own, natural = owned(plan, position, weights)
    new_first, new_second, step_a, step_b, stats = update(
        plan, parts_a, parts_b, first_moment[0], second_moment[0], weight_own, natural
    )

    small = jnp.concatenate([stats, norm_grads[0].astype(jnp.float32).reshape(-1, LANE)])
    small = small + plan.swap(small)
    for axis, count in (("x", plan.nx), ("z", plan.nz)):
        hop = 1
        while hop < count:
            small = small + plan.send(small, axis, [(i, i ^ hop) for i in range(count)])
            hop *= 2
    stats, norm_sum = small[:16], small[16:].reshape(norm_grads.shape[1:])
    hop = 1
    while hop < plan.narrow:
        stats = stats + lax.ppermute(stats, "mp", [(i, i ^ hop) for i in range(plan.narrow)])
        hop *= 2
    squares = jnp.sum(stats, axis=1)
    ratios = jnp.sqrt(squares[:matrices]) / (jnp.sqrt(squares[8 : 8 + matrices]) + epsilon)

    near_a = jnp.concatenate(line_gather(plan, "z", plan.nz, step_a))
    pieces_a = line_gather(plan, "x", plan.nx, near_a)
    near_b = jnp.concatenate(line_gather(plan, "x", plan.nx, step_b))
    pieces_b = line_gather(plan, "z", plan.nz, near_b)
    mine = pieces_b + pieces_a
    pieces = [plan.swap(piece) for piece in mine] + mine
    offsets = [i * size_b for i in range(plan.nz)] + [after_b + i * size_a for i in range(plan.nx)]
    starts = offsets + [plan.half + offset for offset in offsets]
    new_weights = finish(plan, position, learning * ratios, weights, pieces, starts)

    gain_rows = norm_state[0]
    norm_one, norm_two, norm_update = adam_step(norm_sum, norm_state[1], norm_state[2], gain_rows)
    norm_ratio = jnp.sqrt(jnp.sum(gain_rows * gain_rows, axis=1)) / (
        jnp.sqrt(jnp.sum(norm_update * norm_update, axis=1)) + epsilon
    )
    new_gains = gain_rows - learning * norm_ratio[:, None] * norm_update
    new_state = jnp.stack([new_gains, norm_one, norm_two])
    trust_ratios = jnp.concatenate([ratios, norm_ratio])
    return (new_weights, new_first[None], new_second[None], new_state, trust_ratios)


def solution(mesh):
    in_specs = (
        P("dp", "mp", None),
        P("mp", None),
        P("mp", "dp", None),
        P("mp", "dp", None),
        P("mp", None),
        P("dp", None, None),
        P(),
    )
    out_specs = (P("mp", None), P("mp", "dp", None), P("mp", "dp", None), P(), P())
    return jax.shard_map(local, mesh=mesh, in_specs=in_specs, out_specs=out_specs, check_vma=False)
```

time: 390 us -> 322 us (0.83)
  local copies, waits for them, and re-layouts: 136 us -> 6.84 us
  Pallas kernels: 0 us -> 111 us
  starting transfers between devices: 0.08 us -> 83.2 us
  blocking collectives: 73.3 us -> 0 us
  other arithmetic: 34.4 us -> 6.36 us
  waiting for transfers between devices: 131 us -> 113 us
  between operations: 14.2 us -> 1.22 us
    gather x4 -> x0, local copies, waits for them, and re-layouts: 136 us -> none  [the longest x1 62 us: local(): lax.all_gather(fresh_rows, 'dp', axis=0, tiled=True)[position_of]]
    ppermute x0 -> x40, waiting for transfers between devices: none -> 113 us  [the longest x39 113 us: send(): return lax.ppermute(value, 'dp', every)]
    pallas_call x0 -> x4, Pallas kernels: none -> 111 us  [the longest x1 47 us: finish(): pl.pallas_call(functools.partial(finish_kernel, plan, tile, starts), grid...]
    reduce_scatter x1 -> x0, waiting for transfers between devices: 98.2 us -> none  [local(): lax.psum_scatter(local_grads[owner_order].astype(jnp.float32), 'dp', scat...]
    ppermute x0 -> x40, starting transfers between devices: none -> 83.2 us  [the longest x39 81.7 us: send(): return lax.ppermute(value, 'dp', every)]
    psum x2 -> x0, blocking collectives: 73.3 us -> none  [the longest x1 40.5 us: local(): lax.psum(jnp.dot(squares, member, precision=lax.Precision.HIGHEST), ('dp'...]
    all_gather x1 -> x0, waiting for transfers between devices: 32.6 us -> none  [local(): lax.all_gather(fresh_rows, 'dp', axis=0, tiled=True)[position_of]]
    sort x2 -> x0, other arithmetic: 23.3 us -> none  [the longest x1 12 us: local(): owner_order = jnp.argsort(owner_list[0], stable=True)]
  transfers between devices with their start and end apart: 2 -> 40, of which waited for: 2 -> 19; matrix products, arithmetic and copies ran while one was open for 6% -> 2% of each run, Pallas kernels for 0% -> 5%
where the time goes in v1:
time: 322 us; the launch traced here: 321 us
  waiting for transfers between devices  113 us (35%)
  Pallas kernels  111 us (34%)
  starting transfers between devices  83.2 us (26%)
  local copies, waits for them, and re-layouts  6.84 us (2%)
  other arithmetic  6.36 us (2%)
    ppermute x39, waiting for transfers between devices, send(): return lax.ppermute(value, 'dp', every)  113 us
    ppermute x39, starting transfers between devices, send(): return lax.ppermute(value, 'dp', every)  81.7 us
    pallas_call x1, Pallas kernels, finish(): pl.pallas_call(functools.partial(finish_kernel, plan, tile, starts), grid...  47 us
    pallas_call x1, Pallas kernels, place(): pl.pallas_call(functools.partial(place_kernel, plan), out_shape=[jax.Shap...  46.8 us
    pallas_call x1, Pallas kernels, owned(): pl.pallas_call(functools.partial(owned_kernel, plan), out_shape=[jax.Shap...  15.9 us
    unnamed x22, local copies, waits for them, and re-layouts  6.74 us
  transfers between devices with their start and end apart: 40, of which 19 were waited for; matrix products, arithmetic and copies ran while one was open for 2% of the time, Pallas kernels for 5%

profile of v1, /device:TPU:0, one launch (start us, length us, event | category | flops | bytes accessed | tf_op | source)
XLA Modules:
  0.0 321.4 jit_solution(18180829151256017381)
XLA Ops:
  0.8 2.3 copy-done.1
  3.0 0.9 copy-done.4
  3.9 46.8 %place_gradients.1 = (f32[8704,128]{1,0:T(8,128)S(1)}, f32[864,128]{1,0:T(8,128)S(1)}, f32[864,128]{1,0:T(8,128)S(1)}, f32[864,128]{1,0:T(8,128)S(1)}, f32[864,1...) custom-call(s32[3]{0:T(128)S(1)} %pad_add_fusion.place_ref, ...), custom_call_target="tpu_custom_call" | custom-call | tf_op jit(solution)/shard_map/place_gradients/pallas_call | solution.py:165
  50.7 0.5 collective-permute-start
  51.2 7.2 %collective-permute-done = f32[8704,128]{1,0:T(8,128)S(1)} collective-permute-done((f32[8704,128]{1,0:T(8,128)S(1)}, f32[8704,128]{1,0:T(8,128)S(1)}, u32[]{:S(2)}, u32[]{:S(2)}) %collective-permute-start) | collective-permute-done | bytes 4456480 | tf_op jit(solution)/shard_map/ppermute | solution.py:70
  58.4 4.9 %collective-permute-start.8 = (f32[864,128]{1,0:T(8,128)S(1)}, f32[864,128]{1,0:T(8,128)S(1)}, u32[]{:S(2)}, u32[]{:S(2)}) collective-permute-start(f32[864,128]{1,0:T(8,128)S(1)} %slice_add_fusion.2), channel_id=1, source_target_pairs={{0,8},{2,10},{4,12},{6,14},{1,9},{3,11},{5,13},{7,15}} | collective-permute-start | bytes 1327112 | tf_op jit(solution)/shard_map/ppermute | solution.py:70
  63.5 1.6 collective-permute-start.1
  65.0 8.0 %collective-permute-done.8 = f32[864,128]{1,0:T(8,128)S(1)} collective-permute-done((f32[864,128]{1,0:T(8,128)S(1)}, f32[864,128]{1,0:T(8,128)S(1)}, u32[]{:S(2)}, u32[]{:S(2)}) %collective-permute-start.8) | collective-permute-done | bytes 442400 | tf_op jit(solution)/shard_map/ppermute | solution.py:70
  73.1 4.7 %collective-permute-start.9 = (f32[864,128]{1,0:T(8,128)S(1)}, f32[864,128]{1,0:T(8,128)S(1)}, u32[]{:S(2)}, u32[]{:S(2)}) collective-permute-start(f32[864,128]{1,0:T(8,128)S(1)} %fusion.4), channel_id=1, source_target_pairs={{0,8},{2,10},{4,12},{6,14},{8,16},{10,18},{12,20},{14,22},{1,9},{3... | collective-permute-start | bytes 1327112 | tf_op jit(solution)/shard_map/ppermute | solution.py:70
  77.8 8.9 %collective-permute-done.9 = f32[864,128]{1,0:T(8,128)S(1)} collective-permute-done((f32[864,128]{1,0:T(8,128)S(1)}, f32[864,128]{1,0:T(8,128)S(1)}, u32[]{:S(2)}, u32[]{:S(2)}) %collective-permute-start.9) | collective-permute-done | bytes 442400 | tf_op jit(solution)/shard_map/ppermute | solution.py:70
  86.7 0.7 collective-permute-start.11
  87.4 7.4 %collective-permute-done.1 = f32[2624,128]{1,0:T(8,128)S(1)} collective-permute-done((f32[2624,128]{1,0:T(8,128)S(1)}, f32[2624,128]{1,0:T(8,128)S(1)}, u32[]{:S(2)}, u32[]{:S(2)}) %collective-permute-start.1) | collective-permute-done | bytes 1343520 | tf_op jit(solution)/shard_map/ppermute | solution.py:70
  95.0 0.8 collective-permute-start.5
  95.9 0.8 collective-permute-start.12
  96.8 2.2 collective-permute-start.2
  99.0 1.4 collective-permute-start.10
  100.5 1.3 collective-permute-start.13
  101.8 0.7 collective-permute-start.6
  102.5 4.8 %collective-permute-done.2 = f32[656,128]{1,0:T(8,128)S(1)} collective-permute-done((f32[656,128]{1,0:T(8,128)S(1)}, f32[656,128]{1,0:T(8,128)S(1)}, u32[]{:S(2)}, u32[]{:S(2)}) %collective-permute-start.2) | collective-permute-done | bytes 335904 | tf_op jit(solution)/shard_map/ppermute | solution.py:70
  107.4 12.4 %collective-permute-start.3 = (f32[656,128]{1,0:T(8,128)S(1)}, f32[656,128]{1,0:T(8,128)S(1)}, u32[]{:S(2)}, u32[]{:S(2)}) collective-permute-start(f32[656,128]{1,0:T(8,128)S(1)} %slice_add_fusion.7), channel_id=1, source_target_pairs={{0,8},{2,10},{4,12},{6,14},{8,16},{10,18},{12,20},{14,22},{1,9},{3... | collective-permute-start | bytes 1007624 | tf_op jit(solution)/shard_map/ppermute | solution.py:70
  119.8 3.0 collective-permute-done.13
  122.8 1.6 collective-permute-done.3
  124.5 13.6 %collective-permute-start.4 = (f32[656,128]{1,0:T(8,128)S(1)}, f32[656,128]{1,0:T(8,128)S(1)}, u32[]{:S(2)}, u32[]{:S(2)}) collective-permute-start(f32[656,128]{1,0:T(8,128)S(1)} %get-tuple-element.45), channel_id=1, source_target_pairs={{0,8},{2,10},{4,12},{6,14},{8,16},{10,18},{12,20},{14,22},{16,24},... | collective-permute-start | bytes 1007624 | tf_op jit(solution)/shard_map/ppermute | solution.py:70
  138.1 1.3 collective-permute-start.7
  139.5 1.6 collective-permute-start.14
  141.0 15.9 %owned_weights.1 = (f32[1088,128]{1,0:T(8,128)S(1)}, s32[1088,128]{1,0:T(8,128)S(1)}) custom-call(s32[136,128]{1,0:T(8,128)S(1)} %get-tuple-element.20.position_ref, f32[17408,128]{1,0:T(8,128)S(1)} %bitcast.30), custom_call_target="tpu_custom_call" | custom-call | tf_op jit(solution)/shard_map/owned_weights/pallas_call | solution.py:238
  157.0 1.2 moments.1
  158.3 1.3 collective-permute-start.31
  159.6 5.2 %collective-permute-start.32 = (f32[656,128]{1,0:T(8,128)S(1)}, f32[656,128]{1,0:T(8,128)S(1)}, u32[]{:S(2)}, u32[]{:S(2)}) collective-permute-start(f32[656,128]{1,0:T(8,128)S(1)} %get-tuple-element.32), channel_id=1, source_target_pairs={{0,8},{2,10},{4,12},{6,14},{8,16},{10,18},{12,20},{14,22},{16,24},... | collective-permute-start | bytes 1007624 | tf_op jit(solution)/shard_map/ppermute | solution.py:70
  164.8 3.2 %collective-permute-done.31 = f32[656,128]{1,0:T(8,128)S(1)} collective-permute-done((f32[656,128]{1,0:T(8,128)S(1)}, f32[656,128]{1,0:T(8,128)S(1)}, u32[]{:S(2)}, u32[]{:S(2)}) %collective-permute-start.31) | collective-permute-done | bytes 335904 | tf_op jit(solution)/shard_map/ppermute | solution.py:70
  168.0 1.3 collective-permute-start.35
  169.4 0.7 collective-permute-start.33
  170.1 8.6 %collective-permute-done.35 = f32[656,128]{1,0:T(8,128)S(1)} collective-permute-done((f32[656,128]{1,0:T(8,128)S(1)}, f32[656,128]{1,0:T(8,128)S(1)}, u32[]{:S(2)}, u32[]{:S(2)}) %collective-permute-start.35) | collective-permute-done | bytes 335904 | tf_op jit(solution)/shard_map/ppermute | solution.py:70
  178.7 1.3 collective-permute-start.36
  180.0 0.7 collective-permute-start.34
  180.8 7.0 %collective-permute-done.36 = f32[656,128]{1,0:T(8,128)S(1)} collective-permute-done((f32[656,128]{1,0:T(8,128)S(1)}, f32[656,128]{1,0:T(8,128)S(1)}, u32[]{:S(2)}, u32[]{:S(2)}) %collective-permute-start.36) | collective-permute-done | bytes 335904 | tf_op jit(solution)/shard_map/ppermute | solution.py:70
  188.0 0.6 collective-permute-start.38
  188.6 1.5 collective-permute-start.20
  190.1 27.0 %collective-permute-done.20 = f32[432,128]{1,0:T(8,128)S(1)} collective-permute-done((f32[432,128]{1,0:T(8,128)S(1)}, f32[432,128]{1,0:T(8,128)S(1)}, u32[]{:S(2)}, u32[]{:S(2)}) %collective-permute-start.20) | collective-permute-done | bytes 221216 | tf_op jit(solution)/shard_map/ppermute | solution.py:70
  217.2 2.5 collective-permute-start.23
  219.7 1.3 collective-permute-start.22
  221.1 1.2 collective-permute-done.15
  222.3 0.5 collective-permute-start.16
  222.8 3.2 collective-permute-done.16
  226.0 6.0 %collective-permute-start.17 = (f32[32,128]{1,0:T(8,128)S(1)}, f32[32,128]{1,0:T(8,128)S(1)}, u32[]{:S(2)}, u32[]{:S(2)}) collective-permute-start(f32[32,128]{1,0:T(8,128)S(1)} %add.154), channel_id=1, source_target_pairs={{0,8},{2,10},{4,12},{6,14},{8,0},{10,2},{12,4},{14,6},{16,24},{18,... | collective-permute-start | bytes 49160 | tf_op jit(solution)/shard_map/ppermute | solution.py:70
  232.1 1.7 collective-permute-done.17
  233.8 4.4 %collective-permute-start.18 = (f32[32,128]{1,0:T(8,128)S(1)}, f32[32,128]{1,0:T(8,128)S(1)}, u32[]{:S(2)}, u32[]{:S(2)}) collective-permute-start(f32[32,128]{1,0:T(8,128)S(1)} %add.155), channel_id=1, source_target_pairs={{0,16},{2,18},{4,20},{6,22},{8,24},{10,26},{12,28},{14,30},{16,0},... | collective-permute-start | bytes 49160 | tf_op jit(solution)/shard_map/ppermute | solution.py:70
  238.2 1.7 collective-permute-done.18
  239.9 1.5 collective-permute-start.19
  241.4 1.4 collective-permute-start.24
  242.8 1.3 collective-permute-start.27
  244.2 0.5 collective-permute-start.39
  245.3 0.7 collective-permute-start.25
  246.0 11.2 %collective-permute-done.27 = f32[864,128]{1,0:T(8,128)} collective-permute-done((f32[864,128]{1,0:T(8,128)}, f32[864,128]{1,0:T(8,128)}, u32[]{:S(2)}, u32[]{:S(2)}) %collective-permute-start.27) | collective-permute-done | bytes 442400 | tf_op jit(solution)/shard_map/ppermute | solution.py:70
  257.2 1.3 collective-permute-start.29
  258.6 1.2 add.160.refs_8_
  259.9 1.1 add.159.refs_7_
  260.9 6.8 %collective-permute-done.29 = f32[864,128]{1,0:T(8,128)S(1)} collective-permute-done((f32[864,128]{1,0:T(8,128)}, f32[864,128]{1,0:T(8,128)S(1)}, u32[]{:S(2)}, u32[]{:S(2)}) %collective-permute-start.29) | collective-permute-done | bytes 442400 | tf_op jit(solution)/shard_map/ppermute | solution.py:70
  267.8 1.1 add.161.refs_9_
  268.9 0.6 collective-permute-start.30
  269.4 0.6 pad_maximum_fusion.2
  270.1 0.6 pad_maximum_fusion.1
  270.9 3.5 %copy-done = f32[17408,128]{1,0:T(8,128)S(1)} copy-done((f32[17408,128]{1,0:T(8,128)S(1)}, f32[17408,128]{1,0:T(8,128)}, u32[]{:S(2)}) %copy-start) | copy-done | bytes 8912920
  274.4 47.0 %new_weights.1 = f32[17408,128]{1,0:T(8,128)} custom-call(s32[136,128]{1,0:T(8,128)S(1)} %get-tuple-element.20.position_ref, f32[5]{0:T(128)S(1)} %get-tuple-element.40.rates_ref, f32[17408,128]{1,0:T(8,128)S(1)} %copy-done, f32[864,128]{1,0:T(8,128)S(1)} %collective-permute-done.21.refs_0_, f32[864,128]{1,0:T(8,128)S(1)} %collective-permute-done.26.refs_1_, ...), custom_call_target="tpu_custom_call" | custom-call | tf_op jit(solution)/shard_map/new_weights/pallas_call | solution.py:347
  (82 shorter events, 2.7 us)
Async XLA Ops:
  0.7 2.3 copy-start.1
  3.0 0.9 copy-start.4
  50.7 7.7 %collective-permute-start = (f32[8704,128]{1,0:T(8,128)S(1)}, f32[8704,128]{1,0:T(8,128)S(1)}, u32[]{:S(2)}, u32[]{:S(2)}) collective-permute-start(f32[8704,128]{1,0:T(8,128)S(1)} %get-tuple-element.22), channel_id=1, source_target_pairs={{0,2},{2,0},{4,6},{6,4},{8,10},{10,8},{12,14},{14,12},{16,18},{18,... | collective-permute-start | bytes 13369352 | tf_op jit(solution)/shard_map/ppermute | solution.py:70
  58.4 14.6 %collective-permute-start.8 = (f32[864,128]{1,0:T(8,128)S(1)}, f32[864,128]{1,0:T(8,128)S(1)}, u32[]{:S(2)}, u32[]{:S(2)}) collective-permute-start(f32[864,128]{1,0:T(8,128)S(1)} %slice_add_fusion.2), channel_id=1, source_target_pairs={{0,8},{2,10},{4,12},{6,14},{1,9},{3,11},{5,13},{7,15}} | collective-permute-start | bytes 1327112 | tf_op jit(solution)/shard_map/ppermute | solution.py:70
  63.5 31.3 %collective-permute-start.1 = (f32[2624,128]{1,0:T(8,128)S(1)}, f32[2624,128]{1,0:T(8,128)S(1)}, u32[]{:S(2)}, u32[]{:S(2)}) collective-permute-start(f32[2624,128]{1,0:T(8,128)S(1)} %slice_add_fusion), channel_id=1, source_target_pairs={{0,4},{2,6},{4,0},{6,2},{8,12},{10,14},{12,8},{14,10},{16,20},{18,... | collective-permute-start | bytes 4030472 | tf_op jit(solution)/shard_map/ppermute | solution.py:70
  73.0 68.0 %slice-start = ((s8[8912896]{0:T(1024)(128)(4,1)}), s8[4194304]{0:T(1024)(128)(4,1)S(1)}, s32[]{:S(2)}) async-start(s8[8912896]{0:T(1024)(128)(4,1)} %bitcast.29), calls=%async_computation | async-start | bytes 8388608
  73.1 13.5 %collective-permute-start.9 = (f32[864,128]{1,0:T(8,128)S(1)}, f32[864,128]{1,0:T(8,128)S(1)}, u32[]{:S(2)}, u32[]{:S(2)}) collective-permute-start(f32[864,128]{1,0:T(8,128)S(1)} %fusion.4), channel_id=1, source_target_pairs={{0,8},{2,10},{4,12},{6,14},{8,16},{10,18},{12,20},{14,22},{1,9},{3... | collective-permute-start | bytes 1327112 | tf_op jit(solution)/shard_map/ppermute | solution.py:70
  86.7 9.1 %collective-permute-start.11 = (f32[864,128]{1,0:T(8,128)S(1)}, f32[864,128]{1,0:T(8,128)S(1)}, u32[]{:S(2)}, u32[]{:S(2)}) collective-permute-start(f32[864,128]{1,0:T(8,128)S(1)} %get-tuple-element.43), channel_id=1, source_target_pairs={{24,16},{26,18},{28,20},{30,22},{25,17},{27,19},{29,21},{31,23}} | collective-permute-start | bytes 1327112 | tf_op jit(solution)/shard_map/ppermute | solution.py:70
  94.8 46.2 %slice-start.1 = ((s8[8912896]{0:T(1024)(128)(4,1)}), s8[4194304]{0:T(1024)(128)(4,1)S(1)}, s32[]{:S(2)}) async-start(s8[8912896]{0:T(1024)(128)(4,1)} %bitcast.29), calls=%async_computation.1 | async-start | bytes 8388608
  95.0 1.7 collective-permute-start.5
  95.9 4.6 %collective-permute-start.12 = (f32[864,128]{1,0:T(8,128)S(1)}, f32[864,128]{1,0:T(8,128)S(1)}, u32[]{:S(2)}, u32[]{:S(2)}) collective-permute-start(f32[864,128]{1,0:T(8,128)S(1)} %fusion.3), channel_id=1, source_target_pairs={{16,8},{18,10},{20,12},{22,14},{24,16},{26,18},{28,20},{30,22},{17... | collective-permute-start | bytes 1327112 | tf_op jit(solution)/shard_map/ppermute | solution.py:70
  96.8 10.5 %collective-permute-start.2 = (f32[656,128]{1,0:T(8,128)S(1)}, f32[656,128]{1,0:T(8,128)S(1)}, u32[]{:S(2)}, u32[]{:S(2)}) collective-permute-start(f32[656,128]{1,0:T(8,128)S(1)} %get-tuple-element.48), channel_id=1, source_target_pairs={{0,8},{2,10},{4,12},{6,14},{1,9},{3,11},{5,13},{7,15}} | collective-permute-start | bytes 1007624 | tf_op jit(solution)/shard_map/ppermute | solution.py:70
  99.0 42.0 %slice-start.2 = ((s8[8912896]{0:T(1024)(128)(4,1)}), s8[524288]{0:T(1024)(128)(4,1)S(1)}, s32[]{:S(2)}) async-start(s8[8912896]{0:T(1024)(128)(4,1)} %bitcast.29), calls=%async_computation.2 | async-start | bytes 1048576
  99.0 20.8 %collective-permute-start.10 = (f32[864,128]{1,0:T(8,128)S(1)}, f32[864,128]{1,0:T(8,128)S(1)}, u32[]{:S(2)}, u32[]{:S(2)}) collective-permute-start(f32[864,128]{1,0:T(8,128)S(1)} %get-tuple-element.42), channel_id=1, source_target_pairs={{0,8},{2,10},{4,12},{6,14},{8,16},{10,18},{12,20},{14,22},{16,24},... | collective-permute-start | bytes 1327112 | tf_op jit(solution)/shard_map/ppermute | solution.py:70
  100.5 22.2 %collective-permute-start.13 = (f32[864,128]{1,0:T(8,128)S(1)}, f32[864,128]{1,0:T(8,128)S(1)}, u32[]{:S(2)}, u32[]{:S(2)}) collective-permute-start(f32[864,128]{1,0:T(8,128)S(1)} %add.151), channel_id=1, source_target_pairs={{8,0},{10,2},{12,4},{14,6},{16,8},{18,10},{20,12},{22,14},{24,16},... | collective-permute-start | bytes 1327112 | tf_op jit(solution)/shard_map/ppermute | solution.py:70
  101.8 21.0 %collective-permute-start.6 = (f32[656,128]{1,0:T(8,128)S(1)}, f32[656,128]{1,0:T(8,128)S(1)}, u32[]{:S(2)}, u32[]{:S(2)}) collective-permute-start(f32[656,128]{1,0:T(8,128)S(1)} %get-tuple-element.47), channel_id=1, source_target_pairs={{16,8},{18,10},{20,12},{22,14},{24,16},{26,18},{28,20},{30,22},{17... | collective-permute-start | bytes 1007624 | tf_op jit(solution)/shard_map/ppermute | solution.py:70
  107.4 17.1 %collective-permute-start.3 = (f32[656,128]{1,0:T(8,128)S(1)}, f32[656,128]{1,0:T(8,128)S(1)}, u32[]{:S(2)}, u32[]{:S(2)}) collective-permute-start(f32[656,128]{1,0:T(8,128)S(1)} %slice_add_fusion.7), channel_id=1, source_target_pairs={{0,8},{2,10},{4,12},{6,14},{8,16},{10,18},{12,20},{14,22},{1,9},{3... | collective-permute-start | bytes 1007624 | tf_op jit(solution)/shard_map/ppermute | solution.py:70
  124.5 32.4 %collective-permute-start.4 = (f32[656,128]{1,0:T(8,128)S(1)}, f32[656,128]{1,0:T(8,128)S(1)}, u32[]{:S(2)}, u32[]{:S(2)}) collective-permute-start(f32[656,128]{1,0:T(8,128)S(1)} %get-tuple-element.45), channel_id=1, source_target_pairs={{0,8},{2,10},{4,12},{6,14},{8,16},{10,18},{12,20},{14,22},{16,24},... | collective-permute-start | bytes 1007624 | tf_op jit(solution)/shard_map/ppermute | solution.py:70
  138.1 18.9 %collective-permute-start.7 = (f32[656,128]{1,0:T(8,128)S(1)}, f32[656,128]{1,0:T(8,128)S(1)}, u32[]{:S(2)}, u32[]{:S(2)}) collective-permute-start(f32[656,128]{1,0:T(8,128)S(1)} %get-tuple-element.44), channel_id=1, source_target_pairs={{8,0},{10,2},{12,4},{14,6},{16,8},{18,10},{20,12},{22,14},{24,16},... | collective-permute-start | bytes 1007624 | tf_op jit(solution)/shard_map/ppermute | solution.py:70
  139.5 17.5 %collective-permute-start.14 = (f32[432,128]{1,0:T(8,128)S(1)}, f32[432,128]{1,0:T(8,128)S(1)}, u32[]{:S(2)}, u32[]{:S(2)}) collective-permute-start(f32[432,128]{1,0:T(8,128)S(1)} %get-tuple-element.49), channel_id=1, source_target_pairs={{0,4},{2,6},{4,0},{6,2},{8,12},{10,14},{12,8},{14,10},{16,20},{18,... | collective-permute-start | bytes 663560 | tf_op jit(solution)/shard_map/ppermute | solution.py:70
  141.0 16.0 %copy-start.2 = (f32[1,1088,128]{2,1,0:T(8,128)S(1)}, f32[1,1088,128]{2,1,0:T(8,128)}, u32[]{:S(2)}) copy-start(f32[1,1088,128]{2,1,0:T(8,128)} %param.9) | copy-start | bytes 1671172
  141.0 16.0 %copy-start.3 = (f32[1,1088,128]{2,1,0:T(8,128)S(1)}, f32[1,1088,128]{2,1,0:T(8,128)}, u32[]{:S(2)}) copy-start(f32[1,1088,128]{2,1,0:T(8,128)} %param.10) | copy-start | bytes 1671172
  158.3 9.7 %collective-permute-start.31 = (f32[656,128]{1,0:T(8,128)S(1)}, f32[656,128]{1,0:T(8,128)S(1)}, u32[]{:S(2)}, u32[]{:S(2)}) collective-permute-start(f32[656,128]{1,0:T(8,128)S(1)} %get-tuple-element.32), channel_id=1, source_target_pairs={{8,0},{10,2},{12,4},{14,6},{16,8},{18,10},{20,12},{22,14},{24,16},... | collective-permute-start | bytes 1007624 | tf_op jit(solution)/shard_map/ppermute | solution.py:70
  159.6 9.8 %collective-permute-start.32 = (f32[656,128]{1,0:T(8,128)S(1)}, f32[656,128]{1,0:T(8,128)S(1)}, u32[]{:S(2)}, u32[]{:S(2)}) collective-permute-start(f32[656,128]{1,0:T(8,128)S(1)} %get-tuple-element.32), channel_id=1, source_target_pairs={{0,8},{2,10},{4,12},{6,14},{8,16},{10,18},{12,20},{14,22},{16,24},... | collective-permute-start | bytes 1007624 | tf_op jit(solution)/shard_map/ppermute | solution.py:70
  168.0 10.7 %collective-permute-start.35 = (f32[656,128]{1,0:T(8,128)S(1)}, f32[656,128]{1,0:T(8,128)S(1)}, u32[]{:S(2)}, u32[]{:S(2)}) collective-permute-start(f32[656,128]{1,0:T(8,128)S(1)} %collective-permute-done.31), channel_id=1, source_target_pairs={{8,0},{10,2},{12,4},{14,6},{16,8},{18,10},{20,12},{22,14},{9,1},{1... | collective-permute-start | bytes 1007624 | tf_op jit(solution)/shard_map/ppermute | solution.py:70
  169.4 10.6 %collective-permute-start.33 = (f32[656,128]{1,0:T(8,128)S(1)}, f32[656,128]{1,0:T(8,128)S(1)}, u32[]{:S(2)}, u32[]{:S(2)}) collective-permute-start(f32[656,128]{1,0:T(8,128)S(1)} %collective-permute-done.32), channel_id=1, source_target_pairs={{8,16},{10,18},{12,20},{14,22},{16,24},{18,26},{20,28},{22,30},{9,... | collective-permute-start | bytes 1007624 | tf_op jit(solution)/shard_map/ppermute | solution.py:70
  178.7 9.0 %collective-permute-start.36 = (f32[656,128]{1,0:T(8,128)S(1)}, f32[656,128]{1,0:T(8,128)S(1)}, u32[]{:S(2)}, u32[]{:S(2)}) collective-permute-start(f32[656,128]{1,0:T(8,128)S(1)} %collective-permute-done.35), channel_id=1, source_target_pairs={{8,0},{10,2},{12,4},{14,6},{9,1},{11,3},{13,5},{15,7}} | collective-permute-start | bytes 1007624 | tf_op jit(solution)/shard_map/ppermute | solution.py:70
  180.0 7.8 %collective-permute-start.34 = (f32[656,128]{1,0:T(8,128)S(1)}, f32[656,128]{1,0:T(8,128)S(1)}, u32[]{:S(2)}, u32[]{:S(2)}) collective-permute-start(f32[656,128]{1,0:T(8,128)S(1)} %collective-permute-done.33), channel_id=1, source_target_pairs={{16,24},{18,26},{20,28},{22,30},{17,25},{19,27},{21,29},{23,31}} | collective-permute-start | bytes 1007624 | tf_op jit(solution)/shard_map/ppermute | solution.py:70
  187.9 33.1 %copy-start.6 = (bf16[1,2,1024]{2,1,0:T(2,128)(2,1)S(1)}, bf16[1,2,1024]{2,1,0:T(2,128)(2,1)}, u32[]{:S(2)}) copy-start(bf16[1,2,1024]{2,1,0:T(2,128)(2,1)} %param.12) | copy-start | bytes 12292
  187.9 56.8 %copy-start.5 = (f32[3,2,1024]{2,1,0:T(2,128)S(1)}, f32[3,2,1024]{2,1,0:T(2,128)}, u32[]{:S(2)}) copy-start(f32[3,2,1024]{2,1,0:T(2,128)} %param.13) | copy-start | bytes 73732
  188.0 56.2 %collective-permute-start.38 = (f32[2624,128]{1,0:T(8,128)S(1)}, f32[2624,128]{1,0:T(8,128)S(1)}, u32[]{:S(2)}, u32[]{:S(2)}) collective-permute-start(f32[2624,128]{1,0:T(8,128)S(1)} %pad_maximum_fusion.refs_10_), channel_id=1, source_target_pairs={{0,4},{2,6},{4,0},{6,2},{8,12},{10,14},{12,8},{14,10},{16,20},{18,... | collective-permute-start | bytes 4030472 | tf_op jit(solution)/shard_map/ppermute | solution.py:70
  188.6 28.6 %collective-permute-start.20 = (f32[432,128]{1,0:T(8,128)S(1)}, f32[432,128]{1,0:T(8,128)S(1)}, u32[]{:S(2)}, u32[]{:S(2)}) collective-permute-start(f32[432,128]{1,0:T(8,128)S(1)} %get-tuple-element.31), channel_id=1, source_target_pairs={{0,4},{2,6},{4,0},{6,2},{8,12},{10,14},{12,8},{14,10},{16,20},{18,... | collective-permute-start | bytes 663560 | tf_op jit(solution)/shard_map/ppermute | solution.py:70
  217.2 24.2 %collective-permute-start.23 = (f32[864,128]{1,0:T(8,128)S(1)}, f32[864,128]{1,0:T(8,128)}, u32[]{:S(2)}, u32[]{:S(2)}) collective-permute-start(f32[864,128]{1,0:T(8,128)S(1)} %constant_dynamic-update-slice_fusion.2.refs_6_), channel_id=1, source_target_pairs={{0,8},{2,10},{4,12},{6,14},{8,16},{10,18},{12,20},{14,22},{16,24},... | collective-permute-start | bytes 1327112 | tf_op jit(solution)/shard_map/ppermute | solution.py:70
  219.7 23.1 %collective-permute-start.22 = (f32[864,128]{1,0:T(8,128)S(1)}, f32[864,128]{1,0:T(8,128)}, u32[]{:S(2)}, u32[]{:S(2)}) collective-permute-start(f32[864,128]{1,0:T(8,128)S(1)} %constant_dynamic-update-slice_fusion.2.refs_6_), channel_id=1, source_target_pairs={{8,0},{10,2},{12,4},{14,6},{16,8},{18,10},{20,12},{22,14},{24,16},... | collective-permute-start | bytes 1327112 | tf_op jit(solution)/shard_map/ppermute | solution.py:70
  221.0 1.2 collective-permute-start.15
  222.3 3.7 %collective-permute-start.16 = (f32[32,128]{1,0:T(8,128)S(1)}, f32[32,128]{1,0:T(8,128)S(1)}, u32[]{:S(2)}, u32[]{:S(2)}) collective-permute-start(f32[32,128]{1,0:T(8,128)S(1)} %add.153), channel_id=1, source_target_pairs={{0,4},{2,6},{4,0},{6,2},{8,12},{10,14},{12,8},{14,10},{16,20},{18,... | collective-permute-start | bytes 49160 | tf_op jit(solution)/shard_map/ppermute | solution.py:70
  226.0 7.8 %collective-permute-start.17 = (f32[32,128]{1,0:T(8,128)S(1)}, f32[32,128]{1,0:T(8,128)S(1)}, u32[]{:S(2)}, u32[]{:S(2)}) collective-permute-start(f32[32,128]{1,0:T(8,128)S(1)} %add.154), channel_id=1, source_target_pairs={{0,8},{2,10},{4,12},{6,14},{8,0},{10,2},{12,4},{14,6},{16,24},{18,... | collective-permute-start | bytes 49160 | tf_op jit(solution)/shard_map/ppermute | solution.py:70
  233.8 6.1 %collective-permute-start.18 = (f32[32,128]{1,0:T(8,128)S(1)}, f32[32,128]{1,0:T(8,128)S(1)}, u32[]{:S(2)}, u32[]{:S(2)}) collective-permute-start(f32[32,128]{1,0:T(8,128)S(1)} %add.155), channel_id=1, source_target_pairs={{0,16},{2,18},{4,20},{6,22},{8,24},{10,26},{12,28},{14,30},{16,0},... | collective-permute-start | bytes 49160 | tf_op jit(solution)/shard_map/ppermute | solution.py:70
  239.9 4.9 %collective-permute-start.19 = (f32[16,128]{1,0:T(8,128)S(1)}, f32[16,128]{1,0:T(8,128)S(1)}, u32[]{:S(2)}, u32[]{:S(2)}) collective-permute-start(f32[16,128]{1,0:T(8,128)S(1)} %slice.88), channel_id=1, source_target_pairs={{0,1},{1,0},{2,3},{3,2},{4,5},{5,4},{6,7},{7,6},{8,9},{9,8},{10,11... | collective-permute-start | bytes 24584 | tf_op jit(solution)/shard_map/ppermute | solution.py:406
  241.4 3.9 %collective-permute-start.24 = (f32[864,128]{1,0:T(8,128)}, f32[864,128]{1,0:T(8,128)}, u32[]{:S(2)}, u32[]{:S(2)}) collective-permute-start(f32[864,128]{1,0:T(8,128)} %collective-permute-done.23), channel_id=1, source_target_pairs={{8,16},{10,18},{12,20},{14,22},{16,24},{18,26},{20,28},{22,30},{9,... | collective-permute-start | bytes 1327112 | tf_op jit(solution)/shard_map/ppermute | solution.py:70
  242.8 14.3 %collective-permute-start.27 = (f32[864,128]{1,0:T(8,128)}, f32[864,128]{1,0:T(8,128)}, u32[]{:S(2)}, u32[]{:S(2)}) collective-permute-start(f32[864,128]{1,0:T(8,128)} %collective-permute-done.22), channel_id=1, source_target_pairs={{8,0},{10,2},{12,4},{14,6},{16,8},{18,10},{20,12},{22,14},{9,1},{1... | collective-permute-start | bytes 1327112 | tf_op jit(solution)/shard_map/ppermute | solution.py:70
  244.1 26.7 %collective-permute-start.37 = (f32[2624,128]{1,0:T(8,128)S(1)}, f32[2624,128]{1,0:T(8,128)}, u32[]{:S(2)}, u32[]{:S(2)}) collective-permute-start(f32[2624,128]{1,0:T(8,128)S(1)} %pad_maximum_fusion.refs_10_), channel_id=1, source_target_pairs={{0,2},{2,0},{4,6},{6,4},{8,10},{10,8},{12,14},{14,12},{16,18},{18,... | collective-permute-start | bytes 4030472 | tf_op jit(solution)/shard_map/ppermute | solution.py:70
  244.2 26.6 %collective-permute-start.39 = (f32[2624,128]{1,0:T(8,128)S(1)}, f32[2624,128]{1,0:T(8,128)}, u32[]{:S(2)}, u32[]{:S(2)}) collective-permute-start(f32[2624,128]{1,0:T(8,128)S(1)} %collective-permute-done.38.refs_11_), channel_id=1, source_target_pairs={{0,2},{2,0},{4,6},{6,4},{8,10},{10,8},{12,14},{14,12},{16,18},{18,... | collective-permute-start | bytes 4030472 | tf_op jit(solution)/shard_map/ppermute | solution.py:70
  245.1 23.7 %collective-permute-start.21 = (f32[864,128]{1,0:T(8,128)S(1)}, f32[864,128]{1,0:T(8,128)S(1)}, u32[]{:S(2)}, u32[]{:S(2)}) collective-permute-start(f32[864,128]{1,0:T(8,128)S(1)} %constant_dynamic-update-slice_fusion.2.refs_6_), channel_id=1, source_target_pairs={{0,2},{2,0},{4,6},{6,4},{8,10},{10,8},{12,14},{14,12},{16,18},{18,... | collective-permute-start | bytes 1327112 | tf_op jit(solution)/shard_map/ppermute | solution.py:70
  245.3 14.5 %collective-permute-start.25 = (f32[864,128]{1,0:T(8,128)}, f32[864,128]{1,0:T(8,128)S(1)}, u32[]{:S(2)}, u32[]{:S(2)}) collective-permute-start(f32[864,128]{1,0:T(8,128)} %collective-permute-done.24), channel_id=1, source_target_pairs={{16,24},{18,26},{20,28},{22,30},{17,25},{19,27},{21,29},{23,31}} | collective-permute-start | bytes 1327112 | tf_op jit(solution)/shard_map/ppermute | solution.py:70
  257.2 10.6 %collective-permute-start.29 = (f32[864,128]{1,0:T(8,128)}, f32[864,128]{1,0:T(8,128)S(1)}, u32[]{:S(2)}, u32[]{:S(2)}) collective-permute-start(f32[864,128]{1,0:T(8,128)} %collective-permute-done.27), channel_id=1, source_target_pairs={{8,0},{10,2},{12,4},{14,6},{9,1},{11,3},{13,5},{15,7}} | collective-permute-start | bytes 1327112 | tf_op jit(solution)/shard_map/ppermute | solution.py:70
  259.8 10.9 %collective-permute-start.28 = (f32[864,128]{1,0:T(8,128)S(1)}, f32[864,128]{1,0:T(8,128)S(1)}, u32[]{:S(2)}, u32[]{:S(2)}) collective-permute-start(f32[864,128]{1,0:T(8,128)S(1)} %add.160.refs_8_), channel_id=1, source_target_pairs={{0,2},{2,0},{4,6},{6,4},{8,10},{10,8},{12,14},{14,12},{16,18},{18,... | collective-permute-start | bytes 1327112 | tf_op jit(solution)/shard_map/ppermute | solution.py:70
  267.8 2.9 collective-permute-start.26
  268.9 2.0 collective-permute-start.30
  270.9 3.5 %copy-start = (f32[17408,128]{1,0:T(8,128)S(1)}, f32[17408,128]{1,0:T(8,128)}, u32[]{:S(2)}) copy-start(f32[17408,128]{1,0:T(8,128)} %weights_ref.3) | copy-start | bytes 26738692

commit v2 on v1

--- a/solution.py
+++ b/solution.py
@@ -47,30 +47,35 @@
         self.own = blocks // replicas
         self.rows_a = int(self.own * 0.6 / 8 + 0.5) * 8
         self.rows_b = self.own - self.rows_a
-        self.half = self.slots * self.own
+        self.tail = 8
+        self.norm_rows = 2 * D // LANE
+        self.norm_each = -(-self.norm_rows // replicas)
+        self.block_b = self.rows_b + self.tail
+        self.after_b = self.slots * self.block_b
+        self.half = self.after_b + self.slots * self.rows_a
         self.lists = -(-blocks // (8 * LANE)) * 8
         self.bounds = matrix_bounds(narrow)
-        self.size_b = self.nx * self.rows_b
+        self.size_b = self.nx * self.block_b
         self.size_a = self.nz * self.rows_a
 
     def index(self, z, x, c):
         return (z * self.nx + x) * 2 + c
 
-    def send(self, value, axis, pairs):
+    def send(self, value, axis, pairs, keep=()):
         every = []
         for z in range(self.nz):
             for x in range(self.nx):
                 for c in range(2):
                     here = {"z": z, "x": x, "c": c}
                     for source, target in pairs:
-                        if here[axis] == source:
+                        if here[axis] == source and all(least <= here[a] <= most for a, least, most in keep):
                             there = dict(here)
                             there[axis] = target
                             every.append((self.index(z, x, c), self.index(**there)))
         return lax.ppermute(value, "dp", every)
 
-    def swap(self, value):
-        return self.send(value, "c", [(0, 1), (1, 0)])
+    def swap(self, value, keep=()):
+        return self.send(value, "c", [(0, 1), (1, 0)], keep)
 
 
 def line_reduce(plan, axis, count, blocks):
@@ -88,21 +93,27 @@
     return [blocks[0], from_low, from_high]
 
 
-def line_gather(plan, axis, count, value):
-    if count == 1:
-        return [value]
+def line_gather(plan, axis, count, value, keep=()):
+    found = [(value, 0, keep)]
     if count == 2:
-        return [value, plan.send(value, axis, [(0, 1), (1, 0)])]
-    low, high = [value], [value]
-    for step in range(1, count):
-        low.append(plan.send(low[-1], axis, [(i, i + 1) for i in range(count - 1) if i >= step - 1]))
-        high.append(plan.send(high[-1], axis, [(i, i - 1) for i in range(1, count) if i <= count - step]))
-    return [value] + [high[r] + low[count - r] for r in range(1, count)]
-
-
-def place_kernel(plan, place_ref, owner_ref, grads_ref, *refs):
+        found.append((plan.send(value, axis, [(0, 1), (1, 0)], keep), 1, keep))
+    elif count > 2:
+        low = high = value
+        for step in range(1, count):
+            low = plan.send(low, axis, [(i, i + 1) for i in range(count - 1) if i >= step - 1], keep)
+            high = plan.send(high, axis, [(i, i - 1) for i in range(1, count) if i <= count - step], keep)
+            found.append((low, count - step, keep + ((axis, step, count - 1),)))
+            found.append((high, step, keep + ((axis, 0, count - 1 - step),)))
+    return found
+
+
+def merged(found, count):
+    return [sum(value for value, source, _ in found[1:] if source == r) if r else found[0][0] for r in range(count)]
+
+
+def place_kernel(plan, place_ref, owner_ref, norm_ref, grads_ref, *refs):
     count_b, count_a = plan.nz, plan.nx
-    out_refs, refs = refs[: 1 + count_b + count_a], refs[1 + count_b + count_a :]
+    out_refs, refs = refs[: 2 + count_b + count_a], refs[2 + count_b + count_a :]
     position_ref, raw, moved, position, sem_in, sem_position, sem_out = refs
     fetch = pltpu.make_async_copy(grads_ref, raw, sem_in)
     fetch.start()
@@ -129,8 +140,15 @@
                 far_z = lax.rem(z - my_z + plan.nz, plan.nz)
                 far_x = lax.rem(x - my_x + plan.nx, plan.nx)
                 start = jnp.where(my_c == c, plan.half, 0)
-                start_b = start + (far_z * plan.nx + far_x) * plan.rows_b - plan.rows_a
-                start_a = start + plan.slots * plan.rows_b + (far_x * plan.nz + far_z) * plan.rows_a
+                start_b = start + (far_z * plan.nx + far_x) * plan.block_b - plan.rows_a
+                start_a = start + plan.after_b + (far_x * plan.nz + far_z) * plan.rows_a
+                first_norm = plan.index(z, x, c) * plan.norm_each
+                tail = [jnp.zeros((plan.tail, LANE), jnp.float32)]
+                for row in range(min(first_norm + plan.norm_each, plan.norm_rows) - 1, first_norm - 1, -1):
+                    part = norm_ref[row * LANE // D : row * LANE // D + 1, row * LANE % D : row * LANE % D + LANE]
+                    tail.insert(0, part.astype(jnp.float32))
+                tail = jnp.concatenate(tail, 0)[: plan.tail]
+                moved[pl.ds(pl.multiple_of(start_b + plan.own, 8), plan.tail), :] = tail
                 spot = rank + jnp.where(rank < plan.rows_a, start_a, start_b)
                 result = jnp.where(mine, spot, result)
     position_ref[...] = result
@@ -139,19 +157,16 @@
     to_scalar.wait()
     fetch.wait()
 
-    @pl.loop(0, plan.blocks // 64)
-    def _(step):
-        base = step * 64
-        line = step // 2
-        column = (step % 2) * 64
-        for part in range(4):
-            rows = raw[pl.ds(pl.multiple_of(base + part * 16, 16), 16), :].astype(jnp.float32)
+    @pl.loop(0, plan.blocks // LANE)
+    def _(line):
+        for part in range(0, LANE, 16):
+            rows = raw[pl.ds(pl.multiple_of(line * LANE + part, 16), 16), :].astype(jnp.float32)
             for u in range(16):
-                moved[pl.ds(position[line, column + part * 16 + u], 1), :] = rows[u : u + 1, :]
+                moved[pl.ds(position[line, part + u], 1), :] = rows[u : u + 1, :]
 
     copies = []
-    starts = [0] + [plan.half + i * plan.size_b for i in range(count_b)]
-    starts += [plan.half + plan.slots * plan.rows_b + i * plan.size_a for i in range(count_a)]
+    starts = [0, plan.after_b] + [plan.half + i * plan.size_b for i in range(count_b)]
+    starts += [plan.half + plan.after_b + i * plan.size_a for i in range(count_a)]
     for i, (start, out) in enumerate(zip(starts, out_refs)):
         copies.append(pltpu.make_async_copy(moved.at[pl.ds(start, out.shape[0])], out, sem_out.at[i]))
     for copy in copies:
@@ -160,8 +175,9 @@
         copy.wait()
 
 
-def place(plan, my_place, owners, grads):
-    shapes = [(plan.half, LANE)] + [(plan.size_b, LANE)] * plan.nz + [(plan.size_a, LANE)] * plan.nx
+def place(plan, my_place, owners, norm_grads, grads):
+    shapes = [(plan.after_b, LANE), (plan.half - plan.after_b, LANE)]
+    shapes += [(plan.size_b, LANE)] * plan.nz + [(plan.size_a, LANE)] * plan.nx
     outs = pl.pallas_call(
         functools.partial(place_kernel, plan),
         out_shape=[jax.ShapeDtypeStruct(s, jnp.float32) for s in shapes]
@@ -169,22 +185,23 @@
         in_specs=[
             pl.BlockSpec(memory_space=pltpu.SMEM),
             pl.BlockSpec(memory_space=pltpu.VMEM),
+            pl.BlockSpec(memory_space=pltpu.VMEM),
             pl.BlockSpec(memory_space=pl.ANY),
         ],
         out_specs=[pl.BlockSpec(memory_space=pl.ANY)] * len(shapes) + [pl.BlockSpec(memory_space=pltpu.VMEM)],
         scratch_shapes=[
             pltpu.VMEM((plan.blocks, LANE), jnp.bfloat16),
-            pltpu.VMEM((plan.blocks, LANE), jnp.float32),
+            pltpu.VMEM((2 * plan.half, LANE), jnp.float32),
             pltpu.SMEM((plan.lists, LANE), jnp.int32),
             pltpu.SemaphoreType.DMA,
             pltpu.SemaphoreType.DMA,
             pltpu.SemaphoreType.DMA((len(shapes),)),
         ],
-        compiler_params=pltpu.CompilerParams(vmem_limit_bytes=40 * MIB),
+        compiler_params=pltpu.CompilerParams(vmem_limit_bytes=58 * MIB),
         name="place_gradients",
-    )(my_place, owners, grads)
-    sibling, blocks, position = outs[0], outs[1:-1], outs[-1]
-    return sibling, blocks[: plan.nz], blocks[plan.nz :], position
+    )(my_place, owners, norm_grads, grads)
+    siblings, blocks, position = outs[:2], outs[2:-1], outs[-1]
+    return siblings, blocks[: plan.nz], blocks[plan.nz :], position
 
 
 def owned_kernel(plan, position_ref, weights_ref, owned_ref, natural_ref, held, listed, order, sem_in, sem_order):
@@ -192,7 +209,7 @@
     fetch.start()
     high_rows = listed.shape[0]
     start_b = plan.half
-    start_a = plan.half + plan.slots * plan.rows_b
+    start_a = plan.half + plan.after_b
     sub_high = lax.broadcasted_iota(jnp.int32, (high_rows, LANE), 0)
     lanes = lax.broadcasted_iota(jnp.int32, (high_rows, LANE), 1).astype(jnp.float32)
     sub_low = lax.broadcasted_iota(jnp.int32, (LANE, LANE), 0)
@@ -222,15 +239,19 @@
     to_scalar.wait()
     fetch.wait()
 
-    @pl.loop(0, plan.own // 8)
-    def _(step):
-        base = pl.multiple_of(step * 8, 8)
-        line = base // LANE
-        column = base % LANE
-        for u in range(8):
-            block = order[line, column + u]
-            owned_ref[pl.ds(base + u, 1), :] = held[pl.ds(block, 1), :]
-            natural_ref[pl.ds(base + u, 1), :] = jnp.full((1, LANE), block, jnp.int32)
+    def pick(line, count):
+        for u in range(count):
+            block = order[line, u]
+            row = pl.ds(line * LANE + u, 1)
+            owned_ref[row, :] = held[pl.ds(block, 1), :]
+            natural_ref[row, :] = jnp.full((1, LANE), block, jnp.int32)
+
+    @pl.loop(0, plan.own // LANE)
+    def _(line):
+        pick(line, LANE)
+
+    if plan.own % LANE:
+        pick(plan.own // LANE, plan.own % LANE)
 
 
 def owned(plan, position, weights):
@@ -250,7 +271,8 @@
             pltpu.SemaphoreType.DMA,
             pltpu.SemaphoreType.DMA,
         ],
-        compiler_params=pltpu.CompilerParams(vmem_limit_bytes=24 * MIB),
+        compiler_params=pltpu.CompilerParams(vmem_limit_bytes=58 * MIB),
+        cost_estimate=pl.CostEstimate(flops=0, bytes_accessed=20 * MIB, transcendentals=0),
         name="owned_weights",
     )(position, weights)
 
@@ -258,7 +280,7 @@
 def update_kernel(plan, terms_a, terms_b, *refs):
     parts_a, parts_b, refs = refs[:terms_a], refs[terms_a : terms_a + terms_b], refs[terms_a + terms_b :]
     first_ref, second_ref, weight_ref, natural_ref = refs[:4]
-    new_first_ref, new_second_ref, step_a_ref, step_b_ref, stats_ref = refs[4:]
+    new_first_ref, new_second_ref, step_a_ref, step_b_ref, tail_ref, stats_ref = refs[4:]
     weight_sums = [jnp.zeros((8, LANE), jnp.float32)] * matrices
     step_sums = [jnp.zeros((8, LANE), jnp.float32)] * matrices
     for parts, start, rows, step_ref in (
@@ -268,6 +290,11 @@
         gradient = parts[0][:rows, :]
         for part in parts[1:]:
             gradient = gradient + part[:rows, :]
+        if step_ref is step_b_ref:
+            tail = parts[0][rows : rows + plan.tail, :]
+            for part in parts[1:]:
+                tail = tail + part[rows : rows + plan.tail, :]
+            tail_ref[...] = tail
         here = pl.ds(start, rows)
         moment_one = beta_one * first_ref[here, :] + (1.0 - beta_one) * gradient
         moment_two = beta_two * second_ref[here, :] + (1.0 - beta_two) * gradient * gradient
@@ -286,15 +313,19 @@
             for sums, squares in ((weight_sums, weight_square), (step_sums, direction_square)):
                 kept = jnp.where(inside, squares, 0.0).reshape(rows // 8, 8, LANE)
                 sums[k] = sums[k] + jnp.sum(kept, axis=0)
-    for k in range(8):
-        for base, sums in ((0, weight_sums), (8, step_sums)):
-            row = jnp.sum(sums[k], axis=0, keepdims=True) if k < matrices else jnp.zeros((1, LANE), jnp.float32)
-            stats_ref[base + k : base + k + 1, :] = row
+    lane = lax.broadcasted_iota(jnp.int32, (8, LANE), 1)
+    rank = lax.broadcasted_iota(jnp.int32, (8, LANE), 0)
+    stats = jnp.zeros((8, LANE), jnp.float32)
+    for k in range(matrices):
+        for column, sums in enumerate((weight_sums, step_sums)):
+            stats = jnp.where((rank == k) & (lane == column), jnp.sum(sums[k]), stats)
+    stats_ref[...] = stats
 
 
 def update(plan, parts_a, parts_b, first, second, weight, natural):
     vmem = pl.BlockSpec(memory_space=pltpu.VMEM)
-    shapes = [(plan.own, LANE), (plan.own, LANE), (plan.rows_a, LANE), (plan.rows_b, LANE), (16, LANE)]
+    shapes = [(plan.own, LANE), (plan.own, LANE), (plan.rows_a, LANE), (plan.rows_b, LANE), (plan.tail, LANE)]
+    shapes.append((8, LANE))
     return pl.pallas_call(
         functools.partial(update_kernel, plan, len(parts_a), len(parts_b)),
         out_shape=[jax.ShapeDtypeStruct(s, jnp.float32) for s in shapes],
@@ -305,8 +336,68 @@
     )(*parts_a, *parts_b, first, second, weight, natural)
 
 
-def finish_kernel(plan, tile, starts, position_ref, rates_ref, weights_ref, *refs):
-    pieces, refs = refs[: len(starts)], refs[len(starts) :]
+def fetch_pieces(place_ref, copies, keeps):
+    here = {"z": place_ref[0], "x": place_ref[1], "c": place_ref[2]}
+    for act in (lambda copy: copy.start(), lambda copy: copy.wait()):
+        for copy, keep in zip(copies, keeps):
+            valid = None
+            for axis, least, most in keep:
+                inside = (here[axis] >= least) & (here[axis] <= most)
+                valid = inside if valid is None else valid & inside
+            if valid is None:
+                act(copy)
+            else:
+
+                @pl.when(valid)
+                def _(copy=copy, act=act):
+                    act(copy)
+
+
+def tails_kernel(plan, sources, place_ref, *refs):
+    pieces, refs = refs[: len(sources)], refs[len(sources) :]
+    norm_ref, ratio_ref, held, sems = refs
+    copies, keeps = [], []
+    for piece, (far_c, far_z, keep) in zip(pieces, sources):
+        for far_x in range(plan.nx):
+            z = lax.rem(place_ref[0] + far_z, plan.nz)
+            x = lax.rem(place_ref[1] + far_x, plan.nx)
+            d = plan.index(z, x, lax.rem(place_ref[2] + far_c, 2))
+            rows = pl.ds(far_x * plan.block_b + plan.rows_b, plan.tail)
+            copies.append(pltpu.make_async_copy(piece.at[rows], held.at[d], sems.at[len(copies)]))
+            keeps.append(keep)
+    fetch_pieces(place_ref, copies, keeps)
+    total = held[0]
+    for d in range(1, plan.replicas):
+        total = total + held[d]
+    for row in range(plan.norm_rows):
+        norm_ref[row : row + 1, :] = held[row // plan.norm_each, pl.ds(row % plan.norm_each, 1), :]
+    for k in range(matrices):
+        row = plan.norm_each + k
+        weight_square, direction_square = total[row : row + 1, 0:1], total[row : row + 1, 1:2]
+        ratio = jnp.sqrt(weight_square) / (jnp.sqrt(direction_square) + epsilon)
+        ratio_ref[k : k + 1, :] = jnp.broadcast_to(ratio, (1, LANE))
+
+
+def tails(plan, my_place, pieces, sources):
+    vmem = pl.BlockSpec(memory_space=pltpu.VMEM)
+    return pl.pallas_call(
+        functools.partial(tails_kernel, plan, sources),
+        out_shape=[
+            jax.ShapeDtypeStruct((plan.norm_rows, LANE), jnp.float32),
+            jax.ShapeDtypeStruct((matrices, LANE), jnp.float32),
+        ],
+        in_specs=[pl.BlockSpec(memory_space=pltpu.SMEM)] + [pl.BlockSpec(memory_space=pl.ANY)] * len(pieces),
+        out_specs=[vmem, vmem],
+        scratch_shapes=[
+            pltpu.VMEM((plan.replicas, plan.tail, LANE), jnp.float32),
+            pltpu.SemaphoreType.DMA((len(pieces) * plan.nx,)),
+        ],
+        name="tails",
+    )(my_place, *pieces)
+
+
+def finish_kernel(plan, tile, sources, place_ref, position_ref, rates_ref, weights_ref, *refs):
+    pieces, refs = refs[: len(sources)], refs[len(sources) :]
     out_ref, held, sems = refs
     now = pl.program_id(0)
 
@@ -314,12 +405,9 @@
     def _():
         copies = [
             pltpu.make_async_copy(piece, held.at[pl.ds(start, piece.shape[0])], sems.at[i])
-            for i, (piece, start) in enumerate(zip(pieces, starts))
+            for i, (piece, (start, _)) in enumerate(zip(pieces, sources))
         ]
-        for copy in copies:
-            copy.start()
-        for copy in copies:
-            copy.wait()
+        fetch_pieces(place_ref, copies, [keep for _, keep in sources])
 
     matrix = jnp.int32(0)
     for bound in plan.bounds:
@@ -327,37 +415,35 @@
     rate = rates_ref[matrix]
     lines = tile // LANE
 
-    @pl.loop(0, tile // 64)
-    def _(step):
-        line = now * lines + step // 2
-        column = (step % 2) * 64
-        for group in range(8):
-            rows = [held[pl.ds(position_ref[line, column + group * 8 + u], 1), :] for u in range(8)]
-            here = pl.ds(pl.multiple_of(step * 64 + group * 8, 8), 8)
+    @pl.loop(0, lines)
+    def _(line):
+        for group in range(0, LANE, 8):
+            rows = [held[pl.ds(position_ref[now * lines + line, group + u], 1), :] for u in range(8)]
+            here = pl.ds(pl.multiple_of(line * LANE + group, 8), 8)
             weight = weights_ref[here, :]
             direction = jnp.concatenate(rows, 0) + decay_rate * weight
             out_ref[here, :] = weight - rate * direction
 
 
-def finish(plan, position, rates, weights, pieces, starts):
+def finish(plan, my_place, position, rates, weights, pieces, sources):
     tile = LANE
     while tile < 1024 and all(b % (2 * tile) == 0 for b in plan.bounds + (plan.blocks,)):
         tile *= 2
     smem = pl.BlockSpec(memory_space=pltpu.SMEM)
     return pl.pallas_call(
-        functools.partial(finish_kernel, plan, tile, starts),
+        functools.partial(finish_kernel, plan, tile, sources),
         grid=(plan.blocks // tile,),
         out_shape=jax.ShapeDtypeStruct((plan.blocks, LANE), jnp.float32),
-        in_specs=[smem, smem, pl.BlockSpec((tile, LANE), lambda i: (i, 0))]
+        in_specs=[smem, smem, smem, pl.BlockSpec((tile, LANE), lambda i: (i, 0))]
         + [pl.BlockSpec(memory_space=pl.ANY)] * len(pieces),
         out_specs=pl.BlockSpec((tile, LANE), lambda i: (i, 0)),
         scratch_shapes=[
-            pltpu.VMEM((plan.blocks, LANE), jnp.float32),
+            pltpu.VMEM((2 * plan.half, LANE), jnp.float32),
             pltpu.SemaphoreType.DMA((len(pieces),)),
         ],
-        compiler_params=pltpu.CompilerParams(vmem_limit_bytes=24 * MIB),
+        compiler_params=pltpu.CompilerParams(vmem_limit_bytes=58 * MIB),
         name="new_weights",
-    )(position, rates, weights, *pieces)
+    )(my_place, position, rates, weights, *pieces)
 
 
 def adam_step(gradient, moment_one, moment_two, weight):
@@ -373,50 +459,52 @@
     my_place = jnp.stack([me // (2 * plan.nx), (me // 2) % plan.nx, me % 2]).astype(jnp.int32)
     owners = jnp.pad(owner_list[0], (0, plan.lists * LANE - plan.blocks), constant_values=-1)
     owners = owners.reshape(plan.lists, LANE)
-    sibling, blocks_b, blocks_a, position = place(plan, my_place, owners, gradients[0])
-
-    other = plan.swap(sibling)
-    size_b, size_a = plan.size_b, plan.size_a
-    after_b = plan.slots * plan.rows_b
-    blocks_b = [b + other[i * size_b : (i + 1) * size_b] for i, b in enumerate(blocks_b)]
-    blocks_a = [b + other[after_b + i * size_a : after_b + (i + 1) * size_a] for i, b in enumerate(blocks_a)]
-    terms = line_reduce(plan, "x", plan.nx, blocks_a)
-    summed_a = sum(terms[1:], terms[0])
-    rows_a, rows_b = plan.rows_a, plan.rows_b
-    parts_a = line_reduce(plan, "z", plan.nz, [summed_a[i * rows_a : (i + 1) * rows_a] for i in range(plan.nz)])
+    siblings, blocks_b, blocks_a, position = place(plan, my_place, owners, norm_grads[0], gradients[0])
+
+    other_b, other_a = plan.swap(siblings[0]), plan.swap(siblings[1])
+    size_b, rows_a, block_b = plan.size_b, plan.rows_a, plan.block_b
+    blocks_b = [b + other_b[i * size_b : (i + 1) * size_b] for i, b in enumerate(blocks_b)]
     terms = line_reduce(plan, "z", plan.nz, blocks_b)
     summed_b = sum(terms[1:], terms[0])
-    parts_b = line_reduce(plan, "x", plan.nx, [summed_b[i * rows_b : (i + 1) * rows_b] for i in range(plan.nx)])
+    parts_b = line_reduce(plan, "x", plan.nx, [summed_b[i * block_b : (i + 1) * block_b] for i in range(plan.nx)])
+    near_a = []
+    for z in range(plan.nz):
+        blocks = []
+        for x in range(plan.nx):
+            far = (x * plan.nz + z) * rows_a
+            blocks.append(blocks_a[x][z * rows_a : (z + 1) * rows_a] + other_a[far : far + rows_a])
+        terms = line_reduce(plan, "x", plan.nx, blocks)
+        near_a.append(sum(terms[1:], terms[0]))
+    parts_a = line_reduce(plan, "z", plan.nz, near_a)
 
     weight_own, natural = owned(plan, position, weights)
-    new_first, new_second, step_a, step_b, stats = update(
+    new_first, new_second, step_a, step_b, tail, stats = update(
         plan, parts_a, parts_b, first_moment[0], second_moment[0], weight_own, natural
     )
 
-    small = jnp.concatenate([stats, norm_grads[0].astype(jnp.float32).reshape(-1, LANE)])
-    small = small + plan.swap(small)
-    for axis, count in (("x", plan.nx), ("z", plan.nz)):
-        hop = 1
-        while hop < count:
-            small = small + plan.send(small, axis, [(i, i ^ hop) for i in range(count)])
-            hop *= 2
-    stats, norm_sum = small[:16], small[16:].reshape(norm_grads.shape[1:])
     hop = 1
     while hop < plan.narrow:
         stats = stats + lax.ppermute(stats, "mp", [(i, i ^ hop) for i in range(plan.narrow)])
         hop *= 2
-    squares = jnp.sum(stats, axis=1)
-    ratios = jnp.sqrt(squares[:matrices]) / (jnp.sqrt(squares[8 : 8 + matrices]) + epsilon)
-
-    near_a = jnp.concatenate(line_gather(plan, "z", plan.nz, step_a))
-    pieces_a = line_gather(plan, "x", plan.nx, near_a)
-    near_b = jnp.concatenate(line_gather(plan, "x", plan.nx, step_b))
-    pieces_b = line_gather(plan, "z", plan.nz, near_b)
-    mine = pieces_b + pieces_a
-    pieces = [plan.swap(piece) for piece in mine] + mine
-    offsets = [i * size_b for i in range(plan.nz)] + [after_b + i * size_a for i in range(plan.nx)]
-    starts = offsets + [plan.half + offset for offset in offsets]
-    new_weights = finish(plan, position, learning * ratios, weights, pieces, starts)
+    tail = jnp.concatenate([tail[: plan.norm_each], stats[: plan.tail - plan.norm_each]])
+    step_b = jnp.concatenate([step_b, tail])
+    near_b = jnp.concatenate(merged(line_gather(plan, "x", plan.nx, step_b), plan.nx))
+    pieces, sources, tail_pieces, tail_sources = [], [], [], []
+    for value, far_z, keep in line_gather(plan, "z", plan.nz, near_b):
+        for far_c, piece in ((0, value), (1, plan.swap(value, keep))):
+            pieces.append(piece)
+            sources.append(((1 - far_c) * plan.half + far_z * plan.size_b, keep))
+            tail_pieces.append(piece)
+            tail_sources.append((far_c, far_z, keep))
+    for block, far_z, keep_z in line_gather(plan, "z", plan.nz, step_a):
+        for value, far_x, keep in line_gather(plan, "x", plan.nx, block, keep_z):
+            for far_c, piece in ((0, value), (1, plan.swap(value, keep))):
+                pieces.append(piece)
+                start = plan.after_b + (far_x * plan.nz + far_z) * rows_a
+                sources.append(((1 - far_c) * plan.half + start, keep))
+    norm_sum, ratios = tails(plan, my_place, tail_pieces, tail_sources)
+    norm_sum, ratios = norm_sum.reshape(norm_grads.shape[1:]), ratios[:, 0]
+    new_weights = finish(plan, my_place, position, learning * ratios, weights, pieces, sources)
 
     gain_rows = norm_state[0]
     norm_one, norm_two, norm_update = adam_step(norm_sum, norm_state[1], norm_state[2], gain_rows)

time: 322 us -> 274 us (0.85)
  Pallas kernels: 111 us -> 68.7 us
  waiting for transfers between devices: 113 us -> 84.6 us
  starting transfers between devices: 83.2 us -> 106 us
    ppermute x39 -> x60, waiting for transfers between devices: 113 us -> 82.5 us  [send(): return lax.ppermute(value, 'dp', every)]
    pallas_call x1, Pallas kernels: 46.8 us -> 23.9 us  [place(): pl.pallas_call(functools.partial(place_kernel, plan), out_shape=[jax.Shap...]
    ppermute x39 -> x60, starting transfers between devices: 81.7 us -> 104 us  [send(): return lax.ppermute(value, 'dp', every)]
    pallas_call x1 -> x2, Pallas kernels: 47 us -> 27.7 us  [the longest x1 25.2 us: finish(): pl.pallas_call(functools.partial(finish_kernel, plan, tile, sources), gri...]
    unnamed x22 -> x88, local copies, waits for them, and re-layouts: 6.74 us -> 4.29 us
  transfers between devices with their start and end apart: 40 -> 61, of which waited for: 19 -> 19; matrix products, arithmetic and copies ran while one was open for 2% -> 2% of each run, Pallas kernels for 5% -> 6%
where the time goes in v2:
time: 274 us; the launch traced here: 272 us
  starting transfers between devices  106 us (39%)
  waiting for transfers between devices  84.6 us (31%)
  Pallas kernels  68.7 us (25%)
  local copies, waits for them, and re-layouts  6.54 us (2%)
  other arithmetic  4.88 us (2%)
    ppermute x60, starting transfers between devices, send(): return lax.ppermute(value, 'dp', every)  104 us
    ppermute x60, waiting for transfers between devices, send(): return lax.ppermute(value, 'dp', every)  82.5 us
    pallas_call x1, Pallas kernels, finish(): pl.pallas_call(functools.partial(finish_kernel, plan, tile, sources), gri...  25.2 us
    pallas_call x1, Pallas kernels, place(): pl.pallas_call(functools.partial(place_kernel, plan), out_shape=[jax.Shap...  23.9 us
    pallas_call x1, Pallas kernels, owned(): pl.pallas_call(functools.partial(owned_kernel, plan), out_shape=[jax.Shap...  14.6 us
  transfers between devices with their start and end apart: 61, of which 19 were waited for; matrix products, arithmetic and copies ran while one was open for 2% of the time, Pallas kernels for 6%

profile of v2, /device:TPU:0, one launch (start us, length us, event | category | flops | bytes accessed | tf_op | source)
XLA Modules:
  0.0 272.2 jit_solution(12179932475903369426)
XLA Ops:
  1.3 23.9 %place_gradients.1 = (f32[3520,128]{1,0:T(8,128)}, f32[5248,128]{1,0:T(8,128)}, f32[880,128]{1,0:T(8,128)}, f32[880,128]{1,0:T(8,128)}, f32[880,128]{1,0:T(8,128...) custom-call(s32[3]{0:T(128)} %pad_add_fusion.place_ref, ...), custom_call_target="tpu_custom_call" | custom-call | tf_op jit(solution)/shard_map/place_gradients/pallas_call | solution.py:181
  25.8 7.3 %collective-permute-done.11 = f32[3520,128]{1,0:T(8,128)S(1)} collective-permute-done((f32[3520,128]{1,0:T(8,128)}, f32[3520,128]{1,0:T(8,128)S(1)}, u32[]{:S(2)}, u32[]{:S(2)}) %collective-permute-start.11) | collective-permute-done | bytes 1802272 | tf_op jit(solution)/shard_map/ppermute | solution.py:75
  33.1 1.1 slice_add_fusion
  34.2 4.9 %collective-permute-start.12 = (f32[880,128]{1,0:T(8,128)S(1)}, f32[880,128]{1,0:T(8,128)S(1)}, u32[]{:S(2)}, u32[]{:S(2)}) collective-permute-start(f32[880,128]{1,0:T(8,128)S(1)} %slice_add_fusion), channel_id=1, source_target_pairs={{0,8},{2,10},{4,12},{6,14},{1,9},{3,11},{5,13},{7,15}} | collective-permute-start | bytes 1351688 | tf_op jit(solution)/shard_map/ppermute | solution.py:75
  39.3 1.6 collective-permute-start.2
  40.8 8.1 %collective-permute-done.12 = f32[880,128]{1,0:T(8,128)S(1)} collective-permute-done((f32[880,128]{1,0:T(8,128)S(1)}, f32[880,128]{1,0:T(8,128)S(1)}, u32[]{:S(2)}, u32[]{:S(2)}) %collective-permute-start.12) | collective-permute-done | bytes 450592 | tf_op jit(solution)/shard_map/ppermute | solution.py:75
  49.0 4.4 %collective-permute-start.13 = (f32[880,128]{1,0:T(8,128)S(1)}, f32[880,128]{1,0:T(8,128)S(1)}, u32[]{:S(2)}, u32[]{:S(2)}) collective-permute-start(f32[880,128]{1,0:T(8,128)S(1)} %fusion.7), channel_id=1, source_target_pairs={{0,8},{2,10},{4,12},{6,14},{8,16},{10,18},{12,20},{14,22},{1,9},{3... | collective-permute-start | bytes 1351688 | tf_op jit(solution)/shard_map/ppermute | solution.py:75
  53.4 1.6 collective-permute-start.3
  55.7 6.7 %collective-permute-done.13 = f32[880,128]{1,0:T(8,128)S(1)} collective-permute-done((f32[880,128]{1,0:T(8,128)S(1)}, f32[880,128]{1,0:T(8,128)S(1)}, u32[]{:S(2)}, u32[]{:S(2)}) %collective-permute-start.13) | collective-permute-done | bytes 450592 | tf_op jit(solution)/shard_map/ppermute | solution.py:75
  63.3 1.6 collective-permute-start.4
  67.0 7.2 %collective-permute-done.4 = f32[656,128]{1,0:T(8,128)S(1)} collective-permute-done((f32[656,128]{1,0:T(8,128)S(1)}, f32[656,128]{1,0:T(8,128)S(1)}, u32[]{:S(2)}, u32[]{:S(2)}) %collective-permute-start.4) | collective-permute-done | bytes 335904 | tf_op jit(solution)/shard_map/ppermute | solution.py:75
  74.3 5.0 %collective-permute-start.5 = (f32[656,128]{1,0:T(8,128)S(1)}, f32[656,128]{1,0:T(8,128)S(1)}, u32[]{:S(2)}, u32[]{:S(2)}) collective-permute-start(f32[656,128]{1,0:T(8,128)S(1)} %get-tuple-element.51), channel_id=1, source_target_pairs={{0,8},{2,10},{4,12},{6,14},{1,9},{3,11},{5,13},{7,15}} | collective-permute-start | bytes 1007624 | tf_op jit(solution)/shard_map/ppermute | solution.py:75
  79.3 1.3 collective-permute-start.14
  80.7 1.4 collective-permute-start.17
  82.1 5.4 %collective-permute-done.5 = f32[656,128]{1,0:T(8,128)S(1)} collective-permute-done((f32[656,128]{1,0:T(8,128)S(1)}, f32[656,128]{1,0:T(8,128)S(1)}, u32[]{:S(2)}, u32[]{:S(2)}) %collective-permute-start.5) | collective-permute-done | bytes 335904 | tf_op jit(solution)/shard_map/ppermute | solution.py:75
  87.8 7.0 %collective-permute-start.6 = (f32[656,128]{1,0:T(8,128)S(1)}, f32[656,128]{1,0:T(8,128)S(1)}, u32[]{:S(2)}, u32[]{:S(2)}) collective-permute-start(f32[656,128]{1,0:T(8,128)S(1)} %get-tuple-element.52), channel_id=1, source_target_pairs={{0,8},{2,10},{4,12},{6,14},{8,16},{10,18},{12,20},{14,22},{1,9},{3... | collective-permute-start | bytes 1007624 | tf_op jit(solution)/shard_map/ppermute | solution.py:75
  94.7 1.3 collective-permute-start.10
  96.7 2.2 collective-permute-done.17
  99.1 1.5 collective-permute-done.6
  100.6 9.9 %collective-permute-start.7 = (f32[656,128]{1,0:T(8,128)S(1)}, f32[656,128]{1,0:T(8,128)S(1)}, u32[]{:S(2)}, u32[]{:S(2)}) collective-permute-start(f32[656,128]{1,0:T(8,128)S(1)} %add.143), channel_id=1, source_target_pairs={{0,8},{2,10},{4,12},{6,14},{8,16},{10,18},{12,20},{14,22},{16,24},... | collective-permute-start | bytes 1007624 | tf_op jit(solution)/shard_map/ppermute | solution.py:75
  110.6 1.6 collective-permute-start.18
  112.2 14.6 %owned_weights.1 = (f32[1088,128]{1,0:T(8,128)}, s32[1088,128]{1,0:T(8,128)}) custom-call(s32[136,128]{1,0:T(8,128)} %get-tuple-element.24.position_ref, f32[17408,128]{1,0:T(8,128)} %weights_ref.3), custom_call_target="tpu_custom_call" | custom-call | bytes 20971520 | tf_op jit(solution)/shard_map/owned_weights/pallas_call | solution.py:259
  126.9 1.0 copy-done.2
  127.9 1.1 copy-done.3
  129.0 2.5 moments.1
  131.4 1.5 collective-permute-start.19
  132.9 2.1 collective-permute-done.19
  135.7 5.4 %collective-permute-done.20 = f32[440,128]{1,0:T(8,128)S(1)} collective-permute-done((f32[440,128]{1,0:T(8,128)S(1)}, f32[440,128]{1,0:T(8,128)S(1)}, u32[]{:S(2)}, u32[]{:S(2)}) %collective-permute-start.20) | collective-permute-done | bytes 225312 | tf_op jit(solution)/shard_map/ppermute | solution.py:75
  141.1 3.9 %collective-permute-start.22 = (f32[880,128]{1,0:T(8,128)S(1)}, f32[880,128]{1,0:T(8,128)S(1)}, u32[]{:S(2)}, u32[]{:S(2)}) collective-permute-start(f32[880,128]{1,0:T(8,128)S(1)} %pad_maximum_fusion.refs_0_), channel_id=1, source_target_pairs={{0,8},{2,10},{4,12},{6,14},{8,16},{10,18},{12,20},{14,22},{16,24},... | collective-permute-start | bytes 1351688 | tf_op jit(solution)/shard_map/ppermute | solution.py:75
  145.1 1.3 collective-permute-start.24
  147.1 5.3 %collective-permute-start.37 = (f32[656,128]{1,0:T(8,128)S(1)}, f32[656,128]{1,0:T(8,128)}, u32[]{:S(2)}, u32[]{:S(2)}) collective-permute-start(f32[656,128]{1,0:T(8,128)S(1)} %get-tuple-element.39.refs_14_), channel_id=1, source_target_pairs={{0,8},{2,10},{4,12},{6,14},{8,16},{10,18},{12,20},{14,22},{16,24},... | collective-permute-start | bytes 1007624 | tf_op jit(solution)/shard_map/ppermute | solution.py:75
  153.0 2.4 collective-permute-done.24.refs_4_
  155.4 1.3 collective-permute-start.28
  156.7 1.3 collective-permute-start.41
  158.1 1.0 collective-permute-done.37.refs_18_
  159.7 14.6 %collective-permute-done.41.refs_22_ = f32[656,128]{1,0:T(8,128)} collective-permute-done((f32[656,128]{1,0:T(8,128)S(1)}, f32[656,128]{1,0:T(8,128)}, u32[]{:S(2)}, u32[]{:S(2)}) %collective-permute-start.41) | collective-permute-done | bytes 335904 | tf_op jit(solution)/shard_map/ppermute | solution.py:75
  175.8 1.3 collective-permute-start.32
  177.2 1.4 collective-permute-start.39
  178.6 2.4 collective-permute-start.25
  181.7 1.9 collective-permute-start.29
  184.4 6.1 %collective-permute-done.32.refs_12_ = f32[880,128]{1,0:T(8,128)S(1)} collective-permute-done((f32[880,128]{1,0:T(8,128)S(1)}, f32[880,128]{1,0:T(8,128)S(1)}, u32[]{:S(2)}, u32[]{:S(2)}) %collective-permute-start.32) | collective-permute-done | bytes 450592 | tf_op jit(solution)/shard_map/ppermute | solution.py:75
  190.5 1.9 collective-permute-start.33
  192.4 1.4 collective-permute-start.45
  193.8 2.4 collective-permute-start.42
  196.2 3.4 %collective-permute-start.43 = (f32[656,128]{1,0:T(8,128)}, f32[656,128]{1,0:T(8,128)}, u32[]{:S(2)}, u32[]{:S(2)}) collective-permute-start(f32[656,128]{1,0:T(8,128)} %collective-permute-done.41.refs_22_), channel_id=1, source_target_pairs={{0,4},{2,6},{4,0},{6,2},{8,12},{10,14},{12,8},{14,10},{16,20},{18,... | collective-permute-start | bytes 1007624 | tf_op jit(solution)/shard_map/ppermute | solution.py:75
  199.7 1.3 collective-permute-start.49
  201.0 0.8 copy-done.20
  201.8 1.4 collective-permute-start.40
  203.4 2.5 tails.1
  205.9 0.7 reshape.74
  209.6 6.9 %collective-permute-done.49.refs_30_ = f32[656,128]{1,0:T(8,128)} collective-permute-done((f32[656,128]{1,0:T(8,128)}, f32[656,128]{1,0:T(8,128)}, u32[]{:S(2)}, u32[]{:S(2)}) %collective-permute-start.49) | collective-permute-done | bytes 335904 | tf_op jit(solution)/shard_map/ppermute | solution.py:75
  216.5 1.9 collective-permute-start.44
  218.4 1.3 collective-permute-start.57
  219.7 0.8 slice_reduce_fusion
  220.5 2.4 collective-permute-start.50
  223.0 2.4 collective-permute-start.51
  226.8 4.0 %collective-permute-done.57.refs_38_ = f32[656,128]{1,0:T(8,128)S(1)} collective-permute-done((f32[656,128]{1,0:T(8,128)}, f32[656,128]{1,0:T(8,128)S(1)}, u32[]{:S(2)}, u32[]{:S(2)}) %collective-permute-start.57) | collective-permute-done | bytes 335904 | tf_op jit(solution)/shard_map/ppermute | solution.py:75
  230.8 2.4 collective-permute-start.59
  234.9 1.9 collective-permute-start.58
  236.8 2.4 collective-permute-start.52
  239.9 2.2 collective-permute-done.59.refs_40_
  242.2 1.9 collective-permute-start.60
  246.3 0.7 copy-done.42
  247.1 25.2 %new_weights.1 = f32[17408,128]{1,0:T(8,128)} custom-call(s32[3]{0:T(128)} %pad_add_fusion.place_ref, s32[136,128]{1,0:T(8,128)} %get-tuple-element.24.position_ref, f32[5]{0:T(128)} %broadcast_multiply_fusion.1.rates_ref, f32[17408,128]{1,0:T(8,128)} %weights_ref.3, f32[880,128]{1,0:T(8,128)} %copy-done.5, f32[880,128]{1,0:T(8,128)} %copy-done.12, ...), custom_call_target="tpu_custom_call" | custom-call | tf_op jit(solution)/shard_map/new_weights/pallas_call | solution.py:433
  (179 shorter events, 20.9 us)
Async XLA Ops:
  25.2 13.9 %collective-permute-start = (f32[5248,128]{1,0:T(8,128)}, f32[5248,128]{1,0:T(8,128)S(1)}, u32[]{:S(2)}, u32[]{:S(2)}) collective-permute-start(f32[5248,128]{1,0:T(8,128)} %get-tuple-element.26), channel_id=1, source_target_pairs={{0,2},{2,0},{4,6},{6,4},{8,10},{10,8},{12,14},{14,12},{16,18},{18,... | collective-permute-start | bytes 8060936 | tf_op jit(solution)/shard_map/ppermute | solution.py:75
  25.7 7.4 %collective-permute-start.11 = (f32[3520,128]{1,0:T(8,128)}, f32[3520,128]{1,0:T(8,128)S(1)}, u32[]{:S(2)}, u32[]{:S(2)}) collective-permute-start(f32[3520,128]{1,0:T(8,128)} %get-tuple-element.29), channel_id=1, source_target_pairs={{0,2},{2,0},{4,6},{6,4},{8,10},{10,8},{12,14},{14,12},{16,18},{18,... | collective-permute-start | bytes 5406728 | tf_op jit(solution)/shard_map/ppermute | solution.py:75
  34.2 14.7 %collective-permute-start.12 = (f32[880,128]{1,0:T(8,128)S(1)}, f32[880,128]{1,0:T(8,128)S(1)}, u32[]{:S(2)}, u32[]{:S(2)}) collective-permute-start(f32[880,128]{1,0:T(8,128)S(1)} %slice_add_fusion), channel_id=1, source_target_pairs={{0,8},{2,10},{4,12},{6,14},{1,9},{3,11},{5,13},{7,15}} | collective-permute-start | bytes 1351688 | tf_op jit(solution)/shard_map/ppermute | solution.py:75
  39.3 15.7 %collective-permute-start.2 = (f32[656,128]{1,0:T(8,128)S(1)}, f32[656,128]{1,0:T(8,128)S(1)}, u32[]{:S(2)}, u32[]{:S(2)}) collective-permute-start(f32[656,128]{1,0:T(8,128)S(1)} %get-tuple-element.56), channel_id=1, source_target_pairs={{0,4},{2,6},{4,0},{6,2},{8,12},{10,14},{12,8},{14,10},{16,20},{18,... | collective-permute-start | bytes 1007624 | tf_op jit(solution)/shard_map/ppermute | solution.py:75
  49.0 13.5 %collective-permute-start.13 = (f32[880,128]{1,0:T(8,128)S(1)}, f32[880,128]{1,0:T(8,128)S(1)}, u32[]{:S(2)}, u32[]{:S(2)}) collective-permute-start(f32[880,128]{1,0:T(8,128)S(1)} %fusion.7), channel_id=1, source_target_pairs={{0,8},{2,10},{4,12},{6,14},{8,16},{10,18},{12,20},{14,22},{1,9},{3... | collective-permute-start | bytes 1351688 | tf_op jit(solution)/shard_map/ppermute | solution.py:75
  53.4 11.4 %collective-permute-start.3 = (f32[656,128]{1,0:T(8,128)S(1)}, f32[656,128]{1,0:T(8,128)S(1)}, u32[]{:S(2)}, u32[]{:S(2)}) collective-permute-start(f32[656,128]{1,0:T(8,128)S(1)} %get-tuple-element.55), channel_id=1, source_target_pairs={{0,4},{2,6},{4,0},{6,2},{8,12},{10,14},{12,8},{14,10},{16,20},{18,... | collective-permute-start | bytes 1007624 | tf_op jit(solution)/shard_map/ppermute | solution.py:75
  55.1 9.8 %collective-permute-start.8 = (f32[656,128]{1,0:T(8,128)S(1)}, f32[656,128]{1,0:T(8,128)S(1)}, u32[]{:S(2)}, u32[]{:S(2)}) collective-permute-start(f32[656,128]{1,0:T(8,128)S(1)} %fusion.4), channel_id=1, source_target_pairs={{24,16},{26,18},{28,20},{30,22},{25,17},{27,19},{29,21},{31,23}} | collective-permute-start | bytes 1007624 | tf_op jit(solution)/shard_map/ppermute | solution.py:75
  62.6 3.7 %collective-permute-start.15 = (f32[880,128]{1,0:T(8,128)S(1)}, f32[880,128]{1,0:T(8,128)S(1)}, u32[]{:S(2)}, u32[]{:S(2)}) collective-permute-start(f32[880,128]{1,0:T(8,128)S(1)} %get-tuple-element.49), channel_id=1, source_target_pairs={{24,16},{26,18},{28,20},{30,22},{25,17},{27,19},{29,21},{31,23}} | collective-permute-start | bytes 1351688 | tf_op jit(solution)/shard_map/ppermute | solution.py:75
  63.3 10.9 %collective-permute-start.4 = (f32[656,128]{1,0:T(8,128)S(1)}, f32[656,128]{1,0:T(8,128)S(1)}, u32[]{:S(2)}, u32[]{:S(2)}) collective-permute-start(f32[656,128]{1,0:T(8,128)S(1)} %get-tuple-element.54), channel_id=1, source_target_pairs={{0,4},{2,6},{4,0},{6,2},{8,12},{10,14},{12,8},{14,10},{16,20},{18,... | collective-permute-start | bytes 1007624 | tf_op jit(solution)/shard_map/ppermute | solution.py:75
  65.0 9.2 %collective-permute-start.9 = (f32[656,128]{1,0:T(8,128)S(1)}, f32[656,128]{1,0:T(8,128)S(1)}, u32[]{:S(2)}, u32[]{:S(2)}) collective-permute-start(f32[656,128]{1,0:T(8,128)S(1)} %fusion.16), channel_id=1, source_target_pairs={{16,8},{18,10},{20,12},{22,14},{24,16},{26,18},{28,20},{30,22},{17... | collective-permute-start | bytes 1007624 | tf_op jit(solution)/shard_map/ppermute | solution.py:75
  65.6 16.5 %collective-permute-start.1 = (f32[656,128]{1,0:T(8,128)S(1)}, f32[656,128]{1,0:T(8,128)S(1)}, u32[]{:S(2)}, u32[]{:S(2)}) collective-permute-start(f32[656,128]{1,0:T(8,128)S(1)} %get-tuple-element.57), channel_id=1, source_target_pairs={{0,4},{2,6},{4,0},{6,2},{8,12},{10,14},{12,8},{14,10},{16,20},{18,... | collective-permute-start | bytes 1007624 | tf_op jit(solution)/shard_map/ppermute | solution.py:75
  66.3 14.3 %collective-permute-start.16 = (f32[880,128]{1,0:T(8,128)S(1)}, f32[880,128]{1,0:T(8,128)S(1)}, u32[]{:S(2)}, u32[]{:S(2)}) collective-permute-start(f32[880,128]{1,0:T(8,128)S(1)} %fusion.6), channel_id=1, source_target_pairs={{16,8},{18,10},{20,12},{22,14},{24,16},{26,18},{28,20},{30,22},{17... | collective-permute-start | bytes 1351688 | tf_op jit(solution)/shard_map/ppermute | solution.py:75
  74.3 13.3 %collective-permute-start.5 = (f32[656,128]{1,0:T(8,128)S(1)}, f32[656,128]{1,0:T(8,128)S(1)}, u32[]{:S(2)}, u32[]{:S(2)}) collective-permute-start(f32[656,128]{1,0:T(8,128)S(1)} %get-tuple-element.51), channel_id=1, source_target_pairs={{0,8},{2,10},{4,12},{6,14},{1,9},{3,11},{5,13},{7,15}} | collective-permute-start | bytes 1007624 | tf_op jit(solution)/shard_map/ppermute | solution.py:75
  79.3 17.5 %collective-permute-start.14 = (f32[880,128]{1,0:T(8,128)S(1)}, f32[880,128]{1,0:T(8,128)S(1)}, u32[]{:S(2)}, u32[]{:S(2)}) collective-permute-start(f32[880,128]{1,0:T(8,128)S(1)} %get-tuple-element.48), channel_id=1, source_target_pairs={{0,8},{2,10},{4,12},{6,14},{8,16},{10,18},{12,20},{14,22},{16,24},... | collective-permute-start | bytes 1351688 | tf_op jit(solution)/shard_map/ppermute | solution.py:75
  80.7 18.3 %collective-permute-start.17 = (f32[880,128]{1,0:T(8,128)S(1)}, f32[880,128]{1,0:T(8,128)S(1)}, u32[]{:S(2)}, u32[]{:S(2)}) collective-permute-start(f32[880,128]{1,0:T(8,128)S(1)} %add.154), channel_id=1, source_target_pairs={{8,0},{10,2},{12,4},{14,6},{16,8},{18,10},{20,12},{22,14},{24,16},... | collective-permute-start | bytes 1351688 | tf_op jit(solution)/shard_map/ppermute | solution.py:75
  87.8 12.8 %collective-permute-start.6 = (f32[656,128]{1,0:T(8,128)S(1)}, f32[656,128]{1,0:T(8,128)S(1)}, u32[]{:S(2)}, u32[]{:S(2)}) collective-permute-start(f32[656,128]{1,0:T(8,128)S(1)} %get-tuple-element.52), channel_id=1, source_target_pairs={{0,8},{2,10},{4,12},{6,14},{8,16},{10,18},{12,20},{14,22},{1,9},{3... | collective-permute-start | bytes 1007624 | tf_op jit(solution)/shard_map/ppermute | solution.py:75
  94.7 32.1 %collective-permute-start.10 = (f32[656,128]{1,0:T(8,128)S(1)}, f32[656,128]{1,0:T(8,128)S(1)}, u32[]{:S(2)}, u32[]{:S(2)}) collective-permute-start(f32[656,128]{1,0:T(8,128)S(1)} %get-tuple-element.50), channel_id=1, source_target_pairs={{8,0},{10,2},{12,4},{14,6},{16,8},{18,10},{20,12},{22,14},{24,16},... | collective-permute-start | bytes 1007624 | tf_op jit(solution)/shard_map/ppermute | solution.py:75
  100.6 26.2 %collective-permute-start.7 = (f32[656,128]{1,0:T(8,128)S(1)}, f32[656,128]{1,0:T(8,128)S(1)}, u32[]{:S(2)}, u32[]{:S(2)}) collective-permute-start(f32[656,128]{1,0:T(8,128)S(1)} %add.143), channel_id=1, source_target_pairs={{0,8},{2,10},{4,12},{6,14},{8,16},{10,18},{12,20},{14,22},{16,24},... | collective-permute-start | bytes 1007624 | tf_op jit(solution)/shard_map/ppermute | solution.py:75
  110.6 16.2 %collective-permute-start.18 = (f32[440,128]{1,0:T(8,128)S(1)}, f32[440,128]{1,0:T(8,128)S(1)}, u32[]{:S(2)}, u32[]{:S(2)}) collective-permute-start(f32[440,128]{1,0:T(8,128)S(1)} %get-tuple-element.58), channel_id=1, source_target_pairs={{0,4},{2,6},{4,0},{6,2},{8,12},{10,14},{12,8},{14,10},{16,20},{18,... | collective-permute-start | bytes 675848 | tf_op jit(solution)/shard_map/ppermute | solution.py:75
  129.0 74.2 %copy-start.43 = (f32[3,2,1024]{2,1,0:T(2,128)S(1)}, f32[3,2,1024]{2,1,0:T(2,128)}, u32[]{:S(2)}) copy-start(f32[3,2,1024]{2,1,0:T(2,128)} %param.13) | copy-start | bytes 73732
  131.4 74.5 %copy-start.4 = (f32[656,128]{1,0:T(8,128)}, f32[656,128]{1,0:T(8,128)S(1)}, u32[]{:S(2)}) copy-start(f32[656,128]{1,0:T(8,128)S(1)} %get-tuple-element.39.refs_14_) | copy-start | bytes 1007620
  131.4 3.6 %collective-permute-start.19 = (f32[8,128]{1,0:T(8,128)S(1)}, f32[8,128]{1,0:T(8,128)S(1)}, u32[]{:S(2)}, u32[]{:S(2)}) collective-permute-start(f32[8,128]{1,0:T(8,128)S(1)} %get-tuple-element.37), channel_id=1, source_target_pairs={{0,1},{1,0},{2,3},{3,2},{4,5},{5,4},{6,7},{7,6},{8,9},{9,8},{10,11... | collective-permute-start | bytes 12296 | tf_op jit(solution)/shard_map/ppermute | solution.py:487
  135.1 6.0 %collective-permute-start.20 = (f32[440,128]{1,0:T(8,128)S(1)}, f32[440,128]{1,0:T(8,128)S(1)}, u32[]{:S(2)}, u32[]{:S(2)}) collective-permute-start(f32[440,128]{1,0:T(8,128)S(1)} %pad_maximum_fusion.1), channel_id=1, source_target_pairs={{0,4},{2,6},{4,0},{6,2},{8,12},{10,14},{12,8},{14,10},{16,20},{18,... | collective-permute-start | bytes 675848 | tf_op jit(solution)/shard_map/ppermute | solution.py:75
  141.1 62.2 %copy-start.5 = (f32[880,128]{1,0:T(8,128)}, f32[880,128]{1,0:T(8,128)S(1)}, u32[]{:S(2)}) copy-start(f32[880,128]{1,0:T(8,128)S(1)} %pad_maximum_fusion.refs_0_) | copy-start | bytes 1351684
  141.1 11.2 %collective-permute-start.22 = (f32[880,128]{1,0:T(8,128)S(1)}, f32[880,128]{1,0:T(8,128)S(1)}, u32[]{:S(2)}, u32[]{:S(2)}) collective-permute-start(f32[880,128]{1,0:T(8,128)S(1)} %pad_maximum_fusion.refs_0_), channel_id=1, source_target_pairs={{0,8},{2,10},{4,12},{6,14},{8,16},{10,18},{12,20},{14,22},{16,24},... | collective-permute-start | bytes 1351688 | tf_op jit(solution)/shard_map/ppermute | solution.py:75
  145.1 10.3 %collective-permute-start.24 = (f32[880,128]{1,0:T(8,128)S(1)}, f32[880,128]{1,0:T(8,128)S(1)}, u32[]{:S(2)}, u32[]{:S(2)}) collective-permute-start(f32[880,128]{1,0:T(8,128)S(1)} %pad_maximum_fusion.refs_0_), channel_id=1, source_target_pairs={{8,0},{10,2},{12,4},{14,6},{16,8},{18,10},{20,12},{22,14},{24,16},... | collective-permute-start | bytes 1351688 | tf_op jit(solution)/shard_map/ppermute | solution.py:75
  146.4 10.3 %collective-permute-start.34 = (f32[656,128]{1,0:T(8,128)S(1)}, f32[656,128]{1,0:T(8,128)S(1)}, u32[]{:S(2)}, u32[]{:S(2)}) collective-permute-start(f32[656,128]{1,0:T(8,128)S(1)} %get-tuple-element.39.refs_14_), channel_id=1, source_target_pairs={{0,2},{2,0},{4,6},{6,4},{8,10},{10,8},{12,14},{14,12},{16,18},{18,... | collective-permute-start | bytes 1007624 | tf_op jit(solution)/shard_map/ppermute | solution.py:75
  146.5 11.5 %collective-permute-start.35 = (f32[656,128]{1,0:T(8,128)S(1)}, f32[656,128]{1,0:T(8,128)S(1)}, u32[]{:S(2)}, u32[]{:S(2)}) collective-permute-start(f32[656,128]{1,0:T(8,128)S(1)} %get-tuple-element.39.refs_14_), channel_id=1, source_target_pairs={{0,4},{2,6},{4,0},{6,2},{8,12},{10,14},{12,8},{14,10},{16,20},{18,... | collective-permute-start | bytes 1007624 | tf_op jit(solution)/shard_map/ppermute | solution.py:75
  147.1 12.0 %collective-permute-start.37 = (f32[656,128]{1,0:T(8,128)S(1)}, f32[656,128]{1,0:T(8,128)}, u32[]{:S(2)}, u32[]{:S(2)}) collective-permute-start(f32[656,128]{1,0:T(8,128)S(1)} %get-tuple-element.39.refs_14_), channel_id=1, source_target_pairs={{0,8},{2,10},{4,12},{6,14},{8,16},{10,18},{12,20},{14,22},{16,24},... | collective-permute-start | bytes 1007624 | tf_op jit(solution)/shard_map/ppermute | solution.py:75
  152.3 22.8 %collective-permute-start.26 = (f32[880,128]{1,0:T(8,128)S(1)}, f32[880,128]{1,0:T(8,128)S(1)}, u32[]{:S(2)}, u32[]{:S(2)}) collective-permute-start(f32[880,128]{1,0:T(8,128)S(1)} %collective-permute-done.22.refs_2_), channel_id=1, source_target_pairs={{8,16},{10,18},{12,20},{14,22},{16,24},{18,26},{20,28},{22,30},{9,... | collective-permute-start | bytes 1351688 | tf_op jit(solution)/shard_map/ppermute | solution.py:75
  155.4 20.5 %collective-permute-start.28 = (f32[880,128]{1,0:T(8,128)S(1)}, f32[880,128]{1,0:T(8,128)S(1)}, u32[]{:S(2)}, u32[]{:S(2)}) collective-permute-start(f32[880,128]{1,0:T(8,128)S(1)} %collective-permute-done.24.refs_4_), channel_id=1, source_target_pairs={{8,0},{10,2},{12,4},{14,6},{16,8},{18,10},{20,12},{22,14},{9,1},{1... | collective-permute-start | bytes 1351688 | tf_op jit(solution)/shard_map/ppermute | solution.py:75
  156.7 17.7 %collective-permute-start.41 = (f32[656,128]{1,0:T(8,128)S(1)}, f32[656,128]{1,0:T(8,128)}, u32[]{:S(2)}, u32[]{:S(2)}) collective-permute-start(f32[656,128]{1,0:T(8,128)S(1)} %get-tuple-element.39.refs_14_), channel_id=1, source_target_pairs={{8,0},{10,2},{12,4},{14,6},{16,8},{18,10},{20,12},{22,14},{24,16},... | collective-permute-start | bytes 1007624 | tf_op jit(solution)/shard_map/ppermute | solution.py:75
  158.0 16.4 %collective-permute-start.36 = (f32[656,128]{1,0:T(8,128)S(1)}, f32[656,128]{1,0:T(8,128)S(1)}, u32[]{:S(2)}, u32[]{:S(2)}) collective-permute-start(f32[656,128]{1,0:T(8,128)S(1)} %collective-permute-done.35.refs_16_), channel_id=1, source_target_pairs={{0,2},{2,0},{4,6},{6,4},{8,10},{10,8},{12,14},{14,12},{16,18},{18,... | collective-permute-start | bytes 1007624 | tf_op jit(solution)/shard_map/ppermute | solution.py:75
  159.1 18.1 %collective-permute-start.38 = (f32[656,128]{1,0:T(8,128)}, f32[656,128]{1,0:T(8,128)S(1)}, u32[]{:S(2)}, u32[]{:S(2)}) collective-permute-start(f32[656,128]{1,0:T(8,128)} %collective-permute-done.37.refs_18_), channel_id=1, source_target_pairs={{8,10},{10,8},{12,14},{14,12},{16,18},{18,16},{20,22},{22,20},{24,... | collective-permute-start | bytes 1007624 | tf_op jit(solution)/shard_map/ppermute | solution.py:75
  174.4 6.6 %collective-permute-start.21 = (f32[880,128]{1,0:T(8,128)S(1)}, f32[880,128]{1,0:T(8,128)S(1)}, u32[]{:S(2)}, u32[]{:S(2)}) collective-permute-start(f32[880,128]{1,0:T(8,128)S(1)} %pad_maximum_fusion.refs_0_), channel_id=1, source_target_pairs={{0,2},{2,0},{4,6},{6,4},{8,10},{10,8},{12,14},{14,12},{16,18},{18,... | collective-permute-start | bytes 1351688 | tf_op jit(solution)/shard_map/ppermute | solution.py:75
  174.4 7.3 %collective-permute-start.23 = (f32[880,128]{1,0:T(8,128)S(1)}, f32[880,128]{1,0:T(8,128)S(1)}, u32[]{:S(2)}, u32[]{:S(2)}) collective-permute-start(f32[880,128]{1,0:T(8,128)S(1)} %collective-permute-done.22.refs_2_), channel_id=1, source_target_pairs={{8,10},{10,8},{12,14},{14,12},{16,18},{18,16},{20,22},{22,20},{24,... | collective-permute-start | bytes 1351688 | tf_op jit(solution)/shard_map/ppermute | solution.py:75
  175.1 8.5 %collective-permute-start.30 = (f32[880,128]{1,0:T(8,128)S(1)}, f32[880,128]{1,0:T(8,128)S(1)}, u32[]{:S(2)}, u32[]{:S(2)}) collective-permute-start(f32[880,128]{1,0:T(8,128)S(1)} %collective-permute-done.26.refs_6_), channel_id=1, source_target_pairs={{16,24},{18,26},{20,28},{22,30},{17,25},{19,27},{21,29},{23,31}} | collective-permute-start | bytes 1351688 | tf_op jit(solution)/shard_map/ppermute | solution.py:75
  175.8 14.6 %collective-permute-start.32 = (f32[880,128]{1,0:T(8,128)S(1)}, f32[880,128]{1,0:T(8,128)S(1)}, u32[]{:S(2)}, u32[]{:S(2)}) collective-permute-start(f32[880,128]{1,0:T(8,128)S(1)} %collective-permute-done.28.refs_8_), channel_id=1, source_target_pairs={{8,0},{10,2},{12,4},{14,6},{9,1},{11,3},{13,5},{15,7}} | collective-permute-start | bytes 1351688 | tf_op jit(solution)/shard_map/ppermute | solution.py:75
  177.2 1.4 collective-permute-start.39
  178.6 13.8 %collective-permute-start.25 = (f32[880,128]{1,0:T(8,128)S(1)}, f32[880,128]{1,0:T(8,128)S(1)}, u32[]{:S(2)}, u32[]{:S(2)}) collective-permute-start(f32[880,128]{1,0:T(8,128)S(1)} %collective-permute-done.24.refs_4_), channel_id=1, source_target_pairs={{0,2},{2,0},{4,6},{6,4},{8,10},{10,8},{12,14},{14,12},{16,18},{18,... | collective-permute-start | bytes 1351688 | tf_op jit(solution)/shard_map/ppermute | solution.py:75
  181.0 12.8 %collective-permute-start.27 = (f32[880,128]{1,0:T(8,128)S(1)}, f32[880,128]{1,0:T(8,128)S(1)}, u32[]{:S(2)}, u32[]{:S(2)}) collective-permute-start(f32[880,128]{1,0:T(8,128)S(1)} %collective-permute-done.26.refs_6_), channel_id=1, source_target_pairs={{16,18},{18,16},{20,22},{22,20},{24,26},{26,24},{28,30},{30,28},{1... | collective-permute-start | bytes 1351688 | tf_op jit(solution)/shard_map/ppermute | solution.py:75
  181.7 14.5 %collective-permute-start.29 = (f32[880,128]{1,0:T(8,128)S(1)}, f32[880,128]{1,0:T(8,128)S(1)}, u32[]{:S(2)}, u32[]{:S(2)}) collective-permute-start(f32[880,128]{1,0:T(8,128)S(1)} %collective-permute-done.28.refs_8_), channel_id=1, source_target_pairs={{0,2},{2,0},{4,6},{6,4},{8,10},{10,8},{12,14},{14,12},{1,3},{3,1},... | collective-permute-start | bytes 1351688 | tf_op jit(solution)/shard_map/ppermute | solution.py:75
  183.7 16.0 %collective-permute-start.31 = (f32[880,128]{1,0:T(8,128)S(1)}, f32[880,128]{1,0:T(8,128)S(1)}, u32[]{:S(2)}, u32[]{:S(2)}) collective-permute-start(f32[880,128]{1,0:T(8,128)S(1)} %collective-permute-done.30.refs_10_), channel_id=1, source_target_pairs={{24,26},{26,24},{28,30},{30,28},{25,27},{27,25},{29,31},{31,29}} | collective-permute-start | bytes 1351688 | tf_op jit(solution)/shard_map/ppermute | solution.py:75
  190.5 10.5 %collective-permute-start.33 = (f32[880,128]{1,0:T(8,128)S(1)}, f32[880,128]{1,0:T(8,128)S(1)}, u32[]{:S(2)}, u32[]{:S(2)}) collective-permute-start(f32[880,128]{1,0:T(8,128)S(1)} %collective-permute-done.32.refs_12_), channel_id=1, source_target_pairs={{0,2},{2,0},{4,6},{6,4},{1,3},{3,1},{5,7},{7,5}} | collective-permute-start | bytes 1351688 | tf_op jit(solution)/shard_map/ppermute | solution.py:75
  192.4 15.1 %collective-permute-start.45 = (f32[656,128]{1,0:T(8,128)}, f32[656,128]{1,0:T(8,128)}, u32[]{:S(2)}, u32[]{:S(2)}) collective-permute-start(f32[656,128]{1,0:T(8,128)} %collective-permute-done.37.refs_18_), channel_id=1, source_target_pairs={{8,16},{10,18},{12,20},{14,22},{16,24},{18,26},{20,28},{22,30},{9,... | collective-permute-start | bytes 1007624 | tf_op jit(solution)/shard_map/ppermute | solution.py:75
  193.8 14.4 %collective-permute-start.42 = (f32[656,128]{1,0:T(8,128)}, f32[656,128]{1,0:T(8,128)}, u32[]{:S(2)}, u32[]{:S(2)}) collective-permute-start(f32[656,128]{1,0:T(8,128)} %collective-permute-done.41.refs_22_), channel_id=1, source_target_pairs={{0,2},{2,0},{4,6},{6,4},{8,10},{10,8},{12,14},{14,12},{16,18},{18,... | collective-permute-start | bytes 1007624 | tf_op jit(solution)/shard_map/ppermute | solution.py:75
  196.2 12.6 %collective-permute-start.43 = (f32[656,128]{1,0:T(8,128)}, f32[656,128]{1,0:T(8,128)}, u32[]{:S(2)}, u32[]{:S(2)}) collective-permute-start(f32[656,128]{1,0:T(8,128)} %collective-permute-done.41.refs_22_), channel_id=1, source_target_pairs={{0,4},{2,6},{4,0},{6,2},{8,12},{10,14},{12,8},{14,10},{16,20},{18,... | collective-permute-start | bytes 1007624 | tf_op jit(solution)/shard_map/ppermute | solution.py:75
  199.7 16.8 %collective-permute-start.49 = (f32[656,128]{1,0:T(8,128)}, f32[656,128]{1,0:T(8,128)}, u32[]{:S(2)}, u32[]{:S(2)}) collective-permute-start(f32[656,128]{1,0:T(8,128)} %collective-permute-done.41.refs_22_), channel_id=1, source_target_pairs={{8,0},{10,2},{12,4},{14,6},{16,8},{18,10},{20,12},{22,14},{9,1},{1... | collective-permute-start | bytes 1007624 | tf_op jit(solution)/shard_map/ppermute | solution.py:75
  201.8 16.6 %collective-permute-start.40 = (f32[656,128]{1,0:T(8,128)}, f32[656,128]{1,0:T(8,128)}, u32[]{:S(2)}, u32[]{:S(2)}) collective-permute-start(f32[656,128]{1,0:T(8,128)} %collective-permute-done.39.refs_20_), channel_id=1, source_target_pairs={{8,10},{10,8},{12,14},{14,12},{16,18},{18,16},{20,22},{22,20},{24,... | collective-permute-start | bytes 1007624 | tf_op jit(solution)/shard_map/ppermute | solution.py:75
  207.5 15.4 %collective-permute-start.46 = (f32[656,128]{1,0:T(8,128)}, f32[656,128]{1,0:T(8,128)S(1)}, u32[]{:S(2)}, u32[]{:S(2)}) collective-permute-start(f32[656,128]{1,0:T(8,128)} %collective-permute-done.45.refs_26_), channel_id=1, source_target_pairs={{16,18},{18,16},{20,22},{22,20},{24,26},{26,24},{28,30},{30,28},{1... | collective-permute-start | bytes 1007624 | tf_op jit(solution)/shard_map/ppermute | solution.py:75
  208.2 17.2 %collective-permute-start.47 = (f32[656,128]{1,0:T(8,128)}, f32[656,128]{1,0:T(8,128)S(1)}, u32[]{:S(2)}, u32[]{:S(2)}) collective-permute-start(f32[656,128]{1,0:T(8,128)} %collective-permute-done.45.refs_26_), channel_id=1, source_target_pairs={{16,20},{18,22},{20,16},{22,18},{24,28},{26,30},{28,24},{30,26},{1... | collective-permute-start | bytes 1007624 | tf_op jit(solution)/shard_map/ppermute | solution.py:75
  208.9 17.2 %collective-permute-start.53 = (f32[656,128]{1,0:T(8,128)}, f32[656,128]{1,0:T(8,128)S(1)}, u32[]{:S(2)}, u32[]{:S(2)}) collective-permute-start(f32[656,128]{1,0:T(8,128)} %collective-permute-done.45.refs_26_), channel_id=1, source_target_pairs={{16,24},{18,26},{20,28},{22,30},{17,25},{19,27},{21,29},{23,31}} | collective-permute-start | bytes 1007624 | tf_op jit(solution)/shard_map/ppermute | solution.py:75
  216.5 4.0 %collective-permute-start.44 = (f32[656,128]{1,0:T(8,128)}, f32[656,128]{1,0:T(8,128)S(1)}, u32[]{:S(2)}, u32[]{:S(2)}) collective-permute-start(f32[656,128]{1,0:T(8,128)} %collective-permute-done.43.refs_24_), channel_id=1, source_target_pairs={{0,2},{2,0},{4,6},{6,4},{8,10},{10,8},{12,14},{14,12},{16,18},{18,... | collective-permute-start | bytes 1007624 | tf_op jit(solution)/shard_map/ppermute | solution.py:75
  218.4 12.4 %collective-permute-start.57 = (f32[656,128]{1,0:T(8,128)}, f32[656,128]{1,0:T(8,128)S(1)}, u32[]{:S(2)}, u32[]{:S(2)}) collective-permute-start(f32[656,128]{1,0:T(8,128)} %collective-permute-done.49.refs_30_), channel_id=1, source_target_pairs={{8,0},{10,2},{12,4},{14,6},{9,1},{11,3},{13,5},{15,7}} | collective-permute-start | bytes 1007624 | tf_op jit(solution)/shard_map/ppermute | solution.py:75
  220.5 13.4 %collective-permute-start.50 = (f32[656,128]{1,0:T(8,128)}, f32[656,128]{1,0:T(8,128)S(1)}, u32[]{:S(2)}, u32[]{:S(2)}) collective-permute-start(f32[656,128]{1,0:T(8,128)} %collective-permute-done.49.refs_30_), channel_id=1, source_target_pairs={{0,2},{2,0},{4,6},{6,4},{8,10},{10,8},{12,14},{14,12},{1,3},{3,1},... | collective-permute-start | bytes 1007624 | tf_op jit(solution)/shard_map/ppermute | solution.py:75
  223.0 11.9 %collective-permute-start.51 = (f32[656,128]{1,0:T(8,128)}, f32[656,128]{1,0:T(8,128)S(1)}, u32[]{:S(2)}, u32[]{:S(2)}) collective-permute-start(f32[656,128]{1,0:T(8,128)} %collective-permute-done.49.refs_30_), channel_id=1, source_target_pairs={{0,4},{2,6},{4,0},{6,2},{8,12},{10,14},{12,8},{14,10},{1,5},{3,7},... | collective-permute-start | bytes 1007624 | tf_op jit(solution)/shard_map/ppermute | solution.py:75
  225.4 11.4 %collective-permute-start.48 = (f32[656,128]{1,0:T(8,128)S(1)}, f32[656,128]{1,0:T(8,128)S(1)}, u32[]{:S(2)}, u32[]{:S(2)}) collective-permute-start(f32[656,128]{1,0:T(8,128)S(1)} %collective-permute-done.47.refs_28_), channel_id=1, source_target_pairs={{16,18},{18,16},{20,22},{22,20},{24,26},{26,24},{28,30},{30,28},{1... | collective-permute-start | bytes 1007624 | tf_op jit(solution)/shard_map/ppermute | solution.py:75
  226.1 13.1 %collective-permute-start.55 = (f32[656,128]{1,0:T(8,128)S(1)}, f32[656,128]{1,0:T(8,128)S(1)}, u32[]{:S(2)}, u32[]{:S(2)}) collective-permute-start(f32[656,128]{1,0:T(8,128)S(1)} %collective-permute-done.53.refs_34_), channel_id=1, source_target_pairs={{24,28},{26,30},{28,24},{30,26},{25,29},{27,31},{29,25},{31,27}} | collective-permute-start | bytes 1007624 | tf_op jit(solution)/shard_map/ppermute | solution.py:75
  230.8 11.4 %collective-permute-start.59 = (f32[656,128]{1,0:T(8,128)S(1)}, f32[656,128]{1,0:T(8,128)S(1)}, u32[]{:S(2)}, u32[]{:S(2)}) collective-permute-start(f32[656,128]{1,0:T(8,128)S(1)} %collective-permute-done.57.refs_38_), channel_id=1, source_target_pairs={{0,4},{2,6},{4,0},{6,2},{1,5},{3,7},{5,1},{7,3}} | collective-permute-start | bytes 1007624 | tf_op jit(solution)/shard_map/ppermute | solution.py:75
  233.9 11.3 %collective-permute-start.54 = (f32[656,128]{1,0:T(8,128)S(1)}, f32[656,128]{1,0:T(8,128)S(1)}, u32[]{:S(2)}, u32[]{:S(2)}) collective-permute-start(f32[656,128]{1,0:T(8,128)S(1)} %collective-permute-done.53.refs_34_), channel_id=1, source_target_pairs={{24,26},{26,24},{28,30},{30,28},{25,27},{27,25},{29,31},{31,29}} | collective-permute-start | bytes 1007624 | tf_op jit(solution)/shard_map/ppermute | solution.py:75
  234.9 10.4 %collective-permute-start.58 = (f32[656,128]{1,0:T(8,128)S(1)}, f32[656,128]{1,0:T(8,128)S(1)}, u32[]{:S(2)}, u32[]{:S(2)}) collective-permute-start(f32[656,128]{1,0:T(8,128)S(1)} %collective-permute-done.57.refs_38_), channel_id=1, source_target_pairs={{0,2},{2,0},{4,6},{6,4},{1,3},{3,1},{5,7},{7,5}} | collective-permute-start | bytes 1007624 | tf_op jit(solution)/shard_map/ppermute | solution.py:75
  236.8 8.4 %collective-permute-start.52 = (f32[656,128]{1,0:T(8,128)S(1)}, f32[656,128]{1,0:T(8,128)S(1)}, u32[]{:S(2)}, u32[]{:S(2)}) collective-permute-start(f32[656,128]{1,0:T(8,128)S(1)} %collective-permute-done.51.refs_32_), channel_id=1, source_target_pairs={{0,2},{2,0},{4,6},{6,4},{8,10},{10,8},{12,14},{14,12},{1,3},{3,1},... | collective-permute-start | bytes 1007624 | tf_op jit(solution)/shard_map/ppermute | solution.py:75
  239.2 6.0 %collective-permute-start.56 = (f32[656,128]{1,0:T(8,128)S(1)}, f32[656,128]{1,0:T(8,128)S(1)}, u32[]{:S(2)}, u32[]{:S(2)}) collective-permute-start(f32[656,128]{1,0:T(8,128)S(1)} %collective-permute-done.55.refs_36_), channel_id=1, source_target_pairs={{24,26},{26,24},{28,30},{30,28},{25,27},{27,25},{29,31},{31,29}} | collective-permute-start | bytes 1007624 | tf_op jit(solution)/shard_map/ppermute | solution.py:75
  242.2 3.5 %collective-permute-start.60 = (f32[656,128]{1,0:T(8,128)S(1)}, f32[656,128]{1,0:T(8,128)S(1)}, u32[]{:S(2)}, u32[]{:S(2)}) collective-permute-start(f32[656,128]{1,0:T(8,128)S(1)} %collective-permute-done.59.refs_40_), channel_id=1, source_target_pairs={{0,2},{2,0},{4,6},{6,4},{1,3},{3,1},{5,7},{7,5}} | collective-permute-start | bytes 1007624 | tf_op jit(solution)/shard_map/ppermute | solution.py:75
  (41 other events, 543.0 us)

commit v3 on v2

v3 whole, which is shorter than its diff:
```python
import functools

import jax
import jax.numpy as jnp
from jax import lax
from jax.experimental import pallas as pl
from jax.experimental.pallas import tpu as pltpu
from jax.sharding import PartitionSpec as P

D = 1024
NTAB = 8
NKEYS = 256
KDIM = 128
LANE = 128
VROW_DEV = 512

beta_one = 0.9
beta_two = 0.99
bias_one = 1.0 - 0.9**4
bias_two = 1.0 - 0.99**4
epsilon = 1e-06
learning = 0.02
decay_rate = 0.01
matrices = 5
MIB = 1 << 20


def matrix_bounds(narrow):
    query_blocks = D * D // (LANE * narrow)
    key_blocks = NTAB * NKEYS * KDIM // (LANE * narrow)
    value_blocks = VROW_DEV * D // LANE
    return (
        query_blocks,
        query_blocks + key_blocks,
        query_blocks + key_blocks + value_blocks,
        2 * query_blocks + key_blocks + value_blocks,
    )


class Plan:
    def __init__(self, replicas, narrow, blocks):
        self.replicas, self.narrow, self.blocks = replicas, narrow, blocks
        chips = replicas // 2
        self.nz = 4 if chips % 4 == 0 else chips
        self.nx = chips // self.nz
        assert self.nz in (1, 2, 4) and self.nx in (1, 2, 4)
        self.own = blocks // replicas
        self.tail = 8
        self.norm_rows = 2 * D // LANE
        self.norm_each = -(-self.norm_rows // replicas)
        self.block = self.own + self.tail
        self.group = self.nx * self.block
        self.half = self.nz * self.group
        self.lists = -(-blocks // (8 * LANE)) * 8
        self.bounds = matrix_bounds(narrow)

    def index(self, z, x, c):
        return (z * self.nx + x) * 2 + c

    def start(self, far_z, far_x, far_c):
        return (1 - far_c) * self.half + far_z * self.group + far_x * self.block

    def send(self, value, axis, pairs):
        every = []
        for z in range(self.nz):
            for x in range(self.nx):
                for c in range(2):
                    here = {"z": z, "x": x, "c": c}
                    for source, target in pairs:
                        if here[axis] == source:
                            every.append((self.index(z, x, c), self.index(**{**here, axis: target})))
        return lax.ppermute(value, "dp", every)

    def swap(self, value):
        return self.send(value, "c", PAIR)


PAIR = [(0, 1), (1, 0)]
PAIRS = [(0, 1), (1, 0), (2, 3), (3, 2)]
MIDDLE = [(1, 2), (2, 1)]
INWARD = [(0, 1), (3, 2)]
OUTWARD = [(1, 0), (2, 3)]


def line_reduce(plan, axis, blocks):
    if len(blocks) == 1:
        return [blocks[0]]
    if len(blocks) == 2:
        return [blocks[0], plan.send(blocks[1], axis, PAIR)]
    in_three = plan.send(blocks[3], axis, INWARD)
    in_two = plan.send(blocks[2], axis, INWARD)
    across_two = plan.send(blocks[2] + in_three, axis, MIDDLE)
    across_three = plan.send(blocks[3] + in_two, axis, MIDDLE)
    pair = plan.send(blocks[1] + across_two, axis, PAIRS)
    return [blocks[0], pair, across_three]


def line_gather(plan, axis, count, value):
    if count == 1:
        return [value]
    if count == 2:
        return [value, plan.send(value, axis, PAIR)]
    pair = plan.send(value, axis, PAIRS)
    across_three = plan.send(value, axis, MIDDLE)
    across_two = plan.send(pair, axis, MIDDLE)
    out_two = plan.send(across_three, axis, OUTWARD)
    out_three = plan.send(across_two, axis, OUTWARD)
    return [value, pair, across_two + out_two, across_three + out_three]


def place_kernel(plan, place_ref, owner_ref, norm_ref, grads_ref, *refs):
    out_refs, refs = refs[: 2 * plan.nz], refs[2 * plan.nz :]
    position_ref, raw, moved, position, sem_in, sem_position, sem_out = refs
    fetch = pltpu.make_async_copy(grads_ref, raw, sem_in)
    fetch.start()
    lists = plan.lists
    owners = owner_ref[...]
    my_z, my_x, my_c = place_ref[0], place_ref[1], place_ref[2]
    lane_in = lax.broadcasted_iota(jnp.int32, (LANE, LANE), 0)
    lane_out = lax.broadcasted_iota(jnp.int32, (LANE, LANE), 1)
    before = (lane_in < lane_out).astype(jnp.bfloat16)
    every = jnp.ones((LANE, LANE), jnp.bfloat16)
    row_out = lax.broadcasted_iota(jnp.int32, (lists, lists), 0)
    row_in = lax.broadcasted_iota(jnp.int32, (lists, lists), 1)
    above = (row_in < row_out).astype(jnp.bfloat16)
    result = jnp.zeros((lists, LANE), jnp.int32)
    for z in range(plan.nz):
        for x in range(plan.nx):
            for c in range(2):
                mine = owners == plan.index(z, x, c)
                flags = mine.astype(jnp.float32).astype(jnp.bfloat16)
                inner = jnp.dot(flags, before, preferred_element_type=jnp.float32)
                totals = jnp.dot(flags, every, preferred_element_type=jnp.float32)
                outer = jnp.dot(above, totals.astype(jnp.bfloat16), preferred_element_type=jnp.float32)
                rank = (inner + outer).astype(jnp.int32)
                start = plan.start(my_z ^ z, my_x ^ x, my_c ^ c)
                first_norm = plan.index(z, x, c) * plan.norm_each
                tail = [jnp.zeros((plan.tail, LANE), jnp.float32)]
                for row in range(min(first_norm + plan.norm_each, plan.norm_rows) - 1, first_norm - 1, -1):
                    part = norm_ref[row * LANE // D : row * LANE // D + 1, row * LANE % D : row * LANE % D + LANE]
                    tail.insert(0, part.astype(jnp.float32))
                tail = jnp.concatenate(tail, 0)[: plan.tail]
                moved[pl.ds(pl.multiple_of(start + plan.own, 8), plan.tail), :] = tail
                result = jnp.where(mine, rank + start, result)
    position_ref[...] = result
    to_scalar = pltpu.make_async_copy(position_ref, position, sem_position)
    to_scalar.start()
    to_scalar.wait()
    fetch.wait()

    @pl.loop(0, plan.blocks // LANE)
    def _(line):
        for part in range(0, LANE, 16):
            rows = raw[pl.ds(pl.multiple_of(line * LANE + part, 16), 16), :].astype(jnp.float32)
            for u in range(16):
                moved[pl.ds(position[line, part + u], 1), :] = rows[u : u + 1, :]

    copies = []
    for i, out in enumerate(out_refs):
        start = (i // plan.nz) * plan.half + (plan.nz - 1 - i % plan.nz) * plan.group
        copies.append(pltpu.make_async_copy(moved.at[pl.ds(start, plan.group)], out, sem_out.at[i]))
    for copy in copies:
        copy.start()
    for copy in copies:
        copy.wait()


def place(plan, my_place, owners, norm_grads, grads):
    shapes = [(plan.group, LANE)] * (2 * plan.nz)
    outs = pl.pallas_call(
        functools.partial(place_kernel, plan),
        out_shape=[jax.ShapeDtypeStruct(s, jnp.float32) for s in shapes]
        + [jax.ShapeDtypeStruct((plan.lists, LANE), jnp.int32)],
        in_specs=[
            pl.BlockSpec(memory_space=pltpu.SMEM),
            pl.BlockSpec(memory_space=pltpu.VMEM),
            pl.BlockSpec(memory_space=pltpu.VMEM),
            pl.BlockSpec(memory_space=pl.ANY),
        ],
        out_specs=[pl.BlockSpec(memory_space=pl.ANY)] * len(shapes) + [pl.BlockSpec(memory_space=pltpu.VMEM)],
        scratch_shapes=[
            pltpu.VMEM((plan.blocks, LANE), jnp.bfloat16),
            pltpu.VMEM((2 * plan.half, LANE), jnp.float32),
            pltpu.SMEM((plan.lists, LANE), jnp.int32),
            pltpu.SemaphoreType.DMA,
            pltpu.SemaphoreType.DMA,
            pltpu.SemaphoreType.DMA((len(shapes),)),
        ],
        compiler_params=pltpu.CompilerParams(vmem_limit_bytes=58 * MIB),
        name="place_gradients",
    )(my_place, owners, norm_grads, grads)
    return outs[: plan.nz][::-1], outs[plan.nz : 2 * plan.nz][::-1], outs[-1]


def owned_kernel(plan, place_ref, owner_ref, weights_ref, owned_ref, natural_ref, held, listed, order, sem_in, sem_order):
    fetch = pltpu.make_async_copy(weights_ref, held, sem_in)
    fetch.start()
    lists = plan.lists
    me = plan.index(place_ref[0], place_ref[1], place_ref[2])
    flags = (owner_ref[...] == me).astype(jnp.float32).astype(jnp.bfloat16)
    lane_in = lax.broadcasted_iota(jnp.int32, (LANE, LANE), 0)
    lane_out = lax.broadcasted_iota(jnp.int32, (LANE, LANE), 1)
    upto = (lane_in <= lane_out).astype(jnp.float32).astype(jnp.bfloat16)
    inner = jnp.dot(flags, upto, preferred_element_type=jnp.float32).astype(jnp.bfloat16)
    totals = lax.dot_general(
        jnp.ones((8, LANE), jnp.bfloat16), flags, (((1,), (1,)), ((), ())), preferred_element_type=jnp.float32
    )
    row_in = lax.broadcasted_iota(jnp.int32, (lists, lists), 0)
    row_out = lax.broadcasted_iota(jnp.int32, (lists, lists), 1)
    upto = (row_in <= row_out).astype(jnp.float32).astype(jnp.bfloat16)
    ends = jnp.dot(totals.astype(jnp.bfloat16), upto, preferred_element_type=jnp.float32)[0:1, :]
    place_of = lax.broadcasted_iota(jnp.int32, (LANE, lists), 1).astype(jnp.float32)
    rank_of = lax.broadcasted_iota(jnp.int32, (LANE, 1), 0)
    for step in range(listed.shape[0]):
        if step * LANE >= plan.own:
            break
        rank = (rank_of + step * LANE).astype(jnp.float32)
        passed = ends <= rank
        line = jnp.sum(passed.astype(jnp.float32), axis=1, keepdims=True)
        before = jnp.max(jnp.where(passed, ends, 0.0), axis=1, keepdims=True)
        chosen = (place_of == line).astype(jnp.float32).astype(jnp.bfloat16)
        counts = jnp.dot(chosen, inner, preferred_element_type=jnp.float32)
        column = jnp.sum((counts <= rank - before).astype(jnp.float32), axis=1, keepdims=True)
        block = jnp.broadcast_to((line * LANE + column).astype(jnp.int32), (LANE, LANE))
        natural_ref[step * LANE : (step + 1) * LANE, :] = block
        listed[step : step + 1, :] = jnp.sum(jnp.where(lane_in == lane_out, block, 0), axis=0, keepdims=True)
    to_scalar = pltpu.make_async_copy(listed, order, sem_order)
    to_scalar.start()
    to_scalar.wait()
    fetch.wait()

    def pick(line, count):
        for u in range(count):
            owned_ref[pl.ds(line * LANE + u, 1), :] = held[pl.ds(order[line, u], 1), :]

    @pl.loop(0, plan.own // LANE)
    def _(line):
        pick(line, LANE)

    if plan.own % LANE:
        pick(plan.own // LANE, plan.own % LANE)


def owned(plan, my_place, owners, weights):
    high_rows = -(-plan.own // (8 * LANE)) * 8
    ranks = -(-plan.own // LANE) * LANE
    vmem = pl.BlockSpec(memory_space=pltpu.VMEM)
    return pl.pallas_call(
        functools.partial(owned_kernel, plan),
        out_shape=[
            jax.ShapeDtypeStruct((plan.own, LANE), jnp.float32),
            jax.ShapeDtypeStruct((ranks, LANE), jnp.int32),
        ],
        in_specs=[pl.BlockSpec(memory_space=pltpu.SMEM), vmem, pl.BlockSpec(memory_space=pl.ANY)],
        out_specs=[vmem] * 2,
        scratch_shapes=[
            pltpu.VMEM((plan.blocks, LANE), jnp.float32),
            pltpu.VMEM((high_rows, LANE), jnp.int32),
            pltpu.SMEM((high_rows, LANE), jnp.int32),
            pltpu.SemaphoreType.DMA,
            pltpu.SemaphoreType.DMA,
        ],
        compiler_params=pltpu.CompilerParams(vmem_limit_bytes=58 * MIB),
        cost_estimate=pl.CostEstimate(flops=0, bytes_accessed=20 * MIB, transcendentals=0),
        name="owned_weights",
    )(my_place, owners, weights)


def update_kernel(plan, terms, *refs):
    parts, refs = refs[:terms], refs[terms:]
    first_ref, second_ref, weight_ref, natural_ref = refs[:4]
    new_first_ref, new_second_ref, block_ref, stats_ref = refs[4:]
    gradient = parts[0][: plan.block, :]
    for part in parts[1:]:
        gradient = gradient + part[: plan.block, :]
    block_ref[plan.own :, :] = gradient[plan.own :, :]
    gradient = gradient[: plan.own, :]
    moment_one = beta_one * first_ref[...] + (1.0 - beta_one) * gradient
    moment_two = beta_two * second_ref[...] + (1.0 - beta_two) * gradient * gradient
    new_first_ref[...] = moment_one
    new_second_ref[...] = moment_two
    step = moment_one / bias_one / (jnp.sqrt(moment_two / bias_two) + epsilon)
    block_ref[: plan.own, :] = step
    weight = weight_ref[...]
    direction = step + decay_rate * weight
    natural = natural_ref[: plan.own, :]
    limits = (0,) + plan.bounds + (plan.blocks,)
    lane = lax.broadcasted_iota(jnp.int32, (8, LANE), 1)
    rank = lax.broadcasted_iota(jnp.int32, (8, LANE), 0)
    stats = jnp.zeros((8, LANE), jnp.float32)
    for column, squares in enumerate((weight * weight, direction * direction)):
        for k in range(matrices):
            inside = (natural >= limits[k]) & (natural < limits[k + 1])
            kept = jnp.where(inside, squares, 0.0).reshape(plan.own // 8, 8, LANE)
            total = jnp.sum(jnp.sum(kept, axis=0))
            stats = jnp.where((rank == plan.norm_each + k) & (lane == column), total, stats)
    stats_ref[...] = stats


def update(plan, parts, first, second, weight, natural):
    vmem = pl.BlockSpec(memory_space=pltpu.VMEM)
    shapes = [(plan.own, LANE), (plan.own, LANE), (plan.block, LANE), (plan.tail, LANE)]
    return pl.pallas_call(
        functools.partial(update_kernel, plan, len(parts)),
        out_shape=[jax.ShapeDtypeStruct(s, jnp.float32) for s in shapes],
        in_specs=[vmem] * (len(parts) + 4),
        out_specs=[vmem] * len(shapes),
        compiler_params=pltpu.CompilerParams(vmem_limit_bytes=58 * MIB),
        name="moments",
    )(*parts, first, second, weight, natural)


def tails_kernel(plan, slots, place_ref, *refs):
    pieces, refs = refs[: len(slots)], refs[len(slots) :]
    norm_ref, ratio_ref, held, sems = refs
    copies = []
    for i, (piece, (far_z, far_x, far_c)) in enumerate(zip(pieces, slots)):
        d = plan.index(place_ref[0] ^ far_z, place_ref[1] ^ far_x, place_ref[2] ^ far_c)
        copies.append(pltpu.make_async_copy(piece.at[pl.ds(plan.own, plan.tail)], held.at[d], sems.at[i]))
    for copy in copies:
        copy.start()
    for copy in copies:
        copy.wait()
    total = held[0]
    for d in range(1, plan.replicas):
        total = total + held[d]
    for row in range(plan.norm_rows):
        norm_ref[row : row + 1, :] = held[row // plan.norm_each, pl.ds(row % plan.norm_each, 1), :]
    for k in range(matrices):
        row = plan.norm_each + k
        weight_square, direction_square = total[row : row + 1, 0:1], total[row : row + 1, 1:2]
        ratio = jnp.sqrt(weight_square) / (jnp.sqrt(direction_square) + epsilon)
        ratio_ref[k : k + 1, :] = jnp.broadcast_to(ratio, (1, LANE))


def tails(plan, my_place, pieces, slots):
    vmem = pl.BlockSpec(memory_space=pltpu.VMEM)
    return pl.pallas_call(
        functools.partial(tails_kernel, plan, slots),
        out_shape=[
            jax.ShapeDtypeStruct((plan.norm_rows, LANE), jnp.float32),
            jax.ShapeDtypeStruct((matrices, LANE), jnp.float32),
        ],
        in_specs=[pl.BlockSpec(memory_space=pltpu.SMEM)] + [pl.BlockSpec(memory_space=pl.ANY)] * len(pieces),
        out_specs=[vmem, vmem],
        scratch_shapes=[
            pltpu.VMEM((plan.replicas, plan.tail, LANE), jnp.float32),
            pltpu.SemaphoreType.DMA((len(pieces),)),
        ],
        name="tails",
    )(my_place, *pieces)


def finish_kernel(plan, tile, slots, position_ref, rates_ref, weights_ref, *refs):
    pieces, refs = refs[: len(slots)], refs[len(slots) :]
    out_ref, held, sems = refs
    now = pl.program_id(0)

    @pl.when(now == 0)
    def _():
        copies = [
            pltpu.make_async_copy(piece, held.at[pl.ds(plan.start(*slot), plan.block)], sems.at[i])
            for i, (piece, slot) in enumerate(zip(pieces, slots))
        ]
        for copy in copies:
            copy.start()
        for copy in copies:
            copy.wait()

    matrix = jnp.int32(0)
    for bound in plan.bounds:
        matrix = matrix + (now * tile >= bound).astype(jnp.int32)
    rate = rates_ref[matrix]
    lines = tile // LANE

    @pl.loop(0, lines)
    def _(line):
        for group in range(0, LANE, 8):
            rows = [held[pl.ds(position_ref[now * lines + line, group + u], 1), :] for u in range(8)]
            here = pl.ds(pl.multiple_of(line * LANE + group, 8), 8)
            weight = weights_ref[here, :]
            direction = jnp.concatenate(rows, 0) + decay_rate * weight
            out_ref[here, :] = weight - rate * direction


def finish(plan, position, rates, weights, pieces, slots):
    tile = LANE
    while tile < 1024 and all(b % (2 * tile) == 0 for b in plan.bounds + (plan.blocks,)):
        tile *= 2
    smem = pl.BlockSpec(memory_space=pltpu.SMEM)
    return pl.pallas_call(
        functools.partial(finish_kernel, plan, tile, slots),
        grid=(plan.blocks // tile,),
        out_shape=jax.ShapeDtypeStruct((plan.blocks, LANE), jnp.float32),
        in_specs=[smem, smem, pl.BlockSpec((tile, LANE), lambda i: (i, 0))]
        + [pl.BlockSpec(memory_space=pl.ANY)] * len(pieces),
        out_specs=pl.BlockSpec((tile, LANE), lambda i: (i, 0)),
        scratch_shapes=[
            pltpu.VMEM((2 * plan.half, LANE), jnp.float32),
            pltpu.SemaphoreType.DMA((len(pieces),)),
        ],
        compiler_params=pltpu.CompilerParams(vmem_limit_bytes=58 * MIB),
        name="new_weights",
    )(position, rates, weights, *pieces)


def adam_step(gradient, moment_one, moment_two, weight):
    moment_one = beta_one * moment_one + (1.0 - beta_one) * gradient
    moment_two = beta_two * moment_two + (1.0 - beta_two) * gradient * gradient
    step = moment_one / bias_one / (jnp.sqrt(moment_two / bias_two) + epsilon) + decay_rate * weight
    return (moment_one, moment_two, step)


def local(gradients, weights, first_moment, second_moment, owner_list, norm_grads, norm_state):
    plan = Plan(lax.axis_size("dp"), lax.axis_size("mp"), weights.shape[0])
    me = lax.axis_index("dp").astype(jnp.int32)
    my_place = jnp.stack([me // (2 * plan.nx), (me // 2) % plan.nx, me % 2]).astype(jnp.int32)
    owners = jnp.pad(owner_list[0], (0, plan.lists * LANE - plan.blocks), constant_values=-1)
    owners = owners.reshape(plan.lists, LANE)
    siblings, blocks, position = place(plan, my_place, owners, norm_grads[0], gradients[0])
    weight_own, natural = owned(plan, my_place, owners, weights)

    others = [None] * plan.nz
    for z in reversed(range(plan.nz)):
        others[z] = plan.swap(siblings[z])
    near = []
    for z in reversed(range(plan.nz)):
        parts = [
            blocks[z][x * plan.block : (x + 1) * plan.block] + others[z][x * plan.block : (x + 1) * plan.block]
            for x in range(1, plan.nx)
        ]
        terms = line_reduce(plan, "x", [None] + parts)[1:]
        if z:
            mine = blocks[z][: plan.block] + others[z][: plan.block]
            near.insert(0, sum(terms, mine))
        else:
            near.insert(0, None)
            near_terms = [blocks[z], others[z]] + terms
    parts = near_terms + line_reduce(plan, "z", near)[1:]
    new_first, new_second, block, stats = update(
        plan, parts, first_moment[0], second_moment[0], weight_own, natural
    )

    hop = 1
    while hop < plan.narrow:
        stats = stats + lax.ppermute(stats, "mp", [(i, i ^ hop) for i in range(plan.narrow)])
        hop *= 2
    block = lax.dynamic_update_slice(block, block[plan.own :] + stats, (plan.own, 0))
    pieces, slots = [], []
    for far_z, value in enumerate(line_gather(plan, "z", plan.nz, block)):
        for far_x, piece in enumerate(line_gather(plan, "x", plan.nx, value)):
            pieces += [piece, plan.swap(piece)]
            slots += [(far_z, far_x, 0), (far_z, far_x, 1)]
    norm_sum, ratios = tails(plan, my_place, pieces, slots)
    norm_sum, ratios = norm_sum.reshape(norm_grads.shape[1:]), ratios[:, 0]
    new_weights = finish(plan, position, learning * ratios, weights, pieces, slots)

    gain_rows = norm_state[0]
    norm_one, norm_two, norm_update = adam_step(norm_sum, norm_state[1], norm_state[2], gain_rows)
    norm_ratio = jnp.sqrt(jnp.sum(gain_rows * gain_rows, axis=1)) / (
        jnp.sqrt(jnp.sum(norm_update * norm_update, axis=1)) + epsilon
    )
    new_gains = gain_rows - learning * norm_ratio[:, None] * norm_update
    new_state = jnp.stack([new_gains, norm_one, norm_two])
    trust_ratios = jnp.concatenate([ratios, norm_ratio])
    return (new_weights, new_first[None], new_second[None], new_state, trust_ratios)


def solution(mesh):
    in_specs = (
        P("dp", "mp", None),
        P("mp", None),
        P("mp", "dp", None),
        P("mp", "dp", None),
        P("mp", None),
        P("dp", None, None),
        P(),
    )
    out_specs = (P("mp", None), P("mp", "dp", None), P("mp", "dp", None), P(), P())
    return jax.shard_map(local, mesh=mesh, in_specs=in_specs, out_specs=out_specs, check_vma=False)
```

time: 274 us -> 215 us (0.78)
  starting transfers between devices: 106 us -> 47.6 us
  waiting for transfers between devices: 84.6 us -> 92.6 us
  Pallas kernels: 68.7 us -> 62.9 us
    ppermute x60 -> x30, starting transfers between devices: 104 us -> 46.1 us  [send(): return lax.ppermute(value, 'dp', every)]
    pallas_call x1, Pallas kernels: 14.6 us -> 6.33 us  [owned(): pl.pallas_call(functools.partial(owned_kernel, plan), out_shape=[jax.Shap...]
    ppermute x60 -> x30, waiting for transfers between devices: 82.5 us -> 90.3 us  [send(): return lax.ppermute(value, 'dp', every)]
  transfers between devices with their start and end apart: 61 -> 31, of which waited for: 19 -> 16; matrix products, arithmetic and copies ran while one was open for 2% -> 1% of each run, Pallas kernels for 6% -> 3%
where the time goes in v3:
time: 215 us; the launch traced here: 214 us
  waiting for transfers between devices  92.6 us (43%)
  Pallas kernels  62.9 us (29%)
  starting transfers between devices  47.6 us (22%)
  other arithmetic  5.98 us (3%)
  local copies, waits for them, and re-layouts  4.11 us (2%)
    ppermute x30, waiting for transfers between devices, send(): return lax.ppermute(value, 'dp', every)  90.3 us
    ppermute x30, starting transfers between devices, send(): return lax.ppermute(value, 'dp', every)  46.1 us
    pallas_call x1, Pallas kernels, finish(): pl.pallas_call(functools.partial(finish_kernel, plan, tile, slots), grid=...  25 us
    pallas_call x1, Pallas kernels, place(): pl.pallas_call(functools.partial(place_kernel, plan), out_shape=[jax.Shap...  23.9 us
    pallas_call x1, Pallas kernels, owned(): pl.pallas_call(functools.partial(owned_kernel, plan), out_shape=[jax.Shap...  6.33 us
    pallas_call x1, Pallas kernels, update(): pl.pallas_call(functools.partial(update_kernel, plan, len(parts)), out_sh...  5.34 us
  transfers between devices with their start and end apart: 31, of which 16 were waited for; matrix products, arithmetic and copies ran while one was open for 1% of the time, Pallas kernels for 3%

profile of v3, /device:TPU:0, one launch (start us, length us, event | category | flops | bytes accessed | tf_op | source)
XLA Modules:
  0.0 214.4 jit_solution(6510422201511926915)
XLA Ops:
  0.7 0.6 pad_add_fusion.place_ref
  1.3 23.9 %place_gradients.1 = (f32[2192,128]{1,0:T(8,128)}, f32[2192,128]{1,0:T(8,128)}, f32[2192,128]{1,0:T(8,128)}, f32[2192,128]{1,0:T(8,128)}, f32[2192,128]{1,0:T(8,...) custom-call(s32[3]{0:T(128)} %pad_add_fusion.place_ref, ...), custom_call_target="tpu_custom_call" | custom-call | tf_op jit(solution)/shard_map/place_gradients/pallas_call | solution.py:170
  25.3 0.5 collective-permute-start.4
  25.8 2.5 %collective-permute-done.4 = f32[2192,128]{1,0:T(8,128)S(1)} collective-permute-done((f32[2192,128]{1,0:T(8,128)}, f32[2192,128]{1,0:T(8,128)S(1)}, u32[]{:S(2)}, u32[]{:S(2)}) %collective-permute-start.4) | collective-permute-done | bytes 1122336 | tf_op jit(solution)/shard_map/ppermute | solution.py:72
  28.4 1.1 slice_add_fusion.2
  29.5 2.9 %collective-permute-start.5 = (f32[1096,128]{1,0:T(8,128)S(1)}, f32[1096,128]{1,0:T(8,128)S(1)}, u32[]{:S(2)}, u32[]{:S(2)}) collective-permute-start(f32[1096,128]{1,0:T(8,128)S(1)} %slice_add_fusion.2), channel_id=1, source_target_pairs={{0,4},{2,6},{4,0},{6,2},{8,12},{10,14},{12,8},{14,10},{16,20},{18,... | collective-permute-start | bytes 1683464 | tf_op jit(solution)/shard_map/ppermute | solution.py:72
  32.5 0.5 collective-permute-start.7
  33.0 12.9 %collective-permute-done.5 = f32[1096,128]{1,0:T(8,128)S(1)} collective-permute-done((f32[1096,128]{1,0:T(8,128)S(1)}, f32[1096,128]{1,0:T(8,128)S(1)}, u32[]{:S(2)}, u32[]{:S(2)}) %collective-permute-start.5) | collective-permute-done | bytes 561184 | tf_op jit(solution)/shard_map/ppermute | solution.py:72
  45.9 0.1 fusion.1
  46.0 4.1 %collective-permute-start.11 = (f32[1096,128]{1,0:T(8,128)S(1)}, f32[1096,128]{1,0:T(8,128)S(1)}, u32[]{:S(2)}, u32[]{:S(2)}) collective-permute-start(f32[1096,128]{1,0:T(8,128)S(1)} %fusion.1), channel_id=1, source_target_pairs={{0,8},{2,10},{4,12},{6,14},{24,16},{26,18},{28,20},{30,22},{1,9},{... | collective-permute-start | bytes 1683464 | tf_op jit(solution)/shard_map/ppermute | solution.py:72
  50.2 0.5 collective-permute-start
  50.7 6.7 %collective-permute-done.7 = f32[1096,128]{1,0:T(8,128)S(1)} collective-permute-done((f32[1096,128]{1,0:T(8,128)S(1)}, f32[1096,128]{1,0:T(8,128)S(1)}, u32[]{:S(2)}, u32[]{:S(2)}) %collective-permute-start.7) | collective-permute-done | bytes 561184 | tf_op jit(solution)/shard_map/ppermute | solution.py:72
  57.5 3.3 %collective-permute-done.11 = f32[1096,128]{1,0:T(8,128)S(1)} collective-permute-done((f32[1096,128]{1,0:T(8,128)S(1)}, f32[1096,128]{1,0:T(8,128)S(1)}, u32[]{:S(2)}, u32[]{:S(2)}) %collective-permute-start.11) | collective-permute-done | bytes 561184 | tf_op jit(solution)/shard_map/ppermute | solution.py:72
  60.7 0.1 fusion.13
  60.9 4.4 %collective-permute-start.8 = (f32[1096,128]{1,0:T(8,128)S(1)}, f32[1096,128]{1,0:T(8,128)S(1)}, u32[]{:S(2)}, u32[]{:S(2)}) collective-permute-start(f32[1096,128]{1,0:T(8,128)S(1)} %get-tuple-element.45), channel_id=1, source_target_pairs={{0,8},{2,10},{4,12},{6,14},{24,16},{26,18},{28,20},{30,22},{1,9},{... | collective-permute-start | bytes 1683464 | tf_op jit(solution)/shard_map/ppermute | solution.py:72
  65.4 1.6 collective-permute-start.3
  67.0 8.0 %collective-permute-done.8 = f32[1096,128]{1,0:T(8,128)S(1)} collective-permute-done((f32[1096,128]{1,0:T(8,128)S(1)}, f32[1096,128]{1,0:T(8,128)S(1)}, u32[]{:S(2)}, u32[]{:S(2)}) %collective-permute-start.8) | collective-permute-done | bytes 561184 | tf_op jit(solution)/shard_map/ppermute | solution.py:72
  75.0 0.1 add.110
  75.1 0.7 collective-permute-start.9
  75.9 1.6 collective-permute-start.1
  77.4 0.7 collective-permute-start.12
  78.1 1.4 collective-permute-done.3
  79.5 0.1 fusion.3
  79.7 15.6 %collective-permute-start.10 = (f32[1096,128]{1,0:T(8,128)S(1)}, f32[1096,128]{1,0:T(8,128)S(1)}, u32[]{:S(2)}, u32[]{:S(2)}) collective-permute-start(f32[1096,128]{1,0:T(8,128)S(1)} %fusion.3), channel_id=1, source_target_pairs={{0,8},{2,10},{4,12},{6,14},{8,0},{10,2},{12,4},{14,6},{16,24},{18,... | collective-permute-start | bytes 1683464 | tf_op jit(solution)/shard_map/ppermute | solution.py:72
  95.3 6.3 %owned_weights.1 = (f32[1088,128]{1,0:T(8,128)}, s32[1152,128]{1,0:T(8,128)}) custom-call(s32[3]{0:T(128)} %pad_add_fusion.place_ref, s32[136,128]{1,0:T(8,128)} %bitcast.34, f32[17408,128]{1,0:T(8,128)} %weights_ref.3), custom_call_target="tpu_custom_call" | custom-call | bytes 20971520 | tf_op jit(solution)/shard_map/owned_weights/pallas_call | solution.py:248
  101.7 1.2 collective-permute-done.10.refs_3_
  102.9 0.8 copy-done.21
  103.7 5.3 %moments.1 = (f32[1088,128]{1,0:T(8,128)}, f32[1088,128]{1,0:T(8,128)}, f32[1096,128]{1,0:T(8,128)}, f32[8,128]{1,0:T(8,128)}) custom-call(f32[2192,128]{1,0:T(8,128)} %get-tuple-element.23.refs_0_, f32[2192,128]{1,0:T(8,128)} %copy-done.3, f32[1096,128]{1,0:T(8,128)} %copy-done.19, f32[1096,128]{1,0:T(8,128)} %copy-done.21, f32[1096,128]{1,0:T(8,128)} %copy-done.20, ...), custom_call_target="tpu_custom_call" | custom-call | tf_op jit(solution)/shard_map/moments/pallas_call | solution.py:303
  109.0 1.5 collective-permute-start.13
  110.5 2.3 %collective-permute-done.13 = f32[8,128]{1,0:T(8,128)S(1)} collective-permute-done((f32[8,128]{1,0:T(8,128)}, f32[8,128]{1,0:T(8,128)S(1)}, u32[]{:S(2)}, u32[]{:S(2)}) %collective-permute-start.13) | collective-permute-done | bytes 4128 | tf_op jit(solution)/shard_map/ppermute | solution.py:446
  112.8 1.3 add_dynamic-update-slice_fusion.refs_0_
  114.1 2.0 collective-permute-start.17
  116.1 0.7 collective-permute-start.22
  116.8 7.1 %collective-permute-done.17.refs_4_ = f32[1096,128]{1,0:T(8,128)S(1)} collective-permute-done((f32[1096,128]{1,0:T(8,128)}, f32[1096,128]{1,0:T(8,128)S(1)}, u32[]{:S(2)}, u32[]{:S(2)}) %collective-permute-start.17) | collective-permute-done | bytes 561184 | tf_op jit(solution)/shard_map/ppermute | solution.py:72
  123.9 0.7 collective-permute-start.21
  124.6 2.3 %collective-permute-start.15 = (f32[1096,128]{1,0:T(8,128)}, f32[1096,128]{1,0:T(8,128)S(1)}, u32[]{:S(2)}, u32[]{:S(2)}) collective-permute-start(f32[1096,128]{1,0:T(8,128)} %add_dynamic-update-slice_fusion.refs_0_), channel_id=1, source_target_pairs={{0,4},{2,6},{4,0},{6,2},{8,12},{10,14},{12,8},{14,10},{16,20},{18,... | collective-permute-start | bytes 1683464 | tf_op jit(solution)/shard_map/ppermute | solution.py:72
  126.9 1.3 collective-permute-start.23
  128.2 1.3 collective-permute-start.27
  129.6 0.5 collective-permute-start.18
  130.1 4.6 %collective-permute-done.15.refs_2_ = f32[1096,128]{1,0:T(8,128)S(1)} collective-permute-done((f32[1096,128]{1,0:T(8,128)}, f32[1096,128]{1,0:T(8,128)S(1)}, u32[]{:S(2)}, u32[]{:S(2)}) %collective-permute-start.15) | collective-permute-done | bytes 561184 | tf_op jit(solution)/shard_map/ppermute | solution.py:72
  134.7 13.5 %collective-permute-done.23 = f32[1096,128]{1,0:T(8,128)S(1)} collective-permute-done((f32[1096,128]{1,0:T(8,128)S(1)}, f32[1096,128]{1,0:T(8,128)S(1)}, u32[]{:S(2)}, u32[]{:S(2)}) %collective-permute-start.23) | collective-permute-done | bytes 561184 | tf_op jit(solution)/shard_map/ppermute | solution.py:72
  148.2 1.5 collective-permute-start.19
  149.7 4.4 %collective-permute-done.27 = f32[1096,128]{1,0:T(8,128)S(1)} collective-permute-done((f32[1096,128]{1,0:T(8,128)S(1)}, f32[1096,128]{1,0:T(8,128)S(1)}, u32[]{:S(2)}, u32[]{:S(2)}) %collective-permute-start.27) | collective-permute-done | bytes 561184 | tf_op jit(solution)/shard_map/ppermute | solution.py:72
  154.2 1.5 collective-permute-start.25
  155.7 0.1 add.116.refs_12_
  155.8 0.6 collective-permute-start.29
  156.4 7.4 %collective-permute-done.19.refs_6_ = f32[1096,128]{1,0:T(8,128)S(1)} collective-permute-done((f32[1096,128]{1,0:T(8,128)S(1)}, f32[1096,128]{1,0:T(8,128)S(1)}, u32[]{:S(2)}, u32[]{:S(2)}) %collective-permute-start.19) | collective-permute-done | bytes 561184 | tf_op jit(solution)/shard_map/ppermute | solution.py:72
  163.8 0.5 collective-permute-start.28
  164.3 10.4 %collective-permute-done.25.refs_10_ = f32[1096,128]{1,0:T(8,128)S(1)} collective-permute-done((f32[1096,128]{1,0:T(8,128)S(1)}, f32[1096,128]{1,0:T(8,128)S(1)}, u32[]{:S(2)}, u32[]{:S(2)}) %collective-permute-start.25) | collective-permute-done | bytes 561184 | tf_op jit(solution)/shard_map/ppermute | solution.py:72
  174.7 6.0 %collective-permute-done.29.refs_14_ = f32[1096,128]{1,0:T(8,128)S(1)} collective-permute-done((f32[1096,128]{1,0:T(8,128)S(1)}, f32[1096,128]{1,0:T(8,128)S(1)}, u32[]{:S(2)}, u32[]{:S(2)}) %collective-permute-start.29) | collective-permute-done | bytes 561184 | tf_op jit(solution)/shard_map/ppermute | solution.py:72
  180.7 0.1 multiply_reduce_fusion
  180.9 0.6 copy-done.11
  181.5 0.2 copy-done.13
  181.8 0.1 copy-done.15
  181.9 0.9 collective-permute-done.30.refs_15_
  182.8 2.3 %tails.1 = (f32[16,128]{1,0:T(8,128)}, f32[5,128]{1,0:T(8,128)}) custom-call(s32[3]{0:T(128)} %pad_add_fusion.place_ref, f32[1096,128]{1,0:T(8,128)} %add_dynamic-update-slice_fusion.refs_0_, f32[1096,128]{1,0:T(8,128)} %copy-done.6, f32[1096,128]{1,0:T(8,128)} %copy-done.5, f32[1096,128]{1,0:T(8,128)} %copy-done.8, f32[1096,128]{1,0:T(8,128)} %copy-done.4, ...), custom_call_target="tpu_custom_call" | custom-call | tf_op jit(solution)/shard_map/tails/pallas_call | solution.py:338
  185.1 0.7 reshape.74
  185.8 0.7 reshape.75
  186.6 0.8 slice_reduce_fusion
  187.4 0.5 broadcast_multiply_fusion.1.rates_ref
  187.9 0.2 fusion.9
  188.1 0.6 pad_maximum_fusion.1
  188.7 0.6 pad_maximum_fusion
  189.4 25.0 %new_weights.1 = f32[17408,128]{1,0:T(8,128)} custom-call(s32[136,128]{1,0:T(8,128)} %get-tuple-element.22.position_ref, f32[5]{0:T(128)} %broadcast_multiply_fusion.1.rates_ref, f32[17408,128]{1,0:T(8,128)} %weights_ref.3, f32[1096,128]{1,0:T(8,128)} %add_dynamic-update-slice_fusion.refs_0_, f32[1096,128]{1,0:T(8,128)} %copy-done.6, f32[1096,128]{1,0:T(8,128)} %copy-done.5, ...), custom_call_target="tpu_custom_call" | custom-call | tf_op jit(solution)/shard_map/new_weights/pallas_call | solution.py:391
  (75 shorter events, 0.7 us)
Async XLA Ops:
  25.2 7.2 %copy-start.16 = (f32[2192,128]{1,0:T(8,128)S(1)}, f32[2192,128]{1,0:T(8,128)}, u32[]{:S(2)}) copy-start(f32[2192,128]{1,0:T(8,128)} %get-tuple-element.29) | copy-start | bytes 3366916
  25.3 3.1 %collective-permute-start.4 = (f32[2192,128]{1,0:T(8,128)}, f32[2192,128]{1,0:T(8,128)S(1)}, u32[]{:S(2)}, u32[]{:S(2)}) collective-permute-start(f32[2192,128]{1,0:T(8,128)} %get-tuple-element.28), channel_id=1, source_target_pairs={{0,2},{2,0},{4,6},{6,4},{8,10},{10,8},{12,14},{14,12},{16,18},{18,... | collective-permute-start | bytes 3366920 | tf_op jit(solution)/shard_map/ppermute | solution.py:72
  25.8 6.7 %collective-permute-start.6 = (f32[2192,128]{1,0:T(8,128)}, f32[2192,128]{1,0:T(8,128)S(1)}, u32[]{:S(2)}, u32[]{:S(2)}) collective-permute-start(f32[2192,128]{1,0:T(8,128)} %get-tuple-element.30), channel_id=1, source_target_pairs={{0,2},{2,0},{4,6},{6,4},{8,10},{10,8},{12,14},{14,12},{16,18},{18,... | collective-permute-start | bytes 3366920 | tf_op jit(solution)/shard_map/ppermute | solution.py:72
  29.5 16.4 %copy-start.18 = (f32[2192,128]{1,0:T(8,128)S(1)}, f32[2192,128]{1,0:T(8,128)}, u32[]{:S(2)}) copy-start(f32[2192,128]{1,0:T(8,128)} %get-tuple-element.27) | copy-start | bytes 3366916
  29.5 16.4 %collective-permute-start.5 = (f32[1096,128]{1,0:T(8,128)S(1)}, f32[1096,128]{1,0:T(8,128)S(1)}, u32[]{:S(2)}, u32[]{:S(2)}) collective-permute-start(f32[1096,128]{1,0:T(8,128)S(1)} %slice_add_fusion.2), channel_id=1, source_target_pairs={{0,4},{2,6},{4,0},{6,2},{8,12},{10,14},{12,8},{14,10},{16,20},{18,... | collective-permute-start | bytes 1683464 | tf_op jit(solution)/shard_map/ppermute | solution.py:72
  32.5 17.6 %copy-start.24 = (f32[2192,128]{1,0:T(8,128)S(1)}, f32[2192,128]{1,0:T(8,128)}, u32[]{:S(2)}) copy-start(f32[2192,128]{1,0:T(8,128)} %get-tuple-element.26) | copy-start | bytes 3366916
  32.5 17.7 %copy-start.23 = (f32[2192,128]{1,0:T(8,128)S(1)}, f32[2192,128]{1,0:T(8,128)}, u32[]{:S(2)}) copy-start(f32[2192,128]{1,0:T(8,128)} %get-tuple-element.24) | copy-start | bytes 3366916
  32.5 24.9 %collective-permute-start.7 = (f32[1096,128]{1,0:T(8,128)S(1)}, f32[1096,128]{1,0:T(8,128)S(1)}, u32[]{:S(2)}, u32[]{:S(2)}) collective-permute-start(f32[1096,128]{1,0:T(8,128)S(1)} %slice_add_fusion), channel_id=1, source_target_pairs={{0,4},{2,6},{4,0},{6,2},{8,12},{10,14},{12,8},{14,10},{16,20},{18,... | collective-permute-start | bytes 1683464 | tf_op jit(solution)/shard_map/ppermute | solution.py:72
  46.0 14.7 %collective-permute-start.11 = (f32[1096,128]{1,0:T(8,128)S(1)}, f32[1096,128]{1,0:T(8,128)S(1)}, u32[]{:S(2)}, u32[]{:S(2)}) collective-permute-start(f32[1096,128]{1,0:T(8,128)S(1)} %fusion.1), channel_id=1, source_target_pairs={{0,8},{2,10},{4,12},{6,14},{24,16},{26,18},{28,20},{30,22},{1,9},{... | collective-permute-start | bytes 1683464 | tf_op jit(solution)/shard_map/ppermute | solution.py:72
  50.1 15.2 %collective-permute-start.2 = (f32[2192,128]{1,0:T(8,128)S(1)}, f32[2192,128]{1,0:T(8,128)S(1)}, u32[]{:S(2)}, u32[]{:S(2)}) collective-permute-start(f32[2192,128]{1,0:T(8,128)S(1)} %copy-done.24), channel_id=1, source_target_pairs={{0,2},{2,0},{4,6},{6,4},{8,10},{10,8},{12,14},{14,12},{16,18},{18,... | collective-permute-start | bytes 3366920 | tf_op jit(solution)/shard_map/ppermute | solution.py:72
  50.2 15.1 %copy-start.17 = (f32[2192,128]{1,0:T(8,128)S(1)}, f32[2192,128]{1,0:T(8,128)}, u32[]{:S(2)}) copy-start(f32[2192,128]{1,0:T(8,128)} %get-tuple-element.25) | copy-start | bytes 3366916
  50.2 25.5 %collective-permute-start = (f32[2192,128]{1,0:T(8,128)S(1)}, f32[2192,128]{1,0:T(8,128)S(1)}, u32[]{:S(2)}, u32[]{:S(2)}) collective-permute-start(f32[2192,128]{1,0:T(8,128)S(1)} %copy-done.23), channel_id=1, source_target_pairs={{0,2},{2,0},{4,6},{6,4},{8,10},{10,8},{12,14},{14,12},{16,18},{18,... | collective-permute-start | bytes 3366920 | tf_op jit(solution)/shard_map/ppermute | solution.py:72
  60.9 14.1 %collective-permute-start.8 = (f32[1096,128]{1,0:T(8,128)S(1)}, f32[1096,128]{1,0:T(8,128)S(1)}, u32[]{:S(2)}, u32[]{:S(2)}) collective-permute-start(f32[1096,128]{1,0:T(8,128)S(1)} %get-tuple-element.45), channel_id=1, source_target_pairs={{0,8},{2,10},{4,12},{6,14},{24,16},{26,18},{28,20},{30,22},{1,9},{... | collective-permute-start | bytes 1683464 | tf_op jit(solution)/shard_map/ppermute | solution.py:72
  65.4 10.4 %copy-start.2 = (f32[2192,128]{1,0:T(8,128)S(1)}, f32[2192,128]{1,0:T(8,128)}, u32[]{:S(2)}) copy-start(f32[2192,128]{1,0:T(8,128)} %get-tuple-element.23.refs_0_) | copy-start | bytes 3366916
  65.4 14.1 %collective-permute-start.3 = (f32[1096,128]{1,0:T(8,128)S(1)}, f32[1096,128]{1,0:T(8,128)S(1)}, u32[]{:S(2)}, u32[]{:S(2)}) collective-permute-start(f32[1096,128]{1,0:T(8,128)S(1)} %slice_add_fusion.4), channel_id=1, source_target_pairs={{0,4},{2,6},{4,0},{6,2},{8,12},{10,14},{12,8},{14,10},{16,20},{18,... | collective-permute-start | bytes 1683464 | tf_op jit(solution)/shard_map/ppermute | solution.py:72
  75.1 4.5 %collective-permute-start.9 = (f32[1096,128]{1,0:T(8,128)S(1)}, f32[1096,128]{1,0:T(8,128)S(1)}, u32[]{:S(2)}, u32[]{:S(2)}) collective-permute-start(f32[1096,128]{1,0:T(8,128)S(1)} %add.110), channel_id=1, source_target_pairs={{8,16},{10,18},{12,20},{14,22},{16,8},{18,10},{20,12},{22,14},{9,1... | collective-permute-start | bytes 1683464 | tf_op jit(solution)/shard_map/ppermute | solution.py:72
  75.8 3.9 %copy-start.3 = (f32[2192,128]{1,0:T(8,128)}, f32[2192,128]{1,0:T(8,128)S(1)}, u32[]{:S(2)}) copy-start(f32[2192,128]{1,0:T(8,128)S(1)} %collective-permute-done.refs_1_) | copy-start | bytes 3366916
  75.9 25.8 %collective-permute-start.1 = (f32[1096,128]{1,0:T(8,128)S(1)}, f32[1096,128]{1,0:T(8,128)S(1)}, u32[]{:S(2)}, u32[]{:S(2)}) collective-permute-start(f32[1096,128]{1,0:T(8,128)S(1)} %slice_add_fusion.6), channel_id=1, source_target_pairs={{0,4},{2,6},{4,0},{6,2},{8,12},{10,14},{12,8},{14,10},{16,20},{18,... | collective-permute-start | bytes 1683464 | tf_op jit(solution)/shard_map/ppermute | solution.py:72
  77.4 24.2 %collective-permute-start.12 = (f32[1096,128]{1,0:T(8,128)S(1)}, f32[1096,128]{1,0:T(8,128)S(1)}, u32[]{:S(2)}, u32[]{:S(2)}) collective-permute-start(f32[1096,128]{1,0:T(8,128)S(1)} %get-tuple-element.44), channel_id=1, source_target_pairs={{8,16},{10,18},{12,20},{14,22},{16,8},{18,10},{20,12},{22,14},{9,1... | collective-permute-start | bytes 1683464 | tf_op jit(solution)/shard_map/ppermute | solution.py:72
  79.7 23.2 %collective-permute-start.10 = (f32[1096,128]{1,0:T(8,128)S(1)}, f32[1096,128]{1,0:T(8,128)S(1)}, u32[]{:S(2)}, u32[]{:S(2)}) collective-permute-start(f32[1096,128]{1,0:T(8,128)S(1)} %fusion.3), channel_id=1, source_target_pairs={{0,8},{2,10},{4,12},{6,14},{8,0},{10,2},{12,4},{14,6},{16,24},{18,... | collective-permute-start | bytes 1683464 | tf_op jit(solution)/shard_map/ppermute | solution.py:72
  101.7 1.2 copy-start.19
  101.7 1.2 copy-start.20
  102.9 0.8 copy-start.21
  109.0 3.8 %collective-permute-start.13 = (f32[8,128]{1,0:T(8,128)}, f32[8,128]{1,0:T(8,128)S(1)}, u32[]{:S(2)}, u32[]{:S(2)}) collective-permute-start(f32[8,128]{1,0:T(8,128)} %get-tuple-element.34), channel_id=1, source_target_pairs={{0,1},{1,0},{2,3},{3,2},{4,5},{5,4},{6,7},{7,6},{8,9},{9,8},{10,11... | collective-permute-start | bytes 12296 | tf_op jit(solution)/shard_map/ppermute | solution.py:446
  114.1 9.8 %collective-permute-start.17 = (f32[1096,128]{1,0:T(8,128)}, f32[1096,128]{1,0:T(8,128)S(1)}, u32[]{:S(2)}, u32[]{:S(2)}) collective-permute-start(f32[1096,128]{1,0:T(8,128)} %add_dynamic-update-slice_fusion.refs_0_), channel_id=1, source_target_pairs={{0,8},{2,10},{4,12},{6,14},{8,0},{10,2},{12,4},{14,6},{16,24},{18,... | collective-permute-start | bytes 1683464 | tf_op jit(solution)/shard_map/ppermute | solution.py:72
  116.1 10.8 %collective-permute-start.22 = (f32[1096,128]{1,0:T(8,128)}, f32[1096,128]{1,0:T(8,128)S(1)}, u32[]{:S(2)}, u32[]{:S(2)}) collective-permute-start(f32[1096,128]{1,0:T(8,128)} %add_dynamic-update-slice_fusion.refs_0_), channel_id=1, source_target_pairs={{8,16},{10,18},{12,20},{14,22},{16,8},{18,10},{20,12},{22,14},{9,1... | collective-permute-start | bytes 1683464 | tf_op jit(solution)/shard_map/ppermute | solution.py:72
  123.9 31.9 %copy-start.4 = (f32[1096,128]{1,0:T(8,128)}, f32[1096,128]{1,0:T(8,128)S(1)}, u32[]{:S(2)}) copy-start(f32[1096,128]{1,0:T(8,128)S(1)} %collective-permute-done.17.refs_4_) | copy-start | bytes 1683460
  123.9 4.3 %collective-permute-start.21 = (f32[1096,128]{1,0:T(8,128)S(1)}, f32[1096,128]{1,0:T(8,128)S(1)}, u32[]{:S(2)}, u32[]{:S(2)}) collective-permute-start(f32[1096,128]{1,0:T(8,128)S(1)} %collective-permute-done.17.refs_4_), channel_id=1, source_target_pairs={{8,16},{10,18},{12,20},{14,22},{16,8},{18,10},{20,12},{22,14},{9,1... | collective-permute-start | bytes 1683464 | tf_op jit(solution)/shard_map/ppermute | solution.py:72
  124.6 10.1 %collective-permute-start.15 = (f32[1096,128]{1,0:T(8,128)}, f32[1096,128]{1,0:T(8,128)S(1)}, u32[]{:S(2)}, u32[]{:S(2)}) collective-permute-start(f32[1096,128]{1,0:T(8,128)} %add_dynamic-update-slice_fusion.refs_0_), channel_id=1, source_target_pairs={{0,4},{2,6},{4,0},{6,2},{8,12},{10,14},{12,8},{14,10},{16,20},{18,... | collective-permute-start | bytes 1683464 | tf_op jit(solution)/shard_map/ppermute | solution.py:72
  126.9 21.3 %collective-permute-start.23 = (f32[1096,128]{1,0:T(8,128)S(1)}, f32[1096,128]{1,0:T(8,128)S(1)}, u32[]{:S(2)}, u32[]{:S(2)}) collective-permute-start(f32[1096,128]{1,0:T(8,128)S(1)} %collective-permute-done.22), channel_id=1, source_target_pairs={{8,0},{10,2},{12,4},{14,6},{16,24},{18,26},{20,28},{22,30},{9,1},{... | collective-permute-start | bytes 1683464 | tf_op jit(solution)/shard_map/ppermute | solution.py:72
  128.2 26.0 %collective-permute-start.27 = (f32[1096,128]{1,0:T(8,128)S(1)}, f32[1096,128]{1,0:T(8,128)S(1)}, u32[]{:S(2)}, u32[]{:S(2)}) collective-permute-start(f32[1096,128]{1,0:T(8,128)S(1)} %collective-permute-done.21), channel_id=1, source_target_pairs={{8,0},{10,2},{12,4},{14,6},{16,24},{18,26},{20,28},{22,30},{9,1},{... | collective-permute-start | bytes 1683464 | tf_op jit(solution)/shard_map/ppermute | solution.py:72
  129.5 26.3 %collective-permute-start.14 = (f32[1096,128]{1,0:T(8,128)}, f32[1096,128]{1,0:T(8,128)S(1)}, u32[]{:S(2)}, u32[]{:S(2)}) collective-permute-start(f32[1096,128]{1,0:T(8,128)} %add_dynamic-update-slice_fusion.refs_0_), channel_id=1, source_target_pairs={{0,2},{2,0},{4,6},{6,4},{8,10},{10,8},{12,14},{14,12},{16,18},{18,... | collective-permute-start | bytes 1683464 | tf_op jit(solution)/shard_map/ppermute | solution.py:72
  129.6 34.2 %collective-permute-start.18 = (f32[1096,128]{1,0:T(8,128)S(1)}, f32[1096,128]{1,0:T(8,128)S(1)}, u32[]{:S(2)}, u32[]{:S(2)}) collective-permute-start(f32[1096,128]{1,0:T(8,128)S(1)} %collective-permute-done.17.refs_4_), channel_id=1, source_target_pairs={{0,2},{2,0},{4,6},{6,4},{8,10},{10,8},{12,14},{14,12},{16,18},{18,... | collective-permute-start | bytes 1683464 | tf_op jit(solution)/shard_map/ppermute | solution.py:72
  134.7 21.1 %copy-start.5 = (f32[1096,128]{1,0:T(8,128)}, f32[1096,128]{1,0:T(8,128)S(1)}, u32[]{:S(2)}) copy-start(f32[1096,128]{1,0:T(8,128)S(1)} %collective-permute-done.15.refs_2_) | copy-start | bytes 1683460
  134.7 21.7 %collective-permute-start.16 = (f32[1096,128]{1,0:T(8,128)S(1)}, f32[1096,128]{1,0:T(8,128)S(1)}, u32[]{:S(2)}, u32[]{:S(2)}) collective-permute-start(f32[1096,128]{1,0:T(8,128)S(1)} %collective-permute-done.15.refs_2_), channel_id=1, source_target_pairs={{0,2},{2,0},{4,6},{6,4},{8,10},{10,8},{12,14},{14,12},{16,18},{18,... | collective-permute-start | bytes 1683464 | tf_op jit(solution)/shard_map/ppermute | solution.py:72
  148.2 15.6 %collective-permute-start.19 = (f32[1096,128]{1,0:T(8,128)S(1)}, f32[1096,128]{1,0:T(8,128)S(1)}, u32[]{:S(2)}, u32[]{:S(2)}) collective-permute-start(f32[1096,128]{1,0:T(8,128)S(1)} %collective-permute-done.17.refs_4_), channel_id=1, source_target_pairs={{0,4},{2,6},{4,0},{6,2},{8,12},{10,14},{12,8},{14,10},{16,20},{18,... | collective-permute-start | bytes 1683464 | tf_op jit(solution)/shard_map/ppermute | solution.py:72
  149.7 33.1 %copy-start = (f32[1096,128]{1,0:T(8,128)}, f32[1096,128]{1,0:T(8,128)S(1)}, u32[]{:S(2)}) copy-start(f32[1096,128]{1,0:T(8,128)S(1)} %add.115.refs_8_) | copy-start | bytes 1683460
  149.7 30.9 %copy-start.22 = (f32[3,2,1024]{2,1,0:T(2,128)S(1)}, f32[3,2,1024]{2,1,0:T(2,128)}, u32[]{:S(2)}) copy-start(f32[3,2,1024]{2,1,0:T(2,128)} %param.13) | copy-start | bytes 73732
  154.2 20.5 %collective-permute-start.25 = (f32[1096,128]{1,0:T(8,128)S(1)}, f32[1096,128]{1,0:T(8,128)S(1)}, u32[]{:S(2)}, u32[]{:S(2)}) collective-permute-start(f32[1096,128]{1,0:T(8,128)S(1)} %add.115.refs_8_), channel_id=1, source_target_pairs={{0,4},{2,6},{4,0},{6,2},{8,12},{10,14},{12,8},{14,10},{16,20},{18,... | collective-permute-start | bytes 1683464 | tf_op jit(solution)/shard_map/ppermute | solution.py:72
  155.8 27.0 %copy-start.1 = (f32[1096,128]{1,0:T(8,128)}, f32[1096,128]{1,0:T(8,128)S(1)}, u32[]{:S(2)}) copy-start(f32[1096,128]{1,0:T(8,128)S(1)} %add.116.refs_12_) | copy-start | bytes 1683460
  155.8 27.0 %copy-start.6 = (f32[1096,128]{1,0:T(8,128)}, f32[1096,128]{1,0:T(8,128)S(1)}, u32[]{:S(2)}) copy-start(f32[1096,128]{1,0:T(8,128)S(1)} %collective-permute-done.14.refs_1_) | copy-start | bytes 1683460
  155.8 24.9 %collective-permute-start.29 = (f32[1096,128]{1,0:T(8,128)S(1)}, f32[1096,128]{1,0:T(8,128)S(1)}, u32[]{:S(2)}, u32[]{:S(2)}) collective-permute-start(f32[1096,128]{1,0:T(8,128)S(1)} %add.116.refs_12_), channel_id=1, source_target_pairs={{0,4},{2,6},{4,0},{6,2},{8,12},{10,14},{12,8},{14,10},{16,20},{18,... | collective-permute-start | bytes 1683464 | tf_op jit(solution)/shard_map/ppermute | solution.py:72
  156.4 24.5 %copy-start.8 = (f32[1096,128]{1,0:T(8,128)}, f32[1096,128]{1,0:T(8,128)S(1)}, u32[]{:S(2)}) copy-start(f32[1096,128]{1,0:T(8,128)S(1)} %collective-permute-done.16.refs_3_) | copy-start | bytes 1683460
  156.4 24.4 %collective-permute-start.24 = (f32[1096,128]{1,0:T(8,128)S(1)}, f32[1096,128]{1,0:T(8,128)S(1)}, u32[]{:S(2)}, u32[]{:S(2)}) collective-permute-start(f32[1096,128]{1,0:T(8,128)S(1)} %add.115.refs_8_), channel_id=1, source_target_pairs={{0,2},{2,0},{4,6},{6,4},{8,10},{10,8},{12,14},{14,12},{16,18},{18,... | collective-permute-start | bytes 1683464 | tf_op jit(solution)/shard_map/ppermute | solution.py:72
  163.8 17.1 %copy-start.9 = (f32[1096,128]{1,0:T(8,128)}, f32[1096,128]{1,0:T(8,128)S(1)}, u32[]{:S(2)}) copy-start(f32[1096,128]{1,0:T(8,128)S(1)} %collective-permute-done.19.refs_6_) | copy-start | bytes 1683460
  163.8 17.0 %collective-permute-start.20 = (f32[1096,128]{1,0:T(8,128)S(1)}, f32[1096,128]{1,0:T(8,128)S(1)}, u32[]{:S(2)}, u32[]{:S(2)}) collective-permute-start(f32[1096,128]{1,0:T(8,128)S(1)} %collective-permute-done.19.refs_6_), channel_id=1, source_target_pairs={{0,2},{2,0},{4,6},{6,4},{8,10},{10,8},{12,14},{14,12},{16,18},{18,... | collective-permute-start | bytes 1683464 | tf_op jit(solution)/shard_map/ppermute | solution.py:72
  163.8 19.0 %copy-start.7 = (f32[1096,128]{1,0:T(8,128)}, f32[1096,128]{1,0:T(8,128)S(1)}, u32[]{:S(2)}) copy-start(f32[1096,128]{1,0:T(8,128)S(1)} %collective-permute-done.18.refs_5_) | copy-start | bytes 1683460
  163.8 17.1 %collective-permute-start.28 = (f32[1096,128]{1,0:T(8,128)S(1)}, f32[1096,128]{1,0:T(8,128)S(1)}, u32[]{:S(2)}, u32[]{:S(2)}) collective-permute-start(f32[1096,128]{1,0:T(8,128)S(1)} %add.116.refs_12_), channel_id=1, source_target_pairs={{0,2},{2,0},{4,6},{6,4},{8,10},{10,8},{12,14},{14,12},{16,18},{18,... | collective-permute-start | bytes 1683464 | tf_op jit(solution)/shard_map/ppermute | solution.py:72
  174.7 6.2 %copy-start.10 = (f32[1096,128]{1,0:T(8,128)}, f32[1096,128]{1,0:T(8,128)S(1)}, u32[]{:S(2)}) copy-start(f32[1096,128]{1,0:T(8,128)S(1)} %collective-permute-done.25.refs_10_) | copy-start | bytes 1683460
  174.7 6.2 %collective-permute-start.26 = (f32[1096,128]{1,0:T(8,128)S(1)}, f32[1096,128]{1,0:T(8,128)S(1)}, u32[]{:S(2)}, u32[]{:S(2)}) collective-permute-start(f32[1096,128]{1,0:T(8,128)S(1)} %collective-permute-done.25.refs_10_), channel_id=1, source_target_pairs={{0,2},{2,0},{4,6},{6,4},{8,10},{10,8},{12,14},{14,12},{16,18},{18,... | collective-permute-start | bytes 1683464 | tf_op jit(solution)/shard_map/ppermute | solution.py:72
  180.7 0.9 copy-start.11
  180.7 2.1 collective-permute-start.30
  180.8 1.0 copy-start.13
  180.8 2.0 copy-start.12
  180.8 1.1 copy-start.15
  181.9 0.9 copy-start.14

commit v4 on v3

--- a/solution.py
+++ b/solution.py
@@ -93,6 +93,52 @@
     across_three = plan.send(blocks[3] + in_two, axis, MIDDLE)
     pair = plan.send(blocks[1] + across_two, axis, PAIRS)
     return [blocks[0], pair, across_three]
+
+
+def together(*values):
+    return lax.optimization_barrier(values)
+
+
+def gather(plan, block):
+    found = {}
+
+    def add(far_z, line):
+        for far_x, value in enumerate(line):
+            found[far_z, far_x, 0] = value
+
+    def along_x(value):
+        return line_gather(plan, "x", plan.nx, value)
+
+    def swapped(*far_zs):
+        for far_z in far_zs:
+            for far_x in range(plan.nx):
+                found[far_z, far_x, 1] = plan.swap(found[far_z, far_x, 0])
+
+    if plan.nz != 4:
+        for far_z, value in enumerate(line_gather(plan, "z", plan.nz, block)):
+            add(far_z, along_x(value))
+            swapped(far_z)
+        return list(found.items())
+    line = along_x(block)
+    pair = plan.send(block, "z", PAIRS)
+    three = plan.send(block, "z", MIDDLE)
+    pair, three, *line = together(pair, three, *line)
+    add(0, line)
+    line = along_x(pair)
+    two = plan.send(pair, "z", MIDDLE)
+    out_two = plan.send(three, "z", OUTWARD)
+    swapped(0)
+    two, out_two, *line = together(two, out_two, *line)
+    add(1, line)
+    line = along_x(two + out_two)
+    out_three = plan.send(two, "z", OUTWARD)
+    swapped(1)
+    out_three, *line = together(out_three, *line)
+    add(2, line)
+    add(3, along_x(three + out_three))
+    swapped(2)
+    swapped(3)
+    return list(found.items())
 
 
 def line_gather(plan, axis, count, value):
@@ -305,55 +351,21 @@
         out_shape=[jax.ShapeDtypeStruct(s, jnp.float32) for s in shapes],
         in_specs=[vmem] * (len(parts) + 4),
         out_specs=[vmem] * len(shapes),
-        compiler_params=pltpu.CompilerParams(vmem_limit_bytes=58 * MIB),
+        compiler_params=pltpu.CompilerParams(vmem_limit_bytes=20 * MIB),
         name="moments",
     )(*parts, first, second, weight, natural)
 
 
-def tails_kernel(plan, slots, place_ref, *refs):
+def adam_rows(gradient, moment_one, moment_two, weight):
+    moment_one = beta_one * moment_one + (1.0 - beta_one) * gradient
+    moment_two = beta_two * moment_two + (1.0 - beta_two) * gradient * gradient
+    step = moment_one / bias_one / (jnp.sqrt(moment_two / bias_two) + epsilon) + decay_rate * weight
+    return (moment_one, moment_two, step)
+
+
+def finish_kernel(plan, tile, slots, place_ref, position_ref, norm_ref, weights_ref, *refs):
     pieces, refs = refs[: len(slots)], refs[len(slots) :]
-    norm_ref, ratio_ref, held, sems = refs
-    copies = []
-    for i, (piece, (far_z, far_x, far_c)) in enumerate(zip(pieces, slots)):
-        d = plan.index(place_ref[0] ^ far_z, place_ref[1] ^ far_x, place_ref[2] ^ far_c)
-        copies.append(pltpu.make_async_copy(piece.at[pl.ds(plan.own, plan.tail)], held.at[d], sems.at[i]))
-    for copy in copies:
-        copy.start()
-    for copy in copies:
-        copy.wait()
-    total = held[0]
-    for d in range(1, plan.replicas):
-        total = total + held[d]
-    for row in range(plan.norm_rows):
-        norm_ref[row : row + 1, :] = held[row // plan.norm_each, pl.ds(row % plan.norm_each, 1), :]
-    for k in range(matrices):
-        row = plan.norm_each + k
-        weight_square, direction_square = total[row : row + 1, 0:1], total[row : row + 1, 1:2]
-        ratio = jnp.sqrt(weight_square) / (jnp.sqrt(direction_square) + epsilon)
-        ratio_ref[k : k + 1, :] = jnp.broadcast_to(ratio, (1, LANE))
-
-
-def tails(plan, my_place, pieces, slots):
-    vmem = pl.BlockSpec(memory_space=pltpu.VMEM)
-    return pl.pallas_call(
-        functools.partial(tails_kernel, plan, slots),
-        out_shape=[
-            jax.ShapeDtypeStruct((plan.norm_rows, LANE), jnp.float32),
-            jax.ShapeDtypeStruct((matrices, LANE), jnp.float32),
-        ],
-        in_specs=[pl.BlockSpec(memory_space=pltpu.SMEM)] + [pl.BlockSpec(memory_space=pl.ANY)] * len(pieces),
-        out_specs=[vmem, vmem],
-        scratch_shapes=[
-            pltpu.VMEM((plan.replicas, plan.tail, LANE), jnp.float32),
-            pltpu.SemaphoreType.DMA((len(pieces),)),
-        ],
-        name="tails",
-    )(my_place, *pieces)
-
-
-def finish_kernel(plan, tile, slots, position_ref, rates_ref, weights_ref, *refs):
-    pieces, refs = refs[: len(slots)], refs[len(slots) :]
-    out_ref, held, sems = refs
+    out_ref, new_norm_ref, trust_ref, held, norms, rates, sems = refs
     now = pl.program_id(0)
 
     @pl.when(now == 0)
@@ -366,11 +378,39 @@
             copy.start()
         for copy in copies:
             copy.wait()
+        total = jnp.zeros((plan.tail, LANE), jnp.float32)
+        for z in range(plan.nz):
+            for x in range(plan.nx):
+                for c in range(2):
+                    start = plan.start(place_ref[0] ^ z, place_ref[1] ^ x, place_ref[2] ^ c) + plan.own
+                    tail = held[pl.ds(pl.multiple_of(start, 8), plan.tail), :]
+                    total = total + tail
+                    first = plan.index(z, x, c) * plan.norm_each
+                    for row in range(first, min(first + plan.norm_each, plan.norm_rows)):
+                        norms[row : row + 1, :] = tail[row - first : row - first + 1, :]
+        for k in range(matrices):
+            row = plan.norm_each + k
+            weight_square, direction_square = total[row : row + 1, 0:1], total[row : row + 1, 1:2]
+            ratio = jnp.sqrt(weight_square) / (jnp.sqrt(direction_square) + epsilon)
+            rates[k : k + 1, :] = jnp.broadcast_to(learning * ratio, (1, LANE))
+            trust_ref[k] = jnp.sum(ratio)
+        each = plan.norm_rows // 2
+        for i in range(2):
+            rows = pl.ds(i * each, each)
+            gains = norm_ref[0, rows, :]
+            one, two, step = adam_rows(norms[rows, :], norm_ref[1, rows, :], norm_ref[2, rows, :], gains)
+            gain_square = jnp.sum(jnp.sum(gains * gains, axis=1, keepdims=True), axis=0, keepdims=True)
+            step_square = jnp.sum(jnp.sum(step * step, axis=1, keepdims=True), axis=0, keepdims=True)
+            ratio = jnp.sqrt(gain_square) / (jnp.sqrt(step_square) + epsilon)
+            trust_ref[matrices + i] = jnp.sum(ratio)
+            for j, value in enumerate((gains - learning * ratio * step, one, two)):
+                for row in range(each):
+                    new_norm_ref[j, i : i + 1, row * LANE : (row + 1) * LANE] = value[row : row + 1, :]
 
     matrix = jnp.int32(0)
     for bound in plan.bounds:
         matrix = matrix + (now * tile >= bound).astype(jnp.int32)
-    rate = rates_ref[matrix]
+    rate = jnp.broadcast_to(rates[pl.ds(matrix, 1), :], (8, LANE))
     lines = tile // LANE
 
     @pl.loop(0, lines)
@@ -383,32 +423,32 @@
             out_ref[here, :] = weight - rate * direction
 
 
-def finish(plan, position, rates, weights, pieces, slots):
+def finish(plan, my_place, position, norm_state, weights, pieces, slots):
     tile = LANE
     while tile < 1024 and all(b % (2 * tile) == 0 for b in plan.bounds + (plan.blocks,)):
         tile *= 2
     smem = pl.BlockSpec(memory_space=pltpu.SMEM)
+    vmem = pl.BlockSpec(memory_space=pltpu.VMEM)
     return pl.pallas_call(
         functools.partial(finish_kernel, plan, tile, slots),
         grid=(plan.blocks // tile,),
-        out_shape=jax.ShapeDtypeStruct((plan.blocks, LANE), jnp.float32),
-        in_specs=[smem, smem, pl.BlockSpec((tile, LANE), lambda i: (i, 0))]
+        out_shape=[
+            jax.ShapeDtypeStruct((plan.blocks, LANE), jnp.float32),
+            jax.ShapeDtypeStruct(norm_state.shape, jnp.float32),
+            jax.ShapeDtypeStruct((matrices + 2,), jnp.float32),
+        ],
+        in_specs=[smem, smem, vmem, pl.BlockSpec((tile, LANE), lambda i: (i, 0))]
         + [pl.BlockSpec(memory_space=pl.ANY)] * len(pieces),
-        out_specs=pl.BlockSpec((tile, LANE), lambda i: (i, 0)),
+        out_specs=[pl.BlockSpec((tile, LANE), lambda i: (i, 0)), vmem, smem],
         scratch_shapes=[
             pltpu.VMEM((2 * plan.half, LANE), jnp.float32),
+            pltpu.VMEM((plan.norm_rows, LANE), jnp.float32),
+            pltpu.VMEM((8, LANE), jnp.float32),
             pltpu.SemaphoreType.DMA((len(pieces),)),
         ],
         compiler_params=pltpu.CompilerParams(vmem_limit_bytes=58 * MIB),
         name="new_weights",
-    )(position, rates, weights, *pieces)
-
-
-def adam_step(gradient, moment_one, moment_two, weight):
-    moment_one = beta_one * moment_one + (1.0 - beta_one) * gradient
-    moment_two = beta_two * moment_two + (1.0 - beta_two) * gradient * gradient
-    step = moment_one / bias_one / (jnp.sqrt(moment_two / bias_two) + epsilon) + decay_rate * weight
-    return (moment_one, moment_two, step)
+    )(my_place, position, norm_state.reshape(3, plan.norm_rows, LANE), weights, *pieces)
 
 
 def local(gradients, weights, first_moment, second_moment, owner_list, norm_grads, norm_state):
@@ -420,23 +460,22 @@
     siblings, blocks, position = place(plan, my_place, owners, norm_grads[0], gradients[0])
     weight_own, natural = owned(plan, my_place, owners, weights)
 
-    others = [None] * plan.nz
+    mine, theirs = [None] * plan.nz, [None] * plan.nz
     for z in reversed(range(plan.nz)):
-        others[z] = plan.swap(siblings[z])
+        other = plan.swap(siblings[z])
+        both = [
+            blocks[z][x * plan.block : (x + 1) * plan.block] + other[x * plan.block : (x + 1) * plan.block]
+            for x in range(plan.nx)
+        ]
+        mine[z], theirs[z] = both[0], both[1:]
+    if plan.nz == 4:
+        theirs[:3] = together(*theirs[:3])
+        mine[2], weight_own, natural = together(mine[2], weight_own, natural)
     near = []
     for z in reversed(range(plan.nz)):
-        parts = [
-            blocks[z][x * plan.block : (x + 1) * plan.block] + others[z][x * plan.block : (x + 1) * plan.block]
-            for x in range(1, plan.nx)
-        ]
-        terms = line_reduce(plan, "x", [None] + parts)[1:]
-        if z:
-            mine = blocks[z][: plan.block] + others[z][: plan.block]
-            near.insert(0, sum(terms, mine))
-        else:
-            near.insert(0, None)
-            near_terms = [blocks[z], others[z]] + terms
-    parts = near_terms + line_reduce(plan, "z", near)[1:]
+        terms = line_reduce(plan, "x", [mine[z]] + theirs[z])
+        near.insert(0, sum(terms[1:], terms[0]) if z else None)
+    parts = terms + line_reduce(plan, "z", near)[1:]
     new_first, new_second, block, stats = update(
         plan, parts, first_moment[0], second_moment[0], weight_own, natural
     )
@@ -446,23 +485,9 @@
         stats = stats + lax.ppermute(stats, "mp", [(i, i ^ hop) for i in range(plan.narrow)])
         hop *= 2
     block = lax.dynamic_update_slice(block, block[plan.own :] + stats, (plan.own, 0))
-    pieces, slots = [], []
-    for far_z, value in enumerate(line_gather(plan, "z", plan.nz, block)):
-        for far_x, piece in enumerate(line_gather(plan, "x", plan.nx, value)):
-            pieces += [piece, plan.swap(piece)]
-            slots += [(far_z, far_x, 0), (far_z, far_x, 1)]
-    norm_sum, ratios = tails(plan, my_place, pieces, slots)
-    norm_sum, ratios = norm_sum.reshape(norm_grads.shape[1:]), ratios[:, 0]
-    new_weights = finish(plan, position, learning * ratios, weights, pieces, slots)
-
-    gain_rows = norm_state[0]
-    norm_one, norm_two, norm_update = adam_step(norm_sum, norm_state[1], norm_state[2], gain_rows)
-    norm_ratio = jnp.sqrt(jnp.sum(gain_rows * gain_rows, axis=1)) / (
-        jnp.sqrt(jnp.sum(norm_update * norm_update, axis=1)) + epsilon
-    )
-    new_gains = gain_rows - learning * norm_ratio[:, None] * norm_update
-    new_state = jnp.stack([new_gains, norm_one, norm_two])
-    trust_ratios = jnp.concatenate([ratios, norm_ratio])
+    found = gather(plan, block)
+    slots, pieces = [slot for slot, _ in found], [piece for _, piece in found]
+    new_weights, new_state, trust_ratios = finish(plan, my_place, position, norm_state, weights, pieces, slots)
     return (new_weights, new_first[None], new_second[None], new_state, trust_ratios)
 
 

time: 215 us -> 201 us (0.935)
  waiting for transfers between devices: 92.6 us -> 86.5 us
  Pallas kernels: 62.9 us -> 58 us
  local copies, waits for them, and re-layouts: 4.11 us -> 0.7 us
    ppermute x30, waiting for transfers between devices: 90.3 us -> 84.4 us  [send(): return lax.ppermute(value, 'dp', every)]
    pallas_call x1, Pallas kernels: 5.34 us -> 2.62 us  [update(): pl.pallas_call(functools.partial(update_kernel, plan, len(parts)), out_sh...]
    pallas_call x1 -> x0, Pallas kernels: 2.33 us -> none  [tails(): pl.pallas_call(functools.partial(tails_kernel, plan, slots), out_shape=[j...]
  transfers between devices with their start and end apart: 31 -> 31, of which waited for: 16 -> 17; matrix products, arithmetic and copies ran while one was open for 1% -> 3% of each run, Pallas kernels for 3% -> 3%
where the time goes in v4:
time: 201 us; the launch traced here: 200 us
  waiting for transfers between devices  86.5 us (43%)
  Pallas kernels  58 us (29%)
  starting transfers between devices  48 us (24%)
  other arithmetic  5.72 us (3%)
    ppermute x30, waiting for transfers between devices, send(): return lax.ppermute(value, 'dp', every)  84.4 us
    ppermute x30, starting transfers between devices, send(): return lax.ppermute(value, 'dp', every)  46.4 us
    pallas_call x1, Pallas kernels, finish(): pl.pallas_call(functools.partial(finish_kernel, plan, tile, slots), grid=...  25 us
    pallas_call x1, Pallas kernels, place(): pl.pallas_call(functools.partial(place_kernel, plan), out_shape=[jax.Shap...  24 us
    pallas_call x1, Pallas kernels, owned(): pl.pallas_call(functools.partial(owned_kernel, plan), out_shape=[jax.Shap...  6.31 us
  transfers between devices with their start and end apart: 31, of which 17 were waited for; matrix products, arithmetic and copies ran while one was open for 3% of the time, Pallas kernels for 3%

profile of v4, /device:TPU:0, one launch (start us, length us, event | category | flops | bytes accessed | tf_op | source)
XLA Modules:
  0.0 199.9 jit_solution(2081630757381068016)
XLA Ops:
  0.7 0.6 pad_add_fusion.place_ref
  1.3 24.0 %place_gradients.1 = (f32[2192,128]{1,0:T(8,128)}, f32[2192,128]{1,0:T(8,128)}, f32[2192,128]{1,0:T(8,128)}, f32[2192,128]{1,0:T(8,128)}, f32[2192,128]{1,0:T(8,...) custom-call(s32[3]{0:T(128)} %pad_add_fusion.place_ref, ...), custom_call_target="tpu_custom_call" | custom-call | tf_op jit(solution)/shard_map/place_gradients/pallas_call | solution.py:216
  25.3 0.5 collective-permute-start
  25.8 0.1 collective-permute-start.1
  25.9 0.4 collective-permute-start.2
  26.3 0.1 collective-permute-start.6
  26.4 2.0 %collective-permute-done = f32[2192,128]{1,0:T(8,128)S(1)} collective-permute-done((f32[2192,128]{1,0:T(8,128)}, f32[2192,128]{1,0:T(8,128)S(1)}, u32[]{:S(2)}, u32[]{:S(2)}) %collective-permute-start) | collective-permute-done | bytes 1122336 | tf_op jit(solution)/shard_map/ppermute | solution.py:72
  28.4 1.5 slice_add_fusion.6
  29.9 0.1 collective-permute-done.1
  30.0 0.9 slice_add_fusion.5
  30.9 0.7 collective-permute-done.2
  31.6 1.0 slice_add_fusion.2
  32.6 2.9 %collective-permute-start.5 = (f32[1096,128]{1,0:T(8,128)}, f32[1096,128]{1,0:T(8,128)}, u32[]{:S(2)}, u32[]{:S(2)}) collective-permute-start(f32[1096,128]{1,0:T(8,128)} %get-tuple-element.52), channel_id=1, source_target_pairs={{0,4},{2,6},{4,0},{6,2},{8,12},{10,14},{12,8},{14,10},{16,20},{18,... | collective-permute-start | bytes 1683464 | tf_op jit(solution)/shard_map/ppermute | solution.py:72
  35.5 6.3 %owned_weights.1 = (f32[1088,128]{1,0:T(8,128)}, s32[1152,128]{1,0:T(8,128)}) custom-call(s32[3]{0:T(128)} %pad_add_fusion.place_ref, s32[136,128]{1,0:T(8,128)} %bitcast.14, f32[17408,128]{1,0:T(8,128)} %weights_ref.3), custom_call_target="tpu_custom_call" | custom-call | bytes 20971520 | tf_op jit(solution)/shard_map/owned_weights/pallas_call | solution.py:294
  41.8 0.1 slice_add_fusion
  41.9 0.2 collective-permute-start.7
  42.1 7.2 %collective-permute-done.5 = f32[1096,128]{1,0:T(8,128)} collective-permute-done((f32[1096,128]{1,0:T(8,128)}, f32[1096,128]{1,0:T(8,128)}, u32[]{:S(2)}, u32[]{:S(2)}) %collective-permute-start.5) | collective-permute-done | bytes 561184 | tf_op jit(solution)/shard_map/ppermute | solution.py:72
  49.3 1.1 add.72
  50.4 4.2 %collective-permute-start.11 = (f32[1096,128]{1,0:T(8,128)S(1)}, f32[1096,128]{1,0:T(8,128)S(1)}, u32[]{:S(2)}, u32[]{:S(2)}) collective-permute-start(f32[1096,128]{1,0:T(8,128)S(1)} %add.72), channel_id=1, source_target_pairs={{0,8},{2,10},{4,12},{6,14},{24,16},{26,18},{28,20},{30,22},{1,9},{... | collective-permute-start | bytes 1683464 | tf_op jit(solution)/shard_map/ppermute | solution.py:72
  54.6 6.1 %collective-permute-done.7 = f32[1096,128]{1,0:T(8,128)S(1)} collective-permute-done((f32[1096,128]{1,0:T(8,128)S(1)}, f32[1096,128]{1,0:T(8,128)S(1)}, u32[]{:S(2)}, u32[]{:S(2)}) %collective-permute-start.7) | collective-permute-done | bytes 561184 | tf_op jit(solution)/shard_map/ppermute | solution.py:72
  60.7 4.5 %collective-permute-done.11 = f32[1096,128]{1,0:T(8,128)S(1)} collective-permute-done((f32[1096,128]{1,0:T(8,128)S(1)}, f32[1096,128]{1,0:T(8,128)S(1)}, u32[]{:S(2)}, u32[]{:S(2)}) %collective-permute-start.11) | collective-permute-done | bytes 561184 | tf_op jit(solution)/shard_map/ppermute | solution.py:72
  65.2 0.1 fusion.3
  65.4 4.4 %collective-permute-start.8 = (f32[1096,128]{1,0:T(8,128)S(1)}, f32[1096,128]{1,0:T(8,128)S(1)}, u32[]{:S(2)}, u32[]{:S(2)}) collective-permute-start(f32[1096,128]{1,0:T(8,128)S(1)} %get-tuple-element.76), channel_id=1, source_target_pairs={{0,8},{2,10},{4,12},{6,14},{24,16},{26,18},{28,20},{30,22},{1,9},{... | collective-permute-start | bytes 1683464 | tf_op jit(solution)/shard_map/ppermute | solution.py:72
  69.8 1.6 collective-permute-start.4
  71.4 8.1 %collective-permute-done.8 = f32[1096,128]{1,0:T(8,128)S(1)} collective-permute-done((f32[1096,128]{1,0:T(8,128)S(1)}, f32[1096,128]{1,0:T(8,128)S(1)}, u32[]{:S(2)}, u32[]{:S(2)}) %collective-permute-start.8) | collective-permute-done | bytes 561184 | tf_op jit(solution)/shard_map/ppermute | solution.py:72
  79.5 0.1 add.76
  79.6 0.7 collective-permute-start.9
  80.3 1.6 collective-permute-start.3
  81.8 0.8 collective-permute-start.12
  82.7 1.3 collective-permute-done.4
  84.0 0.2 fusion.2
  84.1 15.7 %collective-permute-start.10 = (f32[1096,128]{1,0:T(8,128)S(1)}, f32[1096,128]{1,0:T(8,128)S(1)}, u32[]{:S(2)}, u32[]{:S(2)}) collective-permute-start(f32[1096,128]{1,0:T(8,128)S(1)} %fusion.2), channel_id=1, source_target_pairs={{0,8},{2,10},{4,12},{6,14},{8,0},{10,2},{12,4},{14,6},{16,24},{18,... | collective-permute-start | bytes 1683464 | tf_op jit(solution)/shard_map/ppermute | solution.py:72
  99.8 7.5 %collective-permute-done.10.refs_2_ = f32[1096,128]{1,0:T(8,128)S(1)} collective-permute-done((f32[1096,128]{1,0:T(8,128)S(1)}, f32[1096,128]{1,0:T(8,128)S(1)}, u32[]{:S(2)}, u32[]{:S(2)}) %collective-permute-start.10) | collective-permute-done | bytes 561184 | tf_op jit(solution)/shard_map/ppermute | solution.py:72
  107.4 2.6 %moments.1 = (f32[1088,128]{1,0:T(8,128)}, f32[1088,128]{1,0:T(8,128)}, f32[1096,128]{1,0:T(8,128)S(1)}, f32[8,128]{1,0:T(8,128)S(1)}) custom-call(f32[1096,128]{1,0:T(8,128)S(1)} %get-tuple-element.80.refs_0_, f32[1096,128]{1,0:T(8,128)S(1)} %collective-permute-done.3.refs_1_, f32[1096,128]{1,0:T(8,128)S(1)} %collective-permute-done.10.refs_2_, ...), custom_call_target="tpu_custom_call" | custom-call | tf_op jit(solution)/shard_map/moments/pallas_call | solution.py:349
  110.0 1.5 collective-permute-start.13
  111.5 2.1 %collective-permute-done.13 = f32[8,128]{1,0:T(8,128)S(1)} collective-permute-done((f32[8,128]{1,0:T(8,128)S(1)}, f32[8,128]{1,0:T(8,128)S(1)}, u32[]{:S(2)}, u32[]{:S(2)}) %collective-permute-start.13) | collective-permute-done | bytes 4128 | tf_op jit(solution)/shard_map/ppermute | solution.py:485
  113.6 1.5 collective-permute-start.16
  115.1 0.7 collective-permute-start.15
  115.8 4.9 %collective-permute-start.14 = (f32[1096,128]{1,0:T(8,128)S(1)}, f32[1096,128]{1,0:T(8,128)S(1)}, u32[]{:S(2)}, u32[]{:S(2)}) collective-permute-start(f32[1096,128]{1,0:T(8,128)S(1)} %add_dynamic-update-slice_fusion.refs_0_), channel_id=1, source_target_pairs={{0,8},{2,10},{4,12},{6,14},{8,0},{10,2},{12,4},{14,6},{16,24},{18,... | collective-permute-start | bytes 1683464 | tf_op jit(solution)/shard_map/ppermute | solution.py:72
  120.7 2.5 %collective-permute-done.16.refs_1_ = f32[1096,128]{1,0:T(8,128)S(1)} collective-permute-done((f32[1096,128]{1,0:T(8,128)S(1)}, f32[1096,128]{1,0:T(8,128)S(1)}, u32[]{:S(2)}, u32[]{:S(2)}) %collective-permute-start.16) | collective-permute-done | bytes 561184 | tf_op jit(solution)/shard_map/ppermute | solution.py:72
  123.2 8.9 %collective-permute-done.14.refs_4_ = f32[1096,128]{1,0:T(8,128)S(1)} collective-permute-done((f32[1096,128]{1,0:T(8,128)S(1)}, f32[1096,128]{1,0:T(8,128)S(1)}, u32[]{:S(2)}, u32[]{:S(2)}) %collective-permute-start.14) | collective-permute-done | bytes 561184 | tf_op jit(solution)/shard_map/ppermute | solution.py:72
  132.1 1.3 collective-permute-start.20
  133.4 0.6 collective-permute-start.21
  134.0 0.7 collective-permute-start.19
  134.7 13.4 %collective-permute-done.20 = f32[1096,128]{1,0:T(8,128)S(1)} collective-permute-done((f32[1096,128]{1,0:T(8,128)S(1)}, f32[1096,128]{1,0:T(8,128)S(1)}, u32[]{:S(2)}, u32[]{:S(2)}) %collective-permute-start.20) | collective-permute-done | bytes 561184 | tf_op jit(solution)/shard_map/ppermute | solution.py:72
  148.0 0.8 collective-permute-done.21.refs_5_
  148.9 0.1 add.81.refs_8_
  149.0 0.6 collective-permute-start.25
  149.6 1.3 collective-permute-start.24
  150.9 0.1 collective-permute-start.17
  150.9 0.5 collective-permute-start.18
  151.4 0.1 collective-permute-start.22
  151.5 11.0 %collective-permute-done.25.refs_9_ = f32[1096,128]{1,0:T(8,128)} collective-permute-done((f32[1096,128]{1,0:T(8,128)S(1)}, f32[1096,128]{1,0:T(8,128)}, u32[]{:S(2)}, u32[]{:S(2)}) %collective-permute-start.25) | collective-permute-done | bytes 561184 | tf_op jit(solution)/shard_map/ppermute | solution.py:72
  162.5 0.1 add.82.refs_10_
  162.7 0.1 collective-permute-start.26
  162.7 0.1 collective-permute-start.23
  162.8 0.5 collective-permute-start.29
  163.3 0.1 collective-permute-start.27
  163.4 0.4 collective-permute-start.28
  163.8 8.6 %collective-permute-done.26.refs_11_ = f32[1096,128]{1,0:T(8,128)} collective-permute-done((f32[1096,128]{1,0:T(8,128)S(1)}, f32[1096,128]{1,0:T(8,128)}, u32[]{:S(2)}, u32[]{:S(2)}) %collective-permute-start.26) | collective-permute-done | bytes 561184 | tf_op jit(solution)/shard_map/ppermute | solution.py:72
  172.4 0.1 collective-permute-start.30
  172.5 0.6 reshape.18.norm_ref
  173.2 1.6 collective-permute-done.30.refs_15_
  174.8 25.0 %new_weights.1 = (f32[17408,128]{1,0:T(8,128)}, f32[3,2,1024]{2,1,0:T(2,128)}, f32[7]{0:T(128)}) custom-call(s32[3]{0:T(128)} %pad_add_fusion.place_ref, s32[136,128]{1,0:T(8,128)} %get-tuple-element.40.position_ref, f32[3,16,128]{2,1,0:T(8,128)} %reshape.18.norm_ref, f32[17408,128]{1,0:T(8,128)} %weights_ref.3, f32[1096,128]{1,0:T(8,128)} %copy-done.1, ...), custom_call_target="tpu_custom_call" | custom-call | tf_op jit(solution)/shard_map/new_weights/pallas_call | solution.py:432
  (57 shorter events, 0.1 us)
Async XLA Ops:
  25.3 3.1 %collective-permute-start = (f32[2192,128]{1,0:T(8,128)}, f32[2192,128]{1,0:T(8,128)S(1)}, u32[]{:S(2)}, u32[]{:S(2)}) collective-permute-start(f32[2192,128]{1,0:T(8,128)} %get-tuple-element.42), channel_id=1, source_target_pairs={{0,2},{2,0},{4,6},{6,4},{8,10},{10,8},{12,14},{14,12},{16,18},{18,... | collective-permute-start | bytes 3366920 | tf_op jit(solution)/shard_map/ppermute | solution.py:72
  25.8 4.2 %collective-permute-start.1 = (f32[2192,128]{1,0:T(8,128)}, f32[2192,128]{1,0:T(8,128)S(1)}, u32[]{:S(2)}, u32[]{:S(2)}) collective-permute-start(f32[2192,128]{1,0:T(8,128)} %get-tuple-element.44), channel_id=1, source_target_pairs={{0,2},{2,0},{4,6},{6,4},{8,10},{10,8},{12,14},{14,12},{16,18},{18,... | collective-permute-start | bytes 3366920 | tf_op jit(solution)/shard_map/ppermute | solution.py:72
  25.9 5.7 %collective-permute-start.2 = (f32[2192,128]{1,0:T(8,128)}, f32[2192,128]{1,0:T(8,128)S(1)}, u32[]{:S(2)}, u32[]{:S(2)}) collective-permute-start(f32[2192,128]{1,0:T(8,128)} %get-tuple-element.46), channel_id=1, source_target_pairs={{0,2},{2,0},{4,6},{6,4},{8,10},{10,8},{12,14},{14,12},{16,18},{18,... | collective-permute-start | bytes 3366920 | tf_op jit(solution)/shard_map/ppermute | solution.py:72
  26.3 15.5 %collective-permute-start.6 = (f32[2192,128]{1,0:T(8,128)}, f32[2192,128]{1,0:T(8,128)S(1)}, u32[]{:S(2)}, u32[]{:S(2)}) collective-permute-start(f32[2192,128]{1,0:T(8,128)} %get-tuple-element.54), channel_id=1, source_target_pairs={{0,2},{2,0},{4,6},{6,4},{8,10},{10,8},{12,14},{14,12},{16,18},{18,... | collective-permute-start | bytes 3366920 | tf_op jit(solution)/shard_map/ppermute | solution.py:72
  28.4 1.6 copy-start.8
  29.9 1.7 copy-start.9
  32.6 9.2 %copy-start.7 = (f32[2192,128]{1,0:T(8,128)S(1)}, f32[2192,128]{1,0:T(8,128)}, u32[]{:S(2)}) copy-start(f32[2192,128]{1,0:T(8,128)} %get-tuple-element.53) | copy-start | bytes 3366916
  32.6 16.7 %collective-permute-start.5 = (f32[1096,128]{1,0:T(8,128)}, f32[1096,128]{1,0:T(8,128)}, u32[]{:S(2)}, u32[]{:S(2)}) collective-permute-start(f32[1096,128]{1,0:T(8,128)} %get-tuple-element.52), channel_id=1, source_target_pairs={{0,4},{2,6},{4,0},{6,2},{8,12},{10,14},{12,8},{14,10},{16,20},{18,... | collective-permute-start | bytes 1683464 | tf_op jit(solution)/shard_map/ppermute | solution.py:72
  41.9 18.8 %collective-permute-start.7 = (f32[1096,128]{1,0:T(8,128)S(1)}, f32[1096,128]{1,0:T(8,128)S(1)}, u32[]{:S(2)}, u32[]{:S(2)}) collective-permute-start(f32[1096,128]{1,0:T(8,128)S(1)} %slice_add_fusion), channel_id=1, source_target_pairs={{0,4},{2,6},{4,0},{6,2},{8,12},{10,14},{12,8},{14,10},{16,20},{18,... | collective-permute-start | bytes 1683464 | tf_op jit(solution)/shard_map/ppermute | solution.py:72
  50.4 19.4 %copy-start.19 = (f32[1096,128]{1,0:T(8,128)S(1)}, f32[1096,128]{1,0:T(8,128)}, u32[]{:S(2)}) copy-start(f32[1096,128]{1,0:T(8,128)} %slice_add_fusion.5) | copy-start | bytes 1683460
  50.4 14.8 %collective-permute-start.11 = (f32[1096,128]{1,0:T(8,128)S(1)}, f32[1096,128]{1,0:T(8,128)S(1)}, u32[]{:S(2)}, u32[]{:S(2)}) collective-permute-start(f32[1096,128]{1,0:T(8,128)S(1)} %add.72), channel_id=1, source_target_pairs={{0,8},{2,10},{4,12},{6,14},{24,16},{26,18},{28,20},{30,22},{1,9},{... | collective-permute-start | bytes 1683464 | tf_op jit(solution)/shard_map/ppermute | solution.py:72
  65.4 14.1 %collective-permute-start.8 = (f32[1096,128]{1,0:T(8,128)S(1)}, f32[1096,128]{1,0:T(8,128)S(1)}, u32[]{:S(2)}, u32[]{:S(2)}) collective-permute-start(f32[1096,128]{1,0:T(8,128)S(1)} %get-tuple-element.76), channel_id=1, source_target_pairs={{0,8},{2,10},{4,12},{6,14},{24,16},{26,18},{28,20},{30,22},{1,9},{... | collective-permute-start | bytes 1683464 | tf_op jit(solution)/shard_map/ppermute | solution.py:72
  69.8 14.1 %collective-permute-start.4 = (f32[1096,128]{1,0:T(8,128)S(1)}, f32[1096,128]{1,0:T(8,128)S(1)}, u32[]{:S(2)}, u32[]{:S(2)}) collective-permute-start(f32[1096,128]{1,0:T(8,128)S(1)} %copy-done.19), channel_id=1, source_target_pairs={{0,4},{2,6},{4,0},{6,2},{8,12},{10,14},{12,8},{14,10},{16,20},{18,... | collective-permute-start | bytes 1683464 | tf_op jit(solution)/shard_map/ppermute | solution.py:72
  79.6 4.4 %collective-permute-start.9 = (f32[1096,128]{1,0:T(8,128)S(1)}, f32[1096,128]{1,0:T(8,128)S(1)}, u32[]{:S(2)}, u32[]{:S(2)}) collective-permute-start(f32[1096,128]{1,0:T(8,128)S(1)} %add.76), channel_id=1, source_target_pairs={{8,16},{10,18},{12,20},{14,22},{16,8},{18,10},{20,12},{22,14},{9,1... | collective-permute-start | bytes 1683464 | tf_op jit(solution)/shard_map/ppermute | solution.py:72
  80.3 19.6 %collective-permute-start.3 = (f32[1096,128]{1,0:T(8,128)S(1)}, f32[1096,128]{1,0:T(8,128)S(1)}, u32[]{:S(2)}, u32[]{:S(2)}) collective-permute-start(f32[1096,128]{1,0:T(8,128)S(1)} %get-tuple-element.47), channel_id=1, source_target_pairs={{0,4},{2,6},{4,0},{6,2},{8,12},{10,14},{12,8},{14,10},{16,20},{18,... | collective-permute-start | bytes 1683464 | tf_op jit(solution)/shard_map/ppermute | solution.py:72
  81.8 25.6 %copy-start = (s32[1152,128]{1,0:T(8,128)S(1)}, s32[1152,128]{1,0:T(8,128)}, u32[]{:S(2)}) copy-start(s32[1152,128]{1,0:T(8,128)} %get-tuple-element.56.refs_7_) | copy-start | bytes 1769476
  81.8 25.6 %copy-start.2 = (f32[1,1088,128]{2,1,0:T(8,128)S(1)}, f32[1,1088,128]{2,1,0:T(8,128)}, u32[]{:S(2)}) copy-start(f32[1,1088,128]{2,1,0:T(8,128)} %param.9) | copy-start | bytes 1671172
  81.8 25.6 %copy-start.3 = (f32[1,1088,128]{2,1,0:T(8,128)S(1)}, f32[1,1088,128]{2,1,0:T(8,128)}, u32[]{:S(2)}) copy-start(f32[1,1088,128]{2,1,0:T(8,128)} %param.10) | copy-start | bytes 1671172
  81.8 25.6 %copy-start.4 = (f32[1088,128]{1,0:T(8,128)S(1)}, f32[1088,128]{1,0:T(8,128)}, u32[]{:S(2)}) copy-start(f32[1088,128]{1,0:T(8,128)} %get-tuple-element.55.refs_6_) | copy-start | bytes 1671172
  81.8 18.0 %collective-permute-start.12 = (f32[1096,128]{1,0:T(8,128)S(1)}, f32[1096,128]{1,0:T(8,128)S(1)}, u32[]{:S(2)}, u32[]{:S(2)}) collective-permute-start(f32[1096,128]{1,0:T(8,128)S(1)} %get-tuple-element.75), channel_id=1, source_target_pairs={{8,16},{10,18},{12,20},{14,22},{16,8},{18,10},{20,12},{22,14},{9,1... | collective-permute-start | bytes 1683464 | tf_op jit(solution)/shard_map/ppermute | solution.py:72
  84.1 23.2 %collective-permute-start.10 = (f32[1096,128]{1,0:T(8,128)S(1)}, f32[1096,128]{1,0:T(8,128)S(1)}, u32[]{:S(2)}, u32[]{:S(2)}) collective-permute-start(f32[1096,128]{1,0:T(8,128)S(1)} %fusion.2), channel_id=1, source_target_pairs={{0,8},{2,10},{4,12},{6,14},{8,0},{10,2},{12,4},{14,6},{16,24},{18,... | collective-permute-start | bytes 1683464 | tf_op jit(solution)/shard_map/ppermute | solution.py:72
  110.0 3.6 %collective-permute-start.13 = (f32[8,128]{1,0:T(8,128)S(1)}, f32[8,128]{1,0:T(8,128)S(1)}, u32[]{:S(2)}, u32[]{:S(2)}) collective-permute-start(f32[8,128]{1,0:T(8,128)S(1)} %get-tuple-element.58), channel_id=1, source_target_pairs={{0,1},{1,0},{2,3},{3,2},{4,5},{5,4},{6,7},{7,6},{8,9},{9,8},{10,11... | collective-permute-start | bytes 12296 | tf_op jit(solution)/shard_map/ppermute | solution.py:485
  113.6 49.0 %copy-start.1 = (f32[1096,128]{1,0:T(8,128)}, f32[1096,128]{1,0:T(8,128)S(1)}, u32[]{:S(2)}) copy-start(f32[1096,128]{1,0:T(8,128)S(1)} %add_dynamic-update-slice_fusion.refs_0_) | copy-start | bytes 1683460
  113.6 9.6 %collective-permute-start.16 = (f32[1096,128]{1,0:T(8,128)S(1)}, f32[1096,128]{1,0:T(8,128)S(1)}, u32[]{:S(2)}, u32[]{:S(2)}) collective-permute-start(f32[1096,128]{1,0:T(8,128)S(1)} %add_dynamic-update-slice_fusion.refs_0_), channel_id=1, source_target_pairs={{0,4},{2,6},{4,0},{6,2},{8,12},{10,14},{12,8},{14,10},{16,20},{18,... | collective-permute-start | bytes 1683464 | tf_op jit(solution)/shard_map/ppermute | solution.py:72
  115.1 8.1 %collective-permute-start.15 = (f32[1096,128]{1,0:T(8,128)S(1)}, f32[1096,128]{1,0:T(8,128)S(1)}, u32[]{:S(2)}, u32[]{:S(2)}) collective-permute-start(f32[1096,128]{1,0:T(8,128)S(1)} %add_dynamic-update-slice_fusion.refs_0_), channel_id=1, source_target_pairs={{8,16},{10,18},{12,20},{14,22},{16,8},{18,10},{20,12},{22,14},{9,1... | collective-permute-start | bytes 1683464 | tf_op jit(solution)/shard_map/ppermute | solution.py:72
  115.8 16.3 %collective-permute-start.14 = (f32[1096,128]{1,0:T(8,128)S(1)}, f32[1096,128]{1,0:T(8,128)S(1)}, u32[]{:S(2)}, u32[]{:S(2)}) collective-permute-start(f32[1096,128]{1,0:T(8,128)S(1)} %add_dynamic-update-slice_fusion.refs_0_), channel_id=1, source_target_pairs={{0,8},{2,10},{4,12},{6,14},{8,0},{10,2},{12,4},{14,6},{16,24},{18,... | collective-permute-start | bytes 1683464 | tf_op jit(solution)/shard_map/ppermute | solution.py:72
  123.2 39.4 %copy-start.10 = (f32[1096,128]{1,0:T(8,128)}, f32[1096,128]{1,0:T(8,128)S(1)}, u32[]{:S(2)}) copy-start(f32[1096,128]{1,0:T(8,128)S(1)} %collective-permute-done.16.refs_1_) | copy-start | bytes 1683460
  132.1 30.6 %copy-start.11 = (f32[1096,128]{1,0:T(8,128)}, f32[1096,128]{1,0:T(8,128)S(1)}, u32[]{:S(2)}) copy-start(f32[1096,128]{1,0:T(8,128)S(1)} %collective-permute-done.14.refs_4_) | copy-start | bytes 1683460
  132.1 16.0 %collective-permute-start.20 = (f32[1096,128]{1,0:T(8,128)S(1)}, f32[1096,128]{1,0:T(8,128)S(1)}, u32[]{:S(2)}, u32[]{:S(2)}) collective-permute-start(f32[1096,128]{1,0:T(8,128)S(1)} %collective-permute-done.15), channel_id=1, source_target_pairs={{8,0},{10,2},{12,4},{14,6},{16,24},{18,26},{20,28},{22,30},{9,1},{... | collective-permute-start | bytes 1683464 | tf_op jit(solution)/shard_map/ppermute | solution.py:72
  133.4 15.5 %collective-permute-start.21 = (f32[1096,128]{1,0:T(8,128)S(1)}, f32[1096,128]{1,0:T(8,128)S(1)}, u32[]{:S(2)}, u32[]{:S(2)}) collective-permute-start(f32[1096,128]{1,0:T(8,128)S(1)} %collective-permute-done.14.refs_4_), channel_id=1, source_target_pairs={{0,4},{2,6},{4,0},{6,2},{8,12},{10,14},{12,8},{14,10},{16,20},{18,... | collective-permute-start | bytes 1683464 | tf_op jit(solution)/shard_map/ppermute | solution.py:72
  134.0 14.9 %collective-permute-start.19 = (f32[1096,128]{1,0:T(8,128)S(1)}, f32[1096,128]{1,0:T(8,128)S(1)}, u32[]{:S(2)}, u32[]{:S(2)}) collective-permute-start(f32[1096,128]{1,0:T(8,128)S(1)} %collective-permute-done.14.refs_4_), channel_id=1, source_target_pairs={{8,16},{10,18},{12,20},{14,22},{16,8},{18,10},{20,12},{22,14},{9,1... | collective-permute-start | bytes 1683464 | tf_op jit(solution)/shard_map/ppermute | solution.py:72
  148.9 13.9 %copy-start.12 = (f32[1096,128]{1,0:T(8,128)}, f32[1096,128]{1,0:T(8,128)S(1)}, u32[]{:S(2)}) copy-start(f32[1096,128]{1,0:T(8,128)S(1)} %collective-permute-done.21.refs_5_) | copy-start | bytes 1683460
  149.0 25.8 %copy-start.5 = (f32[1096,128]{1,0:T(8,128)}, f32[1096,128]{1,0:T(8,128)S(1)}, u32[]{:S(2)}) copy-start(f32[1096,128]{1,0:T(8,128)S(1)} %add.81.refs_8_) | copy-start | bytes 1683460
  149.0 23.5 %copy-start.20 = (f32[3,2,1024]{2,1,0:T(2,128)S(1)}, f32[3,2,1024]{2,1,0:T(2,128)}, u32[]{:S(2)}) copy-start(f32[3,2,1024]{2,1,0:T(2,128)} %param.13) | copy-start | bytes 73732
  149.0 13.6 %collective-permute-start.25 = (f32[1096,128]{1,0:T(8,128)S(1)}, f32[1096,128]{1,0:T(8,128)}, u32[]{:S(2)}, u32[]{:S(2)}) collective-permute-start(f32[1096,128]{1,0:T(8,128)S(1)} %add.81.refs_8_), channel_id=1, source_target_pairs={{0,4},{2,6},{4,0},{6,2},{8,12},{10,14},{12,8},{14,10},{16,20},{18,... | collective-permute-start | bytes 1683464 | tf_op jit(solution)/shard_map/ppermute | solution.py:72
  149.6 13.0 %collective-permute-start.24 = (f32[1096,128]{1,0:T(8,128)S(1)}, f32[1096,128]{1,0:T(8,128)S(1)}, u32[]{:S(2)}, u32[]{:S(2)}) collective-permute-start(f32[1096,128]{1,0:T(8,128)S(1)} %collective-permute-done.19), channel_id=1, source_target_pairs={{8,0},{10,2},{12,4},{14,6},{16,24},{18,26},{20,28},{22,30},{9,1},{... | collective-permute-start | bytes 1683464 | tf_op jit(solution)/shard_map/ppermute | solution.py:72
  150.9 12.0 %collective-permute-start.17 = (f32[1096,128]{1,0:T(8,128)S(1)}, f32[1096,128]{1,0:T(8,128)S(1)}, u32[]{:S(2)}, u32[]{:S(2)}) collective-permute-start(f32[1096,128]{1,0:T(8,128)S(1)} %add_dynamic-update-slice_fusion.refs_0_), channel_id=1, source_target_pairs={{0,2},{2,0},{4,6},{6,4},{8,10},{10,8},{12,14},{14,12},{16,18},{18,... | collective-permute-start | bytes 1683464 | tf_op jit(solution)/shard_map/ppermute | solution.py:72
  150.9 12.4 %collective-permute-start.18 = (f32[1096,128]{1,0:T(8,128)S(1)}, f32[1096,128]{1,0:T(8,128)S(1)}, u32[]{:S(2)}, u32[]{:S(2)}) collective-permute-start(f32[1096,128]{1,0:T(8,128)S(1)} %collective-permute-done.16.refs_1_), channel_id=1, source_target_pairs={{0,2},{2,0},{4,6},{6,4},{8,10},{10,8},{12,14},{14,12},{16,18},{18,... | collective-permute-start | bytes 1683464 | tf_op jit(solution)/shard_map/ppermute | solution.py:72
  151.4 12.0 %collective-permute-start.22 = (f32[1096,128]{1,0:T(8,128)S(1)}, f32[1096,128]{1,0:T(8,128)S(1)}, u32[]{:S(2)}, u32[]{:S(2)}) collective-permute-start(f32[1096,128]{1,0:T(8,128)S(1)} %collective-permute-done.14.refs_4_), channel_id=1, source_target_pairs={{0,2},{2,0},{4,6},{6,4},{8,10},{10,8},{12,14},{14,12},{16,18},{18,... | collective-permute-start | bytes 1683464 | tf_op jit(solution)/shard_map/ppermute | solution.py:72
  162.6 12.1 %copy-start.6 = (f32[1096,128]{1,0:T(8,128)}, f32[1096,128]{1,0:T(8,128)S(1)}, u32[]{:S(2)}) copy-start(f32[1096,128]{1,0:T(8,128)S(1)} %add.82.refs_10_) | copy-start | bytes 1683460
  162.7 9.7 %collective-permute-start.26 = (f32[1096,128]{1,0:T(8,128)S(1)}, f32[1096,128]{1,0:T(8,128)}, u32[]{:S(2)}, u32[]{:S(2)}) collective-permute-start(f32[1096,128]{1,0:T(8,128)S(1)} %add.82.refs_10_), channel_id=1, source_target_pairs={{0,4},{2,6},{4,0},{6,2},{8,12},{10,14},{12,8},{14,10},{16,20},{18,... | collective-permute-start | bytes 1683464 | tf_op jit(solution)/shard_map/ppermute | solution.py:72
  162.7 10.4 %collective-permute-start.23 = (f32[1096,128]{1,0:T(8,128)S(1)}, f32[1096,128]{1,0:T(8,128)}, u32[]{:S(2)}, u32[]{:S(2)}) collective-permute-start(f32[1096,128]{1,0:T(8,128)S(1)} %collective-permute-done.21.refs_5_), channel_id=1, source_target_pairs={{0,2},{2,0},{4,6},{6,4},{8,10},{10,8},{12,14},{14,12},{16,18},{18,... | collective-permute-start | bytes 1683464 | tf_op jit(solution)/shard_map/ppermute | solution.py:72
  162.8 9.6 %copy-start.13 = (f32[1096,128]{1,0:T(8,128)}, f32[1096,128]{1,0:T(8,128)S(1)}, u32[]{:S(2)}) copy-start(f32[1096,128]{1,0:T(8,128)S(1)} %collective-permute-done.17.refs_2_) | copy-start | bytes 1683460
  162.8 10.3 %collective-permute-start.29 = (f32[1096,128]{1,0:T(8,128)S(1)}, f32[1096,128]{1,0:T(8,128)S(1)}, u32[]{:S(2)}, u32[]{:S(2)}) collective-permute-start(f32[1096,128]{1,0:T(8,128)S(1)} %add.82.refs_10_), channel_id=1, source_target_pairs={{0,2},{2,0},{4,6},{6,4},{8,10},{10,8},{12,14},{14,12},{16,18},{18,... | collective-permute-start | bytes 1683464 | tf_op jit(solution)/shard_map/ppermute | solution.py:72
  163.3 9.1 %copy-start.14 = (f32[1096,128]{1,0:T(8,128)}, f32[1096,128]{1,0:T(8,128)S(1)}, u32[]{:S(2)}) copy-start(f32[1096,128]{1,0:T(8,128)S(1)} %collective-permute-done.18.refs_3_) | copy-start | bytes 1683460
  163.3 9.8 %collective-permute-start.27 = (f32[1096,128]{1,0:T(8,128)S(1)}, f32[1096,128]{1,0:T(8,128)S(1)}, u32[]{:S(2)}, u32[]{:S(2)}) collective-permute-start(f32[1096,128]{1,0:T(8,128)S(1)} %add.81.refs_8_), channel_id=1, source_target_pairs={{0,2},{2,0},{4,6},{6,4},{8,10},{10,8},{12,14},{14,12},{16,18},{18,... | collective-permute-start | bytes 1683464 | tf_op jit(solution)/shard_map/ppermute | solution.py:72
  163.4 9.0 %copy-start.15 = (f32[1096,128]{1,0:T(8,128)}, f32[1096,128]{1,0:T(8,128)S(1)}, u32[]{:S(2)}) copy-start(f32[1096,128]{1,0:T(8,128)S(1)} %collective-permute-done.22.refs_6_) | copy-start | bytes 1683460
  163.4 9.7 %collective-permute-start.28 = (f32[1096,128]{1,0:T(8,128)}, f32[1096,128]{1,0:T(8,128)S(1)}, u32[]{:S(2)}, u32[]{:S(2)}) collective-permute-start(f32[1096,128]{1,0:T(8,128)} %collective-permute-done.25.refs_9_), channel_id=1, source_target_pairs={{0,2},{2,0},{4,6},{6,4},{8,10},{10,8},{12,14},{14,12},{16,18},{18,... | collective-permute-start | bytes 1683464 | tf_op jit(solution)/shard_map/ppermute | solution.py:72
  172.4 2.4 %collective-permute-start.30 = (f32[1096,128]{1,0:T(8,128)}, f32[1096,128]{1,0:T(8,128)}, u32[]{:S(2)}, u32[]{:S(2)}) collective-permute-start(f32[1096,128]{1,0:T(8,128)} %collective-permute-done.26.refs_11_), channel_id=1, source_target_pairs={{0,2},{2,0},{4,6},{6,4},{8,10},{10,8},{12,14},{14,12},{16,18},{18,... | collective-permute-start | bytes 1683464 | tf_op jit(solution)/shard_map/ppermute | solution.py:72
  173.1 1.7 copy-start.16
  173.1 1.7 copy-start.17
  173.2 1.6 copy-start.18

commit v5 on v4

--- a/solution.py
+++ b/solution.py
@@ -97,6 +97,28 @@
 
 def together(*values):
     return lax.optimization_barrier(values)
+
+
+def reduce(plan, mine, theirs, beside):
+    def along_x(z, own):
+        terms = line_reduce(plan, "x", [own] + theirs[z])
+        return terms
+
+    three = along_x(3, mine[3])
+    two = along_x(2, mine[2])
+    near_three = sum(three[1:], three[0])
+    in_three = plan.send(near_three, "z", INWARD)
+    in_three, *two = together(in_three, *two, *beside)
+    two, beside = two[: -len(beside)], two[-len(beside) :]
+    near_two = sum(two[1:], two[0])
+    one = along_x(1, mine[1])
+    across_two = plan.send(near_two + in_three, "z", MIDDLE)
+    in_two = plan.send(near_two, "z", INWARD)
+    across_two, in_two, *one = together(across_two, in_two, *one)
+    zero = along_x(0, mine[0])
+    pair = plan.send(sum(one[1:], one[0]) + across_two, "z", PAIRS)
+    across_three = plan.send(near_three + in_two, "z", MIDDLE)
+    return zero + [pair, across_three] + beside
 
 
 def gather(plan, block):
@@ -235,7 +257,7 @@
         compiler_params=pltpu.CompilerParams(vmem_limit_bytes=58 * MIB),
         name="place_gradients",
     )(my_place, owners, norm_grads, grads)
-    return outs[: plan.nz][::-1], outs[plan.nz : 2 * plan.nz][::-1], outs[-1]
+    return list(outs[: plan.nz][::-1]), outs[plan.nz : 2 * plan.nz][::-1], outs[-1]
 
 
 def owned_kernel(plan, place_ref, owner_ref, weights_ref, owned_ref, natural_ref, held, listed, order, sem_in, sem_order):
@@ -396,9 +418,11 @@
             trust_ref[k] = jnp.sum(ratio)
         each = plan.norm_rows // 2
         for i in range(2):
-            rows = pl.ds(i * each, each)
-            gains = norm_ref[0, rows, :]
-            one, two, step = adam_rows(norms[rows, :], norm_ref[1, rows, :], norm_ref[2, rows, :], gains)
+            gains, first, second = (
+                jnp.concatenate([norm_ref[j, i : i + 1, row * LANE : (row + 1) * LANE] for row in range(each)], 0)
+                for j in range(3)
+            )
+            one, two, step = adam_rows(norms[i * each : (i + 1) * each, :], first, second, gains)
             gain_square = jnp.sum(jnp.sum(gains * gains, axis=1, keepdims=True), axis=0, keepdims=True)
             step_square = jnp.sum(jnp.sum(step * step, axis=1, keepdims=True), axis=0, keepdims=True)
             ratio = jnp.sqrt(gain_square) / (jnp.sqrt(step_square) + epsilon)
@@ -448,7 +472,7 @@
         ],
         compiler_params=pltpu.CompilerParams(vmem_limit_bytes=58 * MIB),
         name="new_weights",
-    )(my_place, position, norm_state.reshape(3, plan.norm_rows, LANE), weights, *pieces)
+    )(my_place, position, norm_state, weights, *pieces)
 
 
 def local(gradients, weights, first_moment, second_moment, owner_list, norm_grads, norm_state):
@@ -468,14 +492,17 @@
             for x in range(plan.nx)
         ]
         mine[z], theirs[z] = both[0], both[1:]
+        if z == 3:
+            theirs[3], siblings[2], siblings[1], siblings[0] = together(theirs[3], *siblings[2::-1])
     if plan.nz == 4:
-        theirs[:3] = together(*theirs[:3])
-        mine[2], weight_own, natural = together(mine[2], weight_own, natural)
-    near = []
-    for z in reversed(range(plan.nz)):
-        terms = line_reduce(plan, "x", [mine[z]] + theirs[z])
-        near.insert(0, sum(terms[1:], terms[0]) if z else None)
-    parts = terms + line_reduce(plan, "z", near)[1:]
+        parts = reduce(plan, mine, theirs, (weight_own, natural))
+        parts, (weight_own, natural) = parts[:-2], parts[-2:]
+    else:
+        near = []
+        for z in reversed(range(plan.nz)):
+            terms = line_reduce(plan, "x", [mine[z]] + theirs[z])
+            near.insert(0, sum(terms[1:], terms[0]) if z else None)
+        parts = terms + line_reduce(plan, "z", near)[1:]
     new_first, new_second, block, stats = update(
         plan, parts, first_moment[0], second_moment[0], weight_own, natural
     )

time: 201 us -> 185 us (0.920)
  starting transfers between devices: 48 us -> 35.4 us
  other arithmetic: 5.72 us -> 2.64 us
    ppermute x30, starting transfers between devices: 46.4 us -> 33.9 us  [send(): return lax.ppermute(value, 'dp', every)]
  transfers between devices with their start and end apart: 31 -> 31, of which waited for: 17 -> 16; matrix products, arithmetic and copies ran while one was open for 3% -> 0% of each run, Pallas kernels for 3% -> 3%
where the time goes in v5:
time: 185 us; the launch traced here: 183 us
  waiting for transfers between devices  85.4 us (46%)
  Pallas kernels  58 us (31%)
  starting transfers between devices  35.4 us (19%)
  other arithmetic  2.64 us (1%)
    ppermute x30, waiting for transfers between devices, send(): return lax.ppermute(value, 'dp', every)  83.3 us
    ppermute x30, starting transfers between devices, send(): return lax.ppermute(value, 'dp', every)  33.9 us
    pallas_call x1, Pallas kernels, finish(): pl.pallas_call(functools.partial(finish_kernel, plan, tile, slots), grid=...  25.1 us
    pallas_call x1, Pallas kernels, place(): pl.pallas_call(functools.partial(place_kernel, plan), out_shape=[jax.Shap...  24 us
    pallas_call x1, Pallas kernels, owned(): pl.pallas_call(functools.partial(owned_kernel, plan), out_shape=[jax.Shap...  6.31 us
  transfers between devices with their start and end apart: 31, of which 16 were waited for; matrix products, arithmetic and copies ran while one was open for 0% of the time, Pallas kernels for 3%

profile of v5, /device:TPU:0, one launch (start us, length us, event | category | flops | bytes accessed | tf_op | source)
XLA Modules:
  0.0 183.5 jit_solution(16329420218392388121)
XLA Ops:
  0.7 0.6 pad_add_fusion.place_ref
  1.3 24.0 %place_gradients.1 = (f32[2192,128]{1,0:T(8,128)}, f32[2192,128]{1,0:T(8,128)}, f32[2192,128]{1,0:T(8,128)}, f32[2192,128]{1,0:T(8,128)}, f32[2192,128]{1,0:T(8,...) custom-call(s32[3]{0:T(128)} %pad_add_fusion.place_ref, ...), custom_call_target="tpu_custom_call" | custom-call | tf_op jit(solution)/shard_map/place_gradients/pallas_call | solution.py:238
  25.3 0.5 collective-permute-start
  25.8 2.6 %collective-permute-done = f32[2192,128]{1,0:T(8,128)S(1)} collective-permute-done((f32[2192,128]{1,0:T(8,128)}, f32[2192,128]{1,0:T(8,128)S(1)}, u32[]{:S(2)}, u32[]{:S(2)}) %collective-permute-start) | collective-permute-done | bytes 1122336 | tf_op jit(solution)/shard_map/ppermute | solution.py:72
  28.4 1.1 slice_add_fusion.7
  29.5 0.4 collective-permute-start.5
  30.0 2.6 %collective-permute-start.3 = (f32[1096,128]{1,0:T(8,128)S(1)}, f32[1096,128]{1,0:T(8,128)S(1)}, u32[]{:S(2)}, u32[]{:S(2)}) collective-permute-start(f32[1096,128]{1,0:T(8,128)S(1)} %slice_add_fusion.7), channel_id=1, source_target_pairs={{0,4},{2,6},{4,0},{6,2},{8,12},{10,14},{12,8},{14,10},{16,20},{18,... | collective-permute-start | bytes 1683464 | tf_op jit(solution)/shard_map/ppermute | solution.py:72
  32.6 0.1 collective-permute-start.9
  32.7 13.2 %collective-permute-done.3 = f32[1096,128]{1,0:T(8,128)S(1)} collective-permute-done((f32[1096,128]{1,0:T(8,128)S(1)}, f32[1096,128]{1,0:T(8,128)S(1)}, u32[]{:S(2)}, u32[]{:S(2)}) %collective-permute-start.3) | collective-permute-done | bytes 561184 | tf_op jit(solution)/shard_map/ppermute | solution.py:72
  45.8 0.1 fusion
  45.9 3.8 %collective-permute-start.4 = (f32[1096,128]{1,0:T(8,128)S(1)}, f32[1096,128]{1,0:T(8,128)S(1)}, u32[]{:S(2)}, u32[]{:S(2)}) collective-permute-start(f32[1096,128]{1,0:T(8,128)S(1)} %fusion), channel_id=1, source_target_pairs={{0,8},{2,10},{4,12},{6,14},{24,16},{26,18},{28,20},{30,22},{1,9},{... | collective-permute-start | bytes 1683464 | tf_op jit(solution)/shard_map/ppermute | solution.py:72
  49.7 0.0 collective-permute-done.5
  49.7 0.1 slice_add_fusion.2
  49.9 1.6 collective-permute-start.6
  51.5 6.3 %owned_weights.1 = (f32[1088,128]{1,0:T(8,128)}, s32[1152,128]{1,0:T(8,128)}) custom-call(s32[3]{0:T(128)} %pad_add_fusion.place_ref, s32[136,128]{1,0:T(8,128)} %bitcast.14, f32[17408,128]{1,0:T(8,128)} %weights_ref.3), custom_call_target="tpu_custom_call" | custom-call | bytes 20971520 | tf_op jit(solution)/shard_map/owned_weights/pallas_call | solution.py:316
  57.8 0.1 collective-permute-start.1
  57.9 0.1 slice_add_fusion
  58.0 0.7 collective-permute-start.10
  58.7 2.7 %collective-permute-done.4 = f32[1096,128]{1,0:T(8,128)S(1)} collective-permute-done((f32[1096,128]{1,0:T(8,128)S(1)}, f32[1096,128]{1,0:T(8,128)S(1)}, u32[]{:S(2)}, u32[]{:S(2)}) %collective-permute-start.4) | collective-permute-done | bytes 561184 | tf_op jit(solution)/shard_map/ppermute | solution.py:72
  61.4 4.3 %collective-permute-done.6 = f32[1096,128]{1,0:T(8,128)S(1)} collective-permute-done((f32[1096,128]{1,0:T(8,128)S(1)}, f32[1096,128]{1,0:T(8,128)S(1)}, u32[]{:S(2)}, u32[]{:S(2)}) %collective-permute-start.6) | collective-permute-done | bytes 561184 | tf_op jit(solution)/shard_map/ppermute | solution.py:72
  65.6 0.1 fusion.1
  65.7 0.8 collective-permute-start.7
  66.6 4.1 %collective-permute-start.8 = (f32[1096,128]{1,0:T(8,128)S(1)}, f32[1096,128]{1,0:T(8,128)S(1)}, u32[]{:S(2)}, u32[]{:S(2)}) collective-permute-start(f32[1096,128]{1,0:T(8,128)S(1)} %get-tuple-element.90), channel_id=1, source_target_pairs={{0,8},{2,10},{4,12},{6,14},{24,16},{26,18},{28,20},{30,22},{1,9},{... | collective-permute-start | bytes 1683464 | tf_op jit(solution)/shard_map/ppermute | solution.py:72
  70.6 0.1 slice_add_fusion.5
  70.8 1.6 collective-permute-start.2
  72.3 5.3 %collective-permute-done.10 = f32[1096,128]{1,0:T(8,128)S(1)} collective-permute-done((f32[1096,128]{1,0:T(8,128)S(1)}, f32[1096,128]{1,0:T(8,128)S(1)}, u32[]{:S(2)}, u32[]{:S(2)}) %collective-permute-start.10) | collective-permute-done | bytes 561184 | tf_op jit(solution)/shard_map/ppermute | solution.py:72
  77.6 3.0 %collective-permute-done.8 = f32[1096,128]{1,0:T(8,128)S(1)} collective-permute-done((f32[1096,128]{1,0:T(8,128)S(1)}, f32[1096,128]{1,0:T(8,128)S(1)}, u32[]{:S(2)}, u32[]{:S(2)}) %collective-permute-start.8) | collective-permute-done | bytes 561184 | tf_op jit(solution)/shard_map/ppermute | solution.py:72
  80.7 0.1 add_add_fusion
  80.8 0.0 copy-start
  80.8 0.0 copy-start.2
  80.8 0.1 add.78
  80.9 2.5 %collective-permute-start.11 = (f32[1096,128]{1,0:T(8,128)S(1)}, f32[1096,128]{1,0:T(8,128)S(1)}, u32[]{:S(2)}, u32[]{:S(2)}) collective-permute-start(f32[1096,128]{1,0:T(8,128)S(1)} %add_add_fusion), channel_id=1, source_target_pairs={{0,8},{2,10},{4,12},{6,14},{8,0},{10,2},{12,4},{14,6},{16,24},{18,... | collective-permute-start | bytes 1683464 | tf_op jit(solution)/shard_map/ppermute | solution.py:72
  83.5 0.7 collective-permute-start.12
  84.1 3.8 %collective-permute-done.2.refs_1_ = f32[1096,128]{1,0:T(8,128)S(1)} collective-permute-done((f32[1096,128]{1,0:T(8,128)S(1)}, f32[1096,128]{1,0:T(8,128)S(1)}, u32[]{:S(2)}, u32[]{:S(2)}) %collective-permute-start.2) | collective-permute-done | bytes 561184 | tf_op jit(solution)/shard_map/ppermute | solution.py:72
  87.9 4.1 %collective-permute-done.11.refs_2_ = f32[1096,128]{1,0:T(8,128)S(1)} collective-permute-done((f32[1096,128]{1,0:T(8,128)S(1)}, f32[1096,128]{1,0:T(8,128)S(1)}, u32[]{:S(2)}, u32[]{:S(2)}) %collective-permute-start.11) | collective-permute-done | bytes 561184 | tf_op jit(solution)/shard_map/ppermute | solution.py:72
  92.0 2.6 %moments.1 = (f32[1088,128]{1,0:T(8,128)}, f32[1088,128]{1,0:T(8,128)}, f32[1096,128]{1,0:T(8,128)S(1)}, f32[8,128]{1,0:T(8,128)S(1)}) custom-call(f32[1096,128]{1,0:T(8,128)S(1)} %get-tuple-element.96.refs_0_, f32[1096,128]{1,0:T(8,128)S(1)} %collective-permute-done.2.refs_1_, f32[1096,128]{1,0:T(8,128)S(1)} %collective-permute-done.11.refs_2_, ...), custom_call_target="tpu_custom_call" | custom-call | tf_op jit(solution)/shard_map/moments/pallas_call | solution.py:371
  94.6 1.5 collective-permute-start.13
  96.2 2.1 %collective-permute-done.13 = f32[8,128]{1,0:T(8,128)S(1)} collective-permute-done((f32[8,128]{1,0:T(8,128)S(1)}, f32[8,128]{1,0:T(8,128)S(1)}, u32[]{:S(2)}, u32[]{:S(2)}) %collective-permute-start.13) | collective-permute-done | bytes 4128 | tf_op jit(solution)/shard_map/ppermute | solution.py:512
  98.3 1.5 collective-permute-start.16
  99.7 0.7 collective-permute-start.15
  100.4 5.4 %collective-permute-start.14 = (f32[1096,128]{1,0:T(8,128)S(1)}, f32[1096,128]{1,0:T(8,128)S(1)}, u32[]{:S(2)}, u32[]{:S(2)}) collective-permute-start(f32[1096,128]{1,0:T(8,128)S(1)} %add_dynamic-update-slice_fusion.refs_0_), channel_id=1, source_target_pairs={{0,8},{2,10},{4,12},{6,14},{8,0},{10,2},{12,4},{14,6},{16,24},{18,... | collective-permute-start | bytes 1683464 | tf_op jit(solution)/shard_map/ppermute | solution.py:72
  105.9 2.0 %collective-permute-done.16.refs_1_ = f32[1096,128]{1,0:T(8,128)S(1)} collective-permute-done((f32[1096,128]{1,0:T(8,128)S(1)}, f32[1096,128]{1,0:T(8,128)S(1)}, u32[]{:S(2)}, u32[]{:S(2)}) %collective-permute-start.16) | collective-permute-done | bytes 561184 | tf_op jit(solution)/shard_map/ppermute | solution.py:72
  107.8 8.4 %collective-permute-done.14.refs_4_ = f32[1096,128]{1,0:T(8,128)S(1)} collective-permute-done((f32[1096,128]{1,0:T(8,128)S(1)}, f32[1096,128]{1,0:T(8,128)S(1)}, u32[]{:S(2)}, u32[]{:S(2)}) %collective-permute-start.14) | collective-permute-done | bytes 561184 | tf_op jit(solution)/shard_map/ppermute | solution.py:72
  116.2 1.3 collective-permute-start.20
  117.5 0.6 collective-permute-start.21
  118.1 0.7 collective-permute-start.19
  118.8 12.3 %collective-permute-done.20 = f32[1096,128]{1,0:T(8,128)S(1)} collective-permute-done((f32[1096,128]{1,0:T(8,128)S(1)}, f32[1096,128]{1,0:T(8,128)S(1)}, u32[]{:S(2)}, u32[]{:S(2)}) %collective-permute-start.20) | collective-permute-done | bytes 561184 | tf_op jit(solution)/shard_map/ppermute | solution.py:72
  131.1 1.2 collective-permute-done.21.refs_5_
  132.3 0.1 add.81.refs_8_
  132.3 0.6 collective-permute-start.25
  132.9 1.3 collective-permute-start.24
  134.2 0.1 collective-permute-start.17
  134.3 0.5 collective-permute-start.18
  134.8 0.1 collective-permute-start.22
  134.9 10.9 %collective-permute-done.25.refs_9_ = f32[1096,128]{1,0:T(8,128)S(1)} collective-permute-done((f32[1096,128]{1,0:T(8,128)S(1)}, f32[1096,128]{1,0:T(8,128)S(1)}, u32[]{:S(2)}, u32[]{:S(2)}) %collective-permute-start.25) | collective-permute-done | bytes 561184 | tf_op jit(solution)/shard_map/ppermute | solution.py:72
  145.8 0.1 add.82.refs_10_
  145.9 0.8 collective-permute-start.26
  146.7 0.5 collective-permute-start.29
  147.2 0.1 collective-permute-start.27
  147.3 0.4 collective-permute-start.28
  147.7 7.8 %collective-permute-done.26.refs_11_ = f32[1096,128]{1,0:T(8,128)S(1)} collective-permute-done((f32[1096,128]{1,0:T(8,128)S(1)}, f32[1096,128]{1,0:T(8,128)S(1)}, u32[]{:S(2)}, u32[]{:S(2)}) %collective-permute-start.26) | collective-permute-done | bytes 561184 | tf_op jit(solution)/shard_map/ppermute | solution.py:72
  155.6 1.9 %collective-permute-done.30.refs_15_ = f32[1096,128]{1,0:T(8,128)S(1)} collective-permute-done((f32[1096,128]{1,0:T(8,128)S(1)}, f32[1096,128]{1,0:T(8,128)S(1)}, u32[]{:S(2)}, u32[]{:S(2)}) %collective-permute-start.30) | collective-permute-done | bytes 561184 | tf_op jit(solution)/shard_map/ppermute | solution.py:72
  157.5 0.8 copy-done.23
  158.4 25.1 %new_weights.1 = (f32[17408,128]{1,0:T(8,128)}, f32[3,2,1024]{2,1,0:T(2,128)}, f32[7]{0:T(128)}) custom-call(s32[3]{0:T(128)} %pad_add_fusion.place_ref, s32[136,128]{1,0:T(8,128)} %get-tuple-element.47.position_ref, f32[3,2,1024]{2,1,0:T(2,128)} %norm_ref.1, f32[17408,128]{1,0:T(8,128)} %weights_ref.3, f32[1096,128]{1,0:T(8,128)} %copy-done.1, ...), custom_call_target="tpu_custom_call" | custom-call | tf_op jit(solution)/shard_map/new_weights/pallas_call | solution.py:456
  (64 shorter events, 0.1 us)
Async XLA Ops:
  25.3 20.6 %copy-start.10 = (f32[2192,128]{1,0:T(8,128)S(1)}, f32[2192,128]{1,0:T(8,128)}, u32[]{:S(2)}) copy-start(f32[2192,128]{1,0:T(8,128)} %get-tuple-element.49) | copy-start | bytes 3366916
  25.3 3.1 %collective-permute-start = (f32[2192,128]{1,0:T(8,128)}, f32[2192,128]{1,0:T(8,128)S(1)}, u32[]{:S(2)}, u32[]{:S(2)}) collective-permute-start(f32[2192,128]{1,0:T(8,128)} %get-tuple-element.50), channel_id=1, source_target_pairs={{0,2},{2,0},{4,6},{6,4},{8,10},{10,8},{12,14},{14,12},{16,18},{18,... | collective-permute-start | bytes 3366920 | tf_op jit(solution)/shard_map/ppermute | solution.py:72
  29.5 20.2 %copy-start.9 = (f32[2192,128]{1,0:T(8,128)S(1)}, f32[2192,128]{1,0:T(8,128)}, u32[]{:S(2)}) copy-start(f32[2192,128]{1,0:T(8,128)} %get-tuple-element.56) | copy-start | bytes 3366916
  29.5 20.2 %collective-permute-start.5 = (f32[2192,128]{1,0:T(8,128)}, f32[2192,128]{1,0:T(8,128)S(1)}, u32[]{:S(2)}, u32[]{:S(2)}) collective-permute-start(f32[2192,128]{1,0:T(8,128)} %get-tuple-element.57), channel_id=1, source_target_pairs={{0,2},{2,0},{4,6},{6,4},{8,10},{10,8},{12,14},{14,12},{16,18},{18,... | collective-permute-start | bytes 3366920 | tf_op jit(solution)/shard_map/ppermute | solution.py:72
  30.0 15.9 %collective-permute-start.3 = (f32[1096,128]{1,0:T(8,128)S(1)}, f32[1096,128]{1,0:T(8,128)S(1)}, u32[]{:S(2)}, u32[]{:S(2)}) collective-permute-start(f32[1096,128]{1,0:T(8,128)S(1)} %slice_add_fusion.7), channel_id=1, source_target_pairs={{0,4},{2,6},{4,0},{6,2},{8,12},{10,14},{12,8},{14,10},{16,20},{18,... | collective-permute-start | bytes 1683464 | tf_op jit(solution)/shard_map/ppermute | solution.py:72
  32.6 25.3 %collective-permute-start.9 = (f32[2192,128]{1,0:T(8,128)}, f32[2192,128]{1,0:T(8,128)S(1)}, u32[]{:S(2)}, u32[]{:S(2)}) collective-permute-start(f32[2192,128]{1,0:T(8,128)} %get-tuple-element.64), channel_id=1, source_target_pairs={{0,2},{2,0},{4,6},{6,4},{8,10},{10,8},{12,14},{14,12},{16,18},{18,... | collective-permute-start | bytes 3366920 | tf_op jit(solution)/shard_map/ppermute | solution.py:72
  45.9 15.4 %collective-permute-start.4 = (f32[1096,128]{1,0:T(8,128)S(1)}, f32[1096,128]{1,0:T(8,128)S(1)}, u32[]{:S(2)}, u32[]{:S(2)}) collective-permute-start(f32[1096,128]{1,0:T(8,128)S(1)} %fusion), channel_id=1, source_target_pairs={{0,8},{2,10},{4,12},{6,14},{24,16},{26,18},{28,20},{30,22},{1,9},{... | collective-permute-start | bytes 1683464 | tf_op jit(solution)/shard_map/ppermute | solution.py:72
  49.9 7.9 %copy-start.24 = (f32[2192,128]{1,0:T(8,128)S(1)}, f32[2192,128]{1,0:T(8,128)}, u32[]{:S(2)}) copy-start(f32[2192,128]{1,0:T(8,128)} %get-tuple-element.54) | copy-start | bytes 3366916
  49.9 8.0 %copy-start.8 = (f32[2192,128]{1,0:T(8,128)S(1)}, f32[2192,128]{1,0:T(8,128)}, u32[]{:S(2)}) copy-start(f32[2192,128]{1,0:T(8,128)} %get-tuple-element.63) | copy-start | bytes 3366916
  49.9 15.7 %collective-permute-start.6 = (f32[1096,128]{1,0:T(8,128)S(1)}, f32[1096,128]{1,0:T(8,128)S(1)}, u32[]{:S(2)}, u32[]{:S(2)}) collective-permute-start(f32[1096,128]{1,0:T(8,128)S(1)} %get-tuple-element.93), channel_id=1, source_target_pairs={{0,4},{2,6},{4,0},{6,2},{8,12},{10,14},{12,8},{14,10},{16,20},{18,... | collective-permute-start | bytes 1683464 | tf_op jit(solution)/shard_map/ppermute | solution.py:72
  57.8 12.8 %collective-permute-start.1 = (f32[2192,128]{1,0:T(8,128)S(1)}, f32[2192,128]{1,0:T(8,128)S(1)}, u32[]{:S(2)}, u32[]{:S(2)}) collective-permute-start(f32[2192,128]{1,0:T(8,128)S(1)} %copy-done.24), channel_id=1, source_target_pairs={{0,2},{2,0},{4,6},{6,4},{8,10},{10,8},{12,14},{14,12},{16,18},{18,... | collective-permute-start | bytes 3366920 | tf_op jit(solution)/shard_map/ppermute | solution.py:72
  58.0 19.6 %collective-permute-start.10 = (f32[1096,128]{1,0:T(8,128)S(1)}, f32[1096,128]{1,0:T(8,128)S(1)}, u32[]{:S(2)}, u32[]{:S(2)}) collective-permute-start(f32[1096,128]{1,0:T(8,128)S(1)} %get-tuple-element.91), channel_id=1, source_target_pairs={{0,4},{2,6},{4,0},{6,2},{8,12},{10,14},{12,8},{14,10},{16,20},{18,... | collective-permute-start | bytes 1683464 | tf_op jit(solution)/shard_map/ppermute | solution.py:72
  65.6 5.0 %copy-start.7 = (f32[2192,128]{1,0:T(8,128)S(1)}, f32[2192,128]{1,0:T(8,128)}, u32[]{:S(2)}) copy-start(f32[2192,128]{1,0:T(8,128)} %get-tuple-element.48) | copy-start | bytes 3366916
  65.7 11.9 %collective-permute-start.7 = (f32[1096,128]{1,0:T(8,128)S(1)}, f32[1096,128]{1,0:T(8,128)S(1)}, u32[]{:S(2)}, u32[]{:S(2)}) collective-permute-start(f32[1096,128]{1,0:T(8,128)S(1)} %get-tuple-element.89), channel_id=1, source_target_pairs={{8,16},{10,18},{12,20},{14,22},{16,8},{18,10},{20,12},{22,14},{9,1... | collective-permute-start | bytes 1683464 | tf_op jit(solution)/shard_map/ppermute | solution.py:72
  66.6 14.1 %collective-permute-start.8 = (f32[1096,128]{1,0:T(8,128)S(1)}, f32[1096,128]{1,0:T(8,128)S(1)}, u32[]{:S(2)}, u32[]{:S(2)}) collective-permute-start(f32[1096,128]{1,0:T(8,128)S(1)} %get-tuple-element.90), channel_id=1, source_target_pairs={{0,8},{2,10},{4,12},{6,14},{24,16},{26,18},{28,20},{30,22},{1,9},{... | collective-permute-start | bytes 1683464 | tf_op jit(solution)/shard_map/ppermute | solution.py:72
  70.8 17.1 %collective-permute-start.2 = (f32[1096,128]{1,0:T(8,128)S(1)}, f32[1096,128]{1,0:T(8,128)S(1)}, u32[]{:S(2)}, u32[]{:S(2)}) collective-permute-start(f32[1096,128]{1,0:T(8,128)S(1)} %get-tuple-element.95), channel_id=1, source_target_pairs={{0,4},{2,6},{4,0},{6,2},{8,12},{10,14},{12,8},{14,10},{16,20},{18,... | collective-permute-start | bytes 1683464 | tf_op jit(solution)/shard_map/ppermute | solution.py:72
  80.7 11.3 %copy-start.3 = (f32[1,1088,128]{2,1,0:T(8,128)S(1)}, f32[1,1088,128]{2,1,0:T(8,128)}, u32[]{:S(2)}) copy-start(f32[1,1088,128]{2,1,0:T(8,128)} %param.10) | copy-start | bytes 1671172
  80.7 11.3 %copy-start.4 = (f32[1088,128]{1,0:T(8,128)S(1)}, f32[1088,128]{1,0:T(8,128)}, u32[]{:S(2)}) copy-start(f32[1088,128]{1,0:T(8,128)} %get-tuple-element.69.refs_6_) | copy-start | bytes 1671172
  80.8 11.2 %copy-start = (s32[1152,128]{1,0:T(8,128)S(1)}, s32[1152,128]{1,0:T(8,128)}, u32[]{:S(2)}) copy-start(s32[1152,128]{1,0:T(8,128)} %get-tuple-element.70.refs_7_) | copy-start | bytes 1769476
  80.8 11.2 %copy-start.2 = (f32[1,1088,128]{2,1,0:T(8,128)S(1)}, f32[1,1088,128]{2,1,0:T(8,128)}, u32[]{:S(2)}) copy-start(f32[1,1088,128]{2,1,0:T(8,128)} %param.9) | copy-start | bytes 1671172
  80.9 11.1 %collective-permute-start.11 = (f32[1096,128]{1,0:T(8,128)S(1)}, f32[1096,128]{1,0:T(8,128)S(1)}, u32[]{:S(2)}, u32[]{:S(2)}) collective-permute-start(f32[1096,128]{1,0:T(8,128)S(1)} %add_add_fusion), channel_id=1, source_target_pairs={{0,8},{2,10},{4,12},{6,14},{8,0},{10,2},{12,4},{14,6},{16,24},{18,... | collective-permute-start | bytes 1683464 | tf_op jit(solution)/shard_map/ppermute | solution.py:72
  83.5 8.5 %collective-permute-start.12 = (f32[1096,128]{1,0:T(8,128)S(1)}, f32[1096,128]{1,0:T(8,128)S(1)}, u32[]{:S(2)}, u32[]{:S(2)}) collective-permute-start(f32[1096,128]{1,0:T(8,128)S(1)} %add.78), channel_id=1, source_target_pairs={{8,16},{10,18},{12,20},{14,22},{16,8},{18,10},{20,12},{22,14},{9,1... | collective-permute-start | bytes 1683464 | tf_op jit(solution)/shard_map/ppermute | solution.py:72
  94.6 3.6 %collective-permute-start.13 = (f32[8,128]{1,0:T(8,128)S(1)}, f32[8,128]{1,0:T(8,128)S(1)}, u32[]{:S(2)}, u32[]{:S(2)}) collective-permute-start(f32[8,128]{1,0:T(8,128)S(1)} %get-tuple-element.72), channel_id=1, source_target_pairs={{0,1},{1,0},{2,3},{3,2},{4,5},{5,4},{6,7},{7,6},{8,9},{9,8},{10,11... | collective-permute-start | bytes 12296 | tf_op jit(solution)/shard_map/ppermute | solution.py:512
  98.3 47.6 %copy-start.1 = (f32[1096,128]{1,0:T(8,128)}, f32[1096,128]{1,0:T(8,128)S(1)}, u32[]{:S(2)}) copy-start(f32[1096,128]{1,0:T(8,128)S(1)} %add_dynamic-update-slice_fusion.refs_0_) | copy-start | bytes 1683460
  98.3 9.6 %collective-permute-start.16 = (f32[1096,128]{1,0:T(8,128)S(1)}, f32[1096,128]{1,0:T(8,128)S(1)}, u32[]{:S(2)}, u32[]{:S(2)}) collective-permute-start(f32[1096,128]{1,0:T(8,128)S(1)} %add_dynamic-update-slice_fusion.refs_0_), channel_id=1, source_target_pairs={{0,4},{2,6},{4,0},{6,2},{8,12},{10,14},{12,8},{14,10},{16,20},{18,... | collective-permute-start | bytes 1683464 | tf_op jit(solution)/shard_map/ppermute | solution.py:72
  99.7 8.1 %collective-permute-start.15 = (f32[1096,128]{1,0:T(8,128)S(1)}, f32[1096,128]{1,0:T(8,128)S(1)}, u32[]{:S(2)}, u32[]{:S(2)}) collective-permute-start(f32[1096,128]{1,0:T(8,128)S(1)} %add_dynamic-update-slice_fusion.refs_0_), channel_id=1, source_target_pairs={{8,16},{10,18},{12,20},{14,22},{16,8},{18,10},{20,12},{22,14},{9,1... | collective-permute-start | bytes 1683464 | tf_op jit(solution)/shard_map/ppermute | solution.py:72
  100.4 15.8 %collective-permute-start.14 = (f32[1096,128]{1,0:T(8,128)S(1)}, f32[1096,128]{1,0:T(8,128)S(1)}, u32[]{:S(2)}, u32[]{:S(2)}) collective-permute-start(f32[1096,128]{1,0:T(8,128)S(1)} %add_dynamic-update-slice_fusion.refs_0_), channel_id=1, source_target_pairs={{0,8},{2,10},{4,12},{6,14},{8,0},{10,2},{12,4},{14,6},{16,24},{18,... | collective-permute-start | bytes 1683464 | tf_op jit(solution)/shard_map/ppermute | solution.py:72
  107.8 38.1 %copy-start.11 = (f32[1096,128]{1,0:T(8,128)}, f32[1096,128]{1,0:T(8,128)S(1)}, u32[]{:S(2)}) copy-start(f32[1096,128]{1,0:T(8,128)S(1)} %collective-permute-done.16.refs_1_) | copy-start | bytes 1683460
  116.2 29.7 %copy-start.12 = (f32[1096,128]{1,0:T(8,128)}, f32[1096,128]{1,0:T(8,128)S(1)}, u32[]{:S(2)}) copy-start(f32[1096,128]{1,0:T(8,128)S(1)} %collective-permute-done.14.refs_4_) | copy-start | bytes 1683460
  116.2 14.9 %collective-permute-start.20 = (f32[1096,128]{1,0:T(8,128)S(1)}, f32[1096,128]{1,0:T(8,128)S(1)}, u32[]{:S(2)}, u32[]{:S(2)}) collective-permute-start(f32[1096,128]{1,0:T(8,128)S(1)} %collective-permute-done.15), channel_id=1, source_target_pairs={{8,0},{10,2},{12,4},{14,6},{16,24},{18,26},{20,28},{22,30},{9,1},{... | collective-permute-start | bytes 1683464 | tf_op jit(solution)/shard_map/ppermute | solution.py:72
  117.5 14.8 %collective-permute-start.21 = (f32[1096,128]{1,0:T(8,128)S(1)}, f32[1096,128]{1,0:T(8,128)S(1)}, u32[]{:S(2)}, u32[]{:S(2)}) collective-permute-start(f32[1096,128]{1,0:T(8,128)S(1)} %collective-permute-done.14.refs_4_), channel_id=1, source_target_pairs={{0,4},{2,6},{4,0},{6,2},{8,12},{10,14},{12,8},{14,10},{16,20},{18,... | collective-permute-start | bytes 1683464 | tf_op jit(solution)/shard_map/ppermute | solution.py:72
  118.1 14.2 %collective-permute-start.19 = (f32[1096,128]{1,0:T(8,128)S(1)}, f32[1096,128]{1,0:T(8,128)S(1)}, u32[]{:S(2)}, u32[]{:S(2)}) collective-permute-start(f32[1096,128]{1,0:T(8,128)S(1)} %collective-permute-done.14.refs_4_), channel_id=1, source_target_pairs={{8,16},{10,18},{12,20},{14,22},{16,8},{18,10},{20,12},{22,14},{9,1... | collective-permute-start | bytes 1683464 | tf_op jit(solution)/shard_map/ppermute | solution.py:72
  132.3 14.4 %copy-start.13 = (f32[1096,128]{1,0:T(8,128)}, f32[1096,128]{1,0:T(8,128)S(1)}, u32[]{:S(2)}) copy-start(f32[1096,128]{1,0:T(8,128)S(1)} %collective-permute-done.21.refs_5_) | copy-start | bytes 1683460
  132.3 26.0 %copy-start.5 = (f32[1096,128]{1,0:T(8,128)}, f32[1096,128]{1,0:T(8,128)S(1)}, u32[]{:S(2)}) copy-start(f32[1096,128]{1,0:T(8,128)S(1)} %add.81.refs_8_) | copy-start | bytes 1683460
  132.3 13.4 %collective-permute-start.25 = (f32[1096,128]{1,0:T(8,128)S(1)}, f32[1096,128]{1,0:T(8,128)S(1)}, u32[]{:S(2)}, u32[]{:S(2)}) collective-permute-start(f32[1096,128]{1,0:T(8,128)S(1)} %add.81.refs_8_), channel_id=1, source_target_pairs={{0,4},{2,6},{4,0},{6,2},{8,12},{10,14},{12,8},{14,10},{16,20},{18,... | collective-permute-start | bytes 1683464 | tf_op jit(solution)/shard_map/ppermute | solution.py:72
  132.9 12.8 %collective-permute-start.24 = (f32[1096,128]{1,0:T(8,128)S(1)}, f32[1096,128]{1,0:T(8,128)S(1)}, u32[]{:S(2)}, u32[]{:S(2)}) collective-permute-start(f32[1096,128]{1,0:T(8,128)S(1)} %collective-permute-done.19), channel_id=1, source_target_pairs={{8,0},{10,2},{12,4},{14,6},{16,24},{18,26},{20,28},{22,30},{9,1},{... | collective-permute-start | bytes 1683464 | tf_op jit(solution)/shard_map/ppermute | solution.py:72
  134.2 12.5 %collective-permute-start.17 = (f32[1096,128]{1,0:T(8,128)S(1)}, f32[1096,128]{1,0:T(8,128)S(1)}, u32[]{:S(2)}, u32[]{:S(2)}) collective-permute-start(f32[1096,128]{1,0:T(8,128)S(1)} %add_dynamic-update-slice_fusion.refs_0_), channel_id=1, source_target_pairs={{0,2},{2,0},{4,6},{6,4},{8,10},{10,8},{12,14},{14,12},{16,18},{18,... | collective-permute-start | bytes 1683464 | tf_op jit(solution)/shard_map/ppermute | solution.py:72
  134.3 12.9 %collective-permute-start.18 = (f32[1096,128]{1,0:T(8,128)S(1)}, f32[1096,128]{1,0:T(8,128)S(1)}, u32[]{:S(2)}, u32[]{:S(2)}) collective-permute-start(f32[1096,128]{1,0:T(8,128)S(1)} %collective-permute-done.16.refs_1_), channel_id=1, source_target_pairs={{0,2},{2,0},{4,6},{6,4},{8,10},{10,8},{12,14},{14,12},{16,18},{18,... | collective-permute-start | bytes 1683464 | tf_op jit(solution)/shard_map/ppermute | solution.py:72
  134.8 12.5 %collective-permute-start.22 = (f32[1096,128]{1,0:T(8,128)S(1)}, f32[1096,128]{1,0:T(8,128)S(1)}, u32[]{:S(2)}, u32[]{:S(2)}) collective-permute-start(f32[1096,128]{1,0:T(8,128)S(1)} %collective-permute-done.14.refs_4_), channel_id=1, source_target_pairs={{0,2},{2,0},{4,6},{6,4},{8,10},{10,8},{12,14},{14,12},{16,18},{18,... | collective-permute-start | bytes 1683464 | tf_op jit(solution)/shard_map/ppermute | solution.py:72
  145.8 12.6 %copy-start.14 = (f32[1096,128]{1,0:T(8,128)}, f32[1096,128]{1,0:T(8,128)S(1)}, u32[]{:S(2)}) copy-start(f32[1096,128]{1,0:T(8,128)S(1)} %collective-permute-done.25.refs_9_) | copy-start | bytes 1683460
  145.9 12.4 %copy-start.6 = (f32[1096,128]{1,0:T(8,128)}, f32[1096,128]{1,0:T(8,128)S(1)}, u32[]{:S(2)}) copy-start(f32[1096,128]{1,0:T(8,128)S(1)} %add.82.refs_10_) | copy-start | bytes 1683460
  145.9 9.6 %collective-permute-start.26 = (f32[1096,128]{1,0:T(8,128)S(1)}, f32[1096,128]{1,0:T(8,128)S(1)}, u32[]{:S(2)}, u32[]{:S(2)}) collective-permute-start(f32[1096,128]{1,0:T(8,128)S(1)} %add.82.refs_10_), channel_id=1, source_target_pairs={{0,4},{2,6},{4,0},{6,2},{8,12},{10,14},{12,8},{14,10},{16,20},{18,... | collective-permute-start | bytes 1683464 | tf_op jit(solution)/shard_map/ppermute | solution.py:72
  146.7 8.9 %collective-permute-start.23 = (f32[1096,128]{1,0:T(8,128)S(1)}, f32[1096,128]{1,0:T(8,128)S(1)}, u32[]{:S(2)}, u32[]{:S(2)}) collective-permute-start(f32[1096,128]{1,0:T(8,128)S(1)} %collective-permute-done.21.refs_5_), channel_id=1, source_target_pairs={{0,2},{2,0},{4,6},{6,4},{8,10},{10,8},{12,14},{14,12},{16,18},{18,... | collective-permute-start | bytes 1683464 | tf_op jit(solution)/shard_map/ppermute | solution.py:72
  146.7 11.6 %copy-start.15 = (f32[1096,128]{1,0:T(8,128)}, f32[1096,128]{1,0:T(8,128)S(1)}, u32[]{:S(2)}) copy-start(f32[1096,128]{1,0:T(8,128)S(1)} %collective-permute-done.17.refs_2_) | copy-start | bytes 1683460
  146.7 8.9 %collective-permute-start.29 = (f32[1096,128]{1,0:T(8,128)S(1)}, f32[1096,128]{1,0:T(8,128)S(1)}, u32[]{:S(2)}, u32[]{:S(2)}) collective-permute-start(f32[1096,128]{1,0:T(8,128)S(1)} %add.82.refs_10_), channel_id=1, source_target_pairs={{0,2},{2,0},{4,6},{6,4},{8,10},{10,8},{12,14},{14,12},{16,18},{18,... | collective-permute-start | bytes 1683464 | tf_op jit(solution)/shard_map/ppermute | solution.py:72
  147.2 11.1 %copy-start.16 = (f32[1096,128]{1,0:T(8,128)}, f32[1096,128]{1,0:T(8,128)S(1)}, u32[]{:S(2)}) copy-start(f32[1096,128]{1,0:T(8,128)S(1)} %collective-permute-done.18.refs_3_) | copy-start | bytes 1683460
  147.2 8.4 %collective-permute-start.27 = (f32[1096,128]{1,0:T(8,128)S(1)}, f32[1096,128]{1,0:T(8,128)S(1)}, u32[]{:S(2)}, u32[]{:S(2)}) collective-permute-start(f32[1096,128]{1,0:T(8,128)S(1)} %add.81.refs_8_), channel_id=1, source_target_pairs={{0,2},{2,0},{4,6},{6,4},{8,10},{10,8},{12,14},{14,12},{16,18},{18,... | collective-permute-start | bytes 1683464 | tf_op jit(solution)/shard_map/ppermute | solution.py:72
  147.3 11.1 %copy-start.17 = (f32[1096,128]{1,0:T(8,128)}, f32[1096,128]{1,0:T(8,128)S(1)}, u32[]{:S(2)}) copy-start(f32[1096,128]{1,0:T(8,128)S(1)} %collective-permute-done.22.refs_6_) | copy-start | bytes 1683460
  147.3 8.3 %collective-permute-start.28 = (f32[1096,128]{1,0:T(8,128)S(1)}, f32[1096,128]{1,0:T(8,128)S(1)}, u32[]{:S(2)}, u32[]{:S(2)}) collective-permute-start(f32[1096,128]{1,0:T(8,128)S(1)} %collective-permute-done.25.refs_9_), channel_id=1, source_target_pairs={{0,2},{2,0},{4,6},{6,4},{8,10},{10,8},{12,14},{14,12},{16,18},{18,... | collective-permute-start | bytes 1683464 | tf_op jit(solution)/shard_map/ppermute | solution.py:72
  155.6 2.8 %copy-start.18 = (f32[1096,128]{1,0:T(8,128)}, f32[1096,128]{1,0:T(8,128)S(1)}, u32[]{:S(2)}) copy-start(f32[1096,128]{1,0:T(8,128)S(1)} %collective-permute-done.26.refs_11_) | copy-start | bytes 1683460
  155.6 2.0 %collective-permute-start.30 = (f32[1096,128]{1,0:T(8,128)S(1)}, f32[1096,128]{1,0:T(8,128)S(1)}, u32[]{:S(2)}, u32[]{:S(2)}) collective-permute-start(f32[1096,128]{1,0:T(8,128)S(1)} %collective-permute-done.26.refs_11_), channel_id=1, source_target_pairs={{0,2},{2,0},{4,6},{6,4},{8,10},{10,8},{12,14},{14,12},{16,18},{18,... | collective-permute-start | bytes 1683464 | tf_op jit(solution)/shard_map/ppermute | solution.py:72
  155.6 2.0 %copy-start.19 = (f32[1096,128]{1,0:T(8,128)}, f32[1096,128]{1,0:T(8,128)S(1)}, u32[]{:S(2)}) copy-start(f32[1096,128]{1,0:T(8,128)S(1)} %collective-permute-done.23.refs_7_) | copy-start | bytes 1683460
  155.6 2.8 %copy-start.20 = (f32[1096,128]{1,0:T(8,128)}, f32[1096,128]{1,0:T(8,128)S(1)}, u32[]{:S(2)}) copy-start(f32[1096,128]{1,0:T(8,128)S(1)} %collective-permute-done.29.refs_14_) | copy-start | bytes 1683460
  155.6 2.8 %copy-start.21 = (f32[1096,128]{1,0:T(8,128)}, f32[1096,128]{1,0:T(8,128)S(1)}, u32[]{:S(2)}) copy-start(f32[1096,128]{1,0:T(8,128)S(1)} %collective-permute-done.27.refs_12_) | copy-start | bytes 1683460
  155.6 2.8 %copy-start.22 = (f32[1096,128]{1,0:T(8,128)}, f32[1096,128]{1,0:T(8,128)S(1)}, u32[]{:S(2)}) copy-start(f32[1096,128]{1,0:T(8,128)S(1)} %collective-permute-done.28.refs_13_) | copy-start | bytes 1683460
  157.5 0.8 copy-start.23

commit v6 on v5

--- a/solution.py
+++ b/solution.py
@@ -23,6 +23,7 @@
 decay_rate = 0.01
 matrices = 5
 MIB = 1 << 20
+SPLIT = 0.5
 
 
 def matrix_bounds(narrow):
@@ -48,17 +49,24 @@
         self.tail = 8
         self.norm_rows = 2 * D // LANE
         self.norm_each = -(-self.norm_rows // replicas)
-        self.block = self.own + self.tail
-        self.group = self.nx * self.block
-        self.half = self.nz * self.group
+        first = int(self.own * SPLIT / 8 + 0.5) * 8
+        self.rows = (first, self.own - first)
+        self.blocks_of = (first + self.tail, self.own - first)
+        self.groups = tuple(self.nx * block for block in self.blocks_of)
+        self.offsets = (0, self.nz * self.groups[0])
+        self.half = self.nz * sum(self.groups)
         self.lists = -(-blocks // (8 * LANE)) * 8
         self.bounds = matrix_bounds(narrow)
 
+    def order(self):
+        return [(z, stream, far_c) for far_c in (1, 0) for z in reversed(range(self.nz)) for stream in range(2)]
+
     def index(self, z, x, c):
         return (z * self.nx + x) * 2 + c
 
-    def start(self, far_z, far_x, far_c):
-        return (1 - far_c) * self.half + far_z * self.group + far_x * self.block
+    def start(self, stream, far_z, far_x, far_c):
+        there = far_z * self.groups[stream] + far_x * self.blocks_of[stream]
+        return (1 - far_c) * self.half + self.offsets[stream] + there
 
     def send(self, value, axis, pairs):
         every = []
@@ -108,8 +116,9 @@
     two = along_x(2, mine[2])
     near_three = sum(three[1:], three[0])
     in_three = plan.send(near_three, "z", INWARD)
+    count = len(two)
     in_three, *two = together(in_three, *two, *beside)
-    two, beside = two[: -len(beside)], two[-len(beside) :]
+    two, beside = two[:count], two[count:]
     near_two = sum(two[1:], two[0])
     one = along_x(1, mine[1])
     across_two = plan.send(near_two + in_three, "z", MIDDLE)
@@ -177,8 +186,8 @@
 
 
 def place_kernel(plan, place_ref, owner_ref, norm_ref, grads_ref, *refs):
-    out_refs, refs = refs[: 2 * plan.nz], refs[2 * plan.nz :]
-    position_ref, raw, moved, position, sem_in, sem_position, sem_out = refs
+    out_refs, refs = refs[: 4 * plan.nz], refs[4 * plan.nz :]
+    position_ref, limit_ref, raw, moved, position, sem_in, sem_position, sem_out = refs
     fetch = pltpu.make_async_copy(grads_ref, raw, sem_in)
     fetch.start()
     lists = plan.lists
@@ -192,6 +201,7 @@
     row_in = lax.broadcasted_iota(jnp.int32, (lists, lists), 1)
     above = (row_in < row_out).astype(jnp.bfloat16)
     result = jnp.zeros((lists, LANE), jnp.int32)
+    second = jnp.zeros((lists, LANE), jnp.bool_)
     for z in range(plan.nz):
         for x in range(plan.nx):
             for c in range(2):
@@ -201,16 +211,21 @@
                 totals = jnp.dot(flags, every, preferred_element_type=jnp.float32)
                 outer = jnp.dot(above, totals.astype(jnp.bfloat16), preferred_element_type=jnp.float32)
                 rank = (inner + outer).astype(jnp.int32)
-                start = plan.start(my_z ^ z, my_x ^ x, my_c ^ c)
+                slot = (my_z ^ z, my_x ^ x, my_c ^ c)
+                start, start_second = plan.start(0, *slot), plan.start(1, *slot) - plan.rows[0]
                 first_norm = plan.index(z, x, c) * plan.norm_each
                 tail = [jnp.zeros((plan.tail, LANE), jnp.float32)]
                 for row in range(min(first_norm + plan.norm_each, plan.norm_rows) - 1, first_norm - 1, -1):
                     part = norm_ref[row * LANE // D : row * LANE // D + 1, row * LANE % D : row * LANE % D + LANE]
                     tail.insert(0, part.astype(jnp.float32))
                 tail = jnp.concatenate(tail, 0)[: plan.tail]
-                moved[pl.ds(pl.multiple_of(start + plan.own, 8), plan.tail), :] = tail
-                result = jnp.where(mine, rank + start, result)
+                moved[pl.ds(pl.multiple_of(start + plan.rows[0], 8), plan.tail), :] = tail
+                late = mine & (rank >= plan.rows[0])
+                second = second | late
+                result = jnp.where(mine, rank + jnp.where(late, start_second, start), result)
     position_ref[...] = result
+    natural = lax.broadcasted_iota(jnp.int32, (lists, LANE), 0) * LANE + lax.broadcasted_iota(jnp.int32, (lists, LANE), 1)
+    limit_ref[0] = jnp.min(jnp.where(second, natural, plan.blocks))
     to_scalar = pltpu.make_async_copy(position_ref, position, sem_position)
     to_scalar.start()
     to_scalar.wait()
@@ -224,9 +239,9 @@
                 moved[pl.ds(position[line, part + u], 1), :] = rows[u : u + 1, :]
 
     copies = []
-    for i, out in enumerate(out_refs):
-        start = (i // plan.nz) * plan.half + (plan.nz - 1 - i % plan.nz) * plan.group
-        copies.append(pltpu.make_async_copy(moved.at[pl.ds(start, plan.group)], out, sem_out.at[i]))
+    for i, (out, (z, stream, far_c)) in enumerate(zip(out_refs, plan.order())):
+        start = plan.start(stream, z, 0, far_c)
+        copies.append(pltpu.make_async_copy(moved.at[pl.ds(start, plan.groups[stream])], out, sem_out.at[i]))
     for copy in copies:
         copy.start()
     for copy in copies:
@@ -234,18 +249,19 @@
 
 
 def place(plan, my_place, owners, norm_grads, grads):
-    shapes = [(plan.group, LANE)] * (2 * plan.nz)
+    shapes = [(plan.groups[stream], LANE) for _, stream, _ in plan.order()]
     outs = pl.pallas_call(
         functools.partial(place_kernel, plan),
         out_shape=[jax.ShapeDtypeStruct(s, jnp.float32) for s in shapes]
-        + [jax.ShapeDtypeStruct((plan.lists, LANE), jnp.int32)],
+        + [jax.ShapeDtypeStruct((plan.lists, LANE), jnp.int32), jax.ShapeDtypeStruct((1,), jnp.int32)],
         in_specs=[
             pl.BlockSpec(memory_space=pltpu.SMEM),
             pl.BlockSpec(memory_space=pltpu.VMEM),
             pl.BlockSpec(memory_space=pltpu.VMEM),
             pl.BlockSpec(memory_space=pl.ANY),
         ],
-        out_specs=[pl.BlockSpec(memory_space=pl.ANY)] * len(shapes) + [pl.BlockSpec(memory_space=pltpu.VMEM)],
+        out_specs=[pl.BlockSpec(memory_space=pl.ANY)] * len(shapes)
+        + [pl.BlockSpec(memory_space=pltpu.VMEM), pl.BlockSpec(memory_space=pltpu.SMEM)],
         scratch_shapes=[
             pltpu.VMEM((plan.blocks, LANE), jnp.bfloat16),
             pltpu.VMEM((2 * plan.half, LANE), jnp.float32),
@@ -257,7 +273,7 @@
         compiler_params=pltpu.CompilerParams(vmem_limit_bytes=58 * MIB),
         name="place_gradients",
     )(my_place, owners, norm_grads, grads)
-    return list(outs[: plan.nz][::-1]), outs[plan.nz : 2 * plan.nz][::-1], outs[-1]
+    return dict(zip(plan.order(), outs)), outs[-2], outs[-1]
 
 
 def owned_kernel(plan, place_ref, owner_ref, weights_ref, owned_ref, natural_ref, held, listed, order, sem_in, sem_order):
@@ -334,21 +350,25 @@
     )(my_place, owners, weights)
 
 
-def update_kernel(plan, terms, *refs):
-    parts, refs = refs[:terms], refs[terms:]
+def update_kernel(plan, counts, *refs):
+    parts, refs = refs[: sum(counts)], refs[sum(counts) :]
     first_ref, second_ref, weight_ref, natural_ref = refs[:4]
-    new_first_ref, new_second_ref, block_ref, stats_ref = refs[4:]
-    gradient = parts[0][: plan.block, :]
-    for part in parts[1:]:
-        gradient = gradient + part[: plan.block, :]
-    block_ref[plan.own :, :] = gradient[plan.own :, :]
-    gradient = gradient[: plan.own, :]
+    new_first_ref, new_second_ref, block_ref, block_second_ref, stats_ref = refs[4:]
+    gradients = []
+    for stream, terms in enumerate((parts[: counts[0]], parts[counts[0] :])):
+        gradient = terms[0][...]
+        for term in terms[1:]:
+            gradient = gradient + term[...]
+        gradients.append(gradient)
+    block_ref[plan.rows[0] :, :] = gradients[0][plan.rows[0] :, :]
+    gradient = jnp.concatenate([gradients[0][: plan.rows[0], :], gradients[1]], 0)
     moment_one = beta_one * first_ref[...] + (1.0 - beta_one) * gradient
     moment_two = beta_two * second_ref[...] + (1.0 - beta_two) * gradient * gradient
     new_first_ref[...] = moment_one
     new_second_ref[...] = moment_two
     step = moment_one / bias_one / (jnp.sqrt(moment_two / bias_two) + epsilon)
-    block_ref[: plan.own, :] = step
+    block_ref[: plan.rows[0], :] = step[: plan.rows[0], :]
+    block_second_ref[...] = step[plan.rows[0] :, :]
     weight = weight_ref[...]
     direction = step + decay_rate * weight
     natural = natural_ref[: plan.own, :]
@@ -367,15 +387,16 @@
 
 def update(plan, parts, first, second, weight, natural):
     vmem = pl.BlockSpec(memory_space=pltpu.VMEM)
-    shapes = [(plan.own, LANE), (plan.own, LANE), (plan.block, LANE), (plan.tail, LANE)]
+    counts = tuple(len(terms) for terms in parts)
+    shapes = [(plan.own, LANE), (plan.own, LANE)] + [(block, LANE) for block in plan.blocks_of] + [(plan.tail, LANE)]
     return pl.pallas_call(
-        functools.partial(update_kernel, plan, len(parts)),
+        functools.partial(update_kernel, plan, counts),
         out_shape=[jax.ShapeDtypeStruct(s, jnp.float32) for s in shapes],
-        in_specs=[vmem] * (len(parts) + 4),
+        in_specs=[vmem] * (sum(counts) + 4),
         out_specs=[vmem] * len(shapes),
         compiler_params=pltpu.CompilerParams(vmem_limit_bytes=20 * MIB),
         name="moments",
-    )(*parts, first, second, weight, natural)
+    )(*parts[0], *parts[1], first, second, weight, natural)
 
 
 def adam_rows(gradient, moment_one, moment_two, weight):
@@ -385,31 +406,61 @@
     return (moment_one, moment_two, step)
 
 
-def finish_kernel(plan, tile, slots, place_ref, position_ref, norm_ref, weights_ref, *refs):
+def fetch(plan, pieces, slots, held, sems):
+    copies = [
+        pltpu.make_async_copy(piece, held.at[pl.ds(plan.start(*slot), piece.shape[0])], sems.at[i])
+        for i, (piece, slot) in enumerate(zip(pieces, slots))
+    ]
+    for copy in copies:
+        copy.start()
+    for copy in copies:
+        copy.wait()
+
+
+def tile_of(plan):
+    tile = LANE
+    while tile < 512 and all(b % (2 * tile) == 0 for b in plan.bounds + (plan.blocks,)):
+        tile *= 2
+    return tile
+
+
+def new_tile(plan, tile, now, position_ref, rates, weights_ref, held, out_ref):
+    matrix = jnp.int32(0)
+    for bound in plan.bounds:
+        matrix = matrix + (now * tile >= bound).astype(jnp.int32)
+    rate = jnp.broadcast_to(rates[pl.ds(matrix, 1), :], (8, LANE))
+    lines = tile // LANE
+
+    @pl.loop(0, lines)
+    def _(line):
+        for group in range(0, LANE, 8):
+            rows = [held[pl.ds(position_ref[now * lines + line, group + u], 1), :] for u in range(8)]
+            here = pl.ds(pl.multiple_of(line * LANE + group, 8), 8)
+            weight = weights_ref[here, :]
+            direction = jnp.concatenate(rows, 0) + decay_rate * weight
+            out_ref[here, :] = weight - rate * direction
+
+
+def early_kernel(plan, slots, limit_ref, place_ref, position_ref, norm_ref, weights_ref, *refs):
     pieces, refs = refs[: len(slots)], refs[len(slots) :]
-    out_ref, new_norm_ref, trust_ref, held, norms, rates, sems = refs
+    out_ref, rates, new_norm_ref, trust_ref, held, norms, sems = refs
     now = pl.program_id(0)
+    tile = tile_of(plan)
 
     @pl.when(now == 0)
     def _():
-        copies = [
-            pltpu.make_async_copy(piece, held.at[pl.ds(plan.start(*slot), plan.block)], sems.at[i])
-            for i, (piece, slot) in enumerate(zip(pieces, slots))
-        ]
-        for copy in copies:
-            copy.start()
-        for copy in copies:
-            copy.wait()
+        fetch(plan, pieces, slots, held, sems)
         total = jnp.zeros((plan.tail, LANE), jnp.float32)
         for z in range(plan.nz):
             for x in range(plan.nx):
                 for c in range(2):
-                    start = plan.start(place_ref[0] ^ z, place_ref[1] ^ x, place_ref[2] ^ c) + plan.own
+                    start = plan.start(0, place_ref[0] ^ z, place_ref[1] ^ x, place_ref[2] ^ c) + plan.rows[0]
                     tail = held[pl.ds(pl.multiple_of(start, 8), plan.tail), :]
                     total = total + tail
                     first = plan.index(z, x, c) * plan.norm_each
                     for row in range(first, min(first + plan.norm_each, plan.norm_rows)):
                         norms[row : row + 1, :] = tail[row - first : row - first + 1, :]
+        rates[...] = jnp.zeros_like(rates)
         for k in range(matrices):
             row = plan.norm_each + k
             weight_square, direction_square = total[row : row + 1, 0:1], total[row : row + 1, 1:2]
@@ -431,48 +482,85 @@
                 for row in range(each):
                     new_norm_ref[j, i : i + 1, row * LANE : (row + 1) * LANE] = value[row : row + 1, :]
 
-    matrix = jnp.int32(0)
-    for bound in plan.bounds:
-        matrix = matrix + (now * tile >= bound).astype(jnp.int32)
-    rate = jnp.broadcast_to(rates[pl.ds(matrix, 1), :], (8, LANE))
-    lines = tile // LANE
-
-    @pl.loop(0, lines)
-    def _(line):
-        for group in range(0, LANE, 8):
-            rows = [held[pl.ds(position_ref[now * lines + line, group + u], 1), :] for u in range(8)]
-            here = pl.ds(pl.multiple_of(line * LANE + group, 8), 8)
-            weight = weights_ref[here, :]
-            direction = jnp.concatenate(rows, 0) + decay_rate * weight
-            out_ref[here, :] = weight - rate * direction
-
-
-def finish(plan, my_place, position, norm_state, weights, pieces, slots):
-    tile = LANE
-    while tile < 1024 and all(b % (2 * tile) == 0 for b in plan.bounds + (plan.blocks,)):
-        tile *= 2
+    @pl.when((now + 1) * tile <= limit_ref[0])
+    def _():
+        new_tile(plan, tile, now, position_ref, rates, weights_ref, held, out_ref)
+
+
+def late_kernel(plan, slots, limit_ref, position_ref, rates_ref, weights_ref, early_ref, *refs):
+    pieces, refs = refs[: len(slots)], refs[len(slots) :]
+    out_ref, held, sems = refs
+    now = pl.program_id(0)
+    tile = tile_of(plan)
+
+    @pl.when(now == 0)
+    def _():
+        fetch(plan, pieces, slots, held, sems)
+
+    @pl.when((now + 1) * tile > limit_ref[0])
+    def _():
+        new_tile(plan, tile, now, position_ref, rates_ref, weights_ref, held, out_ref)
+
+
+def finish(plan, my_place, limit, position, norm_state, weights, founds):
+    tile = tile_of(plan)
+    count = plan.blocks // tile
     smem = pl.BlockSpec(memory_space=pltpu.SMEM)
     vmem = pl.BlockSpec(memory_space=pltpu.VMEM)
-    return pl.pallas_call(
-        functools.partial(finish_kernel, plan, tile, slots),
-        grid=(plan.blocks // tile,),
+    anywhere = pl.BlockSpec(memory_space=pl.ANY)
+    params = pltpu.CompilerParams(vmem_limit_bytes=24 * MIB)
+    slots = [[(stream,) + slot for slot, _ in found] for stream, found in enumerate(founds)]
+    pieces = [[piece for _, piece in found] for found in founds]
+
+    def early_tile(i, limit_ref):
+        return (jnp.maximum(jnp.minimum(i, limit_ref[0] // tile - 1), 0), 0)
+
+    def late_tile(i, limit_ref):
+        return (jnp.minimum(jnp.maximum(i, limit_ref[0] // tile), count - 1), 0)
+
+    shape = jax.ShapeDtypeStruct((plan.blocks, LANE), jnp.float32)
+    early, rates, new_norm, trust = pl.pallas_call(
+        functools.partial(early_kernel, plan, slots[0]),
+        grid_spec=pltpu.PrefetchScalarGridSpec(
+            num_scalar_prefetch=1,
+            grid=(count,),
+            in_specs=[smem, smem, vmem, pl.BlockSpec((tile, LANE), early_tile)] + [anywhere] * len(pieces[0]),
+            out_specs=[pl.BlockSpec((tile, LANE), early_tile), vmem, vmem, smem],
+            scratch_shapes=[
+                pltpu.VMEM((2 * plan.half, LANE), jnp.float32),
+                pltpu.VMEM((plan.norm_rows, LANE), jnp.float32),
+                pltpu.SemaphoreType.DMA((len(pieces[0]),)),
+            ],
+        ),
         out_shape=[
-            jax.ShapeDtypeStruct((plan.blocks, LANE), jnp.float32),
+            shape,
+            jax.ShapeDtypeStruct((8, LANE), jnp.float32),
             jax.ShapeDtypeStruct(norm_state.shape, jnp.float32),
             jax.ShapeDtypeStruct((matrices + 2,), jnp.float32),
         ],
-        in_specs=[smem, smem, vmem, pl.BlockSpec((tile, LANE), lambda i: (i, 0))]
-        + [pl.BlockSpec(memory_space=pl.ANY)] * len(pieces),
-        out_specs=[pl.BlockSpec((tile, LANE), lambda i: (i, 0)), vmem, smem],
-        scratch_shapes=[
-            pltpu.VMEM((2 * plan.half, LANE), jnp.float32),
-            pltpu.VMEM((plan.norm_rows, LANE), jnp.float32),
-            pltpu.VMEM((8, LANE), jnp.float32),
-            pltpu.SemaphoreType.DMA((len(pieces),)),
-        ],
-        compiler_params=pltpu.CompilerParams(vmem_limit_bytes=58 * MIB),
-        name="new_weights",
-    )(my_place, position, norm_state, weights, *pieces)
+        compiler_params=params,
+        cost_estimate=pl.CostEstimate(flops=0, bytes_accessed=36 * MIB, transcendentals=0),
+        name="new_weights_early",
+    )(limit, my_place, position, norm_state, weights, *pieces[0])
+    new_weights = pl.pallas_call(
+        functools.partial(late_kernel, plan, slots[0] + slots[1]),
+        grid_spec=pltpu.PrefetchScalarGridSpec(
+            num_scalar_prefetch=1,
+            grid=(count,),
+            in_specs=[smem, vmem, pl.BlockSpec((tile, LANE), late_tile), anywhere]
+            + [anywhere] * len(pieces[0] + pieces[1]),
+            out_specs=pl.BlockSpec((tile, LANE), late_tile),
+            scratch_shapes=[
+                pltpu.VMEM((2 * plan.half, LANE), jnp.float32),
+                pltpu.SemaphoreType.DMA((len(pieces[0] + pieces[1]),)),
+            ],
+        ),
+        out_shape=shape,
+        input_output_aliases={4: 0},
+        compiler_params=params,
+        name="new_weights_late",
+    )(limit, position, rates, weights, early, *pieces[0], *pieces[1])
+    return new_weights, new_norm, trust
 
 
 def local(gradients, weights, first_moment, second_moment, owner_list, norm_grads, norm_state):
@@ -481,29 +569,37 @@
     my_place = jnp.stack([me // (2 * plan.nx), (me // 2) % plan.nx, me % 2]).astype(jnp.int32)
     owners = jnp.pad(owner_list[0], (0, plan.lists * LANE - plan.blocks), constant_values=-1)
     owners = owners.reshape(plan.lists, LANE)
-    siblings, blocks, position = place(plan, my_place, owners, norm_grads[0], gradients[0])
+    placed, position, limit = place(plan, my_place, owners, norm_grads[0], gradients[0])
     weight_own, natural = owned(plan, my_place, owners, weights)
 
-    mine, theirs = [None] * plan.nz, [None] * plan.nz
+    mine, theirs = ([None] * plan.nz, [None] * plan.nz), ([None] * plan.nz, [None] * plan.nz)
     for z in reversed(range(plan.nz)):
-        other = plan.swap(siblings[z])
-        both = [
-            blocks[z][x * plan.block : (x + 1) * plan.block] + other[x * plan.block : (x + 1) * plan.block]
-            for x in range(plan.nx)
-        ]
-        mine[z], theirs[z] = both[0], both[1:]
-        if z == 3:
-            theirs[3], siblings[2], siblings[1], siblings[0] = together(theirs[3], *siblings[2::-1])
-    if plan.nz == 4:
-        parts = reduce(plan, mine, theirs, (weight_own, natural))
-        parts, (weight_own, natural) = parts[:-2], parts[-2:]
-    else:
-        near = []
-        for z in reversed(range(plan.nz)):
-            terms = line_reduce(plan, "x", [mine[z]] + theirs[z])
-            near.insert(0, sum(terms[1:], terms[0]) if z else None)
-        parts = terms + line_reduce(plan, "z", near)[1:]
-    new_first, new_second, block, stats = update(
+        for stream in range(2):
+            other, here, block = plan.swap(placed[z, stream, 1]), placed[z, stream, 0], plan.blocks_of[stream]
+            both = [
+                here[x * block : (x + 1) * block] + other[x * block : (x + 1) * block] for x in range(plan.nx)
+            ]
+            mine[stream][z], theirs[stream][z] = both[0], both[1:]
+            if z == 3 and stream == 0:
+                later = [slot for slot in plan.order() if slot[2] == 1 and slot != (3, 0, 1)]
+                theirs[0][3], *values = together(theirs[0][3], *(placed[slot] for slot in later))
+                placed.update(zip(later, values))
+    parts = []
+    for stream in range(2):
+        if plan.nz == 4:
+            beside = (weight_own, natural) if stream == 0 else ()
+            terms = reduce(plan, mine[stream], theirs[stream], beside)
+            if stream == 0:
+                terms, (weight_own, natural) = terms[:-2], terms[-2:]
+                terms = [sum(terms[1:], terms[0])]
+            parts.append(terms)
+        else:
+            near = []
+            for z in reversed(range(plan.nz)):
+                terms = line_reduce(plan, "x", [mine[stream][z]] + theirs[stream][z])
+                near.insert(0, sum(terms[1:], terms[0]) if z else None)
+            parts.append(terms + line_reduce(plan, "z", near)[1:])
+    new_first, new_second, block, block_second, stats = update(
         plan, parts, first_moment[0], second_moment[0], weight_own, natural
     )
 
@@ -511,10 +607,9 @@
     while hop < plan.narrow:
         stats = stats + lax.ppermute(stats, "mp", [(i, i ^ hop) for i in range(plan.narrow)])
         hop *= 2
-    block = lax.dynamic_update_slice(block, block[plan.own :] + stats, (plan.own, 0))
-    found = gather(plan, block)
-    slots, pieces = [slot for slot, _ in found], [piece for _, piece in found]
-    new_weights, new_state, trust_ratios = finish(plan, my_place, position, norm_state, weights, pieces, slots)
+    block = lax.dynamic_update_slice(block, block[plan.rows[0] :] + stats, (plan.rows[0], 0))
+    founds = [gather(plan, block), gather(plan, block_second)]
+    new_weights, new_state, trust_ratios = finish(plan, my_place, limit, position, norm_state, weights, founds)
     return (new_weights, new_first[None], new_second[None], new_state, trust_ratios)
 
 

time: 185 us -> 206 us (1.11)
  starting transfers between devices: 35.4 us -> 57.2 us
  Pallas kernels: 58 us -> 64.8 us
  waiting for transfers between devices: 85.4 us -> 79.4 us
    ppermute x30 -> x60, starting transfers between devices: 33.9 us -> 55.7 us  [send(): return lax.ppermute(value, 'dp', every)]
    pallas_call x2 -> x3, Pallas kernels: 27.7 us -> 34.4 us  [the longest x1 16.5 us: finish(): pl.pallas_call(functools.partial(late_kernel, plan, slots[0] + slots[1]),...]
    ppermute x30 -> x60, waiting for transfers between devices: 83.3 us -> 77.3 us  [send(): return lax.ppermute(value, 'dp', every)]
  transfers between devices with their start and end apart: 31 -> 61, of which waited for: 16 -> 20; matrix products, arithmetic and copies ran while one was open for 0% -> 1% of each run, Pallas kernels for 3% -> 11%
where the time goes in v6:
time: 206 us
  waiting for transfers between devices  79.4 us (39%)
  Pallas kernels  64.8 us (31%)
  starting transfers between devices  57.2 us (28%)
  other arithmetic  2.62 us (1%)
    ppermute x60, waiting for transfers between devices, send(): return lax.ppermute(value, 'dp', every)  77.3 us
    ppermute x60, starting transfers between devices, send(): return lax.ppermute(value, 'dp', every)  55.7 us
    pallas_call x1, Pallas kernels, place(): pl.pallas_call(functools.partial(place_kernel, plan), out_shape=[jax.Shap...  24.1 us
    pallas_call x1, Pallas kernels, finish(): pl.pallas_call(functools.partial(late_kernel, plan, slots[0] + slots[1]),...  16.5 us
    pallas_call x1, Pallas kernels, finish(): pl.pallas_call(functools.partial(early_kernel, plan, slots[0]), grid_spec...  15.3 us
    pallas_call x1, Pallas kernels, owned(): pl.pallas_call(functools.partial(owned_kernel, plan), out_shape=[jax.Shap...  6.39 us
  transfers between devices with their start and end apart: 61, of which 20 were waited for; matrix products, arithmetic and copies ran while one was open for 1% of the time, Pallas kernels for 11%

profile of v6, /device:TPU:0, one launch (start us, length us, event | category | flops | bytes accessed | tf_op | source)
XLA Modules:
  0.0 205.6 jit_solution(1287623445068329839)
XLA Ops:
  0.7 0.6 pad_add_fusion.place_ref
  1.3 24.1 %place_gradients.1 = (f32[1104,128]{1,0:T(8,128)}, f32[1088,128]{1,0:T(8,128)}, f32[1104,128]{1,0:T(8,128)}, f32[1088,128]{1,0:T(8,128)}, f32[1104,128]{1,0:T(8,...) custom-call(s32[3]{0:T(128)} %pad_add_fusion.place_ref, ...), custom_call_target="tpu_custom_call" | custom-call | tf_op jit(solution)/shard_map/place_gradients/pallas_call | solution.py:253
  25.4 0.5 collective-permute-start
  25.9 1.8 collective-permute-done
  27.7 1.0 slice_add_fusion.7
  29.2 2.6 %collective-permute-start.3 = (f32[552,128]{1,0:T(8,128)S(1)}, f32[552,128]{1,0:T(8,128)S(1)}, u32[]{:S(2)}, u32[]{:S(2)}) collective-permute-start(f32[552,128]{1,0:T(8,128)S(1)} %slice_add_fusion.7), channel_id=1, source_target_pairs={{0,4},{2,6},{4,0},{6,2},{8,12},{10,14},{12,8},{14,10},{16,20},{18,... | collective-permute-start | bytes 847880 | tf_op jit(solution)/shard_map/ppermute | solution.py:80
  31.9 6.4 %owned_weights.1 = (f32[1088,128]{1,0:T(8,128)}, s32[1152,128]{1,0:T(8,128)}) custom-call(s32[3]{0:T(128)} %pad_add_fusion.place_ref, s32[136,128]{1,0:T(8,128)} %bitcast.16, f32[17408,128]{1,0:T(8,128)} %weights_ref.5), custom_call_target="tpu_custom_call" | custom-call | bytes 20971520 | tf_op jit(solution)/shard_map/owned_weights/pallas_call | solution.py:332
  40.2 1.2 collective-permute-done.22
  41.4 3.5 %collective-permute-start.4 = (f32[552,128]{1,0:T(8,128)S(1)}, f32[552,128]{1,0:T(8,128)S(1)}, u32[]{:S(2)}, u32[]{:S(2)}) collective-permute-start(f32[552,128]{1,0:T(8,128)S(1)} %fusion), channel_id=1, source_target_pairs={{0,8},{2,10},{4,12},{6,14},{24,16},{26,18},{28,20},{30,22},{1,9},{... | collective-permute-start | bytes 847880 | tf_op jit(solution)/shard_map/ppermute | solution.py:80
  45.0 0.7 collective-permute-start.16
  45.8 1.4 collective-permute-start.6
  47.3 7.3 %collective-permute-done.16 = f32[544,128]{1,0:T(8,128)S(1)} collective-permute-done((f32[544,128]{1,0:T(8,128)S(1)}, f32[544,128]{1,0:T(8,128)S(1)}, u32[]{:S(2)}, u32[]{:S(2)}) %collective-permute-start.16) | collective-permute-done | bytes 278560 | tf_op jit(solution)/shard_map/ppermute | solution.py:80
  54.6 0.7 collective-permute-start.19
  55.3 1.4 collective-permute-start.10
  56.7 3.9 %collective-permute-done.6 = f32[552,128]{1,0:T(8,128)S(1)} collective-permute-done((f32[552,128]{1,0:T(8,128)S(1)}, f32[552,128]{1,0:T(8,128)S(1)}, u32[]{:S(2)}, u32[]{:S(2)}) %collective-permute-start.6) | collective-permute-done | bytes 282656 | tf_op jit(solution)/shard_map/ppermute | solution.py:80
  60.6 1.4 collective-permute-start.17
  62.2 0.7 collective-permute-start.7
  62.8 3.8 %collective-permute-done.19 = f32[544,128]{1,0:T(8,128)S(1)} collective-permute-done((f32[544,128]{1,0:T(8,128)S(1)}, f32[544,128]{1,0:T(8,128)S(1)}, u32[]{:S(2)}, u32[]{:S(2)}) %collective-permute-start.19) | collective-permute-done | bytes 278560 | tf_op jit(solution)/shard_map/ppermute | solution.py:80
  66.6 1.4 collective-permute-start.8
  68.1 0.9 collective-permute-start.23
  69.0 3.6 %collective-permute-done.10 = f32[552,128]{1,0:T(8,128)S(1)} collective-permute-done((f32[552,128]{1,0:T(8,128)S(1)}, f32[552,128]{1,0:T(8,128)S(1)}, u32[]{:S(2)}, u32[]{:S(2)}) %collective-permute-start.10) | collective-permute-done | bytes 282656 | tf_op jit(solution)/shard_map/ppermute | solution.py:80
  72.6 0.7 collective-permute-start.2
  73.3 0.7 collective-permute-start.20
  74.0 4.4 %collective-permute-start.21 = (f32[544,128]{1,0:T(8,128)S(1)}, f32[544,128]{1,0:T(8,128)S(1)}, u32[]{:S(2)}, u32[]{:S(2)}) collective-permute-start(f32[544,128]{1,0:T(8,128)S(1)} %get-tuple-element.156), channel_id=1, source_target_pairs={{0,8},{2,10},{4,12},{6,14},{24,16},{26,18},{28,20},{30,22},{1,9},{... | collective-permute-start | bytes 835592 | tf_op jit(solution)/shard_map/ppermute | solution.py:80
  78.6 0.7 collective-permute-start.12
  79.4 1.3 collective-permute-start.14
  80.6 4.8 %collective-permute-done.21 = f32[544,128]{1,0:T(8,128)S(1)} collective-permute-done((f32[544,128]{1,0:T(8,128)S(1)}, f32[544,128]{1,0:T(8,128)S(1)}, u32[]{:S(2)}, u32[]{:S(2)}) %collective-permute-start.21) | collective-permute-done | bytes 278560 | tf_op jit(solution)/shard_map/ppermute | solution.py:80
  85.6 2.5 %collective-permute-start.24 = (f32[544,128]{1,0:T(8,128)S(1)}, f32[544,128]{1,0:T(8,128)S(1)}, u32[]{:S(2)}, u32[]{:S(2)}) collective-permute-start(f32[544,128]{1,0:T(8,128)S(1)} %add_add_fusion.1), channel_id=1, source_target_pairs={{0,8},{2,10},{4,12},{6,14},{8,0},{10,2},{12,4},{14,6},{16,24},{18,... | collective-permute-start | bytes 835592 | tf_op jit(solution)/shard_map/ppermute | solution.py:80
  88.1 0.7 collective-permute-start.25
  88.8 2.6 %collective-permute-done.11 = f32[552,128]{1,0:T(8,128)S(1)} collective-permute-done((f32[552,128]{1,0:T(8,128)S(1)}, f32[552,128]{1,0:T(8,128)S(1)}, u32[]{:S(2)}, u32[]{:S(2)}) %collective-permute-start.11) | collective-permute-done | bytes 282656 | tf_op jit(solution)/shard_map/ppermute | solution.py:80
  91.6 2.8 %collective-permute-done.24.refs_3_ = f32[544,128]{1,0:T(8,128)S(1)} collective-permute-done((f32[544,128]{1,0:T(8,128)S(1)}, f32[544,128]{1,0:T(8,128)S(1)}, u32[]{:S(2)}, u32[]{:S(2)}) %collective-permute-start.24) | collective-permute-done | bytes 278560 | tf_op jit(solution)/shard_map/ppermute | solution.py:80
  94.4 2.5 %moments.1 = (f32[1088,128]{1,0:T(8,128)}, f32[1088,128]{1,0:T(8,128)}, f32[552,128]{1,0:T(8,128)S(1)}, f32[544,128]{1,0:T(8,128)S(1)}, f32[8,128]{1,0:T(8,128)S(1)}) custom-call(f32[552,128]{1,0:T(8,128)S(1)} %fusion.3.refs_0_, f32[544,128]{1,0:T(8,128)S(1)} %get-tuple-element.168.refs_1_, f32[544,128]{1,0:T(8,128)S(1)} %collective-permute-done.14.refs_2_, ...), custom_call_target="tpu_custom_call" | custom-call | tf_op jit(solution)/shard_map/moments/pallas_call | solution.py:392
  97.0 1.5 collective-permute-start.26
  98.5 2.1 %collective-permute-done.26 = f32[8,128]{1,0:T(8,128)S(1)} collective-permute-done((f32[8,128]{1,0:T(8,128)S(1)}, f32[8,128]{1,0:T(8,128)S(1)}, u32[]{:S(2)}, u32[]{:S(2)}) %collective-permute-start.26) | collective-permute-done | bytes 4128 | tf_op jit(solution)/shard_map/ppermute | solution.py:608
  100.6 1.7 collective-permute-start.29
  102.3 0.7 collective-permute-start.28
  103.0 4.2 %collective-permute-start.27 = (f32[552,128]{1,0:T(8,128)S(1)}, f32[552,128]{1,0:T(8,128)S(1)}, u32[]{:S(2)}, u32[]{:S(2)}) collective-permute-start(f32[552,128]{1,0:T(8,128)S(1)} %add_dynamic-update-slice_fusion.refs_0_), channel_id=1, source_target_pairs={{0,8},{2,10},{4,12},{6,14},{8,0},{10,2},{12,4},{14,6},{16,24},{18,... | collective-permute-start | bytes 847880 | tf_op jit(solution)/shard_map/ppermute | solution.py:80
  107.2 4.8 %collective-permute-done.27.refs_4_ = f32[552,128]{1,0:T(8,128)S(1)} collective-permute-done((f32[552,128]{1,0:T(8,128)S(1)}, f32[552,128]{1,0:T(8,128)S(1)}, u32[]{:S(2)}, u32[]{:S(2)}) %collective-permute-start.27) | collective-permute-done | bytes 282656 | tf_op jit(solution)/shard_map/ppermute | solution.py:80
  112.0 1.3 collective-permute-start.33
  113.3 1.2 collective-permute-start.34
  114.4 0.7 collective-permute-start.32
  115.1 1.0 collective-permute-start.46
  116.1 0.7 collective-permute-start.45
  116.8 5.7 %collective-permute-done.33 = f32[552,128]{1,0:T(8,128)S(1)} collective-permute-done((f32[552,128]{1,0:T(8,128)S(1)}, f32[552,128]{1,0:T(8,128)S(1)}, u32[]{:S(2)}, u32[]{:S(2)}) %collective-permute-start.33) | collective-permute-done | bytes 282656 | tf_op jit(solution)/shard_map/ppermute | solution.py:80
  122.5 1.5 collective-permute-start.44
  124.0 1.2 collective-permute-start.38
  125.2 0.6 collective-permute-done.46.refs_17_
  125.8 4.0 %collective-permute-done.44.refs_20_ = f32[544,128]{1,0:T(8,128)S(1)} collective-permute-done((f32[544,128]{1,0:T(8,128)S(1)}, f32[544,128]{1,0:T(8,128)S(1)}, u32[]{:S(2)}, u32[]{:S(2)}) %collective-permute-start.44) | collective-permute-done | bytes 278560 | tf_op jit(solution)/shard_map/ppermute | solution.py:80
  129.9 1.3 collective-permute-start.50
  131.2 2.6 %collective-permute-start.51 = (f32[544,128]{1,0:T(8,128)S(1)}, f32[544,128]{1,0:T(8,128)S(1)}, u32[]{:S(2)}, u32[]{:S(2)}) collective-permute-start(f32[544,128]{1,0:T(8,128)S(1)} %collective-permute-done.44.refs_20_), channel_id=1, source_target_pairs={{0,4},{2,6},{4,0},{6,2},{8,12},{10,14},{12,8},{14,10},{16,20},{18,... | collective-permute-start | bytes 835592 | tf_op jit(solution)/shard_map/ppermute | solution.py:80
  133.8 1.3 collective-permute-start.37
  135.1 0.7 collective-permute-start.49
  135.8 2.5 %collective-permute-done.50 = f32[544,128]{1,0:T(8,128)S(1)} collective-permute-done((f32[544,128]{1,0:T(8,128)S(1)}, f32[544,128]{1,0:T(8,128)S(1)}, u32[]{:S(2)}, u32[]{:S(2)}) %collective-permute-start.50) | collective-permute-done | bytes 278560 | tf_op jit(solution)/shard_map/ppermute | solution.py:80
  139.4 2.9 %collective-permute-done.37 = f32[552,128]{1,0:T(8,128)S(1)} collective-permute-done((f32[552,128]{1,0:T(8,128)S(1)}, f32[552,128]{1,0:T(8,128)S(1)}, u32[]{:S(2)}, u32[]{:S(2)}) %collective-permute-start.37) | collective-permute-done | bytes 282656 | tf_op jit(solution)/shard_map/ppermute | solution.py:80
  142.3 1.6 collective-permute-start.55
  145.0 6.1 %collective-permute-done.55.refs_25_ = f32[544,128]{1,0:T(8,128)S(1)} collective-permute-done((f32[544,128]{1,0:T(8,128)S(1)}, f32[544,128]{1,0:T(8,128)S(1)}, u32[]{:S(2)}, u32[]{:S(2)}) %collective-permute-start.55) | collective-permute-done | bytes 278560 | tf_op jit(solution)/shard_map/ppermute | solution.py:80
  151.0 1.5 collective-permute-start.54
  152.6 10.0 %collective-permute-done.54 = f32[544,128]{1,0:T(8,128)S(1)} collective-permute-done((f32[544,128]{1,0:T(8,128)S(1)}, f32[544,128]{1,0:T(8,128)S(1)}, u32[]{:S(2)}, u32[]{:S(2)}) %collective-permute-start.54) | collective-permute-done | bytes 278560 | tf_op jit(solution)/shard_map/ppermute | solution.py:80
  162.7 0.5 collective-permute-start.41
  163.3 0.7 collective-permute-start.56
  164.0 8.3 %collective-permute-done.56.refs_27_ = f32[544,128]{1,0:T(8,128)S(1)} collective-permute-done((f32[544,128]{1,0:T(8,128)S(1)}, f32[544,128]{1,0:T(8,128)S(1)}, u32[]{:S(2)}, u32[]{:S(2)}) %collective-permute-start.56) | collective-permute-done | bytes 278560 | tf_op jit(solution)/shard_map/ppermute | solution.py:80
  172.4 0.5 collective-permute-start.59
  173.5 15.3 %new_weights_early.1 = (f32[17408,128]{1,0:T(8,128)}, f32[8,128]{1,0:T(8,128)S(1)}, f32[3,2,1024]{2,1,0:T(2,128)}, f32[7]{0:T(128)}) custom-call(s32[1]{0:T(128)} %get-tuple-element.80.limit_ref, s32[3]{0:T(128)S(1)} %copy-done.6, s32[136,128]{1,0:T(8,128)S(1)} %copy-done.4, f32[3,2,1024]{2,1,0:T(2,128)S(1)} %copy-done.5, f32[17408,128]{1,0:T(8,128)S(1)} %bitcast.11, ...), custom_call_target="tpu_custom_call" | custom-call | bytes 37748736 | tf_op jit(solution)/shard_map/new_weights_early/pallas_call | solution.py:522
  188.9 16.5 %new_weights_late.1 = f32[17408,128]{1,0:T(8,128)} custom-call(s32[1]{0:T(128)} %get-tuple-element.80.limit_ref, s32[136,128]{1,0:T(8,128)S(1)} %copy-done.4, f32[8,128]{1,0:T(8,128)S(1)} %get-tuple-element.137.rates_ref, f32[17408,128]{1,0:T(8,128)S(1)} %bitcast.11, f32[17408,128]{1,0:T(8,128)} %get-tuple-element.138.early_ref, ...), custom_call_target="tpu_custom_call", output_to_operand_aliasing={{}: (4, {})} | custom-call | tf_op jit(solution)/shard_map/new_weights_late/pallas_call | solution.py:545
  (123 shorter events, 6.2 us)
Async XLA Ops:
  25.4 2.3 %collective-permute-start = (f32[1104,128]{1,0:T(8,128)}, f32[1104,128]{1,0:T(8,128)S(1)}, u32[]{:S(2)}, u32[]{:S(2)}) collective-permute-start(f32[1104,128]{1,0:T(8,128)} %get-tuple-element.84), channel_id=1, source_target_pairs={{0,2},{2,0},{4,6},{6,4},{8,10},{10,8},{12,14},{14,12},{16,18},{18,... | collective-permute-start | bytes 1695752 | tf_op jit(solution)/shard_map/ppermute | solution.py:80
  28.7 10.6 %collective-permute-start.18 = (f32[1088,128]{1,0:T(8,128)}, f32[1088,128]{1,0:T(8,128)S(1)}, u32[]{:S(2)}, u32[]{:S(2)}) collective-permute-start(f32[1088,128]{1,0:T(8,128)} %get-tuple-element.112), channel_id=1, source_target_pairs={{0,2},{2,0},{4,6},{6,4},{8,10},{10,8},{12,14},{14,12},{16,18},{18,... | collective-permute-start | bytes 1671176 | tf_op jit(solution)/shard_map/ppermute | solution.py:80
  29.2 9.9 %collective-permute-start.3 = (f32[552,128]{1,0:T(8,128)S(1)}, f32[552,128]{1,0:T(8,128)S(1)}, u32[]{:S(2)}, u32[]{:S(2)}) collective-permute-start(f32[552,128]{1,0:T(8,128)S(1)} %slice_add_fusion.7), channel_id=1, source_target_pairs={{0,4},{2,6},{4,0},{6,2},{8,12},{10,14},{12,8},{14,10},{16,20},{18,... | collective-permute-start | bytes 847880 | tf_op jit(solution)/shard_map/ppermute | solution.py:80
  31.8 8.0 %collective-permute-start.15 = (f32[1088,128]{1,0:T(8,128)}, f32[1088,128]{1,0:T(8,128)S(1)}, u32[]{:S(2)}, u32[]{:S(2)}) collective-permute-start(f32[1088,128]{1,0:T(8,128)} %get-tuple-element.110), channel_id=1, source_target_pairs={{0,2},{2,0},{4,6},{6,4},{8,10},{10,8},{12,14},{14,12},{16,18},{18,... | collective-permute-start | bytes 1671176 | tf_op jit(solution)/shard_map/ppermute | solution.py:80
  38.3 40.2 %collective-permute-start.13 = (f32[1088,128]{1,0:T(8,128)}, f32[1088,128]{1,0:T(8,128)S(1)}, u32[]{:S(2)}, u32[]{:S(2)}) collective-permute-start(f32[1088,128]{1,0:T(8,128)} %get-tuple-element.108), channel_id=1, source_target_pairs={{0,2},{2,0},{4,6},{6,4},{8,10},{10,8},{12,14},{14,12},{16,18},{18,... | collective-permute-start | bytes 1671176 | tf_op jit(solution)/shard_map/ppermute | solution.py:80
  38.8 2.6 %collective-permute-start.22 = (f32[1088,128]{1,0:T(8,128)}, f32[1088,128]{1,0:T(8,128)S(1)}, u32[]{:S(2)}, u32[]{:S(2)}) collective-permute-start(f32[1088,128]{1,0:T(8,128)} %get-tuple-element.117), channel_id=1, source_target_pairs={{0,2},{2,0},{4,6},{6,4},{8,10},{10,8},{12,14},{14,12},{16,18},{18,... | collective-permute-start | bytes 1671176 | tf_op jit(solution)/shard_map/ppermute | solution.py:80
  39.1 23.1 %collective-permute-start.1 = (f32[1104,128]{1,0:T(8,128)}, f32[1104,128]{1,0:T(8,128)S(1)}, u32[]{:S(2)}, u32[]{:S(2)}) collective-permute-start(f32[1104,128]{1,0:T(8,128)} %get-tuple-element.92), channel_id=1, source_target_pairs={{0,2},{2,0},{4,6},{6,4},{8,10},{10,8},{12,14},{14,12},{16,18},{18,... | collective-permute-start | bytes 1695752 | tf_op jit(solution)/shard_map/ppermute | solution.py:80
  39.4 5.6 %collective-permute-start.5 = (f32[1104,128]{1,0:T(8,128)}, f32[1104,128]{1,0:T(8,128)S(1)}, u32[]{:S(2)}, u32[]{:S(2)}) collective-permute-start(f32[1104,128]{1,0:T(8,128)} %get-tuple-element.95), channel_id=1, source_target_pairs={{0,2},{2,0},{4,6},{6,4},{8,10},{10,8},{12,14},{14,12},{16,18},{18,... | collective-permute-start | bytes 1695752 | tf_op jit(solution)/shard_map/ppermute | solution.py:80
  39.8 6.0 %collective-permute-start.9 = (f32[1104,128]{1,0:T(8,128)}, f32[1104,128]{1,0:T(8,128)S(1)}, u32[]{:S(2)}, u32[]{:S(2)}) collective-permute-start(f32[1104,128]{1,0:T(8,128)} %get-tuple-element.102), channel_id=1, source_target_pairs={{0,2},{2,0},{4,6},{6,4},{8,10},{10,8},{12,14},{14,12},{16,18},{18,... | collective-permute-start | bytes 1695752 | tf_op jit(solution)/shard_map/ppermute | solution.py:80
  41.4 13.9 %collective-permute-start.4 = (f32[552,128]{1,0:T(8,128)S(1)}, f32[552,128]{1,0:T(8,128)S(1)}, u32[]{:S(2)}, u32[]{:S(2)}) collective-permute-start(f32[552,128]{1,0:T(8,128)S(1)} %fusion), channel_id=1, source_target_pairs={{0,8},{2,10},{4,12},{6,14},{24,16},{26,18},{28,20},{30,22},{1,9},{... | collective-permute-start | bytes 847880 | tf_op jit(solution)/shard_map/ppermute | solution.py:80
  45.0 9.6 %collective-permute-start.16 = (f32[544,128]{1,0:T(8,128)S(1)}, f32[544,128]{1,0:T(8,128)S(1)}, u32[]{:S(2)}, u32[]{:S(2)}) collective-permute-start(f32[544,128]{1,0:T(8,128)S(1)} %slice_add_fusion.12), channel_id=1, source_target_pairs={{0,4},{2,6},{4,0},{6,2},{8,12},{10,14},{12,8},{14,10},{16,20},{18,... | collective-permute-start | bytes 835592 | tf_op jit(solution)/shard_map/ppermute | solution.py:80
  45.7 127.7 %slice-start = ((s8[8912896]{0:T(1024)(128)(4,1)}), s8[4194304]{0:T(1024)(128)(4,1)S(1)}, s32[]{:S(2)}) async-start(s8[8912896]{0:T(1024)(128)(4,1)} %bitcast.10), calls=%async_computation | async-start | bytes 8388608
  45.8 14.8 %collective-permute-start.6 = (f32[552,128]{1,0:T(8,128)S(1)}, f32[552,128]{1,0:T(8,128)S(1)}, u32[]{:S(2)}, u32[]{:S(2)}) collective-permute-start(f32[552,128]{1,0:T(8,128)S(1)} %get-tuple-element.161), channel_id=1, source_target_pairs={{0,4},{2,6},{4,0},{6,2},{8,12},{10,14},{12,8},{14,10},{16,20},{18,... | collective-permute-start | bytes 847880 | tf_op jit(solution)/shard_map/ppermute | solution.py:80
  54.6 12.0 %collective-permute-start.19 = (f32[544,128]{1,0:T(8,128)S(1)}, f32[544,128]{1,0:T(8,128)S(1)}, u32[]{:S(2)}, u32[]{:S(2)}) collective-permute-start(f32[544,128]{1,0:T(8,128)S(1)} %get-tuple-element.165), channel_id=1, source_target_pairs={{0,4},{2,6},{4,0},{6,2},{8,12},{10,14},{12,8},{14,10},{16,20},{18,... | collective-permute-start | bytes 835592 | tf_op jit(solution)/shard_map/ppermute | solution.py:80
  55.3 17.4 %collective-permute-start.10 = (f32[552,128]{1,0:T(8,128)S(1)}, f32[552,128]{1,0:T(8,128)S(1)}, u32[]{:S(2)}, u32[]{:S(2)}) collective-permute-start(f32[552,128]{1,0:T(8,128)S(1)} %get-tuple-element.159), channel_id=1, source_target_pairs={{0,4},{2,6},{4,0},{6,2},{8,12},{10,14},{12,8},{14,10},{16,20},{18,... | collective-permute-start | bytes 847880 | tf_op jit(solution)/shard_map/ppermute | solution.py:80
  60.6 7.4 %collective-permute-start.17 = (f32[544,128]{1,0:T(8,128)S(1)}, f32[544,128]{1,0:T(8,128)S(1)}, u32[]{:S(2)}, u32[]{:S(2)}) collective-permute-start(f32[544,128]{1,0:T(8,128)S(1)} %fusion.4), channel_id=1, source_target_pairs={{0,8},{2,10},{4,12},{6,14},{24,16},{26,18},{28,20},{30,22},{1,9},{... | collective-permute-start | bytes 835592 | tf_op jit(solution)/shard_map/ppermute | solution.py:80
  62.0 111.4 %copy-start.4 = (s32[136,128]{1,0:T(8,128)S(1)}, s32[136,128]{1,0:T(8,128)}, u32[]{:S(2)}) copy-start(s32[136,128]{1,0:T(8,128)} %get-tuple-element.81.position_ref) | copy-start | bytes 208900
  62.1 111.4 %copy-start.5 = (f32[3,2,1024]{2,1,0:T(2,128)S(1)}, f32[3,2,1024]{2,1,0:T(2,128)}, u32[]{:S(2)}) copy-start(f32[3,2,1024]{2,1,0:T(2,128)} %norm_ref.1) | copy-start | bytes 73732
  62.2 11.2 %collective-permute-start.7 = (f32[552,128]{1,0:T(8,128)S(1)}, f32[552,128]{1,0:T(8,128)S(1)}, u32[]{:S(2)}, u32[]{:S(2)}) collective-permute-start(f32[552,128]{1,0:T(8,128)S(1)} %get-tuple-element.157), channel_id=1, source_target_pairs={{8,16},{10,18},{12,20},{14,22},{16,8},{18,10},{20,12},{22,14},{9,1... | collective-permute-start | bytes 847880 | tf_op jit(solution)/shard_map/ppermute | solution.py:80
  66.6 7.4 %collective-permute-start.8 = (f32[552,128]{1,0:T(8,128)S(1)}, f32[552,128]{1,0:T(8,128)S(1)}, u32[]{:S(2)}, u32[]{:S(2)}) collective-permute-start(f32[552,128]{1,0:T(8,128)S(1)} %get-tuple-element.158), channel_id=1, source_target_pairs={{0,8},{2,10},{4,12},{6,14},{24,16},{26,18},{28,20},{30,22},{1,9},{... | collective-permute-start | bytes 847880 | tf_op jit(solution)/shard_map/ppermute | solution.py:80
  68.1 10.5 %collective-permute-start.23 = (f32[544,128]{1,0:T(8,128)S(1)}, f32[544,128]{1,0:T(8,128)S(1)}, u32[]{:S(2)}, u32[]{:S(2)}) collective-permute-start(f32[544,128]{1,0:T(8,128)S(1)} %get-tuple-element.163), channel_id=1, source_target_pairs={{0,4},{2,6},{4,0},{6,2},{8,12},{10,14},{12,8},{14,10},{16,20},{18,... | collective-permute-start | bytes 835592 | tf_op jit(solution)/shard_map/ppermute | solution.py:80
  72.6 15.5 %collective-permute-start.2 = (f32[552,128]{1,0:T(8,128)S(1)}, f32[552,128]{1,0:T(8,128)S(1)}, u32[]{:S(2)}, u32[]{:S(2)}) collective-permute-start(f32[552,128]{1,0:T(8,128)S(1)} %slice_add_fusion.5), channel_id=1, source_target_pairs={{0,4},{2,6},{4,0},{6,2},{8,12},{10,14},{12,8},{14,10},{16,20},{18,... | collective-permute-start | bytes 847880 | tf_op jit(solution)/shard_map/ppermute | solution.py:80
  73.3 6.1 %collective-permute-start.20 = (f32[544,128]{1,0:T(8,128)S(1)}, f32[544,128]{1,0:T(8,128)S(1)}, u32[]{:S(2)}, u32[]{:S(2)}) collective-permute-start(f32[544,128]{1,0:T(8,128)S(1)} %get-tuple-element.155), channel_id=1, source_target_pairs={{8,16},{10,18},{12,20},{14,22},{16,8},{18,10},{20,12},{22,14},{9,1... | collective-permute-start | bytes 835592 | tf_op jit(solution)/shard_map/ppermute | solution.py:80
  74.0 11.5 %collective-permute-start.21 = (f32[544,128]{1,0:T(8,128)S(1)}, f32[544,128]{1,0:T(8,128)S(1)}, u32[]{:S(2)}, u32[]{:S(2)}) collective-permute-start(f32[544,128]{1,0:T(8,128)S(1)} %get-tuple-element.156), channel_id=1, source_target_pairs={{0,8},{2,10},{4,12},{6,14},{24,16},{26,18},{28,20},{30,22},{1,9},{... | collective-permute-start | bytes 835592 | tf_op jit(solution)/shard_map/ppermute | solution.py:80
  78.5 12.9 %collective-permute-start.11 = (f32[552,128]{1,0:T(8,128)S(1)}, f32[552,128]{1,0:T(8,128)S(1)}, u32[]{:S(2)}, u32[]{:S(2)}) collective-permute-start(f32[552,128]{1,0:T(8,128)S(1)} %add_add_fusion), channel_id=1, source_target_pairs={{0,8},{2,10},{4,12},{6,14},{8,0},{10,2},{12,4},{14,6},{16,24},{18,... | collective-permute-start | bytes 847880 | tf_op jit(solution)/shard_map/ppermute | solution.py:80
  78.6 12.8 %collective-permute-start.12 = (f32[552,128]{1,0:T(8,128)S(1)}, f32[552,128]{1,0:T(8,128)S(1)}, u32[]{:S(2)}, u32[]{:S(2)}) collective-permute-start(f32[552,128]{1,0:T(8,128)S(1)} %add.137), channel_id=1, source_target_pairs={{8,16},{10,18},{12,20},{14,22},{16,8},{18,10},{20,12},{22,14},{9,1... | collective-permute-start | bytes 847880 | tf_op jit(solution)/shard_map/ppermute | solution.py:80
  79.4 12.2 %collective-permute-start.14 = (f32[544,128]{1,0:T(8,128)S(1)}, f32[544,128]{1,0:T(8,128)S(1)}, u32[]{:S(2)}, u32[]{:S(2)}) collective-permute-start(f32[544,128]{1,0:T(8,128)S(1)} %get-tuple-element.167), channel_id=1, source_target_pairs={{0,4},{2,6},{4,0},{6,2},{8,12},{10,14},{12,8},{14,10},{16,20},{18,... | collective-permute-start | bytes 835592 | tf_op jit(solution)/shard_map/ppermute | solution.py:80
  85.6 8.8 %collective-permute-start.24 = (f32[544,128]{1,0:T(8,128)S(1)}, f32[544,128]{1,0:T(8,128)S(1)}, u32[]{:S(2)}, u32[]{:S(2)}) collective-permute-start(f32[544,128]{1,0:T(8,128)S(1)} %add_add_fusion.1), channel_id=1, source_target_pairs={{0,8},{2,10},{4,12},{6,14},{8,0},{10,2},{12,4},{14,6},{16,24},{18,... | collective-permute-start | bytes 835592 | tf_op jit(solution)/shard_map/ppermute | solution.py:80
  88.1 6.3 %collective-permute-start.25 = (f32[544,128]{1,0:T(8,128)S(1)}, f32[544,128]{1,0:T(8,128)S(1)}, u32[]{:S(2)}, u32[]{:S(2)}) collective-permute-start(f32[544,128]{1,0:T(8,128)S(1)} %add.152), channel_id=1, source_target_pairs={{8,16},{10,18},{12,20},{14,22},{16,8},{18,10},{20,12},{22,14},{9,1... | collective-permute-start | bytes 835592 | tf_op jit(solution)/shard_map/ppermute | solution.py:80
  97.0 3.6 %collective-permute-start.26 = (f32[8,128]{1,0:T(8,128)S(1)}, f32[8,128]{1,0:T(8,128)S(1)}, u32[]{:S(2)}, u32[]{:S(2)}) collective-permute-start(f32[8,128]{1,0:T(8,128)S(1)} %get-tuple-element.125), channel_id=1, source_target_pairs={{0,1},{1,0},{2,3},{3,2},{4,5},{5,4},{6,7},{7,6},{8,9},{9,8},{10,11... | collective-permute-start | bytes 12296 | tf_op jit(solution)/shard_map/ppermute | solution.py:608
  100.6 6.6 %collective-permute-start.29 = (f32[552,128]{1,0:T(8,128)S(1)}, f32[552,128]{1,0:T(8,128)S(1)}, u32[]{:S(2)}, u32[]{:S(2)}) collective-permute-start(f32[552,128]{1,0:T(8,128)S(1)} %add_dynamic-update-slice_fusion.refs_0_), channel_id=1, source_target_pairs={{0,4},{2,6},{4,0},{6,2},{8,12},{10,14},{12,8},{14,10},{16,20},{18,... | collective-permute-start | bytes 847880 | tf_op jit(solution)/shard_map/ppermute | solution.py:80
  102.3 4.9 %collective-permute-start.28 = (f32[552,128]{1,0:T(8,128)S(1)}, f32[552,128]{1,0:T(8,128)S(1)}, u32[]{:S(2)}, u32[]{:S(2)}) collective-permute-start(f32[552,128]{1,0:T(8,128)S(1)} %add_dynamic-update-slice_fusion.refs_0_), channel_id=1, source_target_pairs={{8,16},{10,18},{12,20},{14,22},{16,8},{18,10},{20,12},{22,14},{9,1... | collective-permute-start | bytes 847880 | tf_op jit(solution)/shard_map/ppermute | solution.py:80
  103.0 9.0 %collective-permute-start.27 = (f32[552,128]{1,0:T(8,128)S(1)}, f32[552,128]{1,0:T(8,128)S(1)}, u32[]{:S(2)}, u32[]{:S(2)}) collective-permute-start(f32[552,128]{1,0:T(8,128)S(1)} %add_dynamic-update-slice_fusion.refs_0_), channel_id=1, source_target_pairs={{0,8},{2,10},{4,12},{6,14},{8,0},{10,2},{12,4},{14,6},{16,24},{18,... | collective-permute-start | bytes 847880 | tf_op jit(solution)/shard_map/ppermute | solution.py:80
  112.0 10.5 %collective-permute-start.33 = (f32[552,128]{1,0:T(8,128)S(1)}, f32[552,128]{1,0:T(8,128)S(1)}, u32[]{:S(2)}, u32[]{:S(2)}) collective-permute-start(f32[552,128]{1,0:T(8,128)S(1)} %collective-permute-done.28), channel_id=1, source_target_pairs={{8,0},{10,2},{12,4},{14,6},{16,24},{18,26},{20,28},{22,30},{9,1},{... | collective-permute-start | bytes 847880 | tf_op jit(solution)/shard_map/ppermute | solution.py:80
  113.3 10.7 %collective-permute-start.34 = (f32[552,128]{1,0:T(8,128)S(1)}, f32[552,128]{1,0:T(8,128)S(1)}, u32[]{:S(2)}, u32[]{:S(2)}) collective-permute-start(f32[552,128]{1,0:T(8,128)S(1)} %collective-permute-done.27.refs_4_), channel_id=1, source_target_pairs={{0,4},{2,6},{4,0},{6,2},{8,12},{10,14},{12,8},{14,10},{16,20},{18,... | collective-permute-start | bytes 847880 | tf_op jit(solution)/shard_map/ppermute | solution.py:80
  114.4 9.6 %collective-permute-start.32 = (f32[552,128]{1,0:T(8,128)S(1)}, f32[552,128]{1,0:T(8,128)S(1)}, u32[]{:S(2)}, u32[]{:S(2)}) collective-permute-start(f32[552,128]{1,0:T(8,128)S(1)} %collective-permute-done.27.refs_4_), channel_id=1, source_target_pairs={{8,16},{10,18},{12,20},{14,22},{16,8},{18,10},{20,12},{22,14},{9,1... | collective-permute-start | bytes 847880 | tf_op jit(solution)/shard_map/ppermute | solution.py:80
  115.1 10.7 %collective-permute-start.46 = (f32[544,128]{1,0:T(8,128)S(1)}, f32[544,128]{1,0:T(8,128)S(1)}, u32[]{:S(2)}, u32[]{:S(2)}) collective-permute-start(f32[544,128]{1,0:T(8,128)S(1)} %get-tuple-element.140.refs_16_), channel_id=1, source_target_pairs={{0,4},{2,6},{4,0},{6,2},{8,12},{10,14},{12,8},{14,10},{16,20},{18,... | collective-permute-start | bytes 835592 | tf_op jit(solution)/shard_map/ppermute | solution.py:80
  116.1 9.7 %collective-permute-start.45 = (f32[544,128]{1,0:T(8,128)S(1)}, f32[544,128]{1,0:T(8,128)S(1)}, u32[]{:S(2)}, u32[]{:S(2)}) collective-permute-start(f32[544,128]{1,0:T(8,128)S(1)} %get-tuple-element.140.refs_16_), channel_id=1, source_target_pairs={{8,16},{10,18},{12,20},{14,22},{16,8},{18,10},{20,12},{22,14},{9,1... | collective-permute-start | bytes 835592 | tf_op jit(solution)/shard_map/ppermute | solution.py:80
  122.5 7.4 %collective-permute-start.44 = (f32[544,128]{1,0:T(8,128)S(1)}, f32[544,128]{1,0:T(8,128)S(1)}, u32[]{:S(2)}, u32[]{:S(2)}) collective-permute-start(f32[544,128]{1,0:T(8,128)S(1)} %get-tuple-element.140.refs_16_), channel_id=1, source_target_pairs={{0,8},{2,10},{4,12},{6,14},{8,0},{10,2},{12,4},{14,6},{16,24},{18,... | collective-permute-start | bytes 835592 | tf_op jit(solution)/shard_map/ppermute | solution.py:80
  124.0 14.9 %collective-permute-start.38 = (f32[552,128]{1,0:T(8,128)S(1)}, f32[552,128]{1,0:T(8,128)S(1)}, u32[]{:S(2)}, u32[]{:S(2)}) collective-permute-start(f32[552,128]{1,0:T(8,128)S(1)} %add.155.refs_8_), channel_id=1, source_target_pairs={{0,4},{2,6},{4,0},{6,2},{8,12},{10,14},{12,8},{14,10},{16,20},{18,... | collective-permute-start | bytes 847880 | tf_op jit(solution)/shard_map/ppermute | solution.py:80
  129.9 8.4 %collective-permute-start.50 = (f32[544,128]{1,0:T(8,128)S(1)}, f32[544,128]{1,0:T(8,128)S(1)}, u32[]{:S(2)}, u32[]{:S(2)}) collective-permute-start(f32[544,128]{1,0:T(8,128)S(1)} %collective-permute-done.45), channel_id=1, source_target_pairs={{8,0},{10,2},{12,4},{14,6},{16,24},{18,26},{20,28},{22,30},{9,1},{... | collective-permute-start | bytes 835592 | tf_op jit(solution)/shard_map/ppermute | solution.py:80
  131.2 7.2 %collective-permute-start.51 = (f32[544,128]{1,0:T(8,128)S(1)}, f32[544,128]{1,0:T(8,128)S(1)}, u32[]{:S(2)}, u32[]{:S(2)}) collective-permute-start(f32[544,128]{1,0:T(8,128)S(1)} %collective-permute-done.44.refs_20_), channel_id=1, source_target_pairs={{0,4},{2,6},{4,0},{6,2},{8,12},{10,14},{12,8},{14,10},{16,20},{18,... | collective-permute-start | bytes 835592 | tf_op jit(solution)/shard_map/ppermute | solution.py:80
  133.8 8.5 %collective-permute-start.37 = (f32[552,128]{1,0:T(8,128)S(1)}, f32[552,128]{1,0:T(8,128)S(1)}, u32[]{:S(2)}, u32[]{:S(2)}) collective-permute-start(f32[552,128]{1,0:T(8,128)S(1)} %collective-permute-done.32), channel_id=1, source_target_pairs={{8,0},{10,2},{12,4},{14,6},{16,24},{18,26},{20,28},{22,30},{9,1},{... | collective-permute-start | bytes 847880 | tf_op jit(solution)/shard_map/ppermute | solution.py:80
  135.1 3.7 %collective-permute-start.49 = (f32[544,128]{1,0:T(8,128)S(1)}, f32[544,128]{1,0:T(8,128)S(1)}, u32[]{:S(2)}, u32[]{:S(2)}) collective-permute-start(f32[544,128]{1,0:T(8,128)S(1)} %collective-permute-done.44.refs_20_), channel_id=1, source_target_pairs={{8,16},{10,18},{12,20},{14,22},{16,8},{18,10},{20,12},{22,14},{9,1... | collective-permute-start | bytes 835592 | tf_op jit(solution)/shard_map/ppermute | solution.py:80
  138.3 6.1 %collective-permute-start.30 = (f32[552,128]{1,0:T(8,128)S(1)}, f32[552,128]{1,0:T(8,128)S(1)}, u32[]{:S(2)}, u32[]{:S(2)}) collective-permute-start(f32[552,128]{1,0:T(8,128)S(1)} %add_dynamic-update-slice_fusion.refs_0_), channel_id=1, source_target_pairs={{0,2},{2,0},{4,6},{6,4},{8,10},{10,8},{12,14},{14,12},{16,18},{18,... | collective-permute-start | bytes 847880 | tf_op jit(solution)/shard_map/ppermute | solution.py:80
  138.3 6.3 %collective-permute-start.31 = (f32[552,128]{1,0:T(8,128)S(1)}, f32[552,128]{1,0:T(8,128)S(1)}, u32[]{:S(2)}, u32[]{:S(2)}) collective-permute-start(f32[552,128]{1,0:T(8,128)S(1)} %collective-permute-done.29.refs_1_), channel_id=1, source_target_pairs={{0,2},{2,0},{4,6},{6,4},{8,10},{10,8},{12,14},{14,12},{16,18},{18,... | collective-permute-start | bytes 847880 | tf_op jit(solution)/shard_map/ppermute | solution.py:80
  138.8 5.1 %collective-permute-start.47 = (f32[544,128]{1,0:T(8,128)S(1)}, f32[544,128]{1,0:T(8,128)S(1)}, u32[]{:S(2)}, u32[]{:S(2)}) collective-permute-start(f32[544,128]{1,0:T(8,128)S(1)} %get-tuple-element.140.refs_16_), channel_id=1, source_target_pairs={{0,2},{2,0},{4,6},{6,4},{8,10},{10,8},{12,14},{14,12},{16,18},{18,... | collective-permute-start | bytes 835592 | tf_op jit(solution)/shard_map/ppermute | solution.py:80
  138.9 5.1 %collective-permute-start.48 = (f32[544,128]{1,0:T(8,128)S(1)}, f32[544,128]{1,0:T(8,128)S(1)}, u32[]{:S(2)}, u32[]{:S(2)}) collective-permute-start(f32[544,128]{1,0:T(8,128)S(1)} %collective-permute-done.46.refs_17_), channel_id=1, source_target_pairs={{0,2},{2,0},{4,6},{6,4},{8,10},{10,8},{12,14},{14,12},{16,18},{18,... | collective-permute-start | bytes 835592 | tf_op jit(solution)/shard_map/ppermute | solution.py:80
  142.3 8.7 %collective-permute-start.55 = (f32[544,128]{1,0:T(8,128)S(1)}, f32[544,128]{1,0:T(8,128)S(1)}, u32[]{:S(2)}, u32[]{:S(2)}) collective-permute-start(f32[544,128]{1,0:T(8,128)S(1)} %add.157.refs_24_), channel_id=1, source_target_pairs={{0,4},{2,6},{4,0},{6,2},{8,12},{10,14},{12,8},{14,10},{16,20},{18,... | collective-permute-start | bytes 835592 | tf_op jit(solution)/shard_map/ppermute | solution.py:80
  143.9 18.7 %collective-permute-start.35 = (f32[552,128]{1,0:T(8,128)S(1)}, f32[552,128]{1,0:T(8,128)S(1)}, u32[]{:S(2)}, u32[]{:S(2)}) collective-permute-start(f32[552,128]{1,0:T(8,128)S(1)} %collective-permute-done.27.refs_4_), channel_id=1, source_target_pairs={{0,2},{2,0},{4,6},{6,4},{8,10},{10,8},{12,14},{14,12},{16,18},{18,... | collective-permute-start | bytes 847880 | tf_op jit(solution)/shard_map/ppermute | solution.py:80
  144.0 19.2 %collective-permute-start.39 = (f32[552,128]{1,0:T(8,128)S(1)}, f32[552,128]{1,0:T(8,128)S(1)}, u32[]{:S(2)}, u32[]{:S(2)}) collective-permute-start(f32[552,128]{1,0:T(8,128)S(1)} %add.156.refs_10_), channel_id=1, source_target_pairs={{0,4},{2,6},{4,0},{6,2},{8,12},{10,14},{12,8},{14,10},{16,20},{18,... | collective-permute-start | bytes 847880 | tf_op jit(solution)/shard_map/ppermute | solution.py:80
  144.5 18.8 %collective-permute-start.36 = (f32[552,128]{1,0:T(8,128)S(1)}, f32[552,128]{1,0:T(8,128)S(1)}, u32[]{:S(2)}, u32[]{:S(2)}) collective-permute-start(f32[552,128]{1,0:T(8,128)S(1)} %collective-permute-done.34.refs_5_), channel_id=1, source_target_pairs={{0,2},{2,0},{4,6},{6,4},{8,10},{10,8},{12,14},{14,12},{16,18},{18,... | collective-permute-start | bytes 847880 | tf_op jit(solution)/shard_map/ppermute | solution.py:80
  144.7 7.8 %collective-permute-start.52 = (f32[544,128]{1,0:T(8,128)S(1)}, f32[544,128]{1,0:T(8,128)S(1)}, u32[]{:S(2)}, u32[]{:S(2)}) collective-permute-start(f32[544,128]{1,0:T(8,128)S(1)} %collective-permute-done.44.refs_20_), channel_id=1, source_target_pairs={{0,2},{2,0},{4,6},{6,4},{8,10},{10,8},{12,14},{14,12},{16,18},{18,... | collective-permute-start | bytes 835592 | tf_op jit(solution)/shard_map/ppermute | solution.py:80
  151.0 11.6 %collective-permute-start.54 = (f32[544,128]{1,0:T(8,128)S(1)}, f32[544,128]{1,0:T(8,128)S(1)}, u32[]{:S(2)}, u32[]{:S(2)}) collective-permute-start(f32[544,128]{1,0:T(8,128)S(1)} %collective-permute-done.49), channel_id=1, source_target_pairs={{8,0},{10,2},{12,4},{14,6},{16,24},{18,26},{20,28},{22,30},{9,1},{... | collective-permute-start | bytes 835592 | tf_op jit(solution)/shard_map/ppermute | solution.py:80
  152.5 19.8 %collective-permute-start.42 = (f32[552,128]{1,0:T(8,128)S(1)}, f32[552,128]{1,0:T(8,128)S(1)}, u32[]{:S(2)}, u32[]{:S(2)}) collective-permute-start(f32[552,128]{1,0:T(8,128)S(1)} %add.156.refs_10_), channel_id=1, source_target_pairs={{0,2},{2,0},{4,6},{6,4},{8,10},{10,8},{12,14},{14,12},{16,18},{18,... | collective-permute-start | bytes 847880 | tf_op jit(solution)/shard_map/ppermute | solution.py:80
  162.6 10.2 %collective-permute-start.40 = (f32[552,128]{1,0:T(8,128)S(1)}, f32[552,128]{1,0:T(8,128)S(1)}, u32[]{:S(2)}, u32[]{:S(2)}) collective-permute-start(f32[552,128]{1,0:T(8,128)S(1)} %add.155.refs_8_), channel_id=1, source_target_pairs={{0,2},{2,0},{4,6},{6,4},{8,10},{10,8},{12,14},{14,12},{16,18},{18,... | collective-permute-start | bytes 847880 | tf_op jit(solution)/shard_map/ppermute | solution.py:80
  162.7 10.3 %collective-permute-start.41 = (f32[552,128]{1,0:T(8,128)S(1)}, f32[552,128]{1,0:T(8,128)S(1)}, u32[]{:S(2)}, u32[]{:S(2)}) collective-permute-start(f32[552,128]{1,0:T(8,128)S(1)} %collective-permute-done.38.refs_9_), channel_id=1, source_target_pairs={{0,2},{2,0},{4,6},{6,4},{8,10},{10,8},{12,14},{14,12},{16,18},{18,... | collective-permute-start | bytes 847880 | tf_op jit(solution)/shard_map/ppermute | solution.py:80
  163.2 10.2 %collective-permute-start.43 = (f32[552,128]{1,0:T(8,128)S(1)}, f32[552,128]{1,0:T(8,128)S(1)}, u32[]{:S(2)}, u32[]{:S(2)}) collective-permute-start(f32[552,128]{1,0:T(8,128)S(1)} %collective-permute-done.39.refs_11_), channel_id=1, source_target_pairs={{0,2},{2,0},{4,6},{6,4},{8,10},{10,8},{12,14},{14,12},{16,18},{18,... | collective-permute-start | bytes 847880 | tf_op jit(solution)/shard_map/ppermute | solution.py:80
  163.3 9.1 %collective-permute-start.56 = (f32[544,128]{1,0:T(8,128)S(1)}, f32[544,128]{1,0:T(8,128)S(1)}, u32[]{:S(2)}, u32[]{:S(2)}) collective-permute-start(f32[544,128]{1,0:T(8,128)S(1)} %add.158.refs_26_), channel_id=1, source_target_pairs={{0,4},{2,6},{4,0},{6,2},{8,12},{10,14},{12,8},{14,10},{16,20},{18,... | collective-permute-start | bytes 835592 | tf_op jit(solution)/shard_map/ppermute | solution.py:80
  172.3 16.5 %collective-permute-start.53 = (f32[544,128]{1,0:T(8,128)S(1)}, f32[544,128]{1,0:T(8,128)S(1)}, u32[]{:S(2)}, u32[]{:S(2)}) collective-permute-start(f32[544,128]{1,0:T(8,128)S(1)} %collective-permute-done.51.refs_21_), channel_id=1, source_target_pairs={{0,2},{2,0},{4,6},{6,4},{8,10},{10,8},{12,14},{14,12},{16,18},{18,... | collective-permute-start | bytes 835592 | tf_op jit(solution)/shard_map/ppermute | solution.py:80
  172.4 16.5 %collective-permute-start.59 = (f32[544,128]{1,0:T(8,128)S(1)}, f32[544,128]{1,0:T(8,128)S(1)}, u32[]{:S(2)}, u32[]{:S(2)}) collective-permute-start(f32[544,128]{1,0:T(8,128)S(1)} %add.158.refs_26_), channel_id=1, source_target_pairs={{0,2},{2,0},{4,6},{6,4},{8,10},{10,8},{12,14},{14,12},{16,18},{18,... | collective-permute-start | bytes 835592 | tf_op jit(solution)/shard_map/ppermute | solution.py:80
  172.9 16.0 %collective-permute-start.57 = (f32[544,128]{1,0:T(8,128)S(1)}, f32[544,128]{1,0:T(8,128)S(1)}, u32[]{:S(2)}, u32[]{:S(2)}) collective-permute-start(f32[544,128]{1,0:T(8,128)S(1)} %add.157.refs_24_), channel_id=1, source_target_pairs={{0,2},{2,0},{4,6},{6,4},{8,10},{10,8},{12,14},{14,12},{16,18},{18,... | collective-permute-start | bytes 835592 | tf_op jit(solution)/shard_map/ppermute | solution.py:80
  172.9 15.9 %collective-permute-start.58 = (f32[544,128]{1,0:T(8,128)S(1)}, f32[544,128]{1,0:T(8,128)S(1)}, u32[]{:S(2)}, u32[]{:S(2)}) collective-permute-start(f32[544,128]{1,0:T(8,128)S(1)} %collective-permute-done.55.refs_25_), channel_id=1, source_target_pairs={{0,2},{2,0},{4,6},{6,4},{8,10},{10,8},{12,14},{14,12},{16,18},{18,... | collective-permute-start | bytes 835592 | tf_op jit(solution)/shard_map/ppermute | solution.py:80
  173.4 15.5 %collective-permute-start.60 = (f32[544,128]{1,0:T(8,128)S(1)}, f32[544,128]{1,0:T(8,128)S(1)}, u32[]{:S(2)}, u32[]{:S(2)}) collective-permute-start(f32[544,128]{1,0:T(8,128)S(1)} %collective-permute-done.56.refs_27_), channel_id=1, source_target_pairs={{0,2},{2,0},{4,6},{6,4},{8,10},{10,8},{12,14},{14,12},{16,18},{18,... | collective-permute-start | bytes 835592 | tf_op jit(solution)/shard_map/ppermute | solution.py:80
  (15 other events, 706.1 us)

commit v7 on v5

--- a/solution.py
+++ b/solution.py
@@ -23,6 +23,8 @@
 decay_rate = 0.01
 matrices = 5
 MIB = 1 << 20
+TILES = 4
+PHASES = 4
 
 
 def matrix_bounds(narrow):
@@ -134,7 +136,8 @@
     def swapped(*far_zs):
         for far_z in far_zs:
             for far_x in range(plan.nx):
-                found[far_z, far_x, 1] = plan.swap(found[far_z, far_x, 0])
+                if (far_z, far_x, 1) not in found:
+                    found[far_z, far_x, 1] = plan.swap(found[far_z, far_x, 0])
 
     if plan.nz != 4:
         for far_z, value in enumerate(line_gather(plan, "z", plan.nz, block)):
@@ -143,7 +146,8 @@
         return list(found.items())
     line = along_x(block)
     pair = plan.send(block, "z", PAIRS)
-    three = plan.send(block, "z", MIDDLE)
+    found[0, 0, 1], same = together(plan.swap(block), block)
+    three = plan.send(same, "z", MIDDLE)
     pair, three, *line = together(pair, three, *line)
     add(0, line)
     line = along_x(pair)
@@ -192,6 +196,7 @@
     row_in = lax.broadcasted_iota(jnp.int32, (lists, lists), 1)
     above = (row_in < row_out).astype(jnp.bfloat16)
     result = jnp.zeros((lists, LANE), jnp.int32)
+    ranks = jnp.full((lists, LANE), plan.own, jnp.int32)
     for z in range(plan.nz):
         for x in range(plan.nx):
             for c in range(2):
@@ -210,25 +215,39 @@
                 tail = jnp.concatenate(tail, 0)[: plan.tail]
                 moved[pl.ds(pl.multiple_of(start + plan.own, 8), plan.tail), :] = tail
                 result = jnp.where(mine, rank + start, result)
+                ranks = jnp.where(mine, rank, ranks)
     position_ref[...] = result
     to_scalar = pltpu.make_async_copy(position_ref, position, sem_position)
     to_scalar.start()
     to_scalar.wait()
     fetch.wait()
 
-    @pl.loop(0, plan.blocks // LANE)
-    def _(line):
-        for part in range(0, LANE, 16):
-            rows = raw[pl.ds(pl.multiple_of(line * LANE + part, 16), 16), :].astype(jnp.float32)
-            for u in range(16):
-                moved[pl.ds(position[line, part + u], 1), :] = rows[u : u + 1, :]
-
+    line_of = lax.broadcasted_iota(jnp.int32, (lists, LANE), 0)
+    cuts = [plan.own * (i + 1) // (8 * PHASES) * 8 for i in range(PHASES - 1)] + [plan.own]
+    begin = jnp.int32(0)
     copies = []
-    for i, out in enumerate(out_refs):
-        start = (i // plan.nz) * plan.half + (plan.nz - 1 - i % plan.nz) * plan.group
-        copies.append(pltpu.make_async_copy(moved.at[pl.ds(start, plan.group)], out, sem_out.at[i]))
-    for copy in copies:
-        copy.start()
+    for phase, cut in enumerate(cuts):
+        end = plan.blocks // LANE
+        if phase < PHASES - 1:
+            end = jnp.max(jnp.where(ranks < cut, line_of + 1, 0))
+
+        @pl.loop(begin, end)
+        def _(line):
+            for part in range(0, LANE, 16):
+                rows = raw[pl.ds(pl.multiple_of(line * LANE + part, 16), 16), :].astype(jnp.float32)
+                for u in range(16):
+                    moved[pl.ds(position[line, part + u], 1), :] = rows[u : u + 1, :]
+
+        begin = end
+        low = cuts[phase - 1] if phase else 0
+        high = cut if phase < PHASES - 1 else plan.block
+        for i, out in enumerate(out_refs):
+            start = (i // plan.nz) * plan.half + (plan.nz - 1 - i % plan.nz) * plan.group
+            for x in range(plan.nx):
+                rows = pl.ds(x * plan.block + low, high - low)
+                source = moved.at[pl.ds(start + x * plan.block + low, high - low)]
+                copies.append(pltpu.make_async_copy(source, out.at[rows], sem_out.at[len(copies)]))
+                copies[-1].start()
     for copy in copies:
         copy.wait()
 
@@ -252,7 +271,7 @@
             pltpu.SMEM((plan.lists, LANE), jnp.int32),
             pltpu.SemaphoreType.DMA,
             pltpu.SemaphoreType.DMA,
-            pltpu.SemaphoreType.DMA((len(shapes),)),
+            pltpu.SemaphoreType.DMA((len(shapes) * plan.nx * PHASES,)),
         ],
         compiler_params=pltpu.CompilerParams(vmem_limit_bytes=58 * MIB),
         name="place_gradients",
@@ -431,14 +450,14 @@
                 for row in range(each):
                     new_norm_ref[j, i : i + 1, row * LANE : (row + 1) * LANE] = value[row : row + 1, :]
 
-    matrix = jnp.int32(0)
-    for bound in plan.bounds:
-        matrix = matrix + (now * tile >= bound).astype(jnp.int32)
-    rate = jnp.broadcast_to(rates[pl.ds(matrix, 1), :], (8, LANE))
     lines = tile // LANE
 
     @pl.loop(0, lines)
     def _(line):
+        matrix = jnp.int32(0)
+        for bound in plan.bounds:
+            matrix = matrix + (now * lines + line >= bound // LANE).astype(jnp.int32)
+        rate = jnp.broadcast_to(rates[pl.ds(matrix, 1), :], (8, LANE))
         for group in range(0, LANE, 8):
             rows = [held[pl.ds(position_ref[now * lines + line, group + u], 1), :] for u in range(8)]
             here = pl.ds(pl.multiple_of(line * LANE + group, 8), 8)
@@ -448,9 +467,8 @@
 
 
 def finish(plan, my_place, position, norm_state, weights, pieces, slots):
-    tile = LANE
-    while tile < 1024 and all(b % (2 * tile) == 0 for b in plan.bounds + (plan.blocks,)):
-        tile *= 2
+    assert all(bound % LANE == 0 for bound in plan.bounds + (plan.blocks,))
+    tile = plan.blocks // next(n for n in (TILES, 4, 2, 1) if plan.blocks // LANE % n == 0)
     smem = pl.BlockSpec(memory_space=pltpu.SMEM)
     vmem = pl.BlockSpec(memory_space=pltpu.VMEM)
     return pl.pallas_call(

time: 185 us -> 189 us (1.022)
  waiting for transfers between devices: 85.4 us -> 93.5 us
  Pallas kernels: 58 us -> 55.5 us
    ppermute x30, waiting for transfers between devices: 83.3 us -> 91.4 us  [send(): return lax.ppermute(value, 'dp', every)]
where the time goes in v7:
time: 189 us
  waiting for transfers between devices  93.5 us (49%)
  Pallas kernels  55.5 us (29%)
  starting transfers between devices  35.4 us (19%)
  other arithmetic  2.65 us (1%)
    ppermute x30, waiting for transfers between devices, send(): return lax.ppermute(value, 'dp', every)  91.4 us
    ppermute x30, starting transfers between devices, send(): return lax.ppermute(value, 'dp', every)  33.9 us
    pallas_call x1, Pallas kernels, finish(): pl.pallas_call(functools.partial(finish_kernel, plan, tile, slots), grid=...  23.3 us
    pallas_call x1, Pallas kernels, place(): pl.pallas_call(functools.partial(place_kernel, plan), out_shape=[jax.Shap...  23.2 us
    pallas_call x1, Pallas kernels, owned(): pl.pallas_call(functools.partial(owned_kernel, plan), out_shape=[jax.Shap...  6.31 us
  transfers between devices with their start and end apart: 31, of which 16 were waited for; matrix products, arithmetic and copies ran while one was open for 0% of the time, Pallas kernels for 3%

profile of v7, /device:TPU:0, one launch (start us, length us, event | category | flops | bytes accessed | tf_op | source)
XLA Modules:
  0.0 189.0 jit_solution(3478529756073207454)
XLA Ops:
  0.7 0.6 pad_add_fusion.place_ref
  1.3 23.2 %place_gradients.1 = (f32[2192,128]{1,0:T(8,128)}, f32[2192,128]{1,0:T(8,128)}, f32[2192,128]{1,0:T(8,128)}, f32[2192,128]{1,0:T(8,128)}, f32[2192,128]{1,0:T(8,...) custom-call(s32[3]{0:T(128)} %pad_add_fusion.place_ref, ...), custom_call_target="tpu_custom_call" | custom-call | tf_op jit(solution)/shard_map/place_gradients/pallas_call | solution.py:257
  24.5 0.5 collective-permute-start
  25.0 2.6 %collective-permute-done = f32[2192,128]{1,0:T(8,128)S(1)} collective-permute-done((f32[2192,128]{1,0:T(8,128)}, f32[2192,128]{1,0:T(8,128)S(1)}, u32[]{:S(2)}, u32[]{:S(2)}) %collective-permute-start) | collective-permute-done | bytes 1122336 | tf_op jit(solution)/shard_map/ppermute | solution.py:74
  27.6 1.1 slice_add_fusion.7
  28.7 0.4 collective-permute-start.5
  29.2 2.6 %collective-permute-start.3 = (f32[1096,128]{1,0:T(8,128)S(1)}, f32[1096,128]{1,0:T(8,128)S(1)}, u32[]{:S(2)}, u32[]{:S(2)}) collective-permute-start(f32[1096,128]{1,0:T(8,128)S(1)} %slice_add_fusion.7), channel_id=1, source_target_pairs={{0,4},{2,6},{4,0},{6,2},{8,12},{10,14},{12,8},{14,10},{16,20},{18,... | collective-permute-start | bytes 1683464 | tf_op jit(solution)/shard_map/ppermute | solution.py:74
  31.8 0.1 collective-permute-start.9
  31.9 13.2 %collective-permute-done.3 = f32[1096,128]{1,0:T(8,128)S(1)} collective-permute-done((f32[1096,128]{1,0:T(8,128)S(1)}, f32[1096,128]{1,0:T(8,128)S(1)}, u32[]{:S(2)}, u32[]{:S(2)}) %collective-permute-start.3) | collective-permute-done | bytes 561184 | tf_op jit(solution)/shard_map/ppermute | solution.py:74
  45.0 0.1 fusion
  45.1 3.8 %collective-permute-start.4 = (f32[1096,128]{1,0:T(8,128)S(1)}, f32[1096,128]{1,0:T(8,128)S(1)}, u32[]{:S(2)}, u32[]{:S(2)}) collective-permute-start(f32[1096,128]{1,0:T(8,128)S(1)} %fusion), channel_id=1, source_target_pairs={{0,8},{2,10},{4,12},{6,14},{24,16},{26,18},{28,20},{30,22},{1,9},{... | collective-permute-start | bytes 1683464 | tf_op jit(solution)/shard_map/ppermute | solution.py:74
  48.9 0.1 slice_add_fusion.2
  49.1 1.6 collective-permute-start.6
  50.6 6.3 %owned_weights.1 = (f32[1088,128]{1,0:T(8,128)}, s32[1152,128]{1,0:T(8,128)}) custom-call(s32[3]{0:T(128)} %pad_add_fusion.place_ref, s32[136,128]{1,0:T(8,128)} %bitcast.14, f32[17408,128]{1,0:T(8,128)} %weights_ref.3), custom_call_target="tpu_custom_call" | custom-call | bytes 20971520 | tf_op jit(solution)/shard_map/owned_weights/pallas_call | solution.py:335
  57.0 0.1 collective-permute-start.1
  57.1 0.0 collective-permute-done.9
  57.1 0.1 slice_add_fusion
  57.2 0.7 collective-permute-start.10
  57.9 2.7 %collective-permute-done.4 = f32[1096,128]{1,0:T(8,128)S(1)} collective-permute-done((f32[1096,128]{1,0:T(8,128)S(1)}, f32[1096,128]{1,0:T(8,128)S(1)}, u32[]{:S(2)}, u32[]{:S(2)}) %collective-permute-start.4) | collective-permute-done | bytes 561184 | tf_op jit(solution)/shard_map/ppermute | solution.py:74
  60.6 4.3 %collective-permute-done.6 = f32[1096,128]{1,0:T(8,128)S(1)} collective-permute-done((f32[1096,128]{1,0:T(8,128)S(1)}, f32[1096,128]{1,0:T(8,128)S(1)}, u32[]{:S(2)}, u32[]{:S(2)}) %collective-permute-start.6) | collective-permute-done | bytes 561184 | tf_op jit(solution)/shard_map/ppermute | solution.py:74
  64.8 0.1 fusion.1
  64.9 0.8 collective-permute-start.7
  65.7 4.1 %collective-permute-start.8 = (f32[1096,128]{1,0:T(8,128)S(1)}, f32[1096,128]{1,0:T(8,128)S(1)}, u32[]{:S(2)}, u32[]{:S(2)}) collective-permute-start(f32[1096,128]{1,0:T(8,128)S(1)} %get-tuple-element.94), channel_id=1, source_target_pairs={{0,8},{2,10},{4,12},{6,14},{24,16},{26,18},{28,20},{30,22},{1,9},{... | collective-permute-start | bytes 1683464 | tf_op jit(solution)/shard_map/ppermute | solution.py:74
  69.8 0.0 collective-permute-done.1
  69.8 0.1 slice_add_fusion.5
  70.0 1.6 collective-permute-start.2
  71.5 5.3 %collective-permute-done.10 = f32[1096,128]{1,0:T(8,128)S(1)} collective-permute-done((f32[1096,128]{1,0:T(8,128)S(1)}, f32[1096,128]{1,0:T(8,128)S(1)}, u32[]{:S(2)}, u32[]{:S(2)}) %collective-permute-start.10) | collective-permute-done | bytes 561184 | tf_op jit(solution)/shard_map/ppermute | solution.py:74
  76.8 3.0 %collective-permute-done.8 = f32[1096,128]{1,0:T(8,128)S(1)} collective-permute-done((f32[1096,128]{1,0:T(8,128)S(1)}, f32[1096,128]{1,0:T(8,128)S(1)}, u32[]{:S(2)}, u32[]{:S(2)}) %collective-permute-start.8) | collective-permute-done | bytes 561184 | tf_op jit(solution)/shard_map/ppermute | solution.py:74
  79.9 0.1 add_add_fusion
  80.0 0.0 copy-start
  80.0 0.0 copy-start.2
  80.0 0.1 add.78
  80.1 2.5 %collective-permute-start.11 = (f32[1096,128]{1,0:T(8,128)S(1)}, f32[1096,128]{1,0:T(8,128)S(1)}, u32[]{:S(2)}, u32[]{:S(2)}) collective-permute-start(f32[1096,128]{1,0:T(8,128)S(1)} %add_add_fusion), channel_id=1, source_target_pairs={{0,8},{2,10},{4,12},{6,14},{8,0},{10,2},{12,4},{14,6},{16,24},{18,... | collective-permute-start | bytes 1683464 | tf_op jit(solution)/shard_map/ppermute | solution.py:74
  82.6 0.7 collective-permute-start.12
  83.3 3.8 %collective-permute-done.2.refs_1_ = f32[1096,128]{1,0:T(8,128)S(1)} collective-permute-done((f32[1096,128]{1,0:T(8,128)S(1)}, f32[1096,128]{1,0:T(8,128)S(1)}, u32[]{:S(2)}, u32[]{:S(2)}) %collective-permute-start.2) | collective-permute-done | bytes 561184 | tf_op jit(solution)/shard_map/ppermute | solution.py:74
  87.1 4.1 %collective-permute-done.11.refs_2_ = f32[1096,128]{1,0:T(8,128)S(1)} collective-permute-done((f32[1096,128]{1,0:T(8,128)S(1)}, f32[1096,128]{1,0:T(8,128)S(1)}, u32[]{:S(2)}, u32[]{:S(2)}) %collective-permute-start.11) | collective-permute-done | bytes 561184 | tf_op jit(solution)/shard_map/ppermute | solution.py:74
  91.2 2.6 %moments.1 = (f32[1088,128]{1,0:T(8,128)}, f32[1088,128]{1,0:T(8,128)}, f32[1096,128]{1,0:T(8,128)S(1)}, f32[8,128]{1,0:T(8,128)S(1)}) custom-call(f32[1096,128]{1,0:T(8,128)S(1)} %get-tuple-element.100.refs_0_, f32[1096,128]{1,0:T(8,128)S(1)} %collective-permute-done.2.refs_1_, f32[1096,128]{1,0:T(8,128)S(1)} %collective-permute-done.11.refs_2_, ...), custom_call_target="tpu_custom_call" | custom-call | tf_op jit(solution)/shard_map/moments/pallas_call | solution.py:390
  93.8 1.5 collective-permute-start.13
  95.4 2.1 %collective-permute-done.13 = f32[8,128]{1,0:T(8,128)S(1)} collective-permute-done((f32[8,128]{1,0:T(8,128)S(1)}, f32[8,128]{1,0:T(8,128)S(1)}, u32[]{:S(2)}, u32[]{:S(2)}) %collective-permute-start.13) | collective-permute-done | bytes 4128 | tf_op jit(solution)/shard_map/ppermute | solution.py:530
  97.5 1.6 collective-permute-start.17
  99.0 3.7 %collective-permute-start.15 = (f32[1096,128]{1,0:T(8,128)S(1)}, f32[1096,128]{1,0:T(8,128)S(1)}, u32[]{:S(2)}, u32[]{:S(2)}) collective-permute-start(f32[1096,128]{1,0:T(8,128)S(1)} %add_dynamic-update-slice_fusion.refs_1_), channel_id=1, source_target_pairs={{0,8},{2,10},{4,12},{6,14},{8,0},{10,2},{12,4},{14,6},{16,24},{18,... | collective-permute-start | bytes 1683464 | tf_op jit(solution)/shard_map/ppermute | solution.py:74
  102.7 0.7 collective-permute-start.16
  103.4 9.1 %collective-permute-done.17.refs_2_ = f32[1096,128]{1,0:T(8,128)S(1)} collective-permute-done((f32[1096,128]{1,0:T(8,128)S(1)}, f32[1096,128]{1,0:T(8,128)S(1)}, u32[]{:S(2)}, u32[]{:S(2)}) %collective-permute-start.17) | collective-permute-done | bytes 561184 | tf_op jit(solution)/shard_map/ppermute | solution.py:74
  112.6 3.2 %collective-permute-done.15.refs_4_ = f32[1096,128]{1,0:T(8,128)S(1)} collective-permute-done((f32[1096,128]{1,0:T(8,128)S(1)}, f32[1096,128]{1,0:T(8,128)S(1)}, u32[]{:S(2)}, u32[]{:S(2)}) %collective-permute-start.15) | collective-permute-done | bytes 561184 | tf_op jit(solution)/shard_map/ppermute | solution.py:74
  115.8 1.3 collective-permute-start.20
  117.1 0.6 collective-permute-start.21
  117.7 0.7 collective-permute-start.19
  118.4 14.9 %collective-permute-done.20 = f32[1096,128]{1,0:T(8,128)S(1)} collective-permute-done((f32[1096,128]{1,0:T(8,128)S(1)}, f32[1096,128]{1,0:T(8,128)S(1)}, u32[]{:S(2)}, u32[]{:S(2)}) %collective-permute-start.20) | collective-permute-done | bytes 561184 | tf_op jit(solution)/shard_map/ppermute | solution.py:74
  133.2 0.1 add.81.refs_8_
  133.3 1.6 collective-permute-start.25
  134.9 1.3 collective-permute-start.24
  136.2 0.1 collective-permute-start.18
  136.2 0.5 collective-permute-start.22
  136.7 9.9 %collective-permute-done.25.refs_9_ = f32[1096,128]{1,0:T(8,128)S(1)} collective-permute-done((f32[1096,128]{1,0:T(8,128)S(1)}, f32[1096,128]{1,0:T(8,128)S(1)}, u32[]{:S(2)}, u32[]{:S(2)}) %collective-permute-start.25) | collective-permute-done | bytes 561184 | tf_op jit(solution)/shard_map/ppermute | solution.py:74
  146.7 4.1 %collective-permute-done.24 = f32[1096,128]{1,0:T(8,128)S(1)} collective-permute-done((f32[1096,128]{1,0:T(8,128)S(1)}, f32[1096,128]{1,0:T(8,128)S(1)}, u32[]{:S(2)}, u32[]{:S(2)}) %collective-permute-start.24) | collective-permute-done | bytes 561184 | tf_op jit(solution)/shard_map/ppermute | solution.py:74
  150.8 0.1 add.82.refs_10_
  151.0 1.6 collective-permute-start.26
  152.5 0.5 collective-permute-start.29
  153.0 0.1 collective-permute-start.27
  153.1 0.4 collective-permute-start.28
  153.5 9.3 %collective-permute-done.26.refs_11_ = f32[1096,128]{1,0:T(8,128)S(1)} collective-permute-done((f32[1096,128]{1,0:T(8,128)S(1)}, f32[1096,128]{1,0:T(8,128)S(1)}, u32[]{:S(2)}, u32[]{:S(2)}) %collective-permute-start.26) | collective-permute-done | bytes 561184 | tf_op jit(solution)/shard_map/ppermute | solution.py:74
  162.9 1.9 collective-permute-done.30.refs_15_
  164.8 0.8 copy-done.23
  165.7 23.3 %new_weights.1 = (f32[17408,128]{1,0:T(8,128)}, f32[3,2,1024]{2,1,0:T(2,128)}, f32[7]{0:T(128)}) custom-call(s32[3]{0:T(128)} %pad_add_fusion.place_ref, s32[136,128]{1,0:T(8,128)} %get-tuple-element.49.position_ref, f32[3,2,1024]{2,1,0:T(2,128)} %norm_ref.1, f32[17408,128]{1,0:T(8,128)} %weights_ref.3, f32[1096,128]{1,0:T(8,128)} %copy-done.11, ...), custom_call_target="tpu_custom_call" | custom-call | tf_op jit(solution)/shard_map/new_weights/pallas_call | solution.py:474
  (64 shorter events, 0.1 us)
Async XLA Ops:
  24.5 20.6 %copy-start.10 = (f32[2192,128]{1,0:T(8,128)S(1)}, f32[2192,128]{1,0:T(8,128)}, u32[]{:S(2)}) copy-start(f32[2192,128]{1,0:T(8,128)} %get-tuple-element.51) | copy-start | bytes 3366916
  24.5 3.1 %collective-permute-start = (f32[2192,128]{1,0:T(8,128)}, f32[2192,128]{1,0:T(8,128)S(1)}, u32[]{:S(2)}, u32[]{:S(2)}) collective-permute-start(f32[2192,128]{1,0:T(8,128)} %get-tuple-element.52), channel_id=1, source_target_pairs={{0,2},{2,0},{4,6},{6,4},{8,10},{10,8},{12,14},{14,12},{16,18},{18,... | collective-permute-start | bytes 3366920 | tf_op jit(solution)/shard_map/ppermute | solution.py:74
  28.7 20.2 %copy-start.9 = (f32[2192,128]{1,0:T(8,128)S(1)}, f32[2192,128]{1,0:T(8,128)}, u32[]{:S(2)}) copy-start(f32[2192,128]{1,0:T(8,128)} %get-tuple-element.58) | copy-start | bytes 3366916
  28.7 20.2 %collective-permute-start.5 = (f32[2192,128]{1,0:T(8,128)}, f32[2192,128]{1,0:T(8,128)S(1)}, u32[]{:S(2)}, u32[]{:S(2)}) collective-permute-start(f32[2192,128]{1,0:T(8,128)} %get-tuple-element.59), channel_id=1, source_target_pairs={{0,2},{2,0},{4,6},{6,4},{8,10},{10,8},{12,14},{14,12},{16,18},{18,... | collective-permute-start | bytes 3366920 | tf_op jit(solution)/shard_map/ppermute | solution.py:74
  29.2 15.9 %collective-permute-start.3 = (f32[1096,128]{1,0:T(8,128)S(1)}, f32[1096,128]{1,0:T(8,128)S(1)}, u32[]{:S(2)}, u32[]{:S(2)}) collective-permute-start(f32[1096,128]{1,0:T(8,128)S(1)} %slice_add_fusion.7), channel_id=1, source_target_pairs={{0,4},{2,6},{4,0},{6,2},{8,12},{10,14},{12,8},{14,10},{16,20},{18,... | collective-permute-start | bytes 1683464 | tf_op jit(solution)/shard_map/ppermute | solution.py:74
  31.8 25.3 %collective-permute-start.9 = (f32[2192,128]{1,0:T(8,128)}, f32[2192,128]{1,0:T(8,128)S(1)}, u32[]{:S(2)}, u32[]{:S(2)}) collective-permute-start(f32[2192,128]{1,0:T(8,128)} %get-tuple-element.66), channel_id=1, source_target_pairs={{0,2},{2,0},{4,6},{6,4},{8,10},{10,8},{12,14},{14,12},{16,18},{18,... | collective-permute-start | bytes 3366920 | tf_op jit(solution)/shard_map/ppermute | solution.py:74
  45.1 15.4 %collective-permute-start.4 = (f32[1096,128]{1,0:T(8,128)S(1)}, f32[1096,128]{1,0:T(8,128)S(1)}, u32[]{:S(2)}, u32[]{:S(2)}) collective-permute-start(f32[1096,128]{1,0:T(8,128)S(1)} %fusion), channel_id=1, source_target_pairs={{0,8},{2,10},{4,12},{6,14},{24,16},{26,18},{28,20},{30,22},{1,9},{... | collective-permute-start | bytes 1683464 | tf_op jit(solution)/shard_map/ppermute | solution.py:74
  49.1 7.9 %copy-start.24 = (f32[2192,128]{1,0:T(8,128)S(1)}, f32[2192,128]{1,0:T(8,128)}, u32[]{:S(2)}) copy-start(f32[2192,128]{1,0:T(8,128)} %get-tuple-element.56) | copy-start | bytes 3366916
  49.1 8.0 %copy-start.8 = (f32[2192,128]{1,0:T(8,128)S(1)}, f32[2192,128]{1,0:T(8,128)}, u32[]{:S(2)}) copy-start(f32[2192,128]{1,0:T(8,128)} %get-tuple-element.65) | copy-start | bytes 3366916
  49.1 15.7 %collective-permute-start.6 = (f32[1096,128]{1,0:T(8,128)S(1)}, f32[1096,128]{1,0:T(8,128)S(1)}, u32[]{:S(2)}, u32[]{:S(2)}) collective-permute-start(f32[1096,128]{1,0:T(8,128)S(1)} %get-tuple-element.97), channel_id=1, source_target_pairs={{0,4},{2,6},{4,0},{6,2},{8,12},{10,14},{12,8},{14,10},{16,20},{18,... | collective-permute-start | bytes 1683464 | tf_op jit(solution)/shard_map/ppermute | solution.py:74
  57.0 12.8 %collective-permute-start.1 = (f32[2192,128]{1,0:T(8,128)S(1)}, f32[2192,128]{1,0:T(8,128)S(1)}, u32[]{:S(2)}, u32[]{:S(2)}) collective-permute-start(f32[2192,128]{1,0:T(8,128)S(1)} %copy-done.24), channel_id=1, source_target_pairs={{0,2},{2,0},{4,6},{6,4},{8,10},{10,8},{12,14},{14,12},{16,18},{18,... | collective-permute-start | bytes 3366920 | tf_op jit(solution)/shard_map/ppermute | solution.py:74
  57.2 19.6 %collective-permute-start.10 = (f32[1096,128]{1,0:T(8,128)S(1)}, f32[1096,128]{1,0:T(8,128)S(1)}, u32[]{:S(2)}, u32[]{:S(2)}) collective-permute-start(f32[1096,128]{1,0:T(8,128)S(1)} %get-tuple-element.95), channel_id=1, source_target_pairs={{0,4},{2,6},{4,0},{6,2},{8,12},{10,14},{12,8},{14,10},{16,20},{18,... | collective-permute-start | bytes 1683464 | tf_op jit(solution)/shard_map/ppermute | solution.py:74
  64.8 5.0 %copy-start.7 = (f32[2192,128]{1,0:T(8,128)S(1)}, f32[2192,128]{1,0:T(8,128)}, u32[]{:S(2)}) copy-start(f32[2192,128]{1,0:T(8,128)} %get-tuple-element.50) | copy-start | bytes 3366916
  64.9 11.9 %collective-permute-start.7 = (f32[1096,128]{1,0:T(8,128)S(1)}, f32[1096,128]{1,0:T(8,128)S(1)}, u32[]{:S(2)}, u32[]{:S(2)}) collective-permute-start(f32[1096,128]{1,0:T(8,128)S(1)} %get-tuple-element.93), channel_id=1, source_target_pairs={{8,16},{10,18},{12,20},{14,22},{16,8},{18,10},{20,12},{22,14},{9,1... | collective-permute-start | bytes 1683464 | tf_op jit(solution)/shard_map/ppermute | solution.py:74
  65.7 14.1 %collective-permute-start.8 = (f32[1096,128]{1,0:T(8,128)S(1)}, f32[1096,128]{1,0:T(8,128)S(1)}, u32[]{:S(2)}, u32[]{:S(2)}) collective-permute-start(f32[1096,128]{1,0:T(8,128)S(1)} %get-tuple-element.94), channel_id=1, source_target_pairs={{0,8},{2,10},{4,12},{6,14},{24,16},{26,18},{28,20},{30,22},{1,9},{... | collective-permute-start | bytes 1683464 | tf_op jit(solution)/shard_map/ppermute | solution.py:74
  70.0 17.1 %collective-permute-start.2 = (f32[1096,128]{1,0:T(8,128)S(1)}, f32[1096,128]{1,0:T(8,128)S(1)}, u32[]{:S(2)}, u32[]{:S(2)}) collective-permute-start(f32[1096,128]{1,0:T(8,128)S(1)} %get-tuple-element.99), channel_id=1, source_target_pairs={{0,4},{2,6},{4,0},{6,2},{8,12},{10,14},{12,8},{14,10},{16,20},{18,... | collective-permute-start | bytes 1683464 | tf_op jit(solution)/shard_map/ppermute | solution.py:74
  79.9 11.3 %copy-start.3 = (f32[1,1088,128]{2,1,0:T(8,128)S(1)}, f32[1,1088,128]{2,1,0:T(8,128)}, u32[]{:S(2)}) copy-start(f32[1,1088,128]{2,1,0:T(8,128)} %param.10) | copy-start | bytes 1671172
  79.9 11.3 %copy-start.4 = (f32[1088,128]{1,0:T(8,128)S(1)}, f32[1088,128]{1,0:T(8,128)}, u32[]{:S(2)}) copy-start(f32[1088,128]{1,0:T(8,128)} %get-tuple-element.71.refs_6_) | copy-start | bytes 1671172
  80.0 11.2 %copy-start = (s32[1152,128]{1,0:T(8,128)S(1)}, s32[1152,128]{1,0:T(8,128)}, u32[]{:S(2)}) copy-start(s32[1152,128]{1,0:T(8,128)} %get-tuple-element.72.refs_7_) | copy-start | bytes 1769476
  80.0 11.2 %copy-start.2 = (f32[1,1088,128]{2,1,0:T(8,128)S(1)}, f32[1,1088,128]{2,1,0:T(8,128)}, u32[]{:S(2)}) copy-start(f32[1,1088,128]{2,1,0:T(8,128)} %param.9) | copy-start | bytes 1671172
  80.1 11.1 %collective-permute-start.11 = (f32[1096,128]{1,0:T(8,128)S(1)}, f32[1096,128]{1,0:T(8,128)S(1)}, u32[]{:S(2)}, u32[]{:S(2)}) collective-permute-start(f32[1096,128]{1,0:T(8,128)S(1)} %add_add_fusion), channel_id=1, source_target_pairs={{0,8},{2,10},{4,12},{6,14},{8,0},{10,2},{12,4},{14,6},{16,24},{18,... | collective-permute-start | bytes 1683464 | tf_op jit(solution)/shard_map/ppermute | solution.py:74
  82.6 8.5 %collective-permute-start.12 = (f32[1096,128]{1,0:T(8,128)S(1)}, f32[1096,128]{1,0:T(8,128)S(1)}, u32[]{:S(2)}, u32[]{:S(2)}) collective-permute-start(f32[1096,128]{1,0:T(8,128)S(1)} %add.78), channel_id=1, source_target_pairs={{8,16},{10,18},{12,20},{14,22},{16,8},{18,10},{20,12},{22,14},{9,1... | collective-permute-start | bytes 1683464 | tf_op jit(solution)/shard_map/ppermute | solution.py:74
  93.8 3.6 %collective-permute-start.13 = (f32[8,128]{1,0:T(8,128)S(1)}, f32[8,128]{1,0:T(8,128)S(1)}, u32[]{:S(2)}, u32[]{:S(2)}) collective-permute-start(f32[8,128]{1,0:T(8,128)S(1)} %get-tuple-element.74), channel_id=1, source_target_pairs={{0,1},{1,0},{2,3},{3,2},{4,5},{5,4},{6,7},{7,6},{8,9},{9,8},{10,11... | collective-permute-start | bytes 12296 | tf_op jit(solution)/shard_map/ppermute | solution.py:530
  97.5 53.5 %copy-start.1 = (f32[1096,128]{1,0:T(8,128)}, f32[1096,128]{1,0:T(8,128)S(1)}, u32[]{:S(2)}) copy-start(f32[1096,128]{1,0:T(8,128)S(1)} %add_dynamic-update-slice_fusion.refs_1_) | copy-start | bytes 1683460
  97.5 5.3 %collective-permute-start.14 = (f32[1096,128]{1,0:T(8,128)S(1)}, f32[1096,128]{1,0:T(8,128)S(1)}, u32[]{:S(2)}, u32[]{:S(2)}) collective-permute-start(f32[1096,128]{1,0:T(8,128)S(1)} %add_dynamic-update-slice_fusion.refs_1_), channel_id=1, source_target_pairs={{0,2},{2,0},{4,6},{6,4},{8,10},{10,8},{12,14},{14,12},{16,18},{18,... | collective-permute-start | bytes 1683464 | tf_op jit(solution)/shard_map/ppermute | solution.py:74
  97.5 15.1 %collective-permute-start.17 = (f32[1096,128]{1,0:T(8,128)S(1)}, f32[1096,128]{1,0:T(8,128)S(1)}, u32[]{:S(2)}, u32[]{:S(2)}) collective-permute-start(f32[1096,128]{1,0:T(8,128)S(1)} %add_dynamic-update-slice_fusion.refs_1_), channel_id=1, source_target_pairs={{0,4},{2,6},{4,0},{6,2},{8,12},{10,14},{12,8},{14,10},{16,20},{18,... | collective-permute-start | bytes 1683464 | tf_op jit(solution)/shard_map/ppermute | solution.py:74
  99.0 16.8 %collective-permute-start.15 = (f32[1096,128]{1,0:T(8,128)S(1)}, f32[1096,128]{1,0:T(8,128)S(1)}, u32[]{:S(2)}, u32[]{:S(2)}) collective-permute-start(f32[1096,128]{1,0:T(8,128)S(1)} %add_dynamic-update-slice_fusion.refs_1_), channel_id=1, source_target_pairs={{0,8},{2,10},{4,12},{6,14},{8,0},{10,2},{12,4},{14,6},{16,24},{18,... | collective-permute-start | bytes 1683464 | tf_op jit(solution)/shard_map/ppermute | solution.py:74
  102.7 48.2 %copy-start.11 = (f32[1096,128]{1,0:T(8,128)}, f32[1096,128]{1,0:T(8,128)S(1)}, u32[]{:S(2)}) copy-start(f32[1096,128]{1,0:T(8,128)S(1)} %collective-permute-done.14.refs_0_) | copy-start | bytes 1683460
  102.7 13.0 %collective-permute-start.16 = (f32[1096,128]{1,0:T(8,128)S(1)}, f32[1096,128]{1,0:T(8,128)S(1)}, u32[]{:S(2)}, u32[]{:S(2)}) collective-permute-start(f32[1096,128]{1,0:T(8,128)S(1)} %add_dynamic-update-slice_fusion.refs_1_), channel_id=1, source_target_pairs={{8,16},{10,18},{12,20},{14,22},{16,8},{18,10},{20,12},{22,14},{9,1... | collective-permute-start | bytes 1683464 | tf_op jit(solution)/shard_map/ppermute | solution.py:74
  112.6 38.3 %copy-start.12 = (f32[1096,128]{1,0:T(8,128)}, f32[1096,128]{1,0:T(8,128)S(1)}, u32[]{:S(2)}) copy-start(f32[1096,128]{1,0:T(8,128)S(1)} %collective-permute-done.17.refs_2_) | copy-start | bytes 1683460
  115.8 35.2 %copy-start.13 = (f32[1096,128]{1,0:T(8,128)}, f32[1096,128]{1,0:T(8,128)S(1)}, u32[]{:S(2)}) copy-start(f32[1096,128]{1,0:T(8,128)S(1)} %collective-permute-done.15.refs_4_) | copy-start | bytes 1683460
  115.8 17.5 %collective-permute-start.20 = (f32[1096,128]{1,0:T(8,128)S(1)}, f32[1096,128]{1,0:T(8,128)S(1)}, u32[]{:S(2)}, u32[]{:S(2)}) collective-permute-start(f32[1096,128]{1,0:T(8,128)S(1)} %collective-permute-done.16), channel_id=1, source_target_pairs={{8,0},{10,2},{12,4},{14,6},{16,24},{18,26},{20,28},{22,30},{9,1},{... | collective-permute-start | bytes 1683464 | tf_op jit(solution)/shard_map/ppermute | solution.py:74
  117.1 16.2 %collective-permute-start.21 = (f32[1096,128]{1,0:T(8,128)S(1)}, f32[1096,128]{1,0:T(8,128)S(1)}, u32[]{:S(2)}, u32[]{:S(2)}) collective-permute-start(f32[1096,128]{1,0:T(8,128)S(1)} %collective-permute-done.15.refs_4_), channel_id=1, source_target_pairs={{0,4},{2,6},{4,0},{6,2},{8,12},{10,14},{12,8},{14,10},{16,20},{18,... | collective-permute-start | bytes 1683464 | tf_op jit(solution)/shard_map/ppermute | solution.py:74
  117.7 15.6 %collective-permute-start.19 = (f32[1096,128]{1,0:T(8,128)S(1)}, f32[1096,128]{1,0:T(8,128)S(1)}, u32[]{:S(2)}, u32[]{:S(2)}) collective-permute-start(f32[1096,128]{1,0:T(8,128)S(1)} %collective-permute-done.15.refs_4_), channel_id=1, source_target_pairs={{8,16},{10,18},{12,20},{14,22},{16,8},{18,10},{20,12},{22,14},{9,1... | collective-permute-start | bytes 1683464 | tf_op jit(solution)/shard_map/ppermute | solution.py:74
  133.2 19.3 %copy-start.14 = (f32[1096,128]{1,0:T(8,128)}, f32[1096,128]{1,0:T(8,128)S(1)}, u32[]{:S(2)}) copy-start(f32[1096,128]{1,0:T(8,128)S(1)} %collective-permute-done.21.refs_5_) | copy-start | bytes 1683460
  133.3 32.3 %copy-start.5 = (f32[1096,128]{1,0:T(8,128)}, f32[1096,128]{1,0:T(8,128)S(1)}, u32[]{:S(2)}) copy-start(f32[1096,128]{1,0:T(8,128)S(1)} %add.81.refs_8_) | copy-start | bytes 1683460
  133.3 13.4 %collective-permute-start.25 = (f32[1096,128]{1,0:T(8,128)S(1)}, f32[1096,128]{1,0:T(8,128)S(1)}, u32[]{:S(2)}, u32[]{:S(2)}) collective-permute-start(f32[1096,128]{1,0:T(8,128)S(1)} %add.81.refs_8_), channel_id=1, source_target_pairs={{0,4},{2,6},{4,0},{6,2},{8,12},{10,14},{12,8},{14,10},{16,20},{18,... | collective-permute-start | bytes 1683464 | tf_op jit(solution)/shard_map/ppermute | solution.py:74
  134.9 16.0 %collective-permute-start.24 = (f32[1096,128]{1,0:T(8,128)S(1)}, f32[1096,128]{1,0:T(8,128)S(1)}, u32[]{:S(2)}, u32[]{:S(2)}) collective-permute-start(f32[1096,128]{1,0:T(8,128)S(1)} %collective-permute-done.19), channel_id=1, source_target_pairs={{8,0},{10,2},{12,4},{14,6},{16,24},{18,26},{20,28},{22,30},{9,1},{... | collective-permute-start | bytes 1683464 | tf_op jit(solution)/shard_map/ppermute | solution.py:74
  136.2 16.9 %collective-permute-start.18 = (f32[1096,128]{1,0:T(8,128)S(1)}, f32[1096,128]{1,0:T(8,128)S(1)}, u32[]{:S(2)}, u32[]{:S(2)}) collective-permute-start(f32[1096,128]{1,0:T(8,128)S(1)} %collective-permute-done.17.refs_2_), channel_id=1, source_target_pairs={{0,2},{2,0},{4,6},{6,4},{8,10},{10,8},{12,14},{14,12},{16,18},{18,... | collective-permute-start | bytes 1683464 | tf_op jit(solution)/shard_map/ppermute | solution.py:74
  136.2 16.9 %collective-permute-start.22 = (f32[1096,128]{1,0:T(8,128)S(1)}, f32[1096,128]{1,0:T(8,128)S(1)}, u32[]{:S(2)}, u32[]{:S(2)}) collective-permute-start(f32[1096,128]{1,0:T(8,128)S(1)} %collective-permute-done.15.refs_4_), channel_id=1, source_target_pairs={{0,2},{2,0},{4,6},{6,4},{8,10},{10,8},{12,14},{14,12},{16,18},{18,... | collective-permute-start | bytes 1683464 | tf_op jit(solution)/shard_map/ppermute | solution.py:74
  146.7 18.9 %copy-start.15 = (f32[1096,128]{1,0:T(8,128)}, f32[1096,128]{1,0:T(8,128)S(1)}, u32[]{:S(2)}) copy-start(f32[1096,128]{1,0:T(8,128)S(1)} %collective-permute-done.25.refs_9_) | copy-start | bytes 1683460
  150.9 14.7 %copy-start.6 = (f32[1096,128]{1,0:T(8,128)}, f32[1096,128]{1,0:T(8,128)S(1)}, u32[]{:S(2)}) copy-start(f32[1096,128]{1,0:T(8,128)S(1)} %add.82.refs_10_) | copy-start | bytes 1683460
  151.0 11.9 %collective-permute-start.26 = (f32[1096,128]{1,0:T(8,128)S(1)}, f32[1096,128]{1,0:T(8,128)S(1)}, u32[]{:S(2)}, u32[]{:S(2)}) collective-permute-start(f32[1096,128]{1,0:T(8,128)S(1)} %add.82.refs_10_), channel_id=1, source_target_pairs={{0,4},{2,6},{4,0},{6,2},{8,12},{10,14},{12,8},{14,10},{16,20},{18,... | collective-permute-start | bytes 1683464 | tf_op jit(solution)/shard_map/ppermute | solution.py:74
  152.5 10.3 %collective-permute-start.23 = (f32[1096,128]{1,0:T(8,128)S(1)}, f32[1096,128]{1,0:T(8,128)S(1)}, u32[]{:S(2)}, u32[]{:S(2)}) collective-permute-start(f32[1096,128]{1,0:T(8,128)S(1)} %collective-permute-done.21.refs_5_), channel_id=1, source_target_pairs={{0,2},{2,0},{4,6},{6,4},{8,10},{10,8},{12,14},{14,12},{16,18},{18,... | collective-permute-start | bytes 1683464 | tf_op jit(solution)/shard_map/ppermute | solution.py:74
  152.5 10.3 %collective-permute-start.29 = (f32[1096,128]{1,0:T(8,128)S(1)}, f32[1096,128]{1,0:T(8,128)S(1)}, u32[]{:S(2)}, u32[]{:S(2)}) collective-permute-start(f32[1096,128]{1,0:T(8,128)S(1)} %add.82.refs_10_), channel_id=1, source_target_pairs={{0,2},{2,0},{4,6},{6,4},{8,10},{10,8},{12,14},{14,12},{16,18},{18,... | collective-permute-start | bytes 1683464 | tf_op jit(solution)/shard_map/ppermute | solution.py:74
  153.0 12.6 %copy-start.16 = (f32[1096,128]{1,0:T(8,128)}, f32[1096,128]{1,0:T(8,128)S(1)}, u32[]{:S(2)}) copy-start(f32[1096,128]{1,0:T(8,128)S(1)} %collective-permute-done.18.refs_3_) | copy-start | bytes 1683460
  153.0 9.8 %collective-permute-start.27 = (f32[1096,128]{1,0:T(8,128)S(1)}, f32[1096,128]{1,0:T(8,128)S(1)}, u32[]{:S(2)}, u32[]{:S(2)}) collective-permute-start(f32[1096,128]{1,0:T(8,128)S(1)} %add.81.refs_8_), channel_id=1, source_target_pairs={{0,2},{2,0},{4,6},{6,4},{8,10},{10,8},{12,14},{14,12},{16,18},{18,... | collective-permute-start | bytes 1683464 | tf_op jit(solution)/shard_map/ppermute | solution.py:74
  153.1 12.5 %copy-start.17 = (f32[1096,128]{1,0:T(8,128)}, f32[1096,128]{1,0:T(8,128)S(1)}, u32[]{:S(2)}) copy-start(f32[1096,128]{1,0:T(8,128)S(1)} %collective-permute-done.22.refs_6_) | copy-start | bytes 1683460
  153.1 9.8 %collective-permute-start.28 = (f32[1096,128]{1,0:T(8,128)S(1)}, f32[1096,128]{1,0:T(8,128)S(1)}, u32[]{:S(2)}, u32[]{:S(2)}) collective-permute-start(f32[1096,128]{1,0:T(8,128)S(1)} %collective-permute-done.25.refs_9_), channel_id=1, source_target_pairs={{0,2},{2,0},{4,6},{6,4},{8,10},{10,8},{12,14},{14,12},{16,18},{18,... | collective-permute-start | bytes 1683464 | tf_op jit(solution)/shard_map/ppermute | solution.py:74
  162.8 2.8 %copy-start.18 = (f32[1096,128]{1,0:T(8,128)}, f32[1096,128]{1,0:T(8,128)S(1)}, u32[]{:S(2)}) copy-start(f32[1096,128]{1,0:T(8,128)S(1)} %collective-permute-done.26.refs_11_) | copy-start | bytes 1683460
  162.8 2.0 %collective-permute-start.30 = (f32[1096,128]{1,0:T(8,128)S(1)}, f32[1096,128]{1,0:T(8,128)S(1)}, u32[]{:S(2)}, u32[]{:S(2)}) collective-permute-start(f32[1096,128]{1,0:T(8,128)S(1)} %collective-permute-done.26.refs_11_), channel_id=1, source_target_pairs={{0,2},{2,0},{4,6},{6,4},{8,10},{10,8},{12,14},{14,12},{16,18},{18,... | collective-permute-start | bytes 1683464 | tf_op jit(solution)/shard_map/ppermute | solution.py:74
  162.8 2.8 %copy-start.19 = (f32[1096,128]{1,0:T(8,128)}, f32[1096,128]{1,0:T(8,128)S(1)}, u32[]{:S(2)}) copy-start(f32[1096,128]{1,0:T(8,128)S(1)} %collective-permute-done.23.refs_7_) | copy-start | bytes 1683460
  162.9 2.8 %copy-start.20 = (f32[1096,128]{1,0:T(8,128)}, f32[1096,128]{1,0:T(8,128)S(1)}, u32[]{:S(2)}) copy-start(f32[1096,128]{1,0:T(8,128)S(1)} %collective-permute-done.29.refs_14_) | copy-start | bytes 1683460
  162.9 2.8 %copy-start.21 = (f32[1096,128]{1,0:T(8,128)}, f32[1096,128]{1,0:T(8,128)S(1)}, u32[]{:S(2)}) copy-start(f32[1096,128]{1,0:T(8,128)S(1)} %collective-permute-done.27.refs_12_) | copy-start | bytes 1683460
  162.9 2.8 %copy-start.22 = (f32[1096,128]{1,0:T(8,128)}, f32[1096,128]{1,0:T(8,128)S(1)}, u32[]{:S(2)}) copy-start(f32[1096,128]{1,0:T(8,128)S(1)} %collective-permute-done.28.refs_13_) | copy-start | bytes 1683460
  164.8 0.8 copy-start.23

commit v8 on v7

--- a/solution.py
+++ b/solution.py
@@ -23,8 +23,8 @@
 decay_rate = 0.01
 matrices = 5
 MIB = 1 << 20
-TILES = 4
-PHASES = 4
+TILES = 8
+PHASES = 2
 
 
 def matrix_bounds(narrow):
@@ -110,15 +110,13 @@
     two = along_x(2, mine[2])
     near_three = sum(three[1:], three[0])
     in_three = plan.send(near_three, "z", INWARD)
-    in_three, *two = together(in_three, *two, *beside)
-    two, beside = two[: -len(beside)], two[-len(beside) :]
-    near_two = sum(two[1:], two[0])
+    in_three, near_two, *beside = together(in_three, sum(two[1:], two[0]), *beside)
     one = along_x(1, mine[1])
     across_two = plan.send(near_two + in_three, "z", MIDDLE)
     in_two = plan.send(near_two, "z", INWARD)
-    across_two, in_two, *one = together(across_two, in_two, *one)
+    across_two, in_two, near_one = together(across_two, in_two, sum(one[1:], one[0]))
     zero = along_x(0, mine[0])
-    pair = plan.send(sum(one[1:], one[0]) + across_two, "z", PAIRS)
+    pair = plan.send(near_one + across_two, "z", PAIRS)
     across_three = plan.send(near_three + in_two, "z", MIDDLE)
     return zero + [pair, across_three] + beside
 
@@ -146,8 +144,7 @@
         return list(found.items())
     line = along_x(block)
     pair = plan.send(block, "z", PAIRS)
-    found[0, 0, 1], same = together(plan.swap(block), block)
-    three = plan.send(same, "z", MIDDLE)
+    three = plan.send(block, "z", MIDDLE)
     pair, three, *line = together(pair, three, *line)
     add(0, line)
     line = along_x(pair)
@@ -188,26 +185,30 @@
     lists = plan.lists
     owners = owner_ref[...]
     my_z, my_x, my_c = place_ref[0], place_ref[1], place_ref[2]
+    count = plan.replicas
     lane_in = lax.broadcasted_iota(jnp.int32, (LANE, LANE), 0)
     lane_out = lax.broadcasted_iota(jnp.int32, (LANE, LANE), 1)
-    before = (lane_in < lane_out).astype(jnp.bfloat16)
-    every = jnp.ones((LANE, LANE), jnp.bfloat16)
+    before = (lane_in < lane_out).astype(jnp.float32).astype(jnp.bfloat16)
     row_out = lax.broadcasted_iota(jnp.int32, (lists, lists), 0)
     row_in = lax.broadcasted_iota(jnp.int32, (lists, lists), 1)
-    above = (row_in < row_out).astype(jnp.bfloat16)
+    above = (row_in < row_out).astype(jnp.float32).astype(jnp.bfloat16)
+    flags = [(owners == d).astype(jnp.float32).astype(jnp.bfloat16) for d in range(count)]
+    inner = jnp.dot(jnp.concatenate(flags, 0), before, preferred_element_type=jnp.float32)
+    owner_in = lax.broadcasted_iota(jnp.int32, (count * LANE, LANE), 0)
+    owner_out = lax.broadcasted_iota(jnp.int32, (count * LANE, LANE), 1)
+    pick = (owner_in // LANE == owner_out).astype(jnp.float32).astype(jnp.bfloat16)
+    totals = jnp.dot(jnp.concatenate(flags, 1), pick, preferred_element_type=jnp.float32)
+    outer = jnp.dot(above, totals.astype(jnp.bfloat16), preferred_element_type=jnp.float32)
+    ranks = jnp.full((lists, LANE), plan.own, jnp.int32)
     result = jnp.zeros((lists, LANE), jnp.int32)
-    ranks = jnp.full((lists, LANE), plan.own, jnp.int32)
     for z in range(plan.nz):
         for x in range(plan.nx):
             for c in range(2):
-                mine = owners == plan.index(z, x, c)
-                flags = mine.astype(jnp.float32).astype(jnp.bfloat16)
-                inner = jnp.dot(flags, before, preferred_element_type=jnp.float32)
-                totals = jnp.dot(flags, every, preferred_element_type=jnp.float32)
-                outer = jnp.dot(above, totals.astype(jnp.bfloat16), preferred_element_type=jnp.float32)
-                rank = (inner + outer).astype(jnp.int32)
+                d = plan.index(z, x, c)
+                mine = owners == d
+                rank = (inner[d * lists : (d + 1) * lists, :] + outer[:, d : d + 1]).astype(jnp.int32)
                 start = plan.start(my_z ^ z, my_x ^ x, my_c ^ c)
-                first_norm = plan.index(z, x, c) * plan.norm_each
+                first_norm = d * plan.norm_each
                 tail = [jnp.zeros((plan.tail, LANE), jnp.float32)]
                 for row in range(min(first_norm + plan.norm_each, plan.norm_rows) - 1, first_norm - 1, -1):
                     part = norm_ref[row * LANE // D : row * LANE // D + 1, row * LANE % D : row * LANE % D + LANE]
@@ -406,19 +407,13 @@
 
 def finish_kernel(plan, tile, slots, place_ref, position_ref, norm_ref, weights_ref, *refs):
     pieces, refs = refs[: len(slots)], refs[len(slots) :]
-    out_ref, new_norm_ref, trust_ref, held, norms, rates, sems = refs
+    out_ref, new_norm_ref, trust_ref, held, norms, rates = refs
     now = pl.program_id(0)
 
     @pl.when(now == 0)
     def _():
-        copies = [
-            pltpu.make_async_copy(piece, held.at[pl.ds(plan.start(*slot), plan.block)], sems.at[i])
-            for i, (piece, slot) in enumerate(zip(pieces, slots))
-        ]
-        for copy in copies:
-            copy.start()
-        for copy in copies:
-            copy.wait()
+        for piece, slot in zip(pieces, slots):
+            held[pl.ds(plan.start(*slot), plan.block), :] = piece[...]
         total = jnp.zeros((plan.tail, LANE), jnp.float32)
         for z in range(plan.nz):
             for x in range(plan.nx):
@@ -480,15 +475,14 @@
             jax.ShapeDtypeStruct((matrices + 2,), jnp.float32),
         ],
         in_specs=[smem, smem, vmem, pl.BlockSpec((tile, LANE), lambda i: (i, 0))]
-        + [pl.BlockSpec(memory_space=pl.ANY)] * len(pieces),
+        + [vmem] * len(pieces),
         out_specs=[pl.BlockSpec((tile, LANE), lambda i: (i, 0)), vmem, smem],
         scratch_shapes=[
             pltpu.VMEM((2 * plan.half, LANE), jnp.float32),
             pltpu.VMEM((plan.norm_rows, LANE), jnp.float32),
             pltpu.VMEM((8, LANE), jnp.float32),
-            pltpu.SemaphoreType.DMA((len(pieces),)),
         ],
-        compiler_params=pltpu.CompilerParams(vmem_limit_bytes=58 * MIB),
+        compiler_params=pltpu.CompilerParams(vmem_limit_bytes=20 * MIB),
         name="new_weights",
     )(my_place, position, norm_state, weights, *pieces)
 

time: 189 us -> 174 us (0.921)
  waiting for transfers between devices: 93.5 us -> 80 us
  Pallas kernels: 55.5 us -> 50.9 us
  starting transfers between devices: 35.4 us -> 37.9 us
    ppermute x30, waiting for transfers between devices: 91.4 us -> 77.9 us  [send(): return lax.ppermute(value, 'dp', every)]
    pallas_call x1, Pallas kernels: 23.3 us -> 19.6 us  [finish(): pl.pallas_call(functools.partial(finish_kernel, plan, tile, slots), grid=...]
    ppermute x30, starting transfers between devices: 33.9 us -> 36.4 us  [send(): return lax.ppermute(value, 'dp', every)]
  transfers between devices with their start and end apart: 31 -> 31, of which waited for: 16 -> 16; matrix products, arithmetic and copies ran while one was open for 0% -> 1% of each run, Pallas kernels for 3% -> 4%
where the time goes in v8:
time: 174 us; the launch traced here: 173 us
  waiting for transfers between devices  80 us (46%)
  Pallas kernels  50.9 us (29%)
  starting transfers between devices  37.9 us (22%)
  other arithmetic  2.7 us (2%)
    ppermute x30, waiting for transfers between devices, send(): return lax.ppermute(value, 'dp', every)  77.9 us
    ppermute x30, starting transfers between devices, send(): return lax.ppermute(value, 'dp', every)  36.4 us
    pallas_call x1, Pallas kernels, place(): pl.pallas_call(functools.partial(place_kernel, plan), out_shape=[jax.Shap...  22.2 us
    pallas_call x1, Pallas kernels, finish(): pl.pallas_call(functools.partial(finish_kernel, plan, tile, slots), grid=...  19.6 us
    pallas_call x1, Pallas kernels, owned(): pl.pallas_call(functools.partial(owned_kernel, plan), out_shape=[jax.Shap...  6.31 us
  transfers between devices with their start and end apart: 31, of which 16 were waited for; matrix products, arithmetic and copies ran while one was open for 1% of the time, Pallas kernels for 4%

profile of v8, /device:TPU:0, one launch (start us, length us, event | category | flops | bytes accessed | tf_op | source)
XLA Modules:
  0.0 172.6 jit_solution(18384320505662013449)
XLA Ops:
  0.7 0.6 pad_add_fusion.place_ref
  1.3 22.2 %place_gradients.1 = (f32[2192,128]{1,0:T(8,128)}, f32[2192,128]{1,0:T(8,128)}, f32[2192,128]{1,0:T(8,128)}, f32[2192,128]{1,0:T(8,128)}, f32[2192,128]{1,0:T(8,...) custom-call(s32[3]{0:T(128)} %pad_add_fusion.place_ref, ...), custom_call_target="tpu_custom_call" | custom-call | tf_op jit(solution)/shard_map/place_gradients/pallas_call | solution.py:258
  23.5 0.5 collective-permute-start
  24.0 2.6 %collective-permute-done = f32[2192,128]{1,0:T(8,128)S(1)} collective-permute-done((f32[2192,128]{1,0:T(8,128)}, f32[2192,128]{1,0:T(8,128)S(1)}, u32[]{:S(2)}, u32[]{:S(2)}) %collective-permute-start) | collective-permute-done | bytes 1122336 | tf_op jit(solution)/shard_map/ppermute | solution.py:74
  26.6 1.1 slice_add_fusion.7
  27.8 0.4 collective-permute-start.5
  28.2 0.1 collective-permute-start.9
  28.4 2.9 %collective-permute-start.3 = (f32[1096,128]{1,0:T(8,128)S(1)}, f32[1096,128]{1,0:T(8,128)S(1)}, u32[]{:S(2)}, u32[]{:S(2)}) collective-permute-start(f32[1096,128]{1,0:T(8,128)S(1)} %slice_add_fusion.7), channel_id=1, source_target_pairs={{0,4},{2,6},{4,0},{6,2},{8,12},{10,14},{12,8},{14,10},{16,20},{18,... | collective-permute-start | bytes 1683464 | tf_op jit(solution)/shard_map/ppermute | solution.py:74
  31.2 6.3 %owned_weights.1 = (f32[1088,128]{1,0:T(8,128)}, s32[1152,128]{1,0:T(8,128)}) custom-call(s32[3]{0:T(128)} %pad_add_fusion.place_ref, s32[136,128]{1,0:T(8,128)} %bitcast.16, f32[17408,128]{1,0:T(8,128)} %weights_ref.3), custom_call_target="tpu_custom_call" | custom-call | bytes 20971520 | tf_op jit(solution)/shard_map/owned_weights/pallas_call | solution.py:336
  37.6 0.1 collective-permute-start.1
  37.7 0.1 slice_add_fusion.2
  37.7 0.2 collective-permute-start.6
  37.9 6.8 %collective-permute-done.3 = f32[1096,128]{1,0:T(8,128)S(1)} collective-permute-done((f32[1096,128]{1,0:T(8,128)S(1)}, f32[1096,128]{1,0:T(8,128)S(1)}, u32[]{:S(2)}, u32[]{:S(2)}) %collective-permute-start.3) | collective-permute-done | bytes 561184 | tf_op jit(solution)/shard_map/ppermute | solution.py:74
  44.7 0.1 fusion.2
  44.8 4.1 %collective-permute-start.4 = (f32[1096,128]{1,0:T(8,128)S(1)}, f32[1096,128]{1,0:T(8,128)S(1)}, u32[]{:S(2)}, u32[]{:S(2)}) collective-permute-start(f32[1096,128]{1,0:T(8,128)S(1)} %fusion.2), channel_id=1, source_target_pairs={{0,8},{2,10},{4,12},{6,14},{24,16},{26,18},{28,20},{30,22},{1,9},{... | collective-permute-start | bytes 1683464 | tf_op jit(solution)/shard_map/ppermute | solution.py:74
  48.9 0.1 slice_add_fusion
  49.0 1.6 collective-permute-start.10
  50.6 6.2 %collective-permute-done.6 = f32[1096,128]{1,0:T(8,128)S(1)} collective-permute-done((f32[1096,128]{1,0:T(8,128)S(1)}, f32[1096,128]{1,0:T(8,128)S(1)}, u32[]{:S(2)}, u32[]{:S(2)}) %collective-permute-start.6) | collective-permute-done | bytes 561184 | tf_op jit(solution)/shard_map/ppermute | solution.py:74
  56.7 0.1 fusion.1
  56.9 2.7 %collective-permute-done.4 = f32[1096,128]{1,0:T(8,128)S(1)} collective-permute-done((f32[1096,128]{1,0:T(8,128)S(1)}, f32[1096,128]{1,0:T(8,128)S(1)}, u32[]{:S(2)}, u32[]{:S(2)}) %collective-permute-start.4) | collective-permute-done | bytes 561184 | tf_op jit(solution)/shard_map/ppermute | solution.py:74
  59.5 4.4 %collective-permute-start.8 = (f32[1096,128]{1,0:T(8,128)S(1)}, f32[1096,128]{1,0:T(8,128)S(1)}, u32[]{:S(2)}, u32[]{:S(2)}) collective-permute-start(f32[1096,128]{1,0:T(8,128)S(1)} %fusion.1), channel_id=1, source_target_pairs={{0,8},{2,10},{4,12},{6,14},{24,16},{26,18},{28,20},{30,22},{1,9},{... | collective-permute-start | bytes 1683464 | tf_op jit(solution)/shard_map/ppermute | solution.py:74
  63.9 0.1 add.73
  64.0 0.7 collective-permute-start.7
  64.7 0.0 slice-start.1
  64.8 0.1 slice_add_fusion.5
  64.9 1.6 collective-permute-start.2
  66.5 2.3 %collective-permute-done.10 = f32[1096,128]{1,0:T(8,128)S(1)} collective-permute-done((f32[1096,128]{1,0:T(8,128)S(1)}, f32[1096,128]{1,0:T(8,128)S(1)}, u32[]{:S(2)}, u32[]{:S(2)}) %collective-permute-start.10) | collective-permute-done | bytes 561184 | tf_op jit(solution)/shard_map/ppermute | solution.py:74
  68.8 0.1 fusion
  68.9 4.7 %collective-permute-done.8 = f32[1096,128]{1,0:T(8,128)S(1)} collective-permute-done((f32[1096,128]{1,0:T(8,128)S(1)}, f32[1096,128]{1,0:T(8,128)S(1)}, u32[]{:S(2)}, u32[]{:S(2)}) %collective-permute-start.8) | collective-permute-done | bytes 561184 | tf_op jit(solution)/shard_map/ppermute | solution.py:74
  73.6 0.1 add.78
  73.7 0.1 add.77
  73.8 3.9 %collective-permute-start.11 = (f32[1096,128]{1,0:T(8,128)S(1)}, f32[1096,128]{1,0:T(8,128)S(1)}, u32[]{:S(2)}, u32[]{:S(2)}) collective-permute-start(f32[1096,128]{1,0:T(8,128)S(1)} %add.77), channel_id=1, source_target_pairs={{0,8},{2,10},{4,12},{6,14},{8,0},{10,2},{12,4},{14,6},{16,24},{18,... | collective-permute-start | bytes 1683464 | tf_op jit(solution)/shard_map/ppermute | solution.py:74
  77.7 0.7 collective-permute-start.12
  78.4 1.9 %collective-permute-done.2.refs_1_ = f32[1096,128]{1,0:T(8,128)S(1)} collective-permute-done((f32[1096,128]{1,0:T(8,128)S(1)}, f32[1096,128]{1,0:T(8,128)S(1)}, u32[]{:S(2)}, u32[]{:S(2)}) %collective-permute-start.2) | collective-permute-done | bytes 561184 | tf_op jit(solution)/shard_map/ppermute | solution.py:74
  80.3 7.0 %collective-permute-done.11.refs_2_ = f32[1096,128]{1,0:T(8,128)S(1)} collective-permute-done((f32[1096,128]{1,0:T(8,128)S(1)}, f32[1096,128]{1,0:T(8,128)S(1)}, u32[]{:S(2)}, u32[]{:S(2)}) %collective-permute-start.11) | collective-permute-done | bytes 561184 | tf_op jit(solution)/shard_map/ppermute | solution.py:74
  87.3 0.0 slice-start.2
  87.3 2.7 %moments.1 = (f32[1088,128]{1,0:T(8,128)}, f32[1088,128]{1,0:T(8,128)}, f32[1096,128]{1,0:T(8,128)S(1)}, f32[8,128]{1,0:T(8,128)S(1)}) custom-call(f32[1096,128]{1,0:T(8,128)S(1)} %get-tuple-element.86.refs_0_, f32[1096,128]{1,0:T(8,128)S(1)} %collective-permute-done.2.refs_1_, f32[1096,128]{1,0:T(8,128)S(1)} %collective-permute-done.11.refs_2_, ...), custom_call_target="tpu_custom_call" | custom-call | tf_op jit(solution)/shard_map/moments/pallas_call | solution.py:391
  90.0 1.5 collective-permute-start.13
  91.5 2.1 %collective-permute-done.13 = f32[8,128]{1,0:T(8,128)S(1)} collective-permute-done((f32[8,128]{1,0:T(8,128)S(1)}, f32[8,128]{1,0:T(8,128)S(1)}, u32[]{:S(2)}, u32[]{:S(2)}) %collective-permute-start.13) | collective-permute-done | bytes 4128 | tf_op jit(solution)/shard_map/ppermute | solution.py:524
  93.6 1.5 collective-permute-start.16
  95.1 0.7 collective-permute-start.15
  95.8 6.6 %collective-permute-start.14 = (f32[1096,128]{1,0:T(8,128)S(1)}, f32[1096,128]{1,0:T(8,128)S(1)}, u32[]{:S(2)}, u32[]{:S(2)}) collective-permute-start(f32[1096,128]{1,0:T(8,128)S(1)} %add_dynamic-update-slice_fusion.refs_0_), channel_id=1, source_target_pairs={{0,8},{2,10},{4,12},{6,14},{8,0},{10,2},{12,4},{14,6},{16,24},{18,... | collective-permute-start | bytes 1683464 | tf_op jit(solution)/shard_map/ppermute | solution.py:74
  102.4 0.8 collective-permute-done.16.refs_1_
  103.2 8.9 %collective-permute-done.14.refs_4_ = f32[1096,128]{1,0:T(8,128)S(1)} collective-permute-done((f32[1096,128]{1,0:T(8,128)S(1)}, f32[1096,128]{1,0:T(8,128)S(1)}, u32[]{:S(2)}, u32[]{:S(2)}) %collective-permute-start.14) | collective-permute-done | bytes 561184 | tf_op jit(solution)/shard_map/ppermute | solution.py:74
  112.1 1.3 collective-permute-start.20
  113.4 0.5 collective-permute-start.21
  113.9 0.7 collective-permute-start.19
  114.6 11.4 %collective-permute-done.20 = f32[1096,128]{1,0:T(8,128)S(1)} collective-permute-done((f32[1096,128]{1,0:T(8,128)S(1)}, f32[1096,128]{1,0:T(8,128)S(1)}, u32[]{:S(2)}, u32[]{:S(2)}) %collective-permute-start.20) | collective-permute-done | bytes 561184 | tf_op jit(solution)/shard_map/ppermute | solution.py:74
  125.9 1.5 collective-permute-done.21.refs_5_
  127.4 0.1 add.81.refs_8_
  127.5 0.3 collective-permute-start.25
  127.9 1.3 collective-permute-start.24
  129.2 0.1 collective-permute-start.17
  129.2 0.5 collective-permute-start.18
  129.7 0.1 collective-permute-start.22
  129.8 11.5 %collective-permute-done.25.refs_9_ = f32[1096,128]{1,0:T(8,128)S(1)} collective-permute-done((f32[1096,128]{1,0:T(8,128)S(1)}, f32[1096,128]{1,0:T(8,128)S(1)}, u32[]{:S(2)}, u32[]{:S(2)}) %collective-permute-start.25) | collective-permute-done | bytes 561184 | tf_op jit(solution)/shard_map/ppermute | solution.py:74
  141.3 0.1 add.82.refs_10_
  141.3 0.7 collective-permute-start.26
  142.1 0.5 collective-permute-start.29
  142.6 0.1 collective-permute-start.27
  142.7 0.4 collective-permute-start.28
  143.1 7.9 %collective-permute-done.26.refs_11_ = f32[1096,128]{1,0:T(8,128)S(1)} collective-permute-done((f32[1096,128]{1,0:T(8,128)S(1)}, f32[1096,128]{1,0:T(8,128)S(1)}, u32[]{:S(2)}, u32[]{:S(2)}) %collective-permute-start.26) | collective-permute-done | bytes 561184 | tf_op jit(solution)/shard_map/ppermute | solution.py:74
  151.0 1.9 %collective-permute-done.30.refs_15_ = f32[1096,128]{1,0:T(8,128)S(1)} collective-permute-done((f32[1096,128]{1,0:T(8,128)S(1)}, f32[1096,128]{1,0:T(8,128)S(1)}, u32[]{:S(2)}, u32[]{:S(2)}) %collective-permute-start.30) | collective-permute-done | bytes 561184 | tf_op jit(solution)/shard_map/ppermute | solution.py:74
  153.0 19.6 %new_weights.1 = (f32[17408,128]{1,0:T(8,128)}, f32[3,2,1024]{2,1,0:T(2,128)}, f32[7]{0:T(128)}) custom-call(s32[3]{0:T(128)S(1)} %copy-done.6, s32[136,128]{1,0:T(8,128)S(1)} %copy-done.4, f32[3,2,1024]{2,1,0:T(2,128)S(1)} %copy-done.5, f32[17408,128]{1,0:T(8,128)S(1)} %bitcast.11, f32[1096,128]{1,0:T(8,128)S(1)} %add_dynamic-update-slice_fusion.refs_0_, ...), custom_call_target="tpu_custom_call" | custom-call | tf_op jit(solution)/shard_map/new_weights/pallas_call | solution.py:469
  (45 shorter events, 0.1 us)
Async XLA Ops:
  23.5 3.1 %collective-permute-start = (f32[2192,128]{1,0:T(8,128)}, f32[2192,128]{1,0:T(8,128)S(1)}, u32[]{:S(2)}, u32[]{:S(2)}) collective-permute-start(f32[2192,128]{1,0:T(8,128)} %get-tuple-element.48), channel_id=1, source_target_pairs={{0,2},{2,0},{4,6},{6,4},{8,10},{10,8},{12,14},{14,12},{16,18},{18,... | collective-permute-start | bytes 3366920 | tf_op jit(solution)/shard_map/ppermute | solution.py:74
  27.8 9.9 %copy-start.9 = (f32[2192,128]{1,0:T(8,128)S(1)}, f32[2192,128]{1,0:T(8,128)}, u32[]{:S(2)}) copy-start(f32[2192,128]{1,0:T(8,128)} %get-tuple-element.54) | copy-start | bytes 3366916
  27.8 9.8 %collective-permute-start.5 = (f32[2192,128]{1,0:T(8,128)}, f32[2192,128]{1,0:T(8,128)S(1)}, u32[]{:S(2)}, u32[]{:S(2)}) collective-permute-start(f32[2192,128]{1,0:T(8,128)} %get-tuple-element.55), channel_id=1, source_target_pairs={{0,2},{2,0},{4,6},{6,4},{8,10},{10,8},{12,14},{14,12},{16,18},{18,... | collective-permute-start | bytes 3366920 | tf_op jit(solution)/shard_map/ppermute | solution.py:74
  28.2 20.7 %collective-permute-start.9 = (f32[2192,128]{1,0:T(8,128)}, f32[2192,128]{1,0:T(8,128)S(1)}, u32[]{:S(2)}, u32[]{:S(2)}) collective-permute-start(f32[2192,128]{1,0:T(8,128)} %get-tuple-element.61), channel_id=1, source_target_pairs={{0,2},{2,0},{4,6},{6,4},{8,10},{10,8},{12,14},{14,12},{16,18},{18,... | collective-permute-start | bytes 3366920 | tf_op jit(solution)/shard_map/ppermute | solution.py:74
  28.4 16.4 %collective-permute-start.3 = (f32[1096,128]{1,0:T(8,128)S(1)}, f32[1096,128]{1,0:T(8,128)S(1)}, u32[]{:S(2)}, u32[]{:S(2)}) collective-permute-start(f32[1096,128]{1,0:T(8,128)S(1)} %slice_add_fusion.7), channel_id=1, source_target_pairs={{0,4},{2,6},{4,0},{6,2},{8,12},{10,14},{12,8},{14,10},{16,20},{18,... | collective-permute-start | bytes 1683464 | tf_op jit(solution)/shard_map/ppermute | solution.py:74
  37.5 7.2 %copy-start.10 = (f32[2192,128]{1,0:T(8,128)S(1)}, f32[2192,128]{1,0:T(8,128)}, u32[]{:S(2)}) copy-start(f32[2192,128]{1,0:T(8,128)} %get-tuple-element.47) | copy-start | bytes 3366916
  37.6 27.2 %collective-permute-start.1 = (f32[2192,128]{1,0:T(8,128)}, f32[2192,128]{1,0:T(8,128)S(1)}, u32[]{:S(2)}, u32[]{:S(2)}) collective-permute-start(f32[2192,128]{1,0:T(8,128)} %get-tuple-element.52), channel_id=1, source_target_pairs={{0,2},{2,0},{4,6},{6,4},{8,10},{10,8},{12,14},{14,12},{16,18},{18,... | collective-permute-start | bytes 3366920 | tf_op jit(solution)/shard_map/ppermute | solution.py:74
  37.7 11.2 %copy-start.7 = (f32[2192,128]{1,0:T(8,128)S(1)}, f32[2192,128]{1,0:T(8,128)}, u32[]{:S(2)}) copy-start(f32[2192,128]{1,0:T(8,128)} %get-tuple-element.60) | copy-start | bytes 3366916
  37.7 19.0 %collective-permute-start.6 = (f32[1096,128]{1,0:T(8,128)S(1)}, f32[1096,128]{1,0:T(8,128)S(1)}, u32[]{:S(2)}, u32[]{:S(2)}) collective-permute-start(f32[1096,128]{1,0:T(8,128)S(1)} %slice_add_fusion.2), channel_id=1, source_target_pairs={{0,4},{2,6},{4,0},{6,2},{8,12},{10,14},{12,8},{14,10},{16,20},{18,... | collective-permute-start | bytes 1683464 | tf_op jit(solution)/shard_map/ppermute | solution.py:74
  44.8 14.7 %collective-permute-start.4 = (f32[1096,128]{1,0:T(8,128)S(1)}, f32[1096,128]{1,0:T(8,128)S(1)}, u32[]{:S(2)}, u32[]{:S(2)}) collective-permute-start(f32[1096,128]{1,0:T(8,128)S(1)} %fusion.2), channel_id=1, source_target_pairs={{0,8},{2,10},{4,12},{6,14},{24,16},{26,18},{28,20},{30,22},{1,9},{... | collective-permute-start | bytes 1683464 | tf_op jit(solution)/shard_map/ppermute | solution.py:74
  49.0 19.8 %collective-permute-start.10 = (f32[1096,128]{1,0:T(8,128)S(1)}, f32[1096,128]{1,0:T(8,128)S(1)}, u32[]{:S(2)}, u32[]{:S(2)}) collective-permute-start(f32[1096,128]{1,0:T(8,128)S(1)} %slice_add_fusion), channel_id=1, source_target_pairs={{0,4},{2,6},{4,0},{6,2},{8,12},{10,14},{12,8},{14,10},{16,20},{18,... | collective-permute-start | bytes 1683464 | tf_op jit(solution)/shard_map/ppermute | solution.py:74
  50.6 14.2 %copy-start.8 = (f32[2192,128]{1,0:T(8,128)S(1)}, f32[2192,128]{1,0:T(8,128)}, u32[]{:S(2)}) copy-start(f32[2192,128]{1,0:T(8,128)} %get-tuple-element.46) | copy-start | bytes 3366916
  56.7 96.2 %slice-start = ((s8[8912896]{0:T(1024)(128)(4,1)}), s8[4194304]{0:T(1024)(128)(4,1)S(1)}, s32[]{:S(2)}) async-start(s8[8912896]{0:T(1024)(128)(4,1)} %bitcast.10), calls=%async_computation | async-start | bytes 8388608
  59.5 14.1 %collective-permute-start.8 = (f32[1096,128]{1,0:T(8,128)S(1)}, f32[1096,128]{1,0:T(8,128)S(1)}, u32[]{:S(2)}, u32[]{:S(2)}) collective-permute-start(f32[1096,128]{1,0:T(8,128)S(1)} %fusion.1), channel_id=1, source_target_pairs={{0,8},{2,10},{4,12},{6,14},{24,16},{26,18},{28,20},{30,22},{1,9},{... | collective-permute-start | bytes 1683464 | tf_op jit(solution)/shard_map/ppermute | solution.py:74
  64.0 4.8 %collective-permute-start.7 = (f32[1096,128]{1,0:T(8,128)S(1)}, f32[1096,128]{1,0:T(8,128)S(1)}, u32[]{:S(2)}, u32[]{:S(2)}) collective-permute-start(f32[1096,128]{1,0:T(8,128)S(1)} %add.73), channel_id=1, source_target_pairs={{8,16},{10,18},{12,20},{14,22},{16,8},{18,10},{20,12},{22,14},{9,1... | collective-permute-start | bytes 1683464 | tf_op jit(solution)/shard_map/ppermute | solution.py:74
  64.7 88.2 %slice-start.1 = ((s8[8912896]{0:T(1024)(128)(4,1)}), s8[4194304]{0:T(1024)(128)(4,1)S(1)}, s32[]{:S(2)}) async-start(s8[8912896]{0:T(1024)(128)(4,1)} %bitcast.10), calls=%async_computation.1 | async-start | bytes 8388608
  64.9 15.4 %collective-permute-start.2 = (f32[1096,128]{1,0:T(8,128)S(1)}, f32[1096,128]{1,0:T(8,128)S(1)}, u32[]{:S(2)}, u32[]{:S(2)}) collective-permute-start(f32[1096,128]{1,0:T(8,128)S(1)} %get-tuple-element.85), channel_id=1, source_target_pairs={{0,4},{2,6},{4,0},{6,2},{8,12},{10,14},{12,8},{14,10},{16,20},{18,... | collective-permute-start | bytes 1683464 | tf_op jit(solution)/shard_map/ppermute | solution.py:74
  73.6 13.7 %copy-start.2 = (f32[1,1088,128]{2,1,0:T(8,128)S(1)}, f32[1,1088,128]{2,1,0:T(8,128)}, u32[]{:S(2)}) copy-start(f32[1,1088,128]{2,1,0:T(8,128)} %param.10) | copy-start | bytes 1671172
  73.6 13.7 %copy-start.3 = (f32[1088,128]{1,0:T(8,128)S(1)}, f32[1088,128]{1,0:T(8,128)}, u32[]{:S(2)}) copy-start(f32[1088,128]{1,0:T(8,128)} %get-tuple-element.65.refs_6_) | copy-start | bytes 1671172
  73.7 13.6 %copy-start = (s32[1152,128]{1,0:T(8,128)S(1)}, s32[1152,128]{1,0:T(8,128)}, u32[]{:S(2)}) copy-start(s32[1152,128]{1,0:T(8,128)} %get-tuple-element.66.refs_7_) | copy-start | bytes 1769476
  73.7 13.6 %copy-start.1 = (f32[1,1088,128]{2,1,0:T(8,128)S(1)}, f32[1,1088,128]{2,1,0:T(8,128)}, u32[]{:S(2)}) copy-start(f32[1,1088,128]{2,1,0:T(8,128)} %param.9) | copy-start | bytes 1671172
  73.8 13.5 %collective-permute-start.11 = (f32[1096,128]{1,0:T(8,128)S(1)}, f32[1096,128]{1,0:T(8,128)S(1)}, u32[]{:S(2)}, u32[]{:S(2)}) collective-permute-start(f32[1096,128]{1,0:T(8,128)S(1)} %add.77), channel_id=1, source_target_pairs={{0,8},{2,10},{4,12},{6,14},{8,0},{10,2},{12,4},{14,6},{16,24},{18,... | collective-permute-start | bytes 1683464 | tf_op jit(solution)/shard_map/ppermute | solution.py:74
  77.7 9.5 %collective-permute-start.12 = (f32[1096,128]{1,0:T(8,128)S(1)}, f32[1096,128]{1,0:T(8,128)S(1)}, u32[]{:S(2)}, u32[]{:S(2)}) collective-permute-start(f32[1096,128]{1,0:T(8,128)S(1)} %add.78), channel_id=1, source_target_pairs={{8,16},{10,18},{12,20},{14,22},{16,8},{18,10},{20,12},{22,14},{9,1... | collective-permute-start | bytes 1683464 | tf_op jit(solution)/shard_map/ppermute | solution.py:74
  87.3 65.7 %slice-start.2 = ((s8[8912896]{0:T(1024)(128)(4,1)}), s8[524288]{0:T(1024)(128)(4,1)S(1)}, s32[]{:S(2)}) async-start(s8[8912896]{0:T(1024)(128)(4,1)} %bitcast.10), calls=%async_computation.2 | async-start | bytes 1048576
  90.0 3.6 %collective-permute-start.13 = (f32[8,128]{1,0:T(8,128)S(1)}, f32[8,128]{1,0:T(8,128)S(1)}, u32[]{:S(2)}, u32[]{:S(2)}) collective-permute-start(f32[8,128]{1,0:T(8,128)S(1)} %get-tuple-element.68), channel_id=1, source_target_pairs={{0,1},{1,0},{2,3},{3,2},{4,5},{5,4},{6,7},{7,6},{8,9},{9,8},{10,11... | collective-permute-start | bytes 12296 | tf_op jit(solution)/shard_map/ppermute | solution.py:524
  93.6 9.6 %collective-permute-start.16 = (f32[1096,128]{1,0:T(8,128)S(1)}, f32[1096,128]{1,0:T(8,128)S(1)}, u32[]{:S(2)}, u32[]{:S(2)}) collective-permute-start(f32[1096,128]{1,0:T(8,128)S(1)} %add_dynamic-update-slice_fusion.refs_0_), channel_id=1, source_target_pairs={{0,4},{2,6},{4,0},{6,2},{8,12},{10,14},{12,8},{14,10},{16,20},{18,... | collective-permute-start | bytes 1683464 | tf_op jit(solution)/shard_map/ppermute | solution.py:74
  95.1 8.1 %collective-permute-start.15 = (f32[1096,128]{1,0:T(8,128)S(1)}, f32[1096,128]{1,0:T(8,128)S(1)}, u32[]{:S(2)}, u32[]{:S(2)}) collective-permute-start(f32[1096,128]{1,0:T(8,128)S(1)} %add_dynamic-update-slice_fusion.refs_0_), channel_id=1, source_target_pairs={{8,16},{10,18},{12,20},{14,22},{16,8},{18,10},{20,12},{22,14},{9,1... | collective-permute-start | bytes 1683464 | tf_op jit(solution)/shard_map/ppermute | solution.py:74
  95.8 16.3 %collective-permute-start.14 = (f32[1096,128]{1,0:T(8,128)S(1)}, f32[1096,128]{1,0:T(8,128)S(1)}, u32[]{:S(2)}, u32[]{:S(2)}) collective-permute-start(f32[1096,128]{1,0:T(8,128)S(1)} %add_dynamic-update-slice_fusion.refs_0_), channel_id=1, source_target_pairs={{0,8},{2,10},{4,12},{6,14},{8,0},{10,2},{12,4},{14,6},{16,24},{18,... | collective-permute-start | bytes 1683464 | tf_op jit(solution)/shard_map/ppermute | solution.py:74
  112.1 13.8 %collective-permute-start.20 = (f32[1096,128]{1,0:T(8,128)S(1)}, f32[1096,128]{1,0:T(8,128)S(1)}, u32[]{:S(2)}, u32[]{:S(2)}) collective-permute-start(f32[1096,128]{1,0:T(8,128)S(1)} %collective-permute-done.15), channel_id=1, source_target_pairs={{8,0},{10,2},{12,4},{14,6},{16,24},{18,26},{20,28},{22,30},{9,1},{... | collective-permute-start | bytes 1683464 | tf_op jit(solution)/shard_map/ppermute | solution.py:74
  113.4 14.0 %collective-permute-start.21 = (f32[1096,128]{1,0:T(8,128)S(1)}, f32[1096,128]{1,0:T(8,128)S(1)}, u32[]{:S(2)}, u32[]{:S(2)}) collective-permute-start(f32[1096,128]{1,0:T(8,128)S(1)} %collective-permute-done.14.refs_4_), channel_id=1, source_target_pairs={{0,4},{2,6},{4,0},{6,2},{8,12},{10,14},{12,8},{14,10},{16,20},{18,... | collective-permute-start | bytes 1683464 | tf_op jit(solution)/shard_map/ppermute | solution.py:74
  113.9 13.5 %collective-permute-start.19 = (f32[1096,128]{1,0:T(8,128)S(1)}, f32[1096,128]{1,0:T(8,128)S(1)}, u32[]{:S(2)}, u32[]{:S(2)}) collective-permute-start(f32[1096,128]{1,0:T(8,128)S(1)} %collective-permute-done.14.refs_4_), channel_id=1, source_target_pairs={{8,16},{10,18},{12,20},{14,22},{16,8},{18,10},{20,12},{22,14},{9,1... | collective-permute-start | bytes 1683464 | tf_op jit(solution)/shard_map/ppermute | solution.py:74
  127.5 25.5 %copy-start.4 = (s32[136,128]{1,0:T(8,128)S(1)}, s32[136,128]{1,0:T(8,128)}, u32[]{:S(2)}) copy-start(s32[136,128]{1,0:T(8,128)} %get-tuple-element.45.position_ref) | copy-start | bytes 208900
  127.5 25.5 %copy-start.5 = (f32[3,2,1024]{2,1,0:T(2,128)S(1)}, f32[3,2,1024]{2,1,0:T(2,128)}, u32[]{:S(2)}) copy-start(f32[3,2,1024]{2,1,0:T(2,128)} %norm_ref.1) | copy-start | bytes 73732
  127.5 25.5 %copy-start.6 = (s32[3]{0:T(128)S(1)}, s32[3]{0:T(128)}, u32[]{:S(2)}) copy-start(s32[3]{0:T(128)} %pad_add_fusion.place_ref) | copy-start | bytes 40
  127.5 13.7 %collective-permute-start.25 = (f32[1096,128]{1,0:T(8,128)S(1)}, f32[1096,128]{1,0:T(8,128)S(1)}, u32[]{:S(2)}, u32[]{:S(2)}) collective-permute-start(f32[1096,128]{1,0:T(8,128)S(1)} %add.81.refs_8_), channel_id=1, source_target_pairs={{0,4},{2,6},{4,0},{6,2},{8,12},{10,14},{12,8},{14,10},{16,20},{18,... | collective-permute-start | bytes 1683464 | tf_op jit(solution)/shard_map/ppermute | solution.py:74
  127.9 13.4 %collective-permute-start.24 = (f32[1096,128]{1,0:T(8,128)S(1)}, f32[1096,128]{1,0:T(8,128)S(1)}, u32[]{:S(2)}, u32[]{:S(2)}) collective-permute-start(f32[1096,128]{1,0:T(8,128)S(1)} %collective-permute-done.19), channel_id=1, source_target_pairs={{8,0},{10,2},{12,4},{14,6},{16,24},{18,26},{20,28},{22,30},{9,1},{... | collective-permute-start | bytes 1683464 | tf_op jit(solution)/shard_map/ppermute | solution.py:74
  129.2 12.9 %collective-permute-start.17 = (f32[1096,128]{1,0:T(8,128)S(1)}, f32[1096,128]{1,0:T(8,128)S(1)}, u32[]{:S(2)}, u32[]{:S(2)}) collective-permute-start(f32[1096,128]{1,0:T(8,128)S(1)} %add_dynamic-update-slice_fusion.refs_0_), channel_id=1, source_target_pairs={{0,2},{2,0},{4,6},{6,4},{8,10},{10,8},{12,14},{14,12},{16,18},{18,... | collective-permute-start | bytes 1683464 | tf_op jit(solution)/shard_map/ppermute | solution.py:74
  129.2 13.4 %collective-permute-start.18 = (f32[1096,128]{1,0:T(8,128)S(1)}, f32[1096,128]{1,0:T(8,128)S(1)}, u32[]{:S(2)}, u32[]{:S(2)}) collective-permute-start(f32[1096,128]{1,0:T(8,128)S(1)} %collective-permute-done.16.refs_1_), channel_id=1, source_target_pairs={{0,2},{2,0},{4,6},{6,4},{8,10},{10,8},{12,14},{14,12},{16,18},{18,... | collective-permute-start | bytes 1683464 | tf_op jit(solution)/shard_map/ppermute | solution.py:74
  129.7 12.9 %collective-permute-start.22 = (f32[1096,128]{1,0:T(8,128)S(1)}, f32[1096,128]{1,0:T(8,128)S(1)}, u32[]{:S(2)}, u32[]{:S(2)}) collective-permute-start(f32[1096,128]{1,0:T(8,128)S(1)} %collective-permute-done.14.refs_4_), channel_id=1, source_target_pairs={{0,2},{2,0},{4,6},{6,4},{8,10},{10,8},{12,14},{14,12},{16,18},{18,... | collective-permute-start | bytes 1683464 | tf_op jit(solution)/shard_map/ppermute | solution.py:74
  141.3 9.6 %collective-permute-start.26 = (f32[1096,128]{1,0:T(8,128)S(1)}, f32[1096,128]{1,0:T(8,128)S(1)}, u32[]{:S(2)}, u32[]{:S(2)}) collective-permute-start(f32[1096,128]{1,0:T(8,128)S(1)} %add.82.refs_10_), channel_id=1, source_target_pairs={{0,4},{2,6},{4,0},{6,2},{8,12},{10,14},{12,8},{14,10},{16,20},{18,... | collective-permute-start | bytes 1683464 | tf_op jit(solution)/shard_map/ppermute | solution.py:74
  142.1 8.9 %collective-permute-start.23 = (f32[1096,128]{1,0:T(8,128)S(1)}, f32[1096,128]{1,0:T(8,128)S(1)}, u32[]{:S(2)}, u32[]{:S(2)}) collective-permute-start(f32[1096,128]{1,0:T(8,128)S(1)} %collective-permute-done.21.refs_5_), channel_id=1, source_target_pairs={{0,2},{2,0},{4,6},{6,4},{8,10},{10,8},{12,14},{14,12},{16,18},{18,... | collective-permute-start | bytes 1683464 | tf_op jit(solution)/shard_map/ppermute | solution.py:74
  142.1 8.9 %collective-permute-start.29 = (f32[1096,128]{1,0:T(8,128)S(1)}, f32[1096,128]{1,0:T(8,128)S(1)}, u32[]{:S(2)}, u32[]{:S(2)}) collective-permute-start(f32[1096,128]{1,0:T(8,128)S(1)} %add.82.refs_10_), channel_id=1, source_target_pairs={{0,2},{2,0},{4,6},{6,4},{8,10},{10,8},{12,14},{14,12},{16,18},{18,... | collective-permute-start | bytes 1683464 | tf_op jit(solution)/shard_map/ppermute | solution.py:74
  142.6 8.4 %collective-permute-start.27 = (f32[1096,128]{1,0:T(8,128)S(1)}, f32[1096,128]{1,0:T(8,128)S(1)}, u32[]{:S(2)}, u32[]{:S(2)}) collective-permute-start(f32[1096,128]{1,0:T(8,128)S(1)} %add.81.refs_8_), channel_id=1, source_target_pairs={{0,2},{2,0},{4,6},{6,4},{8,10},{10,8},{12,14},{14,12},{16,18},{18,... | collective-permute-start | bytes 1683464 | tf_op jit(solution)/shard_map/ppermute | solution.py:74
  142.7 8.3 %collective-permute-start.28 = (f32[1096,128]{1,0:T(8,128)S(1)}, f32[1096,128]{1,0:T(8,128)S(1)}, u32[]{:S(2)}, u32[]{:S(2)}) collective-permute-start(f32[1096,128]{1,0:T(8,128)S(1)} %collective-permute-done.25.refs_9_), channel_id=1, source_target_pairs={{0,2},{2,0},{4,6},{6,4},{8,10},{10,8},{12,14},{14,12},{16,18},{18,... | collective-permute-start | bytes 1683464 | tf_op jit(solution)/shard_map/ppermute | solution.py:74
  151.0 2.0 %collective-permute-start.30 = (f32[1096,128]{1,0:T(8,128)S(1)}, f32[1096,128]{1,0:T(8,128)S(1)}, u32[]{:S(2)}, u32[]{:S(2)}) collective-permute-start(f32[1096,128]{1,0:T(8,128)S(1)} %collective-permute-done.26.refs_11_), channel_id=1, source_target_pairs={{0,2},{2,0},{4,6},{6,4},{8,10},{10,8},{12,14},{14,12},{16,18},{18,... | collective-permute-start | bytes 1683464 | tf_op jit(solution)/shard_map/ppermute | solution.py:74

commit v9 on v8

--- a/solution.py
+++ b/solution.py
@@ -142,23 +142,23 @@
             add(far_z, along_x(value))
             swapped(far_z)
         return list(found.items())
-    line = along_x(block)
     pair = plan.send(block, "z", PAIRS)
     three = plan.send(block, "z", MIDDLE)
-    pair, three, *line = together(pair, three, *line)
+    line = along_x(block)
+    three, found[1, 0, 1], *line = together(three, plan.swap(pair), *line)
     add(0, line)
     line = along_x(pair)
     two = plan.send(pair, "z", MIDDLE)
     out_two = plan.send(three, "z", OUTWARD)
     swapped(0)
-    two, out_two, *line = together(two, out_two, *line)
+    near_two, two, *line = together(two + out_two, two, *line)
     add(1, line)
-    line = along_x(two + out_two)
+    line = along_x(near_two)
     out_three = plan.send(two, "z", OUTWARD)
     swapped(1)
-    out_three, *line = together(out_three, *line)
+    near_three, *line = together(three + out_three, *line)
     add(2, line)
-    add(3, along_x(three + out_three))
+    add(3, along_x(near_three))
     swapped(2)
     swapped(3)
     return list(found.items())

time: 174 us -> 177 us (1.017)
  waiting for transfers between devices: 80 us -> 83.7 us
    ppermute x30, waiting for transfers between devices: 77.9 us -> 81.6 us  [send(): return lax.ppermute(value, 'dp', every)]
  transfers between devices with their start and end apart: 31 -> 31, of which waited for: 16 -> 15; matrix products, arithmetic and copies ran while one was open for 1% -> 1% of each run, Pallas kernels for 4% -> 4%
where the time goes in v9:
time: 177 us; the launch traced here: 176 us
  waiting for transfers between devices  83.7 us (47%)
  Pallas kernels  50.9 us (29%)
  starting transfers between devices  38.1 us (22%)
  other arithmetic  2.7 us (2%)
    ppermute x30, waiting for transfers between devices, send(): return lax.ppermute(value, 'dp', every)  81.6 us
    ppermute x30, starting transfers between devices, send(): return lax.ppermute(value, 'dp', every)  36.5 us
    pallas_call x1, Pallas kernels, place(): pl.pallas_call(functools.partial(place_kernel, plan), out_shape=[jax.Shap...  22.2 us
    pallas_call x1, Pallas kernels, finish(): pl.pallas_call(functools.partial(finish_kernel, plan, tile, slots), grid=...  19.6 us
    pallas_call x1, Pallas kernels, owned(): pl.pallas_call(functools.partial(owned_kernel, plan), out_shape=[jax.Shap...  6.31 us
  transfers between devices with their start and end apart: 31, of which 15 were waited for; matrix products, arithmetic and copies ran while one was open for 1% of the time, Pallas kernels for 4%

profile of v9, /device:TPU:0, one launch (start us, length us, event | category | flops | bytes accessed | tf_op | source)
XLA Modules:
  0.0 176.5 jit_solution(4445710129210497775)
XLA Ops:
  0.7 0.6 pad_add_fusion.place_ref
  1.3 22.2 %place_gradients.1 = (f32[2192,128]{1,0:T(8,128)}, f32[2192,128]{1,0:T(8,128)}, f32[2192,128]{1,0:T(8,128)}, f32[2192,128]{1,0:T(8,128)}, f32[2192,128]{1,0:T(8,...) custom-call(s32[3]{0:T(128)} %pad_add_fusion.place_ref, ...), custom_call_target="tpu_custom_call" | custom-call | tf_op jit(solution)/shard_map/place_gradients/pallas_call | solution.py:258
  23.5 0.5 collective-permute-start
  24.0 2.6 %collective-permute-done = f32[2192,128]{1,0:T(8,128)S(1)} collective-permute-done((f32[2192,128]{1,0:T(8,128)}, f32[2192,128]{1,0:T(8,128)S(1)}, u32[]{:S(2)}, u32[]{:S(2)}) %collective-permute-start) | collective-permute-done | bytes 1122336 | tf_op jit(solution)/shard_map/ppermute | solution.py:74
  26.7 1.1 slice_add_fusion.7
  27.8 0.4 collective-permute-start.5
  28.2 0.1 collective-permute-start.9
  28.4 2.9 %collective-permute-start.3 = (f32[1096,128]{1,0:T(8,128)S(1)}, f32[1096,128]{1,0:T(8,128)S(1)}, u32[]{:S(2)}, u32[]{:S(2)}) collective-permute-start(f32[1096,128]{1,0:T(8,128)S(1)} %slice_add_fusion.7), channel_id=1, source_target_pairs={{0,4},{2,6},{4,0},{6,2},{8,12},{10,14},{12,8},{14,10},{16,20},{18,... | collective-permute-start | bytes 1683464 | tf_op jit(solution)/shard_map/ppermute | solution.py:74
  31.2 6.3 %owned_weights.1 = (f32[1088,128]{1,0:T(8,128)}, s32[1152,128]{1,0:T(8,128)}) custom-call(s32[3]{0:T(128)} %pad_add_fusion.place_ref, s32[136,128]{1,0:T(8,128)} %bitcast.16, f32[17408,128]{1,0:T(8,128)} %weights_ref.3), custom_call_target="tpu_custom_call" | custom-call | bytes 20971520 | tf_op jit(solution)/shard_map/owned_weights/pallas_call | solution.py:336
  37.6 0.1 collective-permute-start.1
  37.7 0.1 slice_add_fusion.2
  37.7 0.2 collective-permute-start.6
  37.9 6.8 %collective-permute-done.3 = f32[1096,128]{1,0:T(8,128)S(1)} collective-permute-done((f32[1096,128]{1,0:T(8,128)S(1)}, f32[1096,128]{1,0:T(8,128)S(1)}, u32[]{:S(2)}, u32[]{:S(2)}) %collective-permute-start.3) | collective-permute-done | bytes 561184 | tf_op jit(solution)/shard_map/ppermute | solution.py:74
  44.7 0.1 fusion.2
  44.8 4.1 %collective-permute-start.4 = (f32[1096,128]{1,0:T(8,128)S(1)}, f32[1096,128]{1,0:T(8,128)S(1)}, u32[]{:S(2)}, u32[]{:S(2)}) collective-permute-start(f32[1096,128]{1,0:T(8,128)S(1)} %fusion.2), channel_id=1, source_target_pairs={{0,8},{2,10},{4,12},{6,14},{24,16},{26,18},{28,20},{30,22},{1,9},{... | collective-permute-start | bytes 1683464 | tf_op jit(solution)/shard_map/ppermute | solution.py:74
  48.9 0.1 slice_add_fusion
  49.0 1.6 collective-permute-start.10
  50.6 6.2 %collective-permute-done.6 = f32[1096,128]{1,0:T(8,128)S(1)} collective-permute-done((f32[1096,128]{1,0:T(8,128)S(1)}, f32[1096,128]{1,0:T(8,128)S(1)}, u32[]{:S(2)}, u32[]{:S(2)}) %collective-permute-start.6) | collective-permute-done | bytes 561184 | tf_op jit(solution)/shard_map/ppermute | solution.py:74
  56.7 0.1 fusion.1
  56.9 2.7 %collective-permute-done.4 = f32[1096,128]{1,0:T(8,128)S(1)} collective-permute-done((f32[1096,128]{1,0:T(8,128)S(1)}, f32[1096,128]{1,0:T(8,128)S(1)}, u32[]{:S(2)}, u32[]{:S(2)}) %collective-permute-start.4) | collective-permute-done | bytes 561184 | tf_op jit(solution)/shard_map/ppermute | solution.py:74
  59.5 4.4 %collective-permute-start.8 = (f32[1096,128]{1,0:T(8,128)S(1)}, f32[1096,128]{1,0:T(8,128)S(1)}, u32[]{:S(2)}, u32[]{:S(2)}) collective-permute-start(f32[1096,128]{1,0:T(8,128)S(1)} %fusion.1), channel_id=1, source_target_pairs={{0,8},{2,10},{4,12},{6,14},{24,16},{26,18},{28,20},{30,22},{1,9},{... | collective-permute-start | bytes 1683464 | tf_op jit(solution)/shard_map/ppermute | solution.py:74
  63.9 0.1 add.73
  64.0 0.7 collective-permute-start.7
  64.7 0.0 slice-start.1
  64.8 0.1 slice_add_fusion.5
  64.9 1.6 collective-permute-start.2
  66.5 2.3 %collective-permute-done.10 = f32[1096,128]{1,0:T(8,128)S(1)} collective-permute-done((f32[1096,128]{1,0:T(8,128)S(1)}, f32[1096,128]{1,0:T(8,128)S(1)}, u32[]{:S(2)}, u32[]{:S(2)}) %collective-permute-start.10) | collective-permute-done | bytes 561184 | tf_op jit(solution)/shard_map/ppermute | solution.py:74
  68.8 0.1 fusion
  68.9 4.7 %collective-permute-done.8 = f32[1096,128]{1,0:T(8,128)S(1)} collective-permute-done((f32[1096,128]{1,0:T(8,128)S(1)}, f32[1096,128]{1,0:T(8,128)S(1)}, u32[]{:S(2)}, u32[]{:S(2)}) %collective-permute-start.8) | collective-permute-done | bytes 561184 | tf_op jit(solution)/shard_map/ppermute | solution.py:74
  73.6 0.1 add.78
  73.7 0.0 copy-start
  73.7 0.0 copy-start.1
  73.7 0.1 add.77
  73.8 3.9 %collective-permute-start.11 = (f32[1096,128]{1,0:T(8,128)S(1)}, f32[1096,128]{1,0:T(8,128)S(1)}, u32[]{:S(2)}, u32[]{:S(2)}) collective-permute-start(f32[1096,128]{1,0:T(8,128)S(1)} %add.77), channel_id=1, source_target_pairs={{0,8},{2,10},{4,12},{6,14},{8,0},{10,2},{12,4},{14,6},{16,24},{18,... | collective-permute-start | bytes 1683464 | tf_op jit(solution)/shard_map/ppermute | solution.py:74
  77.7 0.7 collective-permute-start.12
  78.4 1.9 %collective-permute-done.2.refs_1_ = f32[1096,128]{1,0:T(8,128)S(1)} collective-permute-done((f32[1096,128]{1,0:T(8,128)S(1)}, f32[1096,128]{1,0:T(8,128)S(1)}, u32[]{:S(2)}, u32[]{:S(2)}) %collective-permute-start.2) | collective-permute-done | bytes 561184 | tf_op jit(solution)/shard_map/ppermute | solution.py:74
  80.3 7.0 %collective-permute-done.11.refs_2_ = f32[1096,128]{1,0:T(8,128)S(1)} collective-permute-done((f32[1096,128]{1,0:T(8,128)S(1)}, f32[1096,128]{1,0:T(8,128)S(1)}, u32[]{:S(2)}, u32[]{:S(2)}) %collective-permute-start.11) | collective-permute-done | bytes 561184 | tf_op jit(solution)/shard_map/ppermute | solution.py:74
  87.3 0.0 slice-start.2
  87.3 2.7 %moments.1 = (f32[1088,128]{1,0:T(8,128)}, f32[1088,128]{1,0:T(8,128)}, f32[1096,128]{1,0:T(8,128)S(1)}, f32[8,128]{1,0:T(8,128)S(1)}) custom-call(f32[1096,128]{1,0:T(8,128)S(1)} %get-tuple-element.86.refs_0_, f32[1096,128]{1,0:T(8,128)S(1)} %collective-permute-done.2.refs_1_, f32[1096,128]{1,0:T(8,128)S(1)} %collective-permute-done.11.refs_2_, ...), custom_call_target="tpu_custom_call" | custom-call | tf_op jit(solution)/shard_map/moments/pallas_call | solution.py:391
  90.0 1.5 collective-permute-start.13
  91.5 2.1 %collective-permute-done.13 = f32[8,128]{1,0:T(8,128)S(1)} collective-permute-done((f32[8,128]{1,0:T(8,128)S(1)}, f32[8,128]{1,0:T(8,128)S(1)}, u32[]{:S(2)}, u32[]{:S(2)}) %collective-permute-start.13) | collective-permute-done | bytes 4128 | tf_op jit(solution)/shard_map/ppermute | solution.py:524
  93.6 3.8 %collective-permute-start.15 = (f32[1096,128]{1,0:T(8,128)S(1)}, f32[1096,128]{1,0:T(8,128)S(1)}, u32[]{:S(2)}, u32[]{:S(2)}) collective-permute-start(f32[1096,128]{1,0:T(8,128)S(1)} %add_dynamic-update-slice_fusion.refs_1_), channel_id=1, source_target_pairs={{0,8},{2,10},{4,12},{6,14},{8,0},{10,2},{12,4},{14,6},{16,24},{18,... | collective-permute-start | bytes 1683464 | tf_op jit(solution)/shard_map/ppermute | solution.py:74
  97.4 1.5 collective-permute-start.17
  98.9 0.7 collective-permute-start.14
  99.6 5.4 %collective-permute-done.15.refs_5_ = f32[1096,128]{1,0:T(8,128)S(1)} collective-permute-done((f32[1096,128]{1,0:T(8,128)S(1)}, f32[1096,128]{1,0:T(8,128)S(1)}, u32[]{:S(2)}, u32[]{:S(2)}) %collective-permute-start.15) | collective-permute-done | bytes 561184 | tf_op jit(solution)/shard_map/ppermute | solution.py:74
  104.9 0.7 collective-permute-start.20
  105.6 1.3 collective-permute-done.17.refs_2_
  107.0 1.3 collective-permute-start.21
  108.3 1.6 collective-permute-start.22
  109.8 15.0 %collective-permute-done.21 = f32[1096,128]{1,0:T(8,128)S(1)} collective-permute-done((f32[1096,128]{1,0:T(8,128)S(1)}, f32[1096,128]{1,0:T(8,128)S(1)}, u32[]{:S(2)}, u32[]{:S(2)}) %collective-permute-start.21) | collective-permute-done | bytes 561184 | tf_op jit(solution)/shard_map/ppermute | solution.py:74
  124.9 0.1 add.81.refs_8_
  124.9 0.0 copy-start.5
  125.0 1.3 collective-permute-start.24
  126.3 1.6 collective-permute-start.25
  127.8 0.5 collective-permute-start.19
  128.3 12.9 %collective-permute-done.24 = f32[1096,128]{1,0:T(8,128)S(1)} collective-permute-done((f32[1096,128]{1,0:T(8,128)S(1)}, f32[1096,128]{1,0:T(8,128)S(1)}, u32[]{:S(2)}, u32[]{:S(2)}) %collective-permute-start.24) | collective-permute-done | bytes 561184 | tf_op jit(solution)/shard_map/ppermute | solution.py:74
  141.2 0.1 add.82.refs_10_
  141.3 1.6 collective-permute-start.26
  142.9 0.5 collective-permute-start.29
  143.4 0.0 collective-permute-start.27
  143.4 0.5 collective-permute-start.28
  143.9 10.9 %collective-permute-done.26.refs_11_ = f32[1096,128]{1,0:T(8,128)S(1)} collective-permute-done((f32[1096,128]{1,0:T(8,128)S(1)}, f32[1096,128]{1,0:T(8,128)S(1)}, u32[]{:S(2)}, u32[]{:S(2)}) %collective-permute-start.26) | collective-permute-done | bytes 561184 | tf_op jit(solution)/shard_map/ppermute | solution.py:74
  154.9 1.9 %collective-permute-done.30.refs_15_ = f32[1096,128]{1,0:T(8,128)S(1)} collective-permute-done((f32[1096,128]{1,0:T(8,128)S(1)}, f32[1096,128]{1,0:T(8,128)S(1)}, u32[]{:S(2)}, u32[]{:S(2)}) %collective-permute-start.30) | collective-permute-done | bytes 561184 | tf_op jit(solution)/shard_map/ppermute | solution.py:74
  156.8 19.6 %new_weights.1 = (f32[17408,128]{1,0:T(8,128)}, f32[3,2,1024]{2,1,0:T(2,128)}, f32[7]{0:T(128)}) custom-call(s32[3]{0:T(128)S(1)} %copy-done.6, s32[136,128]{1,0:T(8,128)S(1)} %copy-done.4, f32[3,2,1024]{2,1,0:T(2,128)S(1)} %copy-done.5, f32[17408,128]{1,0:T(8,128)S(1)} %bitcast.11, f32[1096,128]{1,0:T(8,128)S(1)} %collective-permute-done.16.refs_0_, ...), custom_call_target="tpu_custom_call" | custom-call | tf_op jit(solution)/shard_map/new_weights/pallas_call | solution.py:469
  (45 shorter events, 0.1 us)
Async XLA Ops:
  23.5 3.1 %collective-permute-start = (f32[2192,128]{1,0:T(8,128)}, f32[2192,128]{1,0:T(8,128)S(1)}, u32[]{:S(2)}, u32[]{:S(2)}) collective-permute-start(f32[2192,128]{1,0:T(8,128)} %get-tuple-element.48), channel_id=1, source_target_pairs={{0,2},{2,0},{4,6},{6,4},{8,10},{10,8},{12,14},{14,12},{16,18},{18,... | collective-permute-start | bytes 3366920 | tf_op jit(solution)/shard_map/ppermute | solution.py:74
  27.8 9.9 %copy-start.9 = (f32[2192,128]{1,0:T(8,128)S(1)}, f32[2192,128]{1,0:T(8,128)}, u32[]{:S(2)}) copy-start(f32[2192,128]{1,0:T(8,128)} %get-tuple-element.54) | copy-start | bytes 3366916
  27.8 9.8 %collective-permute-start.5 = (f32[2192,128]{1,0:T(8,128)}, f32[2192,128]{1,0:T(8,128)S(1)}, u32[]{:S(2)}, u32[]{:S(2)}) collective-permute-start(f32[2192,128]{1,0:T(8,128)} %get-tuple-element.55), channel_id=1, source_target_pairs={{0,2},{2,0},{4,6},{6,4},{8,10},{10,8},{12,14},{14,12},{16,18},{18,... | collective-permute-start | bytes 3366920 | tf_op jit(solution)/shard_map/ppermute | solution.py:74
  28.2 20.7 %collective-permute-start.9 = (f32[2192,128]{1,0:T(8,128)}, f32[2192,128]{1,0:T(8,128)S(1)}, u32[]{:S(2)}, u32[]{:S(2)}) collective-permute-start(f32[2192,128]{1,0:T(8,128)} %get-tuple-element.61), channel_id=1, source_target_pairs={{0,2},{2,0},{4,6},{6,4},{8,10},{10,8},{12,14},{14,12},{16,18},{18,... | collective-permute-start | bytes 3366920 | tf_op jit(solution)/shard_map/ppermute | solution.py:74
  28.4 16.4 %collective-permute-start.3 = (f32[1096,128]{1,0:T(8,128)S(1)}, f32[1096,128]{1,0:T(8,128)S(1)}, u32[]{:S(2)}, u32[]{:S(2)}) collective-permute-start(f32[1096,128]{1,0:T(8,128)S(1)} %slice_add_fusion.7), channel_id=1, source_target_pairs={{0,4},{2,6},{4,0},{6,2},{8,12},{10,14},{12,8},{14,10},{16,20},{18,... | collective-permute-start | bytes 1683464 | tf_op jit(solution)/shard_map/ppermute | solution.py:74
  37.5 7.2 %copy-start.10 = (f32[2192,128]{1,0:T(8,128)S(1)}, f32[2192,128]{1,0:T(8,128)}, u32[]{:S(2)}) copy-start(f32[2192,128]{1,0:T(8,128)} %get-tuple-element.47) | copy-start | bytes 3366916
  37.6 27.2 %collective-permute-start.1 = (f32[2192,128]{1,0:T(8,128)}, f32[2192,128]{1,0:T(8,128)S(1)}, u32[]{:S(2)}, u32[]{:S(2)}) collective-permute-start(f32[2192,128]{1,0:T(8,128)} %get-tuple-element.52), channel_id=1, source_target_pairs={{0,2},{2,0},{4,6},{6,4},{8,10},{10,8},{12,14},{14,12},{16,18},{18,... | collective-permute-start | bytes 3366920 | tf_op jit(solution)/shard_map/ppermute | solution.py:74
  37.7 11.2 %copy-start.7 = (f32[2192,128]{1,0:T(8,128)S(1)}, f32[2192,128]{1,0:T(8,128)}, u32[]{:S(2)}) copy-start(f32[2192,128]{1,0:T(8,128)} %get-tuple-element.60) | copy-start | bytes 3366916
  37.7 19.0 %collective-permute-start.6 = (f32[1096,128]{1,0:T(8,128)S(1)}, f32[1096,128]{1,0:T(8,128)S(1)}, u32[]{:S(2)}, u32[]{:S(2)}) collective-permute-start(f32[1096,128]{1,0:T(8,128)S(1)} %slice_add_fusion.2), channel_id=1, source_target_pairs={{0,4},{2,6},{4,0},{6,2},{8,12},{10,14},{12,8},{14,10},{16,20},{18,... | collective-permute-start | bytes 1683464 | tf_op jit(solution)/shard_map/ppermute | solution.py:74
  44.8 14.7 %collective-permute-start.4 = (f32[1096,128]{1,0:T(8,128)S(1)}, f32[1096,128]{1,0:T(8,128)S(1)}, u32[]{:S(2)}, u32[]{:S(2)}) collective-permute-start(f32[1096,128]{1,0:T(8,128)S(1)} %fusion.2), channel_id=1, source_target_pairs={{0,8},{2,10},{4,12},{6,14},{24,16},{26,18},{28,20},{30,22},{1,9},{... | collective-permute-start | bytes 1683464 | tf_op jit(solution)/shard_map/ppermute | solution.py:74
  49.0 19.8 %collective-permute-start.10 = (f32[1096,128]{1,0:T(8,128)S(1)}, f32[1096,128]{1,0:T(8,128)S(1)}, u32[]{:S(2)}, u32[]{:S(2)}) collective-permute-start(f32[1096,128]{1,0:T(8,128)S(1)} %slice_add_fusion), channel_id=1, source_target_pairs={{0,4},{2,6},{4,0},{6,2},{8,12},{10,14},{12,8},{14,10},{16,20},{18,... | collective-permute-start | bytes 1683464 | tf_op jit(solution)/shard_map/ppermute | solution.py:74
  50.6 14.2 %copy-start.8 = (f32[2192,128]{1,0:T(8,128)S(1)}, f32[2192,128]{1,0:T(8,128)}, u32[]{:S(2)}) copy-start(f32[2192,128]{1,0:T(8,128)} %get-tuple-element.46) | copy-start | bytes 3366916
  56.7 100.1 %slice-start = ((s8[8912896]{0:T(1024)(128)(4,1)}), s8[4194304]{0:T(1024)(128)(4,1)S(1)}, s32[]{:S(2)}) async-start(s8[8912896]{0:T(1024)(128)(4,1)} %bitcast.10), calls=%async_computation | async-start | bytes 8388608
  59.5 14.1 %collective-permute-start.8 = (f32[1096,128]{1,0:T(8,128)S(1)}, f32[1096,128]{1,0:T(8,128)S(1)}, u32[]{:S(2)}, u32[]{:S(2)}) collective-permute-start(f32[1096,128]{1,0:T(8,128)S(1)} %fusion.1), channel_id=1, source_target_pairs={{0,8},{2,10},{4,12},{6,14},{24,16},{26,18},{28,20},{30,22},{1,9},{... | collective-permute-start | bytes 1683464 | tf_op jit(solution)/shard_map/ppermute | solution.py:74
  64.0 4.8 %collective-permute-start.7 = (f32[1096,128]{1,0:T(8,128)S(1)}, f32[1096,128]{1,0:T(8,128)S(1)}, u32[]{:S(2)}, u32[]{:S(2)}) collective-permute-start(f32[1096,128]{1,0:T(8,128)S(1)} %add.73), channel_id=1, source_target_pairs={{8,16},{10,18},{12,20},{14,22},{16,8},{18,10},{20,12},{22,14},{9,1... | collective-permute-start | bytes 1683464 | tf_op jit(solution)/shard_map/ppermute | solution.py:74
  64.7 92.1 %slice-start.1 = ((s8[8912896]{0:T(1024)(128)(4,1)}), s8[4194304]{0:T(1024)(128)(4,1)S(1)}, s32[]{:S(2)}) async-start(s8[8912896]{0:T(1024)(128)(4,1)} %bitcast.10), calls=%async_computation.1 | async-start | bytes 8388608
  64.9 15.4 %collective-permute-start.2 = (f32[1096,128]{1,0:T(8,128)S(1)}, f32[1096,128]{1,0:T(8,128)S(1)}, u32[]{:S(2)}, u32[]{:S(2)}) collective-permute-start(f32[1096,128]{1,0:T(8,128)S(1)} %get-tuple-element.85), channel_id=1, source_target_pairs={{0,4},{2,6},{4,0},{6,2},{8,12},{10,14},{12,8},{14,10},{16,20},{18,... | collective-permute-start | bytes 1683464 | tf_op jit(solution)/shard_map/ppermute | solution.py:74
  73.6 13.7 %copy-start.2 = (f32[1,1088,128]{2,1,0:T(8,128)S(1)}, f32[1,1088,128]{2,1,0:T(8,128)}, u32[]{:S(2)}) copy-start(f32[1,1088,128]{2,1,0:T(8,128)} %param.10) | copy-start | bytes 1671172
  73.6 13.7 %copy-start.3 = (f32[1088,128]{1,0:T(8,128)S(1)}, f32[1088,128]{1,0:T(8,128)}, u32[]{:S(2)}) copy-start(f32[1088,128]{1,0:T(8,128)} %get-tuple-element.65.refs_6_) | copy-start | bytes 1671172
  73.7 13.6 %copy-start = (s32[1152,128]{1,0:T(8,128)S(1)}, s32[1152,128]{1,0:T(8,128)}, u32[]{:S(2)}) copy-start(s32[1152,128]{1,0:T(8,128)} %get-tuple-element.66.refs_7_) | copy-start | bytes 1769476
  73.7 13.6 %copy-start.1 = (f32[1,1088,128]{2,1,0:T(8,128)S(1)}, f32[1,1088,128]{2,1,0:T(8,128)}, u32[]{:S(2)}) copy-start(f32[1,1088,128]{2,1,0:T(8,128)} %param.9) | copy-start | bytes 1671172
  73.8 13.5 %collective-permute-start.11 = (f32[1096,128]{1,0:T(8,128)S(1)}, f32[1096,128]{1,0:T(8,128)S(1)}, u32[]{:S(2)}, u32[]{:S(2)}) collective-permute-start(f32[1096,128]{1,0:T(8,128)S(1)} %add.77), channel_id=1, source_target_pairs={{0,8},{2,10},{4,12},{6,14},{8,0},{10,2},{12,4},{14,6},{16,24},{18,... | collective-permute-start | bytes 1683464 | tf_op jit(solution)/shard_map/ppermute | solution.py:74
  77.7 9.5 %collective-permute-start.12 = (f32[1096,128]{1,0:T(8,128)S(1)}, f32[1096,128]{1,0:T(8,128)S(1)}, u32[]{:S(2)}, u32[]{:S(2)}) collective-permute-start(f32[1096,128]{1,0:T(8,128)S(1)} %add.78), channel_id=1, source_target_pairs={{8,16},{10,18},{12,20},{14,22},{16,8},{18,10},{20,12},{22,14},{9,1... | collective-permute-start | bytes 1683464 | tf_op jit(solution)/shard_map/ppermute | solution.py:74
  87.3 69.5 %slice-start.2 = ((s8[8912896]{0:T(1024)(128)(4,1)}), s8[524288]{0:T(1024)(128)(4,1)S(1)}, s32[]{:S(2)}) async-start(s8[8912896]{0:T(1024)(128)(4,1)} %bitcast.10), calls=%async_computation.2 | async-start | bytes 1048576
  90.0 3.6 %collective-permute-start.13 = (f32[8,128]{1,0:T(8,128)S(1)}, f32[8,128]{1,0:T(8,128)S(1)}, u32[]{:S(2)}, u32[]{:S(2)}) collective-permute-start(f32[8,128]{1,0:T(8,128)S(1)} %get-tuple-element.68), channel_id=1, source_target_pairs={{0,1},{1,0},{2,3},{3,2},{4,5},{5,4},{6,7},{7,6},{8,9},{9,8},{10,11... | collective-permute-start | bytes 12296 | tf_op jit(solution)/shard_map/ppermute | solution.py:524
  93.6 11.3 %collective-permute-start.15 = (f32[1096,128]{1,0:T(8,128)S(1)}, f32[1096,128]{1,0:T(8,128)S(1)}, u32[]{:S(2)}, u32[]{:S(2)}) collective-permute-start(f32[1096,128]{1,0:T(8,128)S(1)} %add_dynamic-update-slice_fusion.refs_1_), channel_id=1, source_target_pairs={{0,8},{2,10},{4,12},{6,14},{8,0},{10,2},{12,4},{14,6},{16,24},{18,... | collective-permute-start | bytes 1683464 | tf_op jit(solution)/shard_map/ppermute | solution.py:74
  97.4 9.6 %collective-permute-start.17 = (f32[1096,128]{1,0:T(8,128)S(1)}, f32[1096,128]{1,0:T(8,128)S(1)}, u32[]{:S(2)}, u32[]{:S(2)}) collective-permute-start(f32[1096,128]{1,0:T(8,128)S(1)} %add_dynamic-update-slice_fusion.refs_1_), channel_id=1, source_target_pairs={{0,4},{2,6},{4,0},{6,2},{8,12},{10,14},{12,8},{14,10},{16,20},{18,... | collective-permute-start | bytes 1683464 | tf_op jit(solution)/shard_map/ppermute | solution.py:74
  98.9 8.1 %collective-permute-start.14 = (f32[1096,128]{1,0:T(8,128)S(1)}, f32[1096,128]{1,0:T(8,128)S(1)}, u32[]{:S(2)}, u32[]{:S(2)}) collective-permute-start(f32[1096,128]{1,0:T(8,128)S(1)} %add_dynamic-update-slice_fusion.refs_1_), channel_id=1, source_target_pairs={{8,16},{10,18},{12,20},{14,22},{16,8},{18,10},{20,12},{22,14},{9,1... | collective-permute-start | bytes 1683464 | tf_op jit(solution)/shard_map/ppermute | solution.py:74
  104.9 2.0 %collective-permute-start.16 = (f32[1096,128]{1,0:T(8,128)S(1)}, f32[1096,128]{1,0:T(8,128)S(1)}, u32[]{:S(2)}, u32[]{:S(2)}) collective-permute-start(f32[1096,128]{1,0:T(8,128)S(1)} %collective-permute-done.15.refs_5_), channel_id=1, source_target_pairs={{0,2},{2,0},{4,6},{6,4},{8,10},{10,8},{12,14},{14,12},{16,18},{18,... | collective-permute-start | bytes 1683464 | tf_op jit(solution)/shard_map/ppermute | solution.py:74
  104.9 4.9 %collective-permute-start.20 = (f32[1096,128]{1,0:T(8,128)S(1)}, f32[1096,128]{1,0:T(8,128)S(1)}, u32[]{:S(2)}, u32[]{:S(2)}) collective-permute-start(f32[1096,128]{1,0:T(8,128)S(1)} %collective-permute-done.15.refs_5_), channel_id=1, source_target_pairs={{8,16},{10,18},{12,20},{14,22},{16,8},{18,10},{20,12},{22,14},{9,1... | collective-permute-start | bytes 1683464 | tf_op jit(solution)/shard_map/ppermute | solution.py:74
  107.0 17.9 %collective-permute-start.21 = (f32[1096,128]{1,0:T(8,128)S(1)}, f32[1096,128]{1,0:T(8,128)S(1)}, u32[]{:S(2)}, u32[]{:S(2)}) collective-permute-start(f32[1096,128]{1,0:T(8,128)S(1)} %collective-permute-done.14), channel_id=1, source_target_pairs={{8,0},{10,2},{12,4},{14,6},{16,24},{18,26},{20,28},{22,30},{9,1},{... | collective-permute-start | bytes 1683464 | tf_op jit(solution)/shard_map/ppermute | solution.py:74
  108.3 16.7 %collective-permute-start.22 = (f32[1096,128]{1,0:T(8,128)S(1)}, f32[1096,128]{1,0:T(8,128)S(1)}, u32[]{:S(2)}, u32[]{:S(2)}) collective-permute-start(f32[1096,128]{1,0:T(8,128)S(1)} %collective-permute-done.15.refs_5_), channel_id=1, source_target_pairs={{0,4},{2,6},{4,0},{6,2},{8,12},{10,14},{12,8},{14,10},{16,20},{18,... | collective-permute-start | bytes 1683464 | tf_op jit(solution)/shard_map/ppermute | solution.py:74
  124.9 31.9 %copy-start.4 = (s32[136,128]{1,0:T(8,128)S(1)}, s32[136,128]{1,0:T(8,128)}, u32[]{:S(2)}) copy-start(s32[136,128]{1,0:T(8,128)} %get-tuple-element.45.position_ref) | copy-start | bytes 208900
  124.9 31.9 %copy-start.5 = (f32[3,2,1024]{2,1,0:T(2,128)S(1)}, f32[3,2,1024]{2,1,0:T(2,128)}, u32[]{:S(2)}) copy-start(f32[3,2,1024]{2,1,0:T(2,128)} %norm_ref.1) | copy-start | bytes 73732
  125.0 31.9 %copy-start.6 = (s32[3]{0:T(128)S(1)}, s32[3]{0:T(128)}, u32[]{:S(2)}) copy-start(s32[3]{0:T(128)} %pad_add_fusion.place_ref) | copy-start | bytes 40
  125.0 16.2 %collective-permute-start.24 = (f32[1096,128]{1,0:T(8,128)S(1)}, f32[1096,128]{1,0:T(8,128)S(1)}, u32[]{:S(2)}, u32[]{:S(2)}) collective-permute-start(f32[1096,128]{1,0:T(8,128)S(1)} %collective-permute-done.20), channel_id=1, source_target_pairs={{8,0},{10,2},{12,4},{14,6},{16,24},{18,26},{20,28},{22,30},{9,1},{... | collective-permute-start | bytes 1683464 | tf_op jit(solution)/shard_map/ppermute | solution.py:74
  126.3 15.0 %collective-permute-start.25 = (f32[1096,128]{1,0:T(8,128)S(1)}, f32[1096,128]{1,0:T(8,128)S(1)}, u32[]{:S(2)}, u32[]{:S(2)}) collective-permute-start(f32[1096,128]{1,0:T(8,128)S(1)} %add.81.refs_8_), channel_id=1, source_target_pairs={{0,4},{2,6},{4,0},{6,2},{8,12},{10,14},{12,8},{14,10},{16,20},{18,... | collective-permute-start | bytes 1683464 | tf_op jit(solution)/shard_map/ppermute | solution.py:74
  127.8 15.5 %collective-permute-start.18 = (f32[1096,128]{1,0:T(8,128)S(1)}, f32[1096,128]{1,0:T(8,128)S(1)}, u32[]{:S(2)}, u32[]{:S(2)}) collective-permute-start(f32[1096,128]{1,0:T(8,128)S(1)} %add_dynamic-update-slice_fusion.refs_1_), channel_id=1, source_target_pairs={{0,2},{2,0},{4,6},{6,4},{8,10},{10,8},{12,14},{14,12},{16,18},{18,... | collective-permute-start | bytes 1683464 | tf_op jit(solution)/shard_map/ppermute | solution.py:74
  127.8 15.5 %collective-permute-start.19 = (f32[1096,128]{1,0:T(8,128)S(1)}, f32[1096,128]{1,0:T(8,128)S(1)}, u32[]{:S(2)}, u32[]{:S(2)}) collective-permute-start(f32[1096,128]{1,0:T(8,128)S(1)} %collective-permute-done.17.refs_2_), channel_id=1, source_target_pairs={{0,2},{2,0},{4,6},{6,4},{8,10},{10,8},{12,14},{14,12},{16,18},{18,... | collective-permute-start | bytes 1683464 | tf_op jit(solution)/shard_map/ppermute | solution.py:74
  141.3 13.5 %collective-permute-start.26 = (f32[1096,128]{1,0:T(8,128)S(1)}, f32[1096,128]{1,0:T(8,128)S(1)}, u32[]{:S(2)}, u32[]{:S(2)}) collective-permute-start(f32[1096,128]{1,0:T(8,128)S(1)} %add.82.refs_10_), channel_id=1, source_target_pairs={{0,4},{2,6},{4,0},{6,2},{8,12},{10,14},{12,8},{14,10},{16,20},{18,... | collective-permute-start | bytes 1683464 | tf_op jit(solution)/shard_map/ppermute | solution.py:74
  142.9 12.0 %collective-permute-start.23 = (f32[1096,128]{1,0:T(8,128)S(1)}, f32[1096,128]{1,0:T(8,128)S(1)}, u32[]{:S(2)}, u32[]{:S(2)}) collective-permute-start(f32[1096,128]{1,0:T(8,128)S(1)} %collective-permute-done.22.refs_6_), channel_id=1, source_target_pairs={{0,2},{2,0},{4,6},{6,4},{8,10},{10,8},{12,14},{14,12},{16,18},{18,... | collective-permute-start | bytes 1683464 | tf_op jit(solution)/shard_map/ppermute | solution.py:74
  142.9 12.0 %collective-permute-start.29 = (f32[1096,128]{1,0:T(8,128)S(1)}, f32[1096,128]{1,0:T(8,128)S(1)}, u32[]{:S(2)}, u32[]{:S(2)}) collective-permute-start(f32[1096,128]{1,0:T(8,128)S(1)} %add.82.refs_10_), channel_id=1, source_target_pairs={{0,2},{2,0},{4,6},{6,4},{8,10},{10,8},{12,14},{14,12},{16,18},{18,... | collective-permute-start | bytes 1683464 | tf_op jit(solution)/shard_map/ppermute | solution.py:74
  143.4 11.5 %collective-permute-start.27 = (f32[1096,128]{1,0:T(8,128)S(1)}, f32[1096,128]{1,0:T(8,128)S(1)}, u32[]{:S(2)}, u32[]{:S(2)}) collective-permute-start(f32[1096,128]{1,0:T(8,128)S(1)} %add.81.refs_8_), channel_id=1, source_target_pairs={{0,2},{2,0},{4,6},{6,4},{8,10},{10,8},{12,14},{14,12},{16,18},{18,... | collective-permute-start | bytes 1683464 | tf_op jit(solution)/shard_map/ppermute | solution.py:74
  143.4 11.5 %collective-permute-start.28 = (f32[1096,128]{1,0:T(8,128)S(1)}, f32[1096,128]{1,0:T(8,128)S(1)}, u32[]{:S(2)}, u32[]{:S(2)}) collective-permute-start(f32[1096,128]{1,0:T(8,128)S(1)} %collective-permute-done.25.refs_9_), channel_id=1, source_target_pairs={{0,2},{2,0},{4,6},{6,4},{8,10},{10,8},{12,14},{14,12},{16,18},{18,... | collective-permute-start | bytes 1683464 | tf_op jit(solution)/shard_map/ppermute | solution.py:74
  154.8 2.0 %collective-permute-start.30 = (f32[1096,128]{1,0:T(8,128)S(1)}, f32[1096,128]{1,0:T(8,128)S(1)}, u32[]{:S(2)}, u32[]{:S(2)}) collective-permute-start(f32[1096,128]{1,0:T(8,128)S(1)} %collective-permute-done.26.refs_11_), channel_id=1, source_target_pairs={{0,2},{2,0},{4,6},{6,4},{8,10},{10,8},{12,14},{14,12},{16,18},{18,... | collective-permute-start | bytes 1683464 | tf_op jit(solution)/shard_map/ppermute | solution.py:74

commit v10 on v8

--- a/solution.py
+++ b/solution.py
@@ -122,46 +122,40 @@
 
 
 def gather(plan, block):
-    found = {}
-
-    def add(far_z, line):
-        for far_x, value in enumerate(line):
-            found[far_z, far_x, 0] = value
+    found = []
 
     def along_x(value):
         return line_gather(plan, "x", plan.nx, value)
 
-    def swapped(*far_zs):
-        for far_z in far_zs:
-            for far_x in range(plan.nx):
-                if (far_z, far_x, 1) not in found:
-                    found[far_z, far_x, 1] = plan.swap(found[far_z, far_x, 0])
+    def add(far_z, line, skip=0):
+        for far_x, value in enumerate(line):
+            found.append((value, [(far_z, far_x, 0)]))
+        for far_x, value in enumerate(line):
+            if far_x >= skip:
+                found.append((plan.swap(value), [(far_z, far_x, 1)]))
 
     if plan.nz != 4:
         for far_z, value in enumerate(line_gather(plan, "z", plan.nz, block)):
             add(far_z, along_x(value))
-            swapped(far_z)
-        return list(found.items())
+        return found
     line = along_x(block)
     pair = plan.send(block, "z", PAIRS)
     three = plan.send(block, "z", MIDDLE)
-    pair, three, *line = together(pair, three, *line)
-    add(0, line)
-    line = along_x(pair)
+    both, three, *line = together(jnp.concatenate([block, pair]), three, *line)
+    line_pair = along_x(pair)
     two = plan.send(pair, "z", MIDDLE)
     out_two = plan.send(three, "z", OUTWARD)
-    swapped(0)
-    two, out_two, *line = together(two, out_two, *line)
-    add(1, line)
-    line = along_x(two + out_two)
+    two, out_two, *line_pair = together(two, out_two, *line_pair)
+    found.append((both, [(0, 0, 0), (1, 0, 0)]))
+    found.append((plan.swap(both), [(0, 0, 1), (1, 0, 1)]))
+    line_two = along_x(two + out_two)
     out_three = plan.send(two, "z", OUTWARD)
-    swapped(1)
-    out_three, *line = together(out_three, *line)
-    add(2, line)
+    out_three, *line_two = together(out_three, *line_two)
+    add(0, line, 1)
+    add(1, line_pair, 1)
+    add(2, line_two)
     add(3, along_x(three + out_three))
-    swapped(2)
-    swapped(3)
-    return list(found.items())
+    return [(value, slots) for value, slots in found if slots[0][1:] != (0, 0) or slots[0][0] > 1 or len(slots) > 1]
 
 
 def line_gather(plan, axis, count, value):
@@ -412,8 +406,9 @@
 
     @pl.when(now == 0)
     def _():
-        for piece, slot in zip(pieces, slots):
-            held[pl.ds(plan.start(*slot), plan.block), :] = piece[...]
+        for piece, parts in zip(pieces, slots):
+            for i, slot in enumerate(parts):
+                held[pl.ds(plan.start(*slot), plan.block), :] = piece[i * plan.block : (i + 1) * plan.block, :]
         total = jnp.zeros((plan.tail, LANE), jnp.float32)
         for z in range(plan.nz):
             for x in range(plan.nx):
@@ -525,7 +520,7 @@
         hop *= 2
     block = lax.dynamic_update_slice(block, block[plan.own :] + stats, (plan.own, 0))
     found = gather(plan, block)
-    slots, pieces = [slot for slot, _ in found], [piece for _, piece in found]
+    pieces, slots = [piece for piece, _ in found], [parts for _, parts in found]
     new_weights, new_state, trust_ratios = finish(plan, my_place, position, norm_state, weights, pieces, slots)
     return (new_weights, new_first[None], new_second[None], new_state, trust_ratios)
 

time: 174 us -> 175 us (level)
  starting transfers between devices: 37.9 us -> 40.8 us
    ppermute x30 -> x29, starting transfers between devices: 36.4 us -> 39.2 us  [send(): return lax.ppermute(value, 'dp', every)]
    ppermute x30 -> x29, waiting for transfers between devices: 77.9 us -> 76.7 us  [send(): return lax.ppermute(value, 'dp', every)]
  transfers between devices with their start and end apart: 31 -> 30, of which waited for: 16 -> 17; matrix products, arithmetic and copies ran while one was open for 1% -> 1% of each run, Pallas kernels for 4% -> 4%
where the time goes in v10:
time: 175 us; the launch traced here: 174 us
  waiting for transfers between devices  78.8 us (45%)
  Pallas kernels  50.9 us (29%)
  starting transfers between devices  40.8 us (23%)
  other arithmetic  2.79 us (2%)
    ppermute x29, waiting for transfers between devices, send(): return lax.ppermute(value, 'dp', every)  76.7 us
    ppermute x29, starting transfers between devices, send(): return lax.ppermute(value, 'dp', every)  39.2 us
    pallas_call x1, Pallas kernels, place(): pl.pallas_call(functools.partial(place_kernel, plan), out_shape=[jax.Shap...  22.2 us
    pallas_call x1, Pallas kernels, finish(): pl.pallas_call(functools.partial(finish_kernel, plan, tile, slots), grid=...  19.6 us
    pallas_call x1, Pallas kernels, owned(): pl.pallas_call(functools.partial(owned_kernel, plan), out_shape=[jax.Shap...  6.31 us
  transfers between devices with their start and end apart: 30, of which 17 were waited for; matrix products, arithmetic and copies ran while one was open for 1% of the time, Pallas kernels for 4%

profile of v10, /device:TPU:0, one launch (start us, length us, event | category | flops | bytes accessed | tf_op | source)
XLA Modules:
  0.0 174.4 jit_solution(4525616565891321874)
XLA Ops:
  0.7 0.7 pad_add_fusion.place_ref
  1.3 22.2 %place_gradients.1 = (f32[2192,128]{1,0:T(8,128)}, f32[2192,128]{1,0:T(8,128)}, f32[2192,128]{1,0:T(8,128)}, f32[2192,128]{1,0:T(8,128)}, f32[2192,128]{1,0:T(8,...) custom-call(s32[3]{0:T(128)} %pad_add_fusion.place_ref, ...), custom_call_target="tpu_custom_call" | custom-call | tf_op jit(solution)/shard_map/place_gradients/pallas_call | solution.py:252
  23.6 0.5 collective-permute-start
  24.1 2.6 %collective-permute-done = f32[2192,128]{1,0:T(8,128)S(1)} collective-permute-done((f32[2192,128]{1,0:T(8,128)}, f32[2192,128]{1,0:T(8,128)S(1)}, u32[]{:S(2)}, u32[]{:S(2)}) %collective-permute-start) | collective-permute-done | bytes 1122336 | tf_op jit(solution)/shard_map/ppermute | solution.py:74
  26.7 1.1 slice_add_fusion.7
  27.8 0.4 collective-permute-start.5
  28.3 0.1 collective-permute-start.9
  28.4 2.9 %collective-permute-start.3 = (f32[1096,128]{1,0:T(8,128)S(1)}, f32[1096,128]{1,0:T(8,128)S(1)}, u32[]{:S(2)}, u32[]{:S(2)}) collective-permute-start(f32[1096,128]{1,0:T(8,128)S(1)} %slice_add_fusion.7), channel_id=1, source_target_pairs={{0,4},{2,6},{4,0},{6,2},{8,12},{10,14},{12,8},{14,10},{16,20},{18,... | collective-permute-start | bytes 1683464 | tf_op jit(solution)/shard_map/ppermute | solution.py:74
  31.3 6.3 %owned_weights.1 = (f32[1088,128]{1,0:T(8,128)}, s32[1152,128]{1,0:T(8,128)}) custom-call(s32[3]{0:T(128)} %pad_add_fusion.place_ref, s32[136,128]{1,0:T(8,128)} %bitcast.16, f32[17408,128]{1,0:T(8,128)} %weights_ref.3), custom_call_target="tpu_custom_call" | custom-call | bytes 20971520 | tf_op jit(solution)/shard_map/owned_weights/pallas_call | solution.py:330
  37.6 0.1 collective-permute-start.1
  37.7 0.1 slice_add_fusion.2
  37.8 0.2 collective-permute-start.6
  38.0 6.8 %collective-permute-done.3 = f32[1096,128]{1,0:T(8,128)S(1)} collective-permute-done((f32[1096,128]{1,0:T(8,128)S(1)}, f32[1096,128]{1,0:T(8,128)S(1)}, u32[]{:S(2)}, u32[]{:S(2)}) %collective-permute-start.3) | collective-permute-done | bytes 561184 | tf_op jit(solution)/shard_map/ppermute | solution.py:74
  44.8 0.1 fusion.2
  44.8 4.1 %collective-permute-start.4 = (f32[1096,128]{1,0:T(8,128)S(1)}, f32[1096,128]{1,0:T(8,128)S(1)}, u32[]{:S(2)}, u32[]{:S(2)}) collective-permute-start(f32[1096,128]{1,0:T(8,128)S(1)} %fusion.2), channel_id=1, source_target_pairs={{0,8},{2,10},{4,12},{6,14},{24,16},{26,18},{28,20},{30,22},{1,9},{... | collective-permute-start | bytes 1683464 | tf_op jit(solution)/shard_map/ppermute | solution.py:74
  49.0 0.1 slice_add_fusion
  49.0 1.6 collective-permute-start.10
  50.6 6.2 %collective-permute-done.6 = f32[1096,128]{1,0:T(8,128)S(1)} collective-permute-done((f32[1096,128]{1,0:T(8,128)S(1)}, f32[1096,128]{1,0:T(8,128)S(1)}, u32[]{:S(2)}, u32[]{:S(2)}) %collective-permute-start.6) | collective-permute-done | bytes 561184 | tf_op jit(solution)/shard_map/ppermute | solution.py:74
  56.8 0.1 fusion.1
  56.9 2.6 %collective-permute-done.4 = f32[1096,128]{1,0:T(8,128)S(1)} collective-permute-done((f32[1096,128]{1,0:T(8,128)S(1)}, f32[1096,128]{1,0:T(8,128)S(1)}, u32[]{:S(2)}, u32[]{:S(2)}) %collective-permute-start.4) | collective-permute-done | bytes 561184 | tf_op jit(solution)/shard_map/ppermute | solution.py:74
  59.5 4.4 %collective-permute-start.8 = (f32[1096,128]{1,0:T(8,128)S(1)}, f32[1096,128]{1,0:T(8,128)S(1)}, u32[]{:S(2)}, u32[]{:S(2)}) collective-permute-start(f32[1096,128]{1,0:T(8,128)S(1)} %fusion.1), channel_id=1, source_target_pairs={{0,8},{2,10},{4,12},{6,14},{24,16},{26,18},{28,20},{30,22},{1,9},{... | collective-permute-start | bytes 1683464 | tf_op jit(solution)/shard_map/ppermute | solution.py:74
  64.0 0.1 add.73
  64.0 0.8 collective-permute-start.7
  64.9 0.1 slice_add_fusion.5
  65.1 0.0 slice-start.1
  65.1 1.6 collective-permute-start.2
  66.6 2.2 %collective-permute-done.10 = f32[1096,128]{1,0:T(8,128)S(1)} collective-permute-done((f32[1096,128]{1,0:T(8,128)S(1)}, f32[1096,128]{1,0:T(8,128)S(1)}, u32[]{:S(2)}, u32[]{:S(2)}) %collective-permute-start.10) | collective-permute-done | bytes 561184 | tf_op jit(solution)/shard_map/ppermute | solution.py:74
  68.8 0.1 fusion
  68.9 4.7 %collective-permute-done.8 = f32[1096,128]{1,0:T(8,128)S(1)} collective-permute-done((f32[1096,128]{1,0:T(8,128)S(1)}, f32[1096,128]{1,0:T(8,128)S(1)}, u32[]{:S(2)}, u32[]{:S(2)}) %collective-permute-start.8) | collective-permute-done | bytes 561184 | tf_op jit(solution)/shard_map/ppermute | solution.py:74
  73.6 0.1 add.78
  73.7 0.1 add.77
  73.8 4.2 %collective-permute-start.11 = (f32[1096,128]{1,0:T(8,128)S(1)}, f32[1096,128]{1,0:T(8,128)S(1)}, u32[]{:S(2)}, u32[]{:S(2)}) collective-permute-start(f32[1096,128]{1,0:T(8,128)S(1)} %add.77), channel_id=1, source_target_pairs={{0,8},{2,10},{4,12},{6,14},{8,0},{10,2},{12,4},{14,6},{16,24},{18,... | collective-permute-start | bytes 1683464 | tf_op jit(solution)/shard_map/ppermute | solution.py:74
  78.0 0.7 collective-permute-start.12
  78.7 1.7 collective-permute-done.2.refs_1_
  80.4 7.2 %collective-permute-done.11.refs_2_ = f32[1096,128]{1,0:T(8,128)S(1)} collective-permute-done((f32[1096,128]{1,0:T(8,128)S(1)}, f32[1096,128]{1,0:T(8,128)S(1)}, u32[]{:S(2)}, u32[]{:S(2)}) %collective-permute-start.11) | collective-permute-done | bytes 561184 | tf_op jit(solution)/shard_map/ppermute | solution.py:74
  87.6 2.7 %moments.1 = (f32[1088,128]{1,0:T(8,128)}, f32[1088,128]{1,0:T(8,128)}, f32[1096,128]{1,0:T(8,128)S(1)}, f32[8,128]{1,0:T(8,128)S(1)}) custom-call(f32[1096,128]{1,0:T(8,128)S(1)} %get-tuple-element.82.refs_0_, f32[1096,128]{1,0:T(8,128)S(1)} %collective-permute-done.2.refs_1_, f32[1096,128]{1,0:T(8,128)S(1)} %collective-permute-done.11.refs_2_, ...), custom_call_target="tpu_custom_call" | custom-call | tf_op jit(solution)/shard_map/moments/pallas_call | solution.py:385
  90.3 1.5 collective-permute-start.13
  91.8 2.1 %collective-permute-done.13 = f32[8,128]{1,0:T(8,128)S(1)} collective-permute-done((f32[8,128]{1,0:T(8,128)S(1)}, f32[8,128]{1,0:T(8,128)S(1)}, u32[]{:S(2)}, u32[]{:S(2)}) %collective-permute-start.13) | collective-permute-done | bytes 4128 | tf_op jit(solution)/shard_map/ppermute | solution.py:519
  93.9 3.8 %collective-permute-start.14 = (f32[1096,128]{1,0:T(8,128)S(1)}, f32[1096,128]{1,0:T(8,128)S(1)}, u32[]{:S(2)}, u32[]{:S(2)}) collective-permute-start(f32[1096,128]{1,0:T(8,128)S(1)} %add_dynamic-update-slice_fusion), channel_id=1, source_target_pairs={{0,8},{2,10},{4,12},{6,14},{8,0},{10,2},{12,4},{14,6},{16,24},{18,... | collective-permute-start | bytes 1683464 | tf_op jit(solution)/shard_map/ppermute | solution.py:74
  97.7 1.5 collective-permute-start.16
  99.2 0.7 collective-permute-start.15
  99.8 5.4 %collective-permute-done.14 = f32[1096,128]{1,0:T(8,128)S(1)} collective-permute-done((f32[1096,128]{1,0:T(8,128)S(1)}, f32[1096,128]{1,0:T(8,128)S(1)}, u32[]{:S(2)}, u32[]{:S(2)}) %collective-permute-start.14) | collective-permute-done | bytes 561184 | tf_op jit(solution)/shard_map/ppermute | solution.py:74
  105.2 0.1 pad_maximum_fusion.refs_0_
  105.3 5.8 %collective-permute-done.16.refs_2_ = f32[1096,128]{1,0:T(8,128)S(1)} collective-permute-done((f32[1096,128]{1,0:T(8,128)S(1)}, f32[1096,128]{1,0:T(8,128)S(1)}, u32[]{:S(2)}, u32[]{:S(2)}) %collective-permute-start.16) | collective-permute-done | bytes 561184 | tf_op jit(solution)/shard_map/ppermute | solution.py:74
  111.1 1.5 collective-permute-start.21
  112.6 0.7 collective-permute-start.19
  113.3 1.3 collective-permute-start.20
  114.6 8.1 %collective-permute-done.21.refs_4_ = f32[1096,128]{1,0:T(8,128)S(1)} collective-permute-done((f32[1096,128]{1,0:T(8,128)S(1)}, f32[1096,128]{1,0:T(8,128)S(1)}, u32[]{:S(2)}, u32[]{:S(2)}) %collective-permute-start.21) | collective-permute-done | bytes 561184 | tf_op jit(solution)/shard_map/ppermute | solution.py:74
  122.7 5.1 %collective-permute-done.20 = f32[1096,128]{1,0:T(8,128)S(1)} collective-permute-done((f32[1096,128]{1,0:T(8,128)S(1)}, f32[1096,128]{1,0:T(8,128)S(1)}, u32[]{:S(2)}, u32[]{:S(2)}) %collective-permute-start.20) | collective-permute-done | bytes 561184 | tf_op jit(solution)/shard_map/ppermute | solution.py:74
  127.8 0.1 add.81.refs_6_
  127.9 3.5 %collective-permute-start.24 = (f32[1096,128]{1,0:T(8,128)S(1)}, f32[1096,128]{1,0:T(8,128)S(1)}, u32[]{:S(2)}, u32[]{:S(2)}) collective-permute-start(f32[1096,128]{1,0:T(8,128)S(1)} %add.81.refs_6_), channel_id=1, source_target_pairs={{0,4},{2,6},{4,0},{6,2},{8,12},{10,14},{12,8},{14,10},{16,20},{18,... | collective-permute-start | bytes 1683464 | tf_op jit(solution)/shard_map/ppermute | solution.py:74
  131.4 1.3 collective-permute-start.23
  132.7 0.1 collective-permute-start.18
  132.7 0.5 collective-permute-start.17
  133.2 0.1 collective-permute-start.22
  133.3 9.2 %collective-permute-done.24.refs_7_ = f32[1096,128]{1,0:T(8,128)S(1)} collective-permute-done((f32[1096,128]{1,0:T(8,128)S(1)}, f32[1096,128]{1,0:T(8,128)S(1)}, u32[]{:S(2)}, u32[]{:S(2)}) %collective-permute-start.24) | collective-permute-done | bytes 561184 | tf_op jit(solution)/shard_map/ppermute | solution.py:74
  142.6 0.3 collective-permute-done.23
  142.8 0.1 add.82.refs_10_
  142.9 2.3 %collective-permute-start.27 = (f32[1096,128]{1,0:T(8,128)S(1)}, f32[1096,128]{1,0:T(8,128)S(1)}, u32[]{:S(2)}, u32[]{:S(2)}) collective-permute-start(f32[1096,128]{1,0:T(8,128)S(1)} %add.82.refs_10_), channel_id=1, source_target_pairs={{0,4},{2,6},{4,0},{6,2},{8,12},{10,14},{12,8},{14,10},{16,20},{18,... | collective-permute-start | bytes 1683464 | tf_op jit(solution)/shard_map/ppermute | solution.py:74
  145.2 0.5 collective-permute-start.25
  145.7 0.1 collective-permute-start.26
  145.8 7.0 %collective-permute-done.27.refs_11_ = f32[1096,128]{1,0:T(8,128)S(1)} collective-permute-done((f32[1096,128]{1,0:T(8,128)S(1)}, f32[1096,128]{1,0:T(8,128)S(1)}, u32[]{:S(2)}, u32[]{:S(2)}) %collective-permute-start.27) | collective-permute-done | bytes 561184 | tf_op jit(solution)/shard_map/ppermute | solution.py:74
  152.8 1.9 %collective-permute-done.29.refs_13_ = f32[1096,128]{1,0:T(8,128)S(1)} collective-permute-done((f32[1096,128]{1,0:T(8,128)S(1)}, f32[1096,128]{1,0:T(8,128)S(1)}, u32[]{:S(2)}, u32[]{:S(2)}) %collective-permute-start.29) | collective-permute-done | bytes 561184 | tf_op jit(solution)/shard_map/ppermute | solution.py:74
  154.8 19.6 %new_weights.1 = (f32[17408,128]{1,0:T(8,128)}, f32[3,2,1024]{2,1,0:T(2,128)}, f32[7]{0:T(128)}) custom-call(s32[3]{0:T(128)S(1)} %copy-done.6, s32[136,128]{1,0:T(8,128)S(1)} %copy-done.4, f32[3,2,1024]{2,1,0:T(2,128)S(1)} %copy-done.5, f32[17408,128]{1,0:T(8,128)S(1)} %bitcast.11, f32[2192,128]{1,0:T(8,128)S(1)} %pad_maximum_fusion.refs_0_, ...), custom_call_target="tpu_custom_call" | custom-call | tf_op jit(solution)/shard_map/new_weights/pallas_call | solution.py:464
  (44 shorter events, 0.1 us)
Async XLA Ops:
  23.6 3.1 %collective-permute-start = (f32[2192,128]{1,0:T(8,128)}, f32[2192,128]{1,0:T(8,128)S(1)}, u32[]{:S(2)}, u32[]{:S(2)}) collective-permute-start(f32[2192,128]{1,0:T(8,128)} %get-tuple-element.46), channel_id=1, source_target_pairs={{0,2},{2,0},{4,6},{6,4},{8,10},{10,8},{12,14},{14,12},{16,18},{18,... | collective-permute-start | bytes 3366920 | tf_op jit(solution)/shard_map/ppermute | solution.py:74
  27.8 9.9 %copy-start.9 = (f32[2192,128]{1,0:T(8,128)S(1)}, f32[2192,128]{1,0:T(8,128)}, u32[]{:S(2)}) copy-start(f32[2192,128]{1,0:T(8,128)} %get-tuple-element.52) | copy-start | bytes 3366916
  27.8 9.8 %collective-permute-start.5 = (f32[2192,128]{1,0:T(8,128)}, f32[2192,128]{1,0:T(8,128)S(1)}, u32[]{:S(2)}, u32[]{:S(2)}) collective-permute-start(f32[2192,128]{1,0:T(8,128)} %get-tuple-element.53), channel_id=1, source_target_pairs={{0,2},{2,0},{4,6},{6,4},{8,10},{10,8},{12,14},{14,12},{16,18},{18,... | collective-permute-start | bytes 3366920 | tf_op jit(solution)/shard_map/ppermute | solution.py:74
  28.3 20.7 %collective-permute-start.9 = (f32[2192,128]{1,0:T(8,128)}, f32[2192,128]{1,0:T(8,128)S(1)}, u32[]{:S(2)}, u32[]{:S(2)}) collective-permute-start(f32[2192,128]{1,0:T(8,128)} %get-tuple-element.59), channel_id=1, source_target_pairs={{0,2},{2,0},{4,6},{6,4},{8,10},{10,8},{12,14},{14,12},{16,18},{18,... | collective-permute-start | bytes 3366920 | tf_op jit(solution)/shard_map/ppermute | solution.py:74
  28.4 16.4 %collective-permute-start.3 = (f32[1096,128]{1,0:T(8,128)S(1)}, f32[1096,128]{1,0:T(8,128)S(1)}, u32[]{:S(2)}, u32[]{:S(2)}) collective-permute-start(f32[1096,128]{1,0:T(8,128)S(1)} %slice_add_fusion.7), channel_id=1, source_target_pairs={{0,4},{2,6},{4,0},{6,2},{8,12},{10,14},{12,8},{14,10},{16,20},{18,... | collective-permute-start | bytes 1683464 | tf_op jit(solution)/shard_map/ppermute | solution.py:74
  37.6 7.2 %copy-start.10 = (f32[2192,128]{1,0:T(8,128)S(1)}, f32[2192,128]{1,0:T(8,128)}, u32[]{:S(2)}) copy-start(f32[2192,128]{1,0:T(8,128)} %get-tuple-element.45) | copy-start | bytes 3366916
  37.6 27.3 %collective-permute-start.1 = (f32[2192,128]{1,0:T(8,128)}, f32[2192,128]{1,0:T(8,128)S(1)}, u32[]{:S(2)}, u32[]{:S(2)}) collective-permute-start(f32[2192,128]{1,0:T(8,128)} %get-tuple-element.50), channel_id=1, source_target_pairs={{0,2},{2,0},{4,6},{6,4},{8,10},{10,8},{12,14},{14,12},{16,18},{18,... | collective-permute-start | bytes 3366920 | tf_op jit(solution)/shard_map/ppermute | solution.py:74
  37.8 11.2 %copy-start.7 = (f32[2192,128]{1,0:T(8,128)S(1)}, f32[2192,128]{1,0:T(8,128)}, u32[]{:S(2)}) copy-start(f32[2192,128]{1,0:T(8,128)} %get-tuple-element.58) | copy-start | bytes 3366916
  37.8 19.0 %collective-permute-start.6 = (f32[1096,128]{1,0:T(8,128)S(1)}, f32[1096,128]{1,0:T(8,128)S(1)}, u32[]{:S(2)}, u32[]{:S(2)}) collective-permute-start(f32[1096,128]{1,0:T(8,128)S(1)} %slice_add_fusion.2), channel_id=1, source_target_pairs={{0,4},{2,6},{4,0},{6,2},{8,12},{10,14},{12,8},{14,10},{16,20},{18,... | collective-permute-start | bytes 1683464 | tf_op jit(solution)/shard_map/ppermute | solution.py:74
  44.8 14.7 %collective-permute-start.4 = (f32[1096,128]{1,0:T(8,128)S(1)}, f32[1096,128]{1,0:T(8,128)S(1)}, u32[]{:S(2)}, u32[]{:S(2)}) collective-permute-start(f32[1096,128]{1,0:T(8,128)S(1)} %fusion.2), channel_id=1, source_target_pairs={{0,8},{2,10},{4,12},{6,14},{24,16},{26,18},{28,20},{30,22},{1,9},{... | collective-permute-start | bytes 1683464 | tf_op jit(solution)/shard_map/ppermute | solution.py:74
  49.0 19.8 %collective-permute-start.10 = (f32[1096,128]{1,0:T(8,128)S(1)}, f32[1096,128]{1,0:T(8,128)S(1)}, u32[]{:S(2)}, u32[]{:S(2)}) collective-permute-start(f32[1096,128]{1,0:T(8,128)S(1)} %slice_add_fusion), channel_id=1, source_target_pairs={{0,4},{2,6},{4,0},{6,2},{8,12},{10,14},{12,8},{14,10},{16,20},{18,... | collective-permute-start | bytes 1683464 | tf_op jit(solution)/shard_map/ppermute | solution.py:74
  56.8 8.1 %copy-start.8 = (f32[2192,128]{1,0:T(8,128)S(1)}, f32[2192,128]{1,0:T(8,128)}, u32[]{:S(2)}) copy-start(f32[2192,128]{1,0:T(8,128)} %get-tuple-element.44) | copy-start | bytes 3366916
  59.5 14.1 %collective-permute-start.8 = (f32[1096,128]{1,0:T(8,128)S(1)}, f32[1096,128]{1,0:T(8,128)S(1)}, u32[]{:S(2)}, u32[]{:S(2)}) collective-permute-start(f32[1096,128]{1,0:T(8,128)S(1)} %fusion.1), channel_id=1, source_target_pairs={{0,8},{2,10},{4,12},{6,14},{24,16},{26,18},{28,20},{30,22},{1,9},{... | collective-permute-start | bytes 1683464 | tf_op jit(solution)/shard_map/ppermute | solution.py:74
  64.0 90.8 %slice-start = ((s8[8912896]{0:T(1024)(128)(4,1)}), s8[4194304]{0:T(1024)(128)(4,1)S(1)}, s32[]{:S(2)}) async-start(s8[8912896]{0:T(1024)(128)(4,1)} %bitcast.10), calls=%async_computation | async-start | bytes 8388608
  64.0 4.9 %collective-permute-start.7 = (f32[1096,128]{1,0:T(8,128)S(1)}, f32[1096,128]{1,0:T(8,128)S(1)}, u32[]{:S(2)}, u32[]{:S(2)}) collective-permute-start(f32[1096,128]{1,0:T(8,128)S(1)} %add.73), channel_id=1, source_target_pairs={{8,16},{10,18},{12,20},{14,22},{16,8},{18,10},{20,12},{22,14},{9,1... | collective-permute-start | bytes 1683464 | tf_op jit(solution)/shard_map/ppermute | solution.py:74
  64.9 22.7 %copy-start.2 = (f32[1,1088,128]{2,1,0:T(8,128)S(1)}, f32[1,1088,128]{2,1,0:T(8,128)}, u32[]{:S(2)}) copy-start(f32[1,1088,128]{2,1,0:T(8,128)} %param.10) | copy-start | bytes 1671172
  64.9 22.6 %copy-start.3 = (f32[1088,128]{1,0:T(8,128)S(1)}, f32[1088,128]{1,0:T(8,128)}, u32[]{:S(2)}) copy-start(f32[1088,128]{1,0:T(8,128)} %get-tuple-element.63.refs_6_) | copy-start | bytes 1671172
  65.1 89.7 %slice-start.1 = ((s8[8912896]{0:T(1024)(128)(4,1)}), s8[4194304]{0:T(1024)(128)(4,1)S(1)}, s32[]{:S(2)}) async-start(s8[8912896]{0:T(1024)(128)(4,1)} %bitcast.10), calls=%async_computation.1 | async-start | bytes 8388608
  65.1 15.3 %collective-permute-start.2 = (f32[1096,128]{1,0:T(8,128)S(1)}, f32[1096,128]{1,0:T(8,128)S(1)}, u32[]{:S(2)}, u32[]{:S(2)}) collective-permute-start(f32[1096,128]{1,0:T(8,128)S(1)} %get-tuple-element.81), channel_id=1, source_target_pairs={{0,4},{2,6},{4,0},{6,2},{8,12},{10,14},{12,8},{14,10},{16,20},{18,... | collective-permute-start | bytes 1683464 | tf_op jit(solution)/shard_map/ppermute | solution.py:74
  73.7 13.8 %copy-start = (s32[1152,128]{1,0:T(8,128)S(1)}, s32[1152,128]{1,0:T(8,128)}, u32[]{:S(2)}) copy-start(s32[1152,128]{1,0:T(8,128)} %get-tuple-element.64.refs_7_) | copy-start | bytes 1769476
  73.7 13.8 %copy-start.1 = (f32[1,1088,128]{2,1,0:T(8,128)S(1)}, f32[1,1088,128]{2,1,0:T(8,128)}, u32[]{:S(2)}) copy-start(f32[1,1088,128]{2,1,0:T(8,128)} %param.9) | copy-start | bytes 1671172
  73.8 13.7 %collective-permute-start.11 = (f32[1096,128]{1,0:T(8,128)S(1)}, f32[1096,128]{1,0:T(8,128)S(1)}, u32[]{:S(2)}, u32[]{:S(2)}) collective-permute-start(f32[1096,128]{1,0:T(8,128)S(1)} %add.77), channel_id=1, source_target_pairs={{0,8},{2,10},{4,12},{6,14},{8,0},{10,2},{12,4},{14,6},{16,24},{18,... | collective-permute-start | bytes 1683464 | tf_op jit(solution)/shard_map/ppermute | solution.py:74
  78.0 9.5 %collective-permute-start.12 = (f32[1096,128]{1,0:T(8,128)S(1)}, f32[1096,128]{1,0:T(8,128)S(1)}, u32[]{:S(2)}, u32[]{:S(2)}) collective-permute-start(f32[1096,128]{1,0:T(8,128)S(1)} %add.78), channel_id=1, source_target_pairs={{8,16},{10,18},{12,20},{14,22},{16,8},{18,10},{20,12},{22,14},{9,1... | collective-permute-start | bytes 1683464 | tf_op jit(solution)/shard_map/ppermute | solution.py:74
  87.6 67.2 %slice-start.2 = ((s8[8912896]{0:T(1024)(128)(4,1)}), s8[524288]{0:T(1024)(128)(4,1)S(1)}, s32[]{:S(2)}) async-start(s8[8912896]{0:T(1024)(128)(4,1)} %bitcast.10), calls=%async_computation.2 | async-start | bytes 1048576
  90.3 3.6 %collective-permute-start.13 = (f32[8,128]{1,0:T(8,128)S(1)}, f32[8,128]{1,0:T(8,128)S(1)}, u32[]{:S(2)}, u32[]{:S(2)}) collective-permute-start(f32[8,128]{1,0:T(8,128)S(1)} %get-tuple-element.66), channel_id=1, source_target_pairs={{0,1},{1,0},{2,3},{3,2},{4,5},{5,4},{6,7},{7,6},{8,9},{9,8},{10,11... | collective-permute-start | bytes 12296 | tf_op jit(solution)/shard_map/ppermute | solution.py:519
  93.9 11.3 %collective-permute-start.14 = (f32[1096,128]{1,0:T(8,128)S(1)}, f32[1096,128]{1,0:T(8,128)S(1)}, u32[]{:S(2)}, u32[]{:S(2)}) collective-permute-start(f32[1096,128]{1,0:T(8,128)S(1)} %add_dynamic-update-slice_fusion), channel_id=1, source_target_pairs={{0,8},{2,10},{4,12},{6,14},{8,0},{10,2},{12,4},{14,6},{16,24},{18,... | collective-permute-start | bytes 1683464 | tf_op jit(solution)/shard_map/ppermute | solution.py:74
  97.7 13.4 %collective-permute-start.16 = (f32[1096,128]{1,0:T(8,128)S(1)}, f32[1096,128]{1,0:T(8,128)S(1)}, u32[]{:S(2)}, u32[]{:S(2)}) collective-permute-start(f32[1096,128]{1,0:T(8,128)S(1)} %add_dynamic-update-slice_fusion), channel_id=1, source_target_pairs={{0,4},{2,6},{4,0},{6,2},{8,12},{10,14},{12,8},{14,10},{16,20},{18,... | collective-permute-start | bytes 1683464 | tf_op jit(solution)/shard_map/ppermute | solution.py:74
  99.2 12.0 %collective-permute-start.15 = (f32[1096,128]{1,0:T(8,128)S(1)}, f32[1096,128]{1,0:T(8,128)S(1)}, u32[]{:S(2)}, u32[]{:S(2)}) collective-permute-start(f32[1096,128]{1,0:T(8,128)S(1)} %add_dynamic-update-slice_fusion), channel_id=1, source_target_pairs={{8,16},{10,18},{12,20},{14,22},{16,8},{18,10},{20,12},{22,14},{9,1... | collective-permute-start | bytes 1683464 | tf_op jit(solution)/shard_map/ppermute | solution.py:74
  111.1 11.6 %collective-permute-start.21 = (f32[1096,128]{1,0:T(8,128)S(1)}, f32[1096,128]{1,0:T(8,128)S(1)}, u32[]{:S(2)}, u32[]{:S(2)}) collective-permute-start(f32[1096,128]{1,0:T(8,128)S(1)} %collective-permute-done.14), channel_id=1, source_target_pairs={{0,4},{2,6},{4,0},{6,2},{8,12},{10,14},{12,8},{14,10},{16,20},{18,... | collective-permute-start | bytes 1683464 | tf_op jit(solution)/shard_map/ppermute | solution.py:74
  112.6 10.1 %collective-permute-start.19 = (f32[1096,128]{1,0:T(8,128)S(1)}, f32[1096,128]{1,0:T(8,128)S(1)}, u32[]{:S(2)}, u32[]{:S(2)}) collective-permute-start(f32[1096,128]{1,0:T(8,128)S(1)} %collective-permute-done.14), channel_id=1, source_target_pairs={{8,16},{10,18},{12,20},{14,22},{16,8},{18,10},{20,12},{22,14},{9,1... | collective-permute-start | bytes 1683464 | tf_op jit(solution)/shard_map/ppermute | solution.py:74
  113.3 14.5 %collective-permute-start.20 = (f32[1096,128]{1,0:T(8,128)S(1)}, f32[1096,128]{1,0:T(8,128)S(1)}, u32[]{:S(2)}, u32[]{:S(2)}) collective-permute-start(f32[1096,128]{1,0:T(8,128)S(1)} %collective-permute-done.15), channel_id=1, source_target_pairs={{8,0},{10,2},{12,4},{14,6},{16,24},{18,26},{20,28},{22,30},{9,1},{... | collective-permute-start | bytes 1683464 | tf_op jit(solution)/shard_map/ppermute | solution.py:74
  127.8 26.9 %copy-start.4 = (s32[136,128]{1,0:T(8,128)S(1)}, s32[136,128]{1,0:T(8,128)}, u32[]{:S(2)}) copy-start(s32[136,128]{1,0:T(8,128)} %get-tuple-element.43.position_ref) | copy-start | bytes 208900
  127.9 26.9 %copy-start.5 = (f32[3,2,1024]{2,1,0:T(2,128)S(1)}, f32[3,2,1024]{2,1,0:T(2,128)}, u32[]{:S(2)}) copy-start(f32[3,2,1024]{2,1,0:T(2,128)} %norm_ref.1) | copy-start | bytes 73732
  127.9 26.9 %copy-start.6 = (s32[3]{0:T(128)S(1)}, s32[3]{0:T(128)}, u32[]{:S(2)}) copy-start(s32[3]{0:T(128)} %pad_add_fusion.place_ref) | copy-start | bytes 40
  127.9 14.7 %collective-permute-start.24 = (f32[1096,128]{1,0:T(8,128)S(1)}, f32[1096,128]{1,0:T(8,128)S(1)}, u32[]{:S(2)}, u32[]{:S(2)}) collective-permute-start(f32[1096,128]{1,0:T(8,128)S(1)} %add.81.refs_6_), channel_id=1, source_target_pairs={{0,4},{2,6},{4,0},{6,2},{8,12},{10,14},{12,8},{14,10},{16,20},{18,... | collective-permute-start | bytes 1683464 | tf_op jit(solution)/shard_map/ppermute | solution.py:74
  131.4 11.5 %collective-permute-start.23 = (f32[1096,128]{1,0:T(8,128)S(1)}, f32[1096,128]{1,0:T(8,128)S(1)}, u32[]{:S(2)}, u32[]{:S(2)}) collective-permute-start(f32[1096,128]{1,0:T(8,128)S(1)} %collective-permute-done.19), channel_id=1, source_target_pairs={{8,0},{10,2},{12,4},{14,6},{16,24},{18,26},{20,28},{22,30},{9,1},{... | collective-permute-start | bytes 1683464 | tf_op jit(solution)/shard_map/ppermute | solution.py:74
  132.7 12.5 %collective-permute-start.18 = (f32[1096,128]{1,0:T(8,128)S(1)}, f32[1096,128]{1,0:T(8,128)S(1)}, u32[]{:S(2)}, u32[]{:S(2)}) collective-permute-start(f32[1096,128]{1,0:T(8,128)S(1)} %collective-permute-done.16.refs_2_), channel_id=1, source_target_pairs={{0,2},{2,0},{4,6},{6,4},{8,10},{10,8},{12,14},{14,12},{16,18},{18,... | collective-permute-start | bytes 1683464 | tf_op jit(solution)/shard_map/ppermute | solution.py:74
  132.7 20.0 %collective-permute-start.17 = (f32[2192,128]{1,0:T(8,128)S(1)}, f32[2192,128]{1,0:T(8,128)S(1)}, u32[]{:S(2)}, u32[]{:S(2)}) collective-permute-start(f32[2192,128]{1,0:T(8,128)S(1)} %pad_maximum_fusion.refs_0_), channel_id=1, source_target_pairs={{0,2},{2,0},{4,6},{6,4},{8,10},{10,8},{12,14},{14,12},{16,18},{18,... | collective-permute-start | bytes 3366920 | tf_op jit(solution)/shard_map/ppermute | solution.py:74
  133.2 12.5 %collective-permute-start.22 = (f32[1096,128]{1,0:T(8,128)S(1)}, f32[1096,128]{1,0:T(8,128)S(1)}, u32[]{:S(2)}, u32[]{:S(2)}) collective-permute-start(f32[1096,128]{1,0:T(8,128)S(1)} %collective-permute-done.21.refs_4_), channel_id=1, source_target_pairs={{0,2},{2,0},{4,6},{6,4},{8,10},{10,8},{12,14},{14,12},{16,18},{18,... | collective-permute-start | bytes 1683464 | tf_op jit(solution)/shard_map/ppermute | solution.py:74
  142.9 9.8 %collective-permute-start.27 = (f32[1096,128]{1,0:T(8,128)S(1)}, f32[1096,128]{1,0:T(8,128)S(1)}, u32[]{:S(2)}, u32[]{:S(2)}) collective-permute-start(f32[1096,128]{1,0:T(8,128)S(1)} %add.82.refs_10_), channel_id=1, source_target_pairs={{0,4},{2,6},{4,0},{6,2},{8,12},{10,14},{12,8},{14,10},{16,20},{18,... | collective-permute-start | bytes 1683464 | tf_op jit(solution)/shard_map/ppermute | solution.py:74
  145.2 7.6 %collective-permute-start.28 = (f32[1096,128]{1,0:T(8,128)S(1)}, f32[1096,128]{1,0:T(8,128)S(1)}, u32[]{:S(2)}, u32[]{:S(2)}) collective-permute-start(f32[1096,128]{1,0:T(8,128)S(1)} %add.82.refs_10_), channel_id=1, source_target_pairs={{0,2},{2,0},{4,6},{6,4},{8,10},{10,8},{12,14},{14,12},{16,18},{18,... | collective-permute-start | bytes 1683464 | tf_op jit(solution)/shard_map/ppermute | solution.py:74
  145.2 7.6 %collective-permute-start.25 = (f32[1096,128]{1,0:T(8,128)S(1)}, f32[1096,128]{1,0:T(8,128)S(1)}, u32[]{:S(2)}, u32[]{:S(2)}) collective-permute-start(f32[1096,128]{1,0:T(8,128)S(1)} %add.81.refs_6_), channel_id=1, source_target_pairs={{0,2},{2,0},{4,6},{6,4},{8,10},{10,8},{12,14},{14,12},{16,18},{18,... | collective-permute-start | bytes 1683464 | tf_op jit(solution)/shard_map/ppermute | solution.py:74
  145.7 7.1 %collective-permute-start.26 = (f32[1096,128]{1,0:T(8,128)S(1)}, f32[1096,128]{1,0:T(8,128)S(1)}, u32[]{:S(2)}, u32[]{:S(2)}) collective-permute-start(f32[1096,128]{1,0:T(8,128)S(1)} %collective-permute-done.24.refs_7_), channel_id=1, source_target_pairs={{0,2},{2,0},{4,6},{6,4},{8,10},{10,8},{12,14},{14,12},{16,18},{18,... | collective-permute-start | bytes 1683464 | tf_op jit(solution)/shard_map/ppermute | solution.py:74
  152.8 2.0 %collective-permute-start.29 = (f32[1096,128]{1,0:T(8,128)S(1)}, f32[1096,128]{1,0:T(8,128)S(1)}, u32[]{:S(2)}, u32[]{:S(2)}) collective-permute-start(f32[1096,128]{1,0:T(8,128)S(1)} %collective-permute-done.27.refs_11_), channel_id=1, source_target_pairs={{0,2},{2,0},{4,6},{6,4},{8,10},{10,8},{12,14},{14,12},{16,18},{18,... | collective-permute-start | bytes 1683464 | tf_op jit(solution)/shard_map/ppermute | solution.py:74

commit v11 on v10

--- a/solution.py
+++ b/solution.py
@@ -122,40 +122,32 @@
 
 
 def gather(plan, block):
-    found = []
-
     def along_x(value):
         return line_gather(plan, "x", plan.nx, value)
 
-    def add(far_z, line, skip=0):
-        for far_x, value in enumerate(line):
-            found.append((value, [(far_z, far_x, 0)]))
-        for far_x, value in enumerate(line):
-            if far_x >= skip:
-                found.append((plan.swap(value), [(far_z, far_x, 1)]))
-
     if plan.nz != 4:
-        for far_z, value in enumerate(line_gather(plan, "z", plan.nz, block)):
-            add(far_z, along_x(value))
-        return found
-    line = along_x(block)
-    pair = plan.send(block, "z", PAIRS)
-    three = plan.send(block, "z", MIDDLE)
-    both, three, *line = together(jnp.concatenate([block, pair]), three, *line)
-    line_pair = along_x(pair)
-    two = plan.send(pair, "z", MIDDLE)
-    out_two = plan.send(three, "z", OUTWARD)
-    two, out_two, *line_pair = together(two, out_two, *line_pair)
-    found.append((both, [(0, 0, 0), (1, 0, 0)]))
-    found.append((plan.swap(both), [(0, 0, 1), (1, 0, 1)]))
-    line_two = along_x(two + out_two)
-    out_three = plan.send(two, "z", OUTWARD)
-    out_three, *line_two = together(out_three, *line_two)
-    add(0, line, 1)
-    add(1, line_pair, 1)
-    add(2, line_two)
-    add(3, along_x(three + out_three))
-    return [(value, slots) for value, slots in found if slots[0][1:] != (0, 0) or slots[0][0] > 1 or len(slots) > 1]
+        lines = [along_x(value) for value in line_gather(plan, "z", plan.nz, block)]
+        mine = [(value, [(z, x)]) for z, line in enumerate(lines) for x, value in enumerate(line)]
+    else:
+        line = along_x(block)
+        pair = plan.send(block, "z", PAIRS)
+        three = plan.send(block, "z", MIDDLE)
+        three, own, *line = together(three, jnp.concatenate([block, pair]), *line)
+        line_pair = along_x(pair)
+        two = plan.send(pair, "z", MIDDLE)
+        out_two = plan.send(three, "z", OUTWARD)
+        far = [jnp.concatenate([line[x], line_pair[x]]) for x in range(1, plan.nx)]
+        near_two, *far = together(two + out_two, *far)
+        line_two = along_x(near_two)
+        out_three = plan.send(two, "z", OUTWARD)
+        line_three = along_x(three + out_three)
+        own, *line_two = together(own, *line_two)
+        mine = [(value, [(0, x), (1, x)]) for x, value in enumerate([own] + far)]
+        mine += [(value, [(2, x)]) for x, value in enumerate(line_two)]
+        mine += [(value, [(3, x)]) for x, value in enumerate(line_three)]
+    swapped = [plan.swap(value) for value, _ in mine]
+    found = [(value, [slot + (0,) for slot in slots]) for value, slots in mine]
+    return found + [(value, [slot + (1,) for slot in slots]) for value, (_, slots) in zip(swapped, mine)]
 
 
 def line_gather(plan, axis, count, value):

time: 175 us -> 173 us (0.989)
  starting transfers between devices: 40.8 us -> 37.9 us
    ppermute x29 -> x28, starting transfers between devices: 39.2 us -> 36.4 us  [send(): return lax.ppermute(value, 'dp', every)]
    ppermute x29 -> x28, waiting for transfers between devices: 76.7 us -> 78 us  [send(): return lax.ppermute(value, 'dp', every)]
  transfers between devices with their start and end apart: 30 -> 29, of which waited for: 17 -> 17; matrix products, arithmetic and copies ran while one was open for 1% -> 1% of each run, Pallas kernels for 4% -> 4%
where the time goes in v11:
time: 173 us
  waiting for transfers between devices  80.1 us (46%)
  Pallas kernels  50.9 us (29%)
  starting transfers between devices  37.9 us (22%)
  other arithmetic  2.86 us (2%)
    ppermute x28, waiting for transfers between devices, send(): return lax.ppermute(value, 'dp', every)  78 us
    ppermute x28, starting transfers between devices, send(): return lax.ppermute(value, 'dp', every)  36.4 us
    pallas_call x1, Pallas kernels, place(): pl.pallas_call(functools.partial(place_kernel, plan), out_shape=[jax.Shap...  22.2 us
    pallas_call x1, Pallas kernels, finish(): pl.pallas_call(functools.partial(finish_kernel, plan, tile, slots), grid=...  19.6 us
    pallas_call x1, Pallas kernels, owned(): pl.pallas_call(functools.partial(owned_kernel, plan), out_shape=[jax.Shap...  6.31 us
  transfers between devices with their start and end apart: 29, of which 17 were waited for; matrix products, arithmetic and copies ran while one was open for 1% of the time, Pallas kernels for 4%

profile of v11, /device:TPU:0, one launch (start us, length us, event | category | flops | bytes accessed | tf_op | source)
XLA Modules:
  0.0 172.9 jit_solution(8231795690539628683)
XLA Ops:
  0.7 0.7 pad_add_fusion.place_ref
  1.3 22.2 %place_gradients.1 = (f32[2192,128]{1,0:T(8,128)}, f32[2192,128]{1,0:T(8,128)}, f32[2192,128]{1,0:T(8,128)}, f32[2192,128]{1,0:T(8,128)}, f32[2192,128]{1,0:T(8,...) custom-call(s32[3]{0:T(128)} %pad_add_fusion.place_ref, ...), custom_call_target="tpu_custom_call" | custom-call | tf_op jit(solution)/shard_map/place_gradients/pallas_call | solution.py:244
  23.6 0.5 collective-permute-start
  24.1 2.6 %collective-permute-done = f32[2192,128]{1,0:T(8,128)S(1)} collective-permute-done((f32[2192,128]{1,0:T(8,128)}, f32[2192,128]{1,0:T(8,128)S(1)}, u32[]{:S(2)}, u32[]{:S(2)}) %collective-permute-start) | collective-permute-done | bytes 1122336 | tf_op jit(solution)/shard_map/ppermute | solution.py:74
  26.7 1.1 slice_add_fusion.7
  27.9 0.4 collective-permute-start.5
  28.3 0.1 collective-permute-start.9
  28.4 2.9 %collective-permute-start.3 = (f32[1096,128]{1,0:T(8,128)S(1)}, f32[1096,128]{1,0:T(8,128)S(1)}, u32[]{:S(2)}, u32[]{:S(2)}) collective-permute-start(f32[1096,128]{1,0:T(8,128)S(1)} %slice_add_fusion.7), channel_id=1, source_target_pairs={{0,4},{2,6},{4,0},{6,2},{8,12},{10,14},{12,8},{14,10},{16,20},{18,... | collective-permute-start | bytes 1683464 | tf_op jit(solution)/shard_map/ppermute | solution.py:74
  31.3 6.3 %owned_weights.1 = (f32[1088,128]{1,0:T(8,128)}, s32[1152,128]{1,0:T(8,128)}) custom-call(s32[3]{0:T(128)} %pad_add_fusion.place_ref, s32[136,128]{1,0:T(8,128)} %bitcast.16, f32[17408,128]{1,0:T(8,128)} %weights_ref.3), custom_call_target="tpu_custom_call" | custom-call | bytes 20971520 | tf_op jit(solution)/shard_map/owned_weights/pallas_call | solution.py:322
  37.6 0.1 collective-permute-start.1
  37.7 0.1 slice_add_fusion.2
  37.8 0.2 collective-permute-start.6
  38.0 6.8 %collective-permute-done.3 = f32[1096,128]{1,0:T(8,128)S(1)} collective-permute-done((f32[1096,128]{1,0:T(8,128)S(1)}, f32[1096,128]{1,0:T(8,128)S(1)}, u32[]{:S(2)}, u32[]{:S(2)}) %collective-permute-start.3) | collective-permute-done | bytes 561184 | tf_op jit(solution)/shard_map/ppermute | solution.py:74
  44.8 0.1 fusion.2
  44.9 4.1 %collective-permute-start.4 = (f32[1096,128]{1,0:T(8,128)S(1)}, f32[1096,128]{1,0:T(8,128)S(1)}, u32[]{:S(2)}, u32[]{:S(2)}) collective-permute-start(f32[1096,128]{1,0:T(8,128)S(1)} %fusion.2), channel_id=1, source_target_pairs={{0,8},{2,10},{4,12},{6,14},{24,16},{26,18},{28,20},{30,22},{1,9},{... | collective-permute-start | bytes 1683464 | tf_op jit(solution)/shard_map/ppermute | solution.py:74
  49.0 0.1 slice_add_fusion
  49.1 1.6 collective-permute-start.10
  50.6 6.2 %collective-permute-done.6 = f32[1096,128]{1,0:T(8,128)S(1)} collective-permute-done((f32[1096,128]{1,0:T(8,128)S(1)}, f32[1096,128]{1,0:T(8,128)S(1)}, u32[]{:S(2)}, u32[]{:S(2)}) %collective-permute-start.6) | collective-permute-done | bytes 561184 | tf_op jit(solution)/shard_map/ppermute | solution.py:74
  56.8 0.1 fusion.1
  56.9 2.6 %collective-permute-done.4 = f32[1096,128]{1,0:T(8,128)S(1)} collective-permute-done((f32[1096,128]{1,0:T(8,128)S(1)}, f32[1096,128]{1,0:T(8,128)S(1)}, u32[]{:S(2)}, u32[]{:S(2)}) %collective-permute-start.4) | collective-permute-done | bytes 561184 | tf_op jit(solution)/shard_map/ppermute | solution.py:74
  59.6 4.4 %collective-permute-start.8 = (f32[1096,128]{1,0:T(8,128)S(1)}, f32[1096,128]{1,0:T(8,128)S(1)}, u32[]{:S(2)}, u32[]{:S(2)}) collective-permute-start(f32[1096,128]{1,0:T(8,128)S(1)} %fusion.1), channel_id=1, source_target_pairs={{0,8},{2,10},{4,12},{6,14},{24,16},{26,18},{28,20},{30,22},{1,9},{... | collective-permute-start | bytes 1683464 | tf_op jit(solution)/shard_map/ppermute | solution.py:74
  64.0 0.1 add.73
  64.0 0.7 collective-permute-start.7
  64.8 0.1 slice_add_fusion.5
  64.9 1.6 collective-permute-start.2
  66.5 2.4 %collective-permute-done.10 = f32[1096,128]{1,0:T(8,128)S(1)} collective-permute-done((f32[1096,128]{1,0:T(8,128)S(1)}, f32[1096,128]{1,0:T(8,128)S(1)}, u32[]{:S(2)}, u32[]{:S(2)}) %collective-permute-start.10) | collective-permute-done | bytes 561184 | tf_op jit(solution)/shard_map/ppermute | solution.py:74
  68.8 0.1 fusion
  68.9 0.0 slice-start.1
  69.0 4.7 %collective-permute-done.8 = f32[1096,128]{1,0:T(8,128)S(1)} collective-permute-done((f32[1096,128]{1,0:T(8,128)S(1)}, f32[1096,128]{1,0:T(8,128)S(1)}, u32[]{:S(2)}, u32[]{:S(2)}) %collective-permute-start.8) | collective-permute-done | bytes 561184 | tf_op jit(solution)/shard_map/ppermute | solution.py:74
  73.6 0.1 add.78
  73.7 0.1 add.77
  73.8 3.9 %collective-permute-start.11 = (f32[1096,128]{1,0:T(8,128)S(1)}, f32[1096,128]{1,0:T(8,128)S(1)}, u32[]{:S(2)}, u32[]{:S(2)}) collective-permute-start(f32[1096,128]{1,0:T(8,128)S(1)} %add.77), channel_id=1, source_target_pairs={{0,8},{2,10},{4,12},{6,14},{8,0},{10,2},{12,4},{14,6},{16,24},{18,... | collective-permute-start | bytes 1683464 | tf_op jit(solution)/shard_map/ppermute | solution.py:74
  77.7 0.7 collective-permute-start.12
  78.4 2.0 %collective-permute-done.2.refs_1_ = f32[1096,128]{1,0:T(8,128)S(1)} collective-permute-done((f32[1096,128]{1,0:T(8,128)S(1)}, f32[1096,128]{1,0:T(8,128)S(1)}, u32[]{:S(2)}, u32[]{:S(2)}) %collective-permute-start.2) | collective-permute-done | bytes 561184 | tf_op jit(solution)/shard_map/ppermute | solution.py:74
  80.4 6.9 %collective-permute-done.11.refs_2_ = f32[1096,128]{1,0:T(8,128)S(1)} collective-permute-done((f32[1096,128]{1,0:T(8,128)S(1)}, f32[1096,128]{1,0:T(8,128)S(1)}, u32[]{:S(2)}, u32[]{:S(2)}) %collective-permute-start.11) | collective-permute-done | bytes 561184 | tf_op jit(solution)/shard_map/ppermute | solution.py:74
  87.3 2.7 %moments.1 = (f32[1088,128]{1,0:T(8,128)}, f32[1088,128]{1,0:T(8,128)}, f32[1096,128]{1,0:T(8,128)S(1)}, f32[8,128]{1,0:T(8,128)S(1)}) custom-call(f32[1096,128]{1,0:T(8,128)S(1)} %get-tuple-element.80.refs_0_, f32[1096,128]{1,0:T(8,128)S(1)} %collective-permute-done.2.refs_1_, f32[1096,128]{1,0:T(8,128)S(1)} %collective-permute-done.11.refs_2_, ...), custom_call_target="tpu_custom_call" | custom-call | tf_op jit(solution)/shard_map/moments/pallas_call | solution.py:377
  90.0 1.5 collective-permute-start.13
  91.5 2.1 %collective-permute-done.13 = f32[8,128]{1,0:T(8,128)S(1)} collective-permute-done((f32[8,128]{1,0:T(8,128)S(1)}, f32[8,128]{1,0:T(8,128)S(1)}, u32[]{:S(2)}, u32[]{:S(2)}) %collective-permute-start.13) | collective-permute-done | bytes 4128 | tf_op jit(solution)/shard_map/ppermute | solution.py:511
  93.6 3.6 %collective-permute-start.15 = (f32[1096,128]{1,0:T(8,128)S(1)}, f32[1096,128]{1,0:T(8,128)S(1)}, u32[]{:S(2)}, u32[]{:S(2)}) collective-permute-start(f32[1096,128]{1,0:T(8,128)S(1)} %add_dynamic-update-slice_fusion), channel_id=1, source_target_pairs={{0,8},{2,10},{4,12},{6,14},{8,0},{10,2},{12,4},{14,6},{16,24},{18,... | collective-permute-start | bytes 1683464 | tf_op jit(solution)/shard_map/ppermute | solution.py:74
  97.2 1.5 collective-permute-start.16
  98.7 0.7 collective-permute-start.14
  99.4 5.4 %collective-permute-done.15 = f32[1096,128]{1,0:T(8,128)S(1)} collective-permute-done((f32[1096,128]{1,0:T(8,128)S(1)}, f32[1096,128]{1,0:T(8,128)S(1)}, u32[]{:S(2)}, u32[]{:S(2)}) %collective-permute-start.15) | collective-permute-done | bytes 561184 | tf_op jit(solution)/shard_map/ppermute | solution.py:74
  104.8 1.5 collective-permute-start.19
  106.2 0.7 collective-permute-start.17
  106.9 0.1 pad_maximum_fusion.refs_0_
  107.0 5.5 %collective-permute-done.16 = f32[1096,128]{1,0:T(8,128)S(1)} collective-permute-done((f32[1096,128]{1,0:T(8,128)S(1)}, f32[1096,128]{1,0:T(8,128)S(1)}, u32[]{:S(2)}, u32[]{:S(2)}) %collective-permute-start.16) | collective-permute-done | bytes 561184 | tf_op jit(solution)/shard_map/ppermute | solution.py:74
  112.5 1.3 collective-permute-start.18
  113.8 1.3 collective-permute-start.21
  115.1 6.4 %collective-permute-done.19 = f32[1096,128]{1,0:T(8,128)S(1)} collective-permute-done((f32[1096,128]{1,0:T(8,128)S(1)}, f32[1096,128]{1,0:T(8,128)S(1)}, u32[]{:S(2)}, u32[]{:S(2)}) %collective-permute-start.19) | collective-permute-done | bytes 561184 | tf_op jit(solution)/shard_map/ppermute | solution.py:74
  121.5 0.1 pad_maximum_fusion.1.refs_1_
  121.5 6.0 %collective-permute-done.18 = f32[1096,128]{1,0:T(8,128)S(1)} collective-permute-done((f32[1096,128]{1,0:T(8,128)S(1)}, f32[1096,128]{1,0:T(8,128)S(1)}, u32[]{:S(2)}, u32[]{:S(2)}) %collective-permute-start.18) | collective-permute-done | bytes 561184 | tf_op jit(solution)/shard_map/ppermute | solution.py:74
  127.6 0.1 add.81.refs_2_
  127.7 2.5 %collective-permute-start.20 = (f32[1096,128]{1,0:T(8,128)S(1)}, f32[1096,128]{1,0:T(8,128)S(1)}, u32[]{:S(2)}, u32[]{:S(2)}) collective-permute-start(f32[1096,128]{1,0:T(8,128)S(1)} %add.81.refs_2_), channel_id=1, source_target_pairs={{0,4},{2,6},{4,0},{6,2},{8,12},{10,14},{12,8},{14,10},{16,20},{18,... | collective-permute-start | bytes 1683464 | tf_op jit(solution)/shard_map/ppermute | solution.py:74
  130.2 5.7 %collective-permute-done.21 = f32[1096,128]{1,0:T(8,128)S(1)} collective-permute-done((f32[1096,128]{1,0:T(8,128)S(1)}, f32[1096,128]{1,0:T(8,128)S(1)}, u32[]{:S(2)}, u32[]{:S(2)}) %collective-permute-start.21) | collective-permute-done | bytes 561184 | tf_op jit(solution)/shard_map/ppermute | solution.py:74
  136.0 0.1 add.82.refs_4_
  136.1 0.1 collective-permute-start.27
  136.1 1.6 collective-permute-start.22
  137.7 0.1 collective-permute-done.20.refs_3_
  137.8 0.1 collective-permute-start.23
  137.9 0.4 collective-permute-start.25
  138.3 0.1 collective-permute-start.26
  138.4 12.9 %collective-permute-done.22.refs_5_ = f32[1096,128]{1,0:T(8,128)S(1)} collective-permute-done((f32[1096,128]{1,0:T(8,128)S(1)}, f32[1096,128]{1,0:T(8,128)S(1)}, u32[]{:S(2)}, u32[]{:S(2)}) %collective-permute-start.22) | collective-permute-done | bytes 561184 | tf_op jit(solution)/shard_map/ppermute | solution.py:74
  151.3 1.9 %collective-permute-done.28.refs_11_ = f32[1096,128]{1,0:T(8,128)S(1)} collective-permute-done((f32[1096,128]{1,0:T(8,128)S(1)}, f32[1096,128]{1,0:T(8,128)S(1)}, u32[]{:S(2)}, u32[]{:S(2)}) %collective-permute-start.28) | collective-permute-done | bytes 561184 | tf_op jit(solution)/shard_map/ppermute | solution.py:74
  153.3 19.6 %new_weights.1 = (f32[17408,128]{1,0:T(8,128)}, f32[3,2,1024]{2,1,0:T(2,128)}, f32[7]{0:T(128)}) custom-call(s32[3]{0:T(128)S(1)} %copy-done.6, s32[136,128]{1,0:T(8,128)S(1)} %copy-done.4, f32[3,2,1024]{2,1,0:T(2,128)S(1)} %copy-done.5, f32[17408,128]{1,0:T(8,128)S(1)} %bitcast.11, f32[2192,128]{1,0:T(8,128)S(1)} %pad_maximum_fusion.refs_0_, ...), custom_call_target="tpu_custom_call" | custom-call | tf_op jit(solution)/shard_map/new_weights/pallas_call | solution.py:456
  (43 shorter events, 0.1 us)
Async XLA Ops:
  23.6 3.1 %collective-permute-start = (f32[2192,128]{1,0:T(8,128)}, f32[2192,128]{1,0:T(8,128)S(1)}, u32[]{:S(2)}, u32[]{:S(2)}) collective-permute-start(f32[2192,128]{1,0:T(8,128)} %get-tuple-element.45), channel_id=1, source_target_pairs={{0,2},{2,0},{4,6},{6,4},{8,10},{10,8},{12,14},{14,12},{16,18},{18,... | collective-permute-start | bytes 3366920 | tf_op jit(solution)/shard_map/ppermute | solution.py:74
  27.8 9.9 %copy-start.9 = (f32[2192,128]{1,0:T(8,128)S(1)}, f32[2192,128]{1,0:T(8,128)}, u32[]{:S(2)}) copy-start(f32[2192,128]{1,0:T(8,128)} %get-tuple-element.51) | copy-start | bytes 3366916
  27.9 9.8 %collective-permute-start.5 = (f32[2192,128]{1,0:T(8,128)}, f32[2192,128]{1,0:T(8,128)S(1)}, u32[]{:S(2)}, u32[]{:S(2)}) collective-permute-start(f32[2192,128]{1,0:T(8,128)} %get-tuple-element.52), channel_id=1, source_target_pairs={{0,2},{2,0},{4,6},{6,4},{8,10},{10,8},{12,14},{14,12},{16,18},{18,... | collective-permute-start | bytes 3366920 | tf_op jit(solution)/shard_map/ppermute | solution.py:74
  28.3 20.7 %collective-permute-start.9 = (f32[2192,128]{1,0:T(8,128)}, f32[2192,128]{1,0:T(8,128)S(1)}, u32[]{:S(2)}, u32[]{:S(2)}) collective-permute-start(f32[2192,128]{1,0:T(8,128)} %get-tuple-element.58), channel_id=1, source_target_pairs={{0,2},{2,0},{4,6},{6,4},{8,10},{10,8},{12,14},{14,12},{16,18},{18,... | collective-permute-start | bytes 3366920 | tf_op jit(solution)/shard_map/ppermute | solution.py:74
  28.4 16.4 %collective-permute-start.3 = (f32[1096,128]{1,0:T(8,128)S(1)}, f32[1096,128]{1,0:T(8,128)S(1)}, u32[]{:S(2)}, u32[]{:S(2)}) collective-permute-start(f32[1096,128]{1,0:T(8,128)S(1)} %slice_add_fusion.7), channel_id=1, source_target_pairs={{0,4},{2,6},{4,0},{6,2},{8,12},{10,14},{12,8},{14,10},{16,20},{18,... | collective-permute-start | bytes 1683464 | tf_op jit(solution)/shard_map/ppermute | solution.py:74
  37.6 7.2 %copy-start.10 = (f32[2192,128]{1,0:T(8,128)S(1)}, f32[2192,128]{1,0:T(8,128)}, u32[]{:S(2)}) copy-start(f32[2192,128]{1,0:T(8,128)} %get-tuple-element.44) | copy-start | bytes 3366916
  37.6 27.1 %collective-permute-start.1 = (f32[2192,128]{1,0:T(8,128)}, f32[2192,128]{1,0:T(8,128)S(1)}, u32[]{:S(2)}, u32[]{:S(2)}) collective-permute-start(f32[2192,128]{1,0:T(8,128)} %get-tuple-element.49), channel_id=1, source_target_pairs={{0,2},{2,0},{4,6},{6,4},{8,10},{10,8},{12,14},{14,12},{16,18},{18,... | collective-permute-start | bytes 3366920 | tf_op jit(solution)/shard_map/ppermute | solution.py:74
  37.8 11.2 %copy-start.7 = (f32[2192,128]{1,0:T(8,128)S(1)}, f32[2192,128]{1,0:T(8,128)}, u32[]{:S(2)}) copy-start(f32[2192,128]{1,0:T(8,128)} %get-tuple-element.57) | copy-start | bytes 3366916
  37.8 19.0 %collective-permute-start.6 = (f32[1096,128]{1,0:T(8,128)S(1)}, f32[1096,128]{1,0:T(8,128)S(1)}, u32[]{:S(2)}, u32[]{:S(2)}) collective-permute-start(f32[1096,128]{1,0:T(8,128)S(1)} %slice_add_fusion.2), channel_id=1, source_target_pairs={{0,4},{2,6},{4,0},{6,2},{8,12},{10,14},{12,8},{14,10},{16,20},{18,... | collective-permute-start | bytes 1683464 | tf_op jit(solution)/shard_map/ppermute | solution.py:74
  44.9 14.7 %collective-permute-start.4 = (f32[1096,128]{1,0:T(8,128)S(1)}, f32[1096,128]{1,0:T(8,128)S(1)}, u32[]{:S(2)}, u32[]{:S(2)}) collective-permute-start(f32[1096,128]{1,0:T(8,128)S(1)} %fusion.2), channel_id=1, source_target_pairs={{0,8},{2,10},{4,12},{6,14},{24,16},{26,18},{28,20},{30,22},{1,9},{... | collective-permute-start | bytes 1683464 | tf_op jit(solution)/shard_map/ppermute | solution.py:74
  49.1 19.8 %collective-permute-start.10 = (f32[1096,128]{1,0:T(8,128)S(1)}, f32[1096,128]{1,0:T(8,128)S(1)}, u32[]{:S(2)}, u32[]{:S(2)}) collective-permute-start(f32[1096,128]{1,0:T(8,128)S(1)} %slice_add_fusion), channel_id=1, source_target_pairs={{0,4},{2,6},{4,0},{6,2},{8,12},{10,14},{12,8},{14,10},{16,20},{18,... | collective-permute-start | bytes 1683464 | tf_op jit(solution)/shard_map/ppermute | solution.py:74
  56.9 7.8 %copy-start.8 = (f32[2192,128]{1,0:T(8,128)S(1)}, f32[2192,128]{1,0:T(8,128)}, u32[]{:S(2)}) copy-start(f32[2192,128]{1,0:T(8,128)} %get-tuple-element.43) | copy-start | bytes 3366916
  59.6 14.1 %collective-permute-start.8 = (f32[1096,128]{1,0:T(8,128)S(1)}, f32[1096,128]{1,0:T(8,128)S(1)}, u32[]{:S(2)}, u32[]{:S(2)}) collective-permute-start(f32[1096,128]{1,0:T(8,128)S(1)} %fusion.1), channel_id=1, source_target_pairs={{0,8},{2,10},{4,12},{6,14},{24,16},{26,18},{28,20},{30,22},{1,9},{... | collective-permute-start | bytes 1683464 | tf_op jit(solution)/shard_map/ppermute | solution.py:74
  64.0 4.9 %collective-permute-start.7 = (f32[1096,128]{1,0:T(8,128)S(1)}, f32[1096,128]{1,0:T(8,128)S(1)}, u32[]{:S(2)}, u32[]{:S(2)}) collective-permute-start(f32[1096,128]{1,0:T(8,128)S(1)} %add.73), channel_id=1, source_target_pairs={{8,16},{10,18},{12,20},{14,22},{16,8},{18,10},{20,12},{22,14},{9,1... | collective-permute-start | bytes 1683464 | tf_op jit(solution)/shard_map/ppermute | solution.py:74
  64.8 88.5 %slice-start = ((s8[8912896]{0:T(1024)(128)(4,1)}), s8[4194304]{0:T(1024)(128)(4,1)S(1)}, s32[]{:S(2)}) async-start(s8[8912896]{0:T(1024)(128)(4,1)} %bitcast.10), calls=%async_computation | async-start | bytes 8388608
  64.9 15.5 %collective-permute-start.2 = (f32[1096,128]{1,0:T(8,128)S(1)}, f32[1096,128]{1,0:T(8,128)S(1)}, u32[]{:S(2)}, u32[]{:S(2)}) collective-permute-start(f32[1096,128]{1,0:T(8,128)S(1)} %get-tuple-element.79), channel_id=1, source_target_pairs={{0,4},{2,6},{4,0},{6,2},{8,12},{10,14},{12,8},{14,10},{16,20},{18,... | collective-permute-start | bytes 1683464 | tf_op jit(solution)/shard_map/ppermute | solution.py:74
  68.8 18.4 %copy-start = (s32[1152,128]{1,0:T(8,128)S(1)}, s32[1152,128]{1,0:T(8,128)}, u32[]{:S(2)}) copy-start(s32[1152,128]{1,0:T(8,128)} %get-tuple-element.63.refs_7_) | copy-start | bytes 1769476
  68.8 18.4 %copy-start.1 = (f32[1,1088,128]{2,1,0:T(8,128)S(1)}, f32[1,1088,128]{2,1,0:T(8,128)}, u32[]{:S(2)}) copy-start(f32[1,1088,128]{2,1,0:T(8,128)} %param.9) | copy-start | bytes 1671172
  68.8 18.4 %copy-start.2 = (f32[1,1088,128]{2,1,0:T(8,128)S(1)}, f32[1,1088,128]{2,1,0:T(8,128)}, u32[]{:S(2)}) copy-start(f32[1,1088,128]{2,1,0:T(8,128)} %param.10) | copy-start | bytes 1671172
  68.8 18.4 %copy-start.3 = (f32[1088,128]{1,0:T(8,128)S(1)}, f32[1088,128]{1,0:T(8,128)}, u32[]{:S(2)}) copy-start(f32[1088,128]{1,0:T(8,128)} %get-tuple-element.62.refs_6_) | copy-start | bytes 1671172
  68.9 84.3 %slice-start.1 = ((s8[8912896]{0:T(1024)(128)(4,1)}), s8[4194304]{0:T(1024)(128)(4,1)S(1)}, s32[]{:S(2)}) async-start(s8[8912896]{0:T(1024)(128)(4,1)} %bitcast.10), calls=%async_computation.1 | async-start | bytes 8388608
  73.8 13.5 %collective-permute-start.11 = (f32[1096,128]{1,0:T(8,128)S(1)}, f32[1096,128]{1,0:T(8,128)S(1)}, u32[]{:S(2)}, u32[]{:S(2)}) collective-permute-start(f32[1096,128]{1,0:T(8,128)S(1)} %add.77), channel_id=1, source_target_pairs={{0,8},{2,10},{4,12},{6,14},{8,0},{10,2},{12,4},{14,6},{16,24},{18,... | collective-permute-start | bytes 1683464 | tf_op jit(solution)/shard_map/ppermute | solution.py:74
  77.7 9.5 %collective-permute-start.12 = (f32[1096,128]{1,0:T(8,128)S(1)}, f32[1096,128]{1,0:T(8,128)S(1)}, u32[]{:S(2)}, u32[]{:S(2)}) collective-permute-start(f32[1096,128]{1,0:T(8,128)S(1)} %add.78), channel_id=1, source_target_pairs={{8,16},{10,18},{12,20},{14,22},{16,8},{18,10},{20,12},{22,14},{9,1... | collective-permute-start | bytes 1683464 | tf_op jit(solution)/shard_map/ppermute | solution.py:74
  90.0 3.6 %collective-permute-start.13 = (f32[8,128]{1,0:T(8,128)S(1)}, f32[8,128]{1,0:T(8,128)S(1)}, u32[]{:S(2)}, u32[]{:S(2)}) collective-permute-start(f32[8,128]{1,0:T(8,128)S(1)} %get-tuple-element.65), channel_id=1, source_target_pairs={{0,1},{1,0},{2,3},{3,2},{4,5},{5,4},{6,7},{7,6},{8,9},{9,8},{10,11... | collective-permute-start | bytes 12296 | tf_op jit(solution)/shard_map/ppermute | solution.py:511
  93.6 59.7 %slice-start.2 = ((s8[8912896]{0:T(1024)(128)(4,1)}), s8[524288]{0:T(1024)(128)(4,1)S(1)}, s32[]{:S(2)}) async-start(s8[8912896]{0:T(1024)(128)(4,1)} %bitcast.10), calls=%async_computation.2 | async-start | bytes 1048576
  93.6 11.2 %collective-permute-start.15 = (f32[1096,128]{1,0:T(8,128)S(1)}, f32[1096,128]{1,0:T(8,128)S(1)}, u32[]{:S(2)}, u32[]{:S(2)}) collective-permute-start(f32[1096,128]{1,0:T(8,128)S(1)} %add_dynamic-update-slice_fusion), channel_id=1, source_target_pairs={{0,8},{2,10},{4,12},{6,14},{8,0},{10,2},{12,4},{14,6},{16,24},{18,... | collective-permute-start | bytes 1683464 | tf_op jit(solution)/shard_map/ppermute | solution.py:74
  97.2 15.3 %collective-permute-start.16 = (f32[1096,128]{1,0:T(8,128)S(1)}, f32[1096,128]{1,0:T(8,128)S(1)}, u32[]{:S(2)}, u32[]{:S(2)}) collective-permute-start(f32[1096,128]{1,0:T(8,128)S(1)} %add_dynamic-update-slice_fusion), channel_id=1, source_target_pairs={{0,4},{2,6},{4,0},{6,2},{8,12},{10,14},{12,8},{14,10},{16,20},{18,... | collective-permute-start | bytes 1683464 | tf_op jit(solution)/shard_map/ppermute | solution.py:74
  98.7 13.8 %collective-permute-start.14 = (f32[1096,128]{1,0:T(8,128)S(1)}, f32[1096,128]{1,0:T(8,128)S(1)}, u32[]{:S(2)}, u32[]{:S(2)}) collective-permute-start(f32[1096,128]{1,0:T(8,128)S(1)} %add_dynamic-update-slice_fusion), channel_id=1, source_target_pairs={{8,16},{10,18},{12,20},{14,22},{16,8},{18,10},{20,12},{22,14},{9,1... | collective-permute-start | bytes 1683464 | tf_op jit(solution)/shard_map/ppermute | solution.py:74
  104.8 16.7 %collective-permute-start.19 = (f32[1096,128]{1,0:T(8,128)S(1)}, f32[1096,128]{1,0:T(8,128)S(1)}, u32[]{:S(2)}, u32[]{:S(2)}) collective-permute-start(f32[1096,128]{1,0:T(8,128)S(1)} %collective-permute-done.15), channel_id=1, source_target_pairs={{0,4},{2,6},{4,0},{6,2},{8,12},{10,14},{12,8},{14,10},{16,20},{18,... | collective-permute-start | bytes 1683464 | tf_op jit(solution)/shard_map/ppermute | solution.py:74
  106.2 7.5 %collective-permute-start.17 = (f32[1096,128]{1,0:T(8,128)S(1)}, f32[1096,128]{1,0:T(8,128)S(1)}, u32[]{:S(2)}, u32[]{:S(2)}) collective-permute-start(f32[1096,128]{1,0:T(8,128)S(1)} %collective-permute-done.15), channel_id=1, source_target_pairs={{8,16},{10,18},{12,20},{14,22},{16,8},{18,10},{20,12},{22,14},{9,1... | collective-permute-start | bytes 1683464 | tf_op jit(solution)/shard_map/ppermute | solution.py:74
  112.5 15.1 %collective-permute-start.18 = (f32[1096,128]{1,0:T(8,128)S(1)}, f32[1096,128]{1,0:T(8,128)S(1)}, u32[]{:S(2)}, u32[]{:S(2)}) collective-permute-start(f32[1096,128]{1,0:T(8,128)S(1)} %collective-permute-done.14), channel_id=1, source_target_pairs={{8,0},{10,2},{12,4},{14,6},{16,24},{18,26},{20,28},{22,30},{9,1},{... | collective-permute-start | bytes 1683464 | tf_op jit(solution)/shard_map/ppermute | solution.py:74
  113.8 22.2 %collective-permute-start.21 = (f32[1096,128]{1,0:T(8,128)S(1)}, f32[1096,128]{1,0:T(8,128)S(1)}, u32[]{:S(2)}, u32[]{:S(2)}) collective-permute-start(f32[1096,128]{1,0:T(8,128)S(1)} %collective-permute-done.17), channel_id=1, source_target_pairs={{8,0},{10,2},{12,4},{14,6},{16,24},{18,26},{20,28},{22,30},{9,1},{... | collective-permute-start | bytes 1683464 | tf_op jit(solution)/shard_map/ppermute | solution.py:74
  127.7 25.6 %copy-start.4 = (s32[136,128]{1,0:T(8,128)S(1)}, s32[136,128]{1,0:T(8,128)}, u32[]{:S(2)}) copy-start(s32[136,128]{1,0:T(8,128)} %get-tuple-element.42.position_ref) | copy-start | bytes 208900
  127.7 25.6 %copy-start.5 = (f32[3,2,1024]{2,1,0:T(2,128)S(1)}, f32[3,2,1024]{2,1,0:T(2,128)}, u32[]{:S(2)}) copy-start(f32[3,2,1024]{2,1,0:T(2,128)} %norm_ref.1) | copy-start | bytes 73732
  127.7 25.6 %copy-start.6 = (s32[3]{0:T(128)S(1)}, s32[3]{0:T(128)}, u32[]{:S(2)}) copy-start(s32[3]{0:T(128)} %pad_add_fusion.place_ref) | copy-start | bytes 40
  127.7 10.1 %collective-permute-start.20 = (f32[1096,128]{1,0:T(8,128)S(1)}, f32[1096,128]{1,0:T(8,128)S(1)}, u32[]{:S(2)}, u32[]{:S(2)}) collective-permute-start(f32[1096,128]{1,0:T(8,128)S(1)} %add.81.refs_2_), channel_id=1, source_target_pairs={{0,4},{2,6},{4,0},{6,2},{8,12},{10,14},{12,8},{14,10},{16,20},{18,... | collective-permute-start | bytes 1683464 | tf_op jit(solution)/shard_map/ppermute | solution.py:74
  130.2 21.0 %collective-permute-start.24 = (f32[2192,128]{1,0:T(8,128)S(1)}, f32[2192,128]{1,0:T(8,128)S(1)}, u32[]{:S(2)}, u32[]{:S(2)}) collective-permute-start(f32[2192,128]{1,0:T(8,128)S(1)} %pad_maximum_fusion.1.refs_1_), channel_id=1, source_target_pairs={{0,2},{2,0},{4,6},{6,4},{8,10},{10,8},{12,14},{14,12},{16,18},{18,... | collective-permute-start | bytes 3366920 | tf_op jit(solution)/shard_map/ppermute | solution.py:74
  136.1 2.3 %collective-permute-start.27 = (f32[1096,128]{1,0:T(8,128)S(1)}, f32[1096,128]{1,0:T(8,128)S(1)}, u32[]{:S(2)}, u32[]{:S(2)}) collective-permute-start(f32[1096,128]{1,0:T(8,128)S(1)} %add.82.refs_4_), channel_id=1, source_target_pairs={{0,2},{2,0},{4,6},{6,4},{8,10},{10,8},{12,14},{14,12},{16,18},{18,... | collective-permute-start | bytes 1683464 | tf_op jit(solution)/shard_map/ppermute | solution.py:74
  136.1 15.1 %collective-permute-start.22 = (f32[1096,128]{1,0:T(8,128)S(1)}, f32[1096,128]{1,0:T(8,128)S(1)}, u32[]{:S(2)}, u32[]{:S(2)}) collective-permute-start(f32[1096,128]{1,0:T(8,128)S(1)} %add.82.refs_4_), channel_id=1, source_target_pairs={{0,4},{2,6},{4,0},{6,2},{8,12},{10,14},{12,8},{14,10},{16,20},{18,... | collective-permute-start | bytes 1683464 | tf_op jit(solution)/shard_map/ppermute | solution.py:74
  137.8 15.4 %collective-permute-start.23 = (f32[2192,128]{1,0:T(8,128)S(1)}, f32[2192,128]{1,0:T(8,128)S(1)}, u32[]{:S(2)}, u32[]{:S(2)}) collective-permute-start(f32[2192,128]{1,0:T(8,128)S(1)} %pad_maximum_fusion.refs_0_), channel_id=1, source_target_pairs={{0,2},{2,0},{4,6},{6,4},{8,10},{10,8},{12,14},{14,12},{16,18},{18,... | collective-permute-start | bytes 3366920 | tf_op jit(solution)/shard_map/ppermute | solution.py:74
  137.9 13.4 %collective-permute-start.25 = (f32[1096,128]{1,0:T(8,128)S(1)}, f32[1096,128]{1,0:T(8,128)S(1)}, u32[]{:S(2)}, u32[]{:S(2)}) collective-permute-start(f32[1096,128]{1,0:T(8,128)S(1)} %add.81.refs_2_), channel_id=1, source_target_pairs={{0,2},{2,0},{4,6},{6,4},{8,10},{10,8},{12,14},{14,12},{16,18},{18,... | collective-permute-start | bytes 1683464 | tf_op jit(solution)/shard_map/ppermute | solution.py:74
  138.3 13.0 %collective-permute-start.26 = (f32[1096,128]{1,0:T(8,128)S(1)}, f32[1096,128]{1,0:T(8,128)S(1)}, u32[]{:S(2)}, u32[]{:S(2)}) collective-permute-start(f32[1096,128]{1,0:T(8,128)S(1)} %collective-permute-done.20.refs_3_), channel_id=1, source_target_pairs={{0,2},{2,0},{4,6},{6,4},{8,10},{10,8},{12,14},{14,12},{16,18},{18,... | collective-permute-start | bytes 1683464 | tf_op jit(solution)/shard_map/ppermute | solution.py:74
  151.3 2.0 %collective-permute-start.28 = (f32[1096,128]{1,0:T(8,128)S(1)}, f32[1096,128]{1,0:T(8,128)S(1)}, u32[]{:S(2)}, u32[]{:S(2)}) collective-permute-start(f32[1096,128]{1,0:T(8,128)S(1)} %collective-permute-done.22.refs_5_), channel_id=1, source_target_pairs={{0,2},{2,0},{4,6},{6,4},{8,10},{10,8},{12,14},{14,12},{16,18},{18,... | collective-permute-start | bytes 1683464 | tf_op jit(solution)/shard_map/ppermute | solution.py:74

commit v12 on v11

--- a/solution.py
+++ b/solution.py
@@ -82,6 +82,7 @@
 MIDDLE = [(1, 2), (2, 1)]
 INWARD = [(0, 1), (3, 2)]
 OUTWARD = [(1, 0), (2, 3)]
+SECOND = [(0, 2), (2, 0), (1, 3), (3, 1)]
 
 
 def line_reduce(plan, axis, blocks):
@@ -90,11 +91,8 @@
     if len(blocks) == 2:
         return [blocks[0], plan.send(blocks[1], axis, PAIR)]
     in_three = plan.send(blocks[3], axis, INWARD)
-    in_two = plan.send(blocks[2], axis, INWARD)
-    across_two = plan.send(blocks[2] + in_three, axis, MIDDLE)
-    across_three = plan.send(blocks[3] + in_two, axis, MIDDLE)
-    pair = plan.send(blocks[1] + across_two, axis, PAIRS)
-    return [blocks[0], pair, across_three]
+    second = plan.send(blocks[2] + in_three, axis, SECOND)
+    return [blocks[0], plan.send(blocks[1], axis, PAIRS), second, plan.send(blocks[3], axis, MIDDLE)]
 
 
 def together(*values):
@@ -107,18 +105,35 @@
         return terms
 
     three = along_x(3, mine[3])
-    two = along_x(2, mine[2])
     near_three = sum(three[1:], three[0])
     in_three = plan.send(near_three, "z", INWARD)
-    in_three, near_two, *beside = together(in_three, sum(two[1:], two[0]), *beside)
+    middle = plan.send(near_three, "z", MIDDLE)
+    two = along_x(2, mine[2])
+    in_three, middle, near_two, *beside = together(in_three, middle, sum(two[1:], two[0]), *beside)
+    second = plan.send(near_two + in_three, "z", SECOND)
     one = along_x(1, mine[1])
-    across_two = plan.send(near_two + in_three, "z", MIDDLE)
-    in_two = plan.send(near_two, "z", INWARD)
-    across_two, in_two, near_one = together(across_two, in_two, sum(one[1:], one[0]))
+    pair = plan.send(sum(one[1:], one[0]), "z", PAIRS)
     zero = along_x(0, mine[0])
-    pair = plan.send(near_one + across_two, "z", PAIRS)
-    across_three = plan.send(near_three + in_two, "z", MIDDLE)
-    return zero + [pair, across_three] + beside
+    return [add_early(zero[0], second, middle)] + zero[1:] + [pair] + beside
+
+
+def add_early(*terms):
+    def kernel(*refs):
+        total = refs[0][...]
+        for ref in refs[1:-1]:
+            total = total + ref[...]
+        refs[-1][...] = total
+
+    vmem = pl.BlockSpec(memory_space=pltpu.VMEM)
+    return pl.pallas_call(
+        kernel,
+        out_shape=jax.ShapeDtypeStruct(terms[0].shape, jnp.float32),
+        in_specs=[vmem] * len(terms),
+        out_specs=vmem,
+        compiler_params=pltpu.CompilerParams(vmem_limit_bytes=8 * MIB),
+        cost_estimate=pl.CostEstimate(flops=0, bytes_accessed=36 * MIB, transcendentals=0),
+        name="add_early",
+    )(*terms)
 
 
 def gather(plan, block):
@@ -131,16 +146,17 @@
     else:
         line = along_x(block)
         pair = plan.send(block, "z", PAIRS)
-        three = plan.send(block, "z", MIDDLE)
-        three, own, *line = together(three, jnp.concatenate([block, pair]), *line)
+        second = plan.send(block, "z", SECOND)
         line_pair = along_x(pair)
-        two = plan.send(pair, "z", MIDDLE)
-        out_two = plan.send(three, "z", OUTWARD)
+        tail, own, *line = together(
+            add_early(second[plan.own :], block[plan.own :]), jnp.concatenate([block, pair]), *line
+        )
         far = [jnp.concatenate([line[x], line_pair[x]]) for x in range(1, plan.nx)]
-        near_two, *far = together(two + out_two, *far)
-        line_two = along_x(near_two)
-        out_three = plan.send(two, "z", OUTWARD)
-        line_three = along_x(three + out_three)
+        same, tail, *far = together(block, tail, *far)
+        middle = plan.send(same, "z", MIDDLE)
+        line_two = along_x(second)
+        out_three = plan.send(second, "z", OUTWARD)
+        line_three = along_x(middle + out_three)
         own, *line_two = together(own, *line_two)
         mine = [(value, [(0, x), (1, x)]) for x, value in enumerate([own] + far)]
         mine += [(value, [(2, x)]) for x, value in enumerate(line_two)]
@@ -155,12 +171,9 @@
         return [value]
     if count == 2:
         return [value, plan.send(value, axis, PAIR)]
-    pair = plan.send(value, axis, PAIRS)
-    across_three = plan.send(value, axis, MIDDLE)
-    across_two = plan.send(pair, axis, MIDDLE)
-    out_two = plan.send(across_three, axis, OUTWARD)
-    out_three = plan.send(across_two, axis, OUTWARD)
-    return [value, pair, across_two + out_two, across_three + out_three]
+    second = plan.send(value, axis, SECOND)
+    third = plan.send(value, axis, MIDDLE) + plan.send(second, axis, OUTWARD)
+    return [value, plan.send(value, axis, PAIRS), second, third]
 
 
 def place_kernel(plan, place_ref, owner_ref, norm_ref, grads_ref, *refs):

time: 173 us -> 194 us (1.12)
  waiting for transfers between devices: 80.1 us -> 111 us
  starting transfers between devices: 37.9 us -> 28.4 us
    ppermute x28 -> x26, waiting for transfers between devices: 78 us -> 109 us  [send(): return lax.ppermute(value, 'dp', every)]
    ppermute x28 -> x26, starting transfers between devices: 36.4 us -> 26.9 us  [send(): return lax.ppermute(value, 'dp', every)]
  transfers between devices with their start and end apart: 29 -> 27, of which waited for: 17 -> 13; matrix products, arithmetic and copies ran while one was open for 1% -> 0% of each run, Pallas kernels for 4% -> 3%
where the time goes in v12:
time: 194 us
  waiting for transfers between devices  111 us (57%)
  Pallas kernels  50.9 us (26%)
  starting transfers between devices  28.4 us (15%)
  other arithmetic  2.51 us (1%)
    ppermute x26, waiting for transfers between devices, send(): return lax.ppermute(value, 'dp', every)  109 us
    ppermute x26, starting transfers between devices, send(): return lax.ppermute(value, 'dp', every)  26.9 us
    pallas_call x1, Pallas kernels, place(): pl.pallas_call(functools.partial(place_kernel, plan), out_shape=[jax.Shap...  22.2 us
    pallas_call x1, Pallas kernels, finish(): pl.pallas_call(functools.partial(finish_kernel, plan, tile, slots), grid=...  19.6 us
    pallas_call x1, Pallas kernels, owned(): pl.pallas_call(functools.partial(owned_kernel, plan), out_shape=[jax.Shap...  6.31 us
  transfers between devices with their start and end apart: 27, of which 13 were waited for; matrix products, arithmetic and copies ran while one was open for 0% of the time, Pallas kernels for 3%

profile of v12, /device:TPU:0, one launch (start us, length us, event | category | flops | bytes accessed | tf_op | source)
XLA Modules:
  0.0 193.9 jit_solution(2570943478026429969)
XLA Ops:
  0.7 0.6 pad_add_fusion.place_ref
  1.3 22.2 %place_gradients.1 = (f32[2192,128]{1,0:T(8,128)}, f32[2192,128]{1,0:T(8,128)}, f32[2192,128]{1,0:T(8,128)}, f32[2192,128]{1,0:T(8,128)}, f32[2192,128]{1,0:T(8,...) custom-call(s32[3]{0:T(128)} %pad_add_fusion.place_ref, ...), custom_call_target="tpu_custom_call" | custom-call | tf_op jit(solution)/shard_map/place_gradients/pallas_call | solution.py:257
  23.5 0.5 collective-permute-start
  24.0 2.6 %collective-permute-done = f32[2192,128]{1,0:T(8,128)S(1)} collective-permute-done((f32[2192,128]{1,0:T(8,128)}, f32[2192,128]{1,0:T(8,128)S(1)}, u32[]{:S(2)}, u32[]{:S(2)}) %collective-permute-start) | collective-permute-done | bytes 1122336 | tf_op jit(solution)/shard_map/ppermute | solution.py:74
  26.6 1.1 slice_add_fusion.7
  27.7 0.4 collective-permute-start.5
  28.2 2.6 %collective-permute-start.2 = (f32[1096,128]{1,0:T(8,128)S(1)}, f32[1096,128]{1,0:T(8,128)S(1)}, u32[]{:S(2)}, u32[]{:S(2)}) collective-permute-start(f32[1096,128]{1,0:T(8,128)S(1)} %slice_add_fusion.7), channel_id=1, source_target_pairs={{0,4},{2,6},{4,0},{6,2},{8,12},{10,14},{12,8},{14,10},{16,20},{18,... | collective-permute-start | bytes 1683464 | tf_op jit(solution)/shard_map/ppermute | solution.py:74
  30.8 0.1 collective-permute-start.9
  30.9 6.3 %owned_weights.1 = (f32[1088,128]{1,0:T(8,128)}, s32[1152,128]{1,0:T(8,128)}) custom-call(s32[3]{0:T(128)} %pad_add_fusion.place_ref, s32[136,128]{1,0:T(8,128)} %bitcast.16, f32[17408,128]{1,0:T(8,128)} %weights_ref.3), custom_call_target="tpu_custom_call" | custom-call | bytes 20971520 | tf_op jit(solution)/shard_map/owned_weights/pallas_call | solution.py:335
  37.2 0.5 collective-permute-start.1
  37.7 6.3 %collective-permute-done.2 = f32[1096,128]{1,0:T(8,128)S(1)} collective-permute-done((f32[1096,128]{1,0:T(8,128)S(1)}, f32[1096,128]{1,0:T(8,128)S(1)}, u32[]{:S(2)}, u32[]{:S(2)}) %collective-permute-start.2) | collective-permute-done | bytes 561184 | tf_op jit(solution)/shard_map/ppermute | solution.py:74
  44.0 0.1 fusion.2
  44.2 0.8 collective-permute-start.4
  45.0 6.6 %collective-permute-start.3 = (f32[1096,128]{1,0:T(8,128)S(1)}, f32[1096,128]{1,0:T(8,128)S(1)}, u32[]{:S(2)}, u32[]{:S(2)}) collective-permute-start(f32[1096,128]{1,0:T(8,128)S(1)} %fusion.2), channel_id=1, source_target_pairs={{0,8},{2,10},{4,12},{6,14},{24,16},{26,18},{28,20},{30,22},{1,9},{... | collective-permute-start | bytes 1683464 | tf_op jit(solution)/shard_map/ppermute | solution.py:74
  51.6 0.1 slice_add_fusion.3
  51.7 1.6 collective-permute-start.6
  53.2 0.0 collective-permute-done.9
  53.2 0.1 slice_add_fusion
  53.3 0.6 collective-permute-start.10
  53.9 0.0 collective-permute-done.1
  53.9 0.1 slice_add_fusion.2
  54.0 1.6 collective-permute-start.8
  55.6 11.8 %collective-permute-done.6 = f32[1096,128]{1,0:T(8,128)S(1)} collective-permute-done((f32[1096,128]{1,0:T(8,128)S(1)}, f32[1096,128]{1,0:T(8,128)S(1)}, u32[]{:S(2)}, u32[]{:S(2)}) %collective-permute-start.6) | collective-permute-done | bytes 561184 | tf_op jit(solution)/shard_map/ppermute | solution.py:74
  67.4 0.1 fusion.1
  67.5 0.0 collective-permute-done.4.refs_2_
  67.5 0.0 slice-start.1
  67.5 0.1 add.63
  67.6 0.1 collective-permute-start.7
  67.7 11.7 %collective-permute-done.10 = f32[1096,128]{1,0:T(8,128)S(1)} collective-permute-done((f32[1096,128]{1,0:T(8,128)S(1)}, f32[1096,128]{1,0:T(8,128)S(1)}, u32[]{:S(2)}, u32[]{:S(2)}) %collective-permute-start.10) | collective-permute-done | bytes 561184 | tf_op jit(solution)/shard_map/ppermute | solution.py:74
  79.4 0.1 fusion
  79.5 0.1 collective-permute-start.11
  79.6 11.4 %collective-permute-done.7.refs_1_ = f32[1096,128]{1,0:T(8,128)S(1)} collective-permute-done((f32[1096,128]{1,0:T(8,128)S(1)}, f32[1096,128]{1,0:T(8,128)S(1)}, u32[]{:S(2)}, u32[]{:S(2)}) %collective-permute-start.7) | collective-permute-done | bytes 561184 | tf_op jit(solution)/shard_map/ppermute | solution.py:74
  91.0 0.1 add_early.2.refs_0_
  91.1 0.0 collective-permute-done.8.refs_1_
  91.1 10.9 %collective-permute-done.11.refs_2_ = f32[1096,128]{1,0:T(8,128)S(1)} collective-permute-done((f32[1096,128]{1,0:T(8,128)S(1)}, f32[1096,128]{1,0:T(8,128)S(1)}, u32[]{:S(2)}, u32[]{:S(2)}) %collective-permute-start.11) | collective-permute-done | bytes 561184 | tf_op jit(solution)/shard_map/ppermute | solution.py:74
  102.1 0.0 slice-start.2
  102.1 2.6 %moments.1 = (f32[1088,128]{1,0:T(8,128)}, f32[1088,128]{1,0:T(8,128)}, f32[1096,128]{1,0:T(8,128)S(1)}, f32[8,128]{1,0:T(8,128)S(1)}) custom-call(f32[1096,128]{1,0:T(8,128)S(1)} %add_early.2.refs_0_, f32[1096,128]{1,0:T(8,128)S(1)} %collective-permute-done.8.refs_1_, f32[1096,128]{1,0:T(8,128)S(1)} %collective-permute-done.11.refs_2_, ...), custom_call_target="tpu_custom_call" | custom-call | tf_op jit(solution)/shard_map/moments/pallas_call | solution.py:390
  104.7 1.5 collective-permute-start.12
  106.2 2.1 %collective-permute-done.12 = f32[8,128]{1,0:T(8,128)S(1)} collective-permute-done((f32[8,128]{1,0:T(8,128)S(1)}, f32[8,128]{1,0:T(8,128)S(1)}, u32[]{:S(2)}, u32[]{:S(2)}) %collective-permute-start.12) | collective-permute-done | bytes 4128 | tf_op jit(solution)/shard_map/ppermute | solution.py:524
  108.3 0.0 collective-permute-start.13
  108.3 1.6 collective-permute-start.14
  109.8 2.0 %collective-permute-start.15 = (f32[1096,128]{1,0:T(8,128)S(1)}, f32[1096,128]{1,0:T(8,128)S(1)}, u32[]{:S(2)}, u32[]{:S(2)}) collective-permute-start(f32[1096,128]{1,0:T(8,128)S(1)} %add_dynamic-update-slice_fusion), channel_id=1, source_target_pairs={{0,16},{2,18},{4,20},{6,22},{8,24},{10,26},{12,28},{14,30},{16,0},... | collective-permute-start | bytes 1683464 | tf_op jit(solution)/shard_map/ppermute | solution.py:74
  111.8 18.6 %collective-permute-done.13 = f32[1096,128]{1,0:T(8,128)S(1)} collective-permute-done((f32[1096,128]{1,0:T(8,128)S(1)}, f32[1096,128]{1,0:T(8,128)S(1)}, u32[]{:S(2)}, u32[]{:S(2)}) %collective-permute-start.13) | collective-permute-done | bytes 561184 | tf_op jit(solution)/shard_map/ppermute | solution.py:74
  130.4 2.5 %collective-permute-start.17 = (f32[1096,128]{1,0:T(8,128)S(1)}, f32[1096,128]{1,0:T(8,128)S(1)}, u32[]{:S(2)}, u32[]{:S(2)}) collective-permute-start(f32[1096,128]{1,0:T(8,128)S(1)} %collective-permute-done.13), channel_id=1, source_target_pairs={{0,4},{2,6},{4,0},{6,2},{8,12},{10,14},{12,8},{14,10},{16,20},{18,... | collective-permute-start | bytes 1683464 | tf_op jit(solution)/shard_map/ppermute | solution.py:74
  132.8 0.1 pad_maximum_fusion.refs_0_
  132.9 2.2 %collective-permute-done.15.refs_2_ = f32[1096,128]{1,0:T(8,128)S(1)} collective-permute-done((f32[1096,128]{1,0:T(8,128)S(1)}, f32[1096,128]{1,0:T(8,128)S(1)}, u32[]{:S(2)}, u32[]{:S(2)}) %collective-permute-start.15) | collective-permute-done | bytes 561184 | tf_op jit(solution)/shard_map/ppermute | solution.py:74
  135.1 1.3 collective-permute-start.19
  136.4 0.6 collective-permute-start.16
  137.0 9.5 %collective-permute-done.17 = f32[1096,128]{1,0:T(8,128)S(1)} collective-permute-done((f32[1096,128]{1,0:T(8,128)S(1)}, f32[1096,128]{1,0:T(8,128)S(1)}, u32[]{:S(2)}, u32[]{:S(2)}) %collective-permute-start.17) | collective-permute-done | bytes 561184 | tf_op jit(solution)/shard_map/ppermute | solution.py:74
  146.4 0.1 pad_maximum_fusion.1.refs_1_
  146.5 0.0 copy-start.5
  146.6 0.8 collective-permute-start.18
  147.4 9.1 %collective-permute-done.16.refs_3_ = f32[1096,128]{1,0:T(8,128)S(1)} collective-permute-done((f32[1096,128]{1,0:T(8,128)S(1)}, f32[1096,128]{1,0:T(8,128)S(1)}, u32[]{:S(2)}, u32[]{:S(2)}) %collective-permute-start.16) | collective-permute-done | bytes 561184 | tf_op jit(solution)/shard_map/ppermute | solution.py:74
  156.5 0.0 collective-permute-start.23
  156.5 0.5 collective-permute-start.22
  157.0 0.0 collective-permute-start.21
  157.0 0.0 collective-permute-done.19
  157.0 0.1 add.70.refs_4_
  157.0 1.8 collective-permute-start.20
  158.9 0.2 collective-permute-start.24
  159.1 0.3 collective-permute-start.25
  159.4 12.9 %collective-permute-done.20.refs_5_ = f32[1096,128]{1,0:T(8,128)S(1)} collective-permute-done((f32[1096,128]{1,0:T(8,128)S(1)}, f32[1096,128]{1,0:T(8,128)S(1)}, u32[]{:S(2)}, u32[]{:S(2)}) %collective-permute-start.20) | collective-permute-done | bytes 561184 | tf_op jit(solution)/shard_map/ppermute | solution.py:74
  172.3 1.9 collective-permute-done.26.refs_11_
  174.2 19.6 %new_weights.1 = (f32[17408,128]{1,0:T(8,128)}, f32[3,2,1024]{2,1,0:T(2,128)}, f32[7]{0:T(128)}) custom-call(s32[3]{0:T(128)S(1)} %copy-done.6, s32[136,128]{1,0:T(8,128)S(1)} %copy-done.4, f32[3,2,1024]{2,1,0:T(2,128)S(1)} %copy-done.5, f32[17408,128]{1,0:T(8,128)S(1)} %bitcast.11, f32[2192,128]{1,0:T(8,128)S(1)} %pad_maximum_fusion.refs_0_, ...), custom_call_target="tpu_custom_call" | custom-call | tf_op jit(solution)/shard_map/new_weights/pallas_call | solution.py:469
  (37 shorter events, 0.1 us)
Async XLA Ops:
  23.5 3.1 %collective-permute-start = (f32[2192,128]{1,0:T(8,128)}, f32[2192,128]{1,0:T(8,128)S(1)}, u32[]{:S(2)}, u32[]{:S(2)}) collective-permute-start(f32[2192,128]{1,0:T(8,128)} %get-tuple-element.42), channel_id=1, source_target_pairs={{0,2},{2,0},{4,6},{6,4},{8,10},{10,8},{12,14},{14,12},{16,18},{18,... | collective-permute-start | bytes 3366920 | tf_op jit(solution)/shard_map/ppermute | solution.py:74
  27.7 16.3 %copy-start.10 = (f32[2192,128]{1,0:T(8,128)S(1)}, f32[2192,128]{1,0:T(8,128)}, u32[]{:S(2)}) copy-start(f32[2192,128]{1,0:T(8,128)} %get-tuple-element.41) | copy-start | bytes 3366916
  27.7 23.8 %collective-permute-start.5 = (f32[2192,128]{1,0:T(8,128)}, f32[2192,128]{1,0:T(8,128)S(1)}, u32[]{:S(2)}, u32[]{:S(2)}) collective-permute-start(f32[2192,128]{1,0:T(8,128)} %get-tuple-element.49), channel_id=1, source_target_pairs={{0,2},{2,0},{4,6},{6,4},{8,10},{10,8},{12,14},{14,12},{16,18},{18,... | collective-permute-start | bytes 3366920 | tf_op jit(solution)/shard_map/ppermute | solution.py:74
  28.2 15.9 %collective-permute-start.2 = (f32[1096,128]{1,0:T(8,128)S(1)}, f32[1096,128]{1,0:T(8,128)S(1)}, u32[]{:S(2)}, u32[]{:S(2)}) collective-permute-start(f32[1096,128]{1,0:T(8,128)S(1)} %slice_add_fusion.7), channel_id=1, source_target_pairs={{0,4},{2,6},{4,0},{6,2},{8,12},{10,14},{12,8},{14,10},{16,20},{18,... | collective-permute-start | bytes 1683464 | tf_op jit(solution)/shard_map/ppermute | solution.py:74
  30.8 22.4 %collective-permute-start.9 = (f32[2192,128]{1,0:T(8,128)}, f32[2192,128]{1,0:T(8,128)S(1)}, u32[]{:S(2)}, u32[]{:S(2)}) collective-permute-start(f32[2192,128]{1,0:T(8,128)} %get-tuple-element.56), channel_id=1, source_target_pairs={{0,2},{2,0},{4,6},{6,4},{8,10},{10,8},{12,14},{14,12},{16,18},{18,... | collective-permute-start | bytes 3366920 | tf_op jit(solution)/shard_map/ppermute | solution.py:74
  37.2 14.4 %copy-start.8 = (f32[2192,128]{1,0:T(8,128)S(1)}, f32[2192,128]{1,0:T(8,128)}, u32[]{:S(2)}) copy-start(f32[2192,128]{1,0:T(8,128)} %get-tuple-element.48) | copy-start | bytes 3366916
  37.2 16.7 %collective-permute-start.1 = (f32[2192,128]{1,0:T(8,128)}, f32[2192,128]{1,0:T(8,128)S(1)}, u32[]{:S(2)}, u32[]{:S(2)}) collective-permute-start(f32[2192,128]{1,0:T(8,128)} %get-tuple-element.46), channel_id=1, source_target_pairs={{0,2},{2,0},{4,6},{6,4},{8,10},{10,8},{12,14},{14,12},{16,18},{18,... | collective-permute-start | bytes 3366920 | tf_op jit(solution)/shard_map/ppermute | solution.py:74
  44.2 9.1 %copy-start.7 = (f32[2192,128]{1,0:T(8,128)S(1)}, f32[2192,128]{1,0:T(8,128)}, u32[]{:S(2)}) copy-start(f32[2192,128]{1,0:T(8,128)} %get-tuple-element.55) | copy-start | bytes 3366916
  44.2 23.3 %collective-permute-start.4 = (f32[1096,128]{1,0:T(8,128)S(1)}, f32[1096,128]{1,0:T(8,128)S(1)}, u32[]{:S(2)}, u32[]{:S(2)}) collective-permute-start(f32[1096,128]{1,0:T(8,128)S(1)} %fusion.2), channel_id=1, source_target_pairs={{8,16},{10,18},{12,20},{14,22},{16,8},{18,10},{20,12},{22,14},{9,1... | collective-permute-start | bytes 1683464 | tf_op jit(solution)/shard_map/ppermute | solution.py:74
  45.0 22.5 %collective-permute-start.3 = (f32[1096,128]{1,0:T(8,128)S(1)}, f32[1096,128]{1,0:T(8,128)S(1)}, u32[]{:S(2)}, u32[]{:S(2)}) collective-permute-start(f32[1096,128]{1,0:T(8,128)S(1)} %fusion.2), channel_id=1, source_target_pairs={{0,8},{2,10},{4,12},{6,14},{24,16},{26,18},{28,20},{30,22},{1,9},{... | collective-permute-start | bytes 1683464 | tf_op jit(solution)/shard_map/ppermute | solution.py:74
  51.7 2.2 %copy-start.9 = (f32[2192,128]{1,0:T(8,128)S(1)}, f32[2192,128]{1,0:T(8,128)}, u32[]{:S(2)}) copy-start(f32[2192,128]{1,0:T(8,128)} %get-tuple-element.40) | copy-start | bytes 3366916
  51.7 15.7 %collective-permute-start.6 = (f32[1096,128]{1,0:T(8,128)S(1)}, f32[1096,128]{1,0:T(8,128)S(1)}, u32[]{:S(2)}, u32[]{:S(2)}) collective-permute-start(f32[1096,128]{1,0:T(8,128)S(1)} %slice_add_fusion.3), channel_id=1, source_target_pairs={{0,4},{2,6},{4,0},{6,2},{8,12},{10,14},{12,8},{14,10},{16,20},{18,... | collective-permute-start | bytes 1683464 | tf_op jit(solution)/shard_map/ppermute | solution.py:74
  53.2 121.0 %slice-start = ((s8[8912896]{0:T(1024)(128)(4,1)}), s8[4194304]{0:T(1024)(128)(4,1)S(1)}, s32[]{:S(2)}) async-start(s8[8912896]{0:T(1024)(128)(4,1)} %bitcast.10), calls=%async_computation | async-start | bytes 8388608
  53.3 26.1 %collective-permute-start.10 = (f32[1096,128]{1,0:T(8,128)S(1)}, f32[1096,128]{1,0:T(8,128)S(1)}, u32[]{:S(2)}, u32[]{:S(2)}) collective-permute-start(f32[1096,128]{1,0:T(8,128)S(1)} %slice_add_fusion), channel_id=1, source_target_pairs={{0,4},{2,6},{4,0},{6,2},{8,12},{10,14},{12,8},{14,10},{16,20},{18,... | collective-permute-start | bytes 1683464 | tf_op jit(solution)/shard_map/ppermute | solution.py:74
  54.0 37.1 %collective-permute-start.8 = (f32[1096,128]{1,0:T(8,128)S(1)}, f32[1096,128]{1,0:T(8,128)S(1)}, u32[]{:S(2)}, u32[]{:S(2)}) collective-permute-start(f32[1096,128]{1,0:T(8,128)S(1)} %get-tuple-element.73), channel_id=1, source_target_pairs={{0,4},{2,6},{4,0},{6,2},{8,12},{10,14},{12,8},{14,10},{16,20},{18,... | collective-permute-start | bytes 1683464 | tf_op jit(solution)/shard_map/ppermute | solution.py:74
  67.4 34.7 %copy-start.3 = (f32[1088,128]{1,0:T(8,128)S(1)}, f32[1088,128]{1,0:T(8,128)}, u32[]{:S(2)}) copy-start(f32[1088,128]{1,0:T(8,128)} %get-tuple-element.57.refs_5_) | copy-start | bytes 1671172
  67.5 106.7 %slice-start.1 = ((s8[8912896]{0:T(1024)(128)(4,1)}), s8[4194304]{0:T(1024)(128)(4,1)S(1)}, s32[]{:S(2)}) async-start(s8[8912896]{0:T(1024)(128)(4,1)} %bitcast.10), calls=%async_computation.1 | async-start | bytes 8388608
  67.6 23.4 %collective-permute-start.7 = (f32[1096,128]{1,0:T(8,128)S(1)}, f32[1096,128]{1,0:T(8,128)S(1)}, u32[]{:S(2)}, u32[]{:S(2)}) collective-permute-start(f32[1096,128]{1,0:T(8,128)S(1)} %add.63), channel_id=1, source_target_pairs={{0,16},{2,18},{4,20},{6,22},{8,24},{10,26},{12,28},{14,30},{16,0},... | collective-permute-start | bytes 1683464 | tf_op jit(solution)/shard_map/ppermute | solution.py:74
  79.5 22.5 %collective-permute-start.11 = (f32[1096,128]{1,0:T(8,128)S(1)}, f32[1096,128]{1,0:T(8,128)S(1)}, u32[]{:S(2)}, u32[]{:S(2)}) collective-permute-start(f32[1096,128]{1,0:T(8,128)S(1)} %fusion), channel_id=1, source_target_pairs={{0,8},{2,10},{4,12},{6,14},{8,0},{10,2},{12,4},{14,6},{16,24},{18,... | collective-permute-start | bytes 1683464 | tf_op jit(solution)/shard_map/ppermute | solution.py:74
  91.0 11.0 %copy-start = (s32[1152,128]{1,0:T(8,128)S(1)}, s32[1152,128]{1,0:T(8,128)}, u32[]{:S(2)}) copy-start(s32[1152,128]{1,0:T(8,128)} %get-tuple-element.58.refs_6_) | copy-start | bytes 1769476
  91.0 11.0 %copy-start.1 = (f32[1,1088,128]{2,1,0:T(8,128)S(1)}, f32[1,1088,128]{2,1,0:T(8,128)}, u32[]{:S(2)}) copy-start(f32[1,1088,128]{2,1,0:T(8,128)} %param.9) | copy-start | bytes 1671172
  91.0 11.1 %copy-start.2 = (f32[1,1088,128]{2,1,0:T(8,128)S(1)}, f32[1,1088,128]{2,1,0:T(8,128)}, u32[]{:S(2)}) copy-start(f32[1,1088,128]{2,1,0:T(8,128)} %param.10) | copy-start | bytes 1671172
  102.1 72.1 %slice-start.2 = ((s8[8912896]{0:T(1024)(128)(4,1)}), s8[524288]{0:T(1024)(128)(4,1)S(1)}, s32[]{:S(2)}) async-start(s8[8912896]{0:T(1024)(128)(4,1)} %bitcast.10), calls=%async_computation.2 | async-start | bytes 1048576
  104.7 3.6 %collective-permute-start.12 = (f32[8,128]{1,0:T(8,128)S(1)}, f32[8,128]{1,0:T(8,128)S(1)}, u32[]{:S(2)}, u32[]{:S(2)}) collective-permute-start(f32[8,128]{1,0:T(8,128)S(1)} %get-tuple-element.60), channel_id=1, source_target_pairs={{0,1},{1,0},{2,3},{3,2},{4,5},{5,4},{6,7},{7,6},{8,9},{9,8},{10,11... | collective-permute-start | bytes 12296 | tf_op jit(solution)/shard_map/ppermute | solution.py:524
  108.3 22.1 %collective-permute-start.13 = (f32[1096,128]{1,0:T(8,128)S(1)}, f32[1096,128]{1,0:T(8,128)S(1)}, u32[]{:S(2)}, u32[]{:S(2)}) collective-permute-start(f32[1096,128]{1,0:T(8,128)S(1)} %add_dynamic-update-slice_fusion), channel_id=1, source_target_pairs={{0,8},{2,10},{4,12},{6,14},{8,0},{10,2},{12,4},{14,6},{16,24},{18,... | collective-permute-start | bytes 1683464 | tf_op jit(solution)/shard_map/ppermute | solution.py:74
  108.3 24.6 %collective-permute-start.14 = (f32[1096,128]{1,0:T(8,128)S(1)}, f32[1096,128]{1,0:T(8,128)S(1)}, u32[]{:S(2)}, u32[]{:S(2)}) collective-permute-start(f32[1096,128]{1,0:T(8,128)S(1)} %add_dynamic-update-slice_fusion), channel_id=1, source_target_pairs={{0,4},{2,6},{4,0},{6,2},{8,12},{10,14},{12,8},{14,10},{16,20},{18,... | collective-permute-start | bytes 1683464 | tf_op jit(solution)/shard_map/ppermute | solution.py:74
  109.8 25.2 %collective-permute-start.15 = (f32[1096,128]{1,0:T(8,128)S(1)}, f32[1096,128]{1,0:T(8,128)S(1)}, u32[]{:S(2)}, u32[]{:S(2)}) collective-permute-start(f32[1096,128]{1,0:T(8,128)S(1)} %add_dynamic-update-slice_fusion), channel_id=1, source_target_pairs={{0,16},{2,18},{4,20},{6,22},{8,24},{10,26},{12,28},{14,30},{16,0},... | collective-permute-start | bytes 1683464 | tf_op jit(solution)/shard_map/ppermute | solution.py:74
  130.4 16.1 %collective-permute-start.17 = (f32[1096,128]{1,0:T(8,128)S(1)}, f32[1096,128]{1,0:T(8,128)S(1)}, u32[]{:S(2)}, u32[]{:S(2)}) collective-permute-start(f32[1096,128]{1,0:T(8,128)S(1)} %collective-permute-done.13), channel_id=1, source_target_pairs={{0,4},{2,6},{4,0},{6,2},{8,12},{10,14},{12,8},{14,10},{16,20},{18,... | collective-permute-start | bytes 1683464 | tf_op jit(solution)/shard_map/ppermute | solution.py:74
  135.1 21.9 %collective-permute-start.19 = (f32[1096,128]{1,0:T(8,128)S(1)}, f32[1096,128]{1,0:T(8,128)S(1)}, u32[]{:S(2)}, u32[]{:S(2)}) collective-permute-start(f32[1096,128]{1,0:T(8,128)S(1)} %collective-permute-done.15.refs_2_), channel_id=1, source_target_pairs={{8,0},{10,2},{12,4},{14,6},{16,24},{18,26},{20,28},{22,30},{9,1},{... | collective-permute-start | bytes 1683464 | tf_op jit(solution)/shard_map/ppermute | solution.py:74
  136.4 20.1 %collective-permute-start.16 = (f32[1096,128]{1,0:T(8,128)S(1)}, f32[1096,128]{1,0:T(8,128)S(1)}, u32[]{:S(2)}, u32[]{:S(2)}) collective-permute-start(f32[1096,128]{1,0:T(8,128)S(1)} %collective-permute-done.15.refs_2_), channel_id=1, source_target_pairs={{0,4},{2,6},{4,0},{6,2},{8,12},{10,14},{12,8},{14,10},{16,20},{18,... | collective-permute-start | bytes 1683464 | tf_op jit(solution)/shard_map/ppermute | solution.py:74
  146.5 27.7 %copy-start.4 = (s32[136,128]{1,0:T(8,128)S(1)}, s32[136,128]{1,0:T(8,128)}, u32[]{:S(2)}) copy-start(s32[136,128]{1,0:T(8,128)} %get-tuple-element.39.position_ref) | copy-start | bytes 208900
  146.5 27.7 %copy-start.5 = (f32[3,2,1024]{2,1,0:T(2,128)S(1)}, f32[3,2,1024]{2,1,0:T(2,128)}, u32[]{:S(2)}) copy-start(f32[3,2,1024]{2,1,0:T(2,128)} %norm_ref.1) | copy-start | bytes 73732
  146.5 27.7 %copy-start.6 = (s32[3]{0:T(128)S(1)}, s32[3]{0:T(128)}, u32[]{:S(2)}) copy-start(s32[3]{0:T(128)} %pad_add_fusion.place_ref) | copy-start | bytes 40
  146.6 10.4 %collective-permute-start.18 = (f32[1096,128]{1,0:T(8,128)S(1)}, f32[1096,128]{1,0:T(8,128)S(1)}, u32[]{:S(2)}, u32[]{:S(2)}) collective-permute-start(f32[1096,128]{1,0:T(8,128)S(1)} %add_dynamic-update-slice_fusion), channel_id=1, source_target_pairs={{8,16},{10,18},{12,20},{14,22},{16,8},{18,10},{20,12},{22,14},{9,1... | collective-permute-start | bytes 1683464 | tf_op jit(solution)/shard_map/ppermute | solution.py:74
  156.5 2.6 %collective-permute-start.23 = (f32[1096,128]{1,0:T(8,128)S(1)}, f32[1096,128]{1,0:T(8,128)S(1)}, u32[]{:S(2)}, u32[]{:S(2)}) collective-permute-start(f32[1096,128]{1,0:T(8,128)S(1)} %collective-permute-done.15.refs_2_), channel_id=1, source_target_pairs={{0,2},{2,0},{4,6},{6,4},{8,10},{10,8},{12,14},{14,12},{16,18},{18,... | collective-permute-start | bytes 1683464 | tf_op jit(solution)/shard_map/ppermute | solution.py:74
  156.5 15.8 %collective-permute-start.22 = (f32[2192,128]{1,0:T(8,128)S(1)}, f32[2192,128]{1,0:T(8,128)S(1)}, u32[]{:S(2)}, u32[]{:S(2)}) collective-permute-start(f32[2192,128]{1,0:T(8,128)S(1)} %pad_maximum_fusion.1.refs_1_), channel_id=1, source_target_pairs={{0,2},{2,0},{4,6},{6,4},{8,10},{10,8},{12,14},{14,12},{16,18},{18,... | collective-permute-start | bytes 3366920 | tf_op jit(solution)/shard_map/ppermute | solution.py:74
  157.0 15.3 %collective-permute-start.21 = (f32[2192,128]{1,0:T(8,128)S(1)}, f32[2192,128]{1,0:T(8,128)S(1)}, u32[]{:S(2)}, u32[]{:S(2)}) collective-permute-start(f32[2192,128]{1,0:T(8,128)S(1)} %pad_maximum_fusion.refs_0_), channel_id=1, source_target_pairs={{0,2},{2,0},{4,6},{6,4},{8,10},{10,8},{12,14},{14,12},{16,18},{18,... | collective-permute-start | bytes 3366920 | tf_op jit(solution)/shard_map/ppermute | solution.py:74
  157.0 15.2 %collective-permute-start.20 = (f32[1096,128]{1,0:T(8,128)S(1)}, f32[1096,128]{1,0:T(8,128)S(1)}, u32[]{:S(2)}, u32[]{:S(2)}) collective-permute-start(f32[1096,128]{1,0:T(8,128)S(1)} %add.70.refs_4_), channel_id=1, source_target_pairs={{0,4},{2,6},{4,0},{6,2},{8,12},{10,14},{12,8},{14,10},{16,20},{18,... | collective-permute-start | bytes 1683464 | tf_op jit(solution)/shard_map/ppermute | solution.py:74
  158.9 13.4 %collective-permute-start.24 = (f32[1096,128]{1,0:T(8,128)S(1)}, f32[1096,128]{1,0:T(8,128)S(1)}, u32[]{:S(2)}, u32[]{:S(2)}) collective-permute-start(f32[1096,128]{1,0:T(8,128)S(1)} %collective-permute-done.16.refs_3_), channel_id=1, source_target_pairs={{0,2},{2,0},{4,6},{6,4},{8,10},{10,8},{12,14},{14,12},{16,18},{18,... | collective-permute-start | bytes 1683464 | tf_op jit(solution)/shard_map/ppermute | solution.py:74
  159.1 13.2 %collective-permute-start.25 = (f32[1096,128]{1,0:T(8,128)S(1)}, f32[1096,128]{1,0:T(8,128)S(1)}, u32[]{:S(2)}, u32[]{:S(2)}) collective-permute-start(f32[1096,128]{1,0:T(8,128)S(1)} %add.70.refs_4_), channel_id=1, source_target_pairs={{0,2},{2,0},{4,6},{6,4},{8,10},{10,8},{12,14},{14,12},{16,18},{18,... | collective-permute-start | bytes 1683464 | tf_op jit(solution)/shard_map/ppermute | solution.py:74
  172.2 2.0 %collective-permute-start.26 = (f32[1096,128]{1,0:T(8,128)S(1)}, f32[1096,128]{1,0:T(8,128)S(1)}, u32[]{:S(2)}, u32[]{:S(2)}) collective-permute-start(f32[1096,128]{1,0:T(8,128)S(1)} %collective-permute-done.20.refs_5_), channel_id=1, source_target_pairs={{0,2},{2,0},{4,6},{6,4},{8,10},{10,8},{12,14},{14,12},{16,18},{18,... | collective-permute-start | bytes 1683464 | tf_op jit(solution)/shard_map/ppermute | solution.py:74

commit v13 on v10

--- a/solution.py
+++ b/solution.py
@@ -23,8 +23,8 @@
 decay_rate = 0.01
 matrices = 5
 MIB = 1 << 20
-TILES = 8
 PHASES = 2
+EARLY = 0.5
 
 
 def matrix_bounds(narrow):
@@ -50,7 +50,9 @@
         self.tail = 8
         self.norm_rows = 2 * D // LANE
         self.norm_each = -(-self.norm_rows // replicas)
-        self.block = self.own + self.tail
+        self.block = self.tail + self.own
+        self.early = int(self.own * EARLY / 8 + 0.5) * 8
+        self.cut = self.tail + self.early
         self.group = self.nx * self.block
         self.half = self.nz * self.group
         self.lists = -(-blocks // (8 * LANE)) * 8
@@ -122,40 +124,41 @@
 
 
 def gather(plan, block):
-    found = []
-
     def along_x(value):
         return line_gather(plan, "x", plan.nx, value)
 
-    def add(far_z, line, skip=0):
-        for far_x, value in enumerate(line):
-            found.append((value, [(far_z, far_x, 0)]))
-        for far_x, value in enumerate(line):
-            if far_x >= skip:
-                found.append((plan.swap(value), [(far_z, far_x, 1)]))
+    def parts(x, *zs):
+        return [((z, x), 0, plan.block) for z in zs]
 
     if plan.nz != 4:
-        for far_z, value in enumerate(line_gather(plan, "z", plan.nz, block)):
-            add(far_z, along_x(value))
-        return found
+        lines = [along_x(value) for value in line_gather(plan, "z", plan.nz, block)]
+        return [(value, parts(x, z)) for z, line in enumerate(lines) for x, value in enumerate(line)], []
     line = along_x(block)
     pair = plan.send(block, "z", PAIRS)
     three = plan.send(block, "z", MIDDLE)
-    both, three, *line = together(jnp.concatenate([block, pair]), three, *line)
+    three, own, *line = together(three, jnp.concatenate([block, pair]), *line)
     line_pair = along_x(pair)
     two = plan.send(pair, "z", MIDDLE)
     out_two = plan.send(three, "z", OUTWARD)
-    two, out_two, *line_pair = together(two, out_two, *line_pair)
-    found.append((both, [(0, 0, 0), (1, 0, 0)]))
-    found.append((plan.swap(both), [(0, 0, 1), (1, 0, 1)]))
-    line_two = along_x(two + out_two)
+    far = [jnp.concatenate([line[x], line_pair[x]]) for x in range(1, plan.nx)]
+    near_two, *far = together(two + out_two, *far)
+    line_two = along_x(near_two)
     out_three = plan.send(two, "z", OUTWARD)
-    out_three, *line_two = together(out_three, *line_two)
-    add(0, line, 1)
-    add(1, line_pair, 1)
-    add(2, line_two)
-    add(3, along_x(three + out_three))
-    return [(value, slots) for value, slots in found if slots[0][1:] != (0, 0) or slots[0][0] > 1 or len(slots) > 1]
+    line_early = along_x(three[: plan.cut] + out_three[: plan.cut])
+    line_late = along_x(three[plan.cut :] + out_three[plan.cut :])
+    own, *line_two = together(own, *line_two)
+    found = [(value, parts(x, 0, 1)) for x, value in enumerate([own] + far)]
+    found += [(value, parts(x, 2)) for x, value in enumerate(line_two)]
+    found += [(value, [((3, x), 0, plan.cut)]) for x, value in enumerate(line_early)]
+    late = [(value, [((3, x), plan.cut, plan.block - plan.cut)]) for x, value in enumerate(line_late)]
+    return found, late
+
+
+def both_cores(plan, found):
+    swapped = [(plan.swap(value), parts) for value, parts in found]
+    return [(value, [(slot + (0,), low, rows) for slot, low, rows in parts]) for value, parts in found] + [
+        (value, [(slot + (1,), low, rows) for slot, low, rows in parts]) for value, parts in swapped
+    ]
 
 
 def line_gather(plan, axis, count, value):
@@ -173,7 +176,7 @@
 
 def place_kernel(plan, place_ref, owner_ref, norm_ref, grads_ref, *refs):
     out_refs, refs = refs[: 2 * plan.nz], refs[2 * plan.nz :]
-    position_ref, raw, moved, position, sem_in, sem_position, sem_out = refs
+    position_ref, limit_ref, raw, moved, position, sem_in, sem_position, sem_out = refs
     fetch = pltpu.make_async_copy(grads_ref, raw, sem_in)
     fetch.start()
     lists = plan.lists
@@ -208,10 +211,12 @@
                     part = norm_ref[row * LANE // D : row * LANE // D + 1, row * LANE % D : row * LANE % D + LANE]
                     tail.insert(0, part.astype(jnp.float32))
                 tail = jnp.concatenate(tail, 0)[: plan.tail]
-                moved[pl.ds(pl.multiple_of(start + plan.own, 8), plan.tail), :] = tail
-                result = jnp.where(mine, rank + start, result)
+                moved[pl.ds(pl.multiple_of(start, 8), plan.tail), :] = tail
+                result = jnp.where(mine, rank + (start + plan.tail), result)
                 ranks = jnp.where(mine, rank, ranks)
     position_ref[...] = result
+    natural = lax.broadcasted_iota(jnp.int32, (lists, LANE), 0) * LANE + lax.broadcasted_iota(jnp.int32, (lists, LANE), 1)
+    limit_ref[0] = jnp.min(jnp.where((owners >= 0) & (ranks >= plan.early), natural, plan.blocks))
     to_scalar = pltpu.make_async_copy(position_ref, position, sem_position)
     to_scalar.start()
     to_scalar.wait()
@@ -234,8 +239,8 @@
                     moved[pl.ds(position[line, part + u], 1), :] = rows[u : u + 1, :]
 
         begin = end
-        low = cuts[phase - 1] if phase else 0
-        high = cut if phase < PHASES - 1 else plan.block
+        low = plan.tail + cuts[phase - 1] if phase else 0
+        high = plan.tail + cut
         for i, out in enumerate(out_refs):
             start = (i // plan.nz) * plan.half + (plan.nz - 1 - i % plan.nz) * plan.group
             for x in range(plan.nx):
@@ -252,14 +257,15 @@
     outs = pl.pallas_call(
         functools.partial(place_kernel, plan),
         out_shape=[jax.ShapeDtypeStruct(s, jnp.float32) for s in shapes]
-        + [jax.ShapeDtypeStruct((plan.lists, LANE), jnp.int32)],
+        + [jax.ShapeDtypeStruct((plan.lists, LANE), jnp.int32), jax.ShapeDtypeStruct((1,), jnp.int32)],
         in_specs=[
             pl.BlockSpec(memory_space=pltpu.SMEM),
             pl.BlockSpec(memory_space=pltpu.VMEM),
             pl.BlockSpec(memory_space=pltpu.VMEM),
             pl.BlockSpec(memory_space=pl.ANY),
         ],
-        out_specs=[pl.BlockSpec(memory_space=pl.ANY)] * len(shapes) + [pl.BlockSpec(memory_space=pltpu.VMEM)],
+        out_specs=[pl.BlockSpec(memory_space=pl.ANY)] * len(shapes)
+        + [pl.BlockSpec(memory_space=pltpu.VMEM), pl.BlockSpec(memory_space=pltpu.SMEM)],
         scratch_shapes=[
             pltpu.VMEM((plan.blocks, LANE), jnp.bfloat16),
             pltpu.VMEM((2 * plan.half, LANE), jnp.float32),
@@ -271,7 +277,7 @@
         compiler_params=pltpu.CompilerParams(vmem_limit_bytes=58 * MIB),
         name="place_gradients",
     )(my_place, owners, norm_grads, grads)
-    return list(outs[: plan.nz][::-1]), outs[plan.nz : 2 * plan.nz][::-1], outs[-1]
+    return list(outs[: plan.nz][::-1]), outs[plan.nz : 2 * plan.nz][::-1], outs[-2], outs[-1]
 
 
 def owned_kernel(plan, place_ref, owner_ref, weights_ref, owned_ref, natural_ref, held, listed, order, sem_in, sem_order):
@@ -355,14 +361,14 @@
     gradient = parts[0][: plan.block, :]
     for part in parts[1:]:
         gradient = gradient + part[: plan.block, :]
-    block_ref[plan.own :, :] = gradient[plan.own :, :]
-    gradient = gradient[: plan.own, :]
+    block_ref[: plan.tail, :] = gradient[: plan.tail, :]
+    gradient = gradient[plan.tail :, :]
     moment_one = beta_one * first_ref[...] + (1.0 - beta_one) * gradient
     moment_two = beta_two * second_ref[...] + (1.0 - beta_two) * gradient * gradient
     new_first_ref[...] = moment_one
     new_second_ref[...] = moment_two
     step = moment_one / bias_one / (jnp.sqrt(moment_two / bias_two) + epsilon)
-    block_ref[: plan.own, :] = step
+    block_ref[plan.tail :, :] = step
     weight = weight_ref[...]
     direction = step + decay_rate * weight
     natural = natural_ref[: plan.own, :]
@@ -399,26 +405,55 @@
     return (moment_one, moment_two, step)
 
 
-def finish_kernel(plan, tile, slots, place_ref, position_ref, norm_ref, weights_ref, *refs):
-    pieces, refs = refs[: len(slots)], refs[len(slots) :]
-    out_ref, new_norm_ref, trust_ref, held, norms, rates = refs
+def lay(plan, pieces, parts, held):
+    for piece, own_parts in zip(pieces, parts):
+        first = 0
+        for slot, low, rows in own_parts:
+            held[pl.ds(plan.start(*slot) + low, rows), :] = piece[first : first + rows, :]
+            first += rows
+
+
+def tile_of(plan):
+    assert all(bound % LANE == 0 for bound in plan.bounds + (plan.blocks,))
+    return next(n * LANE for n in (8, 4, 2, 1) if plan.blocks // LANE % n == 0)
+
+
+def new_tile(plan, now, position_ref, rates, weights_ref, held, out_ref):
+    lines = tile_of(plan) // LANE
+
+    @pl.loop(0, lines)
+    def _(line):
+        matrix = jnp.int32(0)
+        for bound in plan.bounds:
+            matrix = matrix + (now * lines + line >= bound // LANE).astype(jnp.int32)
+        rate = jnp.broadcast_to(rates[pl.ds(matrix, 1), :], (8, LANE))
+        for group in range(0, LANE, 8):
+            rows = [held[pl.ds(position_ref[now * lines + line, group + u], 1), :] for u in range(8)]
+            here = pl.ds(pl.multiple_of(line * LANE + group, 8), 8)
+            weight = weights_ref[here, :]
+            direction = jnp.concatenate(rows, 0) + decay_rate * weight
+            out_ref[here, :] = weight - rate * direction
+
+
+def early_kernel(plan, parts, limit_ref, place_ref, position_ref, norm_ref, weights_ref, *refs):
+    pieces, refs = refs[: len(parts)], refs[len(parts) :]
+    out_ref, rates, new_norm_ref, trust_ref, held, norms = refs
     now = pl.program_id(0)
 
     @pl.when(now == 0)
     def _():
-        for piece, parts in zip(pieces, slots):
-            for i, slot in enumerate(parts):
-                held[pl.ds(plan.start(*slot), plan.block), :] = piece[i * plan.block : (i + 1) * plan.block, :]
+        lay(plan, pieces, parts, held)
         total = jnp.zeros((plan.tail, LANE), jnp.float32)
         for z in range(plan.nz):
             for x in range(plan.nx):
                 for c in range(2):
-                    start = plan.start(place_ref[0] ^ z, place_ref[1] ^ x, place_ref[2] ^ c) + plan.own
+                    start = plan.start(place_ref[0] ^ z, place_ref[1] ^ x, place_ref[2] ^ c)
                     tail = held[pl.ds(pl.multiple_of(start, 8), plan.tail), :]
                     total = total + tail
                     first = plan.index(z, x, c) * plan.norm_each
                     for row in range(first, min(first + plan.norm_each, plan.norm_rows)):
                         norms[row : row + 1, :] = tail[row - first : row - first + 1, :]
+        rates[...] = jnp.zeros_like(rates)
         for k in range(matrices):
             row = plan.norm_each + k
             weight_square, direction_square = total[row : row + 1, 0:1], total[row : row + 1, 1:2]
@@ -440,46 +475,81 @@
                 for row in range(each):
                     new_norm_ref[j, i : i + 1, row * LANE : (row + 1) * LANE] = value[row : row + 1, :]
 
-    lines = tile // LANE
-
-    @pl.loop(0, lines)
-    def _(line):
-        matrix = jnp.int32(0)
-        for bound in plan.bounds:
-            matrix = matrix + (now * lines + line >= bound // LANE).astype(jnp.int32)
-        rate = jnp.broadcast_to(rates[pl.ds(matrix, 1), :], (8, LANE))
-        for group in range(0, LANE, 8):
-            rows = [held[pl.ds(position_ref[now * lines + line, group + u], 1), :] for u in range(8)]
-            here = pl.ds(pl.multiple_of(line * LANE + group, 8), 8)
-            weight = weights_ref[here, :]
-            direction = jnp.concatenate(rows, 0) + decay_rate * weight
-            out_ref[here, :] = weight - rate * direction
-
-
-def finish(plan, my_place, position, norm_state, weights, pieces, slots):
-    assert all(bound % LANE == 0 for bound in plan.bounds + (plan.blocks,))
-    tile = plan.blocks // next(n for n in (TILES, 4, 2, 1) if plan.blocks // LANE % n == 0)
+    @pl.when((now + 1) * tile_of(plan) <= limit_ref[0])
+    def _():
+        new_tile(plan, now, position_ref, rates, weights_ref, held, out_ref)
+
+
+def late_kernel(plan, parts, limit_ref, position_ref, rates_ref, weights_ref, early_ref, *refs):
+    pieces, (out_ref, held) = refs[: len(parts)], refs[len(parts) :]
+    now = pl.program_id(0)
+
+    @pl.when(now == 0)
+    def _():
+        lay(plan, pieces, parts, held)
+
+    @pl.when((now + 1) * tile_of(plan) > limit_ref[0])
+    def _():
+        new_tile(plan, now, position_ref, rates_ref, weights_ref, held, out_ref)
+
+
+def finish(plan, my_place, limit, position, norm_state, weights, early, late):
+    tile = tile_of(plan)
+    count = plan.blocks // tile
     smem = pl.BlockSpec(memory_space=pltpu.SMEM)
     vmem = pl.BlockSpec(memory_space=pltpu.VMEM)
-    return pl.pallas_call(
-        functools.partial(finish_kernel, plan, tile, slots),
-        grid=(plan.blocks // tile,),
+    params = pltpu.CompilerParams(vmem_limit_bytes=16 * MIB)
+
+    def early_tile(i, limit_ref):
+        return (jnp.maximum(jnp.minimum(i, limit_ref[0] // tile - 1), 0), 0)
+
+    def late_tile(i, limit_ref):
+        return (jnp.minimum(jnp.maximum(i, limit_ref[0] // tile), count - 1), 0)
+
+    early = both_cores(plan, early)
+    shape = jax.ShapeDtypeStruct((plan.blocks, LANE), jnp.float32)
+    new_weights, rates, new_norm, trust = pl.pallas_call(
+        functools.partial(early_kernel, plan, [parts for _, parts in early]),
+        grid_spec=pltpu.PrefetchScalarGridSpec(
+            num_scalar_prefetch=1,
+            grid=(count,),
+            in_specs=[smem, smem, vmem, pl.BlockSpec((tile, LANE), early_tile)] + [vmem] * len(early),
+            out_specs=[pl.BlockSpec((tile, LANE), early_tile), vmem, vmem, smem],
+            scratch_shapes=[
+                pltpu.VMEM((2 * plan.half, LANE), jnp.float32),
+                pltpu.VMEM((plan.norm_rows, LANE), jnp.float32),
+            ],
+        ),
         out_shape=[
-            jax.ShapeDtypeStruct((plan.blocks, LANE), jnp.float32),
+            shape,
+            jax.ShapeDtypeStruct((8, LANE), jnp.float32),
             jax.ShapeDtypeStruct(norm_state.shape, jnp.float32),
             jax.ShapeDtypeStruct((matrices + 2,), jnp.float32),
         ],
-        in_specs=[smem, smem, vmem, pl.BlockSpec((tile, LANE), lambda i: (i, 0))]
-        + [vmem] * len(pieces),
-        out_specs=[pl.BlockSpec((tile, LANE), lambda i: (i, 0)), vmem, smem],
-        scratch_shapes=[
-            pltpu.VMEM((2 * plan.half, LANE), jnp.float32),
-            pltpu.VMEM((plan.norm_rows, LANE), jnp.float32),
-            pltpu.VMEM((8, LANE), jnp.float32),
-        ],
-        compiler_params=pltpu.CompilerParams(vmem_limit_bytes=20 * MIB),
-        name="new_weights",
-    )(my_place, position, norm_state, weights, *pieces)
+        compiler_params=params,
+        cost_estimate=pl.CostEstimate(flops=0, bytes_accessed=36 * MIB, transcendentals=0),
+        name="new_weights_early",
+    )(limit, my_place, position, norm_state, weights, *(value for value, _ in early))
+    if late:
+        rates, *values = together(rates, *(value for value, _ in late))
+        late = [(value, parts) for value, (_, parts) in zip(values, late)]
+    pieces = early + both_cores(plan, late)
+    new_weights = pl.pallas_call(
+        functools.partial(late_kernel, plan, [parts for _, parts in pieces]),
+        grid_spec=pltpu.PrefetchScalarGridSpec(
+            num_scalar_prefetch=1,
+            grid=(count,),
+            in_specs=[smem, vmem, pl.BlockSpec((tile, LANE), late_tile), pl.BlockSpec(memory_space=pl.ANY)]
+            + [vmem] * len(pieces),
+            out_specs=pl.BlockSpec((tile, LANE), late_tile),
+            scratch_shapes=[pltpu.VMEM((2 * plan.half, LANE), jnp.float32)],
+        ),
+        out_shape=shape,
+        input_output_aliases={4: 0},
+        compiler_params=params,
+        name="new_weights_late",
+    )(limit, position, rates, weights, new_weights, *(value for value, _ in pieces))
+    return new_weights, new_norm, trust
 
 
 def local(gradients, weights, first_moment, second_moment, owner_list, norm_grads, norm_state):
@@ -488,7 +558,7 @@
     my_place = jnp.stack([me // (2 * plan.nx), (me // 2) % plan.nx, me % 2]).astype(jnp.int32)
     owners = jnp.pad(owner_list[0], (0, plan.lists * LANE - plan.blocks), constant_values=-1)
     owners = owners.reshape(plan.lists, LANE)
-    siblings, blocks, position = place(plan, my_place, owners, norm_grads[0], gradients[0])
+    siblings, blocks, position, limit = place(plan, my_place, owners, norm_grads[0], gradients[0])
     weight_own, natural = owned(plan, my_place, owners, weights)
 
     mine, theirs = [None] * plan.nz, [None] * plan.nz
@@ -518,10 +588,11 @@
     while hop < plan.narrow:
         stats = stats + lax.ppermute(stats, "mp", [(i, i ^ hop) for i in range(plan.narrow)])
         hop *= 2
-    block = lax.dynamic_update_slice(block, block[plan.own :] + stats, (plan.own, 0))
-    found = gather(plan, block)
-    pieces, slots = [piece for piece, _ in found], [parts for _, parts in found]
-    new_weights, new_state, trust_ratios = finish(plan, my_place, position, norm_state, weights, pieces, slots)
+    block = lax.dynamic_update_slice(block, block[: plan.tail] + stats, (0, 0))
+    early, late = gather(plan, block)
+    new_weights, new_state, trust_ratios = finish(
+        plan, my_place, limit, position, norm_state, weights, early, late
+    )
     return (new_weights, new_first[None], new_second[None], new_state, trust_ratios)
 
 

time: 175 us -> 181 us (1.034)
  Pallas kernels: 50.9 us -> 56.8 us
  waiting for transfers between devices: 78.8 us -> 82.8 us
  starting transfers between devices: 40.8 us -> 37.2 us
    pallas_call x1 -> x2, Pallas kernels: 19.6 us -> 25.7 us  [the longest x1 14.1 us: finish(): pl.pallas_call(functools.partial(late_kernel, plan, [parts for _, parts i...]
    ppermute x29 -> x31, waiting for transfers between devices: 76.7 us -> 80.8 us  [send(): return lax.ppermute(value, 'dp', every)]
    ppermute x29 -> x31, starting transfers between devices: 39.2 us -> 35.7 us  [send(): return lax.ppermute(value, 'dp', every)]
  transfers between devices with their start and end apart: 30 -> 32, of which waited for: 17 -> 20; matrix products, arithmetic and copies ran while one was open for 1% -> 1% of each run, Pallas kernels for 4% -> 10%
where the time goes in v13:
time: 181 us
  waiting for transfers between devices  82.8 us (46%)
  Pallas kernels  56.8 us (31%)
  starting transfers between devices  37.2 us (21%)
  other arithmetic  2.86 us (2%)
    ppermute x31, waiting for transfers between devices, send(): return lax.ppermute(value, 'dp', every)  80.8 us
    ppermute x31, starting transfers between devices, send(): return lax.ppermute(value, 'dp', every)  35.7 us
    pallas_call x1, Pallas kernels, place(): pl.pallas_call(functools.partial(place_kernel, plan), out_shape=[jax.Shap...  22.1 us
    pallas_call x1, Pallas kernels, finish(): pl.pallas_call(functools.partial(late_kernel, plan, [parts for _, parts i...  14.1 us
    pallas_call x1, Pallas kernels, finish(): pl.pallas_call(functools.partial(early_kernel, plan, [parts for _, parts...  11.6 us
    pallas_call x1, Pallas kernels, owned(): pl.pallas_call(functools.partial(owned_kernel, plan), out_shape=[jax.Shap...  6.31 us
  transfers between devices with their start and end apart: 32, of which 20 were waited for; matrix products, arithmetic and copies ran while one was open for 1% of the time, Pallas kernels for 10%

profile of v13, /device:TPU:0, one launch (start us, length us, event | category | flops | bytes accessed | tf_op | source)
XLA Modules:
  0.0 180.8 jit_solution(12899646436035005384)
XLA Ops:
  0.7 0.7 pad_add_fusion.place_ref
  1.3 22.1 %place_gradients.1 = (f32[2192,128]{1,0:T(8,128)}, f32[2192,128]{1,0:T(8,128)}, f32[2192,128]{1,0:T(8,128)}, f32[2192,128]{1,0:T(8,128)}, f32[2192,128]{1,0:T(8,...) custom-call(s32[3]{0:T(128)} %pad_add_fusion.place_ref, ...), custom_call_target="tpu_custom_call" | custom-call | tf_op jit(solution)/shard_map/place_gradients/pallas_call | solution.py:257
  23.4 0.5 collective-permute-start
  24.0 2.6 %collective-permute-done = f32[2192,128]{1,0:T(8,128)S(1)} collective-permute-done((f32[2192,128]{1,0:T(8,128)}, f32[2192,128]{1,0:T(8,128)S(1)}, u32[]{:S(2)}, u32[]{:S(2)}) %collective-permute-start) | collective-permute-done | bytes 1122336 | tf_op jit(solution)/shard_map/ppermute | solution.py:76
  26.6 1.1 slice_add_fusion.7
  27.7 0.4 collective-permute-start.5
  28.1 0.1 collective-permute-start.9
  28.3 2.9 %collective-permute-start.3 = (f32[1096,128]{1,0:T(8,128)S(1)}, f32[1096,128]{1,0:T(8,128)S(1)}, u32[]{:S(2)}, u32[]{:S(2)}) collective-permute-start(f32[1096,128]{1,0:T(8,128)S(1)} %slice_add_fusion.7), channel_id=1, source_target_pairs={{0,4},{2,6},{4,0},{6,2},{8,12},{10,14},{12,8},{14,10},{16,20},{18,... | collective-permute-start | bytes 1683464 | tf_op jit(solution)/shard_map/ppermute | solution.py:76
  31.1 6.3 %owned_weights.1 = (f32[1088,128]{1,0:T(8,128)}, s32[1152,128]{1,0:T(8,128)}) custom-call(s32[3]{0:T(128)} %pad_add_fusion.place_ref, s32[136,128]{1,0:T(8,128)} %bitcast.16, f32[17408,128]{1,0:T(8,128)} %weights_ref.5), custom_call_target="tpu_custom_call" | custom-call | bytes 20971520 | tf_op jit(solution)/shard_map/owned_weights/pallas_call | solution.py:336
  37.6 0.1 slice_add_fusion.2
  37.7 0.2 collective-permute-start.6
  37.9 6.8 %collective-permute-done.3 = f32[1096,128]{1,0:T(8,128)S(1)} collective-permute-done((f32[1096,128]{1,0:T(8,128)S(1)}, f32[1096,128]{1,0:T(8,128)S(1)}, u32[]{:S(2)}, u32[]{:S(2)}) %collective-permute-start.3) | collective-permute-done | bytes 561184 | tf_op jit(solution)/shard_map/ppermute | solution.py:76
  44.6 0.1 fusion.2
  44.7 4.1 %collective-permute-start.4 = (f32[1096,128]{1,0:T(8,128)S(1)}, f32[1096,128]{1,0:T(8,128)S(1)}, u32[]{:S(2)}, u32[]{:S(2)}) collective-permute-start(f32[1096,128]{1,0:T(8,128)S(1)} %fusion.2), channel_id=1, source_target_pairs={{0,8},{2,10},{4,12},{6,14},{24,16},{26,18},{28,20},{30,22},{1,9},{... | collective-permute-start | bytes 1683464 | tf_op jit(solution)/shard_map/ppermute | solution.py:76
  48.9 1.6 collective-permute-start.10
  50.5 6.2 %collective-permute-done.6 = f32[1096,128]{1,0:T(8,128)S(1)} collective-permute-done((f32[1096,128]{1,0:T(8,128)S(1)}, f32[1096,128]{1,0:T(8,128)S(1)}, u32[]{:S(2)}, u32[]{:S(2)}) %collective-permute-start.6) | collective-permute-done | bytes 561184 | tf_op jit(solution)/shard_map/ppermute | solution.py:76
  56.7 0.1 fusion.1
  56.8 2.6 %collective-permute-done.4 = f32[1096,128]{1,0:T(8,128)S(1)} collective-permute-done((f32[1096,128]{1,0:T(8,128)S(1)}, f32[1096,128]{1,0:T(8,128)S(1)}, u32[]{:S(2)}, u32[]{:S(2)}) %collective-permute-start.4) | collective-permute-done | bytes 561184 | tf_op jit(solution)/shard_map/ppermute | solution.py:76
  59.4 4.4 %collective-permute-start.8 = (f32[1096,128]{1,0:T(8,128)S(1)}, f32[1096,128]{1,0:T(8,128)S(1)}, u32[]{:S(2)}, u32[]{:S(2)}) collective-permute-start(f32[1096,128]{1,0:T(8,128)S(1)} %fusion.1), channel_id=1, source_target_pairs={{0,8},{2,10},{4,12},{6,14},{24,16},{26,18},{28,20},{30,22},{1,9},{... | collective-permute-start | bytes 1683464 | tf_op jit(solution)/shard_map/ppermute | solution.py:76
  63.9 0.7 collective-permute-start.7
  64.6 0.1 slice_add_fusion.5
  64.8 1.6 collective-permute-start.2
  66.3 2.3 %collective-permute-done.10 = f32[1096,128]{1,0:T(8,128)S(1)} collective-permute-done((f32[1096,128]{1,0:T(8,128)S(1)}, f32[1096,128]{1,0:T(8,128)S(1)}, u32[]{:S(2)}, u32[]{:S(2)}) %collective-permute-start.10) | collective-permute-done | bytes 561184 | tf_op jit(solution)/shard_map/ppermute | solution.py:76
  68.7 0.1 fusion
  68.8 4.7 %collective-permute-done.8 = f32[1096,128]{1,0:T(8,128)S(1)} collective-permute-done((f32[1096,128]{1,0:T(8,128)S(1)}, f32[1096,128]{1,0:T(8,128)S(1)}, u32[]{:S(2)}, u32[]{:S(2)}) %collective-permute-start.8) | collective-permute-done | bytes 561184 | tf_op jit(solution)/shard_map/ppermute | solution.py:76
  73.6 0.1 add.80
  73.6 3.9 %collective-permute-start.11 = (f32[1096,128]{1,0:T(8,128)S(1)}, f32[1096,128]{1,0:T(8,128)S(1)}, u32[]{:S(2)}, u32[]{:S(2)}) collective-permute-start(f32[1096,128]{1,0:T(8,128)S(1)} %add.80), channel_id=1, source_target_pairs={{0,8},{2,10},{4,12},{6,14},{8,0},{10,2},{12,4},{14,6},{16,24},{18,... | collective-permute-start | bytes 1683464 | tf_op jit(solution)/shard_map/ppermute | solution.py:76
  77.6 0.7 collective-permute-start.12
  78.3 2.0 %collective-permute-done.2.refs_1_ = f32[1096,128]{1,0:T(8,128)S(1)} collective-permute-done((f32[1096,128]{1,0:T(8,128)S(1)}, f32[1096,128]{1,0:T(8,128)S(1)}, u32[]{:S(2)}, u32[]{:S(2)}) %collective-permute-start.2) | collective-permute-done | bytes 561184 | tf_op jit(solution)/shard_map/ppermute | solution.py:76
  80.2 6.9 %collective-permute-done.11.refs_2_ = f32[1096,128]{1,0:T(8,128)S(1)} collective-permute-done((f32[1096,128]{1,0:T(8,128)S(1)}, f32[1096,128]{1,0:T(8,128)S(1)}, u32[]{:S(2)}, u32[]{:S(2)}) %collective-permute-start.11) | collective-permute-done | bytes 561184 | tf_op jit(solution)/shard_map/ppermute | solution.py:76
  87.1 2.7 %moments.1 = (f32[1088,128]{1,0:T(8,128)}, f32[1088,128]{1,0:T(8,128)}, f32[1096,128]{1,0:T(8,128)S(1)}, f32[8,128]{1,0:T(8,128)S(1)}) custom-call(f32[1096,128]{1,0:T(8,128)S(1)} %get-tuple-element.90.refs_0_, f32[1096,128]{1,0:T(8,128)S(1)} %collective-permute-done.2.refs_1_, f32[1096,128]{1,0:T(8,128)S(1)} %collective-permute-done.11.refs_2_, ...), custom_call_target="tpu_custom_call" | custom-call | tf_op jit(solution)/shard_map/moments/pallas_call | solution.py:391
  89.8 1.5 collective-permute-start.13
  91.3 2.1 %collective-permute-done.13 = f32[8,128]{1,0:T(8,128)S(1)} collective-permute-done((f32[8,128]{1,0:T(8,128)S(1)}, f32[8,128]{1,0:T(8,128)S(1)}, u32[]{:S(2)}, u32[]{:S(2)}) %collective-permute-start.13) | collective-permute-done | bytes 4128 | tf_op jit(solution)/shard_map/ppermute | solution.py:589
  93.4 3.6 %collective-permute-start.15 = (f32[1096,128]{1,0:T(8,128)S(1)}, f32[1096,128]{1,0:T(8,128)S(1)}, u32[]{:S(2)}, u32[]{:S(2)}) collective-permute-start(f32[1096,128]{1,0:T(8,128)S(1)} %add_dynamic-update-slice_fusion), channel_id=1, source_target_pairs={{0,8},{2,10},{4,12},{6,14},{8,0},{10,2},{12,4},{14,6},{16,24},{18,... | collective-permute-start | bytes 1683464 | tf_op jit(solution)/shard_map/ppermute | solution.py:76
  97.1 1.5 collective-permute-start.16
  98.6 0.7 collective-permute-start.14
  99.2 5.4 %collective-permute-done.15 = f32[1096,128]{1,0:T(8,128)S(1)} collective-permute-done((f32[1096,128]{1,0:T(8,128)S(1)}, f32[1096,128]{1,0:T(8,128)S(1)}, u32[]{:S(2)}, u32[]{:S(2)}) %collective-permute-start.15) | collective-permute-done | bytes 561184 | tf_op jit(solution)/shard_map/ppermute | solution.py:76
  104.6 1.5 collective-permute-start.19
  106.1 0.1 pad_maximum_fusion.refs_0_
  106.2 6.2 %collective-permute-done.16 = f32[1096,128]{1,0:T(8,128)S(1)} collective-permute-done((f32[1096,128]{1,0:T(8,128)S(1)}, f32[1096,128]{1,0:T(8,128)S(1)}, u32[]{:S(2)}, u32[]{:S(2)}) %collective-permute-start.16) | collective-permute-done | bytes 561184 | tf_op jit(solution)/shard_map/ppermute | solution.py:76
  112.3 0.7 collective-permute-start.17
  113.0 1.3 collective-permute-start.18
  114.3 5.2 %collective-permute-done.19 = f32[1096,128]{1,0:T(8,128)S(1)} collective-permute-done((f32[1096,128]{1,0:T(8,128)S(1)}, f32[1096,128]{1,0:T(8,128)S(1)}, u32[]{:S(2)}, u32[]{:S(2)}) %collective-permute-start.19) | collective-permute-done | bytes 561184 | tf_op jit(solution)/shard_map/ppermute | solution.py:76
  119.5 0.1 pad_maximum_fusion.1.refs_1_
  119.6 9.5 %collective-permute-done.18 = f32[1096,128]{1,0:T(8,128)S(1)} collective-permute-done((f32[1096,128]{1,0:T(8,128)S(1)}, f32[1096,128]{1,0:T(8,128)S(1)}, u32[]{:S(2)}, u32[]{:S(2)}) %collective-permute-start.18) | collective-permute-done | bytes 561184 | tf_op jit(solution)/shard_map/ppermute | solution.py:76
  129.0 0.1 add.84.refs_2_
  129.2 1.6 collective-permute-start.20
  130.7 1.3 collective-permute-start.21
  132.0 0.1 collective-permute-start.24
  132.1 6.7 %collective-permute-done.20.refs_3_ = f32[1096,128]{1,0:T(8,128)S(1)} collective-permute-done((f32[1096,128]{1,0:T(8,128)S(1)}, f32[1096,128]{1,0:T(8,128)S(1)}, u32[]{:S(2)}, u32[]{:S(2)}) %collective-permute-start.20) | collective-permute-done | bytes 561184 | tf_op jit(solution)/shard_map/ppermute | solution.py:76
  138.8 3.4 %collective-permute-done.21 = f32[1096,128]{1,0:T(8,128)S(1)} collective-permute-done((f32[1096,128]{1,0:T(8,128)S(1)}, f32[1096,128]{1,0:T(8,128)S(1)}, u32[]{:S(2)}, u32[]{:S(2)}) %collective-permute-start.21) | collective-permute-done | bytes 561184 | tf_op jit(solution)/shard_map/ppermute | solution.py:76
  142.3 0.5 collective-permute-start.25
  142.8 0.5 collective-permute-start.22
  143.3 0.5 collective-permute-done.27.refs_10_
  143.8 0.1 collective-permute-start.26
  144.0 7.5 %collective-permute-done.22.refs_5_ = f32[552,128]{1,0:T(8,128)S(1)} collective-permute-done((f32[552,128]{1,0:T(8,128)S(1)}, f32[552,128]{1,0:T(8,128)S(1)}, u32[]{:S(2)}, u32[]{:S(2)}) %collective-permute-start.22) | collective-permute-done | bytes 282656 | tf_op jit(solution)/shard_map/ppermute | solution.py:76
  151.6 0.6 collective-permute-start.29
  152.2 0.9 collective-permute-done.28.refs_11_
  153.1 11.6 %new_weights_early.1 = (f32[17408,128]{1,0:T(8,128)}, f32[8,128]{1,0:T(8,128)S(1)}, f32[3,2,1024]{2,1,0:T(2,128)}, f32[7]{0:T(128)}) custom-call(s32[1]{0:T(128)} %get-tuple-element.47.limit_ref, s32[3]{0:T(128)S(1)} %copy-done.6, s32[136,128]{1,0:T(8,128)S(1)} %copy-done.4, f32[3,2,1024]{2,1,0:T(2,128)S(1)} %copy-done.5, f32[17408,128]{1,0:T(8,128)S(1)} %bitcast.11, ...), custom_call_target="tpu_custom_call" | custom-call | bytes 37748736 | tf_op jit(solution)/shard_map/new_weights_early/pallas_call | solution.py:511
  164.7 0.1 collective-permute-start.30
  164.9 0.4 collective-permute-start.31
  165.3 1.0 collective-permute-done.30.refs_14_
  166.3 0.4 collective-permute-done.31.refs_15_
  166.7 14.1 %new_weights_late.1 = f32[17408,128]{1,0:T(8,128)} custom-call(s32[1]{0:T(128)} %get-tuple-element.47.limit_ref, s32[136,128]{1,0:T(8,128)S(1)} %copy-done.4, f32[8,128]{1,0:T(8,128)S(1)} %get-tuple-element.81.rates_ref, f32[17408,128]{1,0:T(8,128)S(1)} %bitcast.11, f32[17408,128]{1,0:T(8,128)} %get-tuple-element.82.early_ref, ...), custom_call_target="tpu_custom_call", output_to_operand_aliasing={{}: (4, {})} | custom-call | tf_op jit(solution)/shard_map/new_weights_late/pallas_call | solution.py:537
  (51 shorter events, 0.5 us)
Async XLA Ops:
  23.4 3.1 %collective-permute-start = (f32[2192,128]{1,0:T(8,128)}, f32[2192,128]{1,0:T(8,128)S(1)}, u32[]{:S(2)}, u32[]{:S(2)}) collective-permute-start(f32[2192,128]{1,0:T(8,128)} %get-tuple-element.51), channel_id=1, source_target_pairs={{0,2},{2,0},{4,6},{6,4},{8,10},{10,8},{12,14},{14,12},{16,18},{18,... | collective-permute-start | bytes 3366920 | tf_op jit(solution)/shard_map/ppermute | solution.py:76
  27.7 9.9 %copy-start.9 = (f32[2192,128]{1,0:T(8,128)S(1)}, f32[2192,128]{1,0:T(8,128)}, u32[]{:S(2)}) copy-start(f32[2192,128]{1,0:T(8,128)} %get-tuple-element.57) | copy-start | bytes 3366916
  27.7 9.8 %collective-permute-start.5 = (f32[2192,128]{1,0:T(8,128)}, f32[2192,128]{1,0:T(8,128)S(1)}, u32[]{:S(2)}, u32[]{:S(2)}) collective-permute-start(f32[2192,128]{1,0:T(8,128)} %get-tuple-element.58), channel_id=1, source_target_pairs={{0,2},{2,0},{4,6},{6,4},{8,10},{10,8},{12,14},{14,12},{16,18},{18,... | collective-permute-start | bytes 3366920 | tf_op jit(solution)/shard_map/ppermute | solution.py:76
  28.1 20.7 %collective-permute-start.9 = (f32[2192,128]{1,0:T(8,128)}, f32[2192,128]{1,0:T(8,128)S(1)}, u32[]{:S(2)}, u32[]{:S(2)}) collective-permute-start(f32[2192,128]{1,0:T(8,128)} %get-tuple-element.64), channel_id=1, source_target_pairs={{0,2},{2,0},{4,6},{6,4},{8,10},{10,8},{12,14},{14,12},{16,18},{18,... | collective-permute-start | bytes 3366920 | tf_op jit(solution)/shard_map/ppermute | solution.py:76
  28.3 16.4 %collective-permute-start.3 = (f32[1096,128]{1,0:T(8,128)S(1)}, f32[1096,128]{1,0:T(8,128)S(1)}, u32[]{:S(2)}, u32[]{:S(2)}) collective-permute-start(f32[1096,128]{1,0:T(8,128)S(1)} %slice_add_fusion.7), channel_id=1, source_target_pairs={{0,4},{2,6},{4,0},{6,2},{8,12},{10,14},{12,8},{14,10},{16,20},{18,... | collective-permute-start | bytes 1683464 | tf_op jit(solution)/shard_map/ppermute | solution.py:76
  37.5 7.2 %copy-start.10 = (f32[2192,128]{1,0:T(8,128)S(1)}, f32[2192,128]{1,0:T(8,128)}, u32[]{:S(2)}) copy-start(f32[2192,128]{1,0:T(8,128)} %get-tuple-element.50) | copy-start | bytes 3366916
  37.5 27.1 %collective-permute-start.1 = (f32[2192,128]{1,0:T(8,128)}, f32[2192,128]{1,0:T(8,128)S(1)}, u32[]{:S(2)}, u32[]{:S(2)}) collective-permute-start(f32[2192,128]{1,0:T(8,128)} %get-tuple-element.55), channel_id=1, source_target_pairs={{0,2},{2,0},{4,6},{6,4},{8,10},{10,8},{12,14},{14,12},{16,18},{18,... | collective-permute-start | bytes 3366920 | tf_op jit(solution)/shard_map/ppermute | solution.py:76
  37.6 11.2 %copy-start.7 = (f32[2192,128]{1,0:T(8,128)S(1)}, f32[2192,128]{1,0:T(8,128)}, u32[]{:S(2)}) copy-start(f32[2192,128]{1,0:T(8,128)} %get-tuple-element.63) | copy-start | bytes 3366916
  37.7 19.0 %collective-permute-start.6 = (f32[1096,128]{1,0:T(8,128)S(1)}, f32[1096,128]{1,0:T(8,128)S(1)}, u32[]{:S(2)}, u32[]{:S(2)}) collective-permute-start(f32[1096,128]{1,0:T(8,128)S(1)} %slice_add_fusion.2), channel_id=1, source_target_pairs={{0,4},{2,6},{4,0},{6,2},{8,12},{10,14},{12,8},{14,10},{16,20},{18,... | collective-permute-start | bytes 1683464 | tf_op jit(solution)/shard_map/ppermute | solution.py:76
  44.7 14.7 %collective-permute-start.4 = (f32[1096,128]{1,0:T(8,128)S(1)}, f32[1096,128]{1,0:T(8,128)S(1)}, u32[]{:S(2)}, u32[]{:S(2)}) collective-permute-start(f32[1096,128]{1,0:T(8,128)S(1)} %fusion.2), channel_id=1, source_target_pairs={{0,8},{2,10},{4,12},{6,14},{24,16},{26,18},{28,20},{30,22},{1,9},{... | collective-permute-start | bytes 1683464 | tf_op jit(solution)/shard_map/ppermute | solution.py:76
  48.9 19.8 %collective-permute-start.10 = (f32[1096,128]{1,0:T(8,128)S(1)}, f32[1096,128]{1,0:T(8,128)S(1)}, u32[]{:S(2)}, u32[]{:S(2)}) collective-permute-start(f32[1096,128]{1,0:T(8,128)S(1)} %slice_add_fusion), channel_id=1, source_target_pairs={{0,4},{2,6},{4,0},{6,2},{8,12},{10,14},{12,8},{14,10},{16,20},{18,... | collective-permute-start | bytes 1683464 | tf_op jit(solution)/shard_map/ppermute | solution.py:76
  56.8 7.8 %copy-start.8 = (f32[2192,128]{1,0:T(8,128)S(1)}, f32[2192,128]{1,0:T(8,128)}, u32[]{:S(2)}) copy-start(f32[2192,128]{1,0:T(8,128)} %get-tuple-element.49) | copy-start | bytes 3366916
  59.4 14.1 %collective-permute-start.8 = (f32[1096,128]{1,0:T(8,128)S(1)}, f32[1096,128]{1,0:T(8,128)S(1)}, u32[]{:S(2)}, u32[]{:S(2)}) collective-permute-start(f32[1096,128]{1,0:T(8,128)S(1)} %fusion.1), channel_id=1, source_target_pairs={{0,8},{2,10},{4,12},{6,14},{24,16},{26,18},{28,20},{30,22},{1,9},{... | collective-permute-start | bytes 1683464 | tf_op jit(solution)/shard_map/ppermute | solution.py:76
  63.9 4.9 %collective-permute-start.7 = (f32[1096,128]{1,0:T(8,128)S(1)}, f32[1096,128]{1,0:T(8,128)S(1)}, u32[]{:S(2)}, u32[]{:S(2)}) collective-permute-start(f32[1096,128]{1,0:T(8,128)S(1)} %add.76), channel_id=1, source_target_pairs={{8,16},{10,18},{12,20},{14,22},{16,8},{18,10},{20,12},{22,14},{9,1... | collective-permute-start | bytes 1683464 | tf_op jit(solution)/shard_map/ppermute | solution.py:76
  64.6 88.5 %slice-start = ((s8[8912896]{0:T(1024)(128)(4,1)}), s8[4194304]{0:T(1024)(128)(4,1)S(1)}, s32[]{:S(2)}) async-start(s8[8912896]{0:T(1024)(128)(4,1)} %bitcast.10), calls=%async_computation | async-start | bytes 8388608
  64.8 15.4 %collective-permute-start.2 = (f32[1096,128]{1,0:T(8,128)S(1)}, f32[1096,128]{1,0:T(8,128)S(1)}, u32[]{:S(2)}, u32[]{:S(2)}) collective-permute-start(f32[1096,128]{1,0:T(8,128)S(1)} %get-tuple-element.89), channel_id=1, source_target_pairs={{0,4},{2,6},{4,0},{6,2},{8,12},{10,14},{12,8},{14,10},{16,20},{18,... | collective-permute-start | bytes 1683464 | tf_op jit(solution)/shard_map/ppermute | solution.py:76
  68.7 18.4 %copy-start = (s32[1152,128]{1,0:T(8,128)S(1)}, s32[1152,128]{1,0:T(8,128)}, u32[]{:S(2)}) copy-start(s32[1152,128]{1,0:T(8,128)} %get-tuple-element.69.refs_7_) | copy-start | bytes 1769476
  68.7 18.4 %copy-start.1 = (f32[1,1088,128]{2,1,0:T(8,128)S(1)}, f32[1,1088,128]{2,1,0:T(8,128)}, u32[]{:S(2)}) copy-start(f32[1,1088,128]{2,1,0:T(8,128)} %param.9) | copy-start | bytes 1671172
  68.7 18.4 %copy-start.2 = (f32[1,1088,128]{2,1,0:T(8,128)S(1)}, f32[1,1088,128]{2,1,0:T(8,128)}, u32[]{:S(2)}) copy-start(f32[1,1088,128]{2,1,0:T(8,128)} %param.10) | copy-start | bytes 1671172
  68.7 18.4 %copy-start.3 = (f32[1088,128]{1,0:T(8,128)S(1)}, f32[1088,128]{1,0:T(8,128)}, u32[]{:S(2)}) copy-start(f32[1088,128]{1,0:T(8,128)} %get-tuple-element.68.refs_6_) | copy-start | bytes 1671172
  68.8 84.3 %slice-start.1 = ((s8[8912896]{0:T(1024)(128)(4,1)}), s8[4194304]{0:T(1024)(128)(4,1)S(1)}, s32[]{:S(2)}) async-start(s8[8912896]{0:T(1024)(128)(4,1)} %bitcast.10), calls=%async_computation.1 | async-start | bytes 8388608
  73.6 13.5 %collective-permute-start.11 = (f32[1096,128]{1,0:T(8,128)S(1)}, f32[1096,128]{1,0:T(8,128)S(1)}, u32[]{:S(2)}, u32[]{:S(2)}) collective-permute-start(f32[1096,128]{1,0:T(8,128)S(1)} %add.80), channel_id=1, source_target_pairs={{0,8},{2,10},{4,12},{6,14},{8,0},{10,2},{12,4},{14,6},{16,24},{18,... | collective-permute-start | bytes 1683464 | tf_op jit(solution)/shard_map/ppermute | solution.py:76
  77.6 9.5 %collective-permute-start.12 = (f32[1096,128]{1,0:T(8,128)S(1)}, f32[1096,128]{1,0:T(8,128)S(1)}, u32[]{:S(2)}, u32[]{:S(2)}) collective-permute-start(f32[1096,128]{1,0:T(8,128)S(1)} %add.81), channel_id=1, source_target_pairs={{8,16},{10,18},{12,20},{14,22},{16,8},{18,10},{20,12},{22,14},{9,1... | collective-permute-start | bytes 1683464 | tf_op jit(solution)/shard_map/ppermute | solution.py:76
  89.8 3.6 %collective-permute-start.13 = (f32[8,128]{1,0:T(8,128)S(1)}, f32[8,128]{1,0:T(8,128)S(1)}, u32[]{:S(2)}, u32[]{:S(2)}) collective-permute-start(f32[8,128]{1,0:T(8,128)S(1)} %get-tuple-element.71), channel_id=1, source_target_pairs={{0,1},{1,0},{2,3},{3,2},{4,5},{5,4},{6,7},{7,6},{8,9},{9,8},{10,11... | collective-permute-start | bytes 12296 | tf_op jit(solution)/shard_map/ppermute | solution.py:589
  93.4 59.7 %slice-start.2 = ((s8[8912896]{0:T(1024)(128)(4,1)}), s8[524288]{0:T(1024)(128)(4,1)S(1)}, s32[]{:S(2)}) async-start(s8[8912896]{0:T(1024)(128)(4,1)} %bitcast.10), calls=%async_computation.2 | async-start | bytes 1048576
  93.4 11.2 %collective-permute-start.15 = (f32[1096,128]{1,0:T(8,128)S(1)}, f32[1096,128]{1,0:T(8,128)S(1)}, u32[]{:S(2)}, u32[]{:S(2)}) collective-permute-start(f32[1096,128]{1,0:T(8,128)S(1)} %add_dynamic-update-slice_fusion), channel_id=1, source_target_pairs={{0,8},{2,10},{4,12},{6,14},{8,0},{10,2},{12,4},{14,6},{16,24},{18,... | collective-permute-start | bytes 1683464 | tf_op jit(solution)/shard_map/ppermute | solution.py:76
  97.1 15.3 %collective-permute-start.16 = (f32[1096,128]{1,0:T(8,128)S(1)}, f32[1096,128]{1,0:T(8,128)S(1)}, u32[]{:S(2)}, u32[]{:S(2)}) collective-permute-start(f32[1096,128]{1,0:T(8,128)S(1)} %add_dynamic-update-slice_fusion), channel_id=1, source_target_pairs={{0,4},{2,6},{4,0},{6,2},{8,12},{10,14},{12,8},{14,10},{16,20},{18,... | collective-permute-start | bytes 1683464 | tf_op jit(solution)/shard_map/ppermute | solution.py:76
  98.6 13.8 %collective-permute-start.14 = (f32[1096,128]{1,0:T(8,128)S(1)}, f32[1096,128]{1,0:T(8,128)S(1)}, u32[]{:S(2)}, u32[]{:S(2)}) collective-permute-start(f32[1096,128]{1,0:T(8,128)S(1)} %add_dynamic-update-slice_fusion), channel_id=1, source_target_pairs={{8,16},{10,18},{12,20},{14,22},{16,8},{18,10},{20,12},{22,14},{9,1... | collective-permute-start | bytes 1683464 | tf_op jit(solution)/shard_map/ppermute | solution.py:76
  104.6 14.9 %collective-permute-start.19 = (f32[1096,128]{1,0:T(8,128)S(1)}, f32[1096,128]{1,0:T(8,128)S(1)}, u32[]{:S(2)}, u32[]{:S(2)}) collective-permute-start(f32[1096,128]{1,0:T(8,128)S(1)} %collective-permute-done.15), channel_id=1, source_target_pairs={{0,4},{2,6},{4,0},{6,2},{8,12},{10,14},{12,8},{14,10},{16,20},{18,... | collective-permute-start | bytes 1683464 | tf_op jit(solution)/shard_map/ppermute | solution.py:76
  112.3 7.2 %collective-permute-start.17 = (f32[1096,128]{1,0:T(8,128)S(1)}, f32[1096,128]{1,0:T(8,128)S(1)}, u32[]{:S(2)}, u32[]{:S(2)}) collective-permute-start(f32[1096,128]{1,0:T(8,128)S(1)} %collective-permute-done.15), channel_id=1, source_target_pairs={{8,16},{10,18},{12,20},{14,22},{16,8},{18,10},{20,12},{22,14},{9,1... | collective-permute-start | bytes 1683464 | tf_op jit(solution)/shard_map/ppermute | solution.py:76
  113.0 16.0 %collective-permute-start.18 = (f32[1096,128]{1,0:T(8,128)S(1)}, f32[1096,128]{1,0:T(8,128)S(1)}, u32[]{:S(2)}, u32[]{:S(2)}) collective-permute-start(f32[1096,128]{1,0:T(8,128)S(1)} %collective-permute-done.14), channel_id=1, source_target_pairs={{8,0},{10,2},{12,4},{14,6},{16,24},{18,26},{20,28},{22,30},{9,1},{... | collective-permute-start | bytes 1683464 | tf_op jit(solution)/shard_map/ppermute | solution.py:76
  129.1 24.0 %copy-start.4 = (s32[136,128]{1,0:T(8,128)S(1)}, s32[136,128]{1,0:T(8,128)}, u32[]{:S(2)}) copy-start(s32[136,128]{1,0:T(8,128)} %get-tuple-element.48.position_ref) | copy-start | bytes 208900
  129.1 24.0 %copy-start.5 = (f32[3,2,1024]{2,1,0:T(2,128)S(1)}, f32[3,2,1024]{2,1,0:T(2,128)}, u32[]{:S(2)}) copy-start(f32[3,2,1024]{2,1,0:T(2,128)} %norm_ref.1) | copy-start | bytes 73732
  129.1 24.0 %copy-start.6 = (s32[3]{0:T(128)S(1)}, s32[3]{0:T(128)}, u32[]{:S(2)}) copy-start(s32[3]{0:T(128)} %pad_add_fusion.place_ref) | copy-start | bytes 40
  129.2 9.6 %collective-permute-start.20 = (f32[1096,128]{1,0:T(8,128)S(1)}, f32[1096,128]{1,0:T(8,128)S(1)}, u32[]{:S(2)}, u32[]{:S(2)}) collective-permute-start(f32[1096,128]{1,0:T(8,128)S(1)} %add.84.refs_2_), channel_id=1, source_target_pairs={{0,4},{2,6},{4,0},{6,2},{8,12},{10,14},{12,8},{14,10},{16,20},{18,... | collective-permute-start | bytes 1683464 | tf_op jit(solution)/shard_map/ppermute | solution.py:76
  130.7 11.5 %collective-permute-start.21 = (f32[1096,128]{1,0:T(8,128)S(1)}, f32[1096,128]{1,0:T(8,128)S(1)}, u32[]{:S(2)}, u32[]{:S(2)}) collective-permute-start(f32[1096,128]{1,0:T(8,128)S(1)} %collective-permute-done.17), channel_id=1, source_target_pairs={{8,0},{10,2},{12,4},{14,6},{16,24},{18,26},{20,28},{22,30},{9,1},{... | collective-permute-start | bytes 1683464 | tf_op jit(solution)/shard_map/ppermute | solution.py:76
  132.0 20.2 %collective-permute-start.24 = (f32[2192,128]{1,0:T(8,128)S(1)}, f32[2192,128]{1,0:T(8,128)S(1)}, u32[]{:S(2)}, u32[]{:S(2)}) collective-permute-start(f32[2192,128]{1,0:T(8,128)S(1)} %pad_maximum_fusion.1.refs_1_), channel_id=1, source_target_pairs={{0,2},{2,0},{4,6},{6,4},{8,10},{10,8},{12,14},{14,12},{16,18},{18,... | collective-permute-start | bytes 3366920 | tf_op jit(solution)/shard_map/ppermute | solution.py:76
  138.8 14.3 %collective-permute-start.23 = (f32[2192,128]{1,0:T(8,128)S(1)}, f32[2192,128]{1,0:T(8,128)S(1)}, u32[]{:S(2)}, u32[]{:S(2)}) collective-permute-start(f32[2192,128]{1,0:T(8,128)S(1)} %pad_maximum_fusion.refs_0_), channel_id=1, source_target_pairs={{0,2},{2,0},{4,6},{6,4},{8,10},{10,8},{12,14},{14,12},{16,18},{18,... | collective-permute-start | bytes 3366920 | tf_op jit(solution)/shard_map/ppermute | solution.py:76
  142.2 1.6 collective-permute-start.27
  142.3 9.3 %collective-permute-start.25 = (f32[1096,128]{1,0:T(8,128)S(1)}, f32[1096,128]{1,0:T(8,128)S(1)}, u32[]{:S(2)}, u32[]{:S(2)}) collective-permute-start(f32[1096,128]{1,0:T(8,128)S(1)} %add.84.refs_2_), channel_id=1, source_target_pairs={{0,2},{2,0},{4,6},{6,4},{8,10},{10,8},{12,14},{14,12},{16,18},{18,... | collective-permute-start | bytes 1683464 | tf_op jit(solution)/shard_map/ppermute | solution.py:76
  142.8 8.7 %collective-permute-start.22 = (f32[552,128]{1,0:T(8,128)S(1)}, f32[552,128]{1,0:T(8,128)S(1)}, u32[]{:S(2)}, u32[]{:S(2)}) collective-permute-start(f32[552,128]{1,0:T(8,128)S(1)} %slice_add_fusion.8.refs_4_), channel_id=1, source_target_pairs={{0,4},{2,6},{4,0},{6,2},{8,12},{10,14},{12,8},{14,10},{16,20},{18,... | collective-permute-start | bytes 847880 | tf_op jit(solution)/shard_map/ppermute | solution.py:76
  143.8 8.3 %collective-permute-start.26 = (f32[1096,128]{1,0:T(8,128)S(1)}, f32[1096,128]{1,0:T(8,128)S(1)}, u32[]{:S(2)}, u32[]{:S(2)}) collective-permute-start(f32[1096,128]{1,0:T(8,128)S(1)} %collective-permute-done.20.refs_3_), channel_id=1, source_target_pairs={{0,2},{2,0},{4,6},{6,4},{8,10},{10,8},{12,14},{14,12},{16,18},{18,... | collective-permute-start | bytes 1683464 | tf_op jit(solution)/shard_map/ppermute | solution.py:76
  151.5 1.6 collective-permute-start.28
  151.6 13.2 %collective-permute-start.29 = (f32[544,128]{1,0:T(8,128)S(1)}, f32[544,128]{1,0:T(8,128)S(1)}, u32[]{:S(2)}, u32[]{:S(2)}) collective-permute-start(f32[544,128]{1,0:T(8,128)S(1)} %slice_add_fusion.9.refs_12_), channel_id=1, source_target_pairs={{0,4},{2,6},{4,0},{6,2},{8,12},{10,14},{12,8},{14,10},{16,20},{18,... | collective-permute-start | bytes 835592 | tf_op jit(solution)/shard_map/ppermute | solution.py:76
  164.7 1.6 collective-permute-start.30
  164.9 1.8 %collective-permute-start.31 = (f32[544,128]{1,0:T(8,128)S(1)}, f32[544,128]{1,0:T(8,128)S(1)}, u32[]{:S(2)}, u32[]{:S(2)}) collective-permute-start(f32[544,128]{1,0:T(8,128)S(1)} %collective-permute-done.29.refs_13_), channel_id=1, source_target_pairs={{0,2},{2,0},{4,6},{6,4},{8,10},{10,8},{12,14},{14,12},{16,18},{18,... | collective-permute-start | bytes 835592 | tf_op jit(solution)/shard_map/ppermute | solution.py:76

commit v14 on v11

--- a/solution.py
+++ b/solution.py
@@ -121,12 +121,50 @@
     return zero + [pair, across_three] + beside
 
 
-def gather(plan, block):
+def sums_kernel(plan, place_ref, *refs):
+    tails, (out_ref, held) = refs[: plan.nz], refs[plan.nz :]
+    for far_z, tail in enumerate(tails):
+        held[place_ref[0] ^ far_z] = tail[...]
+    total = held[0]
+    for z in range(1, plan.nz):
+        total = total + held[z]
+    out_ref[...] = total
+
+
+def all_sums(plan, my_place, blocks):
+    def tail_of(row):
+        return pl.BlockSpec((plan.tail, LANE), lambda i: ((row + plan.own) // plan.tail, 0))
+
+    specs = [tail_of(row) for _, row in blocks]
+    total = pl.pallas_call(
+        functools.partial(sums_kernel, plan),
+        grid=(1,),
+        out_shape=jax.ShapeDtypeStruct((plan.tail, LANE), jnp.float32),
+        in_specs=[pl.BlockSpec(memory_space=pltpu.SMEM)] + specs,
+        out_specs=pl.BlockSpec(memory_space=pltpu.VMEM),
+        scratch_shapes=[pltpu.VMEM((plan.nz, plan.tail, LANE), jnp.float32)],
+        compiler_params=pltpu.CompilerParams(vmem_limit_bytes=4 * MIB),
+        name="sums",
+    )(my_place, *(value for value, _ in blocks))
+    hop = 1
+    while hop < plan.nx:
+        total = total + plan.send(total, "x", [(i, i ^ hop) for i in range(plan.nx)])
+        hop *= 2
+    total = total + plan.swap(total)
+    hop = 1
+    while hop < plan.narrow:
+        total = total + lax.ppermute(total, "mp", [(i, i ^ hop) for i in range(plan.narrow)])
+        hop *= 2
+    return total
+
+
+def gather(plan, my_place, block):
     def along_x(value):
         return line_gather(plan, "x", plan.nx, value)
 
     if plan.nz != 4:
         lines = [along_x(value) for value in line_gather(plan, "z", plan.nz, block)]
+        total = all_sums(plan, my_place, [(line[0], 0) for line in lines])
         mine = [(value, [(z, x)]) for z, line in enumerate(lines) for x, value in enumerate(line)]
     else:
         line = along_x(block)
@@ -140,14 +178,18 @@
         near_two, *far = together(two + out_two, *far)
         line_two = along_x(near_two)
         out_three = plan.send(two, "z", OUTWARD)
-        line_three = along_x(three + out_three)
+        near_three = three + out_three
+        line_three = along_x(near_three)
+        total = all_sums(plan, my_place, [(own, 0), (own, plan.block), (near_two, 0), (near_three, 0)])
         own, *line_two = together(own, *line_two)
+        total, *line_three = together(total, *line_three)
         mine = [(value, [(0, x), (1, x)]) for x, value in enumerate([own] + far)]
         mine += [(value, [(2, x)]) for x, value in enumerate(line_two)]
         mine += [(value, [(3, x)]) for x, value in enumerate(line_three)]
     swapped = [plan.swap(value) for value, _ in mine]
     found = [(value, [slot + (0,) for slot in slots]) for value, slots in mine]
-    return found + [(value, [slot + (1,) for slot in slots]) for value, (_, slots) in zip(swapped, mine)]
+    found += [(value, [slot + (1,) for slot in slots]) for value, (_, slots) in zip(swapped, mine)]
+    return found, total
 
 
 def line_gather(plan, axis, count, value):
@@ -343,12 +385,11 @@
 def update_kernel(plan, terms, *refs):
     parts, refs = refs[:terms], refs[terms:]
     first_ref, second_ref, weight_ref, natural_ref = refs[:4]
-    new_first_ref, new_second_ref, block_ref, stats_ref = refs[4:]
+    new_first_ref, new_second_ref, block_ref = refs[4:]
     gradient = parts[0][: plan.block, :]
     for part in parts[1:]:
         gradient = gradient + part[: plan.block, :]
-    block_ref[plan.own :, :] = gradient[plan.own :, :]
-    gradient = gradient[: plan.own, :]
+    tail, gradient = gradient[plan.own :, :], gradient[: plan.own, :]
     moment_one = beta_one * first_ref[...] + (1.0 - beta_one) * gradient
     moment_two = beta_two * second_ref[...] + (1.0 - beta_two) * gradient * gradient
     new_first_ref[...] = moment_one
@@ -368,12 +409,12 @@
             kept = jnp.where(inside, squares, 0.0).reshape(plan.own // 8, 8, LANE)
             total = jnp.sum(jnp.sum(kept, axis=0))
             stats = jnp.where((rank == plan.norm_each + k) & (lane == column), total, stats)
-    stats_ref[...] = stats
+    block_ref[plan.own :, :] = tail + stats
 
 
 def update(plan, parts, first, second, weight, natural):
     vmem = pl.BlockSpec(memory_space=pltpu.VMEM)
-    shapes = [(plan.own, LANE), (plan.own, LANE), (plan.block, LANE), (plan.tail, LANE)]
+    shapes = [(plan.own, LANE), (plan.own, LANE), (plan.block, LANE)]
     return pl.pallas_call(
         functools.partial(update_kernel, plan, len(parts)),
         out_shape=[jax.ShapeDtypeStruct(s, jnp.float32) for s in shapes],
@@ -391,7 +432,7 @@
     return (moment_one, moment_two, step)
 
 
-def finish_kernel(plan, tile, slots, place_ref, position_ref, norm_ref, weights_ref, *refs):
+def finish_kernel(plan, tile, slots, place_ref, position_ref, total_ref, norm_ref, weights_ref, *refs):
     pieces, refs = refs[: len(slots)], refs[len(slots) :]
     out_ref, new_norm_ref, trust_ref, held, norms, rates = refs
     now = pl.program_id(0)
@@ -401,13 +442,12 @@
         for piece, parts in zip(pieces, slots):
             for i, slot in enumerate(parts):
                 held[pl.ds(plan.start(*slot), plan.block), :] = piece[i * plan.block : (i + 1) * plan.block, :]
-        total = jnp.zeros((plan.tail, LANE), jnp.float32)
+        total = total_ref[...]
         for z in range(plan.nz):
             for x in range(plan.nx):
                 for c in range(2):
                     start = plan.start(place_ref[0] ^ z, place_ref[1] ^ x, place_ref[2] ^ c) + plan.own
                     tail = held[pl.ds(pl.multiple_of(start, 8), plan.tail), :]
-                    total = total + tail
                     first = plan.index(z, x, c) * plan.norm_each
                     for row in range(first, min(first + plan.norm_each, plan.norm_rows)):
                         norms[row : row + 1, :] = tail[row - first : row - first + 1, :]
@@ -448,7 +488,7 @@
             out_ref[here, :] = weight - rate * direction
 
 
-def finish(plan, my_place, position, norm_state, weights, pieces, slots):
+def finish(plan, my_place, position, total, norm_state, weights, pieces, slots):
     assert all(bound % LANE == 0 for bound in plan.bounds + (plan.blocks,))
     tile = plan.blocks // next(n for n in (TILES, 4, 2, 1) if plan.blocks // LANE % n == 0)
     smem = pl.BlockSpec(memory_space=pltpu.SMEM)
@@ -461,7 +501,7 @@
             jax.ShapeDtypeStruct(norm_state.shape, jnp.float32),
             jax.ShapeDtypeStruct((matrices + 2,), jnp.float32),
         ],
-        in_specs=[smem, smem, vmem, pl.BlockSpec((tile, LANE), lambda i: (i, 0))]
+        in_specs=[smem, smem, vmem, vmem, pl.BlockSpec((tile, LANE), lambda i: (i, 0))]
         + [vmem] * len(pieces),
         out_specs=[pl.BlockSpec((tile, LANE), lambda i: (i, 0)), vmem, smem],
         scratch_shapes=[
@@ -471,7 +511,7 @@
         ],
         compiler_params=pltpu.CompilerParams(vmem_limit_bytes=20 * MIB),
         name="new_weights",
-    )(my_place, position, norm_state, weights, *pieces)
+    )(my_place, position, total, norm_state, weights, *pieces)
 
 
 def local(gradients, weights, first_moment, second_moment, owner_list, norm_grads, norm_state):
@@ -502,18 +542,15 @@
             terms = line_reduce(plan, "x", [mine[z]] + theirs[z])
             near.insert(0, sum(terms[1:], terms[0]) if z else None)
         parts = terms + line_reduce(plan, "z", near)[1:]
-    new_first, new_second, block, stats = update(
+    new_first, new_second, block = update(
         plan, parts, first_moment[0], second_moment[0], weight_own, natural
     )
 
-    hop = 1
-    while hop < plan.narrow:
-        stats = stats + lax.ppermute(stats, "mp", [(i, i ^ hop) for i in range(plan.narrow)])
-        hop *= 2
-    block = lax.dynamic_update_slice(block, block[plan.own :] + stats, (plan.own, 0))
-    found = gather(plan, block)
+    found, total = gather(plan, my_place, block)
     pieces, slots = [piece for piece, _ in found], [parts for _, parts in found]
-    new_weights, new_state, trust_ratios = finish(plan, my_place, position, norm_state, weights, pieces, slots)
+    new_weights, new_state, trust_ratios = finish(
+        plan, my_place, position, total, norm_state, weights, pieces, slots
+    )
     return (new_weights, new_first[None], new_second[None], new_state, trust_ratios)
 
 

time: 173 us -> 174 us (level)
  waiting for transfers between devices: 80.1 us -> 81.9 us
    ppermute x28 -> x30, waiting for transfers between devices: 78 us -> 79.8 us  [send(): return lax.ppermute(value, 'dp', every)]
    ppermute x28 -> x30, starting transfers between devices: 36.4 us -> 35.5 us  [send(): return lax.ppermute(value, 'dp', every)]
  transfers between devices with their start and end apart: 29 -> 31, of which waited for: 17 -> 20; matrix products, arithmetic and copies ran while one was open for 1% -> 1% of each run, Pallas kernels for 4% -> 4%
where the time goes in v14:
time: 174 us
  waiting for transfers between devices  81.9 us (47%)
  Pallas kernels  50.8 us (29%)
  starting transfers between devices  37.1 us (21%)
  other arithmetic  2.79 us (2%)
    ppermute x30, waiting for transfers between devices, send(): return lax.ppermute(value, 'dp', every)  79.8 us
    ppermute x30, starting transfers between devices, send(): return lax.ppermute(value, 'dp', every)  35.5 us
    pallas_call x1, Pallas kernels, place(): pl.pallas_call(functools.partial(place_kernel, plan), out_shape=[jax.Shap...  22.2 us
    pallas_call x1, Pallas kernels, finish(): pl.pallas_call(functools.partial(finish_kernel, plan, tile, slots), grid=...  19.6 us
    pallas_call x1, Pallas kernels, owned(): pl.pallas_call(functools.partial(owned_kernel, plan), out_shape=[jax.Shap...  6.31 us
  transfers between devices with their start and end apart: 31, of which 20 were waited for; matrix products, arithmetic and copies ran while one was open for 1% of the time, Pallas kernels for 4%

profile of v14, /device:TPU:0, one launch (start us, length us, event | category | flops | bytes accessed | tf_op | source)
XLA Modules:
  0.0 173.7 jit_solution(8684676914230993792)
XLA Ops:
  0.7 0.6 pad_add_fusion.place_ref
  1.3 22.2 %place_gradients.1 = (f32[2192,128]{1,0:T(8,128)}, f32[2192,128]{1,0:T(8,128)}, f32[2192,128]{1,0:T(8,128)}, f32[2192,128]{1,0:T(8,128)}, f32[2192,128]{1,0:T(8,...) custom-call(s32[3]{0:T(128)} %pad_add_fusion.place_ref, ...), custom_call_target="tpu_custom_call" | custom-call | tf_op jit(solution)/shard_map/place_gradients/pallas_call | solution.py:286
  23.5 0.5 collective-permute-start
  24.0 2.6 %collective-permute-done = f32[2192,128]{1,0:T(8,128)S(1)} collective-permute-done((f32[2192,128]{1,0:T(8,128)}, f32[2192,128]{1,0:T(8,128)S(1)}, u32[]{:S(2)}, u32[]{:S(2)}) %collective-permute-start) | collective-permute-done | bytes 1122336 | tf_op jit(solution)/shard_map/ppermute | solution.py:74
  26.7 1.1 slice_add_fusion.7
  27.8 0.4 collective-permute-start.5
  28.2 0.1 collective-permute-start.9
  28.4 2.9 %collective-permute-start.3 = (f32[1096,128]{1,0:T(8,128)S(1)}, f32[1096,128]{1,0:T(8,128)S(1)}, u32[]{:S(2)}, u32[]{:S(2)}) collective-permute-start(f32[1096,128]{1,0:T(8,128)S(1)} %slice_add_fusion.7), channel_id=1, source_target_pairs={{0,4},{2,6},{4,0},{6,2},{8,12},{10,14},{12,8},{14,10},{16,20},{18,... | collective-permute-start | bytes 1683464 | tf_op jit(solution)/shard_map/ppermute | solution.py:74
  31.2 6.3 %owned_weights.1 = (f32[1088,128]{1,0:T(8,128)}, s32[1152,128]{1,0:T(8,128)}) custom-call(s32[3]{0:T(128)} %pad_add_fusion.place_ref, s32[136,128]{1,0:T(8,128)} %bitcast.16, f32[17408,128]{1,0:T(8,128)} %weights_ref.3), custom_call_target="tpu_custom_call" | custom-call | bytes 20971520 | tf_op jit(solution)/shard_map/owned_weights/pallas_call | solution.py:364
  37.6 0.1 collective-permute-start.1
  37.7 0.1 slice_add_fusion.2
  37.7 0.2 collective-permute-start.6
  37.9 6.8 %collective-permute-done.3 = f32[1096,128]{1,0:T(8,128)S(1)} collective-permute-done((f32[1096,128]{1,0:T(8,128)S(1)}, f32[1096,128]{1,0:T(8,128)S(1)}, u32[]{:S(2)}, u32[]{:S(2)}) %collective-permute-start.3) | collective-permute-done | bytes 561184 | tf_op jit(solution)/shard_map/ppermute | solution.py:74
  44.7 0.1 fusion.2
  44.8 4.1 %collective-permute-start.4 = (f32[1096,128]{1,0:T(8,128)S(1)}, f32[1096,128]{1,0:T(8,128)S(1)}, u32[]{:S(2)}, u32[]{:S(2)}) collective-permute-start(f32[1096,128]{1,0:T(8,128)S(1)} %fusion.2), channel_id=1, source_target_pairs={{0,8},{2,10},{4,12},{6,14},{24,16},{26,18},{28,20},{30,22},{1,9},{... | collective-permute-start | bytes 1683464 | tf_op jit(solution)/shard_map/ppermute | solution.py:74
  48.9 0.1 slice_add_fusion
  49.0 1.6 collective-permute-start.10
  50.5 6.2 %collective-permute-done.6 = f32[1096,128]{1,0:T(8,128)S(1)} collective-permute-done((f32[1096,128]{1,0:T(8,128)S(1)}, f32[1096,128]{1,0:T(8,128)S(1)}, u32[]{:S(2)}, u32[]{:S(2)}) %collective-permute-start.6) | collective-permute-done | bytes 561184 | tf_op jit(solution)/shard_map/ppermute | solution.py:74
  56.7 0.1 fusion.1
  56.9 2.6 %collective-permute-done.4 = f32[1096,128]{1,0:T(8,128)S(1)} collective-permute-done((f32[1096,128]{1,0:T(8,128)S(1)}, f32[1096,128]{1,0:T(8,128)S(1)}, u32[]{:S(2)}, u32[]{:S(2)}) %collective-permute-start.4) | collective-permute-done | bytes 561184 | tf_op jit(solution)/shard_map/ppermute | solution.py:74
  59.5 4.4 %collective-permute-start.8 = (f32[1096,128]{1,0:T(8,128)S(1)}, f32[1096,128]{1,0:T(8,128)S(1)}, u32[]{:S(2)}, u32[]{:S(2)}) collective-permute-start(f32[1096,128]{1,0:T(8,128)S(1)} %fusion.1), channel_id=1, source_target_pairs={{0,8},{2,10},{4,12},{6,14},{24,16},{26,18},{28,20},{30,22},{1,9},{... | collective-permute-start | bytes 1683464 | tf_op jit(solution)/shard_map/ppermute | solution.py:74
  64.0 0.7 collective-permute-start.7
  64.7 0.1 slice_add_fusion.5
  64.9 1.6 collective-permute-start.2
  66.4 2.3 %collective-permute-done.10 = f32[1096,128]{1,0:T(8,128)S(1)} collective-permute-done((f32[1096,128]{1,0:T(8,128)S(1)}, f32[1096,128]{1,0:T(8,128)S(1)}, u32[]{:S(2)}, u32[]{:S(2)}) %collective-permute-start.10) | collective-permute-done | bytes 561184 | tf_op jit(solution)/shard_map/ppermute | solution.py:74
  68.8 0.1 fusion
  68.9 4.7 %collective-permute-done.8 = f32[1096,128]{1,0:T(8,128)S(1)} collective-permute-done((f32[1096,128]{1,0:T(8,128)S(1)}, f32[1096,128]{1,0:T(8,128)S(1)}, u32[]{:S(2)}, u32[]{:S(2)}) %collective-permute-start.8) | collective-permute-done | bytes 561184 | tf_op jit(solution)/shard_map/ppermute | solution.py:74
  73.7 3.9 %collective-permute-start.11 = (f32[1096,128]{1,0:T(8,128)S(1)}, f32[1096,128]{1,0:T(8,128)S(1)}, u32[]{:S(2)}, u32[]{:S(2)}) collective-permute-start(f32[1096,128]{1,0:T(8,128)S(1)} %add.80), channel_id=1, source_target_pairs={{0,8},{2,10},{4,12},{6,14},{8,0},{10,2},{12,4},{14,6},{16,24},{18,... | collective-permute-start | bytes 1683464 | tf_op jit(solution)/shard_map/ppermute | solution.py:74
  77.7 0.7 collective-permute-start.12
  78.3 2.0 %collective-permute-done.2.refs_1_ = f32[1096,128]{1,0:T(8,128)S(1)} collective-permute-done((f32[1096,128]{1,0:T(8,128)S(1)}, f32[1096,128]{1,0:T(8,128)S(1)}, u32[]{:S(2)}, u32[]{:S(2)}) %collective-permute-start.2) | collective-permute-done | bytes 561184 | tf_op jit(solution)/shard_map/ppermute | solution.py:74
  80.3 6.9 %collective-permute-done.11.refs_2_ = f32[1096,128]{1,0:T(8,128)S(1)} collective-permute-done((f32[1096,128]{1,0:T(8,128)S(1)}, f32[1096,128]{1,0:T(8,128)S(1)}, u32[]{:S(2)}, u32[]{:S(2)}) %collective-permute-start.11) | collective-permute-done | bytes 561184 | tf_op jit(solution)/shard_map/ppermute | solution.py:74
  87.2 2.1 %moments.1 = (f32[1088,128]{1,0:T(8,128)}, f32[1088,128]{1,0:T(8,128)}, f32[1096,128]{1,0:T(8,128)S(1)}) custom-call(f32[1096,128]{1,0:T(8,128)S(1)} %get-tuple-element.84.refs_0_, f32[1096,128]{1,0:T(8,128)S(1)} %collective-permute-done.2.refs_1_, f32[1096,128]{1,0:T(8,128)S(1)} %collective-permute-done.11.refs_2_, ...), custom_call_target="tpu_custom_call" | custom-call | tf_op jit(solution)/shard_map/moments/pallas_call | solution.py:418
  89.3 3.8 %collective-permute-start.14 = (f32[1096,128]{1,0:T(8,128)S(1)}, f32[1096,128]{1,0:T(8,128)S(1)}, u32[]{:S(2)}, u32[]{:S(2)}) collective-permute-start(f32[1096,128]{1,0:T(8,128)S(1)} %get-tuple-element.66), channel_id=1, source_target_pairs={{0,8},{2,10},{4,12},{6,14},{8,0},{10,2},{12,4},{14,6},{16,24},{18,... | collective-permute-start | bytes 1683464 | tf_op jit(solution)/shard_map/ppermute | solution.py:74
  93.2 1.5 collective-permute-start.15
  94.6 0.7 collective-permute-start.13
  95.3 6.4 %collective-permute-done.14 = f32[1096,128]{1,0:T(8,128)S(1)} collective-permute-done((f32[1096,128]{1,0:T(8,128)S(1)}, f32[1096,128]{1,0:T(8,128)S(1)}, u32[]{:S(2)}, u32[]{:S(2)}) %collective-permute-start.14) | collective-permute-done | bytes 561184 | tf_op jit(solution)/shard_map/ppermute | solution.py:74
  101.8 1.5 collective-permute-start.18
  103.3 0.1 pad_maximum_fusion.refs_0_.refs_1_
  103.4 3.6 %collective-permute-done.15 = f32[1096,128]{1,0:T(8,128)S(1)} collective-permute-done((f32[1096,128]{1,0:T(8,128)S(1)}, f32[1096,128]{1,0:T(8,128)S(1)}, u32[]{:S(2)}, u32[]{:S(2)}) %collective-permute-start.15) | collective-permute-done | bytes 561184 | tf_op jit(solution)/shard_map/ppermute | solution.py:74
  106.9 0.7 collective-permute-start.16
  107.6 1.3 collective-permute-start.17
  108.9 6.3 %collective-permute-done.18 = f32[1096,128]{1,0:T(8,128)S(1)} collective-permute-done((f32[1096,128]{1,0:T(8,128)S(1)}, f32[1096,128]{1,0:T(8,128)S(1)}, u32[]{:S(2)}, u32[]{:S(2)}) %collective-permute-start.18) | collective-permute-done | bytes 561184 | tf_op jit(solution)/shard_map/ppermute | solution.py:74
  115.3 0.1 pad_maximum_fusion.1.refs_1_
  115.3 7.2 %collective-permute-done.17 = f32[1096,128]{1,0:T(8,128)S(1)} collective-permute-done((f32[1096,128]{1,0:T(8,128)S(1)}, f32[1096,128]{1,0:T(8,128)S(1)}, u32[]{:S(2)}, u32[]{:S(2)}) %collective-permute-start.17) | collective-permute-done | bytes 561184 | tf_op jit(solution)/shard_map/ppermute | solution.py:74
  122.5 0.1 add.82.refs_2_
  122.6 1.3 collective-permute-start.19
  123.9 0.8 collective-permute-start.24
  124.7 9.3 %collective-permute-done.19 = f32[1096,128]{1,0:T(8,128)S(1)} collective-permute-done((f32[1096,128]{1,0:T(8,128)S(1)}, f32[1096,128]{1,0:T(8,128)S(1)}, u32[]{:S(2)}, u32[]{:S(2)}) %collective-permute-start.19) | collective-permute-done | bytes 561184 | tf_op jit(solution)/shard_map/ppermute | solution.py:74
  134.1 0.1 add.83.refs_3_.refs_4_
  134.2 0.8 collective-permute-start.23
  135.0 3.5 %collective-permute-done.24.refs_3_ = f32[1096,128]{1,0:T(8,128)S(1)} collective-permute-done((f32[1096,128]{1,0:T(8,128)S(1)}, f32[1096,128]{1,0:T(8,128)S(1)}, u32[]{:S(2)}, u32[]{:S(2)}) %collective-permute-start.24) | collective-permute-done | bytes 561184 | tf_op jit(solution)/shard_map/ppermute | solution.py:74
  138.6 0.5 collective-permute-start.25
  139.1 0.6 sums.1
  139.6 0.9 collective-permute-start.20
  140.5 5.1 %collective-permute-done.20 = f32[8,128]{1,0:T(8,128)S(1)} collective-permute-done((f32[8,128]{1,0:T(8,128)S(1)}, f32[8,128]{1,0:T(8,128)S(1)}, u32[]{:S(2)}, u32[]{:S(2)}) %collective-permute-start.20) | collective-permute-done | bytes 4128 | tf_op jit(solution)/shard_map/ppermute | solution.py:74
  145.7 1.2 collective-permute-done.21
  146.8 1.5 collective-permute-start.22
  148.3 2.1 %collective-permute-done.22 = f32[8,128]{1,0:T(8,128)S(1)} collective-permute-done((f32[8,128]{1,0:T(8,128)S(1)}, f32[8,128]{1,0:T(8,128)S(1)}, u32[]{:S(2)}, u32[]{:S(2)}) %collective-permute-start.22) | collective-permute-done | bytes 4128 | tf_op jit(solution)/shard_map/ppermute | solution.py:156
  150.4 0.5 collective-permute-start.29
  150.9 0.1 collective-permute-start.30
  151.0 1.4 collective-permute-done.28.refs_9_
  152.4 0.8 collective-permute-done.29.refs_10_
  153.2 0.8 collective-permute-done.30.refs_11_
  154.0 19.6 %new_weights.1 = (f32[17408,128]{1,0:T(8,128)}, f32[3,2,1024]{2,1,0:T(2,128)}, f32[7]{0:T(128)}) custom-call(s32[3]{0:T(128)S(1)} %copy-done.6, s32[136,128]{1,0:T(8,128)S(1)} %copy-done.4, f32[8,128]{1,0:T(8,128)S(1)} %add.86.total_ref, f32[3,2,1024]{2,1,0:T(2,128)S(1)} %copy-done.5, f32[17408,128]{1,0:T(8,128)S(1)} %bitcast.11, ...), custom_call_target="tpu_custom_call" | custom-call | tf_op jit(solution)/shard_map/new_weights/pallas_call | solution.py:496
  (50 shorter events, 0.3 us)
Async XLA Ops:
  23.5 3.1 %collective-permute-start = (f32[2192,128]{1,0:T(8,128)}, f32[2192,128]{1,0:T(8,128)S(1)}, u32[]{:S(2)}, u32[]{:S(2)}) collective-permute-start(f32[2192,128]{1,0:T(8,128)} %get-tuple-element.47), channel_id=1, source_target_pairs={{0,2},{2,0},{4,6},{6,4},{8,10},{10,8},{12,14},{14,12},{16,18},{18,... | collective-permute-start | bytes 3366920 | tf_op jit(solution)/shard_map/ppermute | solution.py:74
  27.8 9.9 %copy-start.9 = (f32[2192,128]{1,0:T(8,128)S(1)}, f32[2192,128]{1,0:T(8,128)}, u32[]{:S(2)}) copy-start(f32[2192,128]{1,0:T(8,128)} %get-tuple-element.53) | copy-start | bytes 3366916
  27.8 9.8 %collective-permute-start.5 = (f32[2192,128]{1,0:T(8,128)}, f32[2192,128]{1,0:T(8,128)S(1)}, u32[]{:S(2)}, u32[]{:S(2)}) collective-permute-start(f32[2192,128]{1,0:T(8,128)} %get-tuple-element.54), channel_id=1, source_target_pairs={{0,2},{2,0},{4,6},{6,4},{8,10},{10,8},{12,14},{14,12},{16,18},{18,... | collective-permute-start | bytes 3366920 | tf_op jit(solution)/shard_map/ppermute | solution.py:74
  28.2 20.7 %collective-permute-start.9 = (f32[2192,128]{1,0:T(8,128)}, f32[2192,128]{1,0:T(8,128)S(1)}, u32[]{:S(2)}, u32[]{:S(2)}) collective-permute-start(f32[2192,128]{1,0:T(8,128)} %get-tuple-element.60), channel_id=1, source_target_pairs={{0,2},{2,0},{4,6},{6,4},{8,10},{10,8},{12,14},{14,12},{16,18},{18,... | collective-permute-start | bytes 3366920 | tf_op jit(solution)/shard_map/ppermute | solution.py:74
  28.4 16.4 %collective-permute-start.3 = (f32[1096,128]{1,0:T(8,128)S(1)}, f32[1096,128]{1,0:T(8,128)S(1)}, u32[]{:S(2)}, u32[]{:S(2)}) collective-permute-start(f32[1096,128]{1,0:T(8,128)S(1)} %slice_add_fusion.7), channel_id=1, source_target_pairs={{0,4},{2,6},{4,0},{6,2},{8,12},{10,14},{12,8},{14,10},{16,20},{18,... | collective-permute-start | bytes 1683464 | tf_op jit(solution)/shard_map/ppermute | solution.py:74
  37.5 7.2 %copy-start.10 = (f32[2192,128]{1,0:T(8,128)S(1)}, f32[2192,128]{1,0:T(8,128)}, u32[]{:S(2)}) copy-start(f32[2192,128]{1,0:T(8,128)} %get-tuple-element.46) | copy-start | bytes 3366916
  37.6 27.1 %collective-permute-start.1 = (f32[2192,128]{1,0:T(8,128)}, f32[2192,128]{1,0:T(8,128)S(1)}, u32[]{:S(2)}, u32[]{:S(2)}) collective-permute-start(f32[2192,128]{1,0:T(8,128)} %get-tuple-element.51), channel_id=1, source_target_pairs={{0,2},{2,0},{4,6},{6,4},{8,10},{10,8},{12,14},{14,12},{16,18},{18,... | collective-permute-start | bytes 3366920 | tf_op jit(solution)/shard_map/ppermute | solution.py:74
  37.7 11.2 %copy-start.7 = (f32[2192,128]{1,0:T(8,128)S(1)}, f32[2192,128]{1,0:T(8,128)}, u32[]{:S(2)}) copy-start(f32[2192,128]{1,0:T(8,128)} %get-tuple-element.59) | copy-start | bytes 3366916
  37.7 19.0 %collective-permute-start.6 = (f32[1096,128]{1,0:T(8,128)S(1)}, f32[1096,128]{1,0:T(8,128)S(1)}, u32[]{:S(2)}, u32[]{:S(2)}) collective-permute-start(f32[1096,128]{1,0:T(8,128)S(1)} %slice_add_fusion.2), channel_id=1, source_target_pairs={{0,4},{2,6},{4,0},{6,2},{8,12},{10,14},{12,8},{14,10},{16,20},{18,... | collective-permute-start | bytes 1683464 | tf_op jit(solution)/shard_map/ppermute | solution.py:74
  44.8 14.7 %collective-permute-start.4 = (f32[1096,128]{1,0:T(8,128)S(1)}, f32[1096,128]{1,0:T(8,128)S(1)}, u32[]{:S(2)}, u32[]{:S(2)}) collective-permute-start(f32[1096,128]{1,0:T(8,128)S(1)} %fusion.2), channel_id=1, source_target_pairs={{0,8},{2,10},{4,12},{6,14},{24,16},{26,18},{28,20},{30,22},{1,9},{... | collective-permute-start | bytes 1683464 | tf_op jit(solution)/shard_map/ppermute | solution.py:74
  49.0 19.8 %collective-permute-start.10 = (f32[1096,128]{1,0:T(8,128)S(1)}, f32[1096,128]{1,0:T(8,128)S(1)}, u32[]{:S(2)}, u32[]{:S(2)}) collective-permute-start(f32[1096,128]{1,0:T(8,128)S(1)} %slice_add_fusion), channel_id=1, source_target_pairs={{0,4},{2,6},{4,0},{6,2},{8,12},{10,14},{12,8},{14,10},{16,20},{18,... | collective-permute-start | bytes 1683464 | tf_op jit(solution)/shard_map/ppermute | solution.py:74
  56.9 7.8 %copy-start.8 = (f32[2192,128]{1,0:T(8,128)S(1)}, f32[2192,128]{1,0:T(8,128)}, u32[]{:S(2)}) copy-start(f32[2192,128]{1,0:T(8,128)} %get-tuple-element.45) | copy-start | bytes 3366916
  59.5 14.1 %collective-permute-start.8 = (f32[1096,128]{1,0:T(8,128)S(1)}, f32[1096,128]{1,0:T(8,128)S(1)}, u32[]{:S(2)}, u32[]{:S(2)}) collective-permute-start(f32[1096,128]{1,0:T(8,128)S(1)} %fusion.1), channel_id=1, source_target_pairs={{0,8},{2,10},{4,12},{6,14},{24,16},{26,18},{28,20},{30,22},{1,9},{... | collective-permute-start | bytes 1683464 | tf_op jit(solution)/shard_map/ppermute | solution.py:74
  64.0 4.9 %collective-permute-start.7 = (f32[1096,128]{1,0:T(8,128)S(1)}, f32[1096,128]{1,0:T(8,128)S(1)}, u32[]{:S(2)}, u32[]{:S(2)}) collective-permute-start(f32[1096,128]{1,0:T(8,128)S(1)} %add.76), channel_id=1, source_target_pairs={{8,16},{10,18},{12,20},{14,22},{16,8},{18,10},{20,12},{22,14},{9,1... | collective-permute-start | bytes 1683464 | tf_op jit(solution)/shard_map/ppermute | solution.py:74
  64.7 22.5 %copy-start.2 = (f32[1,1088,128]{2,1,0:T(8,128)S(1)}, f32[1,1088,128]{2,1,0:T(8,128)}, u32[]{:S(2)}) copy-start(f32[1,1088,128]{2,1,0:T(8,128)} %param.10) | copy-start | bytes 1671172
  64.7 22.5 %copy-start.3 = (f32[1088,128]{1,0:T(8,128)S(1)}, f32[1088,128]{1,0:T(8,128)}, u32[]{:S(2)}) copy-start(f32[1088,128]{1,0:T(8,128)} %get-tuple-element.64.refs_6_) | copy-start | bytes 1671172
  64.9 15.4 %collective-permute-start.2 = (f32[1096,128]{1,0:T(8,128)S(1)}, f32[1096,128]{1,0:T(8,128)S(1)}, u32[]{:S(2)}, u32[]{:S(2)}) collective-permute-start(f32[1096,128]{1,0:T(8,128)S(1)} %get-tuple-element.83), channel_id=1, source_target_pairs={{0,4},{2,6},{4,0},{6,2},{8,12},{10,14},{12,8},{14,10},{16,20},{18,... | collective-permute-start | bytes 1683464 | tf_op jit(solution)/shard_map/ppermute | solution.py:74
  68.8 85.2 %slice-start = ((s8[8912896]{0:T(1024)(128)(4,1)}), s8[4194304]{0:T(1024)(128)(4,1)S(1)}, s32[]{:S(2)}) async-start(s8[8912896]{0:T(1024)(128)(4,1)} %bitcast.10), calls=%async_computation | async-start | bytes 8388608
  73.6 13.6 %copy-start = (s32[1152,128]{1,0:T(8,128)S(1)}, s32[1152,128]{1,0:T(8,128)}, u32[]{:S(2)}) copy-start(s32[1152,128]{1,0:T(8,128)} %get-tuple-element.65.refs_7_) | copy-start | bytes 1769476
  73.7 13.6 %copy-start.1 = (f32[1,1088,128]{2,1,0:T(8,128)S(1)}, f32[1,1088,128]{2,1,0:T(8,128)}, u32[]{:S(2)}) copy-start(f32[1,1088,128]{2,1,0:T(8,128)} %param.9) | copy-start | bytes 1671172
  73.7 13.5 %collective-permute-start.11 = (f32[1096,128]{1,0:T(8,128)S(1)}, f32[1096,128]{1,0:T(8,128)S(1)}, u32[]{:S(2)}, u32[]{:S(2)}) collective-permute-start(f32[1096,128]{1,0:T(8,128)S(1)} %add.80), channel_id=1, source_target_pairs={{0,8},{2,10},{4,12},{6,14},{8,0},{10,2},{12,4},{14,6},{16,24},{18,... | collective-permute-start | bytes 1683464 | tf_op jit(solution)/shard_map/ppermute | solution.py:74
  77.7 9.5 %collective-permute-start.12 = (f32[1096,128]{1,0:T(8,128)S(1)}, f32[1096,128]{1,0:T(8,128)S(1)}, u32[]{:S(2)}, u32[]{:S(2)}) collective-permute-start(f32[1096,128]{1,0:T(8,128)S(1)} %add.81), channel_id=1, source_target_pairs={{8,16},{10,18},{12,20},{14,22},{16,8},{18,10},{20,12},{22,14},{9,1... | collective-permute-start | bytes 1683464 | tf_op jit(solution)/shard_map/ppermute | solution.py:74
  87.2 66.8 %slice-start.1 = ((s8[8912896]{0:T(1024)(128)(4,1)}), s8[4194304]{0:T(1024)(128)(4,1)S(1)}, s32[]{:S(2)}) async-start(s8[8912896]{0:T(1024)(128)(4,1)} %bitcast.10), calls=%async_computation.1 | async-start | bytes 8388608
  89.3 12.5 %collective-permute-start.14 = (f32[1096,128]{1,0:T(8,128)S(1)}, f32[1096,128]{1,0:T(8,128)S(1)}, u32[]{:S(2)}, u32[]{:S(2)}) collective-permute-start(f32[1096,128]{1,0:T(8,128)S(1)} %get-tuple-element.66), channel_id=1, source_target_pairs={{0,8},{2,10},{4,12},{6,14},{8,0},{10,2},{12,4},{14,6},{16,24},{18,... | collective-permute-start | bytes 1683464 | tf_op jit(solution)/shard_map/ppermute | solution.py:74
  93.2 13.8 %collective-permute-start.15 = (f32[1096,128]{1,0:T(8,128)S(1)}, f32[1096,128]{1,0:T(8,128)S(1)}, u32[]{:S(2)}, u32[]{:S(2)}) collective-permute-start(f32[1096,128]{1,0:T(8,128)S(1)} %get-tuple-element.66), channel_id=1, source_target_pairs={{0,4},{2,6},{4,0},{6,2},{8,12},{10,14},{12,8},{14,10},{16,20},{18,... | collective-permute-start | bytes 1683464 | tf_op jit(solution)/shard_map/ppermute | solution.py:74
  94.6 12.3 %collective-permute-start.13 = (f32[1096,128]{1,0:T(8,128)S(1)}, f32[1096,128]{1,0:T(8,128)S(1)}, u32[]{:S(2)}, u32[]{:S(2)}) collective-permute-start(f32[1096,128]{1,0:T(8,128)S(1)} %get-tuple-element.66), channel_id=1, source_target_pairs={{8,16},{10,18},{12,20},{14,22},{16,8},{18,10},{20,12},{22,14},{9,1... | collective-permute-start | bytes 1683464 | tf_op jit(solution)/shard_map/ppermute | solution.py:74
  101.8 13.5 %collective-permute-start.18 = (f32[1096,128]{1,0:T(8,128)S(1)}, f32[1096,128]{1,0:T(8,128)S(1)}, u32[]{:S(2)}, u32[]{:S(2)}) collective-permute-start(f32[1096,128]{1,0:T(8,128)S(1)} %collective-permute-done.14), channel_id=1, source_target_pairs={{0,4},{2,6},{4,0},{6,2},{8,12},{10,14},{12,8},{14,10},{16,20},{18,... | collective-permute-start | bytes 1683464 | tf_op jit(solution)/shard_map/ppermute | solution.py:74
  103.3 50.7 %slice-start.2 = ((s8[8912896]{0:T(1024)(128)(4,1)}), s8[524288]{0:T(1024)(128)(4,1)S(1)}, s32[]{:S(2)}) async-start(s8[8912896]{0:T(1024)(128)(4,1)} %bitcast.10), calls=%async_computation.2 | async-start | bytes 1048576
  106.9 8.4 %collective-permute-start.16 = (f32[1096,128]{1,0:T(8,128)S(1)}, f32[1096,128]{1,0:T(8,128)S(1)}, u32[]{:S(2)}, u32[]{:S(2)}) collective-permute-start(f32[1096,128]{1,0:T(8,128)S(1)} %collective-permute-done.14), channel_id=1, source_target_pairs={{8,16},{10,18},{12,20},{14,22},{16,8},{18,10},{20,12},{22,14},{9,1... | collective-permute-start | bytes 1683464 | tf_op jit(solution)/shard_map/ppermute | solution.py:74
  107.6 14.9 %collective-permute-start.17 = (f32[1096,128]{1,0:T(8,128)S(1)}, f32[1096,128]{1,0:T(8,128)S(1)}, u32[]{:S(2)}, u32[]{:S(2)}) collective-permute-start(f32[1096,128]{1,0:T(8,128)S(1)} %collective-permute-done.13), channel_id=1, source_target_pairs={{8,0},{10,2},{12,4},{14,6},{16,24},{18,26},{20,28},{22,30},{9,1},{... | collective-permute-start | bytes 1683464 | tf_op jit(solution)/shard_map/ppermute | solution.py:74
  122.6 16.5 %copy-start.6 = (s32[3]{0:T(128)S(1)}, s32[3]{0:T(128)}, u32[]{:S(2)}) copy-start(s32[3]{0:T(128)} %pad_add_fusion.place_ref) | copy-start | bytes 40
  122.6 11.5 %collective-permute-start.19 = (f32[1096,128]{1,0:T(8,128)S(1)}, f32[1096,128]{1,0:T(8,128)S(1)}, u32[]{:S(2)}, u32[]{:S(2)}) collective-permute-start(f32[1096,128]{1,0:T(8,128)S(1)} %collective-permute-done.16), channel_id=1, source_target_pairs={{8,0},{10,2},{12,4},{14,6},{16,24},{18,26},{20,28},{22,30},{9,1},{... | collective-permute-start | bytes 1683464 | tf_op jit(solution)/shard_map/ppermute | solution.py:74
  123.9 14.7 %collective-permute-start.24 = (f32[1096,128]{1,0:T(8,128)S(1)}, f32[1096,128]{1,0:T(8,128)S(1)}, u32[]{:S(2)}, u32[]{:S(2)}) collective-permute-start(f32[1096,128]{1,0:T(8,128)S(1)} %add.82.refs_2_), channel_id=1, source_target_pairs={{0,4},{2,6},{4,0},{6,2},{8,12},{10,14},{12,8},{14,10},{16,20},{18,... | collective-permute-start | bytes 1683464 | tf_op jit(solution)/shard_map/ppermute | solution.py:74
  124.7 27.7 %collective-permute-start.26 = (f32[2192,128]{1,0:T(8,128)S(1)}, f32[2192,128]{1,0:T(8,128)S(1)}, u32[]{:S(2)}, u32[]{:S(2)}) collective-permute-start(f32[2192,128]{1,0:T(8,128)S(1)} %pad_maximum_fusion.1.refs_1_), channel_id=1, source_target_pairs={{0,2},{2,0},{4,6},{6,4},{8,10},{10,8},{12,14},{14,12},{16,18},{18,... | collective-permute-start | bytes 3366920 | tf_op jit(solution)/shard_map/ppermute | solution.py:74
  134.1 19.9 %copy-start.4 = (s32[136,128]{1,0:T(8,128)S(1)}, s32[136,128]{1,0:T(8,128)}, u32[]{:S(2)}) copy-start(s32[136,128]{1,0:T(8,128)} %get-tuple-element.44.position_ref) | copy-start | bytes 208900
  134.2 19.9 %copy-start.5 = (f32[3,2,1024]{2,1,0:T(2,128)S(1)}, f32[3,2,1024]{2,1,0:T(2,128)}, u32[]{:S(2)}) copy-start(f32[3,2,1024]{2,1,0:T(2,128)} %norm_ref.1) | copy-start | bytes 73732
  134.2 16.3 %collective-permute-start.23 = (f32[1096,128]{1,0:T(8,128)S(1)}, f32[1096,128]{1,0:T(8,128)S(1)}, u32[]{:S(2)}, u32[]{:S(2)}) collective-permute-start(f32[1096,128]{1,0:T(8,128)S(1)} %add.83.refs_3_.refs_4_), channel_id=1, source_target_pairs={{0,4},{2,6},{4,0},{6,2},{8,12},{10,14},{12,8},{14,10},{16,20},{18,... | collective-permute-start | bytes 1683464 | tf_op jit(solution)/shard_map/ppermute | solution.py:74
  138.6 12.4 %collective-permute-start.27 = (f32[1096,128]{1,0:T(8,128)S(1)}, f32[1096,128]{1,0:T(8,128)S(1)}, u32[]{:S(2)}, u32[]{:S(2)}) collective-permute-start(f32[1096,128]{1,0:T(8,128)S(1)} %add.82.refs_2_), channel_id=1, source_target_pairs={{0,2},{2,0},{4,6},{6,4},{8,10},{10,8},{12,14},{14,12},{16,18},{18,... | collective-permute-start | bytes 1683464 | tf_op jit(solution)/shard_map/ppermute | solution.py:74
  138.6 15.4 %collective-permute-start.25 = (f32[2192,128]{1,0:T(8,128)S(1)}, f32[2192,128]{1,0:T(8,128)S(1)}, u32[]{:S(2)}, u32[]{:S(2)}) collective-permute-start(f32[2192,128]{1,0:T(8,128)S(1)} %pad_maximum_fusion.refs_0_.refs_1_), channel_id=1, source_target_pairs={{0,2},{2,0},{4,6},{6,4},{8,10},{10,8},{12,14},{14,12},{16,18},{18,... | collective-permute-start | bytes 3366920 | tf_op jit(solution)/shard_map/ppermute | solution.py:74
  139.6 6.0 %collective-permute-start.20 = (f32[8,128]{1,0:T(8,128)S(1)}, f32[8,128]{1,0:T(8,128)S(1)}, u32[]{:S(2)}, u32[]{:S(2)}) collective-permute-start(f32[8,128]{1,0:T(8,128)S(1)} %sums.1), channel_id=1, source_target_pairs={{0,4},{2,6},{4,0},{6,2},{8,12},{10,14},{12,8},{14,10},{16,20},{18,... | collective-permute-start | bytes 12296 | tf_op jit(solution)/shard_map/ppermute | solution.py:74
  145.6 1.2 collective-permute-start.21
  146.8 3.6 %collective-permute-start.22 = (f32[8,128]{1,0:T(8,128)S(1)}, f32[8,128]{1,0:T(8,128)S(1)}, u32[]{:S(2)}, u32[]{:S(2)}) collective-permute-start(f32[8,128]{1,0:T(8,128)S(1)} %add.85), channel_id=1, source_target_pairs={{0,1},{1,0},{2,3},{3,2},{4,5},{5,4},{6,7},{7,6},{8,9},{9,8},{10,11... | collective-permute-start | bytes 12296 | tf_op jit(solution)/shard_map/ppermute | solution.py:156
  150.4 2.0 %collective-permute-start.28 = (f32[1096,128]{1,0:T(8,128)S(1)}, f32[1096,128]{1,0:T(8,128)S(1)}, u32[]{:S(2)}, u32[]{:S(2)}) collective-permute-start(f32[1096,128]{1,0:T(8,128)S(1)} %collective-permute-done.24.refs_3_), channel_id=1, source_target_pairs={{0,2},{2,0},{4,6},{6,4},{8,10},{10,8},{12,14},{14,12},{16,18},{18,... | collective-permute-start | bytes 1683464 | tf_op jit(solution)/shard_map/ppermute | solution.py:74
  150.4 2.8 %collective-permute-start.29 = (f32[1096,128]{1,0:T(8,128)S(1)}, f32[1096,128]{1,0:T(8,128)S(1)}, u32[]{:S(2)}, u32[]{:S(2)}) collective-permute-start(f32[1096,128]{1,0:T(8,128)S(1)} %add.83.refs_3_.refs_4_), channel_id=1, source_target_pairs={{0,2},{2,0},{4,6},{6,4},{8,10},{10,8},{12,14},{14,12},{16,18},{18,... | collective-permute-start | bytes 1683464 | tf_op jit(solution)/shard_map/ppermute | solution.py:74
  150.9 3.0 %collective-permute-start.30 = (f32[1096,128]{1,0:T(8,128)S(1)}, f32[1096,128]{1,0:T(8,128)S(1)}, u32[]{:S(2)}, u32[]{:S(2)}) collective-permute-start(f32[1096,128]{1,0:T(8,128)S(1)} %collective-permute-done.23.refs_5_), channel_id=1, source_target_pairs={{0,2},{2,0},{4,6},{6,4},{8,10},{10,8},{12,14},{14,12},{16,18},{18,... | collective-permute-start | bytes 1683464 | tf_op jit(solution)/shard_map/ppermute | solution.py:74

commit v15 on v14

--- a/solution.py
+++ b/solution.py
@@ -150,6 +150,10 @@
     while hop < plan.nx:
         total = total + plan.send(total, "x", [(i, i ^ hop) for i in range(plan.nx)])
         hop *= 2
+    return total
+
+
+def all_cores(plan, total):
     total = total + plan.swap(total)
     hop = 1
     while hop < plan.narrow:
@@ -164,7 +168,7 @@
 
     if plan.nz != 4:
         lines = [along_x(value) for value in line_gather(plan, "z", plan.nz, block)]
-        total = all_sums(plan, my_place, [(line[0], 0) for line in lines])
+        total = all_cores(plan, all_sums(plan, my_place, [(line[0], 0) for line in lines]))
         mine = [(value, [(z, x)]) for z, line in enumerate(lines) for x, value in enumerate(line)]
     else:
         line = along_x(block)
@@ -174,6 +178,7 @@
         line_pair = along_x(pair)
         two = plan.send(pair, "z", MIDDLE)
         out_two = plan.send(three, "z", OUTWARD)
+        _, *line_pair = together(two, *line_pair)
         far = [jnp.concatenate([line[x], line_pair[x]]) for x in range(1, plan.nx)]
         near_two, *far = together(two + out_two, *far)
         line_two = along_x(near_two)
@@ -181,12 +186,13 @@
         near_three = three + out_three
         line_three = along_x(near_three)
         total = all_sums(plan, my_place, [(own, 0), (own, plan.block), (near_two, 0), (near_three, 0)])
-        own, *line_two = together(own, *line_two)
-        total, *line_three = together(total, *line_three)
+        total, *line_two = together(total, *line_two)
+        early = plan.swap(near_three)
+        early, total, *line_three = together(early, all_cores(plan, total), *line_three)
         mine = [(value, [(0, x), (1, x)]) for x, value in enumerate([own] + far)]
         mine += [(value, [(2, x)]) for x, value in enumerate(line_two)]
         mine += [(value, [(3, x)]) for x, value in enumerate(line_three)]
-    swapped = [plan.swap(value) for value, _ in mine]
+    swapped = [early if plan.nz == 4 and slots == [(3, 0)] else plan.swap(value) for value, slots in mine]
     found = [(value, [slot + (0,) for slot in slots]) for value, slots in mine]
     found += [(value, [slot + (1,) for slot in slots]) for value, (_, slots) in zip(swapped, mine)]
     return found, total

time: 174 us -> 171 us (0.983)
  waiting for transfers between devices: 81.9 us -> 76.2 us
  starting transfers between devices: 37.1 us -> 39.4 us
    ppermute x30, waiting for transfers between devices: 79.8 us -> 74.1 us  [send(): return lax.ppermute(value, 'dp', every)]
    ppermute x30, starting transfers between devices: 35.5 us -> 37.9 us  [send(): return lax.ppermute(value, 'dp', every)]
  transfers between devices with their start and end apart: 31 -> 31, of which waited for: 20 -> 19; matrix products, arithmetic and copies ran while one was open for 1% -> 1% of each run, Pallas kernels for 4% -> 4%
where the time goes in v15:
time: 171 us; the launch traced here: 170 us
  waiting for transfers between devices  76.2 us (45%)
  Pallas kernels  50.8 us (30%)
  starting transfers between devices  39.4 us (23%)
  other arithmetic  2.82 us (2%)
    ppermute x30, waiting for transfers between devices, send(): return lax.ppermute(value, 'dp', every)  74.1 us
    ppermute x30, starting transfers between devices, send(): return lax.ppermute(value, 'dp', every)  37.9 us
    pallas_call x1, Pallas kernels, place(): pl.pallas_call(functools.partial(place_kernel, plan), out_shape=[jax.Shap...  22.2 us
    pallas_call x1, Pallas kernels, finish(): pl.pallas_call(functools.partial(finish_kernel, plan, tile, slots), grid=...  19.6 us
    pallas_call x1, Pallas kernels, owned(): pl.pallas_call(functools.partial(owned_kernel, plan), out_shape=[jax.Shap...  6.31 us
  transfers between devices with their start and end apart: 31, of which 19 were waited for; matrix products, arithmetic and copies ran while one was open for 1% of the time, Pallas kernels for 4%

profile of v15, /device:TPU:0, one launch (start us, length us, event | category | flops | bytes accessed | tf_op | source)
XLA Modules:
  0.0 170.3 jit_solution(11460436324606868877)
XLA Ops:
  0.7 0.6 pad_add_fusion.place_ref
  1.3 22.2 %place_gradients.1 = (f32[2192,128]{1,0:T(8,128)}, f32[2192,128]{1,0:T(8,128)}, f32[2192,128]{1,0:T(8,128)}, f32[2192,128]{1,0:T(8,128)}, f32[2192,128]{1,0:T(8,...) custom-call(s32[3]{0:T(128)} %pad_add_fusion.place_ref, ...), custom_call_target="tpu_custom_call" | custom-call | tf_op jit(solution)/shard_map/place_gradients/pallas_call | solution.py:292
  23.5 0.5 collective-permute-start
  24.0 2.6 %collective-permute-done = f32[2192,128]{1,0:T(8,128)S(1)} collective-permute-done((f32[2192,128]{1,0:T(8,128)}, f32[2192,128]{1,0:T(8,128)S(1)}, u32[]{:S(2)}, u32[]{:S(2)}) %collective-permute-start) | collective-permute-done | bytes 1122336 | tf_op jit(solution)/shard_map/ppermute | solution.py:74
  26.7 1.1 slice_add_fusion.7
  27.8 0.4 collective-permute-start.5
  28.2 0.1 collective-permute-start.9
  28.4 2.9 %collective-permute-start.3 = (f32[1096,128]{1,0:T(8,128)S(1)}, f32[1096,128]{1,0:T(8,128)S(1)}, u32[]{:S(2)}, u32[]{:S(2)}) collective-permute-start(f32[1096,128]{1,0:T(8,128)S(1)} %slice_add_fusion.7), channel_id=1, source_target_pairs={{0,4},{2,6},{4,0},{6,2},{8,12},{10,14},{12,8},{14,10},{16,20},{18,... | collective-permute-start | bytes 1683464 | tf_op jit(solution)/shard_map/ppermute | solution.py:74
  31.2 6.3 %owned_weights.1 = (f32[1088,128]{1,0:T(8,128)}, s32[1152,128]{1,0:T(8,128)}) custom-call(s32[3]{0:T(128)} %pad_add_fusion.place_ref, s32[136,128]{1,0:T(8,128)} %bitcast.16, f32[17408,128]{1,0:T(8,128)} %weights_ref.3), custom_call_target="tpu_custom_call" | custom-call | bytes 20971520 | tf_op jit(solution)/shard_map/owned_weights/pallas_call | solution.py:370
  37.6 0.1 collective-permute-start.1
  37.7 0.1 slice_add_fusion.2
  37.7 0.2 collective-permute-start.6
  37.9 6.8 %collective-permute-done.3 = f32[1096,128]{1,0:T(8,128)S(1)} collective-permute-done((f32[1096,128]{1,0:T(8,128)S(1)}, f32[1096,128]{1,0:T(8,128)S(1)}, u32[]{:S(2)}, u32[]{:S(2)}) %collective-permute-start.3) | collective-permute-done | bytes 561184 | tf_op jit(solution)/shard_map/ppermute | solution.py:74
  44.7 0.1 fusion.2
  44.8 4.1 %collective-permute-start.4 = (f32[1096,128]{1,0:T(8,128)S(1)}, f32[1096,128]{1,0:T(8,128)S(1)}, u32[]{:S(2)}, u32[]{:S(2)}) collective-permute-start(f32[1096,128]{1,0:T(8,128)S(1)} %fusion.2), channel_id=1, source_target_pairs={{0,8},{2,10},{4,12},{6,14},{24,16},{26,18},{28,20},{30,22},{1,9},{... | collective-permute-start | bytes 1683464 | tf_op jit(solution)/shard_map/ppermute | solution.py:74
  48.9 0.1 slice_add_fusion
  49.0 1.6 collective-permute-start.10
  50.5 6.2 %collective-permute-done.6 = f32[1096,128]{1,0:T(8,128)S(1)} collective-permute-done((f32[1096,128]{1,0:T(8,128)S(1)}, f32[1096,128]{1,0:T(8,128)S(1)}, u32[]{:S(2)}, u32[]{:S(2)}) %collective-permute-start.6) | collective-permute-done | bytes 561184 | tf_op jit(solution)/shard_map/ppermute | solution.py:74
  56.7 0.1 fusion.1
  56.9 2.6 %collective-permute-done.4 = f32[1096,128]{1,0:T(8,128)S(1)} collective-permute-done((f32[1096,128]{1,0:T(8,128)S(1)}, f32[1096,128]{1,0:T(8,128)S(1)}, u32[]{:S(2)}, u32[]{:S(2)}) %collective-permute-start.4) | collective-permute-done | bytes 561184 | tf_op jit(solution)/shard_map/ppermute | solution.py:74
  59.5 4.4 %collective-permute-start.8 = (f32[1096,128]{1,0:T(8,128)S(1)}, f32[1096,128]{1,0:T(8,128)S(1)}, u32[]{:S(2)}, u32[]{:S(2)}) collective-permute-start(f32[1096,128]{1,0:T(8,128)S(1)} %fusion.1), channel_id=1, source_target_pairs={{0,8},{2,10},{4,12},{6,14},{24,16},{26,18},{28,20},{30,22},{1,9},{... | collective-permute-start | bytes 1683464 | tf_op jit(solution)/shard_map/ppermute | solution.py:74
  64.0 0.7 collective-permute-start.7
  64.7 0.1 slice_add_fusion.5
  64.9 1.6 collective-permute-start.2
  66.4 2.4 %collective-permute-done.10 = f32[1096,128]{1,0:T(8,128)S(1)} collective-permute-done((f32[1096,128]{1,0:T(8,128)S(1)}, f32[1096,128]{1,0:T(8,128)S(1)}, u32[]{:S(2)}, u32[]{:S(2)}) %collective-permute-start.10) | collective-permute-done | bytes 561184 | tf_op jit(solution)/shard_map/ppermute | solution.py:74
  68.8 0.1 fusion
  68.9 4.7 %collective-permute-done.8 = f32[1096,128]{1,0:T(8,128)S(1)} collective-permute-done((f32[1096,128]{1,0:T(8,128)S(1)}, f32[1096,128]{1,0:T(8,128)S(1)}, u32[]{:S(2)}, u32[]{:S(2)}) %collective-permute-start.8) | collective-permute-done | bytes 561184 | tf_op jit(solution)/shard_map/ppermute | solution.py:74
  73.7 0.1 add.80
  73.8 3.9 %collective-permute-start.11 = (f32[1096,128]{1,0:T(8,128)S(1)}, f32[1096,128]{1,0:T(8,128)S(1)}, u32[]{:S(2)}, u32[]{:S(2)}) collective-permute-start(f32[1096,128]{1,0:T(8,128)S(1)} %add.80), channel_id=1, source_target_pairs={{0,8},{2,10},{4,12},{6,14},{8,0},{10,2},{12,4},{14,6},{16,24},{18,... | collective-permute-start | bytes 1683464 | tf_op jit(solution)/shard_map/ppermute | solution.py:74
  77.7 0.7 collective-permute-start.12
  78.4 1.9 %collective-permute-done.2.refs_1_ = f32[1096,128]{1,0:T(8,128)S(1)} collective-permute-done((f32[1096,128]{1,0:T(8,128)S(1)}, f32[1096,128]{1,0:T(8,128)S(1)}, u32[]{:S(2)}, u32[]{:S(2)}) %collective-permute-start.2) | collective-permute-done | bytes 561184 | tf_op jit(solution)/shard_map/ppermute | solution.py:74
  80.3 6.9 %collective-permute-done.11.refs_2_ = f32[1096,128]{1,0:T(8,128)S(1)} collective-permute-done((f32[1096,128]{1,0:T(8,128)S(1)}, f32[1096,128]{1,0:T(8,128)S(1)}, u32[]{:S(2)}, u32[]{:S(2)}) %collective-permute-start.11) | collective-permute-done | bytes 561184 | tf_op jit(solution)/shard_map/ppermute | solution.py:74
  87.3 2.0 %moments.1 = (f32[1088,128]{1,0:T(8,128)}, f32[1088,128]{1,0:T(8,128)}, f32[1096,128]{1,0:T(8,128)S(1)}) custom-call(f32[1096,128]{1,0:T(8,128)S(1)} %get-tuple-element.88.refs_0_, f32[1096,128]{1,0:T(8,128)S(1)} %collective-permute-done.2.refs_1_, f32[1096,128]{1,0:T(8,128)S(1)} %collective-permute-done.11.refs_2_, ...), custom_call_target="tpu_custom_call" | custom-call | tf_op jit(solution)/shard_map/moments/pallas_call | solution.py:424
  89.3 4.0 %collective-permute-start.14 = (f32[1096,128]{1,0:T(8,128)S(1)}, f32[1096,128]{1,0:T(8,128)S(1)}, u32[]{:S(2)}, u32[]{:S(2)}) collective-permute-start(f32[1096,128]{1,0:T(8,128)S(1)} %get-tuple-element.68), channel_id=1, source_target_pairs={{0,8},{2,10},{4,12},{6,14},{8,0},{10,2},{12,4},{14,6},{16,24},{18,... | collective-permute-start | bytes 1683464 | tf_op jit(solution)/shard_map/ppermute | solution.py:74
  93.2 1.5 collective-permute-start.15
  94.7 0.7 collective-permute-start.13
  95.4 6.4 %collective-permute-done.14 = f32[1096,128]{1,0:T(8,128)S(1)} collective-permute-done((f32[1096,128]{1,0:T(8,128)S(1)}, f32[1096,128]{1,0:T(8,128)S(1)}, u32[]{:S(2)}, u32[]{:S(2)}) %collective-permute-start.14) | collective-permute-done | bytes 561184 | tf_op jit(solution)/shard_map/ppermute | solution.py:74
  101.9 1.5 collective-permute-start.20
  103.4 0.7 collective-permute-start.16
  104.1 0.1 pad_maximum_fusion.refs_0_.refs_1_
  104.1 2.9 %collective-permute-done.15 = f32[1096,128]{1,0:T(8,128)S(1)} collective-permute-done((f32[1096,128]{1,0:T(8,128)S(1)}, f32[1096,128]{1,0:T(8,128)S(1)}, u32[]{:S(2)}, u32[]{:S(2)}) %collective-permute-start.15) | collective-permute-done | bytes 561184 | tf_op jit(solution)/shard_map/ppermute | solution.py:74
  107.0 1.3 collective-permute-start.19
  108.3 1.3 collective-permute-start.17
  109.6 6.4 %collective-permute-done.20 = f32[1096,128]{1,0:T(8,128)S(1)} collective-permute-done((f32[1096,128]{1,0:T(8,128)S(1)}, f32[1096,128]{1,0:T(8,128)S(1)}, u32[]{:S(2)}, u32[]{:S(2)}) %collective-permute-start.20) | collective-permute-done | bytes 561184 | tf_op jit(solution)/shard_map/ppermute | solution.py:74
  116.0 3.7 %collective-permute-done.19 = f32[1096,128]{1,0:T(8,128)S(1)} collective-permute-done((f32[1096,128]{1,0:T(8,128)S(1)}, f32[1096,128]{1,0:T(8,128)S(1)}, u32[]{:S(2)}, u32[]{:S(2)}) %collective-permute-start.19) | collective-permute-done | bytes 561184 | tf_op jit(solution)/shard_map/ppermute | solution.py:74
  119.7 0.1 add.83.refs_2_
  119.8 0.1 pad_maximum_fusion.1.refs_1_
  119.9 2.5 %collective-permute-start.22 = (f32[1096,128]{1,0:T(8,128)S(1)}, f32[1096,128]{1,0:T(8,128)S(1)}, u32[]{:S(2)}, u32[]{:S(2)}) collective-permute-start(f32[1096,128]{1,0:T(8,128)S(1)} %add.83.refs_2_), channel_id=1, source_target_pairs={{0,4},{2,6},{4,0},{6,2},{8,12},{10,14},{12,8},{14,10},{16,20},{18,... | collective-permute-start | bytes 1683464 | tf_op jit(solution)/shard_map/ppermute | solution.py:74
  122.4 8.1 %collective-permute-done.17 = f32[1096,128]{1,0:T(8,128)S(1)} collective-permute-done((f32[1096,128]{1,0:T(8,128)S(1)}, f32[1096,128]{1,0:T(8,128)S(1)}, u32[]{:S(2)}, u32[]{:S(2)}) %collective-permute-start.17) | collective-permute-done | bytes 561184 | tf_op jit(solution)/shard_map/ppermute | solution.py:74
  130.5 0.1 add.82.refs_3_.refs_4_
  130.6 0.6 sums.1
  131.2 1.6 collective-permute-start.21
  132.7 0.5 collective-permute-start.25
  133.3 0.2 collective-permute-start.18
  133.5 1.3 collective-permute-done.21
  134.9 0.5 collective-permute-start.23
  135.4 2.5 %collective-permute-done.23 = f32[8,128]{1,0:T(8,128)S(1)} collective-permute-done((f32[8,128]{1,0:T(8,128)S(1)}, f32[8,128]{1,0:T(8,128)S(1)}, u32[]{:S(2)}, u32[]{:S(2)}) %collective-permute-start.23) | collective-permute-done | bytes 4128 | tf_op jit(solution)/shard_map/ppermute | solution.py:74
  137.9 1.5 collective-permute-start.24
  139.4 2.1 %collective-permute-done.24 = f32[8,128]{1,0:T(8,128)S(1)} collective-permute-done((f32[8,128]{1,0:T(8,128)S(1)}, f32[8,128]{1,0:T(8,128)S(1)}, u32[]{:S(2)}, u32[]{:S(2)}) %collective-permute-start.24) | collective-permute-done | bytes 4128 | tf_op jit(solution)/shard_map/ppermute | solution.py:160
  141.5 6.3 %collective-permute-done.25.refs_5_ = f32[1096,128]{1,0:T(8,128)S(1)} collective-permute-done((f32[1096,128]{1,0:T(8,128)S(1)}, f32[1096,128]{1,0:T(8,128)S(1)}, u32[]{:S(2)}, u32[]{:S(2)}) %collective-permute-start.25) | collective-permute-done | bytes 561184 | tf_op jit(solution)/shard_map/ppermute | solution.py:74
  147.9 0.5 collective-permute-start.30
  148.4 1.4 collective-permute-done.29.refs_9_
  149.8 0.8 collective-permute-done.30.refs_11_
  150.7 19.6 %new_weights.1 = (f32[17408,128]{1,0:T(8,128)}, f32[3,2,1024]{2,1,0:T(2,128)}, f32[7]{0:T(128)}) custom-call(s32[3]{0:T(128)S(1)} %copy-done.6, s32[136,128]{1,0:T(8,128)S(1)} %copy-done.4, f32[8,128]{1,0:T(8,128)S(1)} %add.86.total_ref, f32[3,2,1024]{2,1,0:T(2,128)S(1)} %copy-done.5, f32[17408,128]{1,0:T(8,128)S(1)} %bitcast.11, ...), custom_call_target="tpu_custom_call" | custom-call | tf_op jit(solution)/shard_map/new_weights/pallas_call | solution.py:502
  (50 shorter events, 0.2 us)
Async XLA Ops:
  23.5 3.1 %collective-permute-start = (f32[2192,128]{1,0:T(8,128)}, f32[2192,128]{1,0:T(8,128)S(1)}, u32[]{:S(2)}, u32[]{:S(2)}) collective-permute-start(f32[2192,128]{1,0:T(8,128)} %get-tuple-element.49), channel_id=1, source_target_pairs={{0,2},{2,0},{4,6},{6,4},{8,10},{10,8},{12,14},{14,12},{16,18},{18,... | collective-permute-start | bytes 3366920 | tf_op jit(solution)/shard_map/ppermute | solution.py:74
  27.8 9.9 %copy-start.9 = (f32[2192,128]{1,0:T(8,128)S(1)}, f32[2192,128]{1,0:T(8,128)}, u32[]{:S(2)}) copy-start(f32[2192,128]{1,0:T(8,128)} %get-tuple-element.55) | copy-start | bytes 3366916
  27.8 9.8 %collective-permute-start.5 = (f32[2192,128]{1,0:T(8,128)}, f32[2192,128]{1,0:T(8,128)S(1)}, u32[]{:S(2)}, u32[]{:S(2)}) collective-permute-start(f32[2192,128]{1,0:T(8,128)} %get-tuple-element.56), channel_id=1, source_target_pairs={{0,2},{2,0},{4,6},{6,4},{8,10},{10,8},{12,14},{14,12},{16,18},{18,... | collective-permute-start | bytes 3366920 | tf_op jit(solution)/shard_map/ppermute | solution.py:74
  28.2 20.7 %collective-permute-start.9 = (f32[2192,128]{1,0:T(8,128)}, f32[2192,128]{1,0:T(8,128)S(1)}, u32[]{:S(2)}, u32[]{:S(2)}) collective-permute-start(f32[2192,128]{1,0:T(8,128)} %get-tuple-element.62), channel_id=1, source_target_pairs={{0,2},{2,0},{4,6},{6,4},{8,10},{10,8},{12,14},{14,12},{16,18},{18,... | collective-permute-start | bytes 3366920 | tf_op jit(solution)/shard_map/ppermute | solution.py:74
  28.4 16.4 %collective-permute-start.3 = (f32[1096,128]{1,0:T(8,128)S(1)}, f32[1096,128]{1,0:T(8,128)S(1)}, u32[]{:S(2)}, u32[]{:S(2)}) collective-permute-start(f32[1096,128]{1,0:T(8,128)S(1)} %slice_add_fusion.7), channel_id=1, source_target_pairs={{0,4},{2,6},{4,0},{6,2},{8,12},{10,14},{12,8},{14,10},{16,20},{18,... | collective-permute-start | bytes 1683464 | tf_op jit(solution)/shard_map/ppermute | solution.py:74
  37.5 7.2 %copy-start.10 = (f32[2192,128]{1,0:T(8,128)S(1)}, f32[2192,128]{1,0:T(8,128)}, u32[]{:S(2)}) copy-start(f32[2192,128]{1,0:T(8,128)} %get-tuple-element.48) | copy-start | bytes 3366916
  37.6 27.1 %collective-permute-start.1 = (f32[2192,128]{1,0:T(8,128)}, f32[2192,128]{1,0:T(8,128)S(1)}, u32[]{:S(2)}, u32[]{:S(2)}) collective-permute-start(f32[2192,128]{1,0:T(8,128)} %get-tuple-element.53), channel_id=1, source_target_pairs={{0,2},{2,0},{4,6},{6,4},{8,10},{10,8},{12,14},{14,12},{16,18},{18,... | collective-permute-start | bytes 3366920 | tf_op jit(solution)/shard_map/ppermute | solution.py:74
  37.7 11.2 %copy-start.7 = (f32[2192,128]{1,0:T(8,128)S(1)}, f32[2192,128]{1,0:T(8,128)}, u32[]{:S(2)}) copy-start(f32[2192,128]{1,0:T(8,128)} %get-tuple-element.61) | copy-start | bytes 3366916
  37.7 19.0 %collective-permute-start.6 = (f32[1096,128]{1,0:T(8,128)S(1)}, f32[1096,128]{1,0:T(8,128)S(1)}, u32[]{:S(2)}, u32[]{:S(2)}) collective-permute-start(f32[1096,128]{1,0:T(8,128)S(1)} %slice_add_fusion.2), channel_id=1, source_target_pairs={{0,4},{2,6},{4,0},{6,2},{8,12},{10,14},{12,8},{14,10},{16,20},{18,... | collective-permute-start | bytes 1683464 | tf_op jit(solution)/shard_map/ppermute | solution.py:74
  44.8 14.7 %collective-permute-start.4 = (f32[1096,128]{1,0:T(8,128)S(1)}, f32[1096,128]{1,0:T(8,128)S(1)}, u32[]{:S(2)}, u32[]{:S(2)}) collective-permute-start(f32[1096,128]{1,0:T(8,128)S(1)} %fusion.2), channel_id=1, source_target_pairs={{0,8},{2,10},{4,12},{6,14},{24,16},{26,18},{28,20},{30,22},{1,9},{... | collective-permute-start | bytes 1683464 | tf_op jit(solution)/shard_map/ppermute | solution.py:74
  49.0 19.8 %collective-permute-start.10 = (f32[1096,128]{1,0:T(8,128)S(1)}, f32[1096,128]{1,0:T(8,128)S(1)}, u32[]{:S(2)}, u32[]{:S(2)}) collective-permute-start(f32[1096,128]{1,0:T(8,128)S(1)} %slice_add_fusion), channel_id=1, source_target_pairs={{0,4},{2,6},{4,0},{6,2},{8,12},{10,14},{12,8},{14,10},{16,20},{18,... | collective-permute-start | bytes 1683464 | tf_op jit(solution)/shard_map/ppermute | solution.py:74
  56.9 7.8 %copy-start.8 = (f32[2192,128]{1,0:T(8,128)S(1)}, f32[2192,128]{1,0:T(8,128)}, u32[]{:S(2)}) copy-start(f32[2192,128]{1,0:T(8,128)} %get-tuple-element.47) | copy-start | bytes 3366916
  59.5 14.1 %collective-permute-start.8 = (f32[1096,128]{1,0:T(8,128)S(1)}, f32[1096,128]{1,0:T(8,128)S(1)}, u32[]{:S(2)}, u32[]{:S(2)}) collective-permute-start(f32[1096,128]{1,0:T(8,128)S(1)} %fusion.1), channel_id=1, source_target_pairs={{0,8},{2,10},{4,12},{6,14},{24,16},{26,18},{28,20},{30,22},{1,9},{... | collective-permute-start | bytes 1683464 | tf_op jit(solution)/shard_map/ppermute | solution.py:74
  64.0 4.9 %collective-permute-start.7 = (f32[1096,128]{1,0:T(8,128)S(1)}, f32[1096,128]{1,0:T(8,128)S(1)}, u32[]{:S(2)}, u32[]{:S(2)}) collective-permute-start(f32[1096,128]{1,0:T(8,128)S(1)} %add.76), channel_id=1, source_target_pairs={{8,16},{10,18},{12,20},{14,22},{16,8},{18,10},{20,12},{22,14},{9,1... | collective-permute-start | bytes 1683464 | tf_op jit(solution)/shard_map/ppermute | solution.py:74
  64.7 85.9 %slice-start = ((s8[8912896]{0:T(1024)(128)(4,1)}), s8[4194304]{0:T(1024)(128)(4,1)S(1)}, s32[]{:S(2)}) async-start(s8[8912896]{0:T(1024)(128)(4,1)} %bitcast.10), calls=%async_computation | async-start | bytes 8388608
  64.9 15.4 %collective-permute-start.2 = (f32[1096,128]{1,0:T(8,128)S(1)}, f32[1096,128]{1,0:T(8,128)S(1)}, u32[]{:S(2)}, u32[]{:S(2)}) collective-permute-start(f32[1096,128]{1,0:T(8,128)S(1)} %get-tuple-element.87), channel_id=1, source_target_pairs={{0,4},{2,6},{4,0},{6,2},{8,12},{10,14},{12,8},{14,10},{16,20},{18,... | collective-permute-start | bytes 1683464 | tf_op jit(solution)/shard_map/ppermute | solution.py:74
  73.6 13.7 %copy-start = (s32[1152,128]{1,0:T(8,128)S(1)}, s32[1152,128]{1,0:T(8,128)}, u32[]{:S(2)}) copy-start(s32[1152,128]{1,0:T(8,128)} %get-tuple-element.67.refs_7_) | copy-start | bytes 1769476
  73.6 13.7 %copy-start.1 = (f32[1,1088,128]{2,1,0:T(8,128)S(1)}, f32[1,1088,128]{2,1,0:T(8,128)}, u32[]{:S(2)}) copy-start(f32[1,1088,128]{2,1,0:T(8,128)} %param.9) | copy-start | bytes 1671172
  73.6 13.7 %copy-start.2 = (f32[1,1088,128]{2,1,0:T(8,128)S(1)}, f32[1,1088,128]{2,1,0:T(8,128)}, u32[]{:S(2)}) copy-start(f32[1,1088,128]{2,1,0:T(8,128)} %param.10) | copy-start | bytes 1671172
  73.6 13.7 %copy-start.3 = (f32[1088,128]{1,0:T(8,128)S(1)}, f32[1088,128]{1,0:T(8,128)}, u32[]{:S(2)}) copy-start(f32[1088,128]{1,0:T(8,128)} %get-tuple-element.66.refs_6_) | copy-start | bytes 1671172
  73.7 77.0 %slice-start.1 = ((s8[8912896]{0:T(1024)(128)(4,1)}), s8[4194304]{0:T(1024)(128)(4,1)S(1)}, s32[]{:S(2)}) async-start(s8[8912896]{0:T(1024)(128)(4,1)} %bitcast.10), calls=%async_computation.1 | async-start | bytes 8388608
  73.8 13.5 %collective-permute-start.11 = (f32[1096,128]{1,0:T(8,128)S(1)}, f32[1096,128]{1,0:T(8,128)S(1)}, u32[]{:S(2)}, u32[]{:S(2)}) collective-permute-start(f32[1096,128]{1,0:T(8,128)S(1)} %add.80), channel_id=1, source_target_pairs={{0,8},{2,10},{4,12},{6,14},{8,0},{10,2},{12,4},{14,6},{16,24},{18,... | collective-permute-start | bytes 1683464 | tf_op jit(solution)/shard_map/ppermute | solution.py:74
  77.7 9.5 %collective-permute-start.12 = (f32[1096,128]{1,0:T(8,128)S(1)}, f32[1096,128]{1,0:T(8,128)S(1)}, u32[]{:S(2)}, u32[]{:S(2)}) collective-permute-start(f32[1096,128]{1,0:T(8,128)S(1)} %add.81), channel_id=1, source_target_pairs={{8,16},{10,18},{12,20},{14,22},{16,8},{18,10},{20,12},{22,14},{9,1... | collective-permute-start | bytes 1683464 | tf_op jit(solution)/shard_map/ppermute | solution.py:74
  89.3 12.6 %collective-permute-start.14 = (f32[1096,128]{1,0:T(8,128)S(1)}, f32[1096,128]{1,0:T(8,128)S(1)}, u32[]{:S(2)}, u32[]{:S(2)}) collective-permute-start(f32[1096,128]{1,0:T(8,128)S(1)} %get-tuple-element.68), channel_id=1, source_target_pairs={{0,8},{2,10},{4,12},{6,14},{8,0},{10,2},{12,4},{14,6},{16,24},{18,... | collective-permute-start | bytes 1683464 | tf_op jit(solution)/shard_map/ppermute | solution.py:74
  93.2 13.8 %collective-permute-start.15 = (f32[1096,128]{1,0:T(8,128)S(1)}, f32[1096,128]{1,0:T(8,128)S(1)}, u32[]{:S(2)}, u32[]{:S(2)}) collective-permute-start(f32[1096,128]{1,0:T(8,128)S(1)} %get-tuple-element.68), channel_id=1, source_target_pairs={{0,4},{2,6},{4,0},{6,2},{8,12},{10,14},{12,8},{14,10},{16,20},{18,... | collective-permute-start | bytes 1683464 | tf_op jit(solution)/shard_map/ppermute | solution.py:74
  94.7 12.3 %collective-permute-start.13 = (f32[1096,128]{1,0:T(8,128)S(1)}, f32[1096,128]{1,0:T(8,128)S(1)}, u32[]{:S(2)}, u32[]{:S(2)}) collective-permute-start(f32[1096,128]{1,0:T(8,128)S(1)} %get-tuple-element.68), channel_id=1, source_target_pairs={{8,16},{10,18},{12,20},{14,22},{16,8},{18,10},{20,12},{22,14},{9,1... | collective-permute-start | bytes 1683464 | tf_op jit(solution)/shard_map/ppermute | solution.py:74
  101.9 14.2 %collective-permute-start.20 = (f32[1096,128]{1,0:T(8,128)S(1)}, f32[1096,128]{1,0:T(8,128)S(1)}, u32[]{:S(2)}, u32[]{:S(2)}) collective-permute-start(f32[1096,128]{1,0:T(8,128)S(1)} %collective-permute-done.14), channel_id=1, source_target_pairs={{0,4},{2,6},{4,0},{6,2},{8,12},{10,14},{12,8},{14,10},{16,20},{18,... | collective-permute-start | bytes 1683464 | tf_op jit(solution)/shard_map/ppermute | solution.py:74
  103.4 5.0 %collective-permute-start.16 = (f32[1096,128]{1,0:T(8,128)S(1)}, f32[1096,128]{1,0:T(8,128)S(1)}, u32[]{:S(2)}, u32[]{:S(2)}) collective-permute-start(f32[1096,128]{1,0:T(8,128)S(1)} %collective-permute-done.14), channel_id=1, source_target_pairs={{8,16},{10,18},{12,20},{14,22},{16,8},{18,10},{20,12},{22,14},{9,1... | collective-permute-start | bytes 1683464 | tf_op jit(solution)/shard_map/ppermute | solution.py:74
  104.1 46.5 %slice-start.2 = ((s8[8912896]{0:T(1024)(128)(4,1)}), s8[524288]{0:T(1024)(128)(4,1)S(1)}, s32[]{:S(2)}) async-start(s8[8912896]{0:T(1024)(128)(4,1)} %bitcast.10), calls=%async_computation.2 | async-start | bytes 1048576
  107.0 12.7 %collective-permute-start.19 = (f32[1096,128]{1,0:T(8,128)S(1)}, f32[1096,128]{1,0:T(8,128)S(1)}, u32[]{:S(2)}, u32[]{:S(2)}) collective-permute-start(f32[1096,128]{1,0:T(8,128)S(1)} %collective-permute-done.13), channel_id=1, source_target_pairs={{8,0},{10,2},{12,4},{14,6},{16,24},{18,26},{20,28},{22,30},{9,1},{... | collective-permute-start | bytes 1683464 | tf_op jit(solution)/shard_map/ppermute | solution.py:74
  108.3 22.2 %collective-permute-start.17 = (f32[1096,128]{1,0:T(8,128)S(1)}, f32[1096,128]{1,0:T(8,128)S(1)}, u32[]{:S(2)}, u32[]{:S(2)}) collective-permute-start(f32[1096,128]{1,0:T(8,128)S(1)} %collective-permute-done.16), channel_id=1, source_target_pairs={{8,0},{10,2},{12,4},{14,6},{16,24},{18,26},{20,28},{22,30},{9,1},{... | collective-permute-start | bytes 1683464 | tf_op jit(solution)/shard_map/ppermute | solution.py:74
  119.9 10.7 %copy-start.6 = (s32[3]{0:T(128)S(1)}, s32[3]{0:T(128)}, u32[]{:S(2)}) copy-start(s32[3]{0:T(128)} %pad_add_fusion.place_ref) | copy-start | bytes 40
  119.9 15.0 %collective-permute-start.22 = (f32[1096,128]{1,0:T(8,128)S(1)}, f32[1096,128]{1,0:T(8,128)S(1)}, u32[]{:S(2)}, u32[]{:S(2)}) collective-permute-start(f32[1096,128]{1,0:T(8,128)S(1)} %add.83.refs_2_), channel_id=1, source_target_pairs={{0,4},{2,6},{4,0},{6,2},{8,12},{10,14},{12,8},{14,10},{16,20},{18,... | collective-permute-start | bytes 1683464 | tf_op jit(solution)/shard_map/ppermute | solution.py:74
  130.6 20.0 %copy-start.4 = (s32[136,128]{1,0:T(8,128)S(1)}, s32[136,128]{1,0:T(8,128)}, u32[]{:S(2)}) copy-start(s32[136,128]{1,0:T(8,128)} %get-tuple-element.46.position_ref) | copy-start | bytes 208900
  130.6 20.0 %copy-start.5 = (f32[3,2,1024]{2,1,0:T(2,128)S(1)}, f32[3,2,1024]{2,1,0:T(2,128)}, u32[]{:S(2)}) copy-start(f32[3,2,1024]{2,1,0:T(2,128)} %norm_ref.1) | copy-start | bytes 73732
  131.2 3.7 %collective-permute-start.21 = (f32[8,128]{1,0:T(8,128)S(1)}, f32[8,128]{1,0:T(8,128)S(1)}, u32[]{:S(2)}, u32[]{:S(2)}) collective-permute-start(f32[8,128]{1,0:T(8,128)S(1)} %sums.1), channel_id=1, source_target_pairs={{0,4},{2,6},{4,0},{6,2},{8,12},{10,14},{12,8},{14,10},{16,20},{18,... | collective-permute-start | bytes 12296 | tf_op jit(solution)/shard_map/ppermute | solution.py:74
  132.7 15.6 %collective-permute-start.26 = (f32[2192,128]{1,0:T(8,128)S(1)}, f32[2192,128]{1,0:T(8,128)S(1)}, u32[]{:S(2)}, u32[]{:S(2)}) collective-permute-start(f32[2192,128]{1,0:T(8,128)S(1)} %pad_maximum_fusion.refs_0_.refs_1_), channel_id=1, source_target_pairs={{0,2},{2,0},{4,6},{6,4},{8,10},{10,8},{12,14},{14,12},{16,18},{18,... | collective-permute-start | bytes 3366920 | tf_op jit(solution)/shard_map/ppermute | solution.py:74
  132.7 15.1 %collective-permute-start.25 = (f32[1096,128]{1,0:T(8,128)S(1)}, f32[1096,128]{1,0:T(8,128)S(1)}, u32[]{:S(2)}, u32[]{:S(2)}) collective-permute-start(f32[1096,128]{1,0:T(8,128)S(1)} %add.82.refs_3_.refs_4_), channel_id=1, source_target_pairs={{0,4},{2,6},{4,0},{6,2},{8,12},{10,14},{12,8},{14,10},{16,20},{18,... | collective-permute-start | bytes 1683464 | tf_op jit(solution)/shard_map/ppermute | solution.py:74
  133.3 14.6 %collective-permute-start.18 = (f32[1096,128]{1,0:T(8,128)S(1)}, f32[1096,128]{1,0:T(8,128)S(1)}, u32[]{:S(2)}, u32[]{:S(2)}) collective-permute-start(f32[1096,128]{1,0:T(8,128)S(1)} %add.82.refs_3_.refs_4_), channel_id=1, source_target_pairs={{0,2},{2,0},{4,6},{6,4},{8,10},{10,8},{12,14},{14,12},{16,18},{18,... | collective-permute-start | bytes 1683464 | tf_op jit(solution)/shard_map/ppermute | solution.py:74
  134.9 13.5 %collective-permute-start.27 = (f32[2192,128]{1,0:T(8,128)S(1)}, f32[2192,128]{1,0:T(8,128)S(1)}, u32[]{:S(2)}, u32[]{:S(2)}) collective-permute-start(f32[2192,128]{1,0:T(8,128)S(1)} %pad_maximum_fusion.1.refs_1_), channel_id=1, source_target_pairs={{0,2},{2,0},{4,6},{6,4},{8,10},{10,8},{12,14},{14,12},{16,18},{18,... | collective-permute-start | bytes 3366920 | tf_op jit(solution)/shard_map/ppermute | solution.py:74
  134.9 3.0 %collective-permute-start.23 = (f32[8,128]{1,0:T(8,128)S(1)}, f32[8,128]{1,0:T(8,128)S(1)}, u32[]{:S(2)}, u32[]{:S(2)}) collective-permute-start(f32[8,128]{1,0:T(8,128)S(1)} %add.84), channel_id=1, source_target_pairs={{0,2},{2,0},{4,6},{6,4},{8,10},{10,8},{12,14},{14,12},{16,18},{18,... | collective-permute-start | bytes 12296 | tf_op jit(solution)/shard_map/ppermute | solution.py:74
  137.9 3.6 %collective-permute-start.24 = (f32[8,128]{1,0:T(8,128)S(1)}, f32[8,128]{1,0:T(8,128)S(1)}, u32[]{:S(2)}, u32[]{:S(2)}) collective-permute-start(f32[8,128]{1,0:T(8,128)S(1)} %add.85), channel_id=1, source_target_pairs={{0,1},{1,0},{2,3},{3,2},{4,5},{5,4},{6,7},{7,6},{8,9},{9,8},{10,11... | collective-permute-start | bytes 12296 | tf_op jit(solution)/shard_map/ppermute | solution.py:160
  141.5 6.9 %collective-permute-start.28 = (f32[1096,128]{1,0:T(8,128)S(1)}, f32[1096,128]{1,0:T(8,128)S(1)}, u32[]{:S(2)}, u32[]{:S(2)}) collective-permute-start(f32[1096,128]{1,0:T(8,128)S(1)} %add.83.refs_2_), channel_id=1, source_target_pairs={{0,2},{2,0},{4,6},{6,4},{8,10},{10,8},{12,14},{14,12},{16,18},{18,... | collective-permute-start | bytes 1683464 | tf_op jit(solution)/shard_map/ppermute | solution.py:74
  147.9 2.0 %collective-permute-start.29 = (f32[1096,128]{1,0:T(8,128)S(1)}, f32[1096,128]{1,0:T(8,128)S(1)}, u32[]{:S(2)}, u32[]{:S(2)}) collective-permute-start(f32[1096,128]{1,0:T(8,128)S(1)} %collective-permute-done.22.refs_3_), channel_id=1, source_target_pairs={{0,2},{2,0},{4,6},{6,4},{8,10},{10,8},{12,14},{14,12},{16,18},{18,... | collective-permute-start | bytes 1683464 | tf_op jit(solution)/shard_map/ppermute | solution.py:74
  147.9 2.8 %collective-permute-start.30 = (f32[1096,128]{1,0:T(8,128)S(1)}, f32[1096,128]{1,0:T(8,128)S(1)}, u32[]{:S(2)}, u32[]{:S(2)}) collective-permute-start(f32[1096,128]{1,0:T(8,128)S(1)} %collective-permute-done.25.refs_5_), channel_id=1, source_target_pairs={{0,2},{2,0},{4,6},{6,4},{8,10},{10,8},{12,14},{14,12},{16,18},{18,... | collective-permute-start | bytes 1683464 | tf_op jit(solution)/shard_map/ppermute | solution.py:74

commit v16 on v15

--- a/solution.py
+++ b/solution.py
@@ -24,7 +24,8 @@
 matrices = 5
 MIB = 1 << 20
 TILES = 8
-PHASES = 2
+FETCHES = 4
+EARLY = 0.7
 
 
 def matrix_bounds(narrow):
@@ -62,6 +63,10 @@
     def start(self, far_z, far_x, far_c):
         return (1 - far_c) * self.half + far_z * self.group + far_x * self.block
 
+    def order(self):
+        zs, xs = range(self.nz - 1, -1, -1), range(self.nx - 1, -1, -1)
+        return [(z, x, far_c) for far_c in (1, 0) for z in zs for x in xs]
+
     def send(self, value, axis, pairs):
         every = []
         for z in range(self.nz):
@@ -112,7 +117,8 @@
     in_three = plan.send(near_three, "z", INWARD)
     in_three, near_two, *beside = together(in_three, sum(two[1:], two[0]), *beside)
     one = along_x(1, mine[1])
-    across_two = plan.send(near_two + in_three, "z", MIDDLE)
+    near_two, onward = together(near_two, near_two + in_three)
+    across_two = plan.send(onward, "z", MIDDLE)
     in_two = plan.send(near_two, "z", INWARD)
     across_two, in_two, near_one = together(across_two, in_two, sum(one[1:], one[0]))
     zero = along_x(0, mine[0])
@@ -212,10 +218,16 @@
 
 
 def place_kernel(plan, place_ref, owner_ref, norm_ref, grads_ref, *refs):
-    out_refs, refs = refs[: 2 * plan.nz], refs[2 * plan.nz :]
+    out_refs, refs = refs[: plan.replicas], refs[plan.replicas :]
     position_ref, raw, moved, position, sem_in, sem_position, sem_out = refs
-    fetch = pltpu.make_async_copy(grads_ref, raw, sem_in)
-    fetch.start()
+    lines = plan.blocks // LANE
+    ends = [lines * (i + 1) // FETCHES for i in range(FETCHES)]
+    fetches = []
+    for i, end in enumerate(ends):
+        low = ends[i - 1] * LANE if i else 0
+        rows = pl.ds(low, end * LANE - low)
+        fetches.append(pltpu.make_async_copy(grads_ref.at[rows], raw.at[rows], sem_in.at[i]))
+        fetches[-1].start()
     lists = plan.lists
     owners = owner_ref[...]
     my_z, my_x, my_c = place_ref[0], place_ref[1], place_ref[2]
@@ -255,40 +267,50 @@
     to_scalar = pltpu.make_async_copy(position_ref, position, sem_position)
     to_scalar.start()
     to_scalar.wait()
-    fetch.wait()
-
+
+    def copies(part, low, high):
+        found = []
+        for i, (out, slot) in enumerate(zip(out_refs, plan.order())):
+            source = moved.at[pl.ds(plan.start(*slot) + low, high - low)]
+            found.append(pltpu.make_async_copy(source, out.at[pl.ds(low, high - low)], sem_out.at[part, i]))
+        return found
+
+    cut = int(plan.own * EARLY / 8) * 8
     line_of = lax.broadcasted_iota(jnp.int32, (lists, LANE), 0)
-    cuts = [plan.own * (i + 1) // (8 * PHASES) * 8 for i in range(PHASES - 1)] + [plan.own]
-    begin = jnp.int32(0)
-    copies = []
-    for phase, cut in enumerate(cuts):
-        end = plan.blocks // LANE
-        if phase < PHASES - 1:
-            end = jnp.max(jnp.where(ranks < cut, line_of + 1, 0))
-
-        @pl.loop(begin, end)
+    complete = jnp.max(jnp.where(ranks < cut, line_of + 1, 0))
+    early = copies(0, 0, cut)
+    late = copies(1, cut, plan.block)
+
+    for i, end in enumerate(ends):
+        fetches[i].wait()
+
+        @pl.loop(ends[i - 1] if i else 0, end)
         def _(line):
             for part in range(0, LANE, 16):
                 rows = raw[pl.ds(pl.multiple_of(line * LANE + part, 16), 16), :].astype(jnp.float32)
                 for u in range(16):
                     moved[pl.ds(position[line, part + u], 1), :] = rows[u : u + 1, :]
 
-        begin = end
-        low = cuts[phase - 1] if phase else 0
-        high = cut if phase < PHASES - 1 else plan.block
-        for i, out in enumerate(out_refs):
-            start = (i // plan.nz) * plan.half + (plan.nz - 1 - i % plan.nz) * plan.group
-            for x in range(plan.nx):
-                rows = pl.ds(x * plan.block + low, high - low)
-                source = moved.at[pl.ds(start + x * plan.block + low, high - low)]
-                copies.append(pltpu.make_async_copy(source, out.at[rows], sem_out.at[len(copies)]))
-                copies[-1].start()
-    for copy in copies:
+        if i == FETCHES - 2:
+
+            @pl.when(complete <= end)
+            def _():
+                for copy in early:
+                    copy.start()
+
+    @pl.when(complete > ends[FETCHES - 2])
+    def _():
+        for copy in early:
+            copy.start()
+
+    for copy in late:
+        copy.start()
+    for copy in early + late:
         copy.wait()
 
 
 def place(plan, my_place, owners, norm_grads, grads):
-    shapes = [(plan.group, LANE)] * (2 * plan.nz)
+    shapes = [(plan.block, LANE)] * plan.replicas
     outs = pl.pallas_call(
         functools.partial(place_kernel, plan),
         out_shape=[jax.ShapeDtypeStruct(s, jnp.float32) for s in shapes]
@@ -304,14 +326,14 @@
             pltpu.VMEM((plan.blocks, LANE), jnp.bfloat16),
             pltpu.VMEM((2 * plan.half, LANE), jnp.float32),
             pltpu.SMEM((plan.lists, LANE), jnp.int32),
+            pltpu.SemaphoreType.DMA((FETCHES,)),
             pltpu.SemaphoreType.DMA,
-            pltpu.SemaphoreType.DMA,
-            pltpu.SemaphoreType.DMA((len(shapes) * plan.nx * PHASES,)),
+            pltpu.SemaphoreType.DMA((2, len(shapes))),
         ],
         compiler_params=pltpu.CompilerParams(vmem_limit_bytes=58 * MIB),
         name="place_gradients",
     )(my_place, owners, norm_grads, grads)
-    return list(outs[: plan.nz][::-1]), outs[plan.nz : 2 * plan.nz][::-1], outs[-1]
+    return dict(zip(plan.order(), outs)), outs[-1]
 
 
 def owned_kernel(plan, place_ref, owner_ref, weights_ref, owned_ref, natural_ref, held, listed, order, sem_in, sem_order):
@@ -526,19 +548,19 @@
     my_place = jnp.stack([me // (2 * plan.nx), (me // 2) % plan.nx, me % 2]).astype(jnp.int32)
     owners = jnp.pad(owner_list[0], (0, plan.lists * LANE - plan.blocks), constant_values=-1)
     owners = owners.reshape(plan.lists, LANE)
-    siblings, blocks, position = place(plan, my_place, owners, norm_grads[0], gradients[0])
+    placed, position = place(plan, my_place, owners, norm_grads[0], gradients[0])
     weight_own, natural = owned(plan, my_place, owners, weights)
 
     mine, theirs = [None] * plan.nz, [None] * plan.nz
     for z in reversed(range(plan.nz)):
-        other = plan.swap(siblings[z])
-        both = [
-            blocks[z][x * plan.block : (x + 1) * plan.block] + other[x * plan.block : (x + 1) * plan.block]
-            for x in range(plan.nx)
-        ]
+        both = [None] * plan.nx
+        for x in reversed(range(plan.nx)):
+            both[x] = placed[z, x, 0] + plan.swap(placed[z, x, 1])
+            if (z, x) == (3, plan.nx - 1):
+                later = [slot for slot in plan.order() if slot[2] and slot[:2] != (z, x)]
+                both[x], *values = together(both[x], *(placed[slot] for slot in later))
+                placed.update(zip(later, values))
         mine[z], theirs[z] = both[0], both[1:]
-        if z == 3:
-            theirs[3], siblings[2], siblings[1], siblings[0] = together(theirs[3], *siblings[2::-1])
     if plan.nz == 4:
         parts = reduce(plan, mine, theirs, (weight_own, natural))
         parts, (weight_own, natural) = parts[:-2], parts[-2:]

time: 171 us -> 172 us (level)
  starting transfers between devices: 39.4 us -> 43 us
    ppermute x30 -> x34, starting transfers between devices: 37.9 us -> 41.5 us  [send(): return lax.ppermute(value, 'dp', every)]
    ppermute x30 -> x34, waiting for transfers between devices: 74.1 us -> 72.5 us  [send(): return lax.ppermute(value, 'dp', every)]
  transfers between devices with their start and end apart: 31 -> 35, of which waited for: 19 -> 18; matrix products, arithmetic and copies ran while one was open for 1% -> 1% of each run, Pallas kernels for 4% -> 4%
where the time goes in v16:
time: 172 us
  waiting for transfers between devices  74.6 us (43%)
  Pallas kernels  50 us (29%)
  starting transfers between devices  43 us (25%)
  other arithmetic  2.79 us (2%)
    ppermute x34, waiting for transfers between devices, send(): return lax.ppermute(value, 'dp', every)  72.5 us
    ppermute x34, starting transfers between devices, send(): return lax.ppermute(value, 'dp', every)  41.5 us
    pallas_call x1, Pallas kernels, place(): pl.pallas_call(functools.partial(place_kernel, plan), out_shape=[jax.Shap...  21.4 us
    pallas_call x1, Pallas kernels, finish(): pl.pallas_call(functools.partial(finish_kernel, plan, tile, slots), grid=...  19.6 us
    pallas_call x1, Pallas kernels, owned(): pl.pallas_call(functools.partial(owned_kernel, plan), out_shape=[jax.Shap...  6.32 us
  transfers between devices with their start and end apart: 35, of which 18 were waited for; matrix products, arithmetic and copies ran while one was open for 1% of the time, Pallas kernels for 4%

profile of v16, /device:TPU:0, one launch (start us, length us, event | category | flops | bytes accessed | tf_op | source)
XLA Modules:
  0.0 171.6 jit_solution(11065460946283267615)
XLA Ops:
  0.7 0.6 pad_add_fusion.place_ref
  1.2 21.4 %place_gradients.1 = (f32[1096,128]{1,0:T(8,128)}, f32[1096,128]{1,0:T(8,128)}, f32[1096,128]{1,0:T(8,128)}, f32[1096,128]{1,0:T(8,128)}, f32[1096,128]{1,0:T(8,...) custom-call(s32[3]{0:T(128)} %pad_add_fusion.place_ref, ...), custom_call_target="tpu_custom_call" | custom-call | tf_op jit(solution)/shard_map/place_gradients/pallas_call | solution.py:314
  22.7 0.5 collective-permute-start
  23.2 1.8 %collective-permute-done = f32[1096,128]{1,0:T(8,128)S(1)} collective-permute-done((f32[1096,128]{1,0:T(8,128)}, f32[1096,128]{1,0:T(8,128)S(1)}, u32[]{:S(2)}, u32[]{:S(2)}) %collective-permute-start) | collective-permute-done | bytes 561184 | tf_op jit(solution)/shard_map/ppermute | solution.py:79
  25.0 1.1 add.68
  26.1 0.4 collective-permute-start.8
  26.6 0.1 collective-permute-start.4
  26.7 2.9 %collective-permute-start.5 = (f32[1096,128]{1,0:T(8,128)S(1)}, f32[1096,128]{1,0:T(8,128)S(1)}, u32[]{:S(2)}, u32[]{:S(2)}) collective-permute-start(f32[1096,128]{1,0:T(8,128)S(1)} %add.68), channel_id=1, source_target_pairs={{0,4},{2,6},{4,0},{6,2},{8,12},{10,14},{12,8},{14,10},{16,20},{18,... | collective-permute-start | bytes 1683464 | tf_op jit(solution)/shard_map/ppermute | solution.py:79
  29.6 0.5 collective-permute-start.7
  30.1 0.1 add.74
  30.2 1.2 collective-permute-start.9
  31.4 11.7 %collective-permute-done.5 = f32[1096,128]{1,0:T(8,128)S(1)} collective-permute-done((f32[1096,128]{1,0:T(8,128)S(1)}, f32[1096,128]{1,0:T(8,128)S(1)}, u32[]{:S(2)}, u32[]{:S(2)}) %collective-permute-start.5) | collective-permute-done | bytes 561184 | tf_op jit(solution)/shard_map/ppermute | solution.py:79
  43.0 0.1 add_add_fusion.2
  43.2 4.2 %collective-permute-start.6 = (f32[1096,128]{1,0:T(8,128)S(1)}, f32[1096,128]{1,0:T(8,128)S(1)}, u32[]{:S(2)}, u32[]{:S(2)}) collective-permute-start(f32[1096,128]{1,0:T(8,128)S(1)} %add_add_fusion.2), channel_id=1, source_target_pairs={{0,8},{2,10},{4,12},{6,14},{24,16},{26,18},{28,20},{30,22},{1,9},{... | collective-permute-start | bytes 1683464 | tf_op jit(solution)/shard_map/ppermute | solution.py:79
  47.4 6.3 %owned_weights.1 = (f32[1088,128]{1,0:T(8,128)}, s32[1152,128]{1,0:T(8,128)}) custom-call(s32[3]{0:T(128)} %pad_add_fusion.place_ref, s32[136,128]{1,0:T(8,128)} %bitcast.16, f32[17408,128]{1,0:T(8,128)} %weights_ref.3), custom_call_target="tpu_custom_call" | custom-call | bytes 20971520 | tf_op jit(solution)/shard_map/owned_weights/pallas_call | solution.py:392
  53.9 0.5 collective-permute-start.12
  54.4 1.6 collective-permute-start.14
  56.0 0.1 add_add_fusion.1
  56.1 1.9 %collective-permute-done.6 = f32[1096,128]{1,0:T(8,128)S(1)} collective-permute-done((f32[1096,128]{1,0:T(8,128)S(1)}, f32[1096,128]{1,0:T(8,128)S(1)}, u32[]{:S(2)}, u32[]{:S(2)}) %collective-permute-start.6) | collective-permute-done | bytes 561184 | tf_op jit(solution)/shard_map/ppermute | solution.py:79
  58.0 0.1 add.76
  58.1 0.8 collective-permute-start.10
  58.9 7.2 %collective-permute-start.11 = (f32[1096,128]{1,0:T(8,128)S(1)}, f32[1096,128]{1,0:T(8,128)S(1)}, u32[]{:S(2)}, u32[]{:S(2)}) collective-permute-start(f32[1096,128]{1,0:T(8,128)S(1)} %add_add_fusion.1), channel_id=1, source_target_pairs={{0,8},{2,10},{4,12},{6,14},{24,16},{26,18},{28,20},{30,22},{1,9},{... | collective-permute-start | bytes 1683464 | tf_op jit(solution)/shard_map/ppermute | solution.py:79
  66.2 0.1 collective-permute-start.1
  66.3 0.1 add.70
  66.3 1.6 collective-permute-start.3
  67.9 1.3 collective-permute-done.14
  69.2 0.1 add_add_fusion
  69.3 6.9 %collective-permute-done.11 = f32[1096,128]{1,0:T(8,128)S(1)} collective-permute-done((f32[1096,128]{1,0:T(8,128)S(1)}, f32[1096,128]{1,0:T(8,128)S(1)}, u32[]{:S(2)}, u32[]{:S(2)}) %collective-permute-start.11) | collective-permute-done | bytes 561184 | tf_op jit(solution)/shard_map/ppermute | solution.py:79
  76.4 2.5 %collective-permute-start.15 = (f32[1096,128]{1,0:T(8,128)S(1)}, f32[1096,128]{1,0:T(8,128)S(1)}, u32[]{:S(2)}, u32[]{:S(2)}) collective-permute-start(f32[1096,128]{1,0:T(8,128)S(1)} %add.80), channel_id=1, source_target_pairs={{0,8},{2,10},{4,12},{6,14},{8,0},{10,2},{12,4},{14,6},{16,24},{18,... | collective-permute-start | bytes 1683464 | tf_op jit(solution)/shard_map/ppermute | solution.py:79
  79.0 0.7 collective-permute-start.16
  79.7 0.1 add.69.refs_0_
  79.8 1.7 %collective-permute-done.3.refs_1_ = f32[1096,128]{1,0:T(8,128)S(1)} collective-permute-done((f32[1096,128]{1,0:T(8,128)S(1)}, f32[1096,128]{1,0:T(8,128)S(1)}, u32[]{:S(2)}, u32[]{:S(2)}) %collective-permute-start.3) | collective-permute-done | bytes 561184 | tf_op jit(solution)/shard_map/ppermute | solution.py:79
  81.5 6.0 %collective-permute-done.15.refs_2_ = f32[1096,128]{1,0:T(8,128)S(1)} collective-permute-done((f32[1096,128]{1,0:T(8,128)S(1)}, f32[1096,128]{1,0:T(8,128)S(1)}, u32[]{:S(2)}, u32[]{:S(2)}) %collective-permute-start.15) | collective-permute-done | bytes 561184 | tf_op jit(solution)/shard_map/ppermute | solution.py:79
  87.6 2.0 %moments.1 = (f32[1088,128]{1,0:T(8,128)}, f32[1088,128]{1,0:T(8,128)}, f32[1096,128]{1,0:T(8,128)S(1)}) custom-call(f32[1096,128]{1,0:T(8,128)S(1)} %add.69.refs_0_, f32[1096,128]{1,0:T(8,128)S(1)} %collective-permute-done.3.refs_1_, f32[1096,128]{1,0:T(8,128)S(1)} %collective-permute-done.15.refs_2_, f32[1096,128]{1,0:T(8,128)S(1)} %collective-permute-done.16.refs_3_, ...), custom_call_target="tpu_custom_call" | custom-call | tf_op jit(solution)/shard_map/moments/pallas_call | solution.py:446
  89.7 3.8 %collective-permute-start.18 = (f32[1096,128]{1,0:T(8,128)S(1)}, f32[1096,128]{1,0:T(8,128)S(1)}, u32[]{:S(2)}, u32[]{:S(2)}) collective-permute-start(f32[1096,128]{1,0:T(8,128)S(1)} %get-tuple-element.96), channel_id=1, source_target_pairs={{0,8},{2,10},{4,12},{6,14},{8,0},{10,2},{12,4},{14,6},{16,24},{18,... | collective-permute-start | bytes 1683464 | tf_op jit(solution)/shard_map/ppermute | solution.py:79
  93.5 1.5 collective-permute-start.19
  95.0 0.7 collective-permute-start.17
  95.6 5.4 %collective-permute-done.18 = f32[1096,128]{1,0:T(8,128)S(1)} collective-permute-done((f32[1096,128]{1,0:T(8,128)S(1)}, f32[1096,128]{1,0:T(8,128)S(1)}, u32[]{:S(2)}, u32[]{:S(2)}) %collective-permute-start.18) | collective-permute-done | bytes 561184 | tf_op jit(solution)/shard_map/ppermute | solution.py:79
  101.1 1.5 collective-permute-start.24
  102.6 0.7 collective-permute-start.20
  103.3 0.1 pad_maximum_fusion.refs_0_.refs_1_
  103.4 4.9 %collective-permute-done.19 = f32[1096,128]{1,0:T(8,128)S(1)} collective-permute-done((f32[1096,128]{1,0:T(8,128)S(1)}, f32[1096,128]{1,0:T(8,128)S(1)}, u32[]{:S(2)}, u32[]{:S(2)}) %collective-permute-start.19) | collective-permute-done | bytes 561184 | tf_op jit(solution)/shard_map/ppermute | solution.py:79
  108.3 1.3 collective-permute-start.23
  109.6 1.3 collective-permute-start.21
  110.9 6.4 %collective-permute-done.24 = f32[1096,128]{1,0:T(8,128)S(1)} collective-permute-done((f32[1096,128]{1,0:T(8,128)S(1)}, f32[1096,128]{1,0:T(8,128)S(1)}, u32[]{:S(2)}, u32[]{:S(2)}) %collective-permute-start.24) | collective-permute-done | bytes 561184 | tf_op jit(solution)/shard_map/ppermute | solution.py:79
  117.3 5.5 %collective-permute-done.23 = f32[1096,128]{1,0:T(8,128)S(1)} collective-permute-done((f32[1096,128]{1,0:T(8,128)S(1)}, f32[1096,128]{1,0:T(8,128)S(1)}, u32[]{:S(2)}, u32[]{:S(2)}) %collective-permute-start.23) | collective-permute-done | bytes 561184 | tf_op jit(solution)/shard_map/ppermute | solution.py:79
  122.8 0.1 add.83.refs_2_
  122.9 0.1 pad_maximum_fusion.1.refs_1_
  123.0 2.5 %collective-permute-start.26 = (f32[1096,128]{1,0:T(8,128)S(1)}, f32[1096,128]{1,0:T(8,128)S(1)}, u32[]{:S(2)}, u32[]{:S(2)}) collective-permute-start(f32[1096,128]{1,0:T(8,128)S(1)} %add.83.refs_2_), channel_id=1, source_target_pairs={{0,4},{2,6},{4,0},{6,2},{8,12},{10,14},{12,8},{14,10},{16,20},{18,... | collective-permute-start | bytes 1683464 | tf_op jit(solution)/shard_map/ppermute | solution.py:79
  125.5 6.3 %collective-permute-done.21 = f32[1096,128]{1,0:T(8,128)S(1)} collective-permute-done((f32[1096,128]{1,0:T(8,128)S(1)}, f32[1096,128]{1,0:T(8,128)S(1)}, u32[]{:S(2)}, u32[]{:S(2)}) %collective-permute-start.21) | collective-permute-done | bytes 561184 | tf_op jit(solution)/shard_map/ppermute | solution.py:79
  131.9 0.6 sums.1
  132.4 1.6 collective-permute-start.25
  134.0 0.5 collective-permute-start.29
  134.5 0.2 collective-permute-start.22
  134.8 1.3 collective-permute-done.25
  136.1 0.5 collective-permute-start.27
  136.6 2.5 %collective-permute-done.27 = f32[8,128]{1,0:T(8,128)S(1)} collective-permute-done((f32[8,128]{1,0:T(8,128)S(1)}, f32[8,128]{1,0:T(8,128)S(1)}, u32[]{:S(2)}, u32[]{:S(2)}) %collective-permute-start.27) | collective-permute-done | bytes 4128 | tf_op jit(solution)/shard_map/ppermute | solution.py:79
  139.2 1.5 collective-permute-start.28
  140.7 2.1 %collective-permute-done.28 = f32[8,128]{1,0:T(8,128)S(1)} collective-permute-done((f32[8,128]{1,0:T(8,128)S(1)}, f32[8,128]{1,0:T(8,128)S(1)}, u32[]{:S(2)}, u32[]{:S(2)}) %collective-permute-start.28) | collective-permute-done | bytes 4128 | tf_op jit(solution)/shard_map/ppermute | solution.py:166
  142.8 6.3 %collective-permute-done.29.refs_5_ = f32[1096,128]{1,0:T(8,128)S(1)} collective-permute-done((f32[1096,128]{1,0:T(8,128)S(1)}, f32[1096,128]{1,0:T(8,128)S(1)}, u32[]{:S(2)}, u32[]{:S(2)}) %collective-permute-start.29) | collective-permute-done | bytes 561184 | tf_op jit(solution)/shard_map/ppermute | solution.py:79
  149.1 0.5 collective-permute-start.34
  149.7 1.4 collective-permute-done.33.refs_9_
  151.1 0.8 collective-permute-done.34.refs_11_
  151.9 19.6 %new_weights.1 = (f32[17408,128]{1,0:T(8,128)}, f32[3,2,1024]{2,1,0:T(2,128)}, f32[7]{0:T(128)}) custom-call(s32[3]{0:T(128)S(1)} %copy-done.6, s32[136,128]{1,0:T(8,128)S(1)} %copy-done.4, f32[8,128]{1,0:T(8,128)S(1)} %add.86.total_ref, f32[3,2,1024]{2,1,0:T(2,128)S(1)} %copy-done.5, f32[17408,128]{1,0:T(8,128)S(1)} %bitcast.11, ...), custom_call_target="tpu_custom_call" | custom-call | tf_op jit(solution)/shard_map/new_weights/pallas_call | solution.py:524
  (75 shorter events, 0.5 us)
Async XLA Ops:
  22.6 6.9 %copy-start.18 = (f32[1096,128]{1,0:T(8,128)S(1)}, f32[1096,128]{1,0:T(8,128)}, u32[]{:S(2)}) copy-start(f32[1096,128]{1,0:T(8,128)} %get-tuple-element.90) | copy-start | bytes 1683460
  22.7 6.9 %copy-start.17 = (f32[1096,128]{1,0:T(8,128)S(1)}, f32[1096,128]{1,0:T(8,128)}, u32[]{:S(2)}) copy-start(f32[1096,128]{1,0:T(8,128)} %get-tuple-element.78) | copy-start | bytes 1683460
  22.7 7.4 %copy-start.13 = (f32[1096,128]{1,0:T(8,128)S(1)}, f32[1096,128]{1,0:T(8,128)}, u32[]{:S(2)}) copy-start(f32[1096,128]{1,0:T(8,128)} %get-tuple-element.79) | copy-start | bytes 1683460
  22.7 2.3 %collective-permute-start = (f32[1096,128]{1,0:T(8,128)}, f32[1096,128]{1,0:T(8,128)S(1)}, u32[]{:S(2)}, u32[]{:S(2)}) collective-permute-start(f32[1096,128]{1,0:T(8,128)} %get-tuple-element.63), channel_id=1, source_target_pairs={{0,2},{2,0},{4,6},{6,4},{8,10},{10,8},{12,14},{14,12},{16,18},{18,... | collective-permute-start | bytes 1683464 | tf_op jit(solution)/shard_map/ppermute | solution.py:79
  26.1 16.9 %copy-start.12 = (f32[1096,128]{1,0:T(8,128)S(1)}, f32[1096,128]{1,0:T(8,128)}, u32[]{:S(2)}) copy-start(f32[1096,128]{1,0:T(8,128)} %get-tuple-element.74) | copy-start | bytes 1683460
  26.1 4.0 %collective-permute-start.8 = (f32[1096,128]{1,0:T(8,128)}, f32[1096,128]{1,0:T(8,128)S(1)}, u32[]{:S(2)}, u32[]{:S(2)}) collective-permute-start(f32[1096,128]{1,0:T(8,128)} %get-tuple-element.80), channel_id=1, source_target_pairs={{0,2},{2,0},{4,6},{6,4},{8,10},{10,8},{12,14},{14,12},{16,18},{18,... | collective-permute-start | bytes 1683464 | tf_op jit(solution)/shard_map/ppermute | solution.py:79
  26.6 4.8 %collective-permute-start.4 = (f32[1096,128]{1,0:T(8,128)}, f32[1096,128]{1,0:T(8,128)S(1)}, u32[]{:S(2)}, u32[]{:S(2)}) collective-permute-start(f32[1096,128]{1,0:T(8,128)} %get-tuple-element.75), channel_id=1, source_target_pairs={{0,2},{2,0},{4,6},{6,4},{8,10},{10,8},{12,14},{14,12},{16,18},{18,... | collective-permute-start | bytes 1683464 | tf_op jit(solution)/shard_map/ppermute | solution.py:79
  26.7 16.4 %collective-permute-start.5 = (f32[1096,128]{1,0:T(8,128)S(1)}, f32[1096,128]{1,0:T(8,128)S(1)}, u32[]{:S(2)}, u32[]{:S(2)}) collective-permute-start(f32[1096,128]{1,0:T(8,128)S(1)} %add.68), channel_id=1, source_target_pairs={{0,4},{2,6},{4,0},{6,2},{8,12},{10,14},{12,8},{14,10},{16,20},{18,... | collective-permute-start | bytes 1683464 | tf_op jit(solution)/shard_map/ppermute | solution.py:79
  29.6 24.3 %collective-permute-start.13 = (f32[1096,128]{1,0:T(8,128)S(1)}, f32[1096,128]{1,0:T(8,128)S(1)}, u32[]{:S(2)}, u32[]{:S(2)}) collective-permute-start(f32[1096,128]{1,0:T(8,128)S(1)} %copy-done.18), channel_id=1, source_target_pairs={{0,2},{2,0},{4,6},{6,4},{8,10},{10,8},{12,14},{14,12},{16,18},{18,... | collective-permute-start | bytes 1683464 | tf_op jit(solution)/shard_map/ppermute | solution.py:79
  29.6 24.9 %collective-permute-start.7 = (f32[1096,128]{1,0:T(8,128)S(1)}, f32[1096,128]{1,0:T(8,128)S(1)}, u32[]{:S(2)}, u32[]{:S(2)}) collective-permute-start(f32[1096,128]{1,0:T(8,128)S(1)} %copy-done.17), channel_id=1, source_target_pairs={{0,2},{2,0},{4,6},{6,4},{8,10},{10,8},{12,14},{14,12},{16,18},{18,... | collective-permute-start | bytes 1683464 | tf_op jit(solution)/shard_map/ppermute | solution.py:79
  30.2 25.8 %collective-permute-start.9 = (f32[1096,128]{1,0:T(8,128)S(1)}, f32[1096,128]{1,0:T(8,128)S(1)}, u32[]{:S(2)}, u32[]{:S(2)}) collective-permute-start(f32[1096,128]{1,0:T(8,128)S(1)} %add.74), channel_id=1, source_target_pairs={{0,4},{2,6},{4,0},{6,2},{8,12},{10,14},{12,8},{14,10},{16,20},{18,... | collective-permute-start | bytes 1683464 | tf_op jit(solution)/shard_map/ppermute | solution.py:79
  43.2 10.6 %copy-start.16 = (f32[1096,128]{1,0:T(8,128)S(1)}, f32[1096,128]{1,0:T(8,128)}, u32[]{:S(2)}) copy-start(f32[1096,128]{1,0:T(8,128)} %get-tuple-element.73) | copy-start | bytes 1683460
  43.2 10.7 %copy-start.15 = (f32[1096,128]{1,0:T(8,128)S(1)}, f32[1096,128]{1,0:T(8,128)}, u32[]{:S(2)}) copy-start(f32[1096,128]{1,0:T(8,128)} %get-tuple-element.88) | copy-start | bytes 1683460
  43.2 11.2 %copy-start.11 = (f32[1096,128]{1,0:T(8,128)S(1)}, f32[1096,128]{1,0:T(8,128)}, u32[]{:S(2)}) copy-start(f32[1096,128]{1,0:T(8,128)} %get-tuple-element.89) | copy-start | bytes 1683460
  43.2 14.8 %collective-permute-start.6 = (f32[1096,128]{1,0:T(8,128)S(1)}, f32[1096,128]{1,0:T(8,128)S(1)}, u32[]{:S(2)}, u32[]{:S(2)}) collective-permute-start(f32[1096,128]{1,0:T(8,128)S(1)} %add_add_fusion.2), channel_id=1, source_target_pairs={{0,8},{2,10},{4,12},{6,14},{24,16},{26,18},{28,20},{30,22},{1,9},{... | collective-permute-start | bytes 1683464 | tf_op jit(solution)/shard_map/ppermute | solution.py:79
  53.8 2.2 %copy-start.10 = (f32[1096,128]{1,0:T(8,128)S(1)}, f32[1096,128]{1,0:T(8,128)}, u32[]{:S(2)}) copy-start(f32[1096,128]{1,0:T(8,128)} %get-tuple-element.77) | copy-start | bytes 1683460
  53.8 12.4 %collective-permute-start.2 = (f32[1096,128]{1,0:T(8,128)S(1)}, f32[1096,128]{1,0:T(8,128)S(1)}, u32[]{:S(2)}, u32[]{:S(2)}) collective-permute-start(f32[1096,128]{1,0:T(8,128)S(1)} %copy-done.16), channel_id=1, source_target_pairs={{0,2},{2,0},{4,6},{6,4},{8,10},{10,8},{12,14},{14,12},{16,18},{18,... | collective-permute-start | bytes 1683464 | tf_op jit(solution)/shard_map/ppermute | solution.py:79
  53.9 12.5 %collective-permute-start.12 = (f32[1096,128]{1,0:T(8,128)S(1)}, f32[1096,128]{1,0:T(8,128)S(1)}, u32[]{:S(2)}, u32[]{:S(2)}) collective-permute-start(f32[1096,128]{1,0:T(8,128)S(1)} %copy-done.15), channel_id=1, source_target_pairs={{0,2},{2,0},{4,6},{6,4},{8,10},{10,8},{12,14},{14,12},{16,18},{18,... | collective-permute-start | bytes 1683464 | tf_op jit(solution)/shard_map/ppermute | solution.py:79
  54.4 14.8 %collective-permute-start.14 = (f32[1096,128]{1,0:T(8,128)S(1)}, f32[1096,128]{1,0:T(8,128)S(1)}, u32[]{:S(2)}, u32[]{:S(2)}) collective-permute-start(f32[1096,128]{1,0:T(8,128)S(1)} %add.78), channel_id=1, source_target_pairs={{0,4},{2,6},{4,0},{6,2},{8,12},{10,14},{12,8},{14,10},{16,20},{18,... | collective-permute-start | bytes 1683464 | tf_op jit(solution)/shard_map/ppermute | solution.py:79
  56.1 10.1 %copy-start.14 = (f32[1096,128]{1,0:T(8,128)S(1)}, f32[1096,128]{1,0:T(8,128)}, u32[]{:S(2)}) copy-start(f32[1096,128]{1,0:T(8,128)} %get-tuple-element.71) | copy-start | bytes 1683460
  56.1 10.1 %copy-start.9 = (f32[1096,128]{1,0:T(8,128)S(1)}, f32[1096,128]{1,0:T(8,128)}, u32[]{:S(2)}) copy-start(f32[1096,128]{1,0:T(8,128)} %get-tuple-element.72) | copy-start | bytes 1683460
  58.1 11.1 %copy-start.8 = (f32[1096,128]{1,0:T(8,128)S(1)}, f32[1096,128]{1,0:T(8,128)}, u32[]{:S(2)}) copy-start(f32[1096,128]{1,0:T(8,128)} %get-tuple-element.87) | copy-start | bytes 1683460
  58.1 11.2 %collective-permute-start.10 = (f32[1096,128]{1,0:T(8,128)S(1)}, f32[1096,128]{1,0:T(8,128)S(1)}, u32[]{:S(2)}, u32[]{:S(2)}) collective-permute-start(f32[1096,128]{1,0:T(8,128)S(1)} %add.76), channel_id=1, source_target_pairs={{8,16},{10,18},{12,20},{14,22},{16,8},{18,10},{20,12},{22,14},{9,1... | collective-permute-start | bytes 1683464 | tf_op jit(solution)/shard_map/ppermute | solution.py:79
  58.9 17.3 %collective-permute-start.11 = (f32[1096,128]{1,0:T(8,128)S(1)}, f32[1096,128]{1,0:T(8,128)S(1)}, u32[]{:S(2)}, u32[]{:S(2)}) collective-permute-start(f32[1096,128]{1,0:T(8,128)S(1)} %add_add_fusion.1), channel_id=1, source_target_pairs={{0,8},{2,10},{4,12},{6,14},{24,16},{26,18},{28,20},{30,22},{1,9},{... | collective-permute-start | bytes 1683464 | tf_op jit(solution)/shard_map/ppermute | solution.py:79
  66.2 13.5 %collective-permute-start.1 = (f32[1096,128]{1,0:T(8,128)S(1)}, f32[1096,128]{1,0:T(8,128)S(1)}, u32[]{:S(2)}, u32[]{:S(2)}) collective-permute-start(f32[1096,128]{1,0:T(8,128)S(1)} %copy-done.14), channel_id=1, source_target_pairs={{0,2},{2,0},{4,6},{6,4},{8,10},{10,8},{12,14},{14,12},{16,18},{18,... | collective-permute-start | bytes 1683464 | tf_op jit(solution)/shard_map/ppermute | solution.py:79
  66.3 15.2 %collective-permute-start.3 = (f32[1096,128]{1,0:T(8,128)S(1)}, f32[1096,128]{1,0:T(8,128)S(1)}, u32[]{:S(2)}, u32[]{:S(2)}) collective-permute-start(f32[1096,128]{1,0:T(8,128)S(1)} %add.70), channel_id=1, source_target_pairs={{0,4},{2,6},{4,0},{6,2},{8,12},{10,14},{12,8},{14,10},{16,20},{18,... | collective-permute-start | bytes 1683464 | tf_op jit(solution)/shard_map/ppermute | solution.py:79
  69.2 82.7 %slice-start = ((s8[8912896]{0:T(1024)(128)(4,1)}), s8[4194304]{0:T(1024)(128)(4,1)S(1)}, s32[]{:S(2)}) async-start(s8[8912896]{0:T(1024)(128)(4,1)} %bitcast.10), calls=%async_computation | async-start | bytes 8388608
  76.2 3.4 %copy-start.7 = (f32[1096,128]{1,0:T(8,128)S(1)}, f32[1096,128]{1,0:T(8,128)}, u32[]{:S(2)}) copy-start(f32[1096,128]{1,0:T(8,128)} %get-tuple-element.61) | copy-start | bytes 1683460
  76.3 11.3 %copy-start.2 = (f32[1,1088,128]{2,1,0:T(8,128)S(1)}, f32[1,1088,128]{2,1,0:T(8,128)}, u32[]{:S(2)}) copy-start(f32[1,1088,128]{2,1,0:T(8,128)} %param.10) | copy-start | bytes 1671172
  76.3 11.2 %copy-start.3 = (f32[1088,128]{1,0:T(8,128)S(1)}, f32[1088,128]{1,0:T(8,128)}, u32[]{:S(2)}) copy-start(f32[1088,128]{1,0:T(8,128)} %get-tuple-element.94.refs_6_) | copy-start | bytes 1671172
  76.4 11.2 %copy-start = (s32[1152,128]{1,0:T(8,128)S(1)}, s32[1152,128]{1,0:T(8,128)}, u32[]{:S(2)}) copy-start(s32[1152,128]{1,0:T(8,128)} %get-tuple-element.95.refs_7_) | copy-start | bytes 1769476
  76.4 11.2 %copy-start.1 = (f32[1,1088,128]{2,1,0:T(8,128)S(1)}, f32[1,1088,128]{2,1,0:T(8,128)}, u32[]{:S(2)}) copy-start(f32[1,1088,128]{2,1,0:T(8,128)} %param.9) | copy-start | bytes 1671172
  76.4 11.1 %collective-permute-start.15 = (f32[1096,128]{1,0:T(8,128)S(1)}, f32[1096,128]{1,0:T(8,128)S(1)}, u32[]{:S(2)}, u32[]{:S(2)}) collective-permute-start(f32[1096,128]{1,0:T(8,128)S(1)} %add.80), channel_id=1, source_target_pairs={{0,8},{2,10},{4,12},{6,14},{8,0},{10,2},{12,4},{14,6},{16,24},{18,... | collective-permute-start | bytes 1683464 | tf_op jit(solution)/shard_map/ppermute | solution.py:79
  79.0 8.6 %collective-permute-start.16 = (f32[1096,128]{1,0:T(8,128)S(1)}, f32[1096,128]{1,0:T(8,128)S(1)}, u32[]{:S(2)}, u32[]{:S(2)}) collective-permute-start(f32[1096,128]{1,0:T(8,128)S(1)} %add.81), channel_id=1, source_target_pairs={{8,16},{10,18},{12,20},{14,22},{16,8},{18,10},{20,12},{22,14},{9,1... | collective-permute-start | bytes 1683464 | tf_op jit(solution)/shard_map/ppermute | solution.py:79
  87.6 64.3 %slice-start.1 = ((s8[8912896]{0:T(1024)(128)(4,1)}), s8[4194304]{0:T(1024)(128)(4,1)S(1)}, s32[]{:S(2)}) async-start(s8[8912896]{0:T(1024)(128)(4,1)} %bitcast.10), calls=%async_computation.1 | async-start | bytes 8388608
  89.7 11.4 %collective-permute-start.18 = (f32[1096,128]{1,0:T(8,128)S(1)}, f32[1096,128]{1,0:T(8,128)S(1)}, u32[]{:S(2)}, u32[]{:S(2)}) collective-permute-start(f32[1096,128]{1,0:T(8,128)S(1)} %get-tuple-element.96), channel_id=1, source_target_pairs={{0,8},{2,10},{4,12},{6,14},{8,0},{10,2},{12,4},{14,6},{16,24},{18,... | collective-permute-start | bytes 1683464 | tf_op jit(solution)/shard_map/ppermute | solution.py:79
  93.5 14.8 %collective-permute-start.19 = (f32[1096,128]{1,0:T(8,128)S(1)}, f32[1096,128]{1,0:T(8,128)S(1)}, u32[]{:S(2)}, u32[]{:S(2)}) collective-permute-start(f32[1096,128]{1,0:T(8,128)S(1)} %get-tuple-element.96), channel_id=1, source_target_pairs={{0,4},{2,6},{4,0},{6,2},{8,12},{10,14},{12,8},{14,10},{16,20},{18,... | collective-permute-start | bytes 1683464 | tf_op jit(solution)/shard_map/ppermute | solution.py:79
  95.0 13.4 %collective-permute-start.17 = (f32[1096,128]{1,0:T(8,128)S(1)}, f32[1096,128]{1,0:T(8,128)S(1)}, u32[]{:S(2)}, u32[]{:S(2)}) collective-permute-start(f32[1096,128]{1,0:T(8,128)S(1)} %get-tuple-element.96), channel_id=1, source_target_pairs={{8,16},{10,18},{12,20},{14,22},{16,8},{18,10},{20,12},{22,14},{9,1... | collective-permute-start | bytes 1683464 | tf_op jit(solution)/shard_map/ppermute | solution.py:79
  101.1 16.2 %collective-permute-start.24 = (f32[1096,128]{1,0:T(8,128)S(1)}, f32[1096,128]{1,0:T(8,128)S(1)}, u32[]{:S(2)}, u32[]{:S(2)}) collective-permute-start(f32[1096,128]{1,0:T(8,128)S(1)} %collective-permute-done.18), channel_id=1, source_target_pairs={{0,4},{2,6},{4,0},{6,2},{8,12},{10,14},{12,8},{14,10},{16,20},{18,... | collective-permute-start | bytes 1683464 | tf_op jit(solution)/shard_map/ppermute | solution.py:79
  102.6 7.0 %collective-permute-start.20 = (f32[1096,128]{1,0:T(8,128)S(1)}, f32[1096,128]{1,0:T(8,128)S(1)}, u32[]{:S(2)}, u32[]{:S(2)}) collective-permute-start(f32[1096,128]{1,0:T(8,128)S(1)} %collective-permute-done.18), channel_id=1, source_target_pairs={{8,16},{10,18},{12,20},{14,22},{16,8},{18,10},{20,12},{22,14},{9,1... | collective-permute-start | bytes 1683464 | tf_op jit(solution)/shard_map/ppermute | solution.py:79
  103.4 48.5 %slice-start.2 = ((s8[8912896]{0:T(1024)(128)(4,1)}), s8[524288]{0:T(1024)(128)(4,1)S(1)}, s32[]{:S(2)}) async-start(s8[8912896]{0:T(1024)(128)(4,1)} %bitcast.10), calls=%async_computation.2 | async-start | bytes 1048576
  108.3 14.5 %collective-permute-start.23 = (f32[1096,128]{1,0:T(8,128)S(1)}, f32[1096,128]{1,0:T(8,128)S(1)}, u32[]{:S(2)}, u32[]{:S(2)}) collective-permute-start(f32[1096,128]{1,0:T(8,128)S(1)} %collective-permute-done.17), channel_id=1, source_target_pairs={{8,0},{10,2},{12,4},{14,6},{16,24},{18,26},{20,28},{22,30},{9,1},{... | collective-permute-start | bytes 1683464 | tf_op jit(solution)/shard_map/ppermute | solution.py:79
  109.6 22.2 %collective-permute-start.21 = (f32[1096,128]{1,0:T(8,128)S(1)}, f32[1096,128]{1,0:T(8,128)S(1)}, u32[]{:S(2)}, u32[]{:S(2)}) collective-permute-start(f32[1096,128]{1,0:T(8,128)S(1)} %collective-permute-done.20), channel_id=1, source_target_pairs={{8,0},{10,2},{12,4},{14,6},{16,24},{18,26},{20,28},{22,30},{9,1},{... | collective-permute-start | bytes 1683464 | tf_op jit(solution)/shard_map/ppermute | solution.py:79
  123.0 8.9 %copy-start.6 = (s32[3]{0:T(128)S(1)}, s32[3]{0:T(128)}, u32[]{:S(2)}) copy-start(s32[3]{0:T(128)} %pad_add_fusion.place_ref) | copy-start | bytes 40
  123.0 13.1 %collective-permute-start.26 = (f32[1096,128]{1,0:T(8,128)S(1)}, f32[1096,128]{1,0:T(8,128)S(1)}, u32[]{:S(2)}, u32[]{:S(2)}) collective-permute-start(f32[1096,128]{1,0:T(8,128)S(1)} %add.83.refs_2_), channel_id=1, source_target_pairs={{0,4},{2,6},{4,0},{6,2},{8,12},{10,14},{12,8},{14,10},{16,20},{18,... | collective-permute-start | bytes 1683464 | tf_op jit(solution)/shard_map/ppermute | solution.py:79
  131.9 20.0 %copy-start.4 = (s32[136,128]{1,0:T(8,128)S(1)}, s32[136,128]{1,0:T(8,128)}, u32[]{:S(2)}) copy-start(s32[136,128]{1,0:T(8,128)} %get-tuple-element.60.position_ref) | copy-start | bytes 208900
  131.9 20.0 %copy-start.5 = (f32[3,2,1024]{2,1,0:T(2,128)S(1)}, f32[3,2,1024]{2,1,0:T(2,128)}, u32[]{:S(2)}) copy-start(f32[3,2,1024]{2,1,0:T(2,128)} %norm_ref.1) | copy-start | bytes 73732
  132.4 3.7 %collective-permute-start.25 = (f32[8,128]{1,0:T(8,128)S(1)}, f32[8,128]{1,0:T(8,128)S(1)}, u32[]{:S(2)}, u32[]{:S(2)}) collective-permute-start(f32[8,128]{1,0:T(8,128)S(1)} %sums.1), channel_id=1, source_target_pairs={{0,4},{2,6},{4,0},{6,2},{8,12},{10,14},{12,8},{14,10},{16,20},{18,... | collective-permute-start | bytes 12296 | tf_op jit(solution)/shard_map/ppermute | solution.py:79
  134.0 15.6 %collective-permute-start.30 = (f32[2192,128]{1,0:T(8,128)S(1)}, f32[2192,128]{1,0:T(8,128)S(1)}, u32[]{:S(2)}, u32[]{:S(2)}) collective-permute-start(f32[2192,128]{1,0:T(8,128)S(1)} %pad_maximum_fusion.refs_0_.refs_1_), channel_id=1, source_target_pairs={{0,2},{2,0},{4,6},{6,4},{8,10},{10,8},{12,14},{14,12},{16,18},{18,... | collective-permute-start | bytes 3366920 | tf_op jit(solution)/shard_map/ppermute | solution.py:79
  134.0 15.1 %collective-permute-start.29 = (f32[1096,128]{1,0:T(8,128)S(1)}, f32[1096,128]{1,0:T(8,128)S(1)}, u32[]{:S(2)}, u32[]{:S(2)}) collective-permute-start(f32[1096,128]{1,0:T(8,128)S(1)} %add.82.refs_3_.refs_4_), channel_id=1, source_target_pairs={{0,4},{2,6},{4,0},{6,2},{8,12},{10,14},{12,8},{14,10},{16,20},{18,... | collective-permute-start | bytes 1683464 | tf_op jit(solution)/shard_map/ppermute | solution.py:79
  134.5 14.6 %collective-permute-start.22 = (f32[1096,128]{1,0:T(8,128)S(1)}, f32[1096,128]{1,0:T(8,128)S(1)}, u32[]{:S(2)}, u32[]{:S(2)}) collective-permute-start(f32[1096,128]{1,0:T(8,128)S(1)} %add.82.refs_3_.refs_4_), channel_id=1, source_target_pairs={{0,2},{2,0},{4,6},{6,4},{8,10},{10,8},{12,14},{14,12},{16,18},{18,... | collective-permute-start | bytes 1683464 | tf_op jit(solution)/shard_map/ppermute | solution.py:79
  136.1 13.5 %collective-permute-start.31 = (f32[2192,128]{1,0:T(8,128)S(1)}, f32[2192,128]{1,0:T(8,128)S(1)}, u32[]{:S(2)}, u32[]{:S(2)}) collective-permute-start(f32[2192,128]{1,0:T(8,128)S(1)} %pad_maximum_fusion.1.refs_1_), channel_id=1, source_target_pairs={{0,2},{2,0},{4,6},{6,4},{8,10},{10,8},{12,14},{14,12},{16,18},{18,... | collective-permute-start | bytes 3366920 | tf_op jit(solution)/shard_map/ppermute | solution.py:79
  136.1 3.0 %collective-permute-start.27 = (f32[8,128]{1,0:T(8,128)S(1)}, f32[8,128]{1,0:T(8,128)S(1)}, u32[]{:S(2)}, u32[]{:S(2)}) collective-permute-start(f32[8,128]{1,0:T(8,128)S(1)} %add.84), channel_id=1, source_target_pairs={{0,2},{2,0},{4,6},{6,4},{8,10},{10,8},{12,14},{14,12},{16,18},{18,... | collective-permute-start | bytes 12296 | tf_op jit(solution)/shard_map/ppermute | solution.py:79
  139.2 3.6 %collective-permute-start.28 = (f32[8,128]{1,0:T(8,128)S(1)}, f32[8,128]{1,0:T(8,128)S(1)}, u32[]{:S(2)}, u32[]{:S(2)}) collective-permute-start(f32[8,128]{1,0:T(8,128)S(1)} %add.85), channel_id=1, source_target_pairs={{0,1},{1,0},{2,3},{3,2},{4,5},{5,4},{6,7},{7,6},{8,9},{9,8},{10,11... | collective-permute-start | bytes 12296 | tf_op jit(solution)/shard_map/ppermute | solution.py:166
  142.8 6.9 %collective-permute-start.32 = (f32[1096,128]{1,0:T(8,128)S(1)}, f32[1096,128]{1,0:T(8,128)S(1)}, u32[]{:S(2)}, u32[]{:S(2)}) collective-permute-start(f32[1096,128]{1,0:T(8,128)S(1)} %add.83.refs_2_), channel_id=1, source_target_pairs={{0,2},{2,0},{4,6},{6,4},{8,10},{10,8},{12,14},{14,12},{16,18},{18,... | collective-permute-start | bytes 1683464 | tf_op jit(solution)/shard_map/ppermute | solution.py:79
  149.1 2.0 %collective-permute-start.33 = (f32[1096,128]{1,0:T(8,128)S(1)}, f32[1096,128]{1,0:T(8,128)S(1)}, u32[]{:S(2)}, u32[]{:S(2)}) collective-permute-start(f32[1096,128]{1,0:T(8,128)S(1)} %collective-permute-done.26.refs_3_), channel_id=1, source_target_pairs={{0,2},{2,0},{4,6},{6,4},{8,10},{10,8},{12,14},{14,12},{16,18},{18,... | collective-permute-start | bytes 1683464 | tf_op jit(solution)/shard_map/ppermute | solution.py:79
  149.1 2.8 %collective-permute-start.34 = (f32[1096,128]{1,0:T(8,128)S(1)}, f32[1096,128]{1,0:T(8,128)S(1)}, u32[]{:S(2)}, u32[]{:S(2)}) collective-permute-start(f32[1096,128]{1,0:T(8,128)S(1)} %collective-permute-done.29.refs_5_), channel_id=1, source_target_pairs={{0,2},{2,0},{4,6},{6,4},{8,10},{10,8},{12,14},{14,12},{16,18},{18,... | collective-permute-start | bytes 1683464 | tf_op jit(solution)/shard_map/ppermute | solution.py:79

commit v17 on v16

--- a/solution.py
+++ b/solution.py
@@ -117,8 +117,7 @@
     in_three = plan.send(near_three, "z", INWARD)
     in_three, near_two, *beside = together(in_three, sum(two[1:], two[0]), *beside)
     one = along_x(1, mine[1])
-    near_two, onward = together(near_two, near_two + in_three)
-    across_two = plan.send(onward, "z", MIDDLE)
+    across_two = plan.send(near_two + in_three, "z", MIDDLE)
     in_two = plan.send(near_two, "z", INWARD)
     across_two, in_two, near_one = together(across_two, in_two, sum(one[1:], one[0]))
     zero = along_x(0, mine[0])

time: 172 us -> 172 us (level)
  no operation moved by 1% of the time
where the time goes in v17:
time: 172 us
  waiting for transfers between devices  74.6 us (43%)
  Pallas kernels  50 us (29%)
  starting transfers between devices  43 us (25%)
  other arithmetic  2.79 us (2%)
    ppermute x34, waiting for transfers between devices, send(): return lax.ppermute(value, 'dp', every)  72.5 us
    ppermute x34, starting transfers between devices, send(): return lax.ppermute(value, 'dp', every)  41.5 us
    pallas_call x1, Pallas kernels, place(): pl.pallas_call(functools.partial(place_kernel, plan), out_shape=[jax.Shap...  21.4 us
    pallas_call x1, Pallas kernels, finish(): pl.pallas_call(functools.partial(finish_kernel, plan, tile, slots), grid=...  19.6 us
    pallas_call x1, Pallas kernels, owned(): pl.pallas_call(functools.partial(owned_kernel, plan), out_shape=[jax.Shap...  6.32 us
  transfers between devices with their start and end apart: 35, of which 18 were waited for; matrix products, arithmetic and copies ran while one was open for 1% of the time, Pallas kernels for 4%

profile of v17, /device:TPU:0, one launch (start us, length us, event | category | flops | bytes accessed | tf_op | source)
XLA Modules:
  0.0 171.6 jit_solution(11065460946283267615)
XLA Ops:
  0.7 0.6 pad_add_fusion.place_ref
  1.2 21.4 %place_gradients.1 = (f32[1096,128]{1,0:T(8,128)}, f32[1096,128]{1,0:T(8,128)}, f32[1096,128]{1,0:T(8,128)}, f32[1096,128]{1,0:T(8,128)}, f32[1096,128]{1,0:T(8,...) custom-call(s32[3]{0:T(128)} %pad_add_fusion.place_ref, ...), custom_call_target="tpu_custom_call" | custom-call | tf_op jit(solution)/shard_map/place_gradients/pallas_call | solution.py:313
  22.7 0.5 collective-permute-start
  23.2 1.8 %collective-permute-done = f32[1096,128]{1,0:T(8,128)S(1)} collective-permute-done((f32[1096,128]{1,0:T(8,128)}, f32[1096,128]{1,0:T(8,128)S(1)}, u32[]{:S(2)}, u32[]{:S(2)}) %collective-permute-start) | collective-permute-done | bytes 561184 | tf_op jit(solution)/shard_map/ppermute | solution.py:79
  25.0 1.1 add.68
  26.1 0.4 collective-permute-start.8
  26.6 0.1 collective-permute-start.4
  26.7 2.9 %collective-permute-start.5 = (f32[1096,128]{1,0:T(8,128)S(1)}, f32[1096,128]{1,0:T(8,128)S(1)}, u32[]{:S(2)}, u32[]{:S(2)}) collective-permute-start(f32[1096,128]{1,0:T(8,128)S(1)} %add.68), channel_id=1, source_target_pairs={{0,4},{2,6},{4,0},{6,2},{8,12},{10,14},{12,8},{14,10},{16,20},{18,... | collective-permute-start | bytes 1683464 | tf_op jit(solution)/shard_map/ppermute | solution.py:79
  29.6 0.5 collective-permute-start.7
  30.1 0.1 add.74
  30.2 1.2 collective-permute-start.9
  31.4 11.7 %collective-permute-done.5 = f32[1096,128]{1,0:T(8,128)S(1)} collective-permute-done((f32[1096,128]{1,0:T(8,128)S(1)}, f32[1096,128]{1,0:T(8,128)S(1)}, u32[]{:S(2)}, u32[]{:S(2)}) %collective-permute-start.5) | collective-permute-done | bytes 561184 | tf_op jit(solution)/shard_map/ppermute | solution.py:79
  43.0 0.1 add_add_fusion.2
  43.2 4.2 %collective-permute-start.6 = (f32[1096,128]{1,0:T(8,128)S(1)}, f32[1096,128]{1,0:T(8,128)S(1)}, u32[]{:S(2)}, u32[]{:S(2)}) collective-permute-start(f32[1096,128]{1,0:T(8,128)S(1)} %add_add_fusion.2), channel_id=1, source_target_pairs={{0,8},{2,10},{4,12},{6,14},{24,16},{26,18},{28,20},{30,22},{1,9},{... | collective-permute-start | bytes 1683464 | tf_op jit(solution)/shard_map/ppermute | solution.py:79
  47.4 6.3 %owned_weights.1 = (f32[1088,128]{1,0:T(8,128)}, s32[1152,128]{1,0:T(8,128)}) custom-call(s32[3]{0:T(128)} %pad_add_fusion.place_ref, s32[136,128]{1,0:T(8,128)} %bitcast.16, f32[17408,128]{1,0:T(8,128)} %weights_ref.3), custom_call_target="tpu_custom_call" | custom-call | bytes 20971520 | tf_op jit(solution)/shard_map/owned_weights/pallas_call | solution.py:391
  53.9 0.5 collective-permute-start.12
  54.4 1.6 collective-permute-start.14
  56.0 0.1 add_add_fusion.1
  56.1 1.9 %collective-permute-done.6 = f32[1096,128]{1,0:T(8,128)S(1)} collective-permute-done((f32[1096,128]{1,0:T(8,128)S(1)}, f32[1096,128]{1,0:T(8,128)S(1)}, u32[]{:S(2)}, u32[]{:S(2)}) %collective-permute-start.6) | collective-permute-done | bytes 561184 | tf_op jit(solution)/shard_map/ppermute | solution.py:79
  58.0 0.1 add.76
  58.1 0.8 collective-permute-start.10
  58.9 7.2 %collective-permute-start.11 = (f32[1096,128]{1,0:T(8,128)S(1)}, f32[1096,128]{1,0:T(8,128)S(1)}, u32[]{:S(2)}, u32[]{:S(2)}) collective-permute-start(f32[1096,128]{1,0:T(8,128)S(1)} %add_add_fusion.1), channel_id=1, source_target_pairs={{0,8},{2,10},{4,12},{6,14},{24,16},{26,18},{28,20},{30,22},{1,9},{... | collective-permute-start | bytes 1683464 | tf_op jit(solution)/shard_map/ppermute | solution.py:79
  66.2 0.1 collective-permute-start.1
  66.3 0.1 add.70
  66.3 1.6 collective-permute-start.3
  67.9 1.3 collective-permute-done.14
  69.2 0.1 add_add_fusion
  69.3 6.9 %collective-permute-done.11 = f32[1096,128]{1,0:T(8,128)S(1)} collective-permute-done((f32[1096,128]{1,0:T(8,128)S(1)}, f32[1096,128]{1,0:T(8,128)S(1)}, u32[]{:S(2)}, u32[]{:S(2)}) %collective-permute-start.11) | collective-permute-done | bytes 561184 | tf_op jit(solution)/shard_map/ppermute | solution.py:79
  76.4 2.5 %collective-permute-start.15 = (f32[1096,128]{1,0:T(8,128)S(1)}, f32[1096,128]{1,0:T(8,128)S(1)}, u32[]{:S(2)}, u32[]{:S(2)}) collective-permute-start(f32[1096,128]{1,0:T(8,128)S(1)} %add.80), channel_id=1, source_target_pairs={{0,8},{2,10},{4,12},{6,14},{8,0},{10,2},{12,4},{14,6},{16,24},{18,... | collective-permute-start | bytes 1683464 | tf_op jit(solution)/shard_map/ppermute | solution.py:79
  79.0 0.7 collective-permute-start.16
  79.7 0.1 add.69.refs_0_
  79.8 1.7 %collective-permute-done.3.refs_1_ = f32[1096,128]{1,0:T(8,128)S(1)} collective-permute-done((f32[1096,128]{1,0:T(8,128)S(1)}, f32[1096,128]{1,0:T(8,128)S(1)}, u32[]{:S(2)}, u32[]{:S(2)}) %collective-permute-start.3) | collective-permute-done | bytes 561184 | tf_op jit(solution)/shard_map/ppermute | solution.py:79
  81.5 6.0 %collective-permute-done.15.refs_2_ = f32[1096,128]{1,0:T(8,128)S(1)} collective-permute-done((f32[1096,128]{1,0:T(8,128)S(1)}, f32[1096,128]{1,0:T(8,128)S(1)}, u32[]{:S(2)}, u32[]{:S(2)}) %collective-permute-start.15) | collective-permute-done | bytes 561184 | tf_op jit(solution)/shard_map/ppermute | solution.py:79
  87.6 2.0 %moments.1 = (f32[1088,128]{1,0:T(8,128)}, f32[1088,128]{1,0:T(8,128)}, f32[1096,128]{1,0:T(8,128)S(1)}) custom-call(f32[1096,128]{1,0:T(8,128)S(1)} %add.69.refs_0_, f32[1096,128]{1,0:T(8,128)S(1)} %collective-permute-done.3.refs_1_, f32[1096,128]{1,0:T(8,128)S(1)} %collective-permute-done.15.refs_2_, f32[1096,128]{1,0:T(8,128)S(1)} %collective-permute-done.16.refs_3_, ...), custom_call_target="tpu_custom_call" | custom-call | tf_op jit(solution)/shard_map/moments/pallas_call | solution.py:445
  89.7 3.8 %collective-permute-start.18 = (f32[1096,128]{1,0:T(8,128)S(1)}, f32[1096,128]{1,0:T(8,128)S(1)}, u32[]{:S(2)}, u32[]{:S(2)}) collective-permute-start(f32[1096,128]{1,0:T(8,128)S(1)} %get-tuple-element.92), channel_id=1, source_target_pairs={{0,8},{2,10},{4,12},{6,14},{8,0},{10,2},{12,4},{14,6},{16,24},{18,... | collective-permute-start | bytes 1683464 | tf_op jit(solution)/shard_map/ppermute | solution.py:79
  93.5 1.5 collective-permute-start.19
  95.0 0.7 collective-permute-start.17
  95.6 5.4 %collective-permute-done.18 = f32[1096,128]{1,0:T(8,128)S(1)} collective-permute-done((f32[1096,128]{1,0:T(8,128)S(1)}, f32[1096,128]{1,0:T(8,128)S(1)}, u32[]{:S(2)}, u32[]{:S(2)}) %collective-permute-start.18) | collective-permute-done | bytes 561184 | tf_op jit(solution)/shard_map/ppermute | solution.py:79
  101.1 1.5 collective-permute-start.24
  102.6 0.7 collective-permute-start.20
  103.3 0.1 pad_maximum_fusion.refs_0_.refs_1_
  103.4 4.9 %collective-permute-done.19 = f32[1096,128]{1,0:T(8,128)S(1)} collective-permute-done((f32[1096,128]{1,0:T(8,128)S(1)}, f32[1096,128]{1,0:T(8,128)S(1)}, u32[]{:S(2)}, u32[]{:S(2)}) %collective-permute-start.19) | collective-permute-done | bytes 561184 | tf_op jit(solution)/shard_map/ppermute | solution.py:79
  108.3 1.3 collective-permute-start.23
  109.6 1.3 collective-permute-start.21
  110.9 6.4 %collective-permute-done.24 = f32[1096,128]{1,0:T(8,128)S(1)} collective-permute-done((f32[1096,128]{1,0:T(8,128)S(1)}, f32[1096,128]{1,0:T(8,128)S(1)}, u32[]{:S(2)}, u32[]{:S(2)}) %collective-permute-start.24) | collective-permute-done | bytes 561184 | tf_op jit(solution)/shard_map/ppermute | solution.py:79
  117.3 5.5 %collective-permute-done.23 = f32[1096,128]{1,0:T(8,128)S(1)} collective-permute-done((f32[1096,128]{1,0:T(8,128)S(1)}, f32[1096,128]{1,0:T(8,128)S(1)}, u32[]{:S(2)}, u32[]{:S(2)}) %collective-permute-start.23) | collective-permute-done | bytes 561184 | tf_op jit(solution)/shard_map/ppermute | solution.py:79
  122.8 0.1 add.83.refs_2_
  122.9 0.1 pad_maximum_fusion.1.refs_1_
  123.0 2.5 %collective-permute-start.26 = (f32[1096,128]{1,0:T(8,128)S(1)}, f32[1096,128]{1,0:T(8,128)S(1)}, u32[]{:S(2)}, u32[]{:S(2)}) collective-permute-start(f32[1096,128]{1,0:T(8,128)S(1)} %add.83.refs_2_), channel_id=1, source_target_pairs={{0,4},{2,6},{4,0},{6,2},{8,12},{10,14},{12,8},{14,10},{16,20},{18,... | collective-permute-start | bytes 1683464 | tf_op jit(solution)/shard_map/ppermute | solution.py:79
  125.5 6.3 %collective-permute-done.21 = f32[1096,128]{1,0:T(8,128)S(1)} collective-permute-done((f32[1096,128]{1,0:T(8,128)S(1)}, f32[1096,128]{1,0:T(8,128)S(1)}, u32[]{:S(2)}, u32[]{:S(2)}) %collective-permute-start.21) | collective-permute-done | bytes 561184 | tf_op jit(solution)/shard_map/ppermute | solution.py:79
  131.9 0.6 sums.1
  132.4 1.6 collective-permute-start.25
  134.0 0.5 collective-permute-start.29
  134.5 0.2 collective-permute-start.22
  134.8 1.3 collective-permute-done.25
  136.1 0.5 collective-permute-start.27
  136.6 2.5 %collective-permute-done.27 = f32[8,128]{1,0:T(8,128)S(1)} collective-permute-done((f32[8,128]{1,0:T(8,128)S(1)}, f32[8,128]{1,0:T(8,128)S(1)}, u32[]{:S(2)}, u32[]{:S(2)}) %collective-permute-start.27) | collective-permute-done | bytes 4128 | tf_op jit(solution)/shard_map/ppermute | solution.py:79
  139.2 1.5 collective-permute-start.28
  140.7 2.1 %collective-permute-done.28 = f32[8,128]{1,0:T(8,128)S(1)} collective-permute-done((f32[8,128]{1,0:T(8,128)S(1)}, f32[8,128]{1,0:T(8,128)S(1)}, u32[]{:S(2)}, u32[]{:S(2)}) %collective-permute-start.28) | collective-permute-done | bytes 4128 | tf_op jit(solution)/shard_map/ppermute | solution.py:165
  142.8 6.3 %collective-permute-done.29.refs_5_ = f32[1096,128]{1,0:T(8,128)S(1)} collective-permute-done((f32[1096,128]{1,0:T(8,128)S(1)}, f32[1096,128]{1,0:T(8,128)S(1)}, u32[]{:S(2)}, u32[]{:S(2)}) %collective-permute-start.29) | collective-permute-done | bytes 561184 | tf_op jit(solution)/shard_map/ppermute | solution.py:79
  149.1 0.5 collective-permute-start.34
  149.7 1.4 collective-permute-done.33.refs_9_
  151.1 0.8 collective-permute-done.34.refs_11_
  151.9 19.6 %new_weights.1 = (f32[17408,128]{1,0:T(8,128)}, f32[3,2,1024]{2,1,0:T(2,128)}, f32[7]{0:T(128)}) custom-call(s32[3]{0:T(128)S(1)} %copy-done.6, s32[136,128]{1,0:T(8,128)S(1)} %copy-done.4, f32[8,128]{1,0:T(8,128)S(1)} %add.86.total_ref, f32[3,2,1024]{2,1,0:T(2,128)S(1)} %copy-done.5, f32[17408,128]{1,0:T(8,128)S(1)} %bitcast.11, ...), custom_call_target="tpu_custom_call" | custom-call | tf_op jit(solution)/shard_map/new_weights/pallas_call | solution.py:523
  (75 shorter events, 0.5 us)
Async XLA Ops:
  22.6 6.9 %copy-start.18 = (f32[1096,128]{1,0:T(8,128)S(1)}, f32[1096,128]{1,0:T(8,128)}, u32[]{:S(2)}) copy-start(f32[1096,128]{1,0:T(8,128)} %get-tuple-element.86) | copy-start | bytes 1683460
  22.7 6.9 %copy-start.17 = (f32[1096,128]{1,0:T(8,128)S(1)}, f32[1096,128]{1,0:T(8,128)}, u32[]{:S(2)}) copy-start(f32[1096,128]{1,0:T(8,128)} %get-tuple-element.76) | copy-start | bytes 1683460
  22.7 7.4 %copy-start.13 = (f32[1096,128]{1,0:T(8,128)S(1)}, f32[1096,128]{1,0:T(8,128)}, u32[]{:S(2)}) copy-start(f32[1096,128]{1,0:T(8,128)} %get-tuple-element.77) | copy-start | bytes 1683460
  22.7 2.3 %collective-permute-start = (f32[1096,128]{1,0:T(8,128)}, f32[1096,128]{1,0:T(8,128)S(1)}, u32[]{:S(2)}, u32[]{:S(2)}) collective-permute-start(f32[1096,128]{1,0:T(8,128)} %get-tuple-element.61), channel_id=1, source_target_pairs={{0,2},{2,0},{4,6},{6,4},{8,10},{10,8},{12,14},{14,12},{16,18},{18,... | collective-permute-start | bytes 1683464 | tf_op jit(solution)/shard_map/ppermute | solution.py:79
  26.1 16.9 %copy-start.12 = (f32[1096,128]{1,0:T(8,128)S(1)}, f32[1096,128]{1,0:T(8,128)}, u32[]{:S(2)}) copy-start(f32[1096,128]{1,0:T(8,128)} %get-tuple-element.72) | copy-start | bytes 1683460
  26.1 4.0 %collective-permute-start.8 = (f32[1096,128]{1,0:T(8,128)}, f32[1096,128]{1,0:T(8,128)S(1)}, u32[]{:S(2)}, u32[]{:S(2)}) collective-permute-start(f32[1096,128]{1,0:T(8,128)} %get-tuple-element.78), channel_id=1, source_target_pairs={{0,2},{2,0},{4,6},{6,4},{8,10},{10,8},{12,14},{14,12},{16,18},{18,... | collective-permute-start | bytes 1683464 | tf_op jit(solution)/shard_map/ppermute | solution.py:79
  26.6 4.8 %collective-permute-start.4 = (f32[1096,128]{1,0:T(8,128)}, f32[1096,128]{1,0:T(8,128)S(1)}, u32[]{:S(2)}, u32[]{:S(2)}) collective-permute-start(f32[1096,128]{1,0:T(8,128)} %get-tuple-element.73), channel_id=1, source_target_pairs={{0,2},{2,0},{4,6},{6,4},{8,10},{10,8},{12,14},{14,12},{16,18},{18,... | collective-permute-start | bytes 1683464 | tf_op jit(solution)/shard_map/ppermute | solution.py:79
  26.7 16.4 %collective-permute-start.5 = (f32[1096,128]{1,0:T(8,128)S(1)}, f32[1096,128]{1,0:T(8,128)S(1)}, u32[]{:S(2)}, u32[]{:S(2)}) collective-permute-start(f32[1096,128]{1,0:T(8,128)S(1)} %add.68), channel_id=1, source_target_pairs={{0,4},{2,6},{4,0},{6,2},{8,12},{10,14},{12,8},{14,10},{16,20},{18,... | collective-permute-start | bytes 1683464 | tf_op jit(solution)/shard_map/ppermute | solution.py:79
  29.6 24.3 %collective-permute-start.13 = (f32[1096,128]{1,0:T(8,128)S(1)}, f32[1096,128]{1,0:T(8,128)S(1)}, u32[]{:S(2)}, u32[]{:S(2)}) collective-permute-start(f32[1096,128]{1,0:T(8,128)S(1)} %copy-done.18), channel_id=1, source_target_pairs={{0,2},{2,0},{4,6},{6,4},{8,10},{10,8},{12,14},{14,12},{16,18},{18,... | collective-permute-start | bytes 1683464 | tf_op jit(solution)/shard_map/ppermute | solution.py:79
  29.6 24.9 %collective-permute-start.7 = (f32[1096,128]{1,0:T(8,128)S(1)}, f32[1096,128]{1,0:T(8,128)S(1)}, u32[]{:S(2)}, u32[]{:S(2)}) collective-permute-start(f32[1096,128]{1,0:T(8,128)S(1)} %copy-done.17), channel_id=1, source_target_pairs={{0,2},{2,0},{4,6},{6,4},{8,10},{10,8},{12,14},{14,12},{16,18},{18,... | collective-permute-start | bytes 1683464 | tf_op jit(solution)/shard_map/ppermute | solution.py:79
  30.2 25.8 %collective-permute-start.9 = (f32[1096,128]{1,0:T(8,128)S(1)}, f32[1096,128]{1,0:T(8,128)S(1)}, u32[]{:S(2)}, u32[]{:S(2)}) collective-permute-start(f32[1096,128]{1,0:T(8,128)S(1)} %add.74), channel_id=1, source_target_pairs={{0,4},{2,6},{4,0},{6,2},{8,12},{10,14},{12,8},{14,10},{16,20},{18,... | collective-permute-start | bytes 1683464 | tf_op jit(solution)/shard_map/ppermute | solution.py:79
  43.2 10.6 %copy-start.16 = (f32[1096,128]{1,0:T(8,128)S(1)}, f32[1096,128]{1,0:T(8,128)}, u32[]{:S(2)}) copy-start(f32[1096,128]{1,0:T(8,128)} %get-tuple-element.71) | copy-start | bytes 1683460
  43.2 10.7 %copy-start.15 = (f32[1096,128]{1,0:T(8,128)S(1)}, f32[1096,128]{1,0:T(8,128)}, u32[]{:S(2)}) copy-start(f32[1096,128]{1,0:T(8,128)} %get-tuple-element.84) | copy-start | bytes 1683460
  43.2 11.2 %copy-start.11 = (f32[1096,128]{1,0:T(8,128)S(1)}, f32[1096,128]{1,0:T(8,128)}, u32[]{:S(2)}) copy-start(f32[1096,128]{1,0:T(8,128)} %get-tuple-element.85) | copy-start | bytes 1683460
  43.2 14.8 %collective-permute-start.6 = (f32[1096,128]{1,0:T(8,128)S(1)}, f32[1096,128]{1,0:T(8,128)S(1)}, u32[]{:S(2)}, u32[]{:S(2)}) collective-permute-start(f32[1096,128]{1,0:T(8,128)S(1)} %add_add_fusion.2), channel_id=1, source_target_pairs={{0,8},{2,10},{4,12},{6,14},{24,16},{26,18},{28,20},{30,22},{1,9},{... | collective-permute-start | bytes 1683464 | tf_op jit(solution)/shard_map/ppermute | solution.py:79
  53.8 2.2 %copy-start.10 = (f32[1096,128]{1,0:T(8,128)S(1)}, f32[1096,128]{1,0:T(8,128)}, u32[]{:S(2)}) copy-start(f32[1096,128]{1,0:T(8,128)} %get-tuple-element.75) | copy-start | bytes 1683460
  53.8 12.4 %collective-permute-start.2 = (f32[1096,128]{1,0:T(8,128)S(1)}, f32[1096,128]{1,0:T(8,128)S(1)}, u32[]{:S(2)}, u32[]{:S(2)}) collective-permute-start(f32[1096,128]{1,0:T(8,128)S(1)} %copy-done.16), channel_id=1, source_target_pairs={{0,2},{2,0},{4,6},{6,4},{8,10},{10,8},{12,14},{14,12},{16,18},{18,... | collective-permute-start | bytes 1683464 | tf_op jit(solution)/shard_map/ppermute | solution.py:79
  53.9 12.5 %collective-permute-start.12 = (f32[1096,128]{1,0:T(8,128)S(1)}, f32[1096,128]{1,0:T(8,128)S(1)}, u32[]{:S(2)}, u32[]{:S(2)}) collective-permute-start(f32[1096,128]{1,0:T(8,128)S(1)} %copy-done.15), channel_id=1, source_target_pairs={{0,2},{2,0},{4,6},{6,4},{8,10},{10,8},{12,14},{14,12},{16,18},{18,... | collective-permute-start | bytes 1683464 | tf_op jit(solution)/shard_map/ppermute | solution.py:79
  54.4 14.8 %collective-permute-start.14 = (f32[1096,128]{1,0:T(8,128)S(1)}, f32[1096,128]{1,0:T(8,128)S(1)}, u32[]{:S(2)}, u32[]{:S(2)}) collective-permute-start(f32[1096,128]{1,0:T(8,128)S(1)} %add.78), channel_id=1, source_target_pairs={{0,4},{2,6},{4,0},{6,2},{8,12},{10,14},{12,8},{14,10},{16,20},{18,... | collective-permute-start | bytes 1683464 | tf_op jit(solution)/shard_map/ppermute | solution.py:79
  56.1 10.1 %copy-start.14 = (f32[1096,128]{1,0:T(8,128)S(1)}, f32[1096,128]{1,0:T(8,128)}, u32[]{:S(2)}) copy-start(f32[1096,128]{1,0:T(8,128)} %get-tuple-element.69) | copy-start | bytes 1683460
  56.1 10.1 %copy-start.9 = (f32[1096,128]{1,0:T(8,128)S(1)}, f32[1096,128]{1,0:T(8,128)}, u32[]{:S(2)}) copy-start(f32[1096,128]{1,0:T(8,128)} %get-tuple-element.70) | copy-start | bytes 1683460
  58.1 11.1 %copy-start.8 = (f32[1096,128]{1,0:T(8,128)S(1)}, f32[1096,128]{1,0:T(8,128)}, u32[]{:S(2)}) copy-start(f32[1096,128]{1,0:T(8,128)} %get-tuple-element.83) | copy-start | bytes 1683460
  58.1 11.2 %collective-permute-start.10 = (f32[1096,128]{1,0:T(8,128)S(1)}, f32[1096,128]{1,0:T(8,128)S(1)}, u32[]{:S(2)}, u32[]{:S(2)}) collective-permute-start(f32[1096,128]{1,0:T(8,128)S(1)} %add.76), channel_id=1, source_target_pairs={{8,16},{10,18},{12,20},{14,22},{16,8},{18,10},{20,12},{22,14},{9,1... | collective-permute-start | bytes 1683464 | tf_op jit(solution)/shard_map/ppermute | solution.py:79
  58.9 17.3 %collective-permute-start.11 = (f32[1096,128]{1,0:T(8,128)S(1)}, f32[1096,128]{1,0:T(8,128)S(1)}, u32[]{:S(2)}, u32[]{:S(2)}) collective-permute-start(f32[1096,128]{1,0:T(8,128)S(1)} %add_add_fusion.1), channel_id=1, source_target_pairs={{0,8},{2,10},{4,12},{6,14},{24,16},{26,18},{28,20},{30,22},{1,9},{... | collective-permute-start | bytes 1683464 | tf_op jit(solution)/shard_map/ppermute | solution.py:79
  66.2 13.5 %collective-permute-start.1 = (f32[1096,128]{1,0:T(8,128)S(1)}, f32[1096,128]{1,0:T(8,128)S(1)}, u32[]{:S(2)}, u32[]{:S(2)}) collective-permute-start(f32[1096,128]{1,0:T(8,128)S(1)} %copy-done.14), channel_id=1, source_target_pairs={{0,2},{2,0},{4,6},{6,4},{8,10},{10,8},{12,14},{14,12},{16,18},{18,... | collective-permute-start | bytes 1683464 | tf_op jit(solution)/shard_map/ppermute | solution.py:79
  66.3 15.2 %collective-permute-start.3 = (f32[1096,128]{1,0:T(8,128)S(1)}, f32[1096,128]{1,0:T(8,128)S(1)}, u32[]{:S(2)}, u32[]{:S(2)}) collective-permute-start(f32[1096,128]{1,0:T(8,128)S(1)} %add.70), channel_id=1, source_target_pairs={{0,4},{2,6},{4,0},{6,2},{8,12},{10,14},{12,8},{14,10},{16,20},{18,... | collective-permute-start | bytes 1683464 | tf_op jit(solution)/shard_map/ppermute | solution.py:79
  69.2 82.7 %slice-start = ((s8[8912896]{0:T(1024)(128)(4,1)}), s8[4194304]{0:T(1024)(128)(4,1)S(1)}, s32[]{:S(2)}) async-start(s8[8912896]{0:T(1024)(128)(4,1)} %bitcast.10), calls=%async_computation | async-start | bytes 8388608
  76.2 3.4 %copy-start.7 = (f32[1096,128]{1,0:T(8,128)S(1)}, f32[1096,128]{1,0:T(8,128)}, u32[]{:S(2)}) copy-start(f32[1096,128]{1,0:T(8,128)} %get-tuple-element.59) | copy-start | bytes 1683460
  76.3 11.3 %copy-start.2 = (f32[1,1088,128]{2,1,0:T(8,128)S(1)}, f32[1,1088,128]{2,1,0:T(8,128)}, u32[]{:S(2)}) copy-start(f32[1,1088,128]{2,1,0:T(8,128)} %param.10) | copy-start | bytes 1671172
  76.3 11.2 %copy-start.3 = (f32[1088,128]{1,0:T(8,128)S(1)}, f32[1088,128]{1,0:T(8,128)}, u32[]{:S(2)}) copy-start(f32[1088,128]{1,0:T(8,128)} %get-tuple-element.90.refs_6_) | copy-start | bytes 1671172
  76.4 11.2 %copy-start = (s32[1152,128]{1,0:T(8,128)S(1)}, s32[1152,128]{1,0:T(8,128)}, u32[]{:S(2)}) copy-start(s32[1152,128]{1,0:T(8,128)} %get-tuple-element.91.refs_7_) | copy-start | bytes 1769476
  76.4 11.2 %copy-start.1 = (f32[1,1088,128]{2,1,0:T(8,128)S(1)}, f32[1,1088,128]{2,1,0:T(8,128)}, u32[]{:S(2)}) copy-start(f32[1,1088,128]{2,1,0:T(8,128)} %param.9) | copy-start | bytes 1671172
  76.4 11.1 %collective-permute-start.15 = (f32[1096,128]{1,0:T(8,128)S(1)}, f32[1096,128]{1,0:T(8,128)S(1)}, u32[]{:S(2)}, u32[]{:S(2)}) collective-permute-start(f32[1096,128]{1,0:T(8,128)S(1)} %add.80), channel_id=1, source_target_pairs={{0,8},{2,10},{4,12},{6,14},{8,0},{10,2},{12,4},{14,6},{16,24},{18,... | collective-permute-start | bytes 1683464 | tf_op jit(solution)/shard_map/ppermute | solution.py:79
  79.0 8.6 %collective-permute-start.16 = (f32[1096,128]{1,0:T(8,128)S(1)}, f32[1096,128]{1,0:T(8,128)S(1)}, u32[]{:S(2)}, u32[]{:S(2)}) collective-permute-start(f32[1096,128]{1,0:T(8,128)S(1)} %add.81), channel_id=1, source_target_pairs={{8,16},{10,18},{12,20},{14,22},{16,8},{18,10},{20,12},{22,14},{9,1... | collective-permute-start | bytes 1683464 | tf_op jit(solution)/shard_map/ppermute | solution.py:79
  87.6 64.3 %slice-start.1 = ((s8[8912896]{0:T(1024)(128)(4,1)}), s8[4194304]{0:T(1024)(128)(4,1)S(1)}, s32[]{:S(2)}) async-start(s8[8912896]{0:T(1024)(128)(4,1)} %bitcast.10), calls=%async_computation.1 | async-start | bytes 8388608
  89.7 11.4 %collective-permute-start.18 = (f32[1096,128]{1,0:T(8,128)S(1)}, f32[1096,128]{1,0:T(8,128)S(1)}, u32[]{:S(2)}, u32[]{:S(2)}) collective-permute-start(f32[1096,128]{1,0:T(8,128)S(1)} %get-tuple-element.92), channel_id=1, source_target_pairs={{0,8},{2,10},{4,12},{6,14},{8,0},{10,2},{12,4},{14,6},{16,24},{18,... | collective-permute-start | bytes 1683464 | tf_op jit(solution)/shard_map/ppermute | solution.py:79
  93.5 14.8 %collective-permute-start.19 = (f32[1096,128]{1,0:T(8,128)S(1)}, f32[1096,128]{1,0:T(8,128)S(1)}, u32[]{:S(2)}, u32[]{:S(2)}) collective-permute-start(f32[1096,128]{1,0:T(8,128)S(1)} %get-tuple-element.92), channel_id=1, source_target_pairs={{0,4},{2,6},{4,0},{6,2},{8,12},{10,14},{12,8},{14,10},{16,20},{18,... | collective-permute-start | bytes 1683464 | tf_op jit(solution)/shard_map/ppermute | solution.py:79
  95.0 13.4 %collective-permute-start.17 = (f32[1096,128]{1,0:T(8,128)S(1)}, f32[1096,128]{1,0:T(8,128)S(1)}, u32[]{:S(2)}, u32[]{:S(2)}) collective-permute-start(f32[1096,128]{1,0:T(8,128)S(1)} %get-tuple-element.92), channel_id=1, source_target_pairs={{8,16},{10,18},{12,20},{14,22},{16,8},{18,10},{20,12},{22,14},{9,1... | collective-permute-start | bytes 1683464 | tf_op jit(solution)/shard_map/ppermute | solution.py:79
  101.1 16.2 %collective-permute-start.24 = (f32[1096,128]{1,0:T(8,128)S(1)}, f32[1096,128]{1,0:T(8,128)S(1)}, u32[]{:S(2)}, u32[]{:S(2)}) collective-permute-start(f32[1096,128]{1,0:T(8,128)S(1)} %collective-permute-done.18), channel_id=1, source_target_pairs={{0,4},{2,6},{4,0},{6,2},{8,12},{10,14},{12,8},{14,10},{16,20},{18,... | collective-permute-start | bytes 1683464 | tf_op jit(solution)/shard_map/ppermute | solution.py:79
  102.6 7.0 %collective-permute-start.20 = (f32[1096,128]{1,0:T(8,128)S(1)}, f32[1096,128]{1,0:T(8,128)S(1)}, u32[]{:S(2)}, u32[]{:S(2)}) collective-permute-start(f32[1096,128]{1,0:T(8,128)S(1)} %collective-permute-done.18), channel_id=1, source_target_pairs={{8,16},{10,18},{12,20},{14,22},{16,8},{18,10},{20,12},{22,14},{9,1... | collective-permute-start | bytes 1683464 | tf_op jit(solution)/shard_map/ppermute | solution.py:79
  103.4 48.5 %slice-start.2 = ((s8[8912896]{0:T(1024)(128)(4,1)}), s8[524288]{0:T(1024)(128)(4,1)S(1)}, s32[]{:S(2)}) async-start(s8[8912896]{0:T(1024)(128)(4,1)} %bitcast.10), calls=%async_computation.2 | async-start | bytes 1048576
  108.3 14.5 %collective-permute-start.23 = (f32[1096,128]{1,0:T(8,128)S(1)}, f32[1096,128]{1,0:T(8,128)S(1)}, u32[]{:S(2)}, u32[]{:S(2)}) collective-permute-start(f32[1096,128]{1,0:T(8,128)S(1)} %collective-permute-done.17), channel_id=1, source_target_pairs={{8,0},{10,2},{12,4},{14,6},{16,24},{18,26},{20,28},{22,30},{9,1},{... | collective-permute-start | bytes 1683464 | tf_op jit(solution)/shard_map/ppermute | solution.py:79
  109.6 22.2 %collective-permute-start.21 = (f32[1096,128]{1,0:T(8,128)S(1)}, f32[1096,128]{1,0:T(8,128)S(1)}, u32[]{:S(2)}, u32[]{:S(2)}) collective-permute-start(f32[1096,128]{1,0:T(8,128)S(1)} %collective-permute-done.20), channel_id=1, source_target_pairs={{8,0},{10,2},{12,4},{14,6},{16,24},{18,26},{20,28},{22,30},{9,1},{... | collective-permute-start | bytes 1683464 | tf_op jit(solution)/shard_map/ppermute | solution.py:79
  123.0 8.9 %copy-start.6 = (s32[3]{0:T(128)S(1)}, s32[3]{0:T(128)}, u32[]{:S(2)}) copy-start(s32[3]{0:T(128)} %pad_add_fusion.place_ref) | copy-start | bytes 40
  123.0 13.1 %collective-permute-start.26 = (f32[1096,128]{1,0:T(8,128)S(1)}, f32[1096,128]{1,0:T(8,128)S(1)}, u32[]{:S(2)}, u32[]{:S(2)}) collective-permute-start(f32[1096,128]{1,0:T(8,128)S(1)} %add.83.refs_2_), channel_id=1, source_target_pairs={{0,4},{2,6},{4,0},{6,2},{8,12},{10,14},{12,8},{14,10},{16,20},{18,... | collective-permute-start | bytes 1683464 | tf_op jit(solution)/shard_map/ppermute | solution.py:79
  131.9 20.0 %copy-start.4 = (s32[136,128]{1,0:T(8,128)S(1)}, s32[136,128]{1,0:T(8,128)}, u32[]{:S(2)}) copy-start(s32[136,128]{1,0:T(8,128)} %get-tuple-element.58.position_ref) | copy-start | bytes 208900
  131.9 20.0 %copy-start.5 = (f32[3,2,1024]{2,1,0:T(2,128)S(1)}, f32[3,2,1024]{2,1,0:T(2,128)}, u32[]{:S(2)}) copy-start(f32[3,2,1024]{2,1,0:T(2,128)} %norm_ref.1) | copy-start | bytes 73732
  132.4 3.7 %collective-permute-start.25 = (f32[8,128]{1,0:T(8,128)S(1)}, f32[8,128]{1,0:T(8,128)S(1)}, u32[]{:S(2)}, u32[]{:S(2)}) collective-permute-start(f32[8,128]{1,0:T(8,128)S(1)} %sums.1), channel_id=1, source_target_pairs={{0,4},{2,6},{4,0},{6,2},{8,12},{10,14},{12,8},{14,10},{16,20},{18,... | collective-permute-start | bytes 12296 | tf_op jit(solution)/shard_map/ppermute | solution.py:79
  134.0 15.6 %collective-permute-start.30 = (f32[2192,128]{1,0:T(8,128)S(1)}, f32[2192,128]{1,0:T(8,128)S(1)}, u32[]{:S(2)}, u32[]{:S(2)}) collective-permute-start(f32[2192,128]{1,0:T(8,128)S(1)} %pad_maximum_fusion.refs_0_.refs_1_), channel_id=1, source_target_pairs={{0,2},{2,0},{4,6},{6,4},{8,10},{10,8},{12,14},{14,12},{16,18},{18,... | collective-permute-start | bytes 3366920 | tf_op jit(solution)/shard_map/ppermute | solution.py:79
  134.0 15.1 %collective-permute-start.29 = (f32[1096,128]{1,0:T(8,128)S(1)}, f32[1096,128]{1,0:T(8,128)S(1)}, u32[]{:S(2)}, u32[]{:S(2)}) collective-permute-start(f32[1096,128]{1,0:T(8,128)S(1)} %add.82.refs_3_.refs_4_), channel_id=1, source_target_pairs={{0,4},{2,6},{4,0},{6,2},{8,12},{10,14},{12,8},{14,10},{16,20},{18,... | collective-permute-start | bytes 1683464 | tf_op jit(solution)/shard_map/ppermute | solution.py:79
  134.5 14.6 %collective-permute-start.22 = (f32[1096,128]{1,0:T(8,128)S(1)}, f32[1096,128]{1,0:T(8,128)S(1)}, u32[]{:S(2)}, u32[]{:S(2)}) collective-permute-start(f32[1096,128]{1,0:T(8,128)S(1)} %add.82.refs_3_.refs_4_), channel_id=1, source_target_pairs={{0,2},{2,0},{4,6},{6,4},{8,10},{10,8},{12,14},{14,12},{16,18},{18,... | collective-permute-start | bytes 1683464 | tf_op jit(solution)/shard_map/ppermute | solution.py:79
  136.1 13.5 %collective-permute-start.31 = (f32[2192,128]{1,0:T(8,128)S(1)}, f32[2192,128]{1,0:T(8,128)S(1)}, u32[]{:S(2)}, u32[]{:S(2)}) collective-permute-start(f32[2192,128]{1,0:T(8,128)S(1)} %pad_maximum_fusion.1.refs_1_), channel_id=1, source_target_pairs={{0,2},{2,0},{4,6},{6,4},{8,10},{10,8},{12,14},{14,12},{16,18},{18,... | collective-permute-start | bytes 3366920 | tf_op jit(solution)/shard_map/ppermute | solution.py:79
  136.1 3.0 %collective-permute-start.27 = (f32[8,128]{1,0:T(8,128)S(1)}, f32[8,128]{1,0:T(8,128)S(1)}, u32[]{:S(2)}, u32[]{:S(2)}) collective-permute-start(f32[8,128]{1,0:T(8,128)S(1)} %add.84), channel_id=1, source_target_pairs={{0,2},{2,0},{4,6},{6,4},{8,10},{10,8},{12,14},{14,12},{16,18},{18,... | collective-permute-start | bytes 12296 | tf_op jit(solution)/shard_map/ppermute | solution.py:79
  139.2 3.6 %collective-permute-start.28 = (f32[8,128]{1,0:T(8,128)S(1)}, f32[8,128]{1,0:T(8,128)S(1)}, u32[]{:S(2)}, u32[]{:S(2)}) collective-permute-start(f32[8,128]{1,0:T(8,128)S(1)} %add.85), channel_id=1, source_target_pairs={{0,1},{1,0},{2,3},{3,2},{4,5},{5,4},{6,7},{7,6},{8,9},{9,8},{10,11... | collective-permute-start | bytes 12296 | tf_op jit(solution)/shard_map/ppermute | solution.py:165
  142.8 6.9 %collective-permute-start.32 = (f32[1096,128]{1,0:T(8,128)S(1)}, f32[1096,128]{1,0:T(8,128)S(1)}, u32[]{:S(2)}, u32[]{:S(2)}) collective-permute-start(f32[1096,128]{1,0:T(8,128)S(1)} %add.83.refs_2_), channel_id=1, source_target_pairs={{0,2},{2,0},{4,6},{6,4},{8,10},{10,8},{12,14},{14,12},{16,18},{18,... | collective-permute-start | bytes 1683464 | tf_op jit(solution)/shard_map/ppermute | solution.py:79
  149.1 2.0 %collective-permute-start.33 = (f32[1096,128]{1,0:T(8,128)S(1)}, f32[1096,128]{1,0:T(8,128)S(1)}, u32[]{:S(2)}, u32[]{:S(2)}) collective-permute-start(f32[1096,128]{1,0:T(8,128)S(1)} %collective-permute-done.26.refs_3_), channel_id=1, source_target_pairs={{0,2},{2,0},{4,6},{6,4},{8,10},{10,8},{12,14},{14,12},{16,18},{18,... | collective-permute-start | bytes 1683464 | tf_op jit(solution)/shard_map/ppermute | solution.py:79
  149.1 2.8 %collective-permute-start.34 = (f32[1096,128]{1,0:T(8,128)S(1)}, f32[1096,128]{1,0:T(8,128)S(1)}, u32[]{:S(2)}, u32[]{:S(2)}) collective-permute-start(f32[1096,128]{1,0:T(8,128)S(1)} %collective-permute-done.29.refs_5_), channel_id=1, source_target_pairs={{0,2},{2,0},{4,6},{6,4},{8,10},{10,8},{12,14},{14,12},{16,18},{18,... | collective-permute-start | bytes 1683464 | tf_op jit(solution)/shard_map/ppermute | solution.py:79

commit v18 on v17

--- a/solution.py
+++ b/solution.py
@@ -119,10 +119,10 @@
     one = along_x(1, mine[1])
     across_two = plan.send(near_two + in_three, "z", MIDDLE)
     in_two = plan.send(near_two, "z", INWARD)
-    across_two, in_two, near_one = together(across_two, in_two, sum(one[1:], one[0]))
+    across_two, onward, near_one = together(across_two, near_three + in_two, sum(one[1:], one[0]))
     zero = along_x(0, mine[0])
     pair = plan.send(near_one + across_two, "z", PAIRS)
-    across_three = plan.send(near_three + in_two, "z", MIDDLE)
+    across_three = plan.send(onward, "z", MIDDLE)
     return zero + [pair, across_three] + beside
 
 

time: 172 us -> 169 us (0.983)
  no operation moved by 1% of the time
where the time goes in v18:
time: 169 us
  waiting for transfers between devices  73.1 us (43%)
  Pallas kernels  50 us (30%)
  starting transfers between devices  41.6 us (25%)
  other arithmetic  2.8 us (2%)
    ppermute x34, waiting for transfers between devices, send(): return lax.ppermute(value, 'dp', every)  71 us
    ppermute x34, starting transfers between devices, send(): return lax.ppermute(value, 'dp', every)  40.1 us
    pallas_call x1, Pallas kernels, place(): pl.pallas_call(functools.partial(place_kernel, plan), out_shape=[jax.Shap...  21.4 us
    pallas_call x1, Pallas kernels, finish(): pl.pallas_call(functools.partial(finish_kernel, plan, tile, slots), grid=...  19.6 us
    pallas_call x1, Pallas kernels, owned(): pl.pallas_call(functools.partial(owned_kernel, plan), out_shape=[jax.Shap...  6.32 us
  transfers between devices with their start and end apart: 35, of which 18 were waited for; matrix products, arithmetic and copies ran while one was open for 1% of the time, Pallas kernels for 4%

profile of v18, /device:TPU:0, one launch (start us, length us, event | category | flops | bytes accessed | tf_op | source)
XLA Modules:
  0.0 168.8 jit_solution(15304779523684544857)
XLA Ops:
  0.7 0.6 pad_add_fusion.place_ref
  1.2 21.4 %place_gradients.1 = (f32[1096,128]{1,0:T(8,128)}, f32[1096,128]{1,0:T(8,128)}, f32[1096,128]{1,0:T(8,128)}, f32[1096,128]{1,0:T(8,128)}, f32[1096,128]{1,0:T(8,...) custom-call(s32[3]{0:T(128)} %pad_add_fusion.place_ref, ...), custom_call_target="tpu_custom_call" | custom-call | tf_op jit(solution)/shard_map/place_gradients/pallas_call | solution.py:313
  22.7 0.5 collective-permute-start
  23.2 1.8 %collective-permute-done = f32[1096,128]{1,0:T(8,128)S(1)} collective-permute-done((f32[1096,128]{1,0:T(8,128)}, f32[1096,128]{1,0:T(8,128)S(1)}, u32[]{:S(2)}, u32[]{:S(2)}) %collective-permute-start) | collective-permute-done | bytes 561184 | tf_op jit(solution)/shard_map/ppermute | solution.py:79
  25.0 1.1 add.68
  26.1 0.4 collective-permute-start.8
  26.6 0.1 collective-permute-start.4
  26.7 2.9 %collective-permute-start.5 = (f32[1096,128]{1,0:T(8,128)S(1)}, f32[1096,128]{1,0:T(8,128)S(1)}, u32[]{:S(2)}, u32[]{:S(2)}) collective-permute-start(f32[1096,128]{1,0:T(8,128)S(1)} %add.68), channel_id=1, source_target_pairs={{0,4},{2,6},{4,0},{6,2},{8,12},{10,14},{12,8},{14,10},{16,20},{18,... | collective-permute-start | bytes 1683464 | tf_op jit(solution)/shard_map/ppermute | solution.py:79
  29.6 0.5 collective-permute-start.7
  30.1 0.1 add.74
  30.2 1.2 collective-permute-start.9
  31.4 11.7 %collective-permute-done.5 = f32[1096,128]{1,0:T(8,128)S(1)} collective-permute-done((f32[1096,128]{1,0:T(8,128)S(1)}, f32[1096,128]{1,0:T(8,128)S(1)}, u32[]{:S(2)}, u32[]{:S(2)}) %collective-permute-start.5) | collective-permute-done | bytes 561184 | tf_op jit(solution)/shard_map/ppermute | solution.py:79
  43.0 0.1 add_add_fusion.2
  43.2 4.2 %collective-permute-start.6 = (f32[1096,128]{1,0:T(8,128)S(1)}, f32[1096,128]{1,0:T(8,128)S(1)}, u32[]{:S(2)}, u32[]{:S(2)}) collective-permute-start(f32[1096,128]{1,0:T(8,128)S(1)} %add_add_fusion.2), channel_id=1, source_target_pairs={{0,8},{2,10},{4,12},{6,14},{24,16},{26,18},{28,20},{30,22},{1,9},{... | collective-permute-start | bytes 1683464 | tf_op jit(solution)/shard_map/ppermute | solution.py:79
  47.4 6.3 %owned_weights.1 = (f32[1088,128]{1,0:T(8,128)}, s32[1152,128]{1,0:T(8,128)}) custom-call(s32[3]{0:T(128)} %pad_add_fusion.place_ref, s32[136,128]{1,0:T(8,128)} %bitcast.16, f32[17408,128]{1,0:T(8,128)} %weights_ref.3), custom_call_target="tpu_custom_call" | custom-call | bytes 20971520 | tf_op jit(solution)/shard_map/owned_weights/pallas_call | solution.py:391
  53.9 0.5 collective-permute-start.12
  54.4 1.6 collective-permute-start.14
  56.0 0.1 add_add_fusion.1
  56.1 1.9 %collective-permute-done.6 = f32[1096,128]{1,0:T(8,128)S(1)} collective-permute-done((f32[1096,128]{1,0:T(8,128)S(1)}, f32[1096,128]{1,0:T(8,128)S(1)}, u32[]{:S(2)}, u32[]{:S(2)}) %collective-permute-start.6) | collective-permute-done | bytes 561184 | tf_op jit(solution)/shard_map/ppermute | solution.py:79
  58.0 4.4 %collective-permute-start.11 = (f32[1096,128]{1,0:T(8,128)S(1)}, f32[1096,128]{1,0:T(8,128)S(1)}, u32[]{:S(2)}, u32[]{:S(2)}) collective-permute-start(f32[1096,128]{1,0:T(8,128)S(1)} %add_add_fusion.1), channel_id=1, source_target_pairs={{0,8},{2,10},{4,12},{6,14},{24,16},{26,18},{28,20},{30,22},{1,9},{... | collective-permute-start | bytes 1683464 | tf_op jit(solution)/shard_map/ppermute | solution.py:79
  62.4 0.1 add.76
  62.5 0.8 collective-permute-start.10
  63.5 0.1 add.70
  63.6 1.6 collective-permute-start.3
  65.1 4.9 %collective-permute-done.14 = f32[1096,128]{1,0:T(8,128)S(1)} collective-permute-done((f32[1096,128]{1,0:T(8,128)S(1)}, f32[1096,128]{1,0:T(8,128)S(1)}, u32[]{:S(2)}, u32[]{:S(2)}) %collective-permute-start.14) | collective-permute-done | bytes 561184 | tf_op jit(solution)/shard_map/ppermute | solution.py:79
  70.1 0.1 add_add_fusion
  70.2 1.9 %collective-permute-done.11 = f32[1096,128]{1,0:T(8,128)S(1)} collective-permute-done((f32[1096,128]{1,0:T(8,128)S(1)}, f32[1096,128]{1,0:T(8,128)S(1)}, u32[]{:S(2)}, u32[]{:S(2)}) %collective-permute-start.11) | collective-permute-done | bytes 561184 | tf_op jit(solution)/shard_map/ppermute | solution.py:79
  72.1 0.1 add.77
  72.3 3.9 %collective-permute-start.15 = (f32[1096,128]{1,0:T(8,128)S(1)}, f32[1096,128]{1,0:T(8,128)S(1)}, u32[]{:S(2)}, u32[]{:S(2)}) collective-permute-start(f32[1096,128]{1,0:T(8,128)S(1)} %add.81), channel_id=1, source_target_pairs={{0,8},{2,10},{4,12},{6,14},{8,0},{10,2},{12,4},{14,6},{16,24},{18,... | collective-permute-start | bytes 1683464 | tf_op jit(solution)/shard_map/ppermute | solution.py:79
  76.3 0.7 collective-permute-start.16
  77.0 0.1 add.69.refs_0_
  77.1 4.2 %collective-permute-done.3.refs_1_ = f32[1096,128]{1,0:T(8,128)S(1)} collective-permute-done((f32[1096,128]{1,0:T(8,128)S(1)}, f32[1096,128]{1,0:T(8,128)S(1)}, u32[]{:S(2)}, u32[]{:S(2)}) %collective-permute-start.3) | collective-permute-done | bytes 561184 | tf_op jit(solution)/shard_map/ppermute | solution.py:79
  81.2 4.6 %collective-permute-done.15.refs_2_ = f32[1096,128]{1,0:T(8,128)S(1)} collective-permute-done((f32[1096,128]{1,0:T(8,128)S(1)}, f32[1096,128]{1,0:T(8,128)S(1)}, u32[]{:S(2)}, u32[]{:S(2)}) %collective-permute-start.15) | collective-permute-done | bytes 561184 | tf_op jit(solution)/shard_map/ppermute | solution.py:79
  85.8 2.0 %moments.1 = (f32[1088,128]{1,0:T(8,128)}, f32[1088,128]{1,0:T(8,128)}, f32[1096,128]{1,0:T(8,128)S(1)}) custom-call(f32[1096,128]{1,0:T(8,128)S(1)} %add.69.refs_0_, f32[1096,128]{1,0:T(8,128)S(1)} %collective-permute-done.3.refs_1_, f32[1096,128]{1,0:T(8,128)S(1)} %collective-permute-done.15.refs_2_, f32[1096,128]{1,0:T(8,128)S(1)} %collective-permute-done.16.refs_3_, ...), custom_call_target="tpu_custom_call" | custom-call | tf_op jit(solution)/shard_map/moments/pallas_call | solution.py:445
  87.9 3.8 %collective-permute-start.18 = (f32[1096,128]{1,0:T(8,128)S(1)}, f32[1096,128]{1,0:T(8,128)S(1)}, u32[]{:S(2)}, u32[]{:S(2)}) collective-permute-start(f32[1096,128]{1,0:T(8,128)S(1)} %get-tuple-element.92), channel_id=1, source_target_pairs={{0,8},{2,10},{4,12},{6,14},{8,0},{10,2},{12,4},{14,6},{16,24},{18,... | collective-permute-start | bytes 1683464 | tf_op jit(solution)/shard_map/ppermute | solution.py:79
  91.7 1.5 collective-permute-start.19
  93.2 0.7 collective-permute-start.17
  93.9 6.4 %collective-permute-done.18 = f32[1096,128]{1,0:T(8,128)S(1)} collective-permute-done((f32[1096,128]{1,0:T(8,128)S(1)}, f32[1096,128]{1,0:T(8,128)S(1)}, u32[]{:S(2)}, u32[]{:S(2)}) %collective-permute-start.18) | collective-permute-done | bytes 561184 | tf_op jit(solution)/shard_map/ppermute | solution.py:79
  100.3 1.5 collective-permute-start.24
  101.8 0.7 collective-permute-start.20
  102.5 0.1 pad_maximum_fusion.refs_0_.refs_1_
  102.6 2.9 %collective-permute-done.19 = f32[1096,128]{1,0:T(8,128)S(1)} collective-permute-done((f32[1096,128]{1,0:T(8,128)S(1)}, f32[1096,128]{1,0:T(8,128)S(1)}, u32[]{:S(2)}, u32[]{:S(2)}) %collective-permute-start.19) | collective-permute-done | bytes 561184 | tf_op jit(solution)/shard_map/ppermute | solution.py:79
  105.5 1.3 collective-permute-start.23
  106.8 1.3 collective-permute-start.21
  108.1 6.4 %collective-permute-done.24 = f32[1096,128]{1,0:T(8,128)S(1)} collective-permute-done((f32[1096,128]{1,0:T(8,128)S(1)}, f32[1096,128]{1,0:T(8,128)S(1)}, u32[]{:S(2)}, u32[]{:S(2)}) %collective-permute-start.24) | collective-permute-done | bytes 561184 | tf_op jit(solution)/shard_map/ppermute | solution.py:79
  114.5 3.7 %collective-permute-done.23 = f32[1096,128]{1,0:T(8,128)S(1)} collective-permute-done((f32[1096,128]{1,0:T(8,128)S(1)}, f32[1096,128]{1,0:T(8,128)S(1)}, u32[]{:S(2)}, u32[]{:S(2)}) %collective-permute-start.23) | collective-permute-done | bytes 561184 | tf_op jit(solution)/shard_map/ppermute | solution.py:79
  118.2 0.1 add.83.refs_2_
  118.3 0.1 pad_maximum_fusion.1.refs_1_
  118.4 2.5 %collective-permute-start.26 = (f32[1096,128]{1,0:T(8,128)S(1)}, f32[1096,128]{1,0:T(8,128)S(1)}, u32[]{:S(2)}, u32[]{:S(2)}) collective-permute-start(f32[1096,128]{1,0:T(8,128)S(1)} %add.83.refs_2_), channel_id=1, source_target_pairs={{0,4},{2,6},{4,0},{6,2},{8,12},{10,14},{12,8},{14,10},{16,20},{18,... | collective-permute-start | bytes 1683464 | tf_op jit(solution)/shard_map/ppermute | solution.py:79
  120.9 8.1 %collective-permute-done.21 = f32[1096,128]{1,0:T(8,128)S(1)} collective-permute-done((f32[1096,128]{1,0:T(8,128)S(1)}, f32[1096,128]{1,0:T(8,128)S(1)}, u32[]{:S(2)}, u32[]{:S(2)}) %collective-permute-start.21) | collective-permute-done | bytes 561184 | tf_op jit(solution)/shard_map/ppermute | solution.py:79
  129.1 0.6 sums.1
  129.6 1.6 collective-permute-start.25
  131.2 0.5 collective-permute-start.29
  131.7 0.2 collective-permute-start.22
  132.0 1.3 collective-permute-done.25
  133.3 0.5 collective-permute-start.27
  133.8 2.5 %collective-permute-done.27 = f32[8,128]{1,0:T(8,128)S(1)} collective-permute-done((f32[8,128]{1,0:T(8,128)S(1)}, f32[8,128]{1,0:T(8,128)S(1)}, u32[]{:S(2)}, u32[]{:S(2)}) %collective-permute-start.27) | collective-permute-done | bytes 4128 | tf_op jit(solution)/shard_map/ppermute | solution.py:79
  136.4 1.5 collective-permute-start.28
  137.9 2.1 %collective-permute-done.28 = f32[8,128]{1,0:T(8,128)S(1)} collective-permute-done((f32[8,128]{1,0:T(8,128)S(1)}, f32[8,128]{1,0:T(8,128)S(1)}, u32[]{:S(2)}, u32[]{:S(2)}) %collective-permute-start.28) | collective-permute-done | bytes 4128 | tf_op jit(solution)/shard_map/ppermute | solution.py:165
  140.0 6.3 %collective-permute-done.29.refs_5_ = f32[1096,128]{1,0:T(8,128)S(1)} collective-permute-done((f32[1096,128]{1,0:T(8,128)S(1)}, f32[1096,128]{1,0:T(8,128)S(1)}, u32[]{:S(2)}, u32[]{:S(2)}) %collective-permute-start.29) | collective-permute-done | bytes 561184 | tf_op jit(solution)/shard_map/ppermute | solution.py:79
  146.3 0.5 collective-permute-start.34
  146.9 1.4 collective-permute-done.33.refs_9_
  148.3 0.8 collective-permute-done.34.refs_11_
  149.1 19.6 %new_weights.1 = (f32[17408,128]{1,0:T(8,128)}, f32[3,2,1024]{2,1,0:T(2,128)}, f32[7]{0:T(128)}) custom-call(s32[3]{0:T(128)S(1)} %copy-done.6, s32[136,128]{1,0:T(8,128)S(1)} %copy-done.4, f32[8,128]{1,0:T(8,128)S(1)} %add.86.total_ref, f32[3,2,1024]{2,1,0:T(2,128)S(1)} %copy-done.5, f32[17408,128]{1,0:T(8,128)S(1)} %bitcast.11, ...), custom_call_target="tpu_custom_call" | custom-call | tf_op jit(solution)/shard_map/new_weights/pallas_call | solution.py:523
  (75 shorter events, 0.5 us)
Async XLA Ops:
  22.6 6.9 %copy-start.18 = (f32[1096,128]{1,0:T(8,128)S(1)}, f32[1096,128]{1,0:T(8,128)}, u32[]{:S(2)}) copy-start(f32[1096,128]{1,0:T(8,128)} %get-tuple-element.86) | copy-start | bytes 1683460
  22.7 6.9 %copy-start.17 = (f32[1096,128]{1,0:T(8,128)S(1)}, f32[1096,128]{1,0:T(8,128)}, u32[]{:S(2)}) copy-start(f32[1096,128]{1,0:T(8,128)} %get-tuple-element.76) | copy-start | bytes 1683460
  22.7 7.4 %copy-start.13 = (f32[1096,128]{1,0:T(8,128)S(1)}, f32[1096,128]{1,0:T(8,128)}, u32[]{:S(2)}) copy-start(f32[1096,128]{1,0:T(8,128)} %get-tuple-element.77) | copy-start | bytes 1683460
  22.7 2.3 %collective-permute-start = (f32[1096,128]{1,0:T(8,128)}, f32[1096,128]{1,0:T(8,128)S(1)}, u32[]{:S(2)}, u32[]{:S(2)}) collective-permute-start(f32[1096,128]{1,0:T(8,128)} %get-tuple-element.61), channel_id=1, source_target_pairs={{0,2},{2,0},{4,6},{6,4},{8,10},{10,8},{12,14},{14,12},{16,18},{18,... | collective-permute-start | bytes 1683464 | tf_op jit(solution)/shard_map/ppermute | solution.py:79
  26.1 16.9 %copy-start.12 = (f32[1096,128]{1,0:T(8,128)S(1)}, f32[1096,128]{1,0:T(8,128)}, u32[]{:S(2)}) copy-start(f32[1096,128]{1,0:T(8,128)} %get-tuple-element.72) | copy-start | bytes 1683460
  26.1 4.0 %collective-permute-start.8 = (f32[1096,128]{1,0:T(8,128)}, f32[1096,128]{1,0:T(8,128)S(1)}, u32[]{:S(2)}, u32[]{:S(2)}) collective-permute-start(f32[1096,128]{1,0:T(8,128)} %get-tuple-element.78), channel_id=1, source_target_pairs={{0,2},{2,0},{4,6},{6,4},{8,10},{10,8},{12,14},{14,12},{16,18},{18,... | collective-permute-start | bytes 1683464 | tf_op jit(solution)/shard_map/ppermute | solution.py:79
  26.6 4.8 %collective-permute-start.4 = (f32[1096,128]{1,0:T(8,128)}, f32[1096,128]{1,0:T(8,128)S(1)}, u32[]{:S(2)}, u32[]{:S(2)}) collective-permute-start(f32[1096,128]{1,0:T(8,128)} %get-tuple-element.73), channel_id=1, source_target_pairs={{0,2},{2,0},{4,6},{6,4},{8,10},{10,8},{12,14},{14,12},{16,18},{18,... | collective-permute-start | bytes 1683464 | tf_op jit(solution)/shard_map/ppermute | solution.py:79
  26.7 16.4 %collective-permute-start.5 = (f32[1096,128]{1,0:T(8,128)S(1)}, f32[1096,128]{1,0:T(8,128)S(1)}, u32[]{:S(2)}, u32[]{:S(2)}) collective-permute-start(f32[1096,128]{1,0:T(8,128)S(1)} %add.68), channel_id=1, source_target_pairs={{0,4},{2,6},{4,0},{6,2},{8,12},{10,14},{12,8},{14,10},{16,20},{18,... | collective-permute-start | bytes 1683464 | tf_op jit(solution)/shard_map/ppermute | solution.py:79
  29.6 24.3 %collective-permute-start.13 = (f32[1096,128]{1,0:T(8,128)S(1)}, f32[1096,128]{1,0:T(8,128)S(1)}, u32[]{:S(2)}, u32[]{:S(2)}) collective-permute-start(f32[1096,128]{1,0:T(8,128)S(1)} %copy-done.18), channel_id=1, source_target_pairs={{0,2},{2,0},{4,6},{6,4},{8,10},{10,8},{12,14},{14,12},{16,18},{18,... | collective-permute-start | bytes 1683464 | tf_op jit(solution)/shard_map/ppermute | solution.py:79
  29.6 24.9 %collective-permute-start.7 = (f32[1096,128]{1,0:T(8,128)S(1)}, f32[1096,128]{1,0:T(8,128)S(1)}, u32[]{:S(2)}, u32[]{:S(2)}) collective-permute-start(f32[1096,128]{1,0:T(8,128)S(1)} %copy-done.17), channel_id=1, source_target_pairs={{0,2},{2,0},{4,6},{6,4},{8,10},{10,8},{12,14},{14,12},{16,18},{18,... | collective-permute-start | bytes 1683464 | tf_op jit(solution)/shard_map/ppermute | solution.py:79
  30.2 25.8 %collective-permute-start.9 = (f32[1096,128]{1,0:T(8,128)S(1)}, f32[1096,128]{1,0:T(8,128)S(1)}, u32[]{:S(2)}, u32[]{:S(2)}) collective-permute-start(f32[1096,128]{1,0:T(8,128)S(1)} %add.74), channel_id=1, source_target_pairs={{0,4},{2,6},{4,0},{6,2},{8,12},{10,14},{12,8},{14,10},{16,20},{18,... | collective-permute-start | bytes 1683464 | tf_op jit(solution)/shard_map/ppermute | solution.py:79
  43.2 10.6 %copy-start.16 = (f32[1096,128]{1,0:T(8,128)S(1)}, f32[1096,128]{1,0:T(8,128)}, u32[]{:S(2)}) copy-start(f32[1096,128]{1,0:T(8,128)} %get-tuple-element.71) | copy-start | bytes 1683460
  43.2 10.7 %copy-start.15 = (f32[1096,128]{1,0:T(8,128)S(1)}, f32[1096,128]{1,0:T(8,128)}, u32[]{:S(2)}) copy-start(f32[1096,128]{1,0:T(8,128)} %get-tuple-element.84) | copy-start | bytes 1683460
  43.2 11.2 %copy-start.11 = (f32[1096,128]{1,0:T(8,128)S(1)}, f32[1096,128]{1,0:T(8,128)}, u32[]{:S(2)}) copy-start(f32[1096,128]{1,0:T(8,128)} %get-tuple-element.85) | copy-start | bytes 1683460
  43.2 14.8 %collective-permute-start.6 = (f32[1096,128]{1,0:T(8,128)S(1)}, f32[1096,128]{1,0:T(8,128)S(1)}, u32[]{:S(2)}, u32[]{:S(2)}) collective-permute-start(f32[1096,128]{1,0:T(8,128)S(1)} %add_add_fusion.2), channel_id=1, source_target_pairs={{0,8},{2,10},{4,12},{6,14},{24,16},{26,18},{28,20},{30,22},{1,9},{... | collective-permute-start | bytes 1683464 | tf_op jit(solution)/shard_map/ppermute | solution.py:79
  53.8 2.2 %copy-start.10 = (f32[1096,128]{1,0:T(8,128)S(1)}, f32[1096,128]{1,0:T(8,128)}, u32[]{:S(2)}) copy-start(f32[1096,128]{1,0:T(8,128)} %get-tuple-element.75) | copy-start | bytes 1683460
  53.8 9.6 %collective-permute-start.2 = (f32[1096,128]{1,0:T(8,128)S(1)}, f32[1096,128]{1,0:T(8,128)S(1)}, u32[]{:S(2)}, u32[]{:S(2)}) collective-permute-start(f32[1096,128]{1,0:T(8,128)S(1)} %copy-done.16), channel_id=1, source_target_pairs={{0,2},{2,0},{4,6},{6,4},{8,10},{10,8},{12,14},{14,12},{16,18},{18,... | collective-permute-start | bytes 1683464 | tf_op jit(solution)/shard_map/ppermute | solution.py:79
  53.9 9.7 %collective-permute-start.12 = (f32[1096,128]{1,0:T(8,128)S(1)}, f32[1096,128]{1,0:T(8,128)S(1)}, u32[]{:S(2)}, u32[]{:S(2)}) collective-permute-start(f32[1096,128]{1,0:T(8,128)S(1)} %copy-done.15), channel_id=1, source_target_pairs={{0,2},{2,0},{4,6},{6,4},{8,10},{10,8},{12,14},{14,12},{16,18},{18,... | collective-permute-start | bytes 1683464 | tf_op jit(solution)/shard_map/ppermute | solution.py:79
  54.4 15.6 %collective-permute-start.14 = (f32[1096,128]{1,0:T(8,128)S(1)}, f32[1096,128]{1,0:T(8,128)S(1)}, u32[]{:S(2)}, u32[]{:S(2)}) collective-permute-start(f32[1096,128]{1,0:T(8,128)S(1)} %add.79), channel_id=1, source_target_pairs={{0,4},{2,6},{4,0},{6,2},{8,12},{10,14},{12,8},{14,10},{16,20},{18,... | collective-permute-start | bytes 1683464 | tf_op jit(solution)/shard_map/ppermute | solution.py:79
  56.1 7.3 %copy-start.14 = (f32[1096,128]{1,0:T(8,128)S(1)}, f32[1096,128]{1,0:T(8,128)}, u32[]{:S(2)}) copy-start(f32[1096,128]{1,0:T(8,128)} %get-tuple-element.69) | copy-start | bytes 1683460
  56.1 7.3 %copy-start.9 = (f32[1096,128]{1,0:T(8,128)S(1)}, f32[1096,128]{1,0:T(8,128)}, u32[]{:S(2)}) copy-start(f32[1096,128]{1,0:T(8,128)} %get-tuple-element.70) | copy-start | bytes 1683460
  58.0 14.1 %collective-permute-start.11 = (f32[1096,128]{1,0:T(8,128)S(1)}, f32[1096,128]{1,0:T(8,128)S(1)}, u32[]{:S(2)}, u32[]{:S(2)}) collective-permute-start(f32[1096,128]{1,0:T(8,128)S(1)} %add_add_fusion.1), channel_id=1, source_target_pairs={{0,8},{2,10},{4,12},{6,14},{24,16},{26,18},{28,20},{30,22},{1,9},{... | collective-permute-start | bytes 1683464 | tf_op jit(solution)/shard_map/ppermute | solution.py:79
  62.5 7.6 %copy-start.8 = (f32[1096,128]{1,0:T(8,128)S(1)}, f32[1096,128]{1,0:T(8,128)}, u32[]{:S(2)}) copy-start(f32[1096,128]{1,0:T(8,128)} %get-tuple-element.83) | copy-start | bytes 1683460
  62.5 9.7 %collective-permute-start.10 = (f32[1096,128]{1,0:T(8,128)S(1)}, f32[1096,128]{1,0:T(8,128)S(1)}, u32[]{:S(2)}, u32[]{:S(2)}) collective-permute-start(f32[1096,128]{1,0:T(8,128)S(1)} %add.76), channel_id=1, source_target_pairs={{8,16},{10,18},{12,20},{14,22},{16,8},{18,10},{20,12},{22,14},{9,1... | collective-permute-start | bytes 1683464 | tf_op jit(solution)/shard_map/ppermute | solution.py:79
  63.4 13.6 %collective-permute-start.1 = (f32[1096,128]{1,0:T(8,128)S(1)}, f32[1096,128]{1,0:T(8,128)S(1)}, u32[]{:S(2)}, u32[]{:S(2)}) collective-permute-start(f32[1096,128]{1,0:T(8,128)S(1)} %copy-done.14), channel_id=1, source_target_pairs={{0,2},{2,0},{4,6},{6,4},{8,10},{10,8},{12,14},{14,12},{16,18},{18,... | collective-permute-start | bytes 1683464 | tf_op jit(solution)/shard_map/ppermute | solution.py:79
  63.6 17.7 %collective-permute-start.3 = (f32[1096,128]{1,0:T(8,128)S(1)}, f32[1096,128]{1,0:T(8,128)S(1)}, u32[]{:S(2)}, u32[]{:S(2)}) collective-permute-start(f32[1096,128]{1,0:T(8,128)S(1)} %add.70), channel_id=1, source_target_pairs={{0,4},{2,6},{4,0},{6,2},{8,12},{10,14},{12,8},{14,10},{16,20},{18,... | collective-permute-start | bytes 1683464 | tf_op jit(solution)/shard_map/ppermute | solution.py:79
  70.1 79.0 %slice-start = ((s8[8912896]{0:T(1024)(128)(4,1)}), s8[4194304]{0:T(1024)(128)(4,1)S(1)}, s32[]{:S(2)}) async-start(s8[8912896]{0:T(1024)(128)(4,1)} %bitcast.10), calls=%async_computation | async-start | bytes 8388608
  72.2 4.8 %copy-start.7 = (f32[1096,128]{1,0:T(8,128)S(1)}, f32[1096,128]{1,0:T(8,128)}, u32[]{:S(2)}) copy-start(f32[1096,128]{1,0:T(8,128)} %get-tuple-element.59) | copy-start | bytes 1683460
  72.2 13.6 %copy-start.2 = (f32[1,1088,128]{2,1,0:T(8,128)S(1)}, f32[1,1088,128]{2,1,0:T(8,128)}, u32[]{:S(2)}) copy-start(f32[1,1088,128]{2,1,0:T(8,128)} %param.10) | copy-start | bytes 1671172
  72.2 13.6 %copy-start.3 = (f32[1088,128]{1,0:T(8,128)S(1)}, f32[1088,128]{1,0:T(8,128)}, u32[]{:S(2)}) copy-start(f32[1088,128]{1,0:T(8,128)} %get-tuple-element.90.refs_6_) | copy-start | bytes 1671172
  72.3 13.5 %copy-start = (s32[1152,128]{1,0:T(8,128)S(1)}, s32[1152,128]{1,0:T(8,128)}, u32[]{:S(2)}) copy-start(s32[1152,128]{1,0:T(8,128)} %get-tuple-element.91.refs_7_) | copy-start | bytes 1769476
  72.3 13.5 %copy-start.1 = (f32[1,1088,128]{2,1,0:T(8,128)S(1)}, f32[1,1088,128]{2,1,0:T(8,128)}, u32[]{:S(2)}) copy-start(f32[1,1088,128]{2,1,0:T(8,128)} %param.9) | copy-start | bytes 1671172
  72.3 13.5 %collective-permute-start.15 = (f32[1096,128]{1,0:T(8,128)S(1)}, f32[1096,128]{1,0:T(8,128)S(1)}, u32[]{:S(2)}, u32[]{:S(2)}) collective-permute-start(f32[1096,128]{1,0:T(8,128)S(1)} %add.81), channel_id=1, source_target_pairs={{0,8},{2,10},{4,12},{6,14},{8,0},{10,2},{12,4},{14,6},{16,24},{18,... | collective-permute-start | bytes 1683464 | tf_op jit(solution)/shard_map/ppermute | solution.py:79
  76.3 9.5 %collective-permute-start.16 = (f32[1096,128]{1,0:T(8,128)S(1)}, f32[1096,128]{1,0:T(8,128)S(1)}, u32[]{:S(2)}, u32[]{:S(2)}) collective-permute-start(f32[1096,128]{1,0:T(8,128)S(1)} %add.77), channel_id=1, source_target_pairs={{8,16},{10,18},{12,20},{14,22},{16,8},{18,10},{20,12},{22,14},{9,1... | collective-permute-start | bytes 1683464 | tf_op jit(solution)/shard_map/ppermute | solution.py:79
  85.8 63.3 %slice-start.1 = ((s8[8912896]{0:T(1024)(128)(4,1)}), s8[4194304]{0:T(1024)(128)(4,1)S(1)}, s32[]{:S(2)}) async-start(s8[8912896]{0:T(1024)(128)(4,1)} %bitcast.10), calls=%async_computation.1 | async-start | bytes 8388608
  87.9 12.5 %collective-permute-start.18 = (f32[1096,128]{1,0:T(8,128)S(1)}, f32[1096,128]{1,0:T(8,128)S(1)}, u32[]{:S(2)}, u32[]{:S(2)}) collective-permute-start(f32[1096,128]{1,0:T(8,128)S(1)} %get-tuple-element.92), channel_id=1, source_target_pairs={{0,8},{2,10},{4,12},{6,14},{8,0},{10,2},{12,4},{14,6},{16,24},{18,... | collective-permute-start | bytes 1683464 | tf_op jit(solution)/shard_map/ppermute | solution.py:79
  91.7 13.8 %collective-permute-start.19 = (f32[1096,128]{1,0:T(8,128)S(1)}, f32[1096,128]{1,0:T(8,128)S(1)}, u32[]{:S(2)}, u32[]{:S(2)}) collective-permute-start(f32[1096,128]{1,0:T(8,128)S(1)} %get-tuple-element.92), channel_id=1, source_target_pairs={{0,4},{2,6},{4,0},{6,2},{8,12},{10,14},{12,8},{14,10},{16,20},{18,... | collective-permute-start | bytes 1683464 | tf_op jit(solution)/shard_map/ppermute | solution.py:79
  93.2 12.3 %collective-permute-start.17 = (f32[1096,128]{1,0:T(8,128)S(1)}, f32[1096,128]{1,0:T(8,128)S(1)}, u32[]{:S(2)}, u32[]{:S(2)}) collective-permute-start(f32[1096,128]{1,0:T(8,128)S(1)} %get-tuple-element.92), channel_id=1, source_target_pairs={{8,16},{10,18},{12,20},{14,22},{16,8},{18,10},{20,12},{22,14},{9,1... | collective-permute-start | bytes 1683464 | tf_op jit(solution)/shard_map/ppermute | solution.py:79
  100.3 14.2 %collective-permute-start.24 = (f32[1096,128]{1,0:T(8,128)S(1)}, f32[1096,128]{1,0:T(8,128)S(1)}, u32[]{:S(2)}, u32[]{:S(2)}) collective-permute-start(f32[1096,128]{1,0:T(8,128)S(1)} %collective-permute-done.18), channel_id=1, source_target_pairs={{0,4},{2,6},{4,0},{6,2},{8,12},{10,14},{12,8},{14,10},{16,20},{18,... | collective-permute-start | bytes 1683464 | tf_op jit(solution)/shard_map/ppermute | solution.py:79
  101.8 5.0 %collective-permute-start.20 = (f32[1096,128]{1,0:T(8,128)S(1)}, f32[1096,128]{1,0:T(8,128)S(1)}, u32[]{:S(2)}, u32[]{:S(2)}) collective-permute-start(f32[1096,128]{1,0:T(8,128)S(1)} %collective-permute-done.18), channel_id=1, source_target_pairs={{8,16},{10,18},{12,20},{14,22},{16,8},{18,10},{20,12},{22,14},{9,1... | collective-permute-start | bytes 1683464 | tf_op jit(solution)/shard_map/ppermute | solution.py:79
  102.6 46.5 %slice-start.2 = ((s8[8912896]{0:T(1024)(128)(4,1)}), s8[524288]{0:T(1024)(128)(4,1)S(1)}, s32[]{:S(2)}) async-start(s8[8912896]{0:T(1024)(128)(4,1)} %bitcast.10), calls=%async_computation.2 | async-start | bytes 1048576
  105.5 12.7 %collective-permute-start.23 = (f32[1096,128]{1,0:T(8,128)S(1)}, f32[1096,128]{1,0:T(8,128)S(1)}, u32[]{:S(2)}, u32[]{:S(2)}) collective-permute-start(f32[1096,128]{1,0:T(8,128)S(1)} %collective-permute-done.17), channel_id=1, source_target_pairs={{8,0},{10,2},{12,4},{14,6},{16,24},{18,26},{20,28},{22,30},{9,1},{... | collective-permute-start | bytes 1683464 | tf_op jit(solution)/shard_map/ppermute | solution.py:79
  106.8 22.2 %collective-permute-start.21 = (f32[1096,128]{1,0:T(8,128)S(1)}, f32[1096,128]{1,0:T(8,128)S(1)}, u32[]{:S(2)}, u32[]{:S(2)}) collective-permute-start(f32[1096,128]{1,0:T(8,128)S(1)} %collective-permute-done.20), channel_id=1, source_target_pairs={{8,0},{10,2},{12,4},{14,6},{16,24},{18,26},{20,28},{22,30},{9,1},{... | collective-permute-start | bytes 1683464 | tf_op jit(solution)/shard_map/ppermute | solution.py:79
  118.4 10.7 %copy-start.6 = (s32[3]{0:T(128)S(1)}, s32[3]{0:T(128)}, u32[]{:S(2)}) copy-start(s32[3]{0:T(128)} %pad_add_fusion.place_ref) | copy-start | bytes 40
  118.4 15.0 %collective-permute-start.26 = (f32[1096,128]{1,0:T(8,128)S(1)}, f32[1096,128]{1,0:T(8,128)S(1)}, u32[]{:S(2)}, u32[]{:S(2)}) collective-permute-start(f32[1096,128]{1,0:T(8,128)S(1)} %add.83.refs_2_), channel_id=1, source_target_pairs={{0,4},{2,6},{4,0},{6,2},{8,12},{10,14},{12,8},{14,10},{16,20},{18,... | collective-permute-start | bytes 1683464 | tf_op jit(solution)/shard_map/ppermute | solution.py:79
  129.1 20.0 %copy-start.4 = (s32[136,128]{1,0:T(8,128)S(1)}, s32[136,128]{1,0:T(8,128)}, u32[]{:S(2)}) copy-start(s32[136,128]{1,0:T(8,128)} %get-tuple-element.58.position_ref) | copy-start | bytes 208900
  129.1 20.0 %copy-start.5 = (f32[3,2,1024]{2,1,0:T(2,128)S(1)}, f32[3,2,1024]{2,1,0:T(2,128)}, u32[]{:S(2)}) copy-start(f32[3,2,1024]{2,1,0:T(2,128)} %norm_ref.1) | copy-start | bytes 73732
  129.6 3.7 %collective-permute-start.25 = (f32[8,128]{1,0:T(8,128)S(1)}, f32[8,128]{1,0:T(8,128)S(1)}, u32[]{:S(2)}, u32[]{:S(2)}) collective-permute-start(f32[8,128]{1,0:T(8,128)S(1)} %sums.1), channel_id=1, source_target_pairs={{0,4},{2,6},{4,0},{6,2},{8,12},{10,14},{12,8},{14,10},{16,20},{18,... | collective-permute-start | bytes 12296 | tf_op jit(solution)/shard_map/ppermute | solution.py:79
  131.2 15.6 %collective-permute-start.30 = (f32[2192,128]{1,0:T(8,128)S(1)}, f32[2192,128]{1,0:T(8,128)S(1)}, u32[]{:S(2)}, u32[]{:S(2)}) collective-permute-start(f32[2192,128]{1,0:T(8,128)S(1)} %pad_maximum_fusion.refs_0_.refs_1_), channel_id=1, source_target_pairs={{0,2},{2,0},{4,6},{6,4},{8,10},{10,8},{12,14},{14,12},{16,18},{18,... | collective-permute-start | bytes 3366920 | tf_op jit(solution)/shard_map/ppermute | solution.py:79
  131.2 15.1 %collective-permute-start.29 = (f32[1096,128]{1,0:T(8,128)S(1)}, f32[1096,128]{1,0:T(8,128)S(1)}, u32[]{:S(2)}, u32[]{:S(2)}) collective-permute-start(f32[1096,128]{1,0:T(8,128)S(1)} %add.82.refs_3_.refs_4_), channel_id=1, source_target_pairs={{0,4},{2,6},{4,0},{6,2},{8,12},{10,14},{12,8},{14,10},{16,20},{18,... | collective-permute-start | bytes 1683464 | tf_op jit(solution)/shard_map/ppermute | solution.py:79
  131.7 14.6 %collective-permute-start.22 = (f32[1096,128]{1,0:T(8,128)S(1)}, f32[1096,128]{1,0:T(8,128)S(1)}, u32[]{:S(2)}, u32[]{:S(2)}) collective-permute-start(f32[1096,128]{1,0:T(8,128)S(1)} %add.82.refs_3_.refs_4_), channel_id=1, source_target_pairs={{0,2},{2,0},{4,6},{6,4},{8,10},{10,8},{12,14},{14,12},{16,18},{18,... | collective-permute-start | bytes 1683464 | tf_op jit(solution)/shard_map/ppermute | solution.py:79
  133.3 13.5 %collective-permute-start.31 = (f32[2192,128]{1,0:T(8,128)S(1)}, f32[2192,128]{1,0:T(8,128)S(1)}, u32[]{:S(2)}, u32[]{:S(2)}) collective-permute-start(f32[2192,128]{1,0:T(8,128)S(1)} %pad_maximum_fusion.1.refs_1_), channel_id=1, source_target_pairs={{0,2},{2,0},{4,6},{6,4},{8,10},{10,8},{12,14},{14,12},{16,18},{18,... | collective-permute-start | bytes 3366920 | tf_op jit(solution)/shard_map/ppermute | solution.py:79
  133.3 3.0 %collective-permute-start.27 = (f32[8,128]{1,0:T(8,128)S(1)}, f32[8,128]{1,0:T(8,128)S(1)}, u32[]{:S(2)}, u32[]{:S(2)}) collective-permute-start(f32[8,128]{1,0:T(8,128)S(1)} %add.84), channel_id=1, source_target_pairs={{0,2},{2,0},{4,6},{6,4},{8,10},{10,8},{12,14},{14,12},{16,18},{18,... | collective-permute-start | bytes 12296 | tf_op jit(solution)/shard_map/ppermute | solution.py:79
  136.4 3.6 %collective-permute-start.28 = (f32[8,128]{1,0:T(8,128)S(1)}, f32[8,128]{1,0:T(8,128)S(1)}, u32[]{:S(2)}, u32[]{:S(2)}) collective-permute-start(f32[8,128]{1,0:T(8,128)S(1)} %add.85), channel_id=1, source_target_pairs={{0,1},{1,0},{2,3},{3,2},{4,5},{5,4},{6,7},{7,6},{8,9},{9,8},{10,11... | collective-permute-start | bytes 12296 | tf_op jit(solution)/shard_map/ppermute | solution.py:165
  140.0 6.9 %collective-permute-start.32 = (f32[1096,128]{1,0:T(8,128)S(1)}, f32[1096,128]{1,0:T(8,128)S(1)}, u32[]{:S(2)}, u32[]{:S(2)}) collective-permute-start(f32[1096,128]{1,0:T(8,128)S(1)} %add.83.refs_2_), channel_id=1, source_target_pairs={{0,2},{2,0},{4,6},{6,4},{8,10},{10,8},{12,14},{14,12},{16,18},{18,... | collective-permute-start | bytes 1683464 | tf_op jit(solution)/shard_map/ppermute | solution.py:79
  146.3 2.0 %collective-permute-start.33 = (f32[1096,128]{1,0:T(8,128)S(1)}, f32[1096,128]{1,0:T(8,128)S(1)}, u32[]{:S(2)}, u32[]{:S(2)}) collective-permute-start(f32[1096,128]{1,0:T(8,128)S(1)} %collective-permute-done.26.refs_3_), channel_id=1, source_target_pairs={{0,2},{2,0},{4,6},{6,4},{8,10},{10,8},{12,14},{14,12},{16,18},{18,... | collective-permute-start | bytes 1683464 | tf_op jit(solution)/shard_map/ppermute | solution.py:79
  146.3 2.8 %collective-permute-start.34 = (f32[1096,128]{1,0:T(8,128)S(1)}, f32[1096,128]{1,0:T(8,128)S(1)}, u32[]{:S(2)}, u32[]{:S(2)}) collective-permute-start(f32[1096,128]{1,0:T(8,128)S(1)} %collective-permute-done.29.refs_5_), channel_id=1, source_target_pairs={{0,2},{2,0},{4,6},{6,4},{8,10},{10,8},{12,14},{14,12},{16,18},{18,... | collective-permute-start | bytes 1683464 | tf_op jit(solution)/shard_map/ppermute | solution.py:79

commit v19 on v18

--- a/solution.py
+++ b/solution.py
@@ -172,6 +172,7 @@
         return line_gather(plan, "x", plan.nx, value)
 
     if plan.nz != 4:
+        ready = {}
         lines = [along_x(value) for value in line_gather(plan, "z", plan.nz, block)]
         total = all_cores(plan, all_sums(plan, my_place, [(line[0], 0) for line in lines]))
         mine = [(value, [(z, x)]) for z, line in enumerate(lines) for x, value in enumerate(line)]
@@ -194,10 +195,11 @@
         total, *line_two = together(total, *line_two)
         early = plan.swap(near_three)
         early, total, *line_three = together(early, all_cores(plan, total), *line_three)
+        ready = {(3, 0): early}
         mine = [(value, [(0, x), (1, x)]) for x, value in enumerate([own] + far)]
         mine += [(value, [(2, x)]) for x, value in enumerate(line_two)]
         mine += [(value, [(3, x)]) for x, value in enumerate(line_three)]
-    swapped = [early if plan.nz == 4 and slots == [(3, 0)] else plan.swap(value) for value, slots in mine]
+    swapped = [ready[slots[0]] if slots[0] in ready else plan.swap(value) for value, slots in mine]
     found = [(value, [slot + (0,) for slot in slots]) for value, slots in mine]
     found += [(value, [slot + (1,) for slot in slots]) for value, (_, slots) in zip(swapped, mine)]
     return found, total
@@ -216,7 +218,7 @@
     return [value, pair, across_two + out_two, across_three + out_three]
 
 
-def place_kernel(plan, place_ref, owner_ref, norm_ref, grads_ref, *refs):
+def place_kernel(plan, owner_ref, norm_ref, grads_ref, *refs):
     out_refs, refs = refs[: plan.replicas], refs[plan.replicas :]
     position_ref, raw, moved, position, sem_in, sem_position, sem_out = refs
     lines = plan.blocks // LANE
@@ -229,7 +231,8 @@
         fetches[-1].start()
     lists = plan.lists
     owners = owner_ref[...]
-    my_z, my_x, my_c = place_ref[0], place_ref[1], place_ref[2]
+    me = lax.axis_index("dp").astype(jnp.int32)
+    my_z, my_x, my_c = me // (2 * plan.nx), me // 2 % plan.nx, me % 2
     count = plan.replicas
     lane_in = lax.broadcasted_iota(jnp.int32, (LANE, LANE), 0)
     lane_out = lax.broadcasted_iota(jnp.int32, (LANE, LANE), 1)
@@ -308,14 +311,13 @@
         copy.wait()
 
 
-def place(plan, my_place, owners, norm_grads, grads):
+def place(plan, owners, norm_grads, grads):
     shapes = [(plan.block, LANE)] * plan.replicas
     outs = pl.pallas_call(
         functools.partial(place_kernel, plan),
         out_shape=[jax.ShapeDtypeStruct(s, jnp.float32) for s in shapes]
         + [jax.ShapeDtypeStruct((plan.lists, LANE), jnp.int32)],
         in_specs=[
-            pl.BlockSpec(memory_space=pltpu.SMEM),
             pl.BlockSpec(memory_space=pltpu.VMEM),
             pl.BlockSpec(memory_space=pltpu.VMEM),
             pl.BlockSpec(memory_space=pl.ANY),
@@ -331,7 +333,7 @@
         ],
         compiler_params=pltpu.CompilerParams(vmem_limit_bytes=58 * MIB),
         name="place_gradients",
-    )(my_place, owners, norm_grads, grads)
+    )(owners, norm_grads, grads)
     return dict(zip(plan.order(), outs)), outs[-1]
 
 
@@ -547,7 +549,7 @@
     my_place = jnp.stack([me // (2 * plan.nx), (me // 2) % plan.nx, me % 2]).astype(jnp.int32)
     owners = jnp.pad(owner_list[0], (0, plan.lists * LANE - plan.blocks), constant_values=-1)
     owners = owners.reshape(plan.lists, LANE)
-    placed, position = place(plan, my_place, owners, norm_grads[0], gradients[0])
+    placed, position = place(plan, owners, norm_grads[0], gradients[0])
     weight_own, natural = owned(plan, my_place, owners, weights)
 
     mine, theirs = [None] * plan.nz, [None] * plan.nz

time: 169 us -> 168 us (level)
  waiting for transfers between devices: 73.1 us -> 71.4 us
    ppermute x34, waiting for transfers between devices: 71 us -> 69.3 us  [send(): return lax.ppermute(value, 'dp', every)]
  transfers between devices with their start and end apart: 35 -> 35, of which waited for: 18 -> 18; matrix products, arithmetic and copies ran while one was open for 1% -> 2% of each run, Pallas kernels for 4% -> 4%
where the time goes in v19:
time: 168 us
  waiting for transfers between devices  71.4 us (43%)
  Pallas kernels  50.1 us (30%)
  starting transfers between devices  41.5 us (25%)
  other arithmetic  3.86 us (2%)
    ppermute x34, waiting for transfers between devices, send(): return lax.ppermute(value, 'dp', every)  69.3 us
    ppermute x34, starting transfers between devices, send(): return lax.ppermute(value, 'dp', every)  40 us
    pallas_call x1, Pallas kernels, place(): pl.pallas_call(functools.partial(place_kernel, plan), out_shape=[jax.Shap...  21.4 us
    pallas_call x1, Pallas kernels, finish(): pl.pallas_call(functools.partial(finish_kernel, plan, tile, slots), grid=...  19.6 us
    pallas_call x1, Pallas kernels, owned(): pl.pallas_call(functools.partial(owned_kernel, plan), out_shape=[jax.Shap...  6.44 us
  transfers between devices with their start and end apart: 35, of which 18 were waited for; matrix products, arithmetic and copies ran while one was open for 2% of the time, Pallas kernels for 4%

profile of v19, /device:TPU:0, one launch (start us, length us, event | category | flops | bytes accessed | tf_op | source)
XLA Modules:
  0.0 168.0 jit_solution(13534733321733551875)
XLA Ops:
  0.6 21.4 %place_gradients.1 = (f32[1096,128]{1,0:T(8,128)}, f32[1096,128]{1,0:T(8,128)}, f32[1096,128]{1,0:T(8,128)}, f32[1096,128]{1,0:T(8,128)}, f32[1096,128]{1,0:T(8,...) custom-call(s32[136,128]{1,0:T(8,128)} %bitcast.15, ...), custom_call_target="tpu_custom_call" | custom-call | tf_op jit(solution)/shard_map/place_gradients/pallas_call | solution.py:316
  22.0 0.5 collective-permute-start
  22.6 1.8 %collective-permute-done = f32[1096,128]{1,0:T(8,128)S(1)} collective-permute-done((f32[1096,128]{1,0:T(8,128)}, f32[1096,128]{1,0:T(8,128)S(1)}, u32[]{:S(2)}, u32[]{:S(2)}) %collective-permute-start) | collective-permute-done | bytes 561184 | tf_op jit(solution)/shard_map/ppermute | solution.py:79
  24.4 1.1 add.68
  25.5 0.4 collective-permute-start.8
  25.9 0.1 collective-permute-start.4
  26.1 2.9 %collective-permute-start.5 = (f32[1096,128]{1,0:T(8,128)S(1)}, f32[1096,128]{1,0:T(8,128)S(1)}, u32[]{:S(2)}, u32[]{:S(2)}) collective-permute-start(f32[1096,128]{1,0:T(8,128)S(1)} %add.68), channel_id=1, source_target_pairs={{0,4},{2,6},{4,0},{6,2},{8,12},{10,14},{12,8},{14,10},{16,20},{18,... | collective-permute-start | bytes 1683464 | tf_op jit(solution)/shard_map/ppermute | solution.py:79
  28.9 0.5 collective-permute-start.13
  29.5 1.2 collective-permute-start.9
  30.7 11.7 %collective-permute-done.5 = f32[1096,128]{1,0:T(8,128)S(1)} collective-permute-done((f32[1096,128]{1,0:T(8,128)S(1)}, f32[1096,128]{1,0:T(8,128)S(1)}, u32[]{:S(2)}, u32[]{:S(2)}) %collective-permute-start.5) | collective-permute-done | bytes 561184 | tf_op jit(solution)/shard_map/ppermute | solution.py:79
  42.4 0.1 add_add_fusion.2
  42.5 4.1 %collective-permute-start.6 = (f32[1096,128]{1,0:T(8,128)S(1)}, f32[1096,128]{1,0:T(8,128)S(1)}, u32[]{:S(2)}, u32[]{:S(2)}) collective-permute-start(f32[1096,128]{1,0:T(8,128)S(1)} %add_add_fusion.2), channel_id=1, source_target_pairs={{0,8},{2,10},{4,12},{6,14},{24,16},{26,18},{28,20},{30,22},{1,9},{... | collective-permute-start | bytes 1683464 | tf_op jit(solution)/shard_map/ppermute | solution.py:79
  46.6 0.6 pad_add_fusion.place_ref
  47.2 6.4 %owned_weights.1 = (f32[1088,128]{1,0:T(8,128)}, s32[1152,128]{1,0:T(8,128)}) custom-call(s32[3]{0:T(128)} %pad_add_fusion.place_ref, s32[136,128]{1,0:T(8,128)} %bitcast.16, f32[17408,128]{1,0:T(8,128)} %weights_ref.3), custom_call_target="tpu_custom_call" | custom-call | bytes 20971520 | tf_op jit(solution)/shard_map/owned_weights/pallas_call | solution.py:393
  53.8 0.5 collective-permute-start.12
  54.3 1.1 add.79
  55.4 1.6 collective-permute-start.14
  57.0 0.1 add_add_fusion.1
  57.1 0.1 collective-permute-done.6
  57.2 4.4 %collective-permute-start.11 = (f32[1096,128]{1,0:T(8,128)S(1)}, f32[1096,128]{1,0:T(8,128)S(1)}, u32[]{:S(2)}, u32[]{:S(2)}) collective-permute-start(f32[1096,128]{1,0:T(8,128)S(1)} %add_add_fusion.1), channel_id=1, source_target_pairs={{0,8},{2,10},{4,12},{6,14},{24,16},{26,18},{28,20},{30,22},{1,9},{... | collective-permute-start | bytes 1683464 | tf_op jit(solution)/shard_map/ppermute | solution.py:79
  61.6 0.1 add.76
  61.7 0.8 collective-permute-start.10
  62.7 1.6 collective-permute-start.3
  64.3 6.7 %collective-permute-done.14 = f32[1096,128]{1,0:T(8,128)S(1)} collective-permute-done((f32[1096,128]{1,0:T(8,128)S(1)}, f32[1096,128]{1,0:T(8,128)S(1)}, u32[]{:S(2)}, u32[]{:S(2)}) %collective-permute-start.14) | collective-permute-done | bytes 561184 | tf_op jit(solution)/shard_map/ppermute | solution.py:79
  71.0 0.1 add_add_fusion
  71.1 0.2 collective-permute-done.11
  71.3 0.1 add.77
  71.4 0.1 add.81
  71.5 3.9 %collective-permute-start.15 = (f32[1096,128]{1,0:T(8,128)S(1)}, f32[1096,128]{1,0:T(8,128)S(1)}, u32[]{:S(2)}, u32[]{:S(2)}) collective-permute-start(f32[1096,128]{1,0:T(8,128)S(1)} %add.81), channel_id=1, source_target_pairs={{0,8},{2,10},{4,12},{6,14},{8,0},{10,2},{12,4},{14,6},{16,24},{18,... | collective-permute-start | bytes 1683464 | tf_op jit(solution)/shard_map/ppermute | solution.py:79
  75.5 0.7 collective-permute-start.16
  76.2 0.1 add.69.refs_0_
  76.3 5.9 %collective-permute-done.3.refs_1_ = f32[1096,128]{1,0:T(8,128)S(1)} collective-permute-done((f32[1096,128]{1,0:T(8,128)S(1)}, f32[1096,128]{1,0:T(8,128)S(1)}, u32[]{:S(2)}, u32[]{:S(2)}) %collective-permute-start.3) | collective-permute-done | bytes 561184 | tf_op jit(solution)/shard_map/ppermute | solution.py:79
  82.2 2.8 %collective-permute-done.15.refs_2_ = f32[1096,128]{1,0:T(8,128)S(1)} collective-permute-done((f32[1096,128]{1,0:T(8,128)S(1)}, f32[1096,128]{1,0:T(8,128)S(1)}, u32[]{:S(2)}, u32[]{:S(2)}) %collective-permute-start.15) | collective-permute-done | bytes 561184 | tf_op jit(solution)/shard_map/ppermute | solution.py:79
  85.1 2.0 %moments.1 = (f32[1088,128]{1,0:T(8,128)}, f32[1088,128]{1,0:T(8,128)}, f32[1096,128]{1,0:T(8,128)S(1)}) custom-call(f32[1096,128]{1,0:T(8,128)S(1)} %add.69.refs_0_, f32[1096,128]{1,0:T(8,128)S(1)} %collective-permute-done.3.refs_1_, f32[1096,128]{1,0:T(8,128)S(1)} %collective-permute-done.15.refs_2_, f32[1096,128]{1,0:T(8,128)S(1)} %collective-permute-done.16.refs_3_, ...), custom_call_target="tpu_custom_call" | custom-call | tf_op jit(solution)/shard_map/moments/pallas_call | solution.py:447
  87.1 3.8 %collective-permute-start.18 = (f32[1096,128]{1,0:T(8,128)S(1)}, f32[1096,128]{1,0:T(8,128)S(1)}, u32[]{:S(2)}, u32[]{:S(2)}) collective-permute-start(f32[1096,128]{1,0:T(8,128)S(1)} %get-tuple-element.92), channel_id=1, source_target_pairs={{0,8},{2,10},{4,12},{6,14},{8,0},{10,2},{12,4},{14,6},{16,24},{18,... | collective-permute-start | bytes 1683464 | tf_op jit(solution)/shard_map/ppermute | solution.py:79
  90.9 1.5 collective-permute-start.19
  92.4 0.7 collective-permute-start.17
  93.1 6.4 %collective-permute-done.18 = f32[1096,128]{1,0:T(8,128)S(1)} collective-permute-done((f32[1096,128]{1,0:T(8,128)S(1)}, f32[1096,128]{1,0:T(8,128)S(1)}, u32[]{:S(2)}, u32[]{:S(2)}) %collective-permute-start.18) | collective-permute-done | bytes 561184 | tf_op jit(solution)/shard_map/ppermute | solution.py:79
  99.6 1.5 collective-permute-start.24
  101.0 0.7 collective-permute-start.20
  101.7 0.1 pad_maximum_fusion.refs_0_.refs_1_
  101.8 2.9 %collective-permute-done.19 = f32[1096,128]{1,0:T(8,128)S(1)} collective-permute-done((f32[1096,128]{1,0:T(8,128)S(1)}, f32[1096,128]{1,0:T(8,128)S(1)}, u32[]{:S(2)}, u32[]{:S(2)}) %collective-permute-start.19) | collective-permute-done | bytes 561184 | tf_op jit(solution)/shard_map/ppermute | solution.py:79
  104.7 1.3 collective-permute-start.23
  106.0 1.3 collective-permute-start.21
  107.3 6.4 %collective-permute-done.24 = f32[1096,128]{1,0:T(8,128)S(1)} collective-permute-done((f32[1096,128]{1,0:T(8,128)S(1)}, f32[1096,128]{1,0:T(8,128)S(1)}, u32[]{:S(2)}, u32[]{:S(2)}) %collective-permute-start.24) | collective-permute-done | bytes 561184 | tf_op jit(solution)/shard_map/ppermute | solution.py:79
  113.7 3.7 %collective-permute-done.23 = f32[1096,128]{1,0:T(8,128)S(1)} collective-permute-done((f32[1096,128]{1,0:T(8,128)S(1)}, f32[1096,128]{1,0:T(8,128)S(1)}, u32[]{:S(2)}, u32[]{:S(2)}) %collective-permute-start.23) | collective-permute-done | bytes 561184 | tf_op jit(solution)/shard_map/ppermute | solution.py:79
  117.4 0.1 add.83.refs_2_
  117.5 0.1 pad_maximum_fusion.1.refs_1_
  117.6 2.5 %collective-permute-start.26 = (f32[1096,128]{1,0:T(8,128)S(1)}, f32[1096,128]{1,0:T(8,128)S(1)}, u32[]{:S(2)}, u32[]{:S(2)}) collective-permute-start(f32[1096,128]{1,0:T(8,128)S(1)} %add.83.refs_2_), channel_id=1, source_target_pairs={{0,4},{2,6},{4,0},{6,2},{8,12},{10,14},{12,8},{14,10},{16,20},{18,... | collective-permute-start | bytes 1683464 | tf_op jit(solution)/shard_map/ppermute | solution.py:79
  120.1 8.1 %collective-permute-done.21 = f32[1096,128]{1,0:T(8,128)S(1)} collective-permute-done((f32[1096,128]{1,0:T(8,128)S(1)}, f32[1096,128]{1,0:T(8,128)S(1)}, u32[]{:S(2)}, u32[]{:S(2)}) %collective-permute-start.21) | collective-permute-done | bytes 561184 | tf_op jit(solution)/shard_map/ppermute | solution.py:79
  128.3 0.6 sums.1
  128.9 1.6 collective-permute-start.25
  130.4 0.5 collective-permute-start.29
  131.0 0.2 collective-permute-start.22
  131.2 1.3 collective-permute-done.25
  132.5 0.5 collective-permute-start.27
  133.1 2.5 %collective-permute-done.27 = f32[8,128]{1,0:T(8,128)S(1)} collective-permute-done((f32[8,128]{1,0:T(8,128)S(1)}, f32[8,128]{1,0:T(8,128)S(1)}, u32[]{:S(2)}, u32[]{:S(2)}) %collective-permute-start.27) | collective-permute-done | bytes 4128 | tf_op jit(solution)/shard_map/ppermute | solution.py:79
  135.6 1.5 collective-permute-start.28
  137.1 2.1 %collective-permute-done.28 = f32[8,128]{1,0:T(8,128)S(1)} collective-permute-done((f32[8,128]{1,0:T(8,128)S(1)}, f32[8,128]{1,0:T(8,128)S(1)}, u32[]{:S(2)}, u32[]{:S(2)}) %collective-permute-start.28) | collective-permute-done | bytes 4128 | tf_op jit(solution)/shard_map/ppermute | solution.py:165
  139.2 6.3 %collective-permute-done.29.refs_5_ = f32[1096,128]{1,0:T(8,128)S(1)} collective-permute-done((f32[1096,128]{1,0:T(8,128)S(1)}, f32[1096,128]{1,0:T(8,128)S(1)}, u32[]{:S(2)}, u32[]{:S(2)}) %collective-permute-start.29) | collective-permute-done | bytes 561184 | tf_op jit(solution)/shard_map/ppermute | solution.py:79
  145.6 0.5 collective-permute-start.34
  146.1 1.4 collective-permute-done.33.refs_9_
  147.5 0.8 collective-permute-done.34.refs_11_
  148.3 19.6 %new_weights.1 = (f32[17408,128]{1,0:T(8,128)}, f32[3,2,1024]{2,1,0:T(2,128)}, f32[7]{0:T(128)}) custom-call(s32[3]{0:T(128)S(1)} %copy-done.6, s32[136,128]{1,0:T(8,128)S(1)} %copy-done.4, f32[8,128]{1,0:T(8,128)S(1)} %add.86.total_ref, f32[3,2,1024]{2,1,0:T(2,128)S(1)} %copy-done.5, f32[17408,128]{1,0:T(8,128)S(1)} %bitcast.11, ...), custom_call_target="tpu_custom_call" | custom-call | tf_op jit(solution)/shard_map/new_weights/pallas_call | solution.py:525
  (71 shorter events, 0.5 us)
Async XLA Ops:
  22.0 7.4 %copy-start.13 = (f32[1096,128]{1,0:T(8,128)S(1)}, f32[1096,128]{1,0:T(8,128)}, u32[]{:S(2)}) copy-start(f32[1096,128]{1,0:T(8,128)} %get-tuple-element.77) | copy-start | bytes 1683460
  22.0 2.3 %collective-permute-start = (f32[1096,128]{1,0:T(8,128)}, f32[1096,128]{1,0:T(8,128)S(1)}, u32[]{:S(2)}, u32[]{:S(2)}) collective-permute-start(f32[1096,128]{1,0:T(8,128)} %get-tuple-element.61), channel_id=1, source_target_pairs={{0,2},{2,0},{4,6},{6,4},{8,10},{10,8},{12,14},{14,12},{16,18},{18,... | collective-permute-start | bytes 1683464 | tf_op jit(solution)/shard_map/ppermute | solution.py:79
  25.5 16.9 %copy-start.12 = (f32[1096,128]{1,0:T(8,128)S(1)}, f32[1096,128]{1,0:T(8,128)}, u32[]{:S(2)}) copy-start(f32[1096,128]{1,0:T(8,128)} %get-tuple-element.72) | copy-start | bytes 1683460
  25.5 4.0 %collective-permute-start.8 = (f32[1096,128]{1,0:T(8,128)}, f32[1096,128]{1,0:T(8,128)S(1)}, u32[]{:S(2)}, u32[]{:S(2)}) collective-permute-start(f32[1096,128]{1,0:T(8,128)} %get-tuple-element.78), channel_id=1, source_target_pairs={{0,2},{2,0},{4,6},{6,4},{8,10},{10,8},{12,14},{14,12},{16,18},{18,... | collective-permute-start | bytes 1683464 | tf_op jit(solution)/shard_map/ppermute | solution.py:79
  25.9 4.8 %collective-permute-start.4 = (f32[1096,128]{1,0:T(8,128)}, f32[1096,128]{1,0:T(8,128)S(1)}, u32[]{:S(2)}, u32[]{:S(2)}) collective-permute-start(f32[1096,128]{1,0:T(8,128)} %get-tuple-element.73), channel_id=1, source_target_pairs={{0,2},{2,0},{4,6},{6,4},{8,10},{10,8},{12,14},{14,12},{16,18},{18,... | collective-permute-start | bytes 1683464 | tf_op jit(solution)/shard_map/ppermute | solution.py:79
  26.1 16.4 %collective-permute-start.5 = (f32[1096,128]{1,0:T(8,128)S(1)}, f32[1096,128]{1,0:T(8,128)S(1)}, u32[]{:S(2)}, u32[]{:S(2)}) collective-permute-start(f32[1096,128]{1,0:T(8,128)S(1)} %add.68), channel_id=1, source_target_pairs={{0,4},{2,6},{4,0},{6,2},{8,12},{10,14},{12,8},{14,10},{16,20},{18,... | collective-permute-start | bytes 1683464 | tf_op jit(solution)/shard_map/ppermute | solution.py:79
  28.9 26.5 %collective-permute-start.7 = (f32[1096,128]{1,0:T(8,128)}, f32[1096,128]{1,0:T(8,128)S(1)}, u32[]{:S(2)}, u32[]{:S(2)}) collective-permute-start(f32[1096,128]{1,0:T(8,128)} %get-tuple-element.76), channel_id=1, source_target_pairs={{0,2},{2,0},{4,6},{6,4},{8,10},{10,8},{12,14},{14,12},{16,18},{18,... | collective-permute-start | bytes 1683464 | tf_op jit(solution)/shard_map/ppermute | solution.py:79
  28.9 24.8 %collective-permute-start.13 = (f32[1096,128]{1,0:T(8,128)}, f32[1096,128]{1,0:T(8,128)}, u32[]{:S(2)}, u32[]{:S(2)}) collective-permute-start(f32[1096,128]{1,0:T(8,128)} %get-tuple-element.86), channel_id=1, source_target_pairs={{0,2},{2,0},{4,6},{6,4},{8,10},{10,8},{12,14},{14,12},{16,18},{18,... | collective-permute-start | bytes 1683464 | tf_op jit(solution)/shard_map/ppermute | solution.py:79
  29.5 27.4 %collective-permute-start.9 = (f32[1096,128]{1,0:T(8,128)S(1)}, f32[1096,128]{1,0:T(8,128)S(1)}, u32[]{:S(2)}, u32[]{:S(2)}) collective-permute-start(f32[1096,128]{1,0:T(8,128)S(1)} %add.74), channel_id=1, source_target_pairs={{0,4},{2,6},{4,0},{6,2},{8,12},{10,14},{12,8},{14,10},{16,20},{18,... | collective-permute-start | bytes 1683464 | tf_op jit(solution)/shard_map/ppermute | solution.py:79
  42.5 14.7 %collective-permute-start.6 = (f32[1096,128]{1,0:T(8,128)S(1)}, f32[1096,128]{1,0:T(8,128)S(1)}, u32[]{:S(2)}, u32[]{:S(2)}) collective-permute-start(f32[1096,128]{1,0:T(8,128)S(1)} %add_add_fusion.2), channel_id=1, source_target_pairs={{0,8},{2,10},{4,12},{6,14},{24,16},{26,18},{28,20},{30,22},{1,9},{... | collective-permute-start | bytes 1683464 | tf_op jit(solution)/shard_map/ppermute | solution.py:79
  47.2 6.5 %copy-start.16 = (f32[1096,128]{1,0:T(8,128)S(1)}, f32[1096,128]{1,0:T(8,128)}, u32[]{:S(2)}) copy-start(f32[1096,128]{1,0:T(8,128)} %get-tuple-element.71) | copy-start | bytes 1683460
  47.2 6.6 %copy-start.15 = (f32[1096,128]{1,0:T(8,128)S(1)}, f32[1096,128]{1,0:T(8,128)}, u32[]{:S(2)}) copy-start(f32[1096,128]{1,0:T(8,128)} %get-tuple-element.84) | copy-start | bytes 1683460
  47.2 7.1 %copy-start.11 = (f32[1096,128]{1,0:T(8,128)S(1)}, f32[1096,128]{1,0:T(8,128)}, u32[]{:S(2)}) copy-start(f32[1096,128]{1,0:T(8,128)} %get-tuple-element.85) | copy-start | bytes 1683460
  53.7 3.3 %copy-start.10 = (f32[1096,128]{1,0:T(8,128)S(1)}, f32[1096,128]{1,0:T(8,128)}, u32[]{:S(2)}) copy-start(f32[1096,128]{1,0:T(8,128)} %get-tuple-element.75) | copy-start | bytes 1683460
  53.7 8.9 %collective-permute-start.2 = (f32[1096,128]{1,0:T(8,128)S(1)}, f32[1096,128]{1,0:T(8,128)S(1)}, u32[]{:S(2)}, u32[]{:S(2)}) collective-permute-start(f32[1096,128]{1,0:T(8,128)S(1)} %copy-done.16), channel_id=1, source_target_pairs={{0,2},{2,0},{4,6},{6,4},{8,10},{10,8},{12,14},{14,12},{16,18},{18,... | collective-permute-start | bytes 1683464 | tf_op jit(solution)/shard_map/ppermute | solution.py:79
  53.8 8.9 %collective-permute-start.12 = (f32[1096,128]{1,0:T(8,128)S(1)}, f32[1096,128]{1,0:T(8,128)S(1)}, u32[]{:S(2)}, u32[]{:S(2)}) collective-permute-start(f32[1096,128]{1,0:T(8,128)S(1)} %copy-done.15), channel_id=1, source_target_pairs={{0,2},{2,0},{4,6},{6,4},{8,10},{10,8},{12,14},{14,12},{16,18},{18,... | collective-permute-start | bytes 1683464 | tf_op jit(solution)/shard_map/ppermute | solution.py:79
  55.4 15.6 %collective-permute-start.14 = (f32[1096,128]{1,0:T(8,128)S(1)}, f32[1096,128]{1,0:T(8,128)S(1)}, u32[]{:S(2)}, u32[]{:S(2)}) collective-permute-start(f32[1096,128]{1,0:T(8,128)S(1)} %add.79), channel_id=1, source_target_pairs={{0,4},{2,6},{4,0},{6,2},{8,12},{10,14},{12,8},{14,10},{16,20},{18,... | collective-permute-start | bytes 1683464 | tf_op jit(solution)/shard_map/ppermute | solution.py:79
  57.1 5.5 %copy-start.14 = (f32[1096,128]{1,0:T(8,128)S(1)}, f32[1096,128]{1,0:T(8,128)}, u32[]{:S(2)}) copy-start(f32[1096,128]{1,0:T(8,128)} %get-tuple-element.69) | copy-start | bytes 1683460
  57.1 5.6 %copy-start.9 = (f32[1096,128]{1,0:T(8,128)S(1)}, f32[1096,128]{1,0:T(8,128)}, u32[]{:S(2)}) copy-start(f32[1096,128]{1,0:T(8,128)} %get-tuple-element.70) | copy-start | bytes 1683460
  57.2 14.1 %collective-permute-start.11 = (f32[1096,128]{1,0:T(8,128)S(1)}, f32[1096,128]{1,0:T(8,128)S(1)}, u32[]{:S(2)}, u32[]{:S(2)}) collective-permute-start(f32[1096,128]{1,0:T(8,128)S(1)} %add_add_fusion.1), channel_id=1, source_target_pairs={{0,8},{2,10},{4,12},{6,14},{24,16},{26,18},{28,20},{30,22},{1,9},{... | collective-permute-start | bytes 1683464 | tf_op jit(solution)/shard_map/ppermute | solution.py:79
  61.7 9.3 %copy-start.8 = (f32[1096,128]{1,0:T(8,128)S(1)}, f32[1096,128]{1,0:T(8,128)}, u32[]{:S(2)}) copy-start(f32[1096,128]{1,0:T(8,128)} %get-tuple-element.83) | copy-start | bytes 1683460
  61.7 9.7 %collective-permute-start.10 = (f32[1096,128]{1,0:T(8,128)S(1)}, f32[1096,128]{1,0:T(8,128)S(1)}, u32[]{:S(2)}, u32[]{:S(2)}) collective-permute-start(f32[1096,128]{1,0:T(8,128)S(1)} %add.76), channel_id=1, source_target_pairs={{8,16},{10,18},{12,20},{14,22},{16,8},{18,10},{20,12},{22,14},{9,1... | collective-permute-start | bytes 1683464 | tf_op jit(solution)/shard_map/ppermute | solution.py:79
  62.6 13.6 %collective-permute-start.1 = (f32[1096,128]{1,0:T(8,128)S(1)}, f32[1096,128]{1,0:T(8,128)S(1)}, u32[]{:S(2)}, u32[]{:S(2)}) collective-permute-start(f32[1096,128]{1,0:T(8,128)S(1)} %copy-done.14), channel_id=1, source_target_pairs={{0,2},{2,0},{4,6},{6,4},{8,10},{10,8},{12,14},{14,12},{16,18},{18,... | collective-permute-start | bytes 1683464 | tf_op jit(solution)/shard_map/ppermute | solution.py:79
  62.7 19.5 %collective-permute-start.3 = (f32[1096,128]{1,0:T(8,128)S(1)}, f32[1096,128]{1,0:T(8,128)S(1)}, u32[]{:S(2)}, u32[]{:S(2)}) collective-permute-start(f32[1096,128]{1,0:T(8,128)S(1)} %add.70), channel_id=1, source_target_pairs={{0,4},{2,6},{4,0},{6,2},{8,12},{10,14},{12,8},{14,10},{16,20},{18,... | collective-permute-start | bytes 1683464 | tf_op jit(solution)/shard_map/ppermute | solution.py:79
  71.0 77.3 %slice-start = ((s8[8912896]{0:T(1024)(128)(4,1)}), s8[4194304]{0:T(1024)(128)(4,1)S(1)}, s32[]{:S(2)}) async-start(s8[8912896]{0:T(1024)(128)(4,1)} %bitcast.10), calls=%async_computation | async-start | bytes 8388608
  71.4 4.8 %copy-start.7 = (f32[1096,128]{1,0:T(8,128)S(1)}, f32[1096,128]{1,0:T(8,128)}, u32[]{:S(2)}) copy-start(f32[1096,128]{1,0:T(8,128)} %get-tuple-element.59) | copy-start | bytes 1683460
  71.4 13.6 %copy-start.2 = (f32[1,1088,128]{2,1,0:T(8,128)S(1)}, f32[1,1088,128]{2,1,0:T(8,128)}, u32[]{:S(2)}) copy-start(f32[1,1088,128]{2,1,0:T(8,128)} %param.10) | copy-start | bytes 1671172
  71.4 13.6 %copy-start.3 = (f32[1088,128]{1,0:T(8,128)S(1)}, f32[1088,128]{1,0:T(8,128)}, u32[]{:S(2)}) copy-start(f32[1088,128]{1,0:T(8,128)} %get-tuple-element.90.refs_6_) | copy-start | bytes 1671172
  71.5 13.5 %copy-start = (s32[1152,128]{1,0:T(8,128)S(1)}, s32[1152,128]{1,0:T(8,128)}, u32[]{:S(2)}) copy-start(s32[1152,128]{1,0:T(8,128)} %get-tuple-element.91.refs_7_) | copy-start | bytes 1769476
  71.5 13.5 %copy-start.1 = (f32[1,1088,128]{2,1,0:T(8,128)S(1)}, f32[1,1088,128]{2,1,0:T(8,128)}, u32[]{:S(2)}) copy-start(f32[1,1088,128]{2,1,0:T(8,128)} %param.9) | copy-start | bytes 1671172
  71.5 13.5 %collective-permute-start.15 = (f32[1096,128]{1,0:T(8,128)S(1)}, f32[1096,128]{1,0:T(8,128)S(1)}, u32[]{:S(2)}, u32[]{:S(2)}) collective-permute-start(f32[1096,128]{1,0:T(8,128)S(1)} %add.81), channel_id=1, source_target_pairs={{0,8},{2,10},{4,12},{6,14},{8,0},{10,2},{12,4},{14,6},{16,24},{18,... | collective-permute-start | bytes 1683464 | tf_op jit(solution)/shard_map/ppermute | solution.py:79
  75.5 9.5 %collective-permute-start.16 = (f32[1096,128]{1,0:T(8,128)S(1)}, f32[1096,128]{1,0:T(8,128)S(1)}, u32[]{:S(2)}, u32[]{:S(2)}) collective-permute-start(f32[1096,128]{1,0:T(8,128)S(1)} %add.77), channel_id=1, source_target_pairs={{8,16},{10,18},{12,20},{14,22},{16,8},{18,10},{20,12},{22,14},{9,1... | collective-permute-start | bytes 1683464 | tf_op jit(solution)/shard_map/ppermute | solution.py:79
  85.0 63.3 %slice-start.1 = ((s8[8912896]{0:T(1024)(128)(4,1)}), s8[4194304]{0:T(1024)(128)(4,1)S(1)}, s32[]{:S(2)}) async-start(s8[8912896]{0:T(1024)(128)(4,1)} %bitcast.10), calls=%async_computation.1 | async-start | bytes 8388608
  87.1 12.5 %collective-permute-start.18 = (f32[1096,128]{1,0:T(8,128)S(1)}, f32[1096,128]{1,0:T(8,128)S(1)}, u32[]{:S(2)}, u32[]{:S(2)}) collective-permute-start(f32[1096,128]{1,0:T(8,128)S(1)} %get-tuple-element.92), channel_id=1, source_target_pairs={{0,8},{2,10},{4,12},{6,14},{8,0},{10,2},{12,4},{14,6},{16,24},{18,... | collective-permute-start | bytes 1683464 | tf_op jit(solution)/shard_map/ppermute | solution.py:79
  90.9 13.8 %collective-permute-start.19 = (f32[1096,128]{1,0:T(8,128)S(1)}, f32[1096,128]{1,0:T(8,128)S(1)}, u32[]{:S(2)}, u32[]{:S(2)}) collective-permute-start(f32[1096,128]{1,0:T(8,128)S(1)} %get-tuple-element.92), channel_id=1, source_target_pairs={{0,4},{2,6},{4,0},{6,2},{8,12},{10,14},{12,8},{14,10},{16,20},{18,... | collective-permute-start | bytes 1683464 | tf_op jit(solution)/shard_map/ppermute | solution.py:79
  92.4 12.3 %collective-permute-start.17 = (f32[1096,128]{1,0:T(8,128)S(1)}, f32[1096,128]{1,0:T(8,128)S(1)}, u32[]{:S(2)}, u32[]{:S(2)}) collective-permute-start(f32[1096,128]{1,0:T(8,128)S(1)} %get-tuple-element.92), channel_id=1, source_target_pairs={{8,16},{10,18},{12,20},{14,22},{16,8},{18,10},{20,12},{22,14},{9,1... | collective-permute-start | bytes 1683464 | tf_op jit(solution)/shard_map/ppermute | solution.py:79
  99.6 14.2 %collective-permute-start.24 = (f32[1096,128]{1,0:T(8,128)S(1)}, f32[1096,128]{1,0:T(8,128)S(1)}, u32[]{:S(2)}, u32[]{:S(2)}) collective-permute-start(f32[1096,128]{1,0:T(8,128)S(1)} %collective-permute-done.18), channel_id=1, source_target_pairs={{0,4},{2,6},{4,0},{6,2},{8,12},{10,14},{12,8},{14,10},{16,20},{18,... | collective-permute-start | bytes 1683464 | tf_op jit(solution)/shard_map/ppermute | solution.py:79
  101.0 5.0 %collective-permute-start.20 = (f32[1096,128]{1,0:T(8,128)S(1)}, f32[1096,128]{1,0:T(8,128)S(1)}, u32[]{:S(2)}, u32[]{:S(2)}) collective-permute-start(f32[1096,128]{1,0:T(8,128)S(1)} %collective-permute-done.18), channel_id=1, source_target_pairs={{8,16},{10,18},{12,20},{14,22},{16,8},{18,10},{20,12},{22,14},{9,1... | collective-permute-start | bytes 1683464 | tf_op jit(solution)/shard_map/ppermute | solution.py:79
  101.8 46.5 %slice-start.2 = ((s8[8912896]{0:T(1024)(128)(4,1)}), s8[524288]{0:T(1024)(128)(4,1)S(1)}, s32[]{:S(2)}) async-start(s8[8912896]{0:T(1024)(128)(4,1)} %bitcast.10), calls=%async_computation.2 | async-start | bytes 1048576
  104.7 12.7 %collective-permute-start.23 = (f32[1096,128]{1,0:T(8,128)S(1)}, f32[1096,128]{1,0:T(8,128)S(1)}, u32[]{:S(2)}, u32[]{:S(2)}) collective-permute-start(f32[1096,128]{1,0:T(8,128)S(1)} %collective-permute-done.17), channel_id=1, source_target_pairs={{8,0},{10,2},{12,4},{14,6},{16,24},{18,26},{20,28},{22,30},{9,1},{... | collective-permute-start | bytes 1683464 | tf_op jit(solution)/shard_map/ppermute | solution.py:79
  106.0 22.2 %collective-permute-start.21 = (f32[1096,128]{1,0:T(8,128)S(1)}, f32[1096,128]{1,0:T(8,128)S(1)}, u32[]{:S(2)}, u32[]{:S(2)}) collective-permute-start(f32[1096,128]{1,0:T(8,128)S(1)} %collective-permute-done.20), channel_id=1, source_target_pairs={{8,0},{10,2},{12,4},{14,6},{16,24},{18,26},{20,28},{22,30},{9,1},{... | collective-permute-start | bytes 1683464 | tf_op jit(solution)/shard_map/ppermute | solution.py:79
  117.6 10.7 %copy-start.6 = (s32[3]{0:T(128)S(1)}, s32[3]{0:T(128)}, u32[]{:S(2)}) copy-start(s32[3]{0:T(128)} %pad_add_fusion.place_ref) | copy-start | bytes 40
  117.6 15.0 %collective-permute-start.26 = (f32[1096,128]{1,0:T(8,128)S(1)}, f32[1096,128]{1,0:T(8,128)S(1)}, u32[]{:S(2)}, u32[]{:S(2)}) collective-permute-start(f32[1096,128]{1,0:T(8,128)S(1)} %add.83.refs_2_), channel_id=1, source_target_pairs={{0,4},{2,6},{4,0},{6,2},{8,12},{10,14},{12,8},{14,10},{16,20},{18,... | collective-permute-start | bytes 1683464 | tf_op jit(solution)/shard_map/ppermute | solution.py:79
  128.3 20.0 %copy-start.4 = (s32[136,128]{1,0:T(8,128)S(1)}, s32[136,128]{1,0:T(8,128)}, u32[]{:S(2)}) copy-start(s32[136,128]{1,0:T(8,128)} %get-tuple-element.58.position_ref) | copy-start | bytes 208900
  128.3 20.0 %copy-start.5 = (f32[3,2,1024]{2,1,0:T(2,128)S(1)}, f32[3,2,1024]{2,1,0:T(2,128)}, u32[]{:S(2)}) copy-start(f32[3,2,1024]{2,1,0:T(2,128)} %norm_ref.1) | copy-start | bytes 73732
  128.9 3.7 %collective-permute-start.25 = (f32[8,128]{1,0:T(8,128)S(1)}, f32[8,128]{1,0:T(8,128)S(1)}, u32[]{:S(2)}, u32[]{:S(2)}) collective-permute-start(f32[8,128]{1,0:T(8,128)S(1)} %sums.1), channel_id=1, source_target_pairs={{0,4},{2,6},{4,0},{6,2},{8,12},{10,14},{12,8},{14,10},{16,20},{18,... | collective-permute-start | bytes 12296 | tf_op jit(solution)/shard_map/ppermute | solution.py:79
  130.4 15.6 %collective-permute-start.30 = (f32[2192,128]{1,0:T(8,128)S(1)}, f32[2192,128]{1,0:T(8,128)S(1)}, u32[]{:S(2)}, u32[]{:S(2)}) collective-permute-start(f32[2192,128]{1,0:T(8,128)S(1)} %pad_maximum_fusion.refs_0_.refs_1_), channel_id=1, source_target_pairs={{0,2},{2,0},{4,6},{6,4},{8,10},{10,8},{12,14},{14,12},{16,18},{18,... | collective-permute-start | bytes 3366920 | tf_op jit(solution)/shard_map/ppermute | solution.py:79
  130.4 15.1 %collective-permute-start.29 = (f32[1096,128]{1,0:T(8,128)S(1)}, f32[1096,128]{1,0:T(8,128)S(1)}, u32[]{:S(2)}, u32[]{:S(2)}) collective-permute-start(f32[1096,128]{1,0:T(8,128)S(1)} %add.82.refs_3_.refs_4_), channel_id=1, source_target_pairs={{0,4},{2,6},{4,0},{6,2},{8,12},{10,14},{12,8},{14,10},{16,20},{18,... | collective-permute-start | bytes 1683464 | tf_op jit(solution)/shard_map/ppermute | solution.py:79
  131.0 14.6 %collective-permute-start.22 = (f32[1096,128]{1,0:T(8,128)S(1)}, f32[1096,128]{1,0:T(8,128)S(1)}, u32[]{:S(2)}, u32[]{:S(2)}) collective-permute-start(f32[1096,128]{1,0:T(8,128)S(1)} %add.82.refs_3_.refs_4_), channel_id=1, source_target_pairs={{0,2},{2,0},{4,6},{6,4},{8,10},{10,8},{12,14},{14,12},{16,18},{18,... | collective-permute-start | bytes 1683464 | tf_op jit(solution)/shard_map/ppermute | solution.py:79
  132.5 13.5 %collective-permute-start.31 = (f32[2192,128]{1,0:T(8,128)S(1)}, f32[2192,128]{1,0:T(8,128)S(1)}, u32[]{:S(2)}, u32[]{:S(2)}) collective-permute-start(f32[2192,128]{1,0:T(8,128)S(1)} %pad_maximum_fusion.1.refs_1_), channel_id=1, source_target_pairs={{0,2},{2,0},{4,6},{6,4},{8,10},{10,8},{12,14},{14,12},{16,18},{18,... | collective-permute-start | bytes 3366920 | tf_op jit(solution)/shard_map/ppermute | solution.py:79
  132.5 3.0 %collective-permute-start.27 = (f32[8,128]{1,0:T(8,128)S(1)}, f32[8,128]{1,0:T(8,128)S(1)}, u32[]{:S(2)}, u32[]{:S(2)}) collective-permute-start(f32[8,128]{1,0:T(8,128)S(1)} %add.84), channel_id=1, source_target_pairs={{0,2},{2,0},{4,6},{6,4},{8,10},{10,8},{12,14},{14,12},{16,18},{18,... | collective-permute-start | bytes 12296 | tf_op jit(solution)/shard_map/ppermute | solution.py:79
  135.6 3.6 %collective-permute-start.28 = (f32[8,128]{1,0:T(8,128)S(1)}, f32[8,128]{1,0:T(8,128)S(1)}, u32[]{:S(2)}, u32[]{:S(2)}) collective-permute-start(f32[8,128]{1,0:T(8,128)S(1)} %add.85), channel_id=1, source_target_pairs={{0,1},{1,0},{2,3},{3,2},{4,5},{5,4},{6,7},{7,6},{8,9},{9,8},{10,11... | collective-permute-start | bytes 12296 | tf_op jit(solution)/shard_map/ppermute | solution.py:165
  139.2 6.9 %collective-permute-start.32 = (f32[1096,128]{1,0:T(8,128)S(1)}, f32[1096,128]{1,0:T(8,128)S(1)}, u32[]{:S(2)}, u32[]{:S(2)}) collective-permute-start(f32[1096,128]{1,0:T(8,128)S(1)} %add.83.refs_2_), channel_id=1, source_target_pairs={{0,2},{2,0},{4,6},{6,4},{8,10},{10,8},{12,14},{14,12},{16,18},{18,... | collective-permute-start | bytes 1683464 | tf_op jit(solution)/shard_map/ppermute | solution.py:79
  145.5 2.0 %collective-permute-start.33 = (f32[1096,128]{1,0:T(8,128)S(1)}, f32[1096,128]{1,0:T(8,128)S(1)}, u32[]{:S(2)}, u32[]{:S(2)}) collective-permute-start(f32[1096,128]{1,0:T(8,128)S(1)} %collective-permute-done.26.refs_3_), channel_id=1, source_target_pairs={{0,2},{2,0},{4,6},{6,4},{8,10},{10,8},{12,14},{14,12},{16,18},{18,... | collective-permute-start | bytes 1683464 | tf_op jit(solution)/shard_map/ppermute | solution.py:79
  145.6 2.8 %collective-permute-start.34 = (f32[1096,128]{1,0:T(8,128)S(1)}, f32[1096,128]{1,0:T(8,128)S(1)}, u32[]{:S(2)}, u32[]{:S(2)}) collective-permute-start(f32[1096,128]{1,0:T(8,128)S(1)} %collective-permute-done.29.refs_5_), channel_id=1, source_target_pairs={{0,2},{2,0},{4,6},{6,4},{8,10},{10,8},{12,14},{14,12},{16,18},{18,... | collective-permute-start | bytes 1683464 | tf_op jit(solution)/shard_map/ppermute | solution.py:79

commit v20 on v19

--- a/solution.py
+++ b/solution.py
@@ -512,7 +512,7 @@
         for group in range(0, LANE, 8):
             rows = [held[pl.ds(position_ref[now * lines + line, group + u], 1), :] for u in range(8)]
             here = pl.ds(pl.multiple_of(line * LANE + group, 8), 8)
-            weight = weights_ref[here, :]
+            weight = weights_ref[pl.ds(pl.multiple_of((now * lines + line) * LANE + group, 8), 8), :]
             direction = jnp.concatenate(rows, 0) + decay_rate * weight
             out_ref[here, :] = weight - rate * direction
 
@@ -530,7 +530,7 @@
             jax.ShapeDtypeStruct(norm_state.shape, jnp.float32),
             jax.ShapeDtypeStruct((matrices + 2,), jnp.float32),
         ],
-        in_specs=[smem, smem, vmem, vmem, pl.BlockSpec((tile, LANE), lambda i: (i, 0))]
+        in_specs=[smem, smem, vmem, vmem, vmem]
         + [vmem] * len(pieces),
         out_specs=[pl.BlockSpec((tile, LANE), lambda i: (i, 0)), vmem, smem],
         scratch_shapes=[

time: 168 us -> 168 us (level)
  no operation moved by 1% of the time
where the time goes in v20:
time: 168 us
  waiting for transfers between devices  71.4 us (43%)
  Pallas kernels  50.1 us (30%)
  starting transfers between devices  41.5 us (25%)
  other arithmetic  3.86 us (2%)
    ppermute x34, waiting for transfers between devices, send(): return lax.ppermute(value, 'dp', every)  69.3 us
    ppermute x34, starting transfers between devices, send(): return lax.ppermute(value, 'dp', every)  40 us
    pallas_call x1, Pallas kernels, place(): pl.pallas_call(functools.partial(place_kernel, plan), out_shape=[jax.Shap...  21.4 us
    pallas_call x1, Pallas kernels, finish(): pl.pallas_call(functools.partial(finish_kernel, plan, tile, slots), grid=...  19.6 us
    pallas_call x1, Pallas kernels, owned(): pl.pallas_call(functools.partial(owned_kernel, plan), out_shape=[jax.Shap...  6.44 us
  transfers between devices with their start and end apart: 35, of which 18 were waited for; matrix products, arithmetic and copies ran while one was open for 2% of the time, Pallas kernels for 4%

profile of v20, /device:TPU:0, one launch (start us, length us, event | category | flops | bytes accessed | tf_op | source)
XLA Modules:
  0.0 168.0 jit_solution(17424984156185870531)
XLA Ops:
  0.6 21.4 %place_gradients.1 = (f32[1096,128]{1,0:T(8,128)}, f32[1096,128]{1,0:T(8,128)}, f32[1096,128]{1,0:T(8,128)}, f32[1096,128]{1,0:T(8,128)}, f32[1096,128]{1,0:T(8,...) custom-call(s32[136,128]{1,0:T(8,128)} %bitcast.15, ...), custom_call_target="tpu_custom_call" | custom-call | tf_op jit(solution)/shard_map/place_gradients/pallas_call | solution.py:316
  22.0 0.5 collective-permute-start
  22.6 1.8 %collective-permute-done = f32[1096,128]{1,0:T(8,128)S(1)} collective-permute-done((f32[1096,128]{1,0:T(8,128)}, f32[1096,128]{1,0:T(8,128)S(1)}, u32[]{:S(2)}, u32[]{:S(2)}) %collective-permute-start) | collective-permute-done | bytes 561184 | tf_op jit(solution)/shard_map/ppermute | solution.py:79
  24.4 1.1 add.68
  25.5 0.4 collective-permute-start.8
  25.9 0.1 collective-permute-start.4
  26.1 2.9 %collective-permute-start.5 = (f32[1096,128]{1,0:T(8,128)S(1)}, f32[1096,128]{1,0:T(8,128)S(1)}, u32[]{:S(2)}, u32[]{:S(2)}) collective-permute-start(f32[1096,128]{1,0:T(8,128)S(1)} %add.68), channel_id=1, source_target_pairs={{0,4},{2,6},{4,0},{6,2},{8,12},{10,14},{12,8},{14,10},{16,20},{18,... | collective-permute-start | bytes 1683464 | tf_op jit(solution)/shard_map/ppermute | solution.py:79
  28.9 0.5 collective-permute-start.13
  29.5 1.2 collective-permute-start.9
  30.7 11.7 %collective-permute-done.5 = f32[1096,128]{1,0:T(8,128)S(1)} collective-permute-done((f32[1096,128]{1,0:T(8,128)S(1)}, f32[1096,128]{1,0:T(8,128)S(1)}, u32[]{:S(2)}, u32[]{:S(2)}) %collective-permute-start.5) | collective-permute-done | bytes 561184 | tf_op jit(solution)/shard_map/ppermute | solution.py:79
  42.4 0.1 add_add_fusion.2
  42.5 4.1 %collective-permute-start.6 = (f32[1096,128]{1,0:T(8,128)S(1)}, f32[1096,128]{1,0:T(8,128)S(1)}, u32[]{:S(2)}, u32[]{:S(2)}) collective-permute-start(f32[1096,128]{1,0:T(8,128)S(1)} %add_add_fusion.2), channel_id=1, source_target_pairs={{0,8},{2,10},{4,12},{6,14},{24,16},{26,18},{28,20},{30,22},{1,9},{... | collective-permute-start | bytes 1683464 | tf_op jit(solution)/shard_map/ppermute | solution.py:79
  46.6 0.6 pad_add_fusion.place_ref
  47.2 6.4 %owned_weights.1 = (f32[1088,128]{1,0:T(8,128)}, s32[1152,128]{1,0:T(8,128)}) custom-call(s32[3]{0:T(128)} %pad_add_fusion.place_ref, s32[136,128]{1,0:T(8,128)} %bitcast.16, f32[17408,128]{1,0:T(8,128)} %weights_ref.3), custom_call_target="tpu_custom_call" | custom-call | bytes 20971520 | tf_op jit(solution)/shard_map/owned_weights/pallas_call | solution.py:393
  53.8 0.5 collective-permute-start.12
  54.3 1.1 add.79
  55.4 1.6 collective-permute-start.14
  57.0 0.1 add_add_fusion.1
  57.1 0.1 collective-permute-done.6
  57.2 4.4 %collective-permute-start.11 = (f32[1096,128]{1,0:T(8,128)S(1)}, f32[1096,128]{1,0:T(8,128)S(1)}, u32[]{:S(2)}, u32[]{:S(2)}) collective-permute-start(f32[1096,128]{1,0:T(8,128)S(1)} %add_add_fusion.1), channel_id=1, source_target_pairs={{0,8},{2,10},{4,12},{6,14},{24,16},{26,18},{28,20},{30,22},{1,9},{... | collective-permute-start | bytes 1683464 | tf_op jit(solution)/shard_map/ppermute | solution.py:79
  61.6 0.1 add.76
  61.7 0.8 collective-permute-start.10
  62.7 1.6 collective-permute-start.3
  64.3 6.7 %collective-permute-done.14 = f32[1096,128]{1,0:T(8,128)S(1)} collective-permute-done((f32[1096,128]{1,0:T(8,128)S(1)}, f32[1096,128]{1,0:T(8,128)S(1)}, u32[]{:S(2)}, u32[]{:S(2)}) %collective-permute-start.14) | collective-permute-done | bytes 561184 | tf_op jit(solution)/shard_map/ppermute | solution.py:79
  71.0 0.1 add_add_fusion
  71.1 0.2 collective-permute-done.11
  71.3 0.1 add.77
  71.4 0.1 add.81
  71.5 3.9 %collective-permute-start.15 = (f32[1096,128]{1,0:T(8,128)S(1)}, f32[1096,128]{1,0:T(8,128)S(1)}, u32[]{:S(2)}, u32[]{:S(2)}) collective-permute-start(f32[1096,128]{1,0:T(8,128)S(1)} %add.81), channel_id=1, source_target_pairs={{0,8},{2,10},{4,12},{6,14},{8,0},{10,2},{12,4},{14,6},{16,24},{18,... | collective-permute-start | bytes 1683464 | tf_op jit(solution)/shard_map/ppermute | solution.py:79
  75.5 0.7 collective-permute-start.16
  76.2 0.1 add.69.refs_0_
  76.3 5.9 %collective-permute-done.3.refs_1_ = f32[1096,128]{1,0:T(8,128)S(1)} collective-permute-done((f32[1096,128]{1,0:T(8,128)S(1)}, f32[1096,128]{1,0:T(8,128)S(1)}, u32[]{:S(2)}, u32[]{:S(2)}) %collective-permute-start.3) | collective-permute-done | bytes 561184 | tf_op jit(solution)/shard_map/ppermute | solution.py:79
  82.2 2.8 %collective-permute-done.15.refs_2_ = f32[1096,128]{1,0:T(8,128)S(1)} collective-permute-done((f32[1096,128]{1,0:T(8,128)S(1)}, f32[1096,128]{1,0:T(8,128)S(1)}, u32[]{:S(2)}, u32[]{:S(2)}) %collective-permute-start.15) | collective-permute-done | bytes 561184 | tf_op jit(solution)/shard_map/ppermute | solution.py:79
  85.1 2.0 %moments.1 = (f32[1088,128]{1,0:T(8,128)}, f32[1088,128]{1,0:T(8,128)}, f32[1096,128]{1,0:T(8,128)S(1)}) custom-call(f32[1096,128]{1,0:T(8,128)S(1)} %add.69.refs_0_, f32[1096,128]{1,0:T(8,128)S(1)} %collective-permute-done.3.refs_1_, f32[1096,128]{1,0:T(8,128)S(1)} %collective-permute-done.15.refs_2_, f32[1096,128]{1,0:T(8,128)S(1)} %collective-permute-done.16.refs_3_, ...), custom_call_target="tpu_custom_call" | custom-call | tf_op jit(solution)/shard_map/moments/pallas_call | solution.py:447
  87.1 3.8 %collective-permute-start.18 = (f32[1096,128]{1,0:T(8,128)S(1)}, f32[1096,128]{1,0:T(8,128)S(1)}, u32[]{:S(2)}, u32[]{:S(2)}) collective-permute-start(f32[1096,128]{1,0:T(8,128)S(1)} %get-tuple-element.92), channel_id=1, source_target_pairs={{0,8},{2,10},{4,12},{6,14},{8,0},{10,2},{12,4},{14,6},{16,24},{18,... | collective-permute-start | bytes 1683464 | tf_op jit(solution)/shard_map/ppermute | solution.py:79
  90.9 1.5 collective-permute-start.19
  92.4 0.7 collective-permute-start.17
  93.1 6.4 %collective-permute-done.18 = f32[1096,128]{1,0:T(8,128)S(1)} collective-permute-done((f32[1096,128]{1,0:T(8,128)S(1)}, f32[1096,128]{1,0:T(8,128)S(1)}, u32[]{:S(2)}, u32[]{:S(2)}) %collective-permute-start.18) | collective-permute-done | bytes 561184 | tf_op jit(solution)/shard_map/ppermute | solution.py:79
  99.6 1.5 collective-permute-start.24
  101.0 0.7 collective-permute-start.20
  101.7 0.1 pad_maximum_fusion.refs_0_.refs_1_
  101.8 2.9 %collective-permute-done.19 = f32[1096,128]{1,0:T(8,128)S(1)} collective-permute-done((f32[1096,128]{1,0:T(8,128)S(1)}, f32[1096,128]{1,0:T(8,128)S(1)}, u32[]{:S(2)}, u32[]{:S(2)}) %collective-permute-start.19) | collective-permute-done | bytes 561184 | tf_op jit(solution)/shard_map/ppermute | solution.py:79
  104.7 1.3 collective-permute-start.23
  106.0 1.3 collective-permute-start.21
  107.3 6.4 %collective-permute-done.24 = f32[1096,128]{1,0:T(8,128)S(1)} collective-permute-done((f32[1096,128]{1,0:T(8,128)S(1)}, f32[1096,128]{1,0:T(8,128)S(1)}, u32[]{:S(2)}, u32[]{:S(2)}) %collective-permute-start.24) | collective-permute-done | bytes 561184 | tf_op jit(solution)/shard_map/ppermute | solution.py:79
  113.7 3.7 %collective-permute-done.23 = f32[1096,128]{1,0:T(8,128)S(1)} collective-permute-done((f32[1096,128]{1,0:T(8,128)S(1)}, f32[1096,128]{1,0:T(8,128)S(1)}, u32[]{:S(2)}, u32[]{:S(2)}) %collective-permute-start.23) | collective-permute-done | bytes 561184 | tf_op jit(solution)/shard_map/ppermute | solution.py:79
  117.4 0.1 add.83.refs_2_
  117.5 0.1 pad_maximum_fusion.1.refs_1_
  117.6 2.5 %collective-permute-start.26 = (f32[1096,128]{1,0:T(8,128)S(1)}, f32[1096,128]{1,0:T(8,128)S(1)}, u32[]{:S(2)}, u32[]{:S(2)}) collective-permute-start(f32[1096,128]{1,0:T(8,128)S(1)} %add.83.refs_2_), channel_id=1, source_target_pairs={{0,4},{2,6},{4,0},{6,2},{8,12},{10,14},{12,8},{14,10},{16,20},{18,... | collective-permute-start | bytes 1683464 | tf_op jit(solution)/shard_map/ppermute | solution.py:79
  120.1 8.1 %collective-permute-done.21 = f32[1096,128]{1,0:T(8,128)S(1)} collective-permute-done((f32[1096,128]{1,0:T(8,128)S(1)}, f32[1096,128]{1,0:T(8,128)S(1)}, u32[]{:S(2)}, u32[]{:S(2)}) %collective-permute-start.21) | collective-permute-done | bytes 561184 | tf_op jit(solution)/shard_map/ppermute | solution.py:79
  128.3 0.6 sums.1
  128.9 1.6 collective-permute-start.25
  130.4 0.5 collective-permute-start.29
  131.0 0.2 collective-permute-start.22
  131.2 1.3 collective-permute-done.25
  132.5 0.5 collective-permute-start.27
  133.1 2.5 %collective-permute-done.27 = f32[8,128]{1,0:T(8,128)S(1)} collective-permute-done((f32[8,128]{1,0:T(8,128)S(1)}, f32[8,128]{1,0:T(8,128)S(1)}, u32[]{:S(2)}, u32[]{:S(2)}) %collective-permute-start.27) | collective-permute-done | bytes 4128 | tf_op jit(solution)/shard_map/ppermute | solution.py:79
  135.6 1.5 collective-permute-start.28
  137.1 2.1 %collective-permute-done.28 = f32[8,128]{1,0:T(8,128)S(1)} collective-permute-done((f32[8,128]{1,0:T(8,128)S(1)}, f32[8,128]{1,0:T(8,128)S(1)}, u32[]{:S(2)}, u32[]{:S(2)}) %collective-permute-start.28) | collective-permute-done | bytes 4128 | tf_op jit(solution)/shard_map/ppermute | solution.py:165
  139.2 6.3 %collective-permute-done.29.refs_5_ = f32[1096,128]{1,0:T(8,128)S(1)} collective-permute-done((f32[1096,128]{1,0:T(8,128)S(1)}, f32[1096,128]{1,0:T(8,128)S(1)}, u32[]{:S(2)}, u32[]{:S(2)}) %collective-permute-start.29) | collective-permute-done | bytes 561184 | tf_op jit(solution)/shard_map/ppermute | solution.py:79
  145.6 0.5 collective-permute-start.34
  146.1 1.4 collective-permute-done.33.refs_9_
  147.5 0.8 collective-permute-done.34.refs_11_
  148.3 19.6 %new_weights.1 = (f32[17408,128]{1,0:T(8,128)}, f32[3,2,1024]{2,1,0:T(2,128)}, f32[7]{0:T(128)}) custom-call(s32[3]{0:T(128)S(1)} %copy-done.6, s32[136,128]{1,0:T(8,128)S(1)} %copy-done.4, f32[8,128]{1,0:T(8,128)S(1)} %add.86.total_ref, f32[3,2,1024]{2,1,0:T(2,128)S(1)} %copy-done.5, f32[17408,128]{1,0:T(8,128)S(1)} %bitcast.11, ...), custom_call_target="tpu_custom_call" | custom-call | tf_op jit(solution)/shard_map/new_weights/pallas_call | solution.py:525
  (71 shorter events, 0.5 us)
Async XLA Ops:
  22.0 7.4 %copy-start.13 = (f32[1096,128]{1,0:T(8,128)S(1)}, f32[1096,128]{1,0:T(8,128)}, u32[]{:S(2)}) copy-start(f32[1096,128]{1,0:T(8,128)} %get-tuple-element.77) | copy-start | bytes 1683460
  22.0 2.3 %collective-permute-start = (f32[1096,128]{1,0:T(8,128)}, f32[1096,128]{1,0:T(8,128)S(1)}, u32[]{:S(2)}, u32[]{:S(2)}) collective-permute-start(f32[1096,128]{1,0:T(8,128)} %get-tuple-element.61), channel_id=1, source_target_pairs={{0,2},{2,0},{4,6},{6,4},{8,10},{10,8},{12,14},{14,12},{16,18},{18,... | collective-permute-start | bytes 1683464 | tf_op jit(solution)/shard_map/ppermute | solution.py:79
  25.5 16.9 %copy-start.12 = (f32[1096,128]{1,0:T(8,128)S(1)}, f32[1096,128]{1,0:T(8,128)}, u32[]{:S(2)}) copy-start(f32[1096,128]{1,0:T(8,128)} %get-tuple-element.72) | copy-start | bytes 1683460
  25.5 4.0 %collective-permute-start.8 = (f32[1096,128]{1,0:T(8,128)}, f32[1096,128]{1,0:T(8,128)S(1)}, u32[]{:S(2)}, u32[]{:S(2)}) collective-permute-start(f32[1096,128]{1,0:T(8,128)} %get-tuple-element.78), channel_id=1, source_target_pairs={{0,2},{2,0},{4,6},{6,4},{8,10},{10,8},{12,14},{14,12},{16,18},{18,... | collective-permute-start | bytes 1683464 | tf_op jit(solution)/shard_map/ppermute | solution.py:79
  25.9 4.8 %collective-permute-start.4 = (f32[1096,128]{1,0:T(8,128)}, f32[1096,128]{1,0:T(8,128)S(1)}, u32[]{:S(2)}, u32[]{:S(2)}) collective-permute-start(f32[1096,128]{1,0:T(8,128)} %get-tuple-element.73), channel_id=1, source_target_pairs={{0,2},{2,0},{4,6},{6,4},{8,10},{10,8},{12,14},{14,12},{16,18},{18,... | collective-permute-start | bytes 1683464 | tf_op jit(solution)/shard_map/ppermute | solution.py:79
  26.1 16.4 %collective-permute-start.5 = (f32[1096,128]{1,0:T(8,128)S(1)}, f32[1096,128]{1,0:T(8,128)S(1)}, u32[]{:S(2)}, u32[]{:S(2)}) collective-permute-start(f32[1096,128]{1,0:T(8,128)S(1)} %add.68), channel_id=1, source_target_pairs={{0,4},{2,6},{4,0},{6,2},{8,12},{10,14},{12,8},{14,10},{16,20},{18,... | collective-permute-start | bytes 1683464 | tf_op jit(solution)/shard_map/ppermute | solution.py:79
  28.9 26.5 %collective-permute-start.7 = (f32[1096,128]{1,0:T(8,128)}, f32[1096,128]{1,0:T(8,128)S(1)}, u32[]{:S(2)}, u32[]{:S(2)}) collective-permute-start(f32[1096,128]{1,0:T(8,128)} %get-tuple-element.76), channel_id=1, source_target_pairs={{0,2},{2,0},{4,6},{6,4},{8,10},{10,8},{12,14},{14,12},{16,18},{18,... | collective-permute-start | bytes 1683464 | tf_op jit(solution)/shard_map/ppermute | solution.py:79
  28.9 24.8 %collective-permute-start.13 = (f32[1096,128]{1,0:T(8,128)}, f32[1096,128]{1,0:T(8,128)}, u32[]{:S(2)}, u32[]{:S(2)}) collective-permute-start(f32[1096,128]{1,0:T(8,128)} %get-tuple-element.86), channel_id=1, source_target_pairs={{0,2},{2,0},{4,6},{6,4},{8,10},{10,8},{12,14},{14,12},{16,18},{18,... | collective-permute-start | bytes 1683464 | tf_op jit(solution)/shard_map/ppermute | solution.py:79
  29.5 27.4 %collective-permute-start.9 = (f32[1096,128]{1,0:T(8,128)S(1)}, f32[1096,128]{1,0:T(8,128)S(1)}, u32[]{:S(2)}, u32[]{:S(2)}) collective-permute-start(f32[1096,128]{1,0:T(8,128)S(1)} %add.74), channel_id=1, source_target_pairs={{0,4},{2,6},{4,0},{6,2},{8,12},{10,14},{12,8},{14,10},{16,20},{18,... | collective-permute-start | bytes 1683464 | tf_op jit(solution)/shard_map/ppermute | solution.py:79
  42.5 14.7 %collective-permute-start.6 = (f32[1096,128]{1,0:T(8,128)S(1)}, f32[1096,128]{1,0:T(8,128)S(1)}, u32[]{:S(2)}, u32[]{:S(2)}) collective-permute-start(f32[1096,128]{1,0:T(8,128)S(1)} %add_add_fusion.2), channel_id=1, source_target_pairs={{0,8},{2,10},{4,12},{6,14},{24,16},{26,18},{28,20},{30,22},{1,9},{... | collective-permute-start | bytes 1683464 | tf_op jit(solution)/shard_map/ppermute | solution.py:79
  47.2 6.5 %copy-start.16 = (f32[1096,128]{1,0:T(8,128)S(1)}, f32[1096,128]{1,0:T(8,128)}, u32[]{:S(2)}) copy-start(f32[1096,128]{1,0:T(8,128)} %get-tuple-element.71) | copy-start | bytes 1683460
  47.2 6.6 %copy-start.15 = (f32[1096,128]{1,0:T(8,128)S(1)}, f32[1096,128]{1,0:T(8,128)}, u32[]{:S(2)}) copy-start(f32[1096,128]{1,0:T(8,128)} %get-tuple-element.84) | copy-start | bytes 1683460
  47.2 7.1 %copy-start.11 = (f32[1096,128]{1,0:T(8,128)S(1)}, f32[1096,128]{1,0:T(8,128)}, u32[]{:S(2)}) copy-start(f32[1096,128]{1,0:T(8,128)} %get-tuple-element.85) | copy-start | bytes 1683460
  53.7 3.3 %copy-start.10 = (f32[1096,128]{1,0:T(8,128)S(1)}, f32[1096,128]{1,0:T(8,128)}, u32[]{:S(2)}) copy-start(f32[1096,128]{1,0:T(8,128)} %get-tuple-element.75) | copy-start | bytes 1683460
  53.7 8.9 %collective-permute-start.2 = (f32[1096,128]{1,0:T(8,128)S(1)}, f32[1096,128]{1,0:T(8,128)S(1)}, u32[]{:S(2)}, u32[]{:S(2)}) collective-permute-start(f32[1096,128]{1,0:T(8,128)S(1)} %copy-done.16), channel_id=1, source_target_pairs={{0,2},{2,0},{4,6},{6,4},{8,10},{10,8},{12,14},{14,12},{16,18},{18,... | collective-permute-start | bytes 1683464 | tf_op jit(solution)/shard_map/ppermute | solution.py:79
  53.8 8.9 %collective-permute-start.12 = (f32[1096,128]{1,0:T(8,128)S(1)}, f32[1096,128]{1,0:T(8,128)S(1)}, u32[]{:S(2)}, u32[]{:S(2)}) collective-permute-start(f32[1096,128]{1,0:T(8,128)S(1)} %copy-done.15), channel_id=1, source_target_pairs={{0,2},{2,0},{4,6},{6,4},{8,10},{10,8},{12,14},{14,12},{16,18},{18,... | collective-permute-start | bytes 1683464 | tf_op jit(solution)/shard_map/ppermute | solution.py:79
  55.4 15.6 %collective-permute-start.14 = (f32[1096,128]{1,0:T(8,128)S(1)}, f32[1096,128]{1,0:T(8,128)S(1)}, u32[]{:S(2)}, u32[]{:S(2)}) collective-permute-start(f32[1096,128]{1,0:T(8,128)S(1)} %add.79), channel_id=1, source_target_pairs={{0,4},{2,6},{4,0},{6,2},{8,12},{10,14},{12,8},{14,10},{16,20},{18,... | collective-permute-start | bytes 1683464 | tf_op jit(solution)/shard_map/ppermute | solution.py:79
  57.1 5.5 %copy-start.14 = (f32[1096,128]{1,0:T(8,128)S(1)}, f32[1096,128]{1,0:T(8,128)}, u32[]{:S(2)}) copy-start(f32[1096,128]{1,0:T(8,128)} %get-tuple-element.69) | copy-start | bytes 1683460
  57.1 5.6 %copy-start.9 = (f32[1096,128]{1,0:T(8,128)S(1)}, f32[1096,128]{1,0:T(8,128)}, u32[]{:S(2)}) copy-start(f32[1096,128]{1,0:T(8,128)} %get-tuple-element.70) | copy-start | bytes 1683460
  57.2 14.1 %collective-permute-start.11 = (f32[1096,128]{1,0:T(8,128)S(1)}, f32[1096,128]{1,0:T(8,128)S(1)}, u32[]{:S(2)}, u32[]{:S(2)}) collective-permute-start(f32[1096,128]{1,0:T(8,128)S(1)} %add_add_fusion.1), channel_id=1, source_target_pairs={{0,8},{2,10},{4,12},{6,14},{24,16},{26,18},{28,20},{30,22},{1,9},{... | collective-permute-start | bytes 1683464 | tf_op jit(solution)/shard_map/ppermute | solution.py:79
  61.7 9.3 %copy-start.8 = (f32[1096,128]{1,0:T(8,128)S(1)}, f32[1096,128]{1,0:T(8,128)}, u32[]{:S(2)}) copy-start(f32[1096,128]{1,0:T(8,128)} %get-tuple-element.83) | copy-start | bytes 1683460
  61.7 9.7 %collective-permute-start.10 = (f32[1096,128]{1,0:T(8,128)S(1)}, f32[1096,128]{1,0:T(8,128)S(1)}, u32[]{:S(2)}, u32[]{:S(2)}) collective-permute-start(f32[1096,128]{1,0:T(8,128)S(1)} %add.76), channel_id=1, source_target_pairs={{8,16},{10,18},{12,20},{14,22},{16,8},{18,10},{20,12},{22,14},{9,1... | collective-permute-start | bytes 1683464 | tf_op jit(solution)/shard_map/ppermute | solution.py:79
  62.6 13.6 %collective-permute-start.1 = (f32[1096,128]{1,0:T(8,128)S(1)}, f32[1096,128]{1,0:T(8,128)S(1)}, u32[]{:S(2)}, u32[]{:S(2)}) collective-permute-start(f32[1096,128]{1,0:T(8,128)S(1)} %copy-done.14), channel_id=1, source_target_pairs={{0,2},{2,0},{4,6},{6,4},{8,10},{10,8},{12,14},{14,12},{16,18},{18,... | collective-permute-start | bytes 1683464 | tf_op jit(solution)/shard_map/ppermute | solution.py:79
  62.7 19.5 %collective-permute-start.3 = (f32[1096,128]{1,0:T(8,128)S(1)}, f32[1096,128]{1,0:T(8,128)S(1)}, u32[]{:S(2)}, u32[]{:S(2)}) collective-permute-start(f32[1096,128]{1,0:T(8,128)S(1)} %add.70), channel_id=1, source_target_pairs={{0,4},{2,6},{4,0},{6,2},{8,12},{10,14},{12,8},{14,10},{16,20},{18,... | collective-permute-start | bytes 1683464 | tf_op jit(solution)/shard_map/ppermute | solution.py:79
  71.0 77.3 %slice-start = ((s8[8912896]{0:T(1024)(128)(4,1)}), s8[4194304]{0:T(1024)(128)(4,1)S(1)}, s32[]{:S(2)}) async-start(s8[8912896]{0:T(1024)(128)(4,1)} %bitcast.10), calls=%async_computation | async-start | bytes 8388608
  71.4 4.8 %copy-start.7 = (f32[1096,128]{1,0:T(8,128)S(1)}, f32[1096,128]{1,0:T(8,128)}, u32[]{:S(2)}) copy-start(f32[1096,128]{1,0:T(8,128)} %get-tuple-element.59) | copy-start | bytes 1683460
  71.4 13.6 %copy-start.2 = (f32[1,1088,128]{2,1,0:T(8,128)S(1)}, f32[1,1088,128]{2,1,0:T(8,128)}, u32[]{:S(2)}) copy-start(f32[1,1088,128]{2,1,0:T(8,128)} %param.10) | copy-start | bytes 1671172
  71.4 13.6 %copy-start.3 = (f32[1088,128]{1,0:T(8,128)S(1)}, f32[1088,128]{1,0:T(8,128)}, u32[]{:S(2)}) copy-start(f32[1088,128]{1,0:T(8,128)} %get-tuple-element.90.refs_6_) | copy-start | bytes 1671172
  71.5 13.5 %copy-start = (s32[1152,128]{1,0:T(8,128)S(1)}, s32[1152,128]{1,0:T(8,128)}, u32[]{:S(2)}) copy-start(s32[1152,128]{1,0:T(8,128)} %get-tuple-element.91.refs_7_) | copy-start | bytes 1769476
  71.5 13.5 %copy-start.1 = (f32[1,1088,128]{2,1,0:T(8,128)S(1)}, f32[1,1088,128]{2,1,0:T(8,128)}, u32[]{:S(2)}) copy-start(f32[1,1088,128]{2,1,0:T(8,128)} %param.9) | copy-start | bytes 1671172
  71.5 13.5 %collective-permute-start.15 = (f32[1096,128]{1,0:T(8,128)S(1)}, f32[1096,128]{1,0:T(8,128)S(1)}, u32[]{:S(2)}, u32[]{:S(2)}) collective-permute-start(f32[1096,128]{1,0:T(8,128)S(1)} %add.81), channel_id=1, source_target_pairs={{0,8},{2,10},{4,12},{6,14},{8,0},{10,2},{12,4},{14,6},{16,24},{18,... | collective-permute-start | bytes 1683464 | tf_op jit(solution)/shard_map/ppermute | solution.py:79
  75.5 9.5 %collective-permute-start.16 = (f32[1096,128]{1,0:T(8,128)S(1)}, f32[1096,128]{1,0:T(8,128)S(1)}, u32[]{:S(2)}, u32[]{:S(2)}) collective-permute-start(f32[1096,128]{1,0:T(8,128)S(1)} %add.77), channel_id=1, source_target_pairs={{8,16},{10,18},{12,20},{14,22},{16,8},{18,10},{20,12},{22,14},{9,1... | collective-permute-start | bytes 1683464 | tf_op jit(solution)/shard_map/ppermute | solution.py:79
  85.0 63.3 %slice-start.1 = ((s8[8912896]{0:T(1024)(128)(4,1)}), s8[4194304]{0:T(1024)(128)(4,1)S(1)}, s32[]{:S(2)}) async-start(s8[8912896]{0:T(1024)(128)(4,1)} %bitcast.10), calls=%async_computation.1 | async-start | bytes 8388608
  87.1 12.5 %collective-permute-start.18 = (f32[1096,128]{1,0:T(8,128)S(1)}, f32[1096,128]{1,0:T(8,128)S(1)}, u32[]{:S(2)}, u32[]{:S(2)}) collective-permute-start(f32[1096,128]{1,0:T(8,128)S(1)} %get-tuple-element.92), channel_id=1, source_target_pairs={{0,8},{2,10},{4,12},{6,14},{8,0},{10,2},{12,4},{14,6},{16,24},{18,... | collective-permute-start | bytes 1683464 | tf_op jit(solution)/shard_map/ppermute | solution.py:79
  90.9 13.8 %collective-permute-start.19 = (f32[1096,128]{1,0:T(8,128)S(1)}, f32[1096,128]{1,0:T(8,128)S(1)}, u32[]{:S(2)}, u32[]{:S(2)}) collective-permute-start(f32[1096,128]{1,0:T(8,128)S(1)} %get-tuple-element.92), channel_id=1, source_target_pairs={{0,4},{2,6},{4,0},{6,2},{8,12},{10,14},{12,8},{14,10},{16,20},{18,... | collective-permute-start | bytes 1683464 | tf_op jit(solution)/shard_map/ppermute | solution.py:79
  92.4 12.3 %collective-permute-start.17 = (f32[1096,128]{1,0:T(8,128)S(1)}, f32[1096,128]{1,0:T(8,128)S(1)}, u32[]{:S(2)}, u32[]{:S(2)}) collective-permute-start(f32[1096,128]{1,0:T(8,128)S(1)} %get-tuple-element.92), channel_id=1, source_target_pairs={{8,16},{10,18},{12,20},{14,22},{16,8},{18,10},{20,12},{22,14},{9,1... | collective-permute-start | bytes 1683464 | tf_op jit(solution)/shard_map/ppermute | solution.py:79
  99.6 14.2 %collective-permute-start.24 = (f32[1096,128]{1,0:T(8,128)S(1)}, f32[1096,128]{1,0:T(8,128)S(1)}, u32[]{:S(2)}, u32[]{:S(2)}) collective-permute-start(f32[1096,128]{1,0:T(8,128)S(1)} %collective-permute-done.18), channel_id=1, source_target_pairs={{0,4},{2,6},{4,0},{6,2},{8,12},{10,14},{12,8},{14,10},{16,20},{18,... | collective-permute-start | bytes 1683464 | tf_op jit(solution)/shard_map/ppermute | solution.py:79
  101.0 5.0 %collective-permute-start.20 = (f32[1096,128]{1,0:T(8,128)S(1)}, f32[1096,128]{1,0:T(8,128)S(1)}, u32[]{:S(2)}, u32[]{:S(2)}) collective-permute-start(f32[1096,128]{1,0:T(8,128)S(1)} %collective-permute-done.18), channel_id=1, source_target_pairs={{8,16},{10,18},{12,20},{14,22},{16,8},{18,10},{20,12},{22,14},{9,1... | collective-permute-start | bytes 1683464 | tf_op jit(solution)/shard_map/ppermute | solution.py:79
  101.8 46.5 %slice-start.2 = ((s8[8912896]{0:T(1024)(128)(4,1)}), s8[524288]{0:T(1024)(128)(4,1)S(1)}, s32[]{:S(2)}) async-start(s8[8912896]{0:T(1024)(128)(4,1)} %bitcast.10), calls=%async_computation.2 | async-start | bytes 1048576
  104.7 12.7 %collective-permute-start.23 = (f32[1096,128]{1,0:T(8,128)S(1)}, f32[1096,128]{1,0:T(8,128)S(1)}, u32[]{:S(2)}, u32[]{:S(2)}) collective-permute-start(f32[1096,128]{1,0:T(8,128)S(1)} %collective-permute-done.17), channel_id=1, source_target_pairs={{8,0},{10,2},{12,4},{14,6},{16,24},{18,26},{20,28},{22,30},{9,1},{... | collective-permute-start | bytes 1683464 | tf_op jit(solution)/shard_map/ppermute | solution.py:79
  106.0 22.2 %collective-permute-start.21 = (f32[1096,128]{1,0:T(8,128)S(1)}, f32[1096,128]{1,0:T(8,128)S(1)}, u32[]{:S(2)}, u32[]{:S(2)}) collective-permute-start(f32[1096,128]{1,0:T(8,128)S(1)} %collective-permute-done.20), channel_id=1, source_target_pairs={{8,0},{10,2},{12,4},{14,6},{16,24},{18,26},{20,28},{22,30},{9,1},{... | collective-permute-start | bytes 1683464 | tf_op jit(solution)/shard_map/ppermute | solution.py:79
  117.6 10.7 %copy-start.6 = (s32[3]{0:T(128)S(1)}, s32[3]{0:T(128)}, u32[]{:S(2)}) copy-start(s32[3]{0:T(128)} %pad_add_fusion.place_ref) | copy-start | bytes 40
  117.6 15.0 %collective-permute-start.26 = (f32[1096,128]{1,0:T(8,128)S(1)}, f32[1096,128]{1,0:T(8,128)S(1)}, u32[]{:S(2)}, u32[]{:S(2)}) collective-permute-start(f32[1096,128]{1,0:T(8,128)S(1)} %add.83.refs_2_), channel_id=1, source_target_pairs={{0,4},{2,6},{4,0},{6,2},{8,12},{10,14},{12,8},{14,10},{16,20},{18,... | collective-permute-start | bytes 1683464 | tf_op jit(solution)/shard_map/ppermute | solution.py:79
  128.3 20.0 %copy-start.4 = (s32[136,128]{1,0:T(8,128)S(1)}, s32[136,128]{1,0:T(8,128)}, u32[]{:S(2)}) copy-start(s32[136,128]{1,0:T(8,128)} %get-tuple-element.58.position_ref) | copy-start | bytes 208900
  128.3 20.0 %copy-start.5 = (f32[3,2,1024]{2,1,0:T(2,128)S(1)}, f32[3,2,1024]{2,1,0:T(2,128)}, u32[]{:S(2)}) copy-start(f32[3,2,1024]{2,1,0:T(2,128)} %norm_ref.1) | copy-start | bytes 73732
  128.9 3.7 %collective-permute-start.25 = (f32[8,128]{1,0:T(8,128)S(1)}, f32[8,128]{1,0:T(8,128)S(1)}, u32[]{:S(2)}, u32[]{:S(2)}) collective-permute-start(f32[8,128]{1,0:T(8,128)S(1)} %sums.1), channel_id=1, source_target_pairs={{0,4},{2,6},{4,0},{6,2},{8,12},{10,14},{12,8},{14,10},{16,20},{18,... | collective-permute-start | bytes 12296 | tf_op jit(solution)/shard_map/ppermute | solution.py:79
  130.4 15.6 %collective-permute-start.30 = (f32[2192,128]{1,0:T(8,128)S(1)}, f32[2192,128]{1,0:T(8,128)S(1)}, u32[]{:S(2)}, u32[]{:S(2)}) collective-permute-start(f32[2192,128]{1,0:T(8,128)S(1)} %pad_maximum_fusion.refs_0_.refs_1_), channel_id=1, source_target_pairs={{0,2},{2,0},{4,6},{6,4},{8,10},{10,8},{12,14},{14,12},{16,18},{18,... | collective-permute-start | bytes 3366920 | tf_op jit(solution)/shard_map/ppermute | solution.py:79
  130.4 15.1 %collective-permute-start.29 = (f32[1096,128]{1,0:T(8,128)S(1)}, f32[1096,128]{1,0:T(8,128)S(1)}, u32[]{:S(2)}, u32[]{:S(2)}) collective-permute-start(f32[1096,128]{1,0:T(8,128)S(1)} %add.82.refs_3_.refs_4_), channel_id=1, source_target_pairs={{0,4},{2,6},{4,0},{6,2},{8,12},{10,14},{12,8},{14,10},{16,20},{18,... | collective-permute-start | bytes 1683464 | tf_op jit(solution)/shard_map/ppermute | solution.py:79
  131.0 14.6 %collective-permute-start.22 = (f32[1096,128]{1,0:T(8,128)S(1)}, f32[1096,128]{1,0:T(8,128)S(1)}, u32[]{:S(2)}, u32[]{:S(2)}) collective-permute-start(f32[1096,128]{1,0:T(8,128)S(1)} %add.82.refs_3_.refs_4_), channel_id=1, source_target_pairs={{0,2},{2,0},{4,6},{6,4},{8,10},{10,8},{12,14},{14,12},{16,18},{18,... | collective-permute-start | bytes 1683464 | tf_op jit(solution)/shard_map/ppermute | solution.py:79
  132.5 13.5 %collective-permute-start.31 = (f32[2192,128]{1,0:T(8,128)S(1)}, f32[2192,128]{1,0:T(8,128)S(1)}, u32[]{:S(2)}, u32[]{:S(2)}) collective-permute-start(f32[2192,128]{1,0:T(8,128)S(1)} %pad_maximum_fusion.1.refs_1_), channel_id=1, source_target_pairs={{0,2},{2,0},{4,6},{6,4},{8,10},{10,8},{12,14},{14,12},{16,18},{18,... | collective-permute-start | bytes 3366920 | tf_op jit(solution)/shard_map/ppermute | solution.py:79
  132.5 3.0 %collective-permute-start.27 = (f32[8,128]{1,0:T(8,128)S(1)}, f32[8,128]{1,0:T(8,128)S(1)}, u32[]{:S(2)}, u32[]{:S(2)}) collective-permute-start(f32[8,128]{1,0:T(8,128)S(1)} %add.84), channel_id=1, source_target_pairs={{0,2},{2,0},{4,6},{6,4},{8,10},{10,8},{12,14},{14,12},{16,18},{18,... | collective-permute-start | bytes 12296 | tf_op jit(solution)/shard_map/ppermute | solution.py:79
  135.6 3.6 %collective-permute-start.28 = (f32[8,128]{1,0:T(8,128)S(1)}, f32[8,128]{1,0:T(8,128)S(1)}, u32[]{:S(2)}, u32[]{:S(2)}) collective-permute-start(f32[8,128]{1,0:T(8,128)S(1)} %add.85), channel_id=1, source_target_pairs={{0,1},{1,0},{2,3},{3,2},{4,5},{5,4},{6,7},{7,6},{8,9},{9,8},{10,11... | collective-permute-start | bytes 12296 | tf_op jit(solution)/shard_map/ppermute | solution.py:165
  139.2 6.9 %collective-permute-start.32 = (f32[1096,128]{1,0:T(8,128)S(1)}, f32[1096,128]{1,0:T(8,128)S(1)}, u32[]{:S(2)}, u32[]{:S(2)}) collective-permute-start(f32[1096,128]{1,0:T(8,128)S(1)} %add.83.refs_2_), channel_id=1, source_target_pairs={{0,2},{2,0},{4,6},{6,4},{8,10},{10,8},{12,14},{14,12},{16,18},{18,... | collective-permute-start | bytes 1683464 | tf_op jit(solution)/shard_map/ppermute | solution.py:79
  145.5 2.0 %collective-permute-start.33 = (f32[1096,128]{1,0:T(8,128)S(1)}, f32[1096,128]{1,0:T(8,128)S(1)}, u32[]{:S(2)}, u32[]{:S(2)}) collective-permute-start(f32[1096,128]{1,0:T(8,128)S(1)} %collective-permute-done.26.refs_3_), channel_id=1, source_target_pairs={{0,2},{2,0},{4,6},{6,4},{8,10},{10,8},{12,14},{14,12},{16,18},{18,... | collective-permute-start | bytes 1683464 | tf_op jit(solution)/shard_map/ppermute | solution.py:79
  145.6 2.8 %collective-permute-start.34 = (f32[1096,128]{1,0:T(8,128)S(1)}, f32[1096,128]{1,0:T(8,128)S(1)}, u32[]{:S(2)}, u32[]{:S(2)}) collective-permute-start(f32[1096,128]{1,0:T(8,128)S(1)} %collective-permute-done.29.refs_5_), channel_id=1, source_target_pairs={{0,2},{2,0},{4,6},{6,4},{8,10},{10,8},{12,14},{14,12},{16,18},{18,... | collective-permute-start | bytes 1683464 | tf_op jit(solution)/shard_map/ppermute | solution.py:79

commit v21 on v20

--- a/solution.py
+++ b/solution.py
@@ -197,7 +197,7 @@
         early, total, *line_three = together(early, all_cores(plan, total), *line_three)
         ready = {(3, 0): early}
         mine = [(value, [(0, x), (1, x)]) for x, value in enumerate([own] + far)]
-        mine += [(value, [(2, x)]) for x, value in enumerate(line_two)]
+        mine.append((jnp.concatenate(line_two), [(2, x) for x in range(plan.nx)]))
         mine += [(value, [(3, x)]) for x, value in enumerate(line_three)]
     swapped = [ready[slots[0]] if slots[0] in ready else plan.swap(value) for value, slots in mine]
     found = [(value, [slot + (0,) for slot in slots]) for value, slots in mine]

time: 168 us -> 168 us (level)
    ppermute x34 -> x33, waiting for transfers between devices: 69.3 us -> 68.5 us  [send(): return lax.ppermute(value, 'dp', every)]
    ppermute x34 -> x33, starting transfers between devices: 40 us -> 39.8 us  [send(): return lax.ppermute(value, 'dp', every)]
  transfers between devices with their start and end apart: 35 -> 34, of which waited for: 18 -> 17; matrix products, arithmetic and copies ran while one was open for 2% -> 2% of each run, Pallas kernels for 4% -> 4%
where the time goes in v21:
time: 168 us; the launch traced here: 167 us
  waiting for transfers between devices  70.6 us (42%)
  Pallas kernels  50 us (30%)
  starting transfers between devices  41.3 us (25%)
  other arithmetic  3.91 us (2%)
    ppermute x33, waiting for transfers between devices, send(): return lax.ppermute(value, 'dp', every)  68.5 us
    ppermute x33, starting transfers between devices, send(): return lax.ppermute(value, 'dp', every)  39.8 us
    pallas_call x1, Pallas kernels, place(): pl.pallas_call(functools.partial(place_kernel, plan), out_shape=[jax.Shap...  21.4 us
    pallas_call x1, Pallas kernels, finish(): pl.pallas_call(functools.partial(finish_kernel, plan, tile, slots), grid=...  19.6 us
    pallas_call x1, Pallas kernels, owned(): pl.pallas_call(functools.partial(owned_kernel, plan), out_shape=[jax.Shap...  6.44 us
  transfers between devices with their start and end apart: 34, of which 17 were waited for; matrix products, arithmetic and copies ran while one was open for 2% of the time, Pallas kernels for 4%

profile of v21, /device:TPU:0, one launch (start us, length us, event | category | flops | bytes accessed | tf_op | source)
XLA Modules:
  0.0 167.2 jit_solution(9371248658488960787)
XLA Ops:
  0.6 21.4 %place_gradients.1 = (f32[1096,128]{1,0:T(8,128)}, f32[1096,128]{1,0:T(8,128)}, f32[1096,128]{1,0:T(8,128)}, f32[1096,128]{1,0:T(8,128)}, f32[1096,128]{1,0:T(8,...) custom-call(s32[136,128]{1,0:T(8,128)} %bitcast.15, ...), custom_call_target="tpu_custom_call" | custom-call | tf_op jit(solution)/shard_map/place_gradients/pallas_call | solution.py:316
  22.0 0.5 collective-permute-start
  22.6 1.8 %collective-permute-done = f32[1096,128]{1,0:T(8,128)S(1)} collective-permute-done((f32[1096,128]{1,0:T(8,128)}, f32[1096,128]{1,0:T(8,128)S(1)}, u32[]{:S(2)}, u32[]{:S(2)}) %collective-permute-start) | collective-permute-done | bytes 561184 | tf_op jit(solution)/shard_map/ppermute | solution.py:79
  24.4 1.1 add.68
  25.5 0.4 collective-permute-start.8
  25.9 0.1 collective-permute-start.4
  26.1 2.9 %collective-permute-start.5 = (f32[1096,128]{1,0:T(8,128)S(1)}, f32[1096,128]{1,0:T(8,128)S(1)}, u32[]{:S(2)}, u32[]{:S(2)}) collective-permute-start(f32[1096,128]{1,0:T(8,128)S(1)} %add.68), channel_id=1, source_target_pairs={{0,4},{2,6},{4,0},{6,2},{8,12},{10,14},{12,8},{14,10},{16,20},{18,... | collective-permute-start | bytes 1683464 | tf_op jit(solution)/shard_map/ppermute | solution.py:79
  28.9 0.5 collective-permute-start.13
  29.5 1.2 collective-permute-start.9
  30.7 11.7 %collective-permute-done.5 = f32[1096,128]{1,0:T(8,128)S(1)} collective-permute-done((f32[1096,128]{1,0:T(8,128)S(1)}, f32[1096,128]{1,0:T(8,128)S(1)}, u32[]{:S(2)}, u32[]{:S(2)}) %collective-permute-start.5) | collective-permute-done | bytes 561184 | tf_op jit(solution)/shard_map/ppermute | solution.py:79
  42.4 0.1 add_add_fusion.2
  42.5 4.1 %collective-permute-start.6 = (f32[1096,128]{1,0:T(8,128)S(1)}, f32[1096,128]{1,0:T(8,128)S(1)}, u32[]{:S(2)}, u32[]{:S(2)}) collective-permute-start(f32[1096,128]{1,0:T(8,128)S(1)} %add_add_fusion.2), channel_id=1, source_target_pairs={{0,8},{2,10},{4,12},{6,14},{24,16},{26,18},{28,20},{30,22},{1,9},{... | collective-permute-start | bytes 1683464 | tf_op jit(solution)/shard_map/ppermute | solution.py:79
  46.6 0.7 pad_add_fusion.place_ref
  47.3 6.4 %owned_weights.1 = (f32[1088,128]{1,0:T(8,128)}, s32[1152,128]{1,0:T(8,128)}) custom-call(s32[3]{0:T(128)} %pad_add_fusion.place_ref, s32[136,128]{1,0:T(8,128)} %bitcast.16, f32[17408,128]{1,0:T(8,128)} %weights_ref.3), custom_call_target="tpu_custom_call" | custom-call | bytes 20971520 | tf_op jit(solution)/shard_map/owned_weights/pallas_call | solution.py:393
  53.7 0.1 collective-permute-start.2
  53.8 0.5 collective-permute-start.12
  54.3 1.1 add.79
  55.5 1.6 collective-permute-start.14
  57.0 0.1 add_add_fusion.1
  57.2 4.4 %collective-permute-start.11 = (f32[1096,128]{1,0:T(8,128)S(1)}, f32[1096,128]{1,0:T(8,128)S(1)}, u32[]{:S(2)}, u32[]{:S(2)}) collective-permute-start(f32[1096,128]{1,0:T(8,128)S(1)} %add_add_fusion.1), channel_id=1, source_target_pairs={{0,8},{2,10},{4,12},{6,14},{24,16},{26,18},{28,20},{30,22},{1,9},{... | collective-permute-start | bytes 1683464 | tf_op jit(solution)/shard_map/ppermute | solution.py:79
  61.6 0.1 add.76
  61.7 0.8 collective-permute-start.10
  62.6 0.1 collective-permute-start.1
  62.6 0.1 add.70
  62.7 1.6 collective-permute-start.3
  64.3 6.8 %collective-permute-done.14 = f32[1096,128]{1,0:T(8,128)S(1)} collective-permute-done((f32[1096,128]{1,0:T(8,128)S(1)}, f32[1096,128]{1,0:T(8,128)S(1)}, u32[]{:S(2)}, u32[]{:S(2)}) %collective-permute-start.14) | collective-permute-done | bytes 561184 | tf_op jit(solution)/shard_map/ppermute | solution.py:79
  71.1 0.1 add_add_fusion
  71.2 0.1 collective-permute-done.11
  71.4 0.1 add.81
  71.5 4.0 %collective-permute-start.15 = (f32[1096,128]{1,0:T(8,128)S(1)}, f32[1096,128]{1,0:T(8,128)S(1)}, u32[]{:S(2)}, u32[]{:S(2)}) collective-permute-start(f32[1096,128]{1,0:T(8,128)S(1)} %add.81), channel_id=1, source_target_pairs={{0,8},{2,10},{4,12},{6,14},{8,0},{10,2},{12,4},{14,6},{16,24},{18,... | collective-permute-start | bytes 1683464 | tf_op jit(solution)/shard_map/ppermute | solution.py:79
  75.4 0.7 collective-permute-start.16
  76.2 0.1 add.69.refs_0_
  76.2 6.0 %collective-permute-done.3.refs_1_ = f32[1096,128]{1,0:T(8,128)S(1)} collective-permute-done((f32[1096,128]{1,0:T(8,128)S(1)}, f32[1096,128]{1,0:T(8,128)S(1)}, u32[]{:S(2)}, u32[]{:S(2)}) %collective-permute-start.3) | collective-permute-done | bytes 561184 | tf_op jit(solution)/shard_map/ppermute | solution.py:79
  82.3 2.7 %collective-permute-done.15.refs_2_ = f32[1096,128]{1,0:T(8,128)S(1)} collective-permute-done((f32[1096,128]{1,0:T(8,128)S(1)}, f32[1096,128]{1,0:T(8,128)S(1)}, u32[]{:S(2)}, u32[]{:S(2)}) %collective-permute-start.15) | collective-permute-done | bytes 561184 | tf_op jit(solution)/shard_map/ppermute | solution.py:79
  85.0 2.0 %moments.1 = (f32[1088,128]{1,0:T(8,128)}, f32[1088,128]{1,0:T(8,128)}, f32[1096,128]{1,0:T(8,128)S(1)}) custom-call(f32[1096,128]{1,0:T(8,128)S(1)} %add.69.refs_0_, f32[1096,128]{1,0:T(8,128)S(1)} %collective-permute-done.3.refs_1_, f32[1096,128]{1,0:T(8,128)S(1)} %collective-permute-done.15.refs_2_, f32[1096,128]{1,0:T(8,128)S(1)} %collective-permute-done.16.refs_3_, ...), custom_call_target="tpu_custom_call" | custom-call | tf_op jit(solution)/shard_map/moments/pallas_call | solution.py:447
  87.1 3.8 %collective-permute-start.18 = (f32[1096,128]{1,0:T(8,128)S(1)}, f32[1096,128]{1,0:T(8,128)S(1)}, u32[]{:S(2)}, u32[]{:S(2)}) collective-permute-start(f32[1096,128]{1,0:T(8,128)S(1)} %get-tuple-element.92), channel_id=1, source_target_pairs={{0,8},{2,10},{4,12},{6,14},{8,0},{10,2},{12,4},{14,6},{16,24},{18,... | collective-permute-start | bytes 1683464 | tf_op jit(solution)/shard_map/ppermute | solution.py:79
  90.9 1.5 collective-permute-start.19
  92.4 0.7 collective-permute-start.17
  93.1 6.4 %collective-permute-done.18 = f32[1096,128]{1,0:T(8,128)S(1)} collective-permute-done((f32[1096,128]{1,0:T(8,128)S(1)}, f32[1096,128]{1,0:T(8,128)S(1)}, u32[]{:S(2)}, u32[]{:S(2)}) %collective-permute-start.18) | collective-permute-done | bytes 561184 | tf_op jit(solution)/shard_map/ppermute | solution.py:79
  99.5 1.5 collective-permute-start.24
  101.0 0.7 collective-permute-start.20
  101.7 0.1 pad_maximum_fusion.refs_0_.refs_1_
  101.8 2.9 %collective-permute-done.19 = f32[1096,128]{1,0:T(8,128)S(1)} collective-permute-done((f32[1096,128]{1,0:T(8,128)S(1)}, f32[1096,128]{1,0:T(8,128)S(1)}, u32[]{:S(2)}, u32[]{:S(2)}) %collective-permute-start.19) | collective-permute-done | bytes 561184 | tf_op jit(solution)/shard_map/ppermute | solution.py:79
  104.7 1.3 collective-permute-start.23
  106.0 7.0 %collective-permute-done.24 = f32[1096,128]{1,0:T(8,128)S(1)} collective-permute-done((f32[1096,128]{1,0:T(8,128)S(1)}, f32[1096,128]{1,0:T(8,128)S(1)}, u32[]{:S(2)}, u32[]{:S(2)}) %collective-permute-start.24) | collective-permute-done | bytes 561184 | tf_op jit(solution)/shard_map/ppermute | solution.py:79
  113.0 1.3 collective-permute-start.21
  114.3 0.1 pad_maximum_fusion.1.refs_1_
  114.4 3.0 %collective-permute-done.23 = f32[1096,128]{1,0:T(8,128)S(1)} collective-permute-done((f32[1096,128]{1,0:T(8,128)S(1)}, f32[1096,128]{1,0:T(8,128)S(1)}, u32[]{:S(2)}, u32[]{:S(2)}) %collective-permute-start.23) | collective-permute-done | bytes 561184 | tf_op jit(solution)/shard_map/ppermute | solution.py:79
  117.4 0.1 add.83.refs_2_
  117.5 2.5 %collective-permute-start.26 = (f32[1096,128]{1,0:T(8,128)S(1)}, f32[1096,128]{1,0:T(8,128)S(1)}, u32[]{:S(2)}, u32[]{:S(2)}) collective-permute-start(f32[1096,128]{1,0:T(8,128)S(1)} %add.83.refs_2_), channel_id=1, source_target_pairs={{0,4},{2,6},{4,0},{6,2},{8,12},{10,14},{12,8},{14,10},{16,20},{18,... | collective-permute-start | bytes 1683464 | tf_op jit(solution)/shard_map/ppermute | solution.py:79
  120.0 8.2 %collective-permute-done.21 = f32[1096,128]{1,0:T(8,128)S(1)} collective-permute-done((f32[1096,128]{1,0:T(8,128)S(1)}, f32[1096,128]{1,0:T(8,128)S(1)}, u32[]{:S(2)}, u32[]{:S(2)}) %collective-permute-start.21) | collective-permute-done | bytes 561184 | tf_op jit(solution)/shard_map/ppermute | solution.py:79
  128.2 0.1 add.82.refs_3_
  128.3 0.6 sums.1
  128.8 1.6 collective-permute-start.25
  130.4 0.5 collective-permute-start.31
  130.9 0.5 collective-permute-start.29
  131.4 1.1 collective-permute-done.25
  132.5 0.6 collective-permute-start.27
  133.1 2.4 %collective-permute-done.27 = f32[8,128]{1,0:T(8,128)S(1)} collective-permute-done((f32[8,128]{1,0:T(8,128)S(1)}, f32[8,128]{1,0:T(8,128)S(1)}, u32[]{:S(2)}, u32[]{:S(2)}) %collective-permute-start.27) | collective-permute-done | bytes 4128 | tf_op jit(solution)/shard_map/ppermute | solution.py:79
  135.6 1.5 collective-permute-start.28
  137.1 2.0 %collective-permute-done.28 = f32[8,128]{1,0:T(8,128)S(1)} collective-permute-done((f32[8,128]{1,0:T(8,128)S(1)}, f32[8,128]{1,0:T(8,128)S(1)}, u32[]{:S(2)}, u32[]{:S(2)}) %collective-permute-start.28) | collective-permute-done | bytes 4128 | tf_op jit(solution)/shard_map/ppermute | solution.py:165
  139.2 6.3 %collective-permute-done.29.refs_4_ = f32[1096,128]{1,0:T(8,128)S(1)} collective-permute-done((f32[1096,128]{1,0:T(8,128)S(1)}, f32[1096,128]{1,0:T(8,128)S(1)}, u32[]{:S(2)}, u32[]{:S(2)}) %collective-permute-start.29) | collective-permute-done | bytes 561184 | tf_op jit(solution)/shard_map/ppermute | solution.py:79
  145.5 1.9 %collective-permute-done.33.refs_9_ = f32[1096,128]{1,0:T(8,128)S(1)} collective-permute-done((f32[1096,128]{1,0:T(8,128)S(1)}, f32[1096,128]{1,0:T(8,128)S(1)}, u32[]{:S(2)}, u32[]{:S(2)}) %collective-permute-start.33) | collective-permute-done | bytes 561184 | tf_op jit(solution)/shard_map/ppermute | solution.py:79
  147.5 19.6 %new_weights.1 = (f32[17408,128]{1,0:T(8,128)}, f32[3,2,1024]{2,1,0:T(2,128)}, f32[7]{0:T(128)}) custom-call(s32[3]{0:T(128)S(1)} %copy-done.6, s32[136,128]{1,0:T(8,128)S(1)} %copy-done.4, f32[8,128]{1,0:T(8,128)S(1)} %add.86.total_ref, f32[3,2,1024]{2,1,0:T(2,128)S(1)} %copy-done.5, f32[17408,128]{1,0:T(8,128)S(1)} %bitcast.11, ...), custom_call_target="tpu_custom_call" | custom-call | tf_op jit(solution)/shard_map/new_weights/pallas_call | solution.py:525
  (71 shorter events, 0.4 us)
Async XLA Ops:
  22.0 7.4 %copy-start.13 = (f32[1096,128]{1,0:T(8,128)S(1)}, f32[1096,128]{1,0:T(8,128)}, u32[]{:S(2)}) copy-start(f32[1096,128]{1,0:T(8,128)} %get-tuple-element.77) | copy-start | bytes 1683460
  22.0 2.3 %collective-permute-start = (f32[1096,128]{1,0:T(8,128)}, f32[1096,128]{1,0:T(8,128)S(1)}, u32[]{:S(2)}, u32[]{:S(2)}) collective-permute-start(f32[1096,128]{1,0:T(8,128)} %get-tuple-element.61), channel_id=1, source_target_pairs={{0,2},{2,0},{4,6},{6,4},{8,10},{10,8},{12,14},{14,12},{16,18},{18,... | collective-permute-start | bytes 1683464 | tf_op jit(solution)/shard_map/ppermute | solution.py:79
  25.5 16.9 %copy-start.12 = (f32[1096,128]{1,0:T(8,128)S(1)}, f32[1096,128]{1,0:T(8,128)}, u32[]{:S(2)}) copy-start(f32[1096,128]{1,0:T(8,128)} %get-tuple-element.72) | copy-start | bytes 1683460
  25.5 4.0 %collective-permute-start.8 = (f32[1096,128]{1,0:T(8,128)}, f32[1096,128]{1,0:T(8,128)S(1)}, u32[]{:S(2)}, u32[]{:S(2)}) collective-permute-start(f32[1096,128]{1,0:T(8,128)} %get-tuple-element.78), channel_id=1, source_target_pairs={{0,2},{2,0},{4,6},{6,4},{8,10},{10,8},{12,14},{14,12},{16,18},{18,... | collective-permute-start | bytes 1683464 | tf_op jit(solution)/shard_map/ppermute | solution.py:79
  25.9 4.8 %collective-permute-start.4 = (f32[1096,128]{1,0:T(8,128)}, f32[1096,128]{1,0:T(8,128)S(1)}, u32[]{:S(2)}, u32[]{:S(2)}) collective-permute-start(f32[1096,128]{1,0:T(8,128)} %get-tuple-element.73), channel_id=1, source_target_pairs={{0,2},{2,0},{4,6},{6,4},{8,10},{10,8},{12,14},{14,12},{16,18},{18,... | collective-permute-start | bytes 1683464 | tf_op jit(solution)/shard_map/ppermute | solution.py:79
  26.1 16.4 %collective-permute-start.5 = (f32[1096,128]{1,0:T(8,128)S(1)}, f32[1096,128]{1,0:T(8,128)S(1)}, u32[]{:S(2)}, u32[]{:S(2)}) collective-permute-start(f32[1096,128]{1,0:T(8,128)S(1)} %add.68), channel_id=1, source_target_pairs={{0,4},{2,6},{4,0},{6,2},{8,12},{10,14},{12,8},{14,10},{16,20},{18,... | collective-permute-start | bytes 1683464 | tf_op jit(solution)/shard_map/ppermute | solution.py:79
  28.9 26.5 %collective-permute-start.7 = (f32[1096,128]{1,0:T(8,128)}, f32[1096,128]{1,0:T(8,128)S(1)}, u32[]{:S(2)}, u32[]{:S(2)}) collective-permute-start(f32[1096,128]{1,0:T(8,128)} %get-tuple-element.76), channel_id=1, source_target_pairs={{0,2},{2,0},{4,6},{6,4},{8,10},{10,8},{12,14},{14,12},{16,18},{18,... | collective-permute-start | bytes 1683464 | tf_op jit(solution)/shard_map/ppermute | solution.py:79
  28.9 24.9 %collective-permute-start.13 = (f32[1096,128]{1,0:T(8,128)}, f32[1096,128]{1,0:T(8,128)}, u32[]{:S(2)}, u32[]{:S(2)}) collective-permute-start(f32[1096,128]{1,0:T(8,128)} %get-tuple-element.86), channel_id=1, source_target_pairs={{0,2},{2,0},{4,6},{6,4},{8,10},{10,8},{12,14},{14,12},{16,18},{18,... | collective-permute-start | bytes 1683464 | tf_op jit(solution)/shard_map/ppermute | solution.py:79
  29.5 27.5 %collective-permute-start.9 = (f32[1096,128]{1,0:T(8,128)S(1)}, f32[1096,128]{1,0:T(8,128)S(1)}, u32[]{:S(2)}, u32[]{:S(2)}) collective-permute-start(f32[1096,128]{1,0:T(8,128)S(1)} %add.74), channel_id=1, source_target_pairs={{0,4},{2,6},{4,0},{6,2},{8,12},{10,14},{12,8},{14,10},{16,20},{18,... | collective-permute-start | bytes 1683464 | tf_op jit(solution)/shard_map/ppermute | solution.py:79
  42.5 14.7 %collective-permute-start.6 = (f32[1096,128]{1,0:T(8,128)S(1)}, f32[1096,128]{1,0:T(8,128)S(1)}, u32[]{:S(2)}, u32[]{:S(2)}) collective-permute-start(f32[1096,128]{1,0:T(8,128)S(1)} %add_add_fusion.2), channel_id=1, source_target_pairs={{0,8},{2,10},{4,12},{6,14},{24,16},{26,18},{28,20},{30,22},{1,9},{... | collective-permute-start | bytes 1683464 | tf_op jit(solution)/shard_map/ppermute | solution.py:79
  47.3 6.5 %copy-start.16 = (f32[1096,128]{1,0:T(8,128)S(1)}, f32[1096,128]{1,0:T(8,128)}, u32[]{:S(2)}) copy-start(f32[1096,128]{1,0:T(8,128)} %get-tuple-element.71) | copy-start | bytes 1683460
  47.3 6.6 %copy-start.15 = (f32[1096,128]{1,0:T(8,128)S(1)}, f32[1096,128]{1,0:T(8,128)}, u32[]{:S(2)}) copy-start(f32[1096,128]{1,0:T(8,128)} %get-tuple-element.84) | copy-start | bytes 1683460
  47.3 7.1 %copy-start.11 = (f32[1096,128]{1,0:T(8,128)S(1)}, f32[1096,128]{1,0:T(8,128)}, u32[]{:S(2)}) copy-start(f32[1096,128]{1,0:T(8,128)} %get-tuple-element.85) | copy-start | bytes 1683460
  53.7 3.3 %copy-start.10 = (f32[1096,128]{1,0:T(8,128)S(1)}, f32[1096,128]{1,0:T(8,128)}, u32[]{:S(2)}) copy-start(f32[1096,128]{1,0:T(8,128)} %get-tuple-element.75) | copy-start | bytes 1683460
  53.7 8.8 %collective-permute-start.2 = (f32[1096,128]{1,0:T(8,128)S(1)}, f32[1096,128]{1,0:T(8,128)S(1)}, u32[]{:S(2)}, u32[]{:S(2)}) collective-permute-start(f32[1096,128]{1,0:T(8,128)S(1)} %copy-done.16), channel_id=1, source_target_pairs={{0,2},{2,0},{4,6},{6,4},{8,10},{10,8},{12,14},{14,12},{16,18},{18,... | collective-permute-start | bytes 1683464 | tf_op jit(solution)/shard_map/ppermute | solution.py:79
  53.8 8.9 %collective-permute-start.12 = (f32[1096,128]{1,0:T(8,128)S(1)}, f32[1096,128]{1,0:T(8,128)S(1)}, u32[]{:S(2)}, u32[]{:S(2)}) collective-permute-start(f32[1096,128]{1,0:T(8,128)S(1)} %copy-done.15), channel_id=1, source_target_pairs={{0,2},{2,0},{4,6},{6,4},{8,10},{10,8},{12,14},{14,12},{16,18},{18,... | collective-permute-start | bytes 1683464 | tf_op jit(solution)/shard_map/ppermute | solution.py:79
  55.5 15.6 %collective-permute-start.14 = (f32[1096,128]{1,0:T(8,128)S(1)}, f32[1096,128]{1,0:T(8,128)S(1)}, u32[]{:S(2)}, u32[]{:S(2)}) collective-permute-start(f32[1096,128]{1,0:T(8,128)S(1)} %add.79), channel_id=1, source_target_pairs={{0,4},{2,6},{4,0},{6,2},{8,12},{10,14},{12,8},{14,10},{16,20},{18,... | collective-permute-start | bytes 1683464 | tf_op jit(solution)/shard_map/ppermute | solution.py:79
  57.1 5.4 %copy-start.14 = (f32[1096,128]{1,0:T(8,128)S(1)}, f32[1096,128]{1,0:T(8,128)}, u32[]{:S(2)}) copy-start(f32[1096,128]{1,0:T(8,128)} %get-tuple-element.69) | copy-start | bytes 1683460
  57.1 5.5 %copy-start.9 = (f32[1096,128]{1,0:T(8,128)S(1)}, f32[1096,128]{1,0:T(8,128)}, u32[]{:S(2)}) copy-start(f32[1096,128]{1,0:T(8,128)} %get-tuple-element.70) | copy-start | bytes 1683460
  57.2 14.1 %collective-permute-start.11 = (f32[1096,128]{1,0:T(8,128)S(1)}, f32[1096,128]{1,0:T(8,128)S(1)}, u32[]{:S(2)}, u32[]{:S(2)}) collective-permute-start(f32[1096,128]{1,0:T(8,128)S(1)} %add_add_fusion.1), channel_id=1, source_target_pairs={{0,8},{2,10},{4,12},{6,14},{24,16},{26,18},{28,20},{30,22},{1,9},{... | collective-permute-start | bytes 1683464 | tf_op jit(solution)/shard_map/ppermute | solution.py:79
  61.7 9.4 %copy-start.8 = (f32[1096,128]{1,0:T(8,128)S(1)}, f32[1096,128]{1,0:T(8,128)}, u32[]{:S(2)}) copy-start(f32[1096,128]{1,0:T(8,128)} %get-tuple-element.83) | copy-start | bytes 1683460
  61.7 9.7 %collective-permute-start.10 = (f32[1096,128]{1,0:T(8,128)S(1)}, f32[1096,128]{1,0:T(8,128)S(1)}, u32[]{:S(2)}, u32[]{:S(2)}) collective-permute-start(f32[1096,128]{1,0:T(8,128)S(1)} %add.76), channel_id=1, source_target_pairs={{8,16},{10,18},{12,20},{14,22},{16,8},{18,10},{20,12},{22,14},{9,1... | collective-permute-start | bytes 1683464 | tf_op jit(solution)/shard_map/ppermute | solution.py:79
  62.6 13.6 %collective-permute-start.1 = (f32[1096,128]{1,0:T(8,128)S(1)}, f32[1096,128]{1,0:T(8,128)S(1)}, u32[]{:S(2)}, u32[]{:S(2)}) collective-permute-start(f32[1096,128]{1,0:T(8,128)S(1)} %copy-done.14), channel_id=1, source_target_pairs={{0,2},{2,0},{4,6},{6,4},{8,10},{10,8},{12,14},{14,12},{16,18},{18,... | collective-permute-start | bytes 1683464 | tf_op jit(solution)/shard_map/ppermute | solution.py:79
  62.7 19.5 %collective-permute-start.3 = (f32[1096,128]{1,0:T(8,128)S(1)}, f32[1096,128]{1,0:T(8,128)S(1)}, u32[]{:S(2)}, u32[]{:S(2)}) collective-permute-start(f32[1096,128]{1,0:T(8,128)S(1)} %add.70), channel_id=1, source_target_pairs={{0,4},{2,6},{4,0},{6,2},{8,12},{10,14},{12,8},{14,10},{16,20},{18,... | collective-permute-start | bytes 1683464 | tf_op jit(solution)/shard_map/ppermute | solution.py:79
  71.1 5.1 %copy-start.7 = (f32[1096,128]{1,0:T(8,128)S(1)}, f32[1096,128]{1,0:T(8,128)}, u32[]{:S(2)}) copy-start(f32[1096,128]{1,0:T(8,128)} %get-tuple-element.59) | copy-start | bytes 1683460
  71.1 13.9 %copy-start.1 = (f32[1,1088,128]{2,1,0:T(8,128)S(1)}, f32[1,1088,128]{2,1,0:T(8,128)}, u32[]{:S(2)}) copy-start(f32[1,1088,128]{2,1,0:T(8,128)} %param.9) | copy-start | bytes 1671172
  71.1 13.9 %copy-start.2 = (f32[1,1088,128]{2,1,0:T(8,128)S(1)}, f32[1,1088,128]{2,1,0:T(8,128)}, u32[]{:S(2)}) copy-start(f32[1,1088,128]{2,1,0:T(8,128)} %param.10) | copy-start | bytes 1671172
  71.1 13.9 %copy-start.3 = (f32[1088,128]{1,0:T(8,128)S(1)}, f32[1088,128]{1,0:T(8,128)}, u32[]{:S(2)}) copy-start(f32[1088,128]{1,0:T(8,128)} %get-tuple-element.90.refs_6_) | copy-start | bytes 1671172
  71.3 76.2 %slice-start = ((s8[8912896]{0:T(1024)(128)(4,1)}), s8[4194304]{0:T(1024)(128)(4,1)S(1)}, s32[]{:S(2)}) async-start(s8[8912896]{0:T(1024)(128)(4,1)} %bitcast.10), calls=%async_computation | async-start | bytes 8388608
  71.4 13.6 %copy-start = (s32[1152,128]{1,0:T(8,128)S(1)}, s32[1152,128]{1,0:T(8,128)}, u32[]{:S(2)}) copy-start(s32[1152,128]{1,0:T(8,128)} %get-tuple-element.91.refs_7_) | copy-start | bytes 1769476
  71.5 13.5 %collective-permute-start.15 = (f32[1096,128]{1,0:T(8,128)S(1)}, f32[1096,128]{1,0:T(8,128)S(1)}, u32[]{:S(2)}, u32[]{:S(2)}) collective-permute-start(f32[1096,128]{1,0:T(8,128)S(1)} %add.81), channel_id=1, source_target_pairs={{0,8},{2,10},{4,12},{6,14},{8,0},{10,2},{12,4},{14,6},{16,24},{18,... | collective-permute-start | bytes 1683464 | tf_op jit(solution)/shard_map/ppermute | solution.py:79
  75.4 9.5 %collective-permute-start.16 = (f32[1096,128]{1,0:T(8,128)S(1)}, f32[1096,128]{1,0:T(8,128)S(1)}, u32[]{:S(2)}, u32[]{:S(2)}) collective-permute-start(f32[1096,128]{1,0:T(8,128)S(1)} %add.77), channel_id=1, source_target_pairs={{8,16},{10,18},{12,20},{14,22},{16,8},{18,10},{20,12},{22,14},{9,1... | collective-permute-start | bytes 1683464 | tf_op jit(solution)/shard_map/ppermute | solution.py:79
  85.0 62.5 %slice-start.1 = ((s8[8912896]{0:T(1024)(128)(4,1)}), s8[4194304]{0:T(1024)(128)(4,1)S(1)}, s32[]{:S(2)}) async-start(s8[8912896]{0:T(1024)(128)(4,1)} %bitcast.10), calls=%async_computation.1 | async-start | bytes 8388608
  87.1 12.5 %collective-permute-start.18 = (f32[1096,128]{1,0:T(8,128)S(1)}, f32[1096,128]{1,0:T(8,128)S(1)}, u32[]{:S(2)}, u32[]{:S(2)}) collective-permute-start(f32[1096,128]{1,0:T(8,128)S(1)} %get-tuple-element.92), channel_id=1, source_target_pairs={{0,8},{2,10},{4,12},{6,14},{8,0},{10,2},{12,4},{14,6},{16,24},{18,... | collective-permute-start | bytes 1683464 | tf_op jit(solution)/shard_map/ppermute | solution.py:79
  90.9 13.8 %collective-permute-start.19 = (f32[1096,128]{1,0:T(8,128)S(1)}, f32[1096,128]{1,0:T(8,128)S(1)}, u32[]{:S(2)}, u32[]{:S(2)}) collective-permute-start(f32[1096,128]{1,0:T(8,128)S(1)} %get-tuple-element.92), channel_id=1, source_target_pairs={{0,4},{2,6},{4,0},{6,2},{8,12},{10,14},{12,8},{14,10},{16,20},{18,... | collective-permute-start | bytes 1683464 | tf_op jit(solution)/shard_map/ppermute | solution.py:79
  92.4 12.3 %collective-permute-start.17 = (f32[1096,128]{1,0:T(8,128)S(1)}, f32[1096,128]{1,0:T(8,128)S(1)}, u32[]{:S(2)}, u32[]{:S(2)}) collective-permute-start(f32[1096,128]{1,0:T(8,128)S(1)} %get-tuple-element.92), channel_id=1, source_target_pairs={{8,16},{10,18},{12,20},{14,22},{16,8},{18,10},{20,12},{22,14},{9,1... | collective-permute-start | bytes 1683464 | tf_op jit(solution)/shard_map/ppermute | solution.py:79
  99.5 13.5 %collective-permute-start.24 = (f32[1096,128]{1,0:T(8,128)S(1)}, f32[1096,128]{1,0:T(8,128)S(1)}, u32[]{:S(2)}, u32[]{:S(2)}) collective-permute-start(f32[1096,128]{1,0:T(8,128)S(1)} %collective-permute-done.18), channel_id=1, source_target_pairs={{0,4},{2,6},{4,0},{6,2},{8,12},{10,14},{12,8},{14,10},{16,20},{18,... | collective-permute-start | bytes 1683464 | tf_op jit(solution)/shard_map/ppermute | solution.py:79
  101.0 12.0 %collective-permute-start.20 = (f32[1096,128]{1,0:T(8,128)S(1)}, f32[1096,128]{1,0:T(8,128)S(1)}, u32[]{:S(2)}, u32[]{:S(2)}) collective-permute-start(f32[1096,128]{1,0:T(8,128)S(1)} %collective-permute-done.18), channel_id=1, source_target_pairs={{8,16},{10,18},{12,20},{14,22},{16,8},{18,10},{20,12},{22,14},{9,1... | collective-permute-start | bytes 1683464 | tf_op jit(solution)/shard_map/ppermute | solution.py:79
  104.7 12.7 %collective-permute-start.23 = (f32[1096,128]{1,0:T(8,128)S(1)}, f32[1096,128]{1,0:T(8,128)S(1)}, u32[]{:S(2)}, u32[]{:S(2)}) collective-permute-start(f32[1096,128]{1,0:T(8,128)S(1)} %collective-permute-done.17), channel_id=1, source_target_pairs={{8,0},{10,2},{12,4},{14,6},{16,24},{18,26},{20,28},{22,30},{9,1},{... | collective-permute-start | bytes 1683464 | tf_op jit(solution)/shard_map/ppermute | solution.py:79
  113.0 15.2 %collective-permute-start.21 = (f32[1096,128]{1,0:T(8,128)S(1)}, f32[1096,128]{1,0:T(8,128)S(1)}, u32[]{:S(2)}, u32[]{:S(2)}) collective-permute-start(f32[1096,128]{1,0:T(8,128)S(1)} %collective-permute-done.20), channel_id=1, source_target_pairs={{8,0},{10,2},{12,4},{14,6},{16,24},{18,26},{20,28},{22,30},{9,1},{... | collective-permute-start | bytes 1683464 | tf_op jit(solution)/shard_map/ppermute | solution.py:79
  114.4 33.1 %slice-start.2 = ((s8[8912896]{0:T(1024)(128)(4,1)}), s8[524288]{0:T(1024)(128)(4,1)S(1)}, s32[]{:S(2)}) async-start(s8[8912896]{0:T(1024)(128)(4,1)} %bitcast.10), calls=%async_computation.2 | async-start | bytes 1048576
  117.4 10.8 %copy-start.6 = (s32[3]{0:T(128)S(1)}, s32[3]{0:T(128)}, u32[]{:S(2)}) copy-start(s32[3]{0:T(128)} %pad_add_fusion.place_ref) | copy-start | bytes 40
  117.5 15.1 %collective-permute-start.26 = (f32[1096,128]{1,0:T(8,128)S(1)}, f32[1096,128]{1,0:T(8,128)S(1)}, u32[]{:S(2)}, u32[]{:S(2)}) collective-permute-start(f32[1096,128]{1,0:T(8,128)S(1)} %add.83.refs_2_), channel_id=1, source_target_pairs={{0,4},{2,6},{4,0},{6,2},{8,12},{10,14},{12,8},{14,10},{16,20},{18,... | collective-permute-start | bytes 1683464 | tf_op jit(solution)/shard_map/ppermute | solution.py:79
  128.8 3.7 %collective-permute-start.25 = (f32[8,128]{1,0:T(8,128)S(1)}, f32[8,128]{1,0:T(8,128)S(1)}, u32[]{:S(2)}, u32[]{:S(2)}) collective-permute-start(f32[8,128]{1,0:T(8,128)S(1)} %sums.1), channel_id=1, source_target_pairs={{0,4},{2,6},{4,0},{6,2},{8,12},{10,14},{12,8},{14,10},{16,20},{18,... | collective-permute-start | bytes 12296 | tf_op jit(solution)/shard_map/ppermute | solution.py:79
  130.4 15.1 %collective-permute-start.30 = (f32[2192,128]{1,0:T(8,128)S(1)}, f32[2192,128]{1,0:T(8,128)S(1)}, u32[]{:S(2)}, u32[]{:S(2)}) collective-permute-start(f32[2192,128]{1,0:T(8,128)S(1)} %pad_maximum_fusion.refs_0_.refs_1_), channel_id=1, source_target_pairs={{0,2},{2,0},{4,6},{6,4},{8,10},{10,8},{12,14},{14,12},{16,18},{18,... | collective-permute-start | bytes 3366920 | tf_op jit(solution)/shard_map/ppermute | solution.py:79
  130.4 15.1 %collective-permute-start.31 = (f32[2192,128]{1,0:T(8,128)S(1)}, f32[2192,128]{1,0:T(8,128)S(1)}, u32[]{:S(2)}, u32[]{:S(2)}) collective-permute-start(f32[2192,128]{1,0:T(8,128)S(1)} %pad_maximum_fusion.1.refs_1_), channel_id=1, source_target_pairs={{0,2},{2,0},{4,6},{6,4},{8,10},{10,8},{12,14},{14,12},{16,18},{18,... | collective-permute-start | bytes 3366920 | tf_op jit(solution)/shard_map/ppermute | solution.py:79
  130.9 14.6 %collective-permute-start.29 = (f32[1096,128]{1,0:T(8,128)S(1)}, f32[1096,128]{1,0:T(8,128)S(1)}, u32[]{:S(2)}, u32[]{:S(2)}) collective-permute-start(f32[1096,128]{1,0:T(8,128)S(1)} %add.82.refs_3_), channel_id=1, source_target_pairs={{0,4},{2,6},{4,0},{6,2},{8,12},{10,14},{12,8},{14,10},{16,20},{18,... | collective-permute-start | bytes 1683464 | tf_op jit(solution)/shard_map/ppermute | solution.py:79
  132.5 13.0 %collective-permute-start.22 = (f32[1096,128]{1,0:T(8,128)S(1)}, f32[1096,128]{1,0:T(8,128)S(1)}, u32[]{:S(2)}, u32[]{:S(2)}) collective-permute-start(f32[1096,128]{1,0:T(8,128)S(1)} %add.82.refs_3_), channel_id=1, source_target_pairs={{0,2},{2,0},{4,6},{6,4},{8,10},{10,8},{12,14},{14,12},{16,18},{18,... | collective-permute-start | bytes 1683464 | tf_op jit(solution)/shard_map/ppermute | solution.py:79
  132.5 15.0 %copy-start.4 = (s32[136,128]{1,0:T(8,128)S(1)}, s32[136,128]{1,0:T(8,128)}, u32[]{:S(2)}) copy-start(s32[136,128]{1,0:T(8,128)} %get-tuple-element.58.position_ref) | copy-start | bytes 208900
  132.5 15.0 %copy-start.5 = (f32[3,2,1024]{2,1,0:T(2,128)S(1)}, f32[3,2,1024]{2,1,0:T(2,128)}, u32[]{:S(2)}) copy-start(f32[3,2,1024]{2,1,0:T(2,128)} %norm_ref.1) | copy-start | bytes 73732
  132.5 3.0 %collective-permute-start.27 = (f32[8,128]{1,0:T(8,128)S(1)}, f32[8,128]{1,0:T(8,128)S(1)}, u32[]{:S(2)}, u32[]{:S(2)}) collective-permute-start(f32[8,128]{1,0:T(8,128)S(1)} %add.84), channel_id=1, source_target_pairs={{0,2},{2,0},{4,6},{6,4},{8,10},{10,8},{12,14},{14,12},{16,18},{18,... | collective-permute-start | bytes 12296 | tf_op jit(solution)/shard_map/ppermute | solution.py:79
  135.6 3.6 %collective-permute-start.28 = (f32[8,128]{1,0:T(8,128)S(1)}, f32[8,128]{1,0:T(8,128)S(1)}, u32[]{:S(2)}, u32[]{:S(2)}) collective-permute-start(f32[8,128]{1,0:T(8,128)S(1)} %add.85), channel_id=1, source_target_pairs={{0,1},{1,0},{2,3},{3,2},{4,5},{5,4},{6,7},{7,6},{8,9},{9,8},{10,11... | collective-permute-start | bytes 12296 | tf_op jit(solution)/shard_map/ppermute | solution.py:165
  139.2 8.3 %collective-permute-start.32 = (f32[2192,128]{1,0:T(8,128)S(1)}, f32[2192,128]{1,0:T(8,128)S(1)}, u32[]{:S(2)}, u32[]{:S(2)}) collective-permute-start(f32[2192,128]{1,0:T(8,128)S(1)} %constant_dynamic-update-slice_fusion.refs_2_), channel_id=1, source_target_pairs={{0,2},{2,0},{4,6},{6,4},{8,10},{10,8},{12,14},{14,12},{16,18},{18,... | collective-permute-start | bytes 3366920 | tf_op jit(solution)/shard_map/ppermute | solution.py:79
  145.5 2.0 %collective-permute-start.33 = (f32[1096,128]{1,0:T(8,128)S(1)}, f32[1096,128]{1,0:T(8,128)S(1)}, u32[]{:S(2)}, u32[]{:S(2)}) collective-permute-start(f32[1096,128]{1,0:T(8,128)S(1)} %collective-permute-done.29.refs_4_), channel_id=1, source_target_pairs={{0,2},{2,0},{4,6},{6,4},{8,10},{10,8},{12,14},{14,12},{16,18},{18,... | collective-permute-start | bytes 1683464 | tf_op jit(solution)/shard_map/ppermute | solution.py:79

commit v22 on v21

--- a/solution.py
+++ b/solution.py
@@ -24,8 +24,8 @@
 matrices = 5
 MIB = 1 << 20
 TILES = 8
-FETCHES = 4
-EARLY = 0.7
+FETCHES = 5
+EARLY = 0.74
 
 
 def matrix_bounds(narrow):

time: 168 us -> 168 us (level)
  no operation moved by 1% of the time
where the time goes in v22:
time: 168 us; the launch traced here: 167 us
  waiting for transfers between devices  70.6 us (42%)
  Pallas kernels  50 us (30%)
  starting transfers between devices  41.3 us (25%)
  other arithmetic  3.91 us (2%)
    ppermute x33, waiting for transfers between devices, send(): return lax.ppermute(value, 'dp', every)  68.5 us
    ppermute x33, starting transfers between devices, send(): return lax.ppermute(value, 'dp', every)  39.8 us
    pallas_call x1, Pallas kernels, place(): pl.pallas_call(functools.partial(place_kernel, plan), out_shape=[jax.Shap...  21.3 us
    pallas_call x1, Pallas kernels, finish(): pl.pallas_call(functools.partial(finish_kernel, plan, tile, slots), grid=...  19.6 us
    pallas_call x1, Pallas kernels, owned(): pl.pallas_call(functools.partial(owned_kernel, plan), out_shape=[jax.Shap...  6.44 us
  transfers between devices with their start and end apart: 34, of which 17 were waited for; matrix products, arithmetic and copies ran while one was open for 2% of the time, Pallas kernels for 4%

profile of v22, /device:TPU:0, one launch (start us, length us, event | category | flops | bytes accessed | tf_op | source)
XLA Modules:
  0.0 167.1 jit_solution(15285624226532548371)
XLA Ops:
  0.6 21.3 %place_gradients.1 = (f32[1096,128]{1,0:T(8,128)}, f32[1096,128]{1,0:T(8,128)}, f32[1096,128]{1,0:T(8,128)}, f32[1096,128]{1,0:T(8,128)}, f32[1096,128]{1,0:T(8,...) custom-call(s32[136,128]{1,0:T(8,128)} %bitcast.15, ...), custom_call_target="tpu_custom_call" | custom-call | tf_op jit(solution)/shard_map/place_gradients/pallas_call | solution.py:316
  21.9 0.5 collective-permute-start
  22.5 1.8 %collective-permute-done = f32[1096,128]{1,0:T(8,128)S(1)} collective-permute-done((f32[1096,128]{1,0:T(8,128)}, f32[1096,128]{1,0:T(8,128)S(1)}, u32[]{:S(2)}, u32[]{:S(2)}) %collective-permute-start) | collective-permute-done | bytes 561184 | tf_op jit(solution)/shard_map/ppermute | solution.py:79
  24.3 1.1 add.68
  25.4 0.4 collective-permute-start.8
  25.8 0.1 collective-permute-start.4
  26.0 2.9 %collective-permute-start.5 = (f32[1096,128]{1,0:T(8,128)S(1)}, f32[1096,128]{1,0:T(8,128)S(1)}, u32[]{:S(2)}, u32[]{:S(2)}) collective-permute-start(f32[1096,128]{1,0:T(8,128)S(1)} %add.68), channel_id=1, source_target_pairs={{0,4},{2,6},{4,0},{6,2},{8,12},{10,14},{12,8},{14,10},{16,20},{18,... | collective-permute-start | bytes 1683464 | tf_op jit(solution)/shard_map/ppermute | solution.py:79
  28.8 0.5 collective-permute-start.13
  29.4 1.2 collective-permute-start.9
  30.6 11.7 %collective-permute-done.5 = f32[1096,128]{1,0:T(8,128)S(1)} collective-permute-done((f32[1096,128]{1,0:T(8,128)S(1)}, f32[1096,128]{1,0:T(8,128)S(1)}, u32[]{:S(2)}, u32[]{:S(2)}) %collective-permute-start.5) | collective-permute-done | bytes 561184 | tf_op jit(solution)/shard_map/ppermute | solution.py:79
  42.3 0.1 add_add_fusion.2
  42.4 4.1 %collective-permute-start.6 = (f32[1096,128]{1,0:T(8,128)S(1)}, f32[1096,128]{1,0:T(8,128)S(1)}, u32[]{:S(2)}, u32[]{:S(2)}) collective-permute-start(f32[1096,128]{1,0:T(8,128)S(1)} %add_add_fusion.2), channel_id=1, source_target_pairs={{0,8},{2,10},{4,12},{6,14},{24,16},{26,18},{28,20},{30,22},{1,9},{... | collective-permute-start | bytes 1683464 | tf_op jit(solution)/shard_map/ppermute | solution.py:79
  46.5 0.7 pad_add_fusion.place_ref
  47.2 6.4 %owned_weights.1 = (f32[1088,128]{1,0:T(8,128)}, s32[1152,128]{1,0:T(8,128)}) custom-call(s32[3]{0:T(128)} %pad_add_fusion.place_ref, s32[136,128]{1,0:T(8,128)} %bitcast.16, f32[17408,128]{1,0:T(8,128)} %weights_ref.3), custom_call_target="tpu_custom_call" | custom-call | bytes 20971520 | tf_op jit(solution)/shard_map/owned_weights/pallas_call | solution.py:393
  53.7 0.1 collective-permute-start.2
  53.8 0.5 collective-permute-start.12
  54.2 1.1 add.79
  55.4 1.6 collective-permute-start.14
  56.9 0.1 add_add_fusion.1
  57.1 4.4 %collective-permute-start.11 = (f32[1096,128]{1,0:T(8,128)S(1)}, f32[1096,128]{1,0:T(8,128)S(1)}, u32[]{:S(2)}, u32[]{:S(2)}) collective-permute-start(f32[1096,128]{1,0:T(8,128)S(1)} %add_add_fusion.1), channel_id=1, source_target_pairs={{0,8},{2,10},{4,12},{6,14},{24,16},{26,18},{28,20},{30,22},{1,9},{... | collective-permute-start | bytes 1683464 | tf_op jit(solution)/shard_map/ppermute | solution.py:79
  61.5 0.1 add.76
  61.6 0.8 collective-permute-start.10
  62.5 0.1 collective-permute-start.1
  62.5 0.1 add.70
  62.6 1.6 collective-permute-start.3
  64.2 6.8 %collective-permute-done.14 = f32[1096,128]{1,0:T(8,128)S(1)} collective-permute-done((f32[1096,128]{1,0:T(8,128)S(1)}, f32[1096,128]{1,0:T(8,128)S(1)}, u32[]{:S(2)}, u32[]{:S(2)}) %collective-permute-start.14) | collective-permute-done | bytes 561184 | tf_op jit(solution)/shard_map/ppermute | solution.py:79
  71.0 0.1 add_add_fusion
  71.1 0.1 collective-permute-done.11
  71.3 0.1 add.81
  71.4 4.0 %collective-permute-start.15 = (f32[1096,128]{1,0:T(8,128)S(1)}, f32[1096,128]{1,0:T(8,128)S(1)}, u32[]{:S(2)}, u32[]{:S(2)}) collective-permute-start(f32[1096,128]{1,0:T(8,128)S(1)} %add.81), channel_id=1, source_target_pairs={{0,8},{2,10},{4,12},{6,14},{8,0},{10,2},{12,4},{14,6},{16,24},{18,... | collective-permute-start | bytes 1683464 | tf_op jit(solution)/shard_map/ppermute | solution.py:79
  75.3 0.7 collective-permute-start.16
  76.1 0.1 add.69.refs_0_
  76.1 6.0 %collective-permute-done.3.refs_1_ = f32[1096,128]{1,0:T(8,128)S(1)} collective-permute-done((f32[1096,128]{1,0:T(8,128)S(1)}, f32[1096,128]{1,0:T(8,128)S(1)}, u32[]{:S(2)}, u32[]{:S(2)}) %collective-permute-start.3) | collective-permute-done | bytes 561184 | tf_op jit(solution)/shard_map/ppermute | solution.py:79
  82.2 2.7 %collective-permute-done.15.refs_2_ = f32[1096,128]{1,0:T(8,128)S(1)} collective-permute-done((f32[1096,128]{1,0:T(8,128)S(1)}, f32[1096,128]{1,0:T(8,128)S(1)}, u32[]{:S(2)}, u32[]{:S(2)}) %collective-permute-start.15) | collective-permute-done | bytes 561184 | tf_op jit(solution)/shard_map/ppermute | solution.py:79
  84.9 2.0 %moments.1 = (f32[1088,128]{1,0:T(8,128)}, f32[1088,128]{1,0:T(8,128)}, f32[1096,128]{1,0:T(8,128)S(1)}) custom-call(f32[1096,128]{1,0:T(8,128)S(1)} %add.69.refs_0_, f32[1096,128]{1,0:T(8,128)S(1)} %collective-permute-done.3.refs_1_, f32[1096,128]{1,0:T(8,128)S(1)} %collective-permute-done.15.refs_2_, f32[1096,128]{1,0:T(8,128)S(1)} %collective-permute-done.16.refs_3_, ...), custom_call_target="tpu_custom_call" | custom-call | tf_op jit(solution)/shard_map/moments/pallas_call | solution.py:447
  87.0 3.8 %collective-permute-start.18 = (f32[1096,128]{1,0:T(8,128)S(1)}, f32[1096,128]{1,0:T(8,128)S(1)}, u32[]{:S(2)}, u32[]{:S(2)}) collective-permute-start(f32[1096,128]{1,0:T(8,128)S(1)} %get-tuple-element.92), channel_id=1, source_target_pairs={{0,8},{2,10},{4,12},{6,14},{8,0},{10,2},{12,4},{14,6},{16,24},{18,... | collective-permute-start | bytes 1683464 | tf_op jit(solution)/shard_map/ppermute | solution.py:79
  90.8 1.5 collective-permute-start.19
  92.3 0.7 collective-permute-start.17
  93.0 6.4 %collective-permute-done.18 = f32[1096,128]{1,0:T(8,128)S(1)} collective-permute-done((f32[1096,128]{1,0:T(8,128)S(1)}, f32[1096,128]{1,0:T(8,128)S(1)}, u32[]{:S(2)}, u32[]{:S(2)}) %collective-permute-start.18) | collective-permute-done | bytes 561184 | tf_op jit(solution)/shard_map/ppermute | solution.py:79
  99.4 1.5 collective-permute-start.24
  100.9 0.7 collective-permute-start.20
  101.6 0.1 pad_maximum_fusion.refs_0_.refs_1_
  101.7 2.9 %collective-permute-done.19 = f32[1096,128]{1,0:T(8,128)S(1)} collective-permute-done((f32[1096,128]{1,0:T(8,128)S(1)}, f32[1096,128]{1,0:T(8,128)S(1)}, u32[]{:S(2)}, u32[]{:S(2)}) %collective-permute-start.19) | collective-permute-done | bytes 561184 | tf_op jit(solution)/shard_map/ppermute | solution.py:79
  104.6 1.3 collective-permute-start.23
  105.9 7.0 %collective-permute-done.24 = f32[1096,128]{1,0:T(8,128)S(1)} collective-permute-done((f32[1096,128]{1,0:T(8,128)S(1)}, f32[1096,128]{1,0:T(8,128)S(1)}, u32[]{:S(2)}, u32[]{:S(2)}) %collective-permute-start.24) | collective-permute-done | bytes 561184 | tf_op jit(solution)/shard_map/ppermute | solution.py:79
  112.9 1.3 collective-permute-start.21
  114.2 0.1 pad_maximum_fusion.1.refs_1_
  114.3 3.0 %collective-permute-done.23 = f32[1096,128]{1,0:T(8,128)S(1)} collective-permute-done((f32[1096,128]{1,0:T(8,128)S(1)}, f32[1096,128]{1,0:T(8,128)S(1)}, u32[]{:S(2)}, u32[]{:S(2)}) %collective-permute-start.23) | collective-permute-done | bytes 561184 | tf_op jit(solution)/shard_map/ppermute | solution.py:79
  117.3 0.1 add.83.refs_2_
  117.4 2.5 %collective-permute-start.26 = (f32[1096,128]{1,0:T(8,128)S(1)}, f32[1096,128]{1,0:T(8,128)S(1)}, u32[]{:S(2)}, u32[]{:S(2)}) collective-permute-start(f32[1096,128]{1,0:T(8,128)S(1)} %add.83.refs_2_), channel_id=1, source_target_pairs={{0,4},{2,6},{4,0},{6,2},{8,12},{10,14},{12,8},{14,10},{16,20},{18,... | collective-permute-start | bytes 1683464 | tf_op jit(solution)/shard_map/ppermute | solution.py:79
  119.9 8.2 %collective-permute-done.21 = f32[1096,128]{1,0:T(8,128)S(1)} collective-permute-done((f32[1096,128]{1,0:T(8,128)S(1)}, f32[1096,128]{1,0:T(8,128)S(1)}, u32[]{:S(2)}, u32[]{:S(2)}) %collective-permute-start.21) | collective-permute-done | bytes 561184 | tf_op jit(solution)/shard_map/ppermute | solution.py:79
  128.1 0.1 add.82.refs_3_
  128.2 0.6 sums.1
  128.7 1.6 collective-permute-start.25
  130.3 0.5 collective-permute-start.31
  130.8 0.5 collective-permute-start.29
  131.3 1.1 collective-permute-done.25
  132.4 0.6 collective-permute-start.27
  133.0 2.4 %collective-permute-done.27 = f32[8,128]{1,0:T(8,128)S(1)} collective-permute-done((f32[8,128]{1,0:T(8,128)S(1)}, f32[8,128]{1,0:T(8,128)S(1)}, u32[]{:S(2)}, u32[]{:S(2)}) %collective-permute-start.27) | collective-permute-done | bytes 4128 | tf_op jit(solution)/shard_map/ppermute | solution.py:79
  135.5 1.5 collective-permute-start.28
  137.0 2.0 %collective-permute-done.28 = f32[8,128]{1,0:T(8,128)S(1)} collective-permute-done((f32[8,128]{1,0:T(8,128)S(1)}, f32[8,128]{1,0:T(8,128)S(1)}, u32[]{:S(2)}, u32[]{:S(2)}) %collective-permute-start.28) | collective-permute-done | bytes 4128 | tf_op jit(solution)/shard_map/ppermute | solution.py:165
  139.1 6.3 %collective-permute-done.29.refs_4_ = f32[1096,128]{1,0:T(8,128)S(1)} collective-permute-done((f32[1096,128]{1,0:T(8,128)S(1)}, f32[1096,128]{1,0:T(8,128)S(1)}, u32[]{:S(2)}, u32[]{:S(2)}) %collective-permute-start.29) | collective-permute-done | bytes 561184 | tf_op jit(solution)/shard_map/ppermute | solution.py:79
  145.4 1.9 %collective-permute-done.33.refs_9_ = f32[1096,128]{1,0:T(8,128)S(1)} collective-permute-done((f32[1096,128]{1,0:T(8,128)S(1)}, f32[1096,128]{1,0:T(8,128)S(1)}, u32[]{:S(2)}, u32[]{:S(2)}) %collective-permute-start.33) | collective-permute-done | bytes 561184 | tf_op jit(solution)/shard_map/ppermute | solution.py:79
  147.4 19.6 %new_weights.1 = (f32[17408,128]{1,0:T(8,128)}, f32[3,2,1024]{2,1,0:T(2,128)}, f32[7]{0:T(128)}) custom-call(s32[3]{0:T(128)S(1)} %copy-done.6, s32[136,128]{1,0:T(8,128)S(1)} %copy-done.4, f32[8,128]{1,0:T(8,128)S(1)} %add.86.total_ref, f32[3,2,1024]{2,1,0:T(2,128)S(1)} %copy-done.5, f32[17408,128]{1,0:T(8,128)S(1)} %bitcast.11, ...), custom_call_target="tpu_custom_call" | custom-call | tf_op jit(solution)/shard_map/new_weights/pallas_call | solution.py:525
  (71 shorter events, 0.4 us)
Async XLA Ops:
  21.9 7.4 %copy-start.13 = (f32[1096,128]{1,0:T(8,128)S(1)}, f32[1096,128]{1,0:T(8,128)}, u32[]{:S(2)}) copy-start(f32[1096,128]{1,0:T(8,128)} %get-tuple-element.77) | copy-start | bytes 1683460
  21.9 2.3 %collective-permute-start = (f32[1096,128]{1,0:T(8,128)}, f32[1096,128]{1,0:T(8,128)S(1)}, u32[]{:S(2)}, u32[]{:S(2)}) collective-permute-start(f32[1096,128]{1,0:T(8,128)} %get-tuple-element.61), channel_id=1, source_target_pairs={{0,2},{2,0},{4,6},{6,4},{8,10},{10,8},{12,14},{14,12},{16,18},{18,... | collective-permute-start | bytes 1683464 | tf_op jit(solution)/shard_map/ppermute | solution.py:79
  25.4 16.9 %copy-start.12 = (f32[1096,128]{1,0:T(8,128)S(1)}, f32[1096,128]{1,0:T(8,128)}, u32[]{:S(2)}) copy-start(f32[1096,128]{1,0:T(8,128)} %get-tuple-element.72) | copy-start | bytes 1683460
  25.4 4.0 %collective-permute-start.8 = (f32[1096,128]{1,0:T(8,128)}, f32[1096,128]{1,0:T(8,128)S(1)}, u32[]{:S(2)}, u32[]{:S(2)}) collective-permute-start(f32[1096,128]{1,0:T(8,128)} %get-tuple-element.78), channel_id=1, source_target_pairs={{0,2},{2,0},{4,6},{6,4},{8,10},{10,8},{12,14},{14,12},{16,18},{18,... | collective-permute-start | bytes 1683464 | tf_op jit(solution)/shard_map/ppermute | solution.py:79
  25.8 4.8 %collective-permute-start.4 = (f32[1096,128]{1,0:T(8,128)}, f32[1096,128]{1,0:T(8,128)S(1)}, u32[]{:S(2)}, u32[]{:S(2)}) collective-permute-start(f32[1096,128]{1,0:T(8,128)} %get-tuple-element.73), channel_id=1, source_target_pairs={{0,2},{2,0},{4,6},{6,4},{8,10},{10,8},{12,14},{14,12},{16,18},{18,... | collective-permute-start | bytes 1683464 | tf_op jit(solution)/shard_map/ppermute | solution.py:79
  26.0 16.4 %collective-permute-start.5 = (f32[1096,128]{1,0:T(8,128)S(1)}, f32[1096,128]{1,0:T(8,128)S(1)}, u32[]{:S(2)}, u32[]{:S(2)}) collective-permute-start(f32[1096,128]{1,0:T(8,128)S(1)} %add.68), channel_id=1, source_target_pairs={{0,4},{2,6},{4,0},{6,2},{8,12},{10,14},{12,8},{14,10},{16,20},{18,... | collective-permute-start | bytes 1683464 | tf_op jit(solution)/shard_map/ppermute | solution.py:79
  28.8 26.5 %collective-permute-start.7 = (f32[1096,128]{1,0:T(8,128)}, f32[1096,128]{1,0:T(8,128)S(1)}, u32[]{:S(2)}, u32[]{:S(2)}) collective-permute-start(f32[1096,128]{1,0:T(8,128)} %get-tuple-element.76), channel_id=1, source_target_pairs={{0,2},{2,0},{4,6},{6,4},{8,10},{10,8},{12,14},{14,12},{16,18},{18,... | collective-permute-start | bytes 1683464 | tf_op jit(solution)/shard_map/ppermute | solution.py:79
  28.8 24.9 %collective-permute-start.13 = (f32[1096,128]{1,0:T(8,128)}, f32[1096,128]{1,0:T(8,128)}, u32[]{:S(2)}, u32[]{:S(2)}) collective-permute-start(f32[1096,128]{1,0:T(8,128)} %get-tuple-element.86), channel_id=1, source_target_pairs={{0,2},{2,0},{4,6},{6,4},{8,10},{10,8},{12,14},{14,12},{16,18},{18,... | collective-permute-start | bytes 1683464 | tf_op jit(solution)/shard_map/ppermute | solution.py:79
  29.4 27.5 %collective-permute-start.9 = (f32[1096,128]{1,0:T(8,128)S(1)}, f32[1096,128]{1,0:T(8,128)S(1)}, u32[]{:S(2)}, u32[]{:S(2)}) collective-permute-start(f32[1096,128]{1,0:T(8,128)S(1)} %add.74), channel_id=1, source_target_pairs={{0,4},{2,6},{4,0},{6,2},{8,12},{10,14},{12,8},{14,10},{16,20},{18,... | collective-permute-start | bytes 1683464 | tf_op jit(solution)/shard_map/ppermute | solution.py:79
  42.4 14.7 %collective-permute-start.6 = (f32[1096,128]{1,0:T(8,128)S(1)}, f32[1096,128]{1,0:T(8,128)S(1)}, u32[]{:S(2)}, u32[]{:S(2)}) collective-permute-start(f32[1096,128]{1,0:T(8,128)S(1)} %add_add_fusion.2), channel_id=1, source_target_pairs={{0,8},{2,10},{4,12},{6,14},{24,16},{26,18},{28,20},{30,22},{1,9},{... | collective-permute-start | bytes 1683464 | tf_op jit(solution)/shard_map/ppermute | solution.py:79
  47.2 6.5 %copy-start.16 = (f32[1096,128]{1,0:T(8,128)S(1)}, f32[1096,128]{1,0:T(8,128)}, u32[]{:S(2)}) copy-start(f32[1096,128]{1,0:T(8,128)} %get-tuple-element.71) | copy-start | bytes 1683460
  47.2 6.6 %copy-start.15 = (f32[1096,128]{1,0:T(8,128)S(1)}, f32[1096,128]{1,0:T(8,128)}, u32[]{:S(2)}) copy-start(f32[1096,128]{1,0:T(8,128)} %get-tuple-element.84) | copy-start | bytes 1683460
  47.2 7.1 %copy-start.11 = (f32[1096,128]{1,0:T(8,128)S(1)}, f32[1096,128]{1,0:T(8,128)}, u32[]{:S(2)}) copy-start(f32[1096,128]{1,0:T(8,128)} %get-tuple-element.85) | copy-start | bytes 1683460
  53.6 3.3 %copy-start.10 = (f32[1096,128]{1,0:T(8,128)S(1)}, f32[1096,128]{1,0:T(8,128)}, u32[]{:S(2)}) copy-start(f32[1096,128]{1,0:T(8,128)} %get-tuple-element.75) | copy-start | bytes 1683460
  53.7 8.8 %collective-permute-start.2 = (f32[1096,128]{1,0:T(8,128)S(1)}, f32[1096,128]{1,0:T(8,128)S(1)}, u32[]{:S(2)}, u32[]{:S(2)}) collective-permute-start(f32[1096,128]{1,0:T(8,128)S(1)} %copy-done.16), channel_id=1, source_target_pairs={{0,2},{2,0},{4,6},{6,4},{8,10},{10,8},{12,14},{14,12},{16,18},{18,... | collective-permute-start | bytes 1683464 | tf_op jit(solution)/shard_map/ppermute | solution.py:79
  53.8 8.9 %collective-permute-start.12 = (f32[1096,128]{1,0:T(8,128)S(1)}, f32[1096,128]{1,0:T(8,128)S(1)}, u32[]{:S(2)}, u32[]{:S(2)}) collective-permute-start(f32[1096,128]{1,0:T(8,128)S(1)} %copy-done.15), channel_id=1, source_target_pairs={{0,2},{2,0},{4,6},{6,4},{8,10},{10,8},{12,14},{14,12},{16,18},{18,... | collective-permute-start | bytes 1683464 | tf_op jit(solution)/shard_map/ppermute | solution.py:79
  55.4 15.6 %collective-permute-start.14 = (f32[1096,128]{1,0:T(8,128)S(1)}, f32[1096,128]{1,0:T(8,128)S(1)}, u32[]{:S(2)}, u32[]{:S(2)}) collective-permute-start(f32[1096,128]{1,0:T(8,128)S(1)} %add.79), channel_id=1, source_target_pairs={{0,4},{2,6},{4,0},{6,2},{8,12},{10,14},{12,8},{14,10},{16,20},{18,... | collective-permute-start | bytes 1683464 | tf_op jit(solution)/shard_map/ppermute | solution.py:79
  57.0 5.4 %copy-start.14 = (f32[1096,128]{1,0:T(8,128)S(1)}, f32[1096,128]{1,0:T(8,128)}, u32[]{:S(2)}) copy-start(f32[1096,128]{1,0:T(8,128)} %get-tuple-element.69) | copy-start | bytes 1683460
  57.0 5.5 %copy-start.9 = (f32[1096,128]{1,0:T(8,128)S(1)}, f32[1096,128]{1,0:T(8,128)}, u32[]{:S(2)}) copy-start(f32[1096,128]{1,0:T(8,128)} %get-tuple-element.70) | copy-start | bytes 1683460
  57.1 14.1 %collective-permute-start.11 = (f32[1096,128]{1,0:T(8,128)S(1)}, f32[1096,128]{1,0:T(8,128)S(1)}, u32[]{:S(2)}, u32[]{:S(2)}) collective-permute-start(f32[1096,128]{1,0:T(8,128)S(1)} %add_add_fusion.1), channel_id=1, source_target_pairs={{0,8},{2,10},{4,12},{6,14},{24,16},{26,18},{28,20},{30,22},{1,9},{... | collective-permute-start | bytes 1683464 | tf_op jit(solution)/shard_map/ppermute | solution.py:79
  61.6 9.4 %copy-start.8 = (f32[1096,128]{1,0:T(8,128)S(1)}, f32[1096,128]{1,0:T(8,128)}, u32[]{:S(2)}) copy-start(f32[1096,128]{1,0:T(8,128)} %get-tuple-element.83) | copy-start | bytes 1683460
  61.6 9.7 %collective-permute-start.10 = (f32[1096,128]{1,0:T(8,128)S(1)}, f32[1096,128]{1,0:T(8,128)S(1)}, u32[]{:S(2)}, u32[]{:S(2)}) collective-permute-start(f32[1096,128]{1,0:T(8,128)S(1)} %add.76), channel_id=1, source_target_pairs={{8,16},{10,18},{12,20},{14,22},{16,8},{18,10},{20,12},{22,14},{9,1... | collective-permute-start | bytes 1683464 | tf_op jit(solution)/shard_map/ppermute | solution.py:79
  62.5 13.6 %collective-permute-start.1 = (f32[1096,128]{1,0:T(8,128)S(1)}, f32[1096,128]{1,0:T(8,128)S(1)}, u32[]{:S(2)}, u32[]{:S(2)}) collective-permute-start(f32[1096,128]{1,0:T(8,128)S(1)} %copy-done.14), channel_id=1, source_target_pairs={{0,2},{2,0},{4,6},{6,4},{8,10},{10,8},{12,14},{14,12},{16,18},{18,... | collective-permute-start | bytes 1683464 | tf_op jit(solution)/shard_map/ppermute | solution.py:79
  62.6 19.5 %collective-permute-start.3 = (f32[1096,128]{1,0:T(8,128)S(1)}, f32[1096,128]{1,0:T(8,128)S(1)}, u32[]{:S(2)}, u32[]{:S(2)}) collective-permute-start(f32[1096,128]{1,0:T(8,128)S(1)} %add.70), channel_id=1, source_target_pairs={{0,4},{2,6},{4,0},{6,2},{8,12},{10,14},{12,8},{14,10},{16,20},{18,... | collective-permute-start | bytes 1683464 | tf_op jit(solution)/shard_map/ppermute | solution.py:79
  71.0 5.1 %copy-start.7 = (f32[1096,128]{1,0:T(8,128)S(1)}, f32[1096,128]{1,0:T(8,128)}, u32[]{:S(2)}) copy-start(f32[1096,128]{1,0:T(8,128)} %get-tuple-element.59) | copy-start | bytes 1683460
  71.0 13.9 %copy-start.1 = (f32[1,1088,128]{2,1,0:T(8,128)S(1)}, f32[1,1088,128]{2,1,0:T(8,128)}, u32[]{:S(2)}) copy-start(f32[1,1088,128]{2,1,0:T(8,128)} %param.9) | copy-start | bytes 1671172
  71.0 13.9 %copy-start.2 = (f32[1,1088,128]{2,1,0:T(8,128)S(1)}, f32[1,1088,128]{2,1,0:T(8,128)}, u32[]{:S(2)}) copy-start(f32[1,1088,128]{2,1,0:T(8,128)} %param.10) | copy-start | bytes 1671172
  71.0 13.9 %copy-start.3 = (f32[1088,128]{1,0:T(8,128)S(1)}, f32[1088,128]{1,0:T(8,128)}, u32[]{:S(2)}) copy-start(f32[1088,128]{1,0:T(8,128)} %get-tuple-element.90.refs_6_) | copy-start | bytes 1671172
  71.2 76.2 %slice-start = ((s8[8912896]{0:T(1024)(128)(4,1)}), s8[4194304]{0:T(1024)(128)(4,1)S(1)}, s32[]{:S(2)}) async-start(s8[8912896]{0:T(1024)(128)(4,1)} %bitcast.10), calls=%async_computation | async-start | bytes 8388608
  71.4 13.6 %copy-start = (s32[1152,128]{1,0:T(8,128)S(1)}, s32[1152,128]{1,0:T(8,128)}, u32[]{:S(2)}) copy-start(s32[1152,128]{1,0:T(8,128)} %get-tuple-element.91.refs_7_) | copy-start | bytes 1769476
  71.4 13.5 %collective-permute-start.15 = (f32[1096,128]{1,0:T(8,128)S(1)}, f32[1096,128]{1,0:T(8,128)S(1)}, u32[]{:S(2)}, u32[]{:S(2)}) collective-permute-start(f32[1096,128]{1,0:T(8,128)S(1)} %add.81), channel_id=1, source_target_pairs={{0,8},{2,10},{4,12},{6,14},{8,0},{10,2},{12,4},{14,6},{16,24},{18,... | collective-permute-start | bytes 1683464 | tf_op jit(solution)/shard_map/ppermute | solution.py:79
  75.3 9.5 %collective-permute-start.16 = (f32[1096,128]{1,0:T(8,128)S(1)}, f32[1096,128]{1,0:T(8,128)S(1)}, u32[]{:S(2)}, u32[]{:S(2)}) collective-permute-start(f32[1096,128]{1,0:T(8,128)S(1)} %add.77), channel_id=1, source_target_pairs={{8,16},{10,18},{12,20},{14,22},{16,8},{18,10},{20,12},{22,14},{9,1... | collective-permute-start | bytes 1683464 | tf_op jit(solution)/shard_map/ppermute | solution.py:79
  84.9 62.5 %slice-start.1 = ((s8[8912896]{0:T(1024)(128)(4,1)}), s8[4194304]{0:T(1024)(128)(4,1)S(1)}, s32[]{:S(2)}) async-start(s8[8912896]{0:T(1024)(128)(4,1)} %bitcast.10), calls=%async_computation.1 | async-start | bytes 8388608
  87.0 12.5 %collective-permute-start.18 = (f32[1096,128]{1,0:T(8,128)S(1)}, f32[1096,128]{1,0:T(8,128)S(1)}, u32[]{:S(2)}, u32[]{:S(2)}) collective-permute-start(f32[1096,128]{1,0:T(8,128)S(1)} %get-tuple-element.92), channel_id=1, source_target_pairs={{0,8},{2,10},{4,12},{6,14},{8,0},{10,2},{12,4},{14,6},{16,24},{18,... | collective-permute-start | bytes 1683464 | tf_op jit(solution)/shard_map/ppermute | solution.py:79
  90.8 13.8 %collective-permute-start.19 = (f32[1096,128]{1,0:T(8,128)S(1)}, f32[1096,128]{1,0:T(8,128)S(1)}, u32[]{:S(2)}, u32[]{:S(2)}) collective-permute-start(f32[1096,128]{1,0:T(8,128)S(1)} %get-tuple-element.92), channel_id=1, source_target_pairs={{0,4},{2,6},{4,0},{6,2},{8,12},{10,14},{12,8},{14,10},{16,20},{18,... | collective-permute-start | bytes 1683464 | tf_op jit(solution)/shard_map/ppermute | solution.py:79
  92.3 12.3 %collective-permute-start.17 = (f32[1096,128]{1,0:T(8,128)S(1)}, f32[1096,128]{1,0:T(8,128)S(1)}, u32[]{:S(2)}, u32[]{:S(2)}) collective-permute-start(f32[1096,128]{1,0:T(8,128)S(1)} %get-tuple-element.92), channel_id=1, source_target_pairs={{8,16},{10,18},{12,20},{14,22},{16,8},{18,10},{20,12},{22,14},{9,1... | collective-permute-start | bytes 1683464 | tf_op jit(solution)/shard_map/ppermute | solution.py:79
  99.4 13.5 %collective-permute-start.24 = (f32[1096,128]{1,0:T(8,128)S(1)}, f32[1096,128]{1,0:T(8,128)S(1)}, u32[]{:S(2)}, u32[]{:S(2)}) collective-permute-start(f32[1096,128]{1,0:T(8,128)S(1)} %collective-permute-done.18), channel_id=1, source_target_pairs={{0,4},{2,6},{4,0},{6,2},{8,12},{10,14},{12,8},{14,10},{16,20},{18,... | collective-permute-start | bytes 1683464 | tf_op jit(solution)/shard_map/ppermute | solution.py:79
  100.9 12.0 %collective-permute-start.20 = (f32[1096,128]{1,0:T(8,128)S(1)}, f32[1096,128]{1,0:T(8,128)S(1)}, u32[]{:S(2)}, u32[]{:S(2)}) collective-permute-start(f32[1096,128]{1,0:T(8,128)S(1)} %collective-permute-done.18), channel_id=1, source_target_pairs={{8,16},{10,18},{12,20},{14,22},{16,8},{18,10},{20,12},{22,14},{9,1... | collective-permute-start | bytes 1683464 | tf_op jit(solution)/shard_map/ppermute | solution.py:79
  104.6 12.7 %collective-permute-start.23 = (f32[1096,128]{1,0:T(8,128)S(1)}, f32[1096,128]{1,0:T(8,128)S(1)}, u32[]{:S(2)}, u32[]{:S(2)}) collective-permute-start(f32[1096,128]{1,0:T(8,128)S(1)} %collective-permute-done.17), channel_id=1, source_target_pairs={{8,0},{10,2},{12,4},{14,6},{16,24},{18,26},{20,28},{22,30},{9,1},{... | collective-permute-start | bytes 1683464 | tf_op jit(solution)/shard_map/ppermute | solution.py:79
  112.9 15.2 %collective-permute-start.21 = (f32[1096,128]{1,0:T(8,128)S(1)}, f32[1096,128]{1,0:T(8,128)S(1)}, u32[]{:S(2)}, u32[]{:S(2)}) collective-permute-start(f32[1096,128]{1,0:T(8,128)S(1)} %collective-permute-done.20), channel_id=1, source_target_pairs={{8,0},{10,2},{12,4},{14,6},{16,24},{18,26},{20,28},{22,30},{9,1},{... | collective-permute-start | bytes 1683464 | tf_op jit(solution)/shard_map/ppermute | solution.py:79
  114.3 33.1 %slice-start.2 = ((s8[8912896]{0:T(1024)(128)(4,1)}), s8[524288]{0:T(1024)(128)(4,1)S(1)}, s32[]{:S(2)}) async-start(s8[8912896]{0:T(1024)(128)(4,1)} %bitcast.10), calls=%async_computation.2 | async-start | bytes 1048576
  117.4 10.8 %copy-start.6 = (s32[3]{0:T(128)S(1)}, s32[3]{0:T(128)}, u32[]{:S(2)}) copy-start(s32[3]{0:T(128)} %pad_add_fusion.place_ref) | copy-start | bytes 40
  117.4 15.1 %collective-permute-start.26 = (f32[1096,128]{1,0:T(8,128)S(1)}, f32[1096,128]{1,0:T(8,128)S(1)}, u32[]{:S(2)}, u32[]{:S(2)}) collective-permute-start(f32[1096,128]{1,0:T(8,128)S(1)} %add.83.refs_2_), channel_id=1, source_target_pairs={{0,4},{2,6},{4,0},{6,2},{8,12},{10,14},{12,8},{14,10},{16,20},{18,... | collective-permute-start | bytes 1683464 | tf_op jit(solution)/shard_map/ppermute | solution.py:79
  128.7 3.7 %collective-permute-start.25 = (f32[8,128]{1,0:T(8,128)S(1)}, f32[8,128]{1,0:T(8,128)S(1)}, u32[]{:S(2)}, u32[]{:S(2)}) collective-permute-start(f32[8,128]{1,0:T(8,128)S(1)} %sums.1), channel_id=1, source_target_pairs={{0,4},{2,6},{4,0},{6,2},{8,12},{10,14},{12,8},{14,10},{16,20},{18,... | collective-permute-start | bytes 12296 | tf_op jit(solution)/shard_map/ppermute | solution.py:79
  130.3 15.1 %collective-permute-start.30 = (f32[2192,128]{1,0:T(8,128)S(1)}, f32[2192,128]{1,0:T(8,128)S(1)}, u32[]{:S(2)}, u32[]{:S(2)}) collective-permute-start(f32[2192,128]{1,0:T(8,128)S(1)} %pad_maximum_fusion.refs_0_.refs_1_), channel_id=1, source_target_pairs={{0,2},{2,0},{4,6},{6,4},{8,10},{10,8},{12,14},{14,12},{16,18},{18,... | collective-permute-start | bytes 3366920 | tf_op jit(solution)/shard_map/ppermute | solution.py:79
  130.3 15.1 %collective-permute-start.31 = (f32[2192,128]{1,0:T(8,128)S(1)}, f32[2192,128]{1,0:T(8,128)S(1)}, u32[]{:S(2)}, u32[]{:S(2)}) collective-permute-start(f32[2192,128]{1,0:T(8,128)S(1)} %pad_maximum_fusion.1.refs_1_), channel_id=1, source_target_pairs={{0,2},{2,0},{4,6},{6,4},{8,10},{10,8},{12,14},{14,12},{16,18},{18,... | collective-permute-start | bytes 3366920 | tf_op jit(solution)/shard_map/ppermute | solution.py:79
  130.8 14.6 %collective-permute-start.29 = (f32[1096,128]{1,0:T(8,128)S(1)}, f32[1096,128]{1,0:T(8,128)S(1)}, u32[]{:S(2)}, u32[]{:S(2)}) collective-permute-start(f32[1096,128]{1,0:T(8,128)S(1)} %add.82.refs_3_), channel_id=1, source_target_pairs={{0,4},{2,6},{4,0},{6,2},{8,12},{10,14},{12,8},{14,10},{16,20},{18,... | collective-permute-start | bytes 1683464 | tf_op jit(solution)/shard_map/ppermute | solution.py:79
  132.4 13.0 %collective-permute-start.22 = (f32[1096,128]{1,0:T(8,128)S(1)}, f32[1096,128]{1,0:T(8,128)S(1)}, u32[]{:S(2)}, u32[]{:S(2)}) collective-permute-start(f32[1096,128]{1,0:T(8,128)S(1)} %add.82.refs_3_), channel_id=1, source_target_pairs={{0,2},{2,0},{4,6},{6,4},{8,10},{10,8},{12,14},{14,12},{16,18},{18,... | collective-permute-start | bytes 1683464 | tf_op jit(solution)/shard_map/ppermute | solution.py:79
  132.4 15.0 %copy-start.4 = (s32[136,128]{1,0:T(8,128)S(1)}, s32[136,128]{1,0:T(8,128)}, u32[]{:S(2)}) copy-start(s32[136,128]{1,0:T(8,128)} %get-tuple-element.58.position_ref) | copy-start | bytes 208900
  132.4 15.0 %copy-start.5 = (f32[3,2,1024]{2,1,0:T(2,128)S(1)}, f32[3,2,1024]{2,1,0:T(2,128)}, u32[]{:S(2)}) copy-start(f32[3,2,1024]{2,1,0:T(2,128)} %norm_ref.1) | copy-start | bytes 73732
  132.4 3.0 %collective-permute-start.27 = (f32[8,128]{1,0:T(8,128)S(1)}, f32[8,128]{1,0:T(8,128)S(1)}, u32[]{:S(2)}, u32[]{:S(2)}) collective-permute-start(f32[8,128]{1,0:T(8,128)S(1)} %add.84), channel_id=1, source_target_pairs={{0,2},{2,0},{4,6},{6,4},{8,10},{10,8},{12,14},{14,12},{16,18},{18,... | collective-permute-start | bytes 12296 | tf_op jit(solution)/shard_map/ppermute | solution.py:79
  135.5 3.6 %collective-permute-start.28 = (f32[8,128]{1,0:T(8,128)S(1)}, f32[8,128]{1,0:T(8,128)S(1)}, u32[]{:S(2)}, u32[]{:S(2)}) collective-permute-start(f32[8,128]{1,0:T(8,128)S(1)} %add.85), channel_id=1, source_target_pairs={{0,1},{1,0},{2,3},{3,2},{4,5},{5,4},{6,7},{7,6},{8,9},{9,8},{10,11... | collective-permute-start | bytes 12296 | tf_op jit(solution)/shard_map/ppermute | solution.py:165
  139.1 8.3 %collective-permute-start.32 = (f32[2192,128]{1,0:T(8,128)S(1)}, f32[2192,128]{1,0:T(8,128)S(1)}, u32[]{:S(2)}, u32[]{:S(2)}) collective-permute-start(f32[2192,128]{1,0:T(8,128)S(1)} %constant_dynamic-update-slice_fusion.refs_2_), channel_id=1, source_target_pairs={{0,2},{2,0},{4,6},{6,4},{8,10},{10,8},{12,14},{14,12},{16,18},{18,... | collective-permute-start | bytes 3366920 | tf_op jit(solution)/shard_map/ppermute | solution.py:79
  145.4 2.0 %collective-permute-start.33 = (f32[1096,128]{1,0:T(8,128)S(1)}, f32[1096,128]{1,0:T(8,128)S(1)}, u32[]{:S(2)}, u32[]{:S(2)}) collective-permute-start(f32[1096,128]{1,0:T(8,128)S(1)} %collective-permute-done.29.refs_4_), channel_id=1, source_target_pairs={{0,2},{2,0},{4,6},{6,4},{8,10},{10,8},{12,14},{14,12},{16,18},{18,... | collective-permute-start | bytes 1683464 | tf_op jit(solution)/shard_map/ppermute | solution.py:79
